TPU v7x, 32 devices: a whole 2x2x4 slice. The times are simulated.
32 devices in a mesh: view: 4 (over x, core), tile: 8 (over z, y).
Axes of the slice: x: 2, y: 2, z: 4, core: 2. Of those that a mesh axis runs over, the one named last changes fastest.
Arguments:
- acquired: float32 [4, 128, 128, 256], P('view', 'tile'), may hold values from 0.2 to 5
- estimate: float32 [128, 128, 256], P('tile'), may hold values from 0.5 to 2
- offsets: int32 [4, 3], P('view'), may hold values from -16 to 16, as said below
- view_mask: int32 [4, 128, 128], P('view', 'tile'), may hold values 0 or 1
- kern_x: float32 [4, 31], P('view'), may hold values from 0 to 1, as said below
- kern_y: float32 [4, 31], P('view'), may hold values from 0 to 1, as said below
- kern_z: float32 [4, 61], P('view'), may hold values from 0 to 1, as said below
Outputs:
- refined: float32 [128, 128, 256], P('tile')
Inputs may be any that keep to these rules, and one draw needn't show every extreme that they name: `offsets`: every entry is an integer offset; some view's first offset is 16 and another's is -16. `kern_x`: each row is positive and sums to one. `kern_y`: each row is positive and sums to one. `kern_z`: each row is positive and sums to one.
All inputs are finite; a program needn't handle non-finite values. No bound on the sum of `view_mask` on one device may be relied on, other than what follows from the above.
Results may differ from a plain program's by a relative error of at most 0.0001.
Values sent between devices are 32-bit elements; how exact they have to be, the bound alone decides.
No kernel may reach another device: no remote copies, remote signals or barrier semaphores. Data moves between devices by JAX's collectives and lax.ppermute only.
A program may use at most 64 MiB of HBM per device.

v0:
```python
import jax
import jax.numpy as jnp
from jax import lax
from jax.sharding import PartitionSpec as P

ITERS = 2


def padded_2(block, sides, width):
    for axis, dim in sides:
        count = lax.axis_size(axis)
        forward = [(i, i + 1) for i in range(count - 1)]
        backward = [(target, source) for source, target in forward]
        low = lax.ppermute(
            lax.slice_in_dim(block, block.shape[dim] - width, None, axis=dim), axis, forward
        )
        high = lax.ppermute(lax.slice_in_dim(block, 0, width, axis=dim), axis, backward)
        block = jnp.concatenate([low, block, high], axis=dim)
    return block


def band_matrix(kern, rows, cols, offset):
    rows_idx = lax.broadcasted_iota(jnp.int32, (rows, cols), 0)
    cols_idx = lax.broadcasted_iota(jnp.int32, (rows, cols), 1)
    delta = cols_idx - rows_idx + offset
    total = jnp.zeros((rows, cols), kern.dtype)
    for tap in range(kern.shape[0]):
        total = total + jnp.where(delta == tap, kern[tap], jnp.zeros((), kern.dtype))
    return total


def spread_planes(rimmed, kern):
    planes = rimmed.shape[0] - kern.shape[0] + 1
    matrix = band_matrix(kern, planes, rimmed.shape[0], 0)
    flat = rimmed.reshape(rimmed.shape[0], -1)
    out = jnp.dot(matrix, flat, precision=lax.Precision.HIGHEST, preferred_element_type=jnp.float32)
    return out.reshape(planes, rimmed.shape[1], rimmed.shape[2])


def spread_cross(field, my, mz):
    field = jnp.einsum("xyz,wz->xyw", field, mz, precision=lax.Precision.HIGHEST)
    return jnp.einsum("xyz,wy->xwz", field, my, precision=lax.Precision.HIGHEST)


def shards(acquired, estimate, offsets, view_mask, kern_x, kern_y, kern_z):
    depth = estimate.shape[0]
    cells_y = estimate.shape[1]
    cells_z = estimate.shape[2]
    slabs = lax.axis_size("tile")
    radius = kern_x.shape[1] // 2
    shift_x = offsets[0, 0]
    shift_y = offsets[0, 1]
    shift_z = offsets[0, 2]
    widened = padded_2(acquired[0], (("tile", 0),), depth)
    padded = jnp.pad(widened, ((0, 0), (depth, depth), (depth, depth)))
    image = lax.dynamic_slice(
        padded, (depth + shift_x, depth + shift_y, depth + shift_z), (depth, cells_y, cells_z)
    )
    global_x = lax.axis_index("tile") * depth + jnp.arange(depth, dtype=jnp.int32)
    inside_x = (global_x + shift_x >= 0) & (global_x + shift_x < depth * slabs)
    inside_y = (jnp.arange(cells_y, dtype=jnp.int32) + shift_y >= 0) & (
        jnp.arange(cells_y, dtype=jnp.int32) + shift_y < cells_y
    )
    inside_z = (jnp.arange(cells_z, dtype=jnp.int32) + shift_z >= 0) & (
        jnp.arange(cells_z, dtype=jnp.int32) + shift_z < cells_z
    )
    plane = (view_mask[0] != 0) & inside_x[:, None] & inside_y[None, :]
    covered = plane[:, :, None] & inside_z[None, None, :]
    forward_x = kern_x[0]
    backward_x = kern_x[0][::-1]
    matrix_y = band_matrix(kern_y[0], cells_y, cells_y, kern_y.shape[1] // 2)
    matrix_z = band_matrix(kern_z[0], cells_z, cells_z, kern_z.shape[1] // 2)
    current = estimate
    for step in range(ITERS):
        share_cols = cells_z // lax.axis_size("view")
        col_start = lax.axis_index("view") * share_cols
        own_cols = lax.dynamic_slice_in_dim(current, col_start, share_cols, 2)
        part_rim = padded_2(own_cols, (("tile", 0),), radius)
        rimmed = lax.all_gather(part_rim, "view", axis=2, tiled=True)
        blurred = spread_cross(spread_planes(rimmed, forward_x), matrix_y, matrix_z)
        ratio = jnp.where(covered, image / blurred, jnp.ones((), jnp.float32))
        ratio_rimmed = padded_2(ratio, (("tile", 0),), radius)
        factor = spread_cross(spread_planes(ratio_rimmed, backward_x), matrix_y.T, matrix_z.T)
        log_factor = jnp.log(factor)
        log_total = lax.psum(log_factor, "view")
        current = current * jnp.exp(log_total)
    return current


def solution(mesh):
    in_specs = (
        P("view", "tile", None, None),
        P("tile", None, None),
        P("view", None),
        P("view", "tile", None),
        P("view", None),
        P("view", None),
        P("view", None),
    )
    out_specs = P("tile", None, None)
    return jax.shard_map(shards, mesh=mesh, in_specs=in_specs, out_specs=out_specs, check_vma=False)
```

profile of v0, /device:TPU:17, one launch (start us, length us, event | category | flops | bytes accessed | tf_op | source)
XLA Modules:
  0.0 742.2 jit_solution(6020273595399819517)
XLA Ops:
  6.5 1.6 constant_dynamic-slice_fusion.3
  8.5 3.1 collective-permute-start.2
  11.8 3.2 collective-permute-start.3
  14.9 17.2 %collective-permute-done.2 = f32[15,128,64]{1,2,0:T(8,128)S(1)} collective-permute-done((f32[15,128,64]{1,2,0:T(8,128)S(1)}, f32[15,128,64]{1,2,0:T(8,128)S(1)}, u32[]{:S(2)}, u32[]{:S(2)}) %collective-permute-start.2) | collective-permute-done | bytes 491552 | tf_op jit(solution)/shard_map/ppermute | solution.py:14
  32.1 2.9 collective-permute-done.3
  36.3 1.9 collective-permute-start.1
  38.2 3.4 collective-permute-start
  53.5 38.9 %select_add_fusion = f32[256,256]{1,0:T(8,128)S(1)} fusion(f32[]{:T(128)} %bitcast.132, f32[]{:T(128)} %bitcast.131, f32[]{:T(128)} %bitcast.130, f32[]{:T(128)} %bitcast.129, f32[]{:T(128)} %bitcast.128, f32[]{:T(128)} %bitcast.127, f32[]{:T(128)} %bitcast.126, f32[]{:T(128)} %bitcast.125, f32[]{:T(128)} %bitcast.124, f32[]{:T(128)} %bitcast.123, ...), kind=kLoop, calls=%fused_computation.61 | loop fusion | flops 12058624 | bytes 262388 | tf_op jit(solution)/shard_map/add | solution.py:28
  92.4 1.6 iota_compare_fusion
  94.0 36.0 %collective-permute-done.1 = f32[16,128,256]{2,1,0:T(8,128)} collective-permute-done((f32[16,128,256]{2,1,0:T(8,128)S(1)}, f32[16,128,256]{2,1,0:T(8,128)}, u32[]{:S(2)}, u32[]{:S(2)}) %collective-permute-start.1) | collective-permute-done | bytes 2097184 | tf_op jit(solution)/shard_map/ppermute | solution.py:17
  130.0 7.3 fusion.11
  137.3 6.9 copy.33
  144.2 3.4 slice_bitcast_fusion.3
  147.6 25.1 %fusion.6 = f32[16,128,256]{2,0,1:T(8,128)S(1)} fusion(f32[128,256,46]{1,0,2:T(8,128)S(1)} %slice_bitcast_fusion.3, f32[]{:T(128)} %bitcast.62, f32[]{:T(128)} %bitcast.61, f32[]{:T(128)} %bitcast.60, f32[]{:T(128)} %bitcast.59, f32[]{:T(128)} %bitcast.58, f32[]{:T(128)} %bitcast.57, f32[]{:T(128)} %bitcast.56, f32[]{:T(128)} %bitcast.55, f32[]{:T(128)} %bitcast.54, ...), kind=kOutput, calls=%fused_computation.11 | convolution fusion | flops 289475424 | bytes 8126588 | tf_op jit(solution)/shard_map/dot_general | solution.py:36
  172.8 3.0 fusion.30
  175.8 22.0 %and_select_fusion.1 = f32[16,128,256]{2,1,0:T(8,128)S(1)} fusion(f32[16,128,256]{2,1,0:T(8,128)S(1)} %copy-done.1, f32[16,128,256]{2,1,0:T(8,128)S(1)} %fusion.30, pred[256]{0:T(512)(128)(4,1)S(1)} %compare_and_fusion, pred[16,128]{1,0:T(8,128)(4,1)S(1)} %fusion.196, f32[]{:T(128)} %bitcast.30, f32[]{:T(128)} %bitcast.29, f32[]{:T(128)} %bitcast.28, ...), kind=kOutput, calls=%fused_computation.21 | convolution fusion | flops 808419328 | bytes 6293884 | tf_op jit(solution)/shard_map/xyz,wy->xwz/dot_general | solution.py:42
  198.3 3.8 collective-permute-start.4
  202.1 2.4 collective-permute-start.5
  204.5 81.9 %collective-permute-done.4 = f32[15,128,256]{2,1,0:T(8,128)S(1)} collective-permute-done((f32[15,128,256]{2,1,0:T(8,128)S(1)}, f32[15,128,256]{2,1,0:T(8,128)S(1)}, u32[]{:S(2)}, u32[]{:S(2)}) %collective-permute-start.4) | collective-permute-done | bytes 1966112 | tf_op jit(solution)/shard_map/ppermute | solution.py:14
  286.4 1.6 collective-permute-done.5
  289.4 25.1 %fusion.4 = f32[16,128,256]{2,0,1:T(8,128)S(1)} fusion(f32[128,256,46]{1,0,2:T(8,128)S(1)} %slice_bitcast_fusion.2, f32[]{:T(128)} %bitcast.62, f32[]{:T(128)} %bitcast.61, f32[]{:T(128)} %bitcast.60, f32[]{:T(128)} %bitcast.59, f32[]{:T(128)} %bitcast.58, f32[]{:T(128)} %bitcast.57, f32[]{:T(128)} %bitcast.56, f32[]{:T(128)} %bitcast.55, f32[]{:T(128)} %bitcast.54, ...), kind=kOutput, calls=%fused_computation.9 | convolution fusion | flops 289475424 | bytes 8126588 | tf_op jit(solution)/shard_map/dot_general | solution.py:36
  314.5 2.9 fusion.28
  317.5 22.8 %log_bitcast_fusion.1 = f32[16,128,256]{2,1,0:T(8,128)} fusion(f32[16,128,256]{2,1,0:T(8,128)S(1)} %fusion.28, f32[]{:T(128)} %bitcast.30, f32[]{:T(128)} %bitcast.29, f32[]{:T(128)} %bitcast.28, f32[]{:T(128)} %bitcast.27, f32[]{:T(128)} %bitcast.26, f32[]{:T(128)} %bitcast.25, f32[]{:T(128)} %bitcast.24, f32[]{:T(128)} %bitcast.23, f32[]{:T(128)} %bitcast.22, ...), kind=kOutput, calls=%fused_computation.53 | convolution fusion | flops 806846464 | bytes 4194428 | tf_op jit(solution)/shard_map/xyz,wy->xwz/dot_general | solution.py:42
  340.4 50.7 %all-reduce.4.cloned.1.call-done = f32[16,128,256]{2,1,0:T(8,128)} async-done(((f32[16,128,256]{2,1,0:T(8,128)}), f32[16,128,256]{2,1,0:T(8,128)}) %all-reduce.4.cloned.1.call-update) | async-done | bytes 2097168 | tf_op jit(solution)/shard_map/psum | solution.py:85
  391.1 2.6 exponential_multiply_fusion.1
  395.2 2.3 copy.40
  397.5 3.1 collective-permute-start.7
  401.7 2.2 collective-permute-start.6
  404.2 18.0 %collective-permute-done.7 = f32[15,128,64]{1,2,0:T(8,128)} collective-permute-done((f32[15,128,64]{1,2,0:T(8,128)}, f32[15,128,64]{1,2,0:T(8,128)}, u32[]{:S(2)}, u32[]{:S(2)}) %collective-permute-start.7) | collective-permute-done | bytes 491552 | tf_op jit(solution)/shard_map/ppermute | solution.py:17
  422.3 2.3 copy.42
  424.6 2.3 copy.41
  426.9 3.4 pad_maximum_fusion.2
  430.3 3.2 copy.43
  433.5 45.7 %all-gather.5.cloned.1.call-done = f32[46,128,256]{1,2,0:T(8,128)} async-done(((f32[46,128,64]{1,2,0:T(8,128)}), f32[46,128,256]{1,2,0:T(8,128)}) %all-gather.5.cloned.1.call-update) | async-done | bytes 6029328 | tf_op jit(solution)/shard_map/all_gather | solution.py:79
  479.2 6.9 copy.44
  486.1 3.4 slice_bitcast_fusion.1
  489.5 25.1 %fusion.2 = f32[16,128,256]{2,0,1:T(8,128)S(1)} fusion(f32[128,256,46]{1,0,2:T(8,128)S(1)} %slice_bitcast_fusion.1, f32[]{:T(128)} %bitcast.62, f32[]{:T(128)} %bitcast.61, f32[]{:T(128)} %bitcast.60, f32[]{:T(128)} %bitcast.59, f32[]{:T(128)} %bitcast.58, f32[]{:T(128)} %bitcast.57, f32[]{:T(128)} %bitcast.56, f32[]{:T(128)} %bitcast.55, f32[]{:T(128)} %bitcast.54, ...), kind=kOutput, calls=%fused_computation.7 | convolution fusion | flops 289475424 | bytes 8126588 | tf_op jit(solution)/shard_map/dot_general | solution.py:36
  514.7 3.0 fusion.26
  517.6 21.8 %and_select_fusion = f32[16,128,256]{2,1,0:T(8,128)S(1)} fusion(f32[16,128,256]{2,1,0:T(8,128)S(1)} %copy-done.2, f32[16,128,256]{2,1,0:T(8,128)S(1)} %fusion.26, pred[256]{0:T(512)(128)(4,1)S(1)} %compare_and_fusion, pred[16,128]{1,0:T(8,128)(4,1)S(1)} %fusion.196, f32[]{:T(128)} %bitcast.30, f32[]{:T(128)} %bitcast.29, f32[]{:T(128)} %bitcast.28, ...), kind=kOutput, calls=%fused_computation.20 | convolution fusion | flops 808419328 | bytes 6293884 | tf_op jit(solution)/shard_map/xyz,wy->xwz/dot_general | solution.py:42
  540.0 3.1 collective-permute-start.8
  543.1 3.2 collective-permute-start.9
  546.4 80.8 %collective-permute-done.8 = f32[15,128,256]{2,1,0:T(8,128)S(1)} collective-permute-done((f32[15,128,256]{2,1,0:T(8,128)S(1)}, f32[15,128,256]{2,1,0:T(8,128)S(1)}, u32[]{:S(2)}, u32[]{:S(2)}) %collective-permute-start.8) | collective-permute-done | bytes 1966112 | tf_op jit(solution)/shard_map/ppermute | solution.py:14
  627.2 2.5 collective-permute-done.9
  631.1 25.1 %fusion = f32[16,128,256]{2,0,1:T(8,128)S(1)} fusion(f32[128,256,46]{1,0,2:T(8,128)S(1)} %slice_bitcast_fusion, f32[]{:T(128)} %bitcast.62, f32[]{:T(128)} %bitcast.61, f32[]{:T(128)} %bitcast.60, f32[]{:T(128)} %bitcast.59, f32[]{:T(128)} %bitcast.58, f32[]{:T(128)} %bitcast.57, f32[]{:T(128)} %bitcast.56, f32[]{:T(128)} %bitcast.55, f32[]{:T(128)} %bitcast.54, ...), kind=kOutput, calls=%fused_computation.5 | convolution fusion | flops 289475424 | bytes 8126588 | tf_op jit(solution)/shard_map/dot_general | solution.py:36
  656.2 2.9 fusion.24
  659.1 22.8 %log_bitcast_fusion = f32[16,128,256]{2,1,0:T(8,128)} fusion(f32[16,128,256]{2,1,0:T(8,128)S(1)} %fusion.24, f32[]{:T(128)} %bitcast.30, f32[]{:T(128)} %bitcast.29, f32[]{:T(128)} %bitcast.28, f32[]{:T(128)} %bitcast.27, f32[]{:T(128)} %bitcast.26, f32[]{:T(128)} %bitcast.25, f32[]{:T(128)} %bitcast.24, f32[]{:T(128)} %bitcast.23, f32[]{:T(128)} %bitcast.22, ...), kind=kOutput, calls=%fused_computation.51 | convolution fusion | flops 806846464 | bytes 4194428 | tf_op jit(solution)/shard_map/xyz,wy->xwz/dot_general | solution.py:42
  682.0 50.4 %all-reduce.6.cloned.1.call-done = f32[16,128,256]{2,1,0:T(8,128)} async-done(((f32[16,128,256]{2,1,0:T(8,128)}), f32[16,128,256]{2,1,0:T(8,128)}) %all-reduce.6.cloned.1.call-update) | async-done | bytes 2097168 | tf_op jit(solution)/shard_map/psum | solution.py:85
  732.3 3.2 exponential_multiply_fusion
  (52 shorter events, 16.9 us)
Async XLA Ops:
  6.5 130.7 %all-gather.3.cloned.1.call-start = ((), (), s32[]{:S(2)}) async-start(), calls=%async_computation | async-start | bytes 7536640 | tf_op jit(solution)/shard_map/all_gather | solution.py:79
  8.5 23.6 %collective-permute-start.2 = (f32[15,128,64]{1,2,0:T(8,128)S(1)}, f32[15,128,64]{1,2,0:T(8,128)S(1)}, u32[]{:S(2)}, u32[]{:S(2)}) collective-permute-start(f32[15,128,64]{1,2,0:T(8,128)S(1)} %get-tuple-element.11), channel_id=1, source_target_pairs={{0,1},{1,2},{2,3},{3,4},{4,5},{5,6},{6,7},{8,9},{9,10},{10,11},{11... | collective-permute-start | bytes 1474568 | tf_op jit(solution)/shard_map/ppermute | solution.py:14
  11.7 24.6 %copy-start = (f32[1,16,128,256]{3,2,1,0:T(8,128)S(1)}, f32[1,16,128,256]{3,2,1,0:T(8,128)}, u32[]{:S(2)}) copy-start(f32[1,16,128,256]{3,2,1,0:T(8,128)} %param.7) | copy-start | bytes 6291460
  11.7 29.9 %copy-start.7 = (s32[1,3]{1,0:T(1,128)S(1)}, s32[1,3]{1,0:T(1,128)}, u32[]{:S(2)}) copy-start(s32[1,3]{1,0:T(1,128)} %param.9) | copy-start | bytes 40
  11.7 31.8 %copy-start.3 = (f32[1,61]{1,0:T(1,128)S(1)}, f32[1,61]{1,0:T(1,128)}, u32[]{:S(2)}) copy-start(f32[1,61]{1,0:T(1,128)} %param.13) | copy-start | bytes 736
  11.7 32.4 %copy-start.4 = (f32[1,31]{1,0:T(1,128)S(1)}, f32[1,31]{1,0:T(1,128)}, u32[]{:S(2)}) copy-start(f32[1,31]{1,0:T(1,128)} %param.11) | copy-start | bytes 376
  11.7 33.1 %copy-start.5 = (f32[1,31]{1,0:T(1,128)S(1)}, f32[1,31]{1,0:T(1,128)}, u32[]{:S(2)}) copy-start(f32[1,31]{1,0:T(1,128)} %param.12) | copy-start | bytes 376
  11.8 41.7 %copy-start.6 = (s32[1,16,128]{2,1,0:T(8,128)S(1)}, s32[1,16,128]{2,1,0:T(8,128)}, u32[]{:S(2)}) copy-start(s32[1,16,128]{2,1,0:T(8,128)} %param.10) | copy-start | bytes 24580
  11.8 23.2 %collective-permute-start.3 = (f32[15,128,64]{1,2,0:T(8,128)S(1)}, f32[15,128,64]{1,2,0:T(8,128)S(1)}, u32[]{:S(2)}, u32[]{:S(2)}) collective-permute-start(f32[15,128,64]{1,2,0:T(8,128)S(1)} %get-tuple-element.12), channel_id=1, source_target_pairs={{1,0},{2,1},{3,2},{4,3},{5,4},{6,5},{7,6},{9,8},{10,9},{11,10},{12... | collective-permute-start | bytes 1474568 | tf_op jit(solution)/shard_map/ppermute | solution.py:17
  36.2 354.8 %all-reduce.4.cloned.1.call-start = ((), (), s32[]{:S(2)}) async-start(), calls=%async_computation.1 | async-start | bytes 4194304 | tf_op jit(solution)/shard_map/psum | solution.py:85
  36.3 93.6 %collective-permute-start.1 = (f32[16,128,256]{2,1,0:T(8,128)S(1)}, f32[16,128,256]{2,1,0:T(8,128)}, u32[]{:S(2)}, u32[]{:S(2)}) collective-permute-start(f32[16,128,256]{2,1,0:T(8,128)S(1)} %bitcast.223), channel_id=1, source_target_pairs={{1,0},{2,1},{3,2},{4,3},{5,4},{6,5},{7,6},{9,8},{10,9},{11,10},{12... | collective-permute-start | bytes 6291464 | tf_op jit(solution)/shard_map/ppermute | solution.py:17
  38.2 91.7 %collective-permute-start = (f32[16,128,256]{2,1,0:T(8,128)S(1)}, f32[16,128,256]{2,1,0:T(8,128)}, u32[]{:S(2)}, u32[]{:S(2)}) collective-permute-start(f32[16,128,256]{2,1,0:T(8,128)S(1)} %bitcast.224), channel_id=1, source_target_pairs={{0,1},{1,2},{2,3},{3,4},{4,5},{5,6},{6,7},{8,9},{9,10},{10,11},{11... | collective-permute-start | bytes 6291464 | tf_op jit(solution)/shard_map/ppermute | solution.py:14
  172.8 3.0 copy-start.1
  198.3 88.1 %collective-permute-start.4 = (f32[15,128,256]{2,1,0:T(8,128)S(1)}, f32[15,128,256]{2,1,0:T(8,128)S(1)}, u32[]{:S(2)}, u32[]{:S(2)}) collective-permute-start(f32[15,128,256]{2,1,0:T(8,128)S(1)} %get-tuple-element.9), channel_id=1, source_target_pairs={{0,1},{1,2},{2,3},{3,4},{4,5},{5,6},{6,7},{8,9},{9,10},{10,11},{11... | collective-permute-start | bytes 5898248 | tf_op jit(solution)/shard_map/ppermute | solution.py:14
  202.1 85.9 %collective-permute-start.5 = (f32[15,128,256]{2,1,0:T(8,128)S(1)}, f32[15,128,256]{2,1,0:T(8,128)S(1)}, u32[]{:S(2)}, u32[]{:S(2)}) collective-permute-start(f32[15,128,256]{2,1,0:T(8,128)S(1)} %get-tuple-element.10), channel_id=1, source_target_pairs={{1,0},{2,1},{3,2},{4,3},{5,4},{6,5},{7,6},{9,8},{10,9},{11,10},{12... | collective-permute-start | bytes 5898248 | tf_op jit(solution)/shard_map/ppermute | solution.py:17
  340.3 138.9 %all-gather.5.cloned.1.call-start = ((), (), s32[]{:S(2)}) async-start(), calls=%async_computation.2 | async-start | bytes 7536640 | tf_op jit(solution)/shard_map/all_gather | solution.py:79
  397.5 24.7 %collective-permute-start.7 = (f32[15,128,64]{1,2,0:T(8,128)}, f32[15,128,64]{1,2,0:T(8,128)}, u32[]{:S(2)}, u32[]{:S(2)}) collective-permute-start(f32[15,128,64]{1,2,0:T(8,128)} %copy.40), channel_id=1, source_target_pairs={{1,0},{2,1},{3,2},{4,3},{5,4},{6,5},{7,6},{9,8},{10,9},{11,10},{12... | collective-permute-start | bytes 1474568 | tf_op jit(solution)/shard_map/ppermute | solution.py:17
  401.7 22.9 %collective-permute-start.6 = (f32[15,128,64]{1,2,0:T(8,128)}, f32[15,128,64]{1,2,0:T(8,128)}, u32[]{:S(2)}, u32[]{:S(2)}) collective-permute-start(f32[15,128,64]{1,2,0:T(8,128)} %copy.39), channel_id=1, source_target_pairs={{0,1},{1,2},{2,3},{3,4},{4,5},{5,6},{6,7},{8,9},{9,10},{10,11},{11... | collective-permute-start | bytes 1474568 | tf_op jit(solution)/shard_map/ppermute | solution.py:14
  433.5 298.8 %all-reduce.6.cloned.1.call-start = ((), (), s32[]{:S(2)}) async-start(), calls=%async_computation.3 | async-start | bytes 4194304 | tf_op jit(solution)/shard_map/psum | solution.py:85
  514.6 3.0 copy-start.2
  540.0 87.2 %collective-permute-start.8 = (f32[15,128,256]{2,1,0:T(8,128)S(1)}, f32[15,128,256]{2,1,0:T(8,128)S(1)}, u32[]{:S(2)}, u32[]{:S(2)}) collective-permute-start(f32[15,128,256]{2,1,0:T(8,128)S(1)} %get-tuple-element.5), channel_id=1, source_target_pairs={{0,1},{1,2},{2,3},{3,4},{4,5},{5,6},{6,7},{8,9},{9,10},{10,11},{11... | collective-permute-start | bytes 5898248 | tf_op jit(solution)/shard_map/ppermute | solution.py:14
  543.1 86.6 %collective-permute-start.9 = (f32[15,128,256]{2,1,0:T(8,128)S(1)}, f32[15,128,256]{2,1,0:T(8,128)S(1)}, u32[]{:S(2)}, u32[]{:S(2)}) collective-permute-start(f32[15,128,256]{2,1,0:T(8,128)S(1)} %get-tuple-element.6), channel_id=1, source_target_pairs={{1,0},{2,1},{3,2},{4,3},{5,4},{6,5},{7,6},{9,8},{10,9},{11,10},{12... | collective-permute-start | bytes 5898248 | tf_op jit(solution)/shard_map/ppermute | solution.py:17
Sparse Core Ops, SparseCore 0:
  36.4 45.2 all-gather.2
  340.4 50.5 all-reduce.3
  433.6 45.5 all-gather.4
  682.1 50.2 all-reduce.5
where the time goes:
time: 754 us; the launch traced here: 742 us
  waiting for transfers between devices  388 us (51%)
  matrix products  202 us (27%)
  other arithmetic  61.4 us (8%)
  local copies, waits for them, and re-layouts  44.5 us (6%)
  starting transfers between devices  29.5 us (4%)
  between operations  17.4 us (2%)
    ppermute x5, waiting for transfers between devices, padded_2(): lax.ppermute(lax.slice_in_dim(block, block.shape[dim] - width, None, axis...  180 us
    psum x2, waiting for transfers between devices, shards(): log_total = lax.psum(log_factor, 'view')  101 us
    dot_general x4, matrix products, spread_planes(): jnp.dot(matrix, flat, precision=lax.Precision.HIGHEST, preferred_element_...  101 us
    dot_general x4, matrix products, spread_cross(): return jnp.einsum('xyz,wy->xwz', field, my, precision=lax.Precision.HIGHEST)  89.4 us
    ppermute x5, waiting for transfers between devices, padded_2(): lax.ppermute(lax.slice_in_dim(block, 0, width, axis=dim), axis, backward)  61 us
    all_gather x2, waiting for transfers between devices, shards(): rimmed = lax.all_gather(part_rim, 'view', axis=2, tiled=True)  45.7 us
    add x1, other arithmetic, band_matrix(): total + jnp.where(delta == tap, kern[tap], jnp.zeros((), kern.dtype))  38.9 us
    ppermute x5, starting transfers between devices, padded_2(): lax.ppermute(lax.slice_in_dim(block, block.shape[dim] - width, None, axis...  15.6 us
  transfers between devices with their start and end apart: 14, of which 11 were waited for; matrix products, arithmetic and copies ran while one was open for 8% of the time, Pallas kernels for 0%

commit v1 on v0

v1 whole, which is shorter than its diff:
```python
import functools

import jax
import jax.numpy as jnp
from jax import lax
from jax.experimental import pallas as pl
from jax.experimental.pallas import tpu as pltpu
from jax.sharding import PartitionSpec as P

ITERS = 2
AXES = ("view", "tile")
F32 = jnp.float32
BF16 = jnp.bfloat16
VMEM = pl.BlockSpec(memory_space=pltpu.VMEM)
SMEM = pl.BlockSpec(memory_space=pltpu.SMEM)
PARAMS = pltpu.CompilerParams(vmem_limit_bytes=48 * 1024 * 1024)


def moves(move):
    views, tiles = lax.axis_size("view"), lax.axis_size("tile")
    pairs = []
    for view in range(views):
        for tile in range(tiles):
            target = move(view // 2, view % 2, tile // 2, tile % 2)
            if target is not None:
                g, c, q, r = target
                pairs.append((view * tiles + tile, (2 * g + c) * tiles + 2 * q + r))
    return pairs


def send(array, move):
    return lax.ppermute(array, AXES, moves(move))


def to_next(g, c, q, r):
    s = 2 * q + c + 1
    return (g, s % 2, s // 2, r) if s < lax.axis_size("tile") else None


def to_previous(g, c, q, r):
    s = 2 * q + c - 1
    return (g, s % 2, s // 2, r) if s >= 0 else None


def to_row_partner(g, c, q, r):
    return (g, c, q, 1 - r)


def to_core_partner(g, c, q, r):
    return (g, 1 - c, q, r)


def split(x):
    high = x.astype(BF16)
    return high, (x - high.astype(F32)).astype(BF16)


def dot(a, b):
    return jnp.dot(a, b, preferred_element_type=F32)


def tables_kernel(half_ref, taps_ref, y_ref, zhi_ref, zlo_ref, *, rows, halo, radius_y, radius_z):
    lanes = taps_ref.shape[1]
    width = rows + halo
    half = half_ref[0]
    lane = lax.broadcasted_iota(jnp.int32, (rows, lanes), 1)
    for index in range(4):
        base = pltpu.roll(taps_ref[index:index + 1, :], lanes - radius_y, 1)
        band = pltpu.roll(jnp.broadcast_to(base, (rows, lanes)), 0, 1, stride=1, stride_axis=0)
        beyond = jnp.where(half == 1, pltpu.roll(band, width, 1), band)
        band = jnp.where(lane < rows, band, jnp.where(lane < width, beyond, jnp.zeros_like(band)))
        high, low = split(band)
        high, low = high.astype(F32), low.astype(F32)
        row = high + pltpu.roll(high, width, 1) + pltpu.roll(low, 2 * width, 1)
        y_ref[index] = row.astype(BF16)
    lane = lax.broadcasted_iota(jnp.int32, (lanes, lanes), 1)
    row = lax.broadcasted_iota(jnp.int32, (lanes, lanes), 0)
    near = jnp.abs(lane - row) <= radius_z
    for index in range(4):
        base = pltpu.roll(taps_ref[4 + index:5 + index, :], lanes - radius_z, 1)
        band = pltpu.roll(jnp.broadcast_to(base, (lanes, lanes)), 0, 1, stride=1, stride_axis=0)
        high, low = split(jnp.where(near, band, jnp.zeros_like(band)))
        zhi_ref[index] = high
        zlo_ref[index] = low


def make_tables(half, taps, rows, halo, radius_y, radius_z):
    lanes = taps.shape[1]
    kernel = functools.partial(tables_kernel, rows=rows, halo=halo, radius_y=radius_y, radius_z=radius_z)
    return pl.pallas_call(
        kernel,
        out_shape=(
            jax.ShapeDtypeStruct((4, rows, lanes), BF16),
            jax.ShapeDtypeStruct((4, lanes, lanes), BF16),
            jax.ShapeDtypeStruct((4, lanes, lanes), BF16),
        ),
        in_specs=[SMEM, VMEM],
        out_specs=(VMEM, VMEM, VMEM),
        compiler_params=PARAMS,
        name="band_matrices",
    )(half, taps)


def shift_kernel(scal_ref, acq_ref, mask_ref, first_ref, second_ref):
    planes, cells_y, cells_z = acq_ref.shape
    rows = cells_y // 2
    shift_y, shift_z, core = scal_ref[0], scal_ref[1], scal_ref[2]
    row = lax.broadcasted_iota(jnp.int32, (cells_y, cells_z), 0) + shift_y
    col = lax.broadcasted_iota(jnp.int32, (cells_y, cells_z), 1) + shift_z
    inside = (row >= 0) & (row < cells_y) & (col >= 0) & (col < cells_z)
    turn_y = lax.rem(cells_y - shift_y, cells_y)
    turn_z = lax.rem(cells_z - shift_z, cells_z)

    def body(p, carry):
        x = acq_ref[p]
        x = pltpu.roll(x, turn_z, 1)
        x = pltpu.roll(x, turn_y, 0)
        x = jnp.where(inside, x, jnp.zeros_like(x))
        low, high = x[:rows], x[rows:]
        first_ref[p] = jnp.where(core == 0, low, high)
        second_ref[p] = jnp.where(core == 0, high, low)
        return carry

    lax.fori_loop(0, planes, body, 0)
    mask = mask_ref[...].astype(F32)
    turned = pltpu.roll(mask, rows, 1)
    first_ref[planes] = jnp.zeros((rows, cells_z), F32)
    second_ref[planes] = jnp.zeros((rows, cells_z), F32)
    first_ref[planes, :planes, :cells_y] = jnp.where(core == 0, mask, turned)
    second_ref[planes, :planes, :cells_y] = jnp.where(core == 0, turned, mask)


def shift_and_cut(scal, acquired, mask):
    planes, cells_y, cells_z = acquired.shape
    shape = jax.ShapeDtypeStruct((planes + 1, cells_y // 2, cells_z), F32)
    return pl.pallas_call(
        shift_kernel,
        out_shape=(shape, shape),
        in_specs=[SMEM, VMEM, VMEM],
        out_specs=(VMEM, VMEM),
        compiler_params=PARAMS,
        name="shift_recorded",
    )(scal, acquired, mask)


def image_kernel(shift_ref, place_ref, *refs, extent_x, cells_y):
    blocks, out_ref = (refs[:3], refs[3:6]), refs[6]
    _, planes, rows, cells_z = out_ref.shape
    slab, half = place_ref[0], place_ref[1]
    eye = lax.broadcasted_iota(jnp.int32, (rows, rows), 0) == lax.broadcasted_iota(jnp.int32, (rows, rows), 1)
    eye = eye.astype(F32).astype(BF16)
    for order, (low_ref, own_ref, high_ref) in enumerate(blocks):
        view = half if order == 0 else 1 - half
        shift_x, shift_y, shift_z = (shift_ref[view, i] for i in range(3))
        mask = own_ref[planes, :planes, :rows].astype(BF16)
        columns = lax.dot_general(eye, mask, (((1,), (1,)), ((), ())), preferred_element_type=F32)
        row = lax.broadcasted_iota(jnp.int32, (rows, cells_z), 0) + shift_y + half * rows
        col = lax.broadcasted_iota(jnp.int32, (rows, cells_z), 1) + shift_z
        inside = (row >= 0) & (row < cells_y) & (col >= 0) & (col < cells_z)
        for p in range(planes):
            source = p + shift_x
            x = slab * planes + source
            own = own_ref[jnp.clip(source, 0, planes - 1)]
            low = low_ref[jnp.clip(source + planes, 0, planes - 1)]
            high = high_ref[jnp.clip(source - planes, 0, planes - 1)]
            value = jnp.where(source < 0, low, jnp.where(source < planes, own, high))
            weight = jnp.broadcast_to(columns[:, p:p + 1], (rows, cells_z))
            covered = inside & (weight > 0.5) & (x >= 0) & (x < extent_x)
            out_ref[view, p] = jnp.where(covered, value, jnp.full_like(value, -1.0))


def make_images(shifts, place, first, second, extent_x, cells_y):
    return pl.pallas_call(
        functools.partial(image_kernel, extent_x=extent_x, cells_y=cells_y),
        out_shape=jax.ShapeDtypeStruct((2,) + first[0].shape, F32),
        in_specs=[SMEM, SMEM] + [VMEM] * 6,
        out_specs=VMEM,
        compiler_params=PARAMS,
        name="images",
    )(shifts, place, *first, *second)


def spread_x(kx_ref, view, refs, store, rows, lanes, adjoint):
    low_ref, own_ref, high_ref = refs
    radius, planes = low_ref.shape[0], own_ref.shape[0]
    count = 2 * radius + 1
    parts = [(low_ref, i) for i in range(radius)] + [(own_ref, i) for i in range(planes)]
    parts += [(high_ref, i) for i in range(radius)]
    taps = [kx_ref[view, count - 1 - a if adjoint else a] for a in range(count)]

    def body(step, carry):
        row = pl.multiple_of(step * 8, 8)
        for column in range(0, lanes, 128):
            total = [None] * planes
            for i, (ref, index) in enumerate(parts):
                x = ref[index, pl.ds(row, 8), column:column + 128]
                for o in range(max(0, i - count + 1), min(planes - 1, i) + 1):
                    term = taps[i - o] * x
                    total[o] = term if total[o] is None else total[o] + term
            for o in range(planes):
                store(o, row, column, total[o])
        return carry

    lax.fori_loop(0, rows // 8, body, 0)


def spread_yz(fetch, y_ref, zhi_ref, zlo_ref, view, planes, width, lanes, store):
    band = y_ref[view]
    rest = band.shape[1] - 3 * width
    group = 4
    for start in range(0, planes, group):
        spread = []
        for p in range(start, min(start + group, planes)):
            high, low = split(fetch(p))
            parts = [high, low, high]
            if rest:
                parts.append(jnp.zeros((rest, lanes), BF16))
            spread.append(dot(band, jnp.concatenate(parts, axis=0)))
        high, low = split(jnp.concatenate(spread, axis=0))
        out = dot(high, zhi_ref[view]) + (dot(low, zhi_ref[view]) + dot(high, zlo_ref[view]))
        rows = band.shape[0]
        for index in range(len(spread)):
            store(start + index, out[index * rows:(index + 1) * rows])


def ratio_kernel(kx_ref, low_ref, own_ref, high_ref, image_ref, y_ref, zhi_ref, zlo_ref, ratio_ref, edge_ref, wide_ref, *, view):
    planes, rows, lanes = ratio_ref.shape
    width = own_ref.shape[1]
    halo = width - rows

    def store(o, row, column, value):
        wide_ref[o, pl.ds(row, 8), column:column + 128] = value

    spread_x(kx_ref, view, (low_ref, own_ref, high_ref), store, width, lanes, False)

    def finish(p, blurred):
        image = image_ref[0, p]
        ratio = jnp.where(image >= 0, image / blurred, jnp.ones_like(image))
        ratio_ref[p] = ratio
        edge_ref[0, p] = ratio[:halo]
        edge_ref[1, p] = ratio[rows - halo:]

    spread_yz(lambda p: wide_ref[p], y_ref, zhi_ref, zlo_ref, view, planes, width, lanes, finish)


def make_ratio(kx, low, own, high, images, tables, view):
    _, planes, rows, lanes = images.shape
    width = own.shape[1]
    return pl.pallas_call(
        functools.partial(ratio_kernel, view=view),
        out_shape=(
            jax.ShapeDtypeStruct(images.shape[1:], F32),
            jax.ShapeDtypeStruct((2, planes, width - rows, lanes), F32),
        ),
        grid=(1,),
        in_specs=[SMEM] + [VMEM] * 3 + [pl.BlockSpec((1, planes, rows, lanes), lambda i: (view, 0, 0, 0))] + [VMEM] * 3,
        out_specs=(VMEM, VMEM),
        scratch_shapes=[pltpu.VMEM((planes, width, lanes), F32)],
        compiler_params=PARAMS,
        name="ratio",
    )(kx, low, own, high, images, *tables)


def spread_kernel(ratio_ref, halo_ref, y_ref, zhi_ref, zlo_ref, out_ref, lower_ref, upper_ref, *, view):
    planes, rows, lanes = out_ref.shape
    width = rows + halo_ref.shape[1]
    radius = lower_ref.shape[0]

    def store(p, value):
        out_ref[p] = value
        if p < radius:
            lower_ref[p] = value
        if p >= planes - radius:
            upper_ref[p - planes + radius] = value

    spread_yz(
        lambda p: jnp.concatenate([ratio_ref[p], halo_ref[p]], axis=0),
        y_ref, zhi_ref, zlo_ref, 2 + view, planes, width, lanes, store,
    )


def make_spread(ratio, halo, tables, view, radius):
    planes, rows, lanes = ratio.shape
    edge = jax.ShapeDtypeStruct((radius, rows, lanes), F32)
    return pl.pallas_call(
        functools.partial(spread_kernel, view=view),
        out_shape=(jax.ShapeDtypeStruct(ratio.shape, F32), edge, edge),
        in_specs=[VMEM] * 5,
        out_specs=(VMEM, VMEM, VMEM),
        compiler_params=PARAMS,
        name="adjoint_yz",
    )(ratio, halo, *tables)


def factor_kernel(kx_ref, low0, own0, high0, low1, own1, high1, out_ref):
    planes, rows, lanes = out_ref.shape

    def first(o, row, column, value):
        out_ref[o, pl.ds(row, 8), column:column + 128] = jnp.log(value)

    def second(o, row, column, value):
        place = (o, pl.ds(row, 8), slice(column, column + 128))
        out_ref[place] = out_ref[place] + jnp.log(value)

    spread_x(kx_ref, 0, (low0, own0, high0), first, rows, lanes, True)
    spread_x(kx_ref, 1, (low1, own1, high1), second, rows, lanes, True)


def make_factor(kx, view0, view1):
    return pl.pallas_call(
        factor_kernel,
        out_shape=jax.ShapeDtypeStruct(view0[1].shape, F32),
        in_specs=[SMEM] + [VMEM] * 6,
        out_specs=VMEM,
        compiler_params=PARAMS,
        name="log_factor",
    )(kx, *view0, *view1)


def shards(acquired, estimate, offsets, view_mask, kern_x, kern_y, kern_z):
    planes, cells_y, cells_z = estimate.shape
    views, slabs = lax.axis_size("view"), lax.axis_size("tile")
    groups = views // 2
    rows = cells_y // 2
    taps_x, taps_y, taps_z = kern_x.shape[1], kern_y.shape[1], kern_z.shape[1]
    radius = taps_x // 2
    halo = -(-(taps_y // 2) // 16) * 16
    core = lax.rem(lax.axis_index("view"), 2)
    half = lax.rem(lax.axis_index("tile"), 2)
    slab = lax.axis_index("tile") - half + core
    straight = core == half

    mine = jnp.concatenate([kern_x[0], kern_y[0], kern_z[0], offsets[0].astype(F32)])
    other = send(mine, to_core_partner)
    both = jnp.where(core == 0, jnp.stack([mine, other]), jnp.stack([other, mine]))
    kx = both[:, :taps_x]
    ky = both[:, taps_x:taps_x + taps_y]
    kz = both[:, taps_x + taps_y:taps_x + taps_y + taps_z]
    shifts = both[:, taps_x + taps_y + taps_z:].astype(jnp.int32)
    pad_y = ((0, 0), (0, cells_z - taps_y))
    pad_z = ((0, 0), (0, cells_z - taps_z))
    taps = jnp.concatenate(
        [jnp.pad(ky, pad_y), jnp.pad(ky[:, ::-1], pad_y), jnp.pad(kz[:, ::-1], pad_z), jnp.pad(kz, pad_z)]
    )
    tables = make_tables(half.reshape(1), taps, rows, halo, taps_y // 2, taps_z // 2)

    def widen(array, side):
        own = lax.dynamic_slice_in_dim(array, side * rows, rows, 1)
        edge = lax.dynamic_slice_in_dim(array, rows - side * halo, halo, 1)
        return jnp.concatenate([own, edge], axis=1)

    crossing = send(widen(estimate, 1 - half), lambda g, c, q, r: (g, c, q, 1 - r) if c == r else None)
    current = jnp.where(straight, widen(estimate, half), crossing)

    scal = jnp.stack([offsets[0, 1], offsets[0, 2], core])
    first, second = shift_and_cut(scal, acquired[0], view_mask[0])
    first = send(first, lambda g, c, q, r: (g, r, q, c))
    second = send(second, lambda g, c, q, r: (g, r, q, 1 - c))
    first, second = (
        (send(block[:planes], to_next), block, send(block[:planes], to_previous)) for block in (first, second)
    )
    place = jnp.stack([slab, half])
    images = make_images(shifts, place, first, second, planes * slabs, cells_y)

    for step in range(ITERS):
        low = send(current[planes - radius:], to_next)
        high = send(current[:radius], to_previous)
        sides = []
        for view in range(2):
            ratio, edges = make_ratio(kx, low, current, high, images, tables, view)
            edge = lax.dynamic_index_in_dim(edges, 1 - half, 0, keepdims=False)
            beyond = send(edge, to_row_partner)
            spread, lower, upper = make_spread(ratio, beyond, tables, view, radius)
            sides.append((send(upper, to_next), spread, send(lower, to_previous)))
        total = make_factor(kx, *sides)
        summed = total
        for turn in range(1, groups):
            summed = summed + send(total, lambda g, c, q, r: ((g + turn) % groups, c, q, r))
        own = current[:, :rows] * jnp.exp(summed)
        if step < ITERS - 1:
            edge = lax.dynamic_slice_in_dim(own, (rows - halo) * (1 - half), halo, 1)
            current = jnp.concatenate([own, send(edge, to_row_partner)], axis=1)

    crossed = send(own, lambda g, c, q, r: (g, c, q, 1 - r) if c != r else None)
    low_rows = jnp.where(half == 0, own, crossed)
    high_rows = jnp.where(half == 0, crossed, own)
    whole = jnp.concatenate([low_rows, high_rows], axis=1)
    copied = send(whole, lambda g, c, q, r: (g, 1 - c, q, r) if c == r else None)
    return jnp.where(straight, whole, copied)


def solution(mesh):
    in_specs = (
        P("view", "tile", None, None),
        P("tile", None, None),
        P("view", None),
        P("view", "tile", None),
        P("view", None),
        P("view", None),
        P("view", None),
    )
    out_specs = P("tile", None, None)
    return jax.shard_map(shards, mesh=mesh, in_specs=in_specs, out_specs=out_specs, check_vma=False)
```

time: 754 us -> 301 us (0.40); the launches traced: 742 us -> 300 us
  waiting for transfers between devices: 388 us -> 164 us
  matrix products: 202 us -> 0 us
  other arithmetic: 61.4 us -> 9.3 us
  Pallas kernels: 0 us -> 48.7 us
  starting transfers between devices: 29.5 us -> 63.5 us
  local copies, waits for them, and re-layouts: 44.5 us -> 14 us
  between operations: 17.4 us -> 0.55 us
    dot_general x12 -> x0, matrix products: 202 us -> none  [the longest x4 101 us: spread_planes(): jnp.dot(matrix, flat, precision=lax.Precision.HIGHEST, preferred_element_...]
    psum x2 -> x0, waiting for transfers between devices: 101 us -> none  [shards(): log_total = lax.psum(log_factor, 'view')]
    ppermute x10 -> x29, waiting for transfers between devices: 241 us -> 164 us  [send(): return lax.ppermute(array, AXES, moves(move))]
    pallas_call x0 -> x13, Pallas kernels: none -> 48.7 us  [the longest x4 22.8 us: make_ratio(): pl.pallas_call(functools.partial(ratio_kernel, view=view), out_shape=(jax...]
    all_gather x2 -> x0, waiting for transfers between devices: 45.7 us -> none  [shards(): rimmed = lax.all_gather(part_rim, 'view', axis=2, tiled=True)]
    add x1 -> x0, other arithmetic: 38.9 us -> none  [band_matrix(): total + jnp.where(delta == tap, kern[tap], jnp.zeros((), kern.dtype))]
    ppermute x10 -> x29, starting transfers between devices: 29.4 us -> 63.5 us  [send(): return lax.ppermute(array, AXES, moves(move))]
    all_gather x2 -> x0, local copies, waits for them, and re-layouts: 13.8 us -> none  [shards(): rimmed = lax.all_gather(part_rim, 'view', axis=2, tiled=True)]
  transfers between devices with their start and end apart: 14 -> 29, of which waited for: 11 -> 19; matrix products, arithmetic and copies ran while one was open for 8% -> 4% of each run, Pallas kernels for 0% -> 8%
where the time goes in v1:
time: 301 us; the launch traced here: 300 us
  waiting for transfers between devices  164 us (54%)
  starting transfers between devices  63.5 us (21%)
  Pallas kernels  48.7 us (16%)
  local copies, waits for them, and re-layouts  14 us (5%)
  other arithmetic  9.3 us (3%)
    ppermute x29, waiting for transfers between devices, send(): return lax.ppermute(array, AXES, moves(move))  164 us
    ppermute x29, starting transfers between devices, send(): return lax.ppermute(array, AXES, moves(move))  63.5 us
    pallas_call x4, Pallas kernels, make_ratio(): pl.pallas_call(functools.partial(ratio_kernel, view=view), out_shape=(jax...  22.8 us
    pallas_call x2, Pallas kernels, make_factor(): pl.pallas_call(factor_kernel, out_shape=jax.ShapeDtypeStruct(view0[1].sha...  12.6 us
  transfers between devices with their start and end apart: 29, of which 19 were waited for; matrix products, arithmetic and copies ran while one was open for 4% of the time, Pallas kernels for 8%

profile of v1, /device:TPU:17, one launch (start us, length us, event | category | flops | bytes accessed | tf_op | source)
XLA Modules:
  0.0 299.7 jit_solution(14619567966606663610)
XLA Ops:
  0.0 1.8 constant_dynamic-slice_fusion.3
  1.8 1.7 constant_dynamic-slice_fusion.4
  7.9 4.1 %shift_recorded.1 = (f32[17,64,256]{2,1,0:T(8,128)S(1)}, f32[17,64,256]{2,1,0:T(8,128)}) custom-call(s32[3]{0:T(128)S(1)} %pad_add_fusion.1.scal_ref, f32[16,128,256]{2,1,0:T(8,128)S(1)} %bitcast.22, s32[16,128]{1,0:T(8,128)S(1)} %bitcast.23), custom_call_target="tpu_custom_call" | custom-call | tf_op jit(solution)/shard_map/shift_recorded/pallas_call | solution.py:136
  11.9 3.7 %collective-permute-start.4 = (f32[17,64,256]{2,1,0:T(8,128)S(1)}, f32[17,64,256]{2,1,0:T(8,128)S(1)}, u32[]{:S(2)}, u32[]{:S(2)}) collective-permute-start(f32[17,64,256]{2,1,0:T(8,128)S(1)} %get-tuple-element.30), channel_id=1, source_target_pairs={{0,0},{1,8},{2,2},{3,10},{4,4},{5,12},{6,6},{7,14},{8,1},{9,9},{10... | collective-permute-start | bytes 3342344 | tf_op jit(solution)/shard_map/ppermute | solution.py:32
  16.6 24.2 %collective-permute-done.4.refs_1_ = f32[17,64,256]{2,1,0:T(8,128)S(1)} collective-permute-done((f32[17,64,256]{2,1,0:T(8,128)S(1)}, f32[17,64,256]{2,1,0:T(8,128)S(1)}, u32[]{:S(2)}, u32[]{:S(2)}) %collective-permute-start.4) | collective-permute-done | bytes 1114144 | tf_op jit(solution)/shard_map/ppermute | solution.py:32
  41.9 1.9 collective-permute-start.6
  45.4 1.9 fusion.4
  47.2 2.1 collective-permute-start.3
  49.3 3.5 %collective-permute-start.2 = (f32[15,80,256]{2,1,0:T(8,128)}, f32[15,80,256]{2,1,0:T(8,128)}, u32[]{:S(2)}, u32[]{:S(2)}) collective-permute-start(f32[15,80,256]{2,1,0:T(8,128)} %get-tuple-element.64), channel_id=1, source_target_pairs={{0,8},{1,9},{2,10},{3,11},{4,12},{5,13},{6,14},{7,15},{8,2},{9,3},... | collective-permute-start | bytes 3686408 | tf_op jit(solution)/shard_map/ppermute | solution.py:32
  52.9 2.1 collective-permute-start.5
  55.0 2.3 slice.58
  57.4 2.2 collective-permute-start.9
  60.6 3.3 %collective-permute-start.8 = (f32[16,64,256]{2,1,0:T(8,128)}, f32[16,64,256]{2,1,0:T(8,128)}, u32[]{:S(2)}, u32[]{:S(2)}) collective-permute-start(f32[16,64,256]{2,1,0:T(8,128)} %slice.58), channel_id=1, source_target_pairs={{0,8},{1,9},{2,10},{3,11},{4,12},{5,13},{6,14},{7,15},{8,2},{9,3},... | collective-permute-start | bytes 3145736 | tf_op jit(solution)/shard_map/ppermute | solution.py:32
  65.3 12.7 %collective-permute-done.5.refs_0_ = f32[16,64,256]{2,1,0:T(8,128)} collective-permute-done((f32[16,64,256]{2,1,0:T(8,128)}, f32[16,64,256]{2,1,0:T(8,128)}, u32[]{:S(2)}, u32[]{:S(2)}) %collective-permute-start.5) | collective-permute-done | bytes 1048608 | tf_op jit(solution)/shard_map/ppermute | solution.py:32
  78.0 5.0 %collective-permute-done.9.refs_5_ = f32[16,64,256]{2,1,0:T(8,128)} collective-permute-done((f32[16,64,256]{2,1,0:T(8,128)}, f32[16,64,256]{2,1,0:T(8,128)}, u32[]{:S(2)}, u32[]{:S(2)}) %collective-permute-start.9) | collective-permute-done | bytes 1048608 | tf_op jit(solution)/shard_map/ppermute | solution.py:32
  83.0 6.2 %collective-permute-done.8.refs_3_ = f32[16,64,256]{2,1,0:T(8,128)} collective-permute-done((f32[16,64,256]{2,1,0:T(8,128)}, f32[16,64,256]{2,1,0:T(8,128)}, u32[]{:S(2)}, u32[]{:S(2)}) %collective-permute-start.8) | collective-permute-done | bytes 1048608 | tf_op jit(solution)/shard_map/ppermute | solution.py:32
  90.5 4.4 %images.1.image_ref = f32[2,16,64,256]{3,2,1,0:T(8,128)} custom-call(s32[2,3]{1,0:T(2,128)S(1)} %slice_convert_fusion.shift_ref, s32[2]{0:T(128)S(1)} %pad_add_fusion.place_ref, f32[16,64,256]{2,1,0:T(8,128)} %collective-permute-done.5.refs_0_, f32[17,64,256]{2,1,0:T(8,128)S(1)} %collective-permute-done.4.refs_1_, f32[16,64,256]{2,1,0:T(8,128)S(1)} %copy-done.2, ...), custom_call_target="tpu_custom_call" | custom-call | tf_op jit(solution)/shard_map/images/pallas_call | solution.py:173
  94.8 5.9 %ratio.5 = (f32[16,64,256]{2,1,0:T(8,128)S(1)}, f32[2,16,16,256]{3,2,1,0:T(8,128)S(1)}) custom-call(f32[2,31]{1,0:T(2,128)S(1)} %get-tuple-element.66.kx_ref, f32[15,80,256]{2,1,0:T(8,128)} %collective-permute-done.2.low_ref, f32[16,80,256]{2,1,0:T(8,128)} %copy-done.6, f32[15,80,256]{2,1,0:T(8,128)S(1)} %collective-permute-done.3.high_ref, ...), custom_call_target="tpu_custom_call" | custom-call | tf_op jit(solution)/shard_map/ratio/pallas_call | solution.py:249
  102.3 5.9 %ratio.4 = (f32[16,64,256]{2,1,0:T(8,128)S(1)}, f32[2,16,16,256]{3,2,1,0:T(8,128)S(1)}) custom-call(f32[2,31]{1,0:T(2,128)S(1)} %get-tuple-element.66.kx_ref, f32[15,80,256]{2,1,0:T(8,128)} %collective-permute-done.2.low_ref, f32[16,80,256]{2,1,0:T(8,128)} %copy-done.6, f32[15,80,256]{2,1,0:T(8,128)S(1)} %collective-permute-done.3.high_ref, ...), custom_call_target="tpu_custom_call" | custom-call | tf_op jit(solution)/shard_map/ratio/pallas_call | solution.py:249
  110.4 4.9 %collective-permute-start.14 = (f32[15,64,256]{2,1,0:T(8,128)S(1)}, f32[15,64,256]{2,1,0:T(8,128)S(1)}, u32[]{:S(2)}, u32[]{:S(2)}) collective-permute-start(f32[15,64,256]{2,1,0:T(8,128)S(1)} %get-tuple-element.42), channel_id=1, source_target_pairs={{0,8},{1,9},{2,10},{3,11},{4,12},{5,13},{6,14},{7,15},{8,2},{9,3},... | collective-permute-start | bytes 2949128 | tf_op jit(solution)/shard_map/ppermute | solution.py:32
  115.3 1.9 collective-permute-start.15
  118.2 3.6 %collective-permute-start.11 = (f32[15,64,256]{2,1,0:T(8,128)S(1)}, f32[15,64,256]{2,1,0:T(8,128)S(1)}, u32[]{:S(2)}, u32[]{:S(2)}) collective-permute-start(f32[15,64,256]{2,1,0:T(8,128)S(1)} %get-tuple-element.37), channel_id=1, source_target_pairs={{0,8},{1,9},{2,10},{3,11},{4,12},{5,13},{6,14},{7,15},{8,2},{9,3},... | collective-permute-start | bytes 2949128 | tf_op jit(solution)/shard_map/ppermute | solution.py:32
  121.9 1.9 collective-permute-start.12
  123.8 2.5 collective-permute-done.14.low1
  126.3 4.7 %collective-permute-done.15.high1 = f32[15,64,256]{2,1,0:T(8,128)S(1)} collective-permute-done((f32[15,64,256]{2,1,0:T(8,128)S(1)}, f32[15,64,256]{2,1,0:T(8,128)S(1)}, u32[]{:S(2)}, u32[]{:S(2)}) %collective-permute-start.15) | collective-permute-done | bytes 983072 | tf_op jit(solution)/shard_map/ppermute | solution.py:32
  131.0 5.8 %collective-permute-done.11.low0 = f32[15,64,256]{2,1,0:T(8,128)S(1)} collective-permute-done((f32[15,64,256]{2,1,0:T(8,128)S(1)}, f32[15,64,256]{2,1,0:T(8,128)S(1)}, u32[]{:S(2)}, u32[]{:S(2)}) %collective-permute-start.11) | collective-permute-done | bytes 983072 | tf_op jit(solution)/shard_map/ppermute | solution.py:32
  136.9 4.4 %collective-permute-done.12.high0 = f32[15,64,256]{2,1,0:T(8,128)S(1)} collective-permute-done((f32[15,64,256]{2,1,0:T(8,128)S(1)}, f32[15,64,256]{2,1,0:T(8,128)S(1)}, u32[]{:S(2)}, u32[]{:S(2)}) %collective-permute-start.12) | collective-permute-done | bytes 983072 | tf_op jit(solution)/shard_map/ppermute | solution.py:32
  141.3 6.4 %log_factor.2 = f32[16,64,256]{2,1,0:T(8,128)S(1)} custom-call(f32[2,31]{1,0:T(2,128)S(1)} %get-tuple-element.66.kx_ref, f32[15,64,256]{2,1,0:T(8,128)S(1)} %collective-permute-done.11.low0, f32[16,64,256]{2,1,0:T(8,128)S(1)} %get-tuple-element.38.own0, f32[15,64,256]{2,1,0:T(8,128)S(1)} %collective-permute-done.12.high0, ...), custom_call_target="tpu_custom_call" | custom-call | tf_op jit(solution)/shard_map/log_factor/pallas_call | solution.py:310
  148.9 22.9 %collective-permute-done.16 = f32[16,64,256]{2,1,0:T(8,128)} collective-permute-done((f32[16,64,256]{2,1,0:T(8,128)S(1)}, f32[16,64,256]{2,1,0:T(8,128)}, u32[]{:S(2)}, u32[]{:S(2)}) %collective-permute-start.16) | collective-permute-done | bytes 1048608 | tf_op jit(solution)/shard_map/ppermute | solution.py:32
  174.8 6.6 %collective-permute-done.17 = f32[16,16,256]{2,1,0:T(8,128)S(1)} collective-permute-done((f32[16,16,256]{2,1,0:T(8,128)S(1)}, f32[16,16,256]{2,1,0:T(8,128)S(1)}, u32[]{:S(2)}, u32[]{:S(2)}) %collective-permute-start.17) | collective-permute-done | bytes 262176 | tf_op jit(solution)/shard_map/ppermute | solution.py:32
  181.7 2.6 collective-permute-start.19
  184.3 3.2 %collective-permute-start.18 = (f32[15,80,256]{2,1,0:T(8,128)S(1)}, f32[15,80,256]{2,1,0:T(8,128)S(1)}, u32[]{:S(2)}, u32[]{:S(2)}) collective-permute-start(f32[15,80,256]{2,1,0:T(8,128)S(1)} %get-tuple-element.62), channel_id=1, source_target_pairs={{0,8},{1,9},{2,10},{3,11},{4,12},{5,13},{6,14},{7,15},{8,2},{9,3},... | collective-permute-start | bytes 3686408 | tf_op jit(solution)/shard_map/ppermute | solution.py:32
  188.7 11.4 %collective-permute-done.19.high_ref = f32[15,80,256]{2,1,0:T(8,128)S(1)} collective-permute-done((f32[15,80,256]{2,1,0:T(8,128)S(1)}, f32[15,80,256]{2,1,0:T(8,128)S(1)}, u32[]{:S(2)}, u32[]{:S(2)}) %collective-permute-start.19) | collective-permute-done | bytes 1228832 | tf_op jit(solution)/shard_map/ppermute | solution.py:32
  200.9 5.5 %ratio.6 = (f32[16,64,256]{2,1,0:T(8,128)S(1)}, f32[2,16,16,256]{3,2,1,0:T(8,128)S(1)}) custom-call(f32[2,31]{1,0:T(2,128)S(1)} %get-tuple-element.66.kx_ref, f32[15,80,256]{2,1,0:T(8,128)S(1)} %collective-permute-done.18.low_ref, f32[16,80,256]{2,1,0:T(8,128)} %pad_maximum_fusion.own_ref, f32[15,80,256]{2,1,0:T(8,128)S(1)} %collective-permute-done.19.high_ref, ...), custom_call_target="tpu_custom_call" | custom-call | tf_op jit(solution)/shard_map/ratio/pallas_call | solution.py:249
  208.0 5.5 %ratio.7 = (f32[16,64,256]{2,1,0:T(8,128)S(1)}, f32[2,16,16,256]{3,2,1,0:T(8,128)S(1)}) custom-call(f32[2,31]{1,0:T(2,128)S(1)} %get-tuple-element.66.kx_ref, f32[15,80,256]{2,1,0:T(8,128)S(1)} %collective-permute-done.18.low_ref, f32[16,80,256]{2,1,0:T(8,128)} %pad_maximum_fusion.own_ref, f32[15,80,256]{2,1,0:T(8,128)S(1)} %collective-permute-done.19.high_ref, ...), custom_call_target="tpu_custom_call" | custom-call | tf_op jit(solution)/shard_map/ratio/pallas_call | solution.py:249
  214.6 4.9 %collective-permute-start.21 = (f32[15,64,256]{2,1,0:T(8,128)S(1)}, f32[15,64,256]{2,1,0:T(8,128)S(1)}, u32[]{:S(2)}, u32[]{:S(2)}) collective-permute-start(f32[15,64,256]{2,1,0:T(8,128)S(1)} %get-tuple-element.47), channel_id=1, source_target_pairs={{0,8},{1,9},{2,10},{3,11},{4,12},{5,13},{6,14},{7,15},{8,2},{9,3},... | collective-permute-start | bytes 2949128 | tf_op jit(solution)/shard_map/ppermute | solution.py:32
  219.5 1.9 collective-permute-start.22
  223.4 3.6 %collective-permute-start.24 = (f32[15,64,256]{2,1,0:T(8,128)S(1)}, f32[15,64,256]{2,1,0:T(8,128)S(1)}, u32[]{:S(2)}, u32[]{:S(2)}) collective-permute-start(f32[15,64,256]{2,1,0:T(8,128)S(1)} %get-tuple-element.52), channel_id=1, source_target_pairs={{0,8},{1,9},{2,10},{3,11},{4,12},{5,13},{6,14},{7,15},{8,2},{9,3},... | collective-permute-start | bytes 2949128 | tf_op jit(solution)/shard_map/ppermute | solution.py:32
  227.1 1.9 collective-permute-start.25
  230.6 4.7 %collective-permute-done.22.high0 = f32[15,64,256]{2,1,0:T(8,128)S(1)} collective-permute-done((f32[15,64,256]{2,1,0:T(8,128)S(1)}, f32[15,64,256]{2,1,0:T(8,128)S(1)}, u32[]{:S(2)}, u32[]{:S(2)}) %collective-permute-start.22) | collective-permute-done | bytes 983072 | tf_op jit(solution)/shard_map/ppermute | solution.py:32
  235.3 5.8 %collective-permute-done.24.low1 = f32[15,64,256]{2,1,0:T(8,128)S(1)} collective-permute-done((f32[15,64,256]{2,1,0:T(8,128)S(1)}, f32[15,64,256]{2,1,0:T(8,128)S(1)}, u32[]{:S(2)}, u32[]{:S(2)}) %collective-permute-start.24) | collective-permute-done | bytes 983072 | tf_op jit(solution)/shard_map/ppermute | solution.py:32
  241.1 4.4 %collective-permute-done.25.high1 = f32[15,64,256]{2,1,0:T(8,128)S(1)} collective-permute-done((f32[15,64,256]{2,1,0:T(8,128)S(1)}, f32[15,64,256]{2,1,0:T(8,128)S(1)}, u32[]{:S(2)}, u32[]{:S(2)}) %collective-permute-start.25) | collective-permute-done | bytes 983072 | tf_op jit(solution)/shard_map/ppermute | solution.py:32
  245.5 6.3 %log_factor.3 = f32[16,64,256]{2,1,0:T(8,128)S(1)} custom-call(f32[2,31]{1,0:T(2,128)S(1)} %get-tuple-element.66.kx_ref, f32[15,64,256]{2,1,0:T(8,128)S(1)} %collective-permute-done.21.low0, f32[16,64,256]{2,1,0:T(8,128)S(1)} %get-tuple-element.48.own0, f32[15,64,256]{2,1,0:T(8,128)S(1)} %collective-permute-done.22.high0, ...), custom_call_target="tpu_custom_call" | custom-call | tf_op jit(solution)/shard_map/log_factor/pallas_call | solution.py:310
  253.0 22.9 %collective-permute-done.26 = f32[16,64,256]{2,1,0:T(8,128)S(1)} collective-permute-done((f32[16,64,256]{2,1,0:T(8,128)S(1)}, f32[16,64,256]{2,1,0:T(8,128)S(1)}, u32[]{:S(2)}, u32[]{:S(2)}) %collective-permute-start.26) | collective-permute-done | bytes 1048608 | tf_op jit(solution)/shard_map/ppermute | solution.py:32
  276.2 3.4 %collective-permute-start.27 = (f32[16,64,256]{2,1,0:T(8,128)S(1)}, f32[16,64,256]{2,1,0:T(8,128)S(1)}, u32[]{:S(2)}, u32[]{:S(2)}) collective-permute-start(f32[16,64,256]{2,1,0:T(8,128)S(1)} %exponential_multiply_fusion), channel_id=1, source_target_pairs={{1,0},{3,2},{5,4},{7,6},{8,9},{10,11},{12,13},{14,15},{17,16},{19,... | collective-permute-start | bytes 3145736 | tf_op jit(solution)/shard_map/ppermute | solution.py:32
  279.6 11.7 %collective-permute-done.27 = f32[16,64,256]{2,1,0:T(8,128)S(1)} collective-permute-done((f32[16,64,256]{2,1,0:T(8,128)S(1)}, f32[16,64,256]{2,1,0:T(8,128)S(1)}, u32[]{:S(2)}, u32[]{:S(2)}) %collective-permute-start.27) | collective-permute-done | bytes 1048608 | tf_op jit(solution)/shard_map/ppermute | solution.py:32
  292.9 5.2 %collective-permute-done.28 = f32[16,128,256]{2,1,0:T(8,128)S(1)} collective-permute-done((f32[16,128,256]{2,1,0:T(8,128)S(1)}, f32[16,128,256]{2,1,0:T(8,128)S(1)}, u32[]{:S(2)}, u32[]{:S(2)}) %collective-permute-start.28) | collective-permute-done | bytes 2097184 | tf_op jit(solution)/shard_map/ppermute | solution.py:32
  298.1 1.6 broadcast_select_fusion
  (78 shorter events, 32.1 us)
Async XLA Ops:
  3.5 2.5 copy-start.8
  3.5 4.4 %copy-start = (f32[1,16,128,256]{3,2,1,0:T(8,128)S(1)}, f32[1,16,128,256]{3,2,1,0:T(8,128)}, u32[]{:S(2)}) copy-start(f32[1,16,128,256]{3,2,1,0:T(8,128)} %param.7) | copy-start | bytes 6291460
  3.5 4.4 %copy-start.5 = (s32[1,16,128]{2,1,0:T(8,128)S(1)}, s32[1,16,128]{2,1,0:T(8,128)}, u32[]{:S(2)}) copy-start(s32[1,16,128]{2,1,0:T(8,128)} %param.10) | copy-start | bytes 24580
  4.6 39.1 %collective-permute-start = (f32[16,80,256]{2,1,0:T(8,128)}, f32[16,80,256]{2,1,0:T(8,128)}, u32[]{:S(2)}, u32[]{:S(2)}) collective-permute-start(f32[16,80,256]{2,1,0:T(8,128)} %pad_maximum_fusion.2), channel_id=1, source_target_pairs={{0,1},{2,3},{4,5},{6,7},{9,8},{11,10},{13,12},{15,14},{16,17},{18,... | collective-permute-start | bytes 3932168 | tf_op jit(solution)/shard_map/ppermute | solution.py:32
  11.9 28.9 %collective-permute-start.4 = (f32[17,64,256]{2,1,0:T(8,128)S(1)}, f32[17,64,256]{2,1,0:T(8,128)S(1)}, u32[]{:S(2)}, u32[]{:S(2)}) collective-permute-start(f32[17,64,256]{2,1,0:T(8,128)S(1)} %get-tuple-element.30), channel_id=1, source_target_pairs={{0,0},{1,8},{2,2},{3,10},{4,4},{5,12},{6,6},{7,14},{8,1},{9,9},{10... | collective-permute-start | bytes 3342344 | tf_op jit(solution)/shard_map/ppermute | solution.py:32
  15.7 37.3 %collective-permute-start.7 = (f32[17,64,256]{2,1,0:T(8,128)}, f32[17,64,256]{2,1,0:T(8,128)}, u32[]{:S(2)}, u32[]{:S(2)}) collective-permute-start(f32[17,64,256]{2,1,0:T(8,128)} %get-tuple-element.31), channel_id=1, source_target_pairs={{0,1},{1,9},{2,3},{3,11},{4,5},{5,13},{6,7},{7,15},{8,0},{9,8},{10... | collective-permute-start | bytes 3342344 | tf_op jit(solution)/shard_map/ppermute | solution.py:32
  41.9 17.7 %collective-permute-start.6 = (f32[16,64,256]{2,1,0:T(8,128)}, f32[16,64,256]{2,1,0:T(8,128)S(1)}, u32[]{:S(2)}, u32[]{:S(2)}) collective-permute-start(f32[16,64,256]{2,1,0:T(8,128)} %slice.57), channel_id=1, source_target_pairs={{2,8},{3,9},{4,10},{5,11},{6,12},{7,13},{8,0},{9,1},{10,2},{11,3},... | collective-permute-start | bytes 3145736 | tf_op jit(solution)/shard_map/ppermute | solution.py:32
  45.3 1.9 copy-start.6
  45.3 7.5 %copy-start.9 = (f32[1,61]{1,0:T(1,128)S(1)}, f32[1,61]{1,0:T(1,128)}, u32[]{:S(2)}) copy-start(f32[1,61]{1,0:T(1,128)} %param.13) | copy-start | bytes 736
  45.4 7.5 %copy-start.10 = (f32[1,31]{1,0:T(1,128)S(1)}, f32[1,31]{1,0:T(1,128)}, u32[]{:S(2)}) copy-start(f32[1,31]{1,0:T(1,128)} %param.12) | copy-start | bytes 376
  45.4 7.5 %copy-start.11 = (f32[1,31]{1,0:T(1,128)S(1)}, f32[1,31]{1,0:T(1,128)}, u32[]{:S(2)}) copy-start(f32[1,31]{1,0:T(1,128)} %param.11) | copy-start | bytes 376
  47.2 47.6 %collective-permute-start.3 = (f32[15,80,256]{2,1,0:T(8,128)}, f32[15,80,256]{2,1,0:T(8,128)S(1)}, u32[]{:S(2)}, u32[]{:S(2)}) collective-permute-start(f32[15,80,256]{2,1,0:T(8,128)} %get-tuple-element.63), channel_id=1, source_target_pairs={{2,8},{3,9},{4,10},{5,11},{6,12},{7,13},{8,0},{9,1},{10,2},{11,3},... | collective-permute-start | bytes 3686408 | tf_op jit(solution)/shard_map/ppermute | solution.py:32
  49.3 45.5 %collective-permute-start.2 = (f32[15,80,256]{2,1,0:T(8,128)}, f32[15,80,256]{2,1,0:T(8,128)}, u32[]{:S(2)}, u32[]{:S(2)}) collective-permute-start(f32[15,80,256]{2,1,0:T(8,128)} %get-tuple-element.64), channel_id=1, source_target_pairs={{0,8},{1,9},{2,10},{3,11},{4,12},{5,13},{6,14},{7,15},{8,2},{9,3},... | collective-permute-start | bytes 3686408 | tf_op jit(solution)/shard_map/ppermute | solution.py:32
  52.9 4.4 %collective-permute-start.1 = (f32[126]{0:T(128)S(1)}, f32[126]{0:T(128)S(1)}, u32[]{:S(2)}, u32[]{:S(2)}) collective-permute-start(f32[126]{0:T(128)S(1)} %pad_maximum_fusion.3), channel_id=1, source_target_pairs={{0,8},{1,9},{2,10},{3,11},{4,12},{5,13},{6,14},{7,15},{8,0},{9,1},... | collective-permute-start | bytes 1520 | tf_op jit(solution)/shard_map/ppermute | solution.py:32
  52.9 25.1 %collective-permute-start.5 = (f32[16,64,256]{2,1,0:T(8,128)}, f32[16,64,256]{2,1,0:T(8,128)}, u32[]{:S(2)}, u32[]{:S(2)}) collective-permute-start(f32[16,64,256]{2,1,0:T(8,128)} %slice.57), channel_id=1, source_target_pairs={{0,8},{1,9},{2,10},{3,11},{4,12},{5,13},{6,14},{7,15},{8,2},{9,3},... | collective-permute-start | bytes 3145736 | tf_op jit(solution)/shard_map/ppermute | solution.py:32
  57.4 25.6 %collective-permute-start.9 = (f32[16,64,256]{2,1,0:T(8,128)}, f32[16,64,256]{2,1,0:T(8,128)}, u32[]{:S(2)}, u32[]{:S(2)}) collective-permute-start(f32[16,64,256]{2,1,0:T(8,128)} %slice.58), channel_id=1, source_target_pairs={{2,8},{3,9},{4,10},{5,11},{6,12},{7,13},{8,0},{9,1},{10,2},{11,3},... | collective-permute-start | bytes 3145736 | tf_op jit(solution)/shard_map/ppermute | solution.py:32
  59.6 1.0 copy-start.1
  60.6 28.7 %collective-permute-start.8 = (f32[16,64,256]{2,1,0:T(8,128)}, f32[16,64,256]{2,1,0:T(8,128)}, u32[]{:S(2)}, u32[]{:S(2)}) collective-permute-start(f32[16,64,256]{2,1,0:T(8,128)} %slice.58), channel_id=1, source_target_pairs={{0,8},{1,9},{2,10},{3,11},{4,12},{5,13},{6,14},{7,15},{8,2},{9,3},... | collective-permute-start | bytes 3145736 | tf_op jit(solution)/shard_map/ppermute | solution.py:32
  89.2 1.2 copy-start.2
  100.8 7.6 %collective-permute-start.13 = (f32[16,16,256]{2,1,0:T(8,128)S(1)}, f32[16,16,256]{2,1,0:T(8,128)S(1)}, u32[]{:S(2)}, u32[]{:S(2)}) collective-permute-start(f32[16,16,256]{2,1,0:T(8,128)S(1)} %dynamic-slice_bitcast_fusion.2), channel_id=1, source_target_pairs={{0,1},{1,0},{2,3},{3,2},{4,5},{5,4},{6,7},{7,6},{8,9},{9,8},{10,11... | collective-permute-start | bytes 786440 | tf_op jit(solution)/shard_map/ppermute | solution.py:32
  108.3 8.9 %collective-permute-start.10 = (f32[16,16,256]{2,1,0:T(8,128)S(1)}, f32[16,16,256]{2,1,0:T(8,128)S(1)}, u32[]{:S(2)}, u32[]{:S(2)}) collective-permute-start(f32[16,16,256]{2,1,0:T(8,128)S(1)} %dynamic-slice_bitcast_fusion.3), channel_id=1, source_target_pairs={{0,1},{1,0},{2,3},{3,2},{4,5},{5,4},{6,7},{7,6},{8,9},{9,8},{10,11... | collective-permute-start | bytes 786440 | tf_op jit(solution)/shard_map/ppermute | solution.py:32
  109.4 1.0 copy-start.3
  110.4 16.0 %collective-permute-start.14 = (f32[15,64,256]{2,1,0:T(8,128)S(1)}, f32[15,64,256]{2,1,0:T(8,128)S(1)}, u32[]{:S(2)}, u32[]{:S(2)}) collective-permute-start(f32[15,64,256]{2,1,0:T(8,128)S(1)} %get-tuple-element.42), channel_id=1, source_target_pairs={{0,8},{1,9},{2,10},{3,11},{4,12},{5,13},{6,14},{7,15},{8,2},{9,3},... | collective-permute-start | bytes 2949128 | tf_op jit(solution)/shard_map/ppermute | solution.py:32
  115.3 15.7 %collective-permute-start.15 = (f32[15,64,256]{2,1,0:T(8,128)S(1)}, f32[15,64,256]{2,1,0:T(8,128)S(1)}, u32[]{:S(2)}, u32[]{:S(2)}) collective-permute-start(f32[15,64,256]{2,1,0:T(8,128)S(1)} %get-tuple-element.44), channel_id=1, source_target_pairs={{2,8},{3,9},{4,10},{5,11},{6,12},{7,13},{8,0},{9,1},{10,2},{11,3},... | collective-permute-start | bytes 2949128 | tf_op jit(solution)/shard_map/ppermute | solution.py:32
  118.2 18.6 %collective-permute-start.11 = (f32[15,64,256]{2,1,0:T(8,128)S(1)}, f32[15,64,256]{2,1,0:T(8,128)S(1)}, u32[]{:S(2)}, u32[]{:S(2)}) collective-permute-start(f32[15,64,256]{2,1,0:T(8,128)S(1)} %get-tuple-element.37), channel_id=1, source_target_pairs={{0,8},{1,9},{2,10},{3,11},{4,12},{5,13},{6,14},{7,15},{8,2},{9,3},... | collective-permute-start | bytes 2949128 | tf_op jit(solution)/shard_map/ppermute | solution.py:32
  121.9 19.4 %collective-permute-start.12 = (f32[15,64,256]{2,1,0:T(8,128)S(1)}, f32[15,64,256]{2,1,0:T(8,128)S(1)}, u32[]{:S(2)}, u32[]{:S(2)}) collective-permute-start(f32[15,64,256]{2,1,0:T(8,128)S(1)} %get-tuple-element.39), channel_id=1, source_target_pairs={{2,8},{3,9},{4,10},{5,11},{6,12},{7,13},{8,0},{9,1},{10,2},{11,3},... | collective-permute-start | bytes 2949128 | tf_op jit(solution)/shard_map/ppermute | solution.py:32
  141.3 30.6 %copy-start.7 = (f32[16,80,256]{2,1,0:T(8,128)S(1)}, f32[16,80,256]{2,1,0:T(8,128)}, u32[]{:S(2)}) copy-start(f32[16,80,256]{2,1,0:T(8,128)} %copy-done.6) | copy-start | bytes 3932164
  147.6 24.2 %collective-permute-start.16 = (f32[16,64,256]{2,1,0:T(8,128)S(1)}, f32[16,64,256]{2,1,0:T(8,128)}, u32[]{:S(2)}, u32[]{:S(2)}) collective-permute-start(f32[16,64,256]{2,1,0:T(8,128)S(1)} %log_factor.2), channel_id=1, source_target_pairs={{0,16},{1,17},{2,18},{3,19},{4,20},{5,21},{6,22},{7,23},{8,24},{9,... | collective-permute-start | bytes 3145736 | tf_op jit(solution)/shard_map/ppermute | solution.py:32
  173.3 8.1 %collective-permute-start.17 = (f32[16,16,256]{2,1,0:T(8,128)S(1)}, f32[16,16,256]{2,1,0:T(8,128)S(1)}, u32[]{:S(2)}, u32[]{:S(2)}) collective-permute-start(f32[16,16,256]{2,1,0:T(8,128)S(1)} %constant_dynamic-slice_fusion), channel_id=1, source_target_pairs={{0,1},{1,0},{2,3},{3,2},{4,5},{5,4},{6,7},{7,6},{8,9},{9,8},{10,11... | collective-permute-start | bytes 786440 | tf_op jit(solution)/shard_map/ppermute | solution.py:32
  181.7 18.3 %collective-permute-start.19 = (f32[15,80,256]{2,1,0:T(8,128)S(1)}, f32[15,80,256]{2,1,0:T(8,128)S(1)}, u32[]{:S(2)}, u32[]{:S(2)}) collective-permute-start(f32[15,80,256]{2,1,0:T(8,128)S(1)} %get-tuple-element.61), channel_id=1, source_target_pairs={{2,8},{3,9},{4,10},{5,11},{6,12},{7,13},{8,0},{9,1},{10,2},{11,3},... | collective-permute-start | bytes 3686408 | tf_op jit(solution)/shard_map/ppermute | solution.py:32
  184.3 16.6 %collective-permute-start.18 = (f32[15,80,256]{2,1,0:T(8,128)S(1)}, f32[15,80,256]{2,1,0:T(8,128)S(1)}, u32[]{:S(2)}, u32[]{:S(2)}) collective-permute-start(f32[15,80,256]{2,1,0:T(8,128)S(1)} %get-tuple-element.62), channel_id=1, source_target_pairs={{0,8},{1,9},{2,10},{3,11},{4,12},{5,13},{6,14},{7,15},{8,2},{9,3},... | collective-permute-start | bytes 3686408 | tf_op jit(solution)/shard_map/ppermute | solution.py:32
  206.5 7.1 %collective-permute-start.20 = (f32[16,16,256]{2,1,0:T(8,128)S(1)}, f32[16,16,256]{2,1,0:T(8,128)S(1)}, u32[]{:S(2)}, u32[]{:S(2)}) collective-permute-start(f32[16,16,256]{2,1,0:T(8,128)S(1)} %dynamic-slice_bitcast_fusion.1), channel_id=1, source_target_pairs={{0,1},{1,0},{2,3},{3,2},{4,5},{5,4},{6,7},{7,6},{8,9},{9,8},{10,11... | collective-permute-start | bytes 786440 | tf_op jit(solution)/shard_map/ppermute | solution.py:32
  213.5 8.0 %collective-permute-start.23 = (f32[16,16,256]{2,1,0:T(8,128)S(1)}, f32[16,16,256]{2,1,0:T(8,128)S(1)}, u32[]{:S(2)}, u32[]{:S(2)}) collective-permute-start(f32[16,16,256]{2,1,0:T(8,128)S(1)} %dynamic-slice_bitcast_fusion), channel_id=1, source_target_pairs={{0,1},{1,0},{2,3},{3,2},{4,5},{5,4},{6,7},{7,6},{8,9},{9,8},{10,11... | collective-permute-start | bytes 786440 | tf_op jit(solution)/shard_map/ppermute | solution.py:32
  214.6 16.0 %collective-permute-start.21 = (f32[15,64,256]{2,1,0:T(8,128)S(1)}, f32[15,64,256]{2,1,0:T(8,128)S(1)}, u32[]{:S(2)}, u32[]{:S(2)}) collective-permute-start(f32[15,64,256]{2,1,0:T(8,128)S(1)} %get-tuple-element.47), channel_id=1, source_target_pairs={{0,8},{1,9},{2,10},{3,11},{4,12},{5,13},{6,14},{7,15},{8,2},{9,3},... | collective-permute-start | bytes 2949128 | tf_op jit(solution)/shard_map/ppermute | solution.py:32
  219.5 15.7 %collective-permute-start.22 = (f32[15,64,256]{2,1,0:T(8,128)S(1)}, f32[15,64,256]{2,1,0:T(8,128)S(1)}, u32[]{:S(2)}, u32[]{:S(2)}) collective-permute-start(f32[15,64,256]{2,1,0:T(8,128)S(1)} %get-tuple-element.49), channel_id=1, source_target_pairs={{2,8},{3,9},{4,10},{5,11},{6,12},{7,13},{8,0},{9,1},{10,2},{11,3},... | collective-permute-start | bytes 2949128 | tf_op jit(solution)/shard_map/ppermute | solution.py:32
  222.5 1.0 copy-start.4
  223.4 17.7 %collective-permute-start.24 = (f32[15,64,256]{2,1,0:T(8,128)S(1)}, f32[15,64,256]{2,1,0:T(8,128)S(1)}, u32[]{:S(2)}, u32[]{:S(2)}) collective-permute-start(f32[15,64,256]{2,1,0:T(8,128)S(1)} %get-tuple-element.52), channel_id=1, source_target_pairs={{0,8},{1,9},{2,10},{3,11},{4,12},{5,13},{6,14},{7,15},{8,2},{9,3},... | collective-permute-start | bytes 2949128 | tf_op jit(solution)/shard_map/ppermute | solution.py:32
  227.1 18.4 %collective-permute-start.25 = (f32[15,64,256]{2,1,0:T(8,128)S(1)}, f32[15,64,256]{2,1,0:T(8,128)S(1)}, u32[]{:S(2)}, u32[]{:S(2)}) collective-permute-start(f32[15,64,256]{2,1,0:T(8,128)S(1)} %get-tuple-element.54), channel_id=1, source_target_pairs={{2,8},{3,9},{4,10},{5,11},{6,12},{7,13},{8,0},{9,1},{10,2},{11,3},... | collective-permute-start | bytes 2949128 | tf_op jit(solution)/shard_map/ppermute | solution.py:32
  251.8 24.2 %collective-permute-start.26 = (f32[16,64,256]{2,1,0:T(8,128)S(1)}, f32[16,64,256]{2,1,0:T(8,128)S(1)}, u32[]{:S(2)}, u32[]{:S(2)}) collective-permute-start(f32[16,64,256]{2,1,0:T(8,128)S(1)} %log_factor.3), channel_id=1, source_target_pairs={{0,16},{1,17},{2,18},{3,19},{4,20},{5,21},{6,22},{7,23},{8,24},{9,... | collective-permute-start | bytes 3145736 | tf_op jit(solution)/shard_map/ppermute | solution.py:32
  276.2 15.1 %collective-permute-start.27 = (f32[16,64,256]{2,1,0:T(8,128)S(1)}, f32[16,64,256]{2,1,0:T(8,128)S(1)}, u32[]{:S(2)}, u32[]{:S(2)}) collective-permute-start(f32[16,64,256]{2,1,0:T(8,128)S(1)} %exponential_multiply_fusion), channel_id=1, source_target_pairs={{1,0},{3,2},{5,4},{7,6},{8,9},{10,11},{12,13},{14,15},{17,16},{19,... | collective-permute-start | bytes 3145736 | tf_op jit(solution)/shard_map/ppermute | solution.py:32
  291.6 6.5 %collective-permute-start.28 = (f32[16,128,256]{2,1,0:T(8,128)S(1)}, f32[16,128,256]{2,1,0:T(8,128)S(1)}, u32[]{:S(2)}, u32[]{:S(2)}) collective-permute-start(f32[16,128,256]{2,1,0:T(8,128)S(1)} %pad_maximum_fusion.1), channel_id=1, source_target_pairs={{0,8},{2,10},{4,12},{6,14},{9,1},{11,3},{13,5},{15,7},{16,24},{18,... | collective-permute-start | bytes 6291464 | tf_op jit(solution)/shard_map/ppermute | solution.py:32

commit v2 on v0

v2 whole, which is shorter than its diff:
```python
import functools

import jax
import jax.numpy as jnp
from jax import lax
from jax.experimental import pallas as pl
from jax.experimental.pallas import tpu as pltpu
from jax.sharding import PartitionSpec as P

ITERS = 2
AXES = ("view", "tile")
F32 = jnp.float32
BF16 = jnp.bfloat16
VMEM = pl.BlockSpec(memory_space=pltpu.VMEM)
SMEM = pl.BlockSpec(memory_space=pltpu.SMEM)
PARAMS = pltpu.CompilerParams(vmem_limit_bytes=48 * 1024 * 1024)
GROUP = 16


def moves(move):
    views, tiles = lax.axis_size("view"), lax.axis_size("tile")
    pairs = []
    for view in range(views):
        for tile in range(tiles):
            target = move(view // 2, view % 2, tile // 2, tile % 2)
            if target is not None:
                g, c, q, r = target
                pairs.append((view * tiles + tile, (2 * g + c) * tiles + 2 * q + r))
    return pairs


def send(array, move):
    return lax.ppermute(array, AXES, moves(move))


def to_next(g, c, q, r):
    s = 2 * q + c + 1
    return (g, s % 2, s // 2, r) if s < lax.axis_size("tile") else None


def to_previous(g, c, q, r):
    s = 2 * q + c - 1
    return (g, s % 2, s // 2, r) if s >= 0 else None


def to_row_partner(g, c, q, r):
    return (g, c, q, 1 - r)


def to_core_partner(g, c, q, r):
    return (g, 1 - c, q, r)


def split(x):
    high = x.astype(BF16)
    return high, (x - high.astype(F32)).astype(BF16)


def dot(a, b):
    return jnp.dot(a, b, preferred_element_type=F32)


def iota(shape, dim):
    return lax.broadcasted_iota(jnp.int32, shape, dim)


def group_row(half, group, cells_y):
    return group * GROUP + half * (cells_y - GROUP - 2 * group * GROUP)


def global_row(half, local, cells_y):
    group = local // GROUP
    return group_row(half, group, cells_y) + (local - group * GROUP)


def pad_to(value, unit):
    return -(-value // unit) * unit


def call(kernel, out_shape, in_specs, name, scratch=()):
    return pl.pallas_call(
        kernel,
        out_shape=out_shape,
        in_specs=in_specs,
        out_specs=jax.tree.map(lambda _: VMEM, out_shape),
        scratch_shapes=list(scratch),
        compiler_params=PARAMS,
        name=name,
    )


def tables_kernel(
    half_ref, ky_ref, tz_ref, tx_ref, yf_ref, ya_ref, zhi_ref, zlo_ref, xhi_ref, xlo_ref, *, sizes, cells_y, radius_z
):
    taps = ky_ref.shape[1]
    radius = taps // 2
    half = half_ref[0]
    own, near, wide = sizes
    for index in range(4):
        adjoint = index >= 2
        out_ref, rows, width = (ya_ref, own, near) if adjoint else (yf_ref, near, wide)
        lanes = out_ref.shape[2]
        row = global_row(half, iota((rows, lanes), 0), cells_y)
        lane = iota((rows, lanes), 1)
        col = global_row(half, lane, cells_y)
        delta = (row - col if adjoint else col - row) + radius
        delta = jnp.where(lane < width, delta, -1)
        band = jnp.zeros((rows, lanes), F32)
        for a in range(taps):
            band = jnp.where(delta == a, ky_ref[index % 2, a], band)
        high, low = split(band)
        high, low = high.astype(F32), low.astype(F32)
        out_ref[index % 2] = (high + pltpu.roll(high, width, 1) + pltpu.roll(low, 2 * width, 1)).astype(BF16)

    lanes = tz_ref.shape[1]
    near_z = jnp.abs(iota((lanes, lanes), 1) - iota((lanes, lanes), 0)) <= radius_z
    for index in range(4):
        base = pltpu.roll(tz_ref[index:index + 1, :], lanes - radius_z, 1)
        band = pltpu.roll(jnp.broadcast_to(base, (lanes, lanes)), 0, 1, stride=1, stride_axis=0)
        zhi_ref[index], zlo_ref[index] = split(jnp.where(near_z, band, jnp.zeros_like(band)))

    rows, lanes = xhi_ref.shape[1] // 2, tx_ref.shape[1]
    for index in range(4):
        base = jnp.broadcast_to(tx_ref[index:index + 1, :], (rows, lanes))
        band = pltpu.roll(base, 0, 1, stride=1, stride_axis=0)[:, :xhi_ref.shape[2]]
        place = (index // 2, slice(index % 2 * rows, index % 2 * rows + rows))
        xhi_ref[place], xlo_ref[place] = split(band)


def make_tables(half, kx, ky, kz, planes, cells_y, cells_z, sizes):
    own, near, wide = sizes
    taps_x, taps_z = kx.shape[1], kz.shape[1]
    depth = 8 * pad_to(planes + taps_x - 1, 16)
    lanes = max(512, 1 << (depth - 1).bit_length())
    zero = jnp.zeros((), F32)
    tx = jnp.concatenate([kx, kx[:, ::-1]])
    tx = lax.pad(tx, zero, ((0, 0, 0), (0, lanes - 8 * taps_x + 7, 7)))
    tz = jnp.concatenate([kz[:, ::-1], kz])
    tz = lax.pad(tz, zero, ((0, 0, 0), (0, cells_z - taps_z, 0)))
    kernel = functools.partial(tables_kernel, sizes=sizes, cells_y=cells_y, radius_z=taps_z // 2)
    shape = jax.ShapeDtypeStruct
    out_shape = (
        shape((2, near, pad_to(3 * wide, 128)), BF16),
        shape((2, own, pad_to(3 * near, 128)), BF16),
        shape((4, cells_z, cells_z), BF16),
        shape((4, cells_z, cells_z), BF16),
        shape((2, 2 * 8 * planes, depth), BF16),
        shape((2, 2 * 8 * planes, depth), BF16),
    )
    return call(kernel, out_shape, [SMEM, SMEM, VMEM, VMEM], "band_matrices")(half.reshape(1), ky, tz, tx)


def window_kernel(half_ref, estimate_ref, own_ref, other_ref):
    cells_y = estimate_ref.shape[1]
    half = half_ref[0]
    for side, out_ref in ((half, own_ref), (1 - half, other_ref)):
        for group in range(out_ref.shape[1] // GROUP):
            start = pl.multiple_of(group_row(side, group, cells_y), GROUP)
            out_ref[:, group * GROUP:(group + 1) * GROUP, :] = estimate_ref[:, pl.ds(start, GROUP), :]


def make_windows(half, estimate, wide):
    planes, _, cells_z = estimate.shape
    shape = jax.ShapeDtypeStruct((planes, wide, cells_z), F32)
    return call(window_kernel, (shape, shape), [SMEM, VMEM], "estimate_windows")(half.reshape(1), estimate)


def shift_kernel(scal_ref, acq_ref, mask_ref, first_ref, second_ref, turned_ref):
    planes, cells_y, cells_z = acq_ref.shape
    near = first_ref.shape[1]
    shift_y, shift_z, core = scal_ref[0], scal_ref[1], scal_ref[2]
    row = iota((cells_y, cells_z), 0) + shift_y
    col = iota((cells_y, cells_z), 1) + shift_z
    inside = (row >= 0) & (row < cells_y) & (col >= 0) & (col < cells_z)
    turn_y = lax.rem(cells_y - shift_y, cells_y)
    turn_z = lax.rem(cells_z - shift_z, cells_z)

    def body(p, carry):
        x = pltpu.roll(pltpu.roll(acq_ref[p], turn_z, 1), turn_y, 0)
        turned_ref[...] = jnp.where(inside, x, jnp.zeros_like(x))
        for side, out_ref in ((core, first_ref), (1 - core, second_ref)):
            for group in range(near // GROUP):
                start = pl.multiple_of(group_row(side, group, cells_y), GROUP)
                out_ref[p, group * GROUP:(group + 1) * GROUP, :] = turned_ref[pl.ds(start, GROUP), :]
        return carry

    lax.fori_loop(0, planes, body, 0)
    mask = mask_ref[...].astype(F32)
    for out_ref in (first_ref, second_ref):
        out_ref[planes] = jnp.zeros((near, cells_z), F32)
        out_ref[planes, :planes, :cells_y] = mask


def shift_and_cut(scal, acquired, mask, near):
    planes, cells_y, cells_z = acquired.shape
    shape = jax.ShapeDtypeStruct((planes + 1, near, cells_z), F32)
    scratch = [pltpu.VMEM((cells_y, cells_z), F32)]
    return call(shift_kernel, (shape, shape), [SMEM, VMEM, VMEM], "shift_recorded", scratch)(scal, acquired, mask)


def spread_x(hi_ref, lo_ref, index, start, count, refs, row):
    low_ref, own_ref, high_ref = refs
    lanes = own_ref.shape[2]
    depth = hi_ref.shape[2]
    parts = [ref[:, pl.ds(row, 8), :] for ref in refs]
    missing = depth // 8 - sum(part.shape[0] for part in parts)
    if missing:
        parts.append(jnp.zeros((missing, 8, lanes), F32))
    high, low = split(jnp.concatenate(parts, axis=0).reshape(depth, lanes))
    band = hi_ref[index, start:start + count, :]
    out = dot(band, high) + (dot(band, low) + dot(lo_ref[index, start:start + count, :], high))
    return out.reshape(count // 8, 8, lanes)


def blur_x_kernel(hi_ref, lo_ref, low_ref, own_ref, high_ref, first_ref, second_ref):
    planes, rows, lanes = own_ref.shape

    def body(step, carry):
        row = pl.multiple_of(step * 8, 8)
        out = spread_x(hi_ref, lo_ref, 0, 0, hi_ref.shape[1], (low_ref, own_ref, high_ref), row)
        first_ref[:, pl.ds(row, 8), :] = out[:planes]
        second_ref[:, pl.ds(row, 8), :] = out[planes:]
        return carry

    lax.fori_loop(0, rows // 8, body, 0)


def blur_x(tables, low, own, high):
    shape = jax.ShapeDtypeStruct(own.shape, F32)
    return call(blur_x_kernel, (shape, shape), [VMEM] * 5, "blur_x")(*tables[4:], low, own, high)


def spread_y(band, x):
    high, low = split(x)
    parts = [high, low, high]
    rest = band.shape[1] - 3 * x.shape[0]
    if rest:
        parts.append(jnp.zeros((rest, x.shape[1]), BF16))
    return dot(band, jnp.concatenate(parts, axis=0))


def spread_z(x, hi_ref, lo_ref, index):
    high, low = split(x)
    return dot(high, hi_ref[index]) + (dot(low, hi_ref[index]) + dot(high, lo_ref[index]))


def ratio_planes(wide_ref, fetch, yf_ref, ya_ref, zhi_ref, zlo_ref, order, outs):
    out_ref, lower_ref, upper_ref = outs
    planes, rows, _ = out_ref.shape
    radius = lower_ref.shape[0]
    near = yf_ref.shape[1]
    step = 4
    for start in range(0, planes, step):
        block = range(start, min(start + step, planes))
        blurred = jnp.concatenate([spread_y(yf_ref[order], wide_ref[p]) for p in block], axis=0)
        blurred = spread_z(blurred, zhi_ref, zlo_ref, order)
        image = jnp.concatenate([fetch(p) for p in block], axis=0)
        ratio = jnp.where(image >= 0, image / blurred, jnp.ones_like(image))
        spread = jnp.concatenate(
            [spread_y(ya_ref[order], ratio[k * near:(k + 1) * near]) for k in range(len(block))], axis=0
        )
        spread = spread_z(spread, zhi_ref, zlo_ref, 2 + order)
        for k, p in enumerate(block):
            value = spread[k * rows:(k + 1) * rows]
            out_ref[p] = value
            if p < radius:
                lower_ref[p] = value
            if p >= planes - radius:
                upper_ref[p - planes + radius] = value


def first_ratio_kernel(
    shift_ref, place_ref, low_ref, own_ref, high_ref, wide_ref, yf_ref, ya_ref, zhi_ref, zlo_ref,
    out_ref, lower_ref, upper_ref, image_ref, *, order, extent_x, cells_y
):
    planes, near, cells_z = image_ref.shape
    slab, half = place_ref[0], place_ref[1]
    shift_x, shift_y, shift_z = (shift_ref[order, i] for i in range(3))
    lanes = pad_to(cells_y, 128)
    pick = iota((near, lanes), 1) == global_row(half, iota((near, lanes), 0), cells_y)
    mask = own_ref[planes, :planes, :lanes].astype(BF16)
    columns = lax.dot_general(
        pick.astype(F32).astype(BF16), mask, (((1,), (1,)), ((), ())), preferred_element_type=F32
    )
    row = global_row(half, iota((near, cells_z), 0), cells_y) + shift_y
    col = iota((near, cells_z), 1) + shift_z
    inside = (row >= 0) & (row < cells_y) & (col >= 0) & (col < cells_z)

    def fetch(p):
        source = p + shift_x
        x = slab * planes + source
        own = own_ref[jnp.clip(source, 0, planes - 1)]
        low = low_ref[jnp.clip(source + planes, 0, planes - 1)]
        high = high_ref[jnp.clip(source - planes, 0, planes - 1)]
        value = jnp.where(source < 0, low, jnp.where(source < planes, own, high))
        weight = jnp.broadcast_to(columns[:, p:p + 1], (near, cells_z))
        covered = inside & (weight > 0.5) & (x >= 0) & (x < extent_x)
        value = jnp.where(covered, value, jnp.full_like(value, -1.0))
        image_ref[p] = value
        return value

    ratio_planes(wide_ref, fetch, yf_ref, ya_ref, zhi_ref, zlo_ref, order, (out_ref, lower_ref, upper_ref))


def next_ratio_kernel(
    image_ref, wide_ref, yf_ref, ya_ref, zhi_ref, zlo_ref, out_ref, lower_ref, upper_ref, *, order
):
    ratio_planes(
        wide_ref, lambda p: image_ref[p], yf_ref, ya_ref, zhi_ref, zlo_ref, order, (out_ref, lower_ref, upper_ref)
    )


def ratio_shapes(wide, tables, radius):
    planes, _, lanes = wide.shape
    rows = tables[1].shape[1]
    edge = jax.ShapeDtypeStruct((radius, rows, lanes), F32)
    return jax.ShapeDtypeStruct((planes, rows, lanes), F32), edge, edge


def first_ratio(shifts, place, blocks, wide, tables, order, radius, extent_x, cells_y):
    near = tables[0].shape[1]
    kernel = functools.partial(first_ratio_kernel, order=order, extent_x=extent_x, cells_y=cells_y)
    image = jax.ShapeDtypeStruct((wide.shape[0], near, wide.shape[2]), F32)
    out_shape = ratio_shapes(wide, tables, radius) + (image,)
    return call(kernel, out_shape, [SMEM] * 2 + [VMEM] * 8, "image_and_ratio")(
        shifts, place, *blocks, wide, *tables[:4]
    )


def next_ratio(image, wide, tables, order, radius):
    kernel = functools.partial(next_ratio_kernel, order=order)
    return call(kernel, ratio_shapes(wide, tables, radius), [VMEM] * 6, "ratio")(image, wide, *tables[:4])


def factor_kernel(hi_ref, lo_ref, current_ref, *refs, start, share):
    views, out_ref = (refs[:3], refs[3:6]), refs[6]
    planes, rows, _ = out_ref.shape

    def body(step, carry):
        row = pl.multiple_of(step * 8, 8)
        source = pl.multiple_of(start + row, 8)
        total = share * jnp.log(current_ref[:, pl.ds(source, 8), :])
        for order, view in enumerate(views):
            total = total + jnp.log(spread_x(hi_ref, lo_ref, 1, order * 8 * planes, 8 * planes, view, source))
        out_ref[:, pl.ds(row, 8), :] = total
        return carry

    lax.fori_loop(0, rows // 8, body, 0)


def log_factor(tables, current, sides, start, rows, share):
    planes, _, lanes = current.shape
    kernel = functools.partial(factor_kernel, start=start, share=share)
    shape = jax.ShapeDtypeStruct((planes, rows, lanes), F32)
    return call(kernel, shape, [VMEM] * 9, "log_factor")(*tables[4:], current, *sides[0], *sides[1])


def finish_kernel(half_ref, own_ref, *refs, groups):
    out_ref = refs[-1]
    half = half_ref[0]
    cells_y = out_ref.shape[1]
    own = [own_ref] + list(refs[:groups - 1])
    other = list(refs[groups - 1:2 * groups - 1])
    for side, parts in ((half, own), (1 - half, other)):
        for group in range(own_ref.shape[1] // GROUP):
            rows = slice(group * GROUP, (group + 1) * GROUP)
            total = parts[0][:, rows, :]
            for part in parts[1:]:
                total = total + part[:, rows, :]
            start = pl.multiple_of(group_row(side, group, cells_y), GROUP)
            out_ref[:, pl.ds(start, GROUP), :] = jnp.exp(total)


def finish(half, own, own_parts, other_parts, shape):
    groups = len(own_parts) + 1
    kernel = functools.partial(finish_kernel, groups=groups)
    return call(kernel, jax.ShapeDtypeStruct(shape, F32), [SMEM] + [VMEM] * (2 * groups), "update")(
        half.reshape(1), own, *own_parts, *other_parts
    )


def shards(acquired, estimate, offsets, view_mask, kern_x, kern_y, kern_z):
    planes, cells_y, cells_z = estimate.shape
    views, slabs = lax.axis_size("view"), lax.axis_size("tile")
    groups = views // 2
    taps_x, taps_y, taps_z = kern_x.shape[1], kern_y.shape[1], kern_z.shape[1]
    radius = taps_x // 2
    own_rows = cells_y // 2
    near = own_rows + pad_to(taps_y // 2, GROUP)
    wide = own_rows + pad_to(2 * (taps_y // 2), GROUP)
    edge_rows = wide - own_rows
    inner_rows = own_rows - edge_rows
    core = lax.rem(lax.axis_index("view"), 2)
    half = lax.rem(lax.axis_index("tile"), 2)
    slab = lax.axis_index("tile") - half + core
    straight = core == half

    window, crossing = make_windows(half, estimate, wide)
    crossing = send(crossing, lambda g, c, q, r: (g, c, q, 1 - r) if c == r else None)

    scal = jnp.stack([offsets[0, 1], offsets[0, 2], core])
    acquired, window = lax.optimization_barrier((acquired, window))
    first, second = shift_and_cut(scal, acquired[0], view_mask[0], near)

    mine = jnp.concatenate([kern_x[0], kern_y[0], kern_z[0], offsets[0].astype(F32)])
    other = send(mine, to_core_partner)
    both = jnp.where(straight, jnp.stack([mine, other]), jnp.stack([other, mine]))
    kx = both[:, :taps_x]
    ky = both[:, taps_x:taps_x + taps_y]
    kz = both[:, taps_x + taps_y:taps_x + taps_y + taps_z]
    shifts = both[:, taps_x + taps_y + taps_z:].astype(jnp.int32)
    tables = make_tables(half, kx, ky, kz, planes, cells_y, cells_z, (own_rows, near, wide))

    first, crossing = lax.optimization_barrier((first, crossing))
    current = jnp.where(straight, window, crossing)
    low = send(current[planes - radius:], to_next)
    high = send(current[:radius], to_previous)
    first = send(first, lambda g, c, q, r: (g, r, q, c))
    second, first = lax.optimization_barrier((second, first))
    second = send(second, lambda g, c, q, r: (g, r, q, 1 - c))
    place = jnp.stack([slab, half])
    blocks = [(send(block, to_next), block, send(block, to_previous)) for block in (first, second)]
    images = [None, None]

    for step in range(ITERS):
        wides = blur_x(tables, low, current, high)
        sides = []
        for order in range(2):
            if step == 0:
                spread, lower, upper, images[order] = first_ratio(
                    shifts, place, blocks[order], wides[order], tables, order, radius, planes * slabs, cells_y
                )
            else:
                spread, lower, upper = next_ratio(images[order], wides[order], tables, order, radius)
            sides.append((send(upper, to_next), spread, send(lower, to_previous)))
        if step < ITERS - 1:
            edge = log_factor(tables, current, sides, inner_rows, edge_rows, 1.0 / groups)
            inner = log_factor(tables, current, sides, 0, inner_rows, 1.0 / groups)
            edge_sum, inner_sum = edge, inner
            for turn in range(1, groups):
                edge_sum = edge_sum + send(edge, lambda g, c, q, r: ((g + turn) % groups, c, q, r))
            for turn in range(1, groups):
                inner_sum = inner_sum + send(inner, lambda g, c, q, r: ((g + turn) % groups, c, q, r))
            edge = jnp.exp(edge_sum)
            beyond = send(edge, to_row_partner)
            beyond = beyond.reshape(planes, edge_rows // GROUP, GROUP, cells_z)[:, ::-1].reshape(edge.shape)
            current = jnp.concatenate([jnp.exp(inner_sum), edge, beyond], axis=1)
            low = send(current[planes - radius:], to_next)
            high = send(current[:radius], to_previous)

    own = log_factor(tables, current, sides, 0, own_rows, 1.0 / groups)
    own_parts, other_parts = [], []
    for turn in range(groups):
        other_parts.append(
            send(own, lambda g, c, q, r: ((g + turn) % groups, c, q, 1 - r) if c != r else None)
        )
        if turn:
            own_parts.append(send(own, lambda g, c, q, r: ((g + turn) % groups, c, q, r) if c == r else None))
    whole = finish(half, own, own_parts, other_parts, estimate.shape)
    copied = send(whole, lambda g, c, q, r: (g, 1 - c, q, r) if c == r else None)
    return jnp.where(straight, whole, copied)


def solution(mesh):
    in_specs = (
        P("view", "tile", None, None),
        P("tile", None, None),
        P("view", None),
        P("view", "tile", None),
        P("view", None),
        P("view", None),
        P("view", None),
    )
    out_specs = P("tile", None, None)
    return jax.shard_map(shards, mesh=mesh, in_specs=in_specs, out_specs=out_specs, check_vma=False)
```

time: 754 us -> 274 us (0.36); the launches traced: 742 us -> 271 us
  waiting for transfers between devices: 388 us -> 123 us
  matrix products: 202 us -> 0 us
  Pallas kernels: 0 us -> 58.6 us
  other arithmetic: 61.4 us -> 7.38 us
  starting transfers between devices: 29.5 us -> 65.3 us
  local copies, waits for them, and re-layouts: 44.5 us -> 15.8 us
  between operations: 17.4 us -> 0.53 us
    dot_general x12 -> x0, matrix products: 202 us -> none  [the longest x4 101 us: spread_planes(): jnp.dot(matrix, flat, precision=lax.Precision.HIGHEST, preferred_element_...]
    ppermute x10 -> x27, waiting for transfers between devices: 241 us -> 123 us  [send(): return lax.ppermute(array, AXES, moves(move))]
    psum x2 -> x0, waiting for transfers between devices: 101 us -> none  [shards(): log_total = lax.psum(log_factor, 'view')]
    pallas_call x0 -> x13, Pallas kernels: none -> 58.6 us  [the longest x2 14.2 us: blur_x(): call(blur_x_kernel, (shape, shape), [VMEM] * 5, 'blur_x')]
    all_gather x2 -> x0, waiting for transfers between devices: 45.7 us -> none  [shards(): rimmed = lax.all_gather(part_rim, 'view', axis=2, tiled=True)]
    add x1 -> x0, other arithmetic: 38.9 us -> none  [band_matrix(): total + jnp.where(delta == tap, kern[tap], jnp.zeros((), kern.dtype))]
    ppermute x10 -> x27, starting transfers between devices: 29.4 us -> 65.3 us  [send(): return lax.ppermute(array, AXES, moves(move))]
    all_gather x2 -> x0, local copies, waits for them, and re-layouts: 13.8 us -> none  [shards(): rimmed = lax.all_gather(part_rim, 'view', axis=2, tiled=True)]
  transfers between devices with their start and end apart: 14 -> 27, of which waited for: 11 -> 17; matrix products, arithmetic and copies ran while one was open for 8% -> 2% of each run, Pallas kernels for 0% -> 13%
where the time goes in v2:
time: 274 us; the launch traced here: 271 us
  waiting for transfers between devices  123 us (45%)
  starting transfers between devices  65.3 us (24%)
  Pallas kernels  58.6 us (21%)
  local copies, waits for them, and re-layouts  15.8 us (6%)
  other arithmetic  7.38 us (3%)
    ppermute x27, waiting for transfers between devices, send(): return lax.ppermute(array, AXES, moves(move))  123 us
    ppermute x27, starting transfers between devices, send(): return lax.ppermute(array, AXES, moves(move))  65.3 us
    pallas_call x2, Pallas kernels, blur_x(): call(blur_x_kernel, (shape, shape), [VMEM] * 5, 'blur_x')  14.2 us
    pallas_call x3, Pallas kernels, log_factor(): call(kernel, shape, [VMEM] * 9, 'log_factor')  12.8 us
    pallas_call x2, Pallas kernels, first_ratio(): call(kernel, out_shape, [SMEM] * 2 + [VMEM] * 8, 'image_and_ratio')  12.8 us
    unnamed x44, local copies, waits for them, and re-layouts  11.1 us
    pallas_call x2, Pallas kernels, next_ratio(): call(kernel, ratio_shapes(wide, tables, radius), [VMEM] * 6, 'ratio')  9.85 us
  transfers between devices with their start and end apart: 27, of which 17 were waited for; matrix products, arithmetic and copies ran while one was open for 2% of the time, Pallas kernels for 13%

profile of v2, /device:TPU:17, one launch (start us, length us, event | category | flops | bytes accessed | tf_op | source)
XLA Modules:
  0.0 270.9 jit_solution(13015646968077702563)
XLA Ops:
  7.3 4.2 %shift_recorded.1 = (f32[17,80,256]{2,1,0:T(8,128)}, f32[17,80,256]{2,1,0:T(8,128)S(1)}) custom-call(s32[3]{0:T(128)S(1)} %pad_add_fusion.scal_ref, f32[16,128,256]{2,1,0:T(8,128)S(1)} %bitcast.16, s32[16,128]{1,0:T(8,128)S(1)} %bitcast.17), custom_call_target="tpu_custom_call" | custom-call | tf_op jit(solution)/shard_map/shift_recorded/pallas_call | solution.py:198
  12.6 13.0 %collective-permute-done.1 = f32[16,96,256]{2,1,0:T(8,128)} collective-permute-done((f32[16,96,256]{2,1,0:T(8,128)}, f32[16,96,256]{2,1,0:T(8,128)}, u32[]{:S(2)}, u32[]{:S(2)}) %collective-permute-start.1) | collective-permute-done | bytes 1572896 | tf_op jit(solution)/shard_map/ppermute | solution.py:33
  25.6 4.8 %collective-permute-start.2 = (f32[17,80,256]{2,1,0:T(8,128)}, f32[17,80,256]{2,1,0:T(8,128)}, u32[]{:S(2)}, u32[]{:S(2)}) collective-permute-start(f32[17,80,256]{2,1,0:T(8,128)} %get-tuple-element.48), channel_id=1, source_target_pairs={{0,0},{1,8},{2,2},{3,10},{4,4},{5,12},{6,6},{7,14},{8,1},{9,9},{10... | collective-permute-start | bytes 4177928 | tf_op jit(solution)/shard_map/ppermute | solution.py:33
  33.8 11.3 %collective-permute-start.5 = (f32[15,96,256]{2,1,0:T(8,128)S(1)}, f32[15,96,256]{2,1,0:T(8,128)S(1)}, u32[]{:S(2)}, u32[]{:S(2)}) collective-permute-start(f32[15,96,256]{2,1,0:T(8,128)S(1)} %get-tuple-element.76), channel_id=1, source_target_pairs={{0,8},{1,9},{2,10},{3,11},{4,12},{5,13},{6,14},{7,15},{8,2},{9,3},... | collective-permute-start | bytes 4423688 | tf_op jit(solution)/shard_map/ppermute | solution.py:33
  45.1 2.1 collective-permute-done.2.own_ref
  47.1 3.8 %collective-permute-start.6 = (f32[15,96,256]{2,1,0:T(8,128)}, f32[15,96,256]{2,1,0:T(8,128)}, u32[]{:S(2)}, u32[]{:S(2)}) collective-permute-start(f32[15,96,256]{2,1,0:T(8,128)} %get-tuple-element.75), channel_id=1, source_target_pairs={{2,8},{3,9},{4,10},{5,11},{6,12},{7,13},{8,0},{9,1},{10,2},{11,3},... | collective-permute-start | bytes 4423688 | tf_op jit(solution)/shard_map/ppermute | solution.py:33
  51.1 4.7 %collective-permute-start.3 = (f32[17,80,256]{2,1,0:T(8,128)}, f32[17,80,256]{2,1,0:T(8,128)}, u32[]{:S(2)}, u32[]{:S(2)}) collective-permute-start(f32[17,80,256]{2,1,0:T(8,128)} %collective-permute-done.2.own_ref), channel_id=1, source_target_pairs={{0,8},{1,9},{2,10},{3,11},{4,12},{5,13},{6,14},{7,15},{8,2},{9,3},... | collective-permute-start | bytes 4177928 | tf_op jit(solution)/shard_map/ppermute | solution.py:33
  55.8 1.9 collective-permute-start.4
  57.7 7.2 %collective-permute-done.9.own_ref = f32[17,80,256]{2,1,0:T(8,128)} collective-permute-done((f32[17,80,256]{2,1,0:T(8,128)S(1)}, f32[17,80,256]{2,1,0:T(8,128)}, u32[]{:S(2)}, u32[]{:S(2)}) %collective-permute-start.9) | collective-permute-done | bytes 1392672 | tf_op jit(solution)/shard_map/ppermute | solution.py:33
  64.9 3.3 %collective-permute-start.10 = (f32[17,80,256]{2,1,0:T(8,128)}, f32[17,80,256]{2,1,0:T(8,128)}, u32[]{:S(2)}, u32[]{:S(2)}) collective-permute-start(f32[17,80,256]{2,1,0:T(8,128)} %collective-permute-done.9.own_ref), channel_id=1, source_target_pairs={{0,8},{1,9},{2,10},{3,11},{4,12},{5,13},{6,14},{7,15},{8,2},{9,3},... | collective-permute-start | bytes 4177928 | tf_op jit(solution)/shard_map/ppermute | solution.py:33
  68.2 1.9 collective-permute-start.11
  70.7 1.7 band_matrices.1
  72.5 7.3 %blur_x.2 = (f32[16,96,256]{2,1,0:T(8,128)S(1)}, f32[16,96,256]{2,1,0:T(8,128)}) custom-call(bf16[2,256,384]{2,1,0:T(8,128)(2,1)S(1)} %get-tuple-element.39.hi_ref, bf16[2,256,384]{2,1,0:T(8,128)(2,1)S(1)} %get-tuple-element.40.lo_ref, f32[15,96,256]{2,1,0:T(8,128)S(1)} %collective-permute-done.5.low_ref, f32[16,96,256]{2,1,0:T(8,128)} %copy-done.14, ...), custom_call_target="tpu_custom_call" | custom-call | tf_op jit(solution)/shard_map/blur_x/pallas_call | solution.py:230
  80.9 3.8 %collective-permute-done.4.high_ref = f32[17,80,256]{2,1,0:T(8,128)} collective-permute-done((f32[17,80,256]{2,1,0:T(8,128)}, f32[17,80,256]{2,1,0:T(8,128)}, u32[]{:S(2)}, u32[]{:S(2)}) %collective-permute-start.4) | collective-permute-done | bytes 1392672 | tf_op jit(solution)/shard_map/ppermute | solution.py:33
  84.7 6.4 %image_and_ratio.2 = (f32[16,64,256]{2,1,0:T(8,128)S(1)}, f32[15,64,256]{2,1,0:T(8,128)S(1)}, f32[15,64,256]{2,1,0:T(8,128)S(1)}, f32[16,80,256]{2,1,0:T(8,128)S(1)}) custom-call(s32[2,3]{1,0:T(2,128)S(1)} %slice_convert_fusion.shift_ref, s32[2]{0:T(128)S(1)} %pad_add_fusion.1.place_ref, f32[17,80,256]{2,1,0:T(8,128)} %collective-permute-done.3.low_ref, ...), custom_call_target="tpu_custom_call" | custom-call | tf_op jit(solution)/shard_map/image_and_ratio/pallas_call | solution.py:325
  91.2 1.9 collective-permute-start.7
  93.1 2.4 collective-permute-start.8
  95.5 4.0 %collective-permute-done.11.high_ref = f32[17,80,256]{2,1,0:T(8,128)} collective-permute-done((f32[17,80,256]{2,1,0:T(8,128)}, f32[17,80,256]{2,1,0:T(8,128)}, u32[]{:S(2)}, u32[]{:S(2)}) %collective-permute-start.11) | collective-permute-done | bytes 1392672 | tf_op jit(solution)/shard_map/ppermute | solution.py:33
  99.5 6.4 %image_and_ratio.3 = (f32[16,64,256]{2,1,0:T(8,128)S(1)}, f32[15,64,256]{2,1,0:T(8,128)S(1)}, f32[15,64,256]{2,1,0:T(8,128)S(1)}, f32[16,80,256]{2,1,0:T(8,128)S(1)}) custom-call(s32[2,3]{1,0:T(2,128)S(1)} %slice_convert_fusion.shift_ref, s32[2]{0:T(128)S(1)} %pad_add_fusion.1.place_ref, f32[17,80,256]{2,1,0:T(8,128)} %collective-permute-done.10.low_ref, ...), custom_call_target="tpu_custom_call" | custom-call | tf_op jit(solution)/shard_map/image_and_ratio/pallas_call | solution.py:325
  108.0 1.9 collective-permute-start.12
  110.0 2.4 collective-permute-start.13
  112.4 8.6 %collective-permute-done.12.refs_3_ = f32[15,64,256]{2,1,0:T(8,128)S(1)} collective-permute-done((f32[15,64,256]{2,1,0:T(8,128)S(1)}, f32[15,64,256]{2,1,0:T(8,128)S(1)}, u32[]{:S(2)}, u32[]{:S(2)}) %collective-permute-start.12) | collective-permute-done | bytes 983072 | tf_op jit(solution)/shard_map/ppermute | solution.py:33
  121.0 4.4 %collective-permute-done.13.refs_5_ = f32[15,64,256]{2,1,0:T(8,128)S(1)} collective-permute-done((f32[15,64,256]{2,1,0:T(8,128)S(1)}, f32[15,64,256]{2,1,0:T(8,128)S(1)}, u32[]{:S(2)}, u32[]{:S(2)}) %collective-permute-start.13) | collective-permute-done | bytes 983072 | tf_op jit(solution)/shard_map/ppermute | solution.py:33
  125.4 3.7 %log_factor.4 = f32[16,32,256]{2,1,0:T(8,128)S(1)} custom-call(bf16[2,256,384]{2,1,0:T(8,128)(2,1)S(1)} %get-tuple-element.39.hi_ref, bf16[2,256,384]{2,1,0:T(8,128)(2,1)S(1)} %get-tuple-element.40.lo_ref, f32[16,96,256]{2,1,0:T(8,128)} %copy-done.14, f32[15,64,256]{2,1,0:T(8,128)S(1)} %collective-permute-done.7.refs_0_, f32[16,64,256]{2,1,0:T(8,128)} %copy-done, ...), custom_call_target="tpu_custom_call" | custom-call | tf_op jit(solution)/shard_map/log_factor/pallas_call | solution.py:355
  130.4 3.7 %log_factor.3 = f32[16,32,256]{2,1,0:T(8,128)S(1)} custom-call(bf16[2,256,384]{2,1,0:T(8,128)(2,1)S(1)} %get-tuple-element.39.hi_ref, bf16[2,256,384]{2,1,0:T(8,128)(2,1)S(1)} %get-tuple-element.40.lo_ref, f32[16,96,256]{2,1,0:T(8,128)} %copy-done.14, f32[15,64,256]{2,1,0:T(8,128)S(1)} %collective-permute-done.7.refs_0_, f32[16,64,256]{2,1,0:T(8,128)} %copy-done, ...), custom_call_target="tpu_custom_call" | custom-call | tf_op jit(solution)/shard_map/log_factor/pallas_call | solution.py:355
  134.4 8.6 %collective-permute-done.15 = f32[16,32,256]{2,1,0:T(8,128)S(1)} collective-permute-done((f32[16,32,256]{2,1,0:T(8,128)S(1)}, f32[16,32,256]{2,1,0:T(8,128)S(1)}, u32[]{:S(2)}, u32[]{:S(2)}) %collective-permute-start.15) | collective-permute-done | bytes 524320 | tf_op jit(solution)/shard_map/ppermute | solution.py:33
  143.3 10.1 %collective-permute-done.14 = f32[16,32,256]{2,1,0:T(8,128)S(1)} collective-permute-done((f32[16,32,256]{2,1,0:T(8,128)S(1)}, f32[16,32,256]{2,1,0:T(8,128)S(1)}, u32[]{:S(2)}, u32[]{:S(2)}) %collective-permute-start.14) | collective-permute-done | bytes 524320 | tf_op jit(solution)/shard_map/ppermute | solution.py:33
  154.4 1.7 collective-permute-done.16
  156.8 1.9 rev.11
  161.4 1.9 collective-permute-start.17
  163.3 2.7 %collective-permute-start.18 = (f32[15,96,256]{2,1,0:T(8,128)S(1)}, f32[15,96,256]{2,1,0:T(8,128)S(1)}, u32[]{:S(2)}, u32[]{:S(2)}) collective-permute-start(f32[15,96,256]{2,1,0:T(8,128)S(1)} %get-tuple-element.73), channel_id=1, source_target_pairs={{2,8},{3,9},{4,10},{5,11},{6,12},{7,13},{8,0},{9,1},{10,2},{11,3},... | collective-permute-start | bytes 4423688 | tf_op jit(solution)/shard_map/ppermute | solution.py:33
  166.0 13.5 %collective-permute-done.17.low_ref = f32[15,96,256]{2,1,0:T(8,128)S(1)} collective-permute-done((f32[15,96,256]{2,1,0:T(8,128)S(1)}, f32[15,96,256]{2,1,0:T(8,128)S(1)}, u32[]{:S(2)}, u32[]{:S(2)}) %collective-permute-start.17) | collective-permute-done | bytes 1474592 | tf_op jit(solution)/shard_map/ppermute | solution.py:33
  179.6 4.5 %collective-permute-done.18.high_ref = f32[15,96,256]{2,1,0:T(8,128)S(1)} collective-permute-done((f32[15,96,256]{2,1,0:T(8,128)S(1)}, f32[15,96,256]{2,1,0:T(8,128)S(1)}, u32[]{:S(2)}, u32[]{:S(2)}) %collective-permute-start.18) | collective-permute-done | bytes 1474592 | tf_op jit(solution)/shard_map/ppermute | solution.py:33
  184.1 6.9 %blur_x.3 = (f32[16,96,256]{2,1,0:T(8,128)S(1)}, f32[16,96,256]{2,1,0:T(8,128)}) custom-call(bf16[2,256,384]{2,1,0:T(8,128)(2,1)S(1)} %get-tuple-element.39.hi_ref, bf16[2,256,384]{2,1,0:T(8,128)(2,1)S(1)} %get-tuple-element.40.lo_ref, f32[15,96,256]{2,1,0:T(8,128)S(1)} %collective-permute-done.17.low_ref, f32[16,96,256]{2,1,0:T(8,128)} %copy-done.15, ...), custom_call_target="tpu_custom_call" | custom-call | tf_op jit(solution)/shard_map/blur_x/pallas_call | solution.py:230
  192.2 4.9 %ratio.3 = (f32[16,64,256]{2,1,0:T(8,128)S(1)}, f32[15,64,256]{2,1,0:T(8,128)S(1)}, f32[15,64,256]{2,1,0:T(8,128)S(1)}) custom-call(f32[16,80,256]{2,1,0:T(8,128)S(1)} %copy-done.8, f32[16,96,256]{2,1,0:T(8,128)} %get-tuple-element.69.wide_ref, bf16[2,80,384]{2,1,0:T(8,128)(2,1)S(1)} %get-tuple-element.51.yf_ref, ...), custom_call_target="tpu_custom_call" | custom-call | tf_op jit(solution)/shard_map/ratio/pallas_call | solution.py:332
  197.1 1.9 collective-permute-start.21
  199.1 2.4 collective-permute-start.22
  201.5 4.9 %ratio.2 = (f32[16,64,256]{2,1,0:T(8,128)S(1)}, f32[15,64,256]{2,1,0:T(8,128)S(1)}, f32[15,64,256]{2,1,0:T(8,128)S(1)}) custom-call(f32[16,80,256]{2,1,0:T(8,128)S(1)} %get-tuple-element.63.image_ref, f32[16,96,256]{2,1,0:T(8,128)} %copy-done.5, bf16[2,80,384]{2,1,0:T(8,128)(2,1)S(1)} %get-tuple-element.51.yf_ref, ...), custom_call_target="tpu_custom_call" | custom-call | tf_op jit(solution)/shard_map/ratio/pallas_call | solution.py:332
  207.4 3.1 %collective-permute-start.19 = (f32[15,64,256]{2,1,0:T(8,128)S(1)}, f32[15,64,256]{2,1,0:T(8,128)S(1)}, u32[]{:S(2)}, u32[]{:S(2)}) collective-permute-start(f32[15,64,256]{2,1,0:T(8,128)S(1)} %get-tuple-element.65), channel_id=1, source_target_pairs={{0,8},{1,9},{2,10},{3,11},{4,12},{5,13},{6,14},{7,15},{8,2},{9,3},... | collective-permute-start | bytes 2949128 | tf_op jit(solution)/shard_map/ppermute | solution.py:33
  210.6 1.9 collective-permute-start.20
  212.5 2.2 collective-permute-done.22.refs_5_
  214.8 6.8 %collective-permute-done.19.refs_0_ = f32[15,64,256]{2,1,0:T(8,128)S(1)} collective-permute-done((f32[15,64,256]{2,1,0:T(8,128)S(1)}, f32[15,64,256]{2,1,0:T(8,128)S(1)}, u32[]{:S(2)}, u32[]{:S(2)}) %collective-permute-start.19) | collective-permute-done | bytes 983072 | tf_op jit(solution)/shard_map/ppermute | solution.py:33
  221.6 4.4 %collective-permute-done.20.refs_2_ = f32[15,64,256]{2,1,0:T(8,128)S(1)} collective-permute-done((f32[15,64,256]{2,1,0:T(8,128)S(1)}, f32[15,64,256]{2,1,0:T(8,128)S(1)}, u32[]{:S(2)}, u32[]{:S(2)}) %collective-permute-start.20) | collective-permute-done | bytes 983072 | tf_op jit(solution)/shard_map/ppermute | solution.py:33
  226.0 5.4 %log_factor.5.own_ref = f32[16,64,256]{2,1,0:T(8,128)S(1)} custom-call(bf16[2,256,384]{2,1,0:T(8,128)(2,1)S(1)} %get-tuple-element.39.hi_ref, bf16[2,256,384]{2,1,0:T(8,128)(2,1)S(1)} %get-tuple-element.40.lo_ref, f32[16,96,256]{2,1,0:T(8,128)} %copy-done.15, f32[15,64,256]{2,1,0:T(8,128)S(1)} %collective-permute-done.19.refs_0_, f32[16,64,256]{2,1,0:T(8,128)} %copy-done.10, ...), custom_call_target="tpu_custom_call" | custom-call | tf_op jit(solution)/shard_map/log_factor/pallas_call | solution.py:355
  232.1 4.4 %collective-permute-start.24 = (f32[16,64,256]{2,1,0:T(8,128)S(1)}, f32[16,64,256]{2,1,0:T(8,128)S(1)}, u32[]{:S(2)}, u32[]{:S(2)}) collective-permute-start(f32[16,64,256]{2,1,0:T(8,128)S(1)} %log_factor.5.own_ref), channel_id=1, source_target_pairs={{1,0},{3,2},{5,4},{7,6},{8,9},{10,11},{12,13},{14,15},{17,16},{19,... | collective-permute-start | bytes 3145736 | tf_op jit(solution)/shard_map/ppermute | solution.py:33
  238.0 21.5 %collective-permute-done.24.refs_1_ = f32[16,64,256]{2,1,0:T(8,128)S(1)} collective-permute-done((f32[16,64,256]{2,1,0:T(8,128)S(1)}, f32[16,64,256]{2,1,0:T(8,128)S(1)}, u32[]{:S(2)}, u32[]{:S(2)}) %collective-permute-start.24) | collective-permute-done | bytes 1048608 | tf_op jit(solution)/shard_map/ppermute | solution.py:33
  262.4 6.8 %collective-permute-done.26 = f32[16,128,256]{2,1,0:T(8,128)S(1)} collective-permute-done((f32[16,128,256]{2,1,0:T(8,128)}, f32[16,128,256]{2,1,0:T(8,128)S(1)}, u32[]{:S(2)}, u32[]{:S(2)}) %collective-permute-start.26) | collective-permute-done | bytes 2097184 | tf_op jit(solution)/shard_map/ppermute | solution.py:33
  269.2 1.7 broadcast_select_fusion
  (85 shorter events, 28.9 us)
Async XLA Ops:
  0.0 5.4 %copy-start.18 = (s32[1,3]{1,0:T(1,128)S(1)}, s32[1,3]{1,0:T(1,128)}, u32[]{:S(2)}) copy-start(s32[1,3]{1,0:T(1,128)} %param.9) | copy-start | bytes 40
  0.0 7.3 %copy-start.11 = (s32[1,16,128]{2,1,0:T(8,128)S(1)}, s32[1,16,128]{2,1,0:T(8,128)}, u32[]{:S(2)}) copy-start(s32[1,16,128]{2,1,0:T(8,128)} %param.10) | copy-start | bytes 24580
  0.0 1.6 copy-start.2
  1.6 5.7 %copy-start.3 = (f32[1,16,128,256]{3,2,1,0:T(8,128)S(1)}, f32[1,16,128,256]{3,2,1,0:T(8,128)}, u32[]{:S(2)}) copy-start(f32[1,16,128,256]{3,2,1,0:T(8,128)} %param.7) | copy-start | bytes 6291460
  3.0 1.2 copy-start.4
  4.1 21.5 %collective-permute-start.1 = (f32[16,96,256]{2,1,0:T(8,128)}, f32[16,96,256]{2,1,0:T(8,128)}, u32[]{:S(2)}, u32[]{:S(2)}) collective-permute-start(f32[16,96,256]{2,1,0:T(8,128)} %get-tuple-element.45), channel_id=1, source_target_pairs={{0,1},{2,3},{4,5},{6,7},{9,8},{11,10},{13,12},{15,14},{16,17},{18,... | collective-permute-start | bytes 4718600 | tf_op jit(solution)/shard_map/ppermute | solution.py:33
  11.5 1.1 copy-start.12
  25.6 21.5 %collective-permute-start.2 = (f32[17,80,256]{2,1,0:T(8,128)}, f32[17,80,256]{2,1,0:T(8,128)}, u32[]{:S(2)}, u32[]{:S(2)}) collective-permute-start(f32[17,80,256]{2,1,0:T(8,128)} %get-tuple-element.48), channel_id=1, source_target_pairs={{0,0},{1,8},{2,2},{3,10},{4,4},{5,12},{6,6},{7,14},{8,1},{9,9},{10... | collective-permute-start | bytes 4177928 | tf_op jit(solution)/shard_map/ppermute | solution.py:33
  32.1 1.6 copy-start.14
  32.1 15.0 %copy-start.13 = (f32[17,80,256]{2,1,0:T(8,128)S(1)}, f32[17,80,256]{2,1,0:T(8,128)}, u32[]{:S(2)}) copy-start(f32[17,80,256]{2,1,0:T(8,128)} %copy-done.12) | copy-start | bytes 4177924
  32.1 18.8 %copy-start.19 = (f32[1,61]{1,0:T(1,128)S(1)}, f32[1,61]{1,0:T(1,128)}, u32[]{:S(2)}) copy-start(f32[1,61]{1,0:T(1,128)} %param.13) | copy-start | bytes 736
  32.2 18.8 %copy-start.20 = (f32[1,31]{1,0:T(1,128)S(1)}, f32[1,31]{1,0:T(1,128)}, u32[]{:S(2)}) copy-start(f32[1,31]{1,0:T(1,128)} %param.12) | copy-start | bytes 376
  32.2 18.8 %copy-start.21 = (f32[1,31]{1,0:T(1,128)S(1)}, f32[1,31]{1,0:T(1,128)}, u32[]{:S(2)}) copy-start(f32[1,31]{1,0:T(1,128)} %param.11) | copy-start | bytes 376
  33.8 34.4 %collective-permute-start.5 = (f32[15,96,256]{2,1,0:T(8,128)S(1)}, f32[15,96,256]{2,1,0:T(8,128)S(1)}, u32[]{:S(2)}, u32[]{:S(2)}) collective-permute-start(f32[15,96,256]{2,1,0:T(8,128)S(1)} %get-tuple-element.76), channel_id=1, source_target_pairs={{0,8},{1,9},{2,10},{3,11},{4,12},{5,13},{6,14},{7,15},{8,2},{9,3},... | collective-permute-start | bytes 4423688 | tf_op jit(solution)/shard_map/ppermute | solution.py:33
  47.1 17.7 %collective-permute-start.9 = (f32[17,80,256]{2,1,0:T(8,128)S(1)}, f32[17,80,256]{2,1,0:T(8,128)}, u32[]{:S(2)}, u32[]{:S(2)}) collective-permute-start(f32[17,80,256]{2,1,0:T(8,128)S(1)} %copy-done.13), channel_id=1, source_target_pairs={{0,1},{1,9},{2,3},{3,11},{4,5},{5,13},{6,7},{7,15},{8,0},{9,8},{10... | collective-permute-start | bytes 4177928 | tf_op jit(solution)/shard_map/ppermute | solution.py:33
  47.1 25.3 %collective-permute-start.6 = (f32[15,96,256]{2,1,0:T(8,128)}, f32[15,96,256]{2,1,0:T(8,128)}, u32[]{:S(2)}, u32[]{:S(2)}) collective-permute-start(f32[15,96,256]{2,1,0:T(8,128)} %get-tuple-element.75), channel_id=1, source_target_pairs={{2,8},{3,9},{4,10},{5,11},{6,12},{7,13},{8,0},{9,1},{10,2},{11,3},... | collective-permute-start | bytes 4423688 | tf_op jit(solution)/shard_map/ppermute | solution.py:33
  51.1 4.7 %collective-permute-start = (f32[126]{0:T(128)S(1)}, f32[126]{0:T(128)S(1)}, u32[]{:S(2)}, u32[]{:S(2)}) collective-permute-start(f32[126]{0:T(128)S(1)} %pad_maximum_fusion.2), channel_id=1, source_target_pairs={{0,8},{1,9},{2,10},{3,11},{4,12},{5,13},{6,14},{7,15},{8,0},{9,1},... | collective-permute-start | bytes 1520 | tf_op jit(solution)/shard_map/ppermute | solution.py:33
  51.1 29.8 %collective-permute-start.3 = (f32[17,80,256]{2,1,0:T(8,128)}, f32[17,80,256]{2,1,0:T(8,128)}, u32[]{:S(2)}, u32[]{:S(2)}) collective-permute-start(f32[17,80,256]{2,1,0:T(8,128)} %collective-permute-done.2.own_ref), channel_id=1, source_target_pairs={{0,8},{1,9},{2,10},{3,11},{4,12},{5,13},{6,14},{7,15},{8,2},{9,3},... | collective-permute-start | bytes 4177928 | tf_op jit(solution)/shard_map/ppermute | solution.py:33
  55.8 28.9 %collective-permute-start.4 = (f32[17,80,256]{2,1,0:T(8,128)}, f32[17,80,256]{2,1,0:T(8,128)}, u32[]{:S(2)}, u32[]{:S(2)}) collective-permute-start(f32[17,80,256]{2,1,0:T(8,128)} %collective-permute-done.2.own_ref), channel_id=1, source_target_pairs={{2,8},{3,9},{4,10},{5,11},{6,12},{7,13},{8,0},{9,1},{10,2},{11,3},... | collective-permute-start | bytes 4177928 | tf_op jit(solution)/shard_map/ppermute | solution.py:33
  64.9 30.6 %collective-permute-start.10 = (f32[17,80,256]{2,1,0:T(8,128)}, f32[17,80,256]{2,1,0:T(8,128)}, u32[]{:S(2)}, u32[]{:S(2)}) collective-permute-start(f32[17,80,256]{2,1,0:T(8,128)} %collective-permute-done.9.own_ref), channel_id=1, source_target_pairs={{0,8},{1,9},{2,10},{3,11},{4,12},{5,13},{6,14},{7,15},{8,2},{9,3},... | collective-permute-start | bytes 4177928 | tf_op jit(solution)/shard_map/ppermute | solution.py:33
  68.2 31.4 %collective-permute-start.11 = (f32[17,80,256]{2,1,0:T(8,128)}, f32[17,80,256]{2,1,0:T(8,128)}, u32[]{:S(2)}, u32[]{:S(2)}) collective-permute-start(f32[17,80,256]{2,1,0:T(8,128)} %collective-permute-done.9.own_ref), channel_id=1, source_target_pairs={{2,8},{3,9},{4,10},{5,11},{6,12},{7,13},{8,0},{9,1},{10,2},{11,3},... | collective-permute-start | bytes 4177928 | tf_op jit(solution)/shard_map/ppermute | solution.py:33
  79.8 1.1 copy-start.6
  91.1 14.8 %copy-start = (f32[16,64,256]{2,1,0:T(8,128)}, f32[16,64,256]{2,1,0:T(8,128)S(1)}, u32[]{:S(2)}) copy-start(f32[16,64,256]{2,1,0:T(8,128)S(1)} %get-tuple-element.56.refs_1_) | copy-start | bytes 3145732
  91.2 21.2 %collective-permute-start.7 = (f32[15,64,256]{2,1,0:T(8,128)S(1)}, f32[15,64,256]{2,1,0:T(8,128)S(1)}, u32[]{:S(2)}, u32[]{:S(2)}) collective-permute-start(f32[15,64,256]{2,1,0:T(8,128)S(1)} %get-tuple-element.55), channel_id=1, source_target_pairs={{0,8},{1,9},{2,10},{3,11},{4,12},{5,13},{6,14},{7,15},{8,2},{9,3},... | collective-permute-start | bytes 2949128 | tf_op jit(solution)/shard_map/ppermute | solution.py:33
  93.1 19.3 %collective-permute-start.8 = (f32[15,64,256]{2,1,0:T(8,128)S(1)}, f32[15,64,256]{2,1,0:T(8,128)S(1)}, u32[]{:S(2)}, u32[]{:S(2)}) collective-permute-start(f32[15,64,256]{2,1,0:T(8,128)S(1)} %get-tuple-element.57), channel_id=1, source_target_pairs={{2,8},{3,9},{4,10},{5,11},{6,12},{7,13},{8,0},{9,1},{10,2},{11,3},... | collective-permute-start | bytes 2949128 | tf_op jit(solution)/shard_map/ppermute | solution.py:33
  106.0 1.0 copy-start.1
  107.0 1.0 copy-start.7
  108.0 12.9 %collective-permute-start.12 = (f32[15,64,256]{2,1,0:T(8,128)S(1)}, f32[15,64,256]{2,1,0:T(8,128)S(1)}, u32[]{:S(2)}, u32[]{:S(2)}) collective-permute-start(f32[15,64,256]{2,1,0:T(8,128)S(1)} %get-tuple-element.60), channel_id=1, source_target_pairs={{0,8},{1,9},{2,10},{3,11},{4,12},{5,13},{6,14},{7,15},{8,2},{9,3},... | collective-permute-start | bytes 2949128 | tf_op jit(solution)/shard_map/ppermute | solution.py:33
  110.0 15.4 %collective-permute-start.13 = (f32[15,64,256]{2,1,0:T(8,128)S(1)}, f32[15,64,256]{2,1,0:T(8,128)S(1)}, u32[]{:S(2)}, u32[]{:S(2)}) collective-permute-start(f32[15,64,256]{2,1,0:T(8,128)S(1)} %get-tuple-element.62), channel_id=1, source_target_pairs={{2,8},{3,9},{4,10},{5,11},{6,12},{7,13},{8,0},{9,1},{10,2},{11,3},... | collective-permute-start | bytes 2949128 | tf_op jit(solution)/shard_map/ppermute | solution.py:33
  129.1 14.0 %collective-permute-start.15 = (f32[16,32,256]{2,1,0:T(8,128)S(1)}, f32[16,32,256]{2,1,0:T(8,128)S(1)}, u32[]{:S(2)}, u32[]{:S(2)}) collective-permute-start(f32[16,32,256]{2,1,0:T(8,128)S(1)} %log_factor.4), channel_id=1, source_target_pairs={{0,16},{1,17},{2,18},{3,19},{4,20},{5,21},{6,22},{7,23},{8,24},{9,... | collective-permute-start | bytes 1572872 | tf_op jit(solution)/shard_map/ppermute | solution.py:33
  134.1 19.3 %collective-permute-start.14 = (f32[16,32,256]{2,1,0:T(8,128)S(1)}, f32[16,32,256]{2,1,0:T(8,128)S(1)}, u32[]{:S(2)}, u32[]{:S(2)}) collective-permute-start(f32[16,32,256]{2,1,0:T(8,128)S(1)} %log_factor.3), channel_id=1, source_target_pairs={{0,16},{1,17},{2,18},{3,19},{4,20},{5,21},{6,22},{7,23},{8,24},{9,... | collective-permute-start | bytes 1572872 | tf_op jit(solution)/shard_map/ppermute | solution.py:33
  143.2 11.2 %copy-start.16 = (f32[16,32,256]{2,1,0:T(8,128)}, f32[16,32,256]{2,1,0:T(8,128)S(1)}, u32[]{:S(2)}) copy-start(f32[16,32,256]{2,1,0:T(8,128)S(1)} %add_exponential_fusion) | copy-start | bytes 1572868
  143.2 12.9 %collective-permute-start.16 = (f32[16,32,256]{2,1,0:T(8,128)S(1)}, f32[16,32,256]{2,1,0:T(8,128)S(1)}, u32[]{:S(2)}, u32[]{:S(2)}) collective-permute-start(f32[16,32,256]{2,1,0:T(8,128)S(1)} %add_exponential_fusion), channel_id=1, source_target_pairs={{0,1},{1,0},{2,3},{3,2},{4,5},{5,4},{6,7},{7,6},{8,9},{9,8},{10,11... | collective-permute-start | bytes 1572872 | tf_op jit(solution)/shard_map/ppermute | solution.py:33
  160.2 1.1 copy-start.15
  161.4 18.2 %collective-permute-start.17 = (f32[15,96,256]{2,1,0:T(8,128)S(1)}, f32[15,96,256]{2,1,0:T(8,128)S(1)}, u32[]{:S(2)}, u32[]{:S(2)}) collective-permute-start(f32[15,96,256]{2,1,0:T(8,128)S(1)} %get-tuple-element.74), channel_id=1, source_target_pairs={{0,8},{1,9},{2,10},{3,11},{4,12},{5,13},{6,14},{7,15},{8,2},{9,3},... | collective-permute-start | bytes 4423688 | tf_op jit(solution)/shard_map/ppermute | solution.py:33
  163.3 28.9 %copy-start.8 = (f32[16,80,256]{2,1,0:T(8,128)S(1)}, f32[16,80,256]{2,1,0:T(8,128)}, u32[]{:S(2)}) copy-start(f32[16,80,256]{2,1,0:T(8,128)} %copy-done.7) | copy-start | bytes 3932164
  163.3 20.8 %collective-permute-start.18 = (f32[15,96,256]{2,1,0:T(8,128)S(1)}, f32[15,96,256]{2,1,0:T(8,128)S(1)}, u32[]{:S(2)}, u32[]{:S(2)}) collective-permute-start(f32[15,96,256]{2,1,0:T(8,128)S(1)} %get-tuple-element.73), channel_id=1, source_target_pairs={{2,8},{3,9},{4,10},{5,11},{6,12},{7,13},{8,0},{9,1},{10,2},{11,3},... | collective-permute-start | bytes 4423688 | tf_op jit(solution)/shard_map/ppermute | solution.py:33
  191.0 1.2 copy-start.5
  197.1 9.3 %copy-start.9 = (f32[16,64,256]{2,1,0:T(8,128)}, f32[16,64,256]{2,1,0:T(8,128)S(1)}, u32[]{:S(2)}) copy-start(f32[16,64,256]{2,1,0:T(8,128)S(1)} %get-tuple-element.71.refs_4_) | copy-start | bytes 3145732
  197.1 15.4 %collective-permute-start.21 = (f32[15,64,256]{2,1,0:T(8,128)S(1)}, f32[15,64,256]{2,1,0:T(8,128)S(1)}, u32[]{:S(2)}, u32[]{:S(2)}) collective-permute-start(f32[15,64,256]{2,1,0:T(8,128)S(1)} %get-tuple-element.70), channel_id=1, source_target_pairs={{0,8},{1,9},{2,10},{3,11},{4,12},{5,13},{6,14},{7,15},{8,2},{9,3},... | collective-permute-start | bytes 2949128 | tf_op jit(solution)/shard_map/ppermute | solution.py:33
  199.1 15.7 %collective-permute-start.22 = (f32[15,64,256]{2,1,0:T(8,128)S(1)}, f32[15,64,256]{2,1,0:T(8,128)S(1)}, u32[]{:S(2)}, u32[]{:S(2)}) collective-permute-start(f32[15,64,256]{2,1,0:T(8,128)S(1)} %get-tuple-element.72), channel_id=1, source_target_pairs={{2,8},{3,9},{4,10},{5,11},{6,12},{7,13},{8,0},{9,1},{10,2},{11,3},... | collective-permute-start | bytes 2949128 | tf_op jit(solution)/shard_map/ppermute | solution.py:33
  206.4 1.0 copy-start.10
  207.4 14.2 %collective-permute-start.19 = (f32[15,64,256]{2,1,0:T(8,128)S(1)}, f32[15,64,256]{2,1,0:T(8,128)S(1)}, u32[]{:S(2)}, u32[]{:S(2)}) collective-permute-start(f32[15,64,256]{2,1,0:T(8,128)S(1)} %get-tuple-element.65), channel_id=1, source_target_pairs={{0,8},{1,9},{2,10},{3,11},{4,12},{5,13},{6,14},{7,15},{8,2},{9,3},... | collective-permute-start | bytes 2949128 | tf_op jit(solution)/shard_map/ppermute | solution.py:33
  210.6 15.4 %collective-permute-start.20 = (f32[15,64,256]{2,1,0:T(8,128)S(1)}, f32[15,64,256]{2,1,0:T(8,128)S(1)}, u32[]{:S(2)}, u32[]{:S(2)}) collective-permute-start(f32[15,64,256]{2,1,0:T(8,128)S(1)} %get-tuple-element.67), channel_id=1, source_target_pairs={{2,8},{3,9},{4,10},{5,11},{6,12},{7,13},{8,0},{9,1},{10,2},{11,3},... | collective-permute-start | bytes 2949128 | tf_op jit(solution)/shard_map/ppermute | solution.py:33
  231.4 6.6 %collective-permute-start.23 = (f32[16,64,256]{2,1,0:T(8,128)S(1)}, f32[16,64,256]{2,1,0:T(8,128)S(1)}, u32[]{:S(2)}, u32[]{:S(2)}) collective-permute-start(f32[16,64,256]{2,1,0:T(8,128)S(1)} %log_factor.5.own_ref), channel_id=1, source_target_pairs={{0,16},{2,18},{4,20},{6,22},{9,25},{11,27},{13,29},{15,31},{16,0},... | collective-permute-start | bytes 3145736 | tf_op jit(solution)/shard_map/ppermute | solution.py:33
  232.1 27.3 %collective-permute-start.24 = (f32[16,64,256]{2,1,0:T(8,128)S(1)}, f32[16,64,256]{2,1,0:T(8,128)S(1)}, u32[]{:S(2)}, u32[]{:S(2)}) collective-permute-start(f32[16,64,256]{2,1,0:T(8,128)S(1)} %log_factor.5.own_ref), channel_id=1, source_target_pairs={{1,0},{3,2},{5,4},{7,6},{8,9},{10,11},{12,13},{14,15},{17,16},{19,... | collective-permute-start | bytes 3145736 | tf_op jit(solution)/shard_map/ppermute | solution.py:33
  236.6 22.9 %collective-permute-start.25 = (f32[16,64,256]{2,1,0:T(8,128)S(1)}, f32[16,64,256]{2,1,0:T(8,128)S(1)}, u32[]{:S(2)}, u32[]{:S(2)}) collective-permute-start(f32[16,64,256]{2,1,0:T(8,128)S(1)} %log_factor.5.own_ref), channel_id=1, source_target_pairs={{1,16},{3,18},{5,20},{7,22},{8,25},{10,27},{12,29},{14,31},{17,0},... | collective-permute-start | bytes 3145736 | tf_op jit(solution)/shard_map/ppermute | solution.py:33
  261.1 8.1 %collective-permute-start.26 = (f32[16,128,256]{2,1,0:T(8,128)}, f32[16,128,256]{2,1,0:T(8,128)S(1)}, u32[]{:S(2)}, u32[]{:S(2)}) collective-permute-start(f32[16,128,256]{2,1,0:T(8,128)} %update.1), channel_id=1, source_target_pairs={{0,8},{2,10},{4,12},{6,14},{9,1},{11,3},{13,5},{15,7},{16,24},{18,... | collective-permute-start | bytes 6291464 | tf_op jit(solution)/shard_map/ppermute | solution.py:33
  (1 other events, 0.8 us)

commit v3 on v2

--- a/solution.py
+++ b/solution.py
@@ -13,7 +13,7 @@
 BF16 = jnp.bfloat16
 VMEM = pl.BlockSpec(memory_space=pltpu.VMEM)
 SMEM = pl.BlockSpec(memory_space=pltpu.SMEM)
-PARAMS = pltpu.CompilerParams(vmem_limit_bytes=48 * 1024 * 1024)
+PARAMS = pltpu.CompilerParams(vmem_limit_bytes=20 * 1024 * 1024)
 GROUP = 16
 
 
@@ -71,6 +71,15 @@
 def global_row(half, local, cells_y):
     group = local // GROUP
     return group_row(half, group, cells_y) + (local - group * GROUP)
+
+
+def wide_local(place, own, wide):
+    group = (place - own) // GROUP
+    return own + (wide - own) - GROUP - group * GROUP + (place - own - group * GROUP)
+
+
+def wide_group(group, own_groups, groups):
+    return group if group < own_groups else own_groups + groups - 1 - group
 
 
 def pad_to(value, unit):
@@ -102,7 +111,8 @@
         lanes = out_ref.shape[2]
         row = global_row(half, iota((rows, lanes), 0), cells_y)
         lane = iota((rows, lanes), 1)
-        col = global_row(half, lane, cells_y)
+        turned = lane if adjoint else jnp.where(lane < own, lane, wide_local(lane, own, wide))
+        col = global_row(half, turned, cells_y)
         delta = (row - col if adjoint else col - row) + radius
         delta = jnp.where(lane < width, delta, -1)
         band = jnp.zeros((rows, lanes), F32)
@@ -153,9 +163,11 @@
 def window_kernel(half_ref, estimate_ref, own_ref, other_ref):
     cells_y = estimate_ref.shape[1]
     half = half_ref[0]
+    groups = own_ref.shape[1] // GROUP
     for side, out_ref in ((half, own_ref), (1 - half, other_ref)):
-        for group in range(out_ref.shape[1] // GROUP):
-            start = pl.multiple_of(group_row(side, group, cells_y), GROUP)
+        for group in range(groups):
+            local = wide_group(group, cells_y // 2 // GROUP, groups)
+            start = pl.multiple_of(group_row(side, local, cells_y), GROUP)
             out_ref[:, group * GROUP:(group + 1) * GROUP, :] = estimate_ref[:, pl.ds(start, GROUP), :]
 
 
@@ -163,6 +175,33 @@
     planes, _, cells_z = estimate.shape
     shape = jax.ShapeDtypeStruct((planes, wide, cells_z), F32)
     return call(window_kernel, (shape, shape), [SMEM, VMEM], "estimate_windows")(half.reshape(1), estimate)
+
+
+def assemble_kernel(place_ref, window_ref, *refs):
+    pieces, (out_ref, lower_ref, upper_ref) = refs[:-3], refs[-3:]
+    straight, group = place_ref[0] != 0, place_ref[1]
+    planes, radius, share = out_ref.shape[0], lower_ref.shape[0], pieces[0].shape[0]
+    for p in range(planes):
+        turn = lax.rem(group - p // share + len(pieces), len(pieces))
+        value = pieces[0][p % share]
+        for k in range(1, len(pieces)):
+            value = jnp.where(turn == k, pieces[k][p % share], value)
+        value = jnp.where(straight, window_ref[p], value)
+        out_ref[p] = value
+        if p < radius:
+            lower_ref[p] = value
+        if p >= planes - radius:
+            upper_ref[p - planes + radius] = value
+
+
+def edge_shapes(shape, radius):
+    edge = jax.ShapeDtypeStruct((radius,) + shape[1:], F32)
+    return jax.ShapeDtypeStruct(shape, F32), edge, edge
+
+
+def assemble(place, window, pieces, radius):
+    out_shape = edge_shapes(window.shape, radius)
+    return call(assemble_kernel, out_shape, [SMEM] + [VMEM] * (1 + len(pieces)), "estimate")(place, window, *pieces)
 
 
 def shift_kernel(scal_ref, acq_ref, mask_ref, first_ref, second_ref, turned_ref):
@@ -244,7 +283,7 @@
     return dot(high, hi_ref[index]) + (dot(low, hi_ref[index]) + dot(high, lo_ref[index]))
 
 
-def ratio_planes(wide_ref, fetch, yf_ref, ya_ref, zhi_ref, zlo_ref, order, outs):
+def ratio_planes(wide_refs, fetch, yf_ref, ya_ref, zhi_ref, zlo_ref, order, outs):
     out_ref, lower_ref, upper_ref = outs
     planes, rows, _ = out_ref.shape
     radius = lower_ref.shape[0]
@@ -252,7 +291,9 @@
     step = 4
     for start in range(0, planes, step):
         block = range(start, min(start + step, planes))
-        blurred = jnp.concatenate([spread_y(yf_ref[order], wide_ref[p]) for p in block], axis=0)
+        blurred = jnp.concatenate(
+            [spread_y(yf_ref[order], jnp.concatenate([ref[p] for ref in wide_refs], axis=0)) for p in block], axis=0
+        )
         blurred = spread_z(blurred, zhi_ref, zlo_ref, order)
         image = jnp.concatenate([fetch(p) for p in block], axis=0)
         ratio = jnp.where(image >= 0, image / blurred, jnp.ones_like(image))
@@ -269,10 +310,8 @@
                 upper_ref[p - planes + radius] = value
 
 
-def first_ratio_kernel(
-    shift_ref, place_ref, low_ref, own_ref, high_ref, wide_ref, yf_ref, ya_ref, zhi_ref, zlo_ref,
-    out_ref, lower_ref, upper_ref, image_ref, *, order, extent_x, cells_y
-):
+def first_ratio_kernel(shift_ref, place_ref, low_ref, own_ref, high_ref, *refs, order, extent_x, cells_y):
+    image_ref = refs[-1]
     planes, near, cells_z = image_ref.shape
     slab, half = place_ref[0], place_ref[1]
     shift_x, shift_y, shift_z = (shift_ref[order, i] for i in range(3))
@@ -299,60 +338,77 @@
         image_ref[p] = value
         return value
 
-    ratio_planes(wide_ref, fetch, yf_ref, ya_ref, zhi_ref, zlo_ref, order, (out_ref, lower_ref, upper_ref))
-
-
-def next_ratio_kernel(
-    image_ref, wide_ref, yf_ref, ya_ref, zhi_ref, zlo_ref, out_ref, lower_ref, upper_ref, *, order
-):
-    ratio_planes(
-        wide_ref, lambda p: image_ref[p], yf_ref, ya_ref, zhi_ref, zlo_ref, order, (out_ref, lower_ref, upper_ref)
-    )
-
-
-def ratio_shapes(wide, tables, radius):
-    planes, _, lanes = wide.shape
-    rows = tables[1].shape[1]
-    edge = jax.ShapeDtypeStruct((radius, rows, lanes), F32)
-    return jax.ShapeDtypeStruct((planes, rows, lanes), F32), edge, edge
-
-
-def first_ratio(shifts, place, blocks, wide, tables, order, radius, extent_x, cells_y):
-    near = tables[0].shape[1]
+    ratio_planes(refs[:-8], fetch, *refs[-8:-4], order, refs[-4:-1])
+
+
+def next_ratio_kernel(image_ref, *refs, order):
+    ratio_planes(refs[:-7], lambda p: image_ref[p], *refs[-7:-3], order, refs[-3:])
+
+
+def ratio_shapes(wides, tables, radius):
+    planes, _, lanes = wides[0].shape
+    return edge_shapes((planes, tables[1].shape[1], lanes), radius)
+
+
+def first_ratio(shifts, place, blocks, wides, tables, order, radius, extent_x, cells_y):
+    planes, _, lanes = wides[0].shape
     kernel = functools.partial(first_ratio_kernel, order=order, extent_x=extent_x, cells_y=cells_y)
-    image = jax.ShapeDtypeStruct((wide.shape[0], near, wide.shape[2]), F32)
-    out_shape = ratio_shapes(wide, tables, radius) + (image,)
-    return call(kernel, out_shape, [SMEM] * 2 + [VMEM] * 8, "image_and_ratio")(
-        shifts, place, *blocks, wide, *tables[:4]
-    )
-
-
-def next_ratio(image, wide, tables, order, radius):
+    image = jax.ShapeDtypeStruct((planes, tables[0].shape[1], lanes), F32)
+    out_shape = ratio_shapes(wides, tables, radius) + (image,)
+    return call(kernel, out_shape, [SMEM] * 2 + [VMEM] * (7 + len(wides)), "image_and_ratio")(
+        shifts, place, *blocks, *wides, *tables[:4]
+    )
+
+
+def next_ratio(image, wides, tables, order, radius):
     kernel = functools.partial(next_ratio_kernel, order=order)
-    return call(kernel, ratio_shapes(wide, tables, radius), [VMEM] * 6, "ratio")(image, wide, *tables[:4])
-
-
-def factor_kernel(hi_ref, lo_ref, current_ref, *refs, start, share):
-    views, out_ref = (refs[:3], refs[3:6]), refs[6]
+    return call(kernel, ratio_shapes(wides, tables, radius), [VMEM] * (5 + len(wides)), "ratio")(
+        image, *wides, *tables[:4]
+    )
+
+
+def factor_kernel(hi_ref, lo_ref, before_ref, low_ref, own_ref, high_ref, out_ref, *, order, start, share):
     planes, rows, _ = out_ref.shape
 
     def body(step, carry):
         row = pl.multiple_of(step * 8, 8)
         source = pl.multiple_of(start + row, 8)
-        total = share * jnp.log(current_ref[:, pl.ds(source, 8), :])
-        for order, view in enumerate(views):
-            total = total + jnp.log(spread_x(hi_ref, lo_ref, 1, order * 8 * planes, 8 * planes, view, source))
-        out_ref[:, pl.ds(row, 8), :] = total
+        total = before_ref[:, pl.ds(source, 8), :]
+        if share:
+            total = share * jnp.log(total)
+        factor = spread_x(hi_ref, lo_ref, 1, order * 8 * planes, 8 * planes, (low_ref, own_ref, high_ref), source)
+        out_ref[:, pl.ds(row, 8), :] = total + jnp.log(factor)
         return carry
 
     lax.fori_loop(0, rows // 8, body, 0)
 
 
-def log_factor(tables, current, sides, start, rows, share):
-    planes, _, lanes = current.shape
-    kernel = functools.partial(factor_kernel, start=start, share=share)
+def log_factor(tables, before, side, order, start, rows, share):
+    planes, _, lanes = side[1].shape
+    kernel = functools.partial(factor_kernel, order=order, start=start, share=share)
     shape = jax.ShapeDtypeStruct((planes, rows, lanes), F32)
-    return call(kernel, shape, [VMEM] * 9, "log_factor")(*tables[4:], current, *sides[0], *sides[1])
+    return call(kernel, shape, [VMEM] * 6, "log_factor")(*tables[4:], before, *side)
+
+
+def update_kernel(*refs):
+    parts, edge_ref, (out_ref, lower_ref, upper_ref) = refs[:-4], refs[-4], refs[-3:]
+    planes, radius, rows = out_ref.shape[0], lower_ref.shape[0], parts[0].shape[1]
+    for p in range(planes):
+        total = parts[0][p]
+        for part in parts[1:]:
+            total = total + part[p]
+        value = jnp.concatenate([jnp.exp(total), edge_ref[p]], axis=0)
+        out_ref[p] = value
+        if p < radius:
+            lower_ref[p] = value
+        if p >= planes - radius:
+            upper_ref[p - planes + radius] = value
+
+
+def update(parts, edge, radius):
+    planes, rows, lanes = parts[0].shape
+    out_shape = edge_shapes((planes, rows + edge.shape[1], lanes), radius)
+    return call(update_kernel, out_shape, [VMEM] * (len(parts) + 1), "update")(*parts, edge)
 
 
 def finish_kernel(half_ref, own_ref, *refs, groups):
@@ -374,9 +430,32 @@
 def finish(half, own, own_parts, other_parts, shape):
     groups = len(own_parts) + 1
     kernel = functools.partial(finish_kernel, groups=groups)
-    return call(kernel, jax.ShapeDtypeStruct(shape, F32), [SMEM] + [VMEM] * (2 * groups), "update")(
+    return call(kernel, jax.ShapeDtypeStruct(shape, F32), [SMEM] + [VMEM] * (2 * groups), "last_update")(
         half.reshape(1), own, *own_parts, *other_parts
     )
+
+
+def choose_kernel(flag_ref, one_ref, other_ref, out_ref, semaphore):
+    def copy(source_ref):
+        move = pltpu.make_async_copy(source_ref, out_ref, semaphore)
+        move.start()
+        move.wait()
+
+    pl.when(flag_ref[0] != 0)(lambda: copy(one_ref))
+    pl.when(flag_ref[0] == 0)(lambda: copy(other_ref))
+
+
+def choose(flag, one, other):
+    anywhere = pl.BlockSpec(memory_space=pl.ANY)
+    return pl.pallas_call(
+        choose_kernel,
+        out_shape=jax.ShapeDtypeStruct(one.shape, one.dtype),
+        in_specs=[SMEM, anywhere, anywhere],
+        out_specs=anywhere,
+        scratch_shapes=[pltpu.SemaphoreType.DMA],
+        compiler_params=PARAMS,
+        name="choose",
+    )(flag, one, other)
 
 
 def shards(acquired, estimate, offsets, view_mask, kern_x, kern_y, kern_z):
@@ -395,15 +474,33 @@
     slab = lax.axis_index("tile") - half + core
     straight = core == half
 
+    group = lax.axis_index("view") // 2
+    flag = jnp.stack([straight.astype(jnp.int32), group])
+
+    def across(turn, half_of=lambda r: r, when=lambda c, r: True):
+        return lambda g, c, q, r: ((g + turn) % groups, c, q, half_of(r)) if when(c, r) else None
+
     window, crossing = make_windows(half, estimate, wide)
-    crossing = send(crossing, lambda g, c, q, r: (g, c, q, 1 - r) if c == r else None)
+    piece = lax.dynamic_slice_in_dim(crossing, group * (planes // groups), planes // groups, 0)
+    piece = send(piece, across(0, lambda r: 1 - r, lambda c, r: c == r))
+
+    mine = jnp.concatenate([kern_x[0], kern_y[0], kern_z[0], offsets[0].astype(F32)])
+    mine, window = lax.optimization_barrier((mine, window))
+    other = send(mine, to_core_partner)
 
     scal = jnp.stack([offsets[0, 1], offsets[0, 2], core])
     acquired, window = lax.optimization_barrier((acquired, window))
     first, second = shift_and_cut(scal, acquired[0], view_mask[0], near)
 
-    mine = jnp.concatenate([kern_x[0], kern_y[0], kern_z[0], offsets[0].astype(F32)])
-    other = send(mine, to_core_partner)
+    pieces = [piece] + [send(piece, across(turn, when=lambda c, r: c != r)) for turn in range(1, groups)]
+    first, piece = lax.optimization_barrier((first, piece))
+    arrived = send(first, lambda g, c, q, r: (g, r, q, c) if c != r else None)
+    current, lower, upper = assemble(flag, window, pieces, radius)
+    low, high = send(upper, to_next), send(lower, to_previous)
+    arrived, second = lax.optimization_barrier((arrived, second))
+    second = send(second, lambda g, c, q, r: (g, r, q, 1 - c))
+    first = jnp.where(straight, first, arrived)
+
     both = jnp.where(straight, jnp.stack([mine, other]), jnp.stack([other, mine]))
     kx = both[:, :taps_x]
     ky = both[:, taps_x:taps_x + taps_y]
@@ -411,54 +508,46 @@
     shifts = both[:, taps_x + taps_y + taps_z:].astype(jnp.int32)
     tables = make_tables(half, kx, ky, kz, planes, cells_y, cells_z, (own_rows, near, wide))
 
-    first, crossing = lax.optimization_barrier((first, crossing))
-    current = jnp.where(straight, window, crossing)
-    low = send(current[planes - radius:], to_next)
-    high = send(current[:radius], to_previous)
-    first = send(first, lambda g, c, q, r: (g, r, q, c))
-    second, first = lax.optimization_barrier((second, first))
-    second = send(second, lambda g, c, q, r: (g, r, q, 1 - c))
     place = jnp.stack([slab, half])
     blocks = [(send(block, to_next), block, send(block, to_previous)) for block in (first, second)]
     images = [None, None]
+    chunks = [(low, current, high)]
 
     for step in range(ITERS):
-        wides = blur_x(tables, low, current, high)
+        wides = [blur_x(tables, *chunk) for chunk in chunks]
         sides = []
         for order in range(2):
+            parts = [chunk[order] for chunk in wides]
             if step == 0:
                 spread, lower, upper, images[order] = first_ratio(
-                    shifts, place, blocks[order], wides[order], tables, order, radius, planes * slabs, cells_y
+                    shifts, place, blocks[order], parts, tables, order, radius, planes * slabs, cells_y
                 )
             else:
-                spread, lower, upper = next_ratio(images[order], wides[order], tables, order, radius)
+                spread, lower, upper = next_ratio(images[order], parts, tables, order, radius)
             sides.append((send(upper, to_next), spread, send(lower, to_previous)))
+        total = log_factor(tables, current, sides[0], 0, 0, own_rows, 1.0 / groups)
         if step < ITERS - 1:
-            edge = log_factor(tables, current, sides, inner_rows, edge_rows, 1.0 / groups)
-            inner = log_factor(tables, current, sides, 0, inner_rows, 1.0 / groups)
-            edge_sum, inner_sum = edge, inner
-            for turn in range(1, groups):
-                edge_sum = edge_sum + send(edge, lambda g, c, q, r: ((g + turn) % groups, c, q, r))
-            for turn in range(1, groups):
-                inner_sum = inner_sum + send(inner, lambda g, c, q, r: ((g + turn) % groups, c, q, r))
-            edge = jnp.exp(edge_sum)
+            edge = log_factor(tables, total, sides[1], 1, inner_rows, edge_rows, 0)
+            inner = log_factor(tables, total, sides[1], 1, 0, inner_rows, 0)
+            edge_parts = [edge] + [send(edge, across(turn)) for turn in range(1, groups)]
+            inner_parts = [inner] + [send(inner, across(turn)) for turn in range(1, groups)]
+            edge = jnp.exp(sum(edge_parts[1:], edge_parts[0]))
             beyond = send(edge, to_row_partner)
-            beyond = beyond.reshape(planes, edge_rows // GROUP, GROUP, cells_z)[:, ::-1].reshape(edge.shape)
-            current = jnp.concatenate([jnp.exp(inner_sum), edge, beyond], axis=1)
-            low = send(current[planes - radius:], to_next)
-            high = send(current[:radius], to_previous)
-
-    own = log_factor(tables, current, sides, 0, own_rows, 1.0 / groups)
+            current, lower, upper = update(inner_parts, edge, radius)
+            chunks = [
+                (send(upper, to_next), current, send(lower, to_previous)),
+                (send(beyond[planes - radius:], to_next), beyond, send(beyond[:radius], to_previous)),
+            ]
+
+    own = log_factor(tables, total, sides[1], 1, 0, own_rows, 0)
     own_parts, other_parts = [], []
     for turn in range(groups):
-        other_parts.append(
-            send(own, lambda g, c, q, r: ((g + turn) % groups, c, q, 1 - r) if c != r else None)
-        )
+        other_parts.append(send(own, across(turn, lambda r: 1 - r, lambda c, r: c != r)))
         if turn:
-            own_parts.append(send(own, lambda g, c, q, r: ((g + turn) % groups, c, q, r) if c == r else None))
+            own_parts.append(send(own, across(turn, when=lambda c, r: c == r)))
     whole = finish(half, own, own_parts, other_parts, estimate.shape)
     copied = send(whole, lambda g, c, q, r: (g, 1 - c, q, r) if c == r else None)
-    return jnp.where(straight, whole, copied)
+    return choose(flag, whole, copied)
 
 
 def solution(mesh):

time: 274 us -> 237 us (0.86)
  waiting for transfers between devices: 123 us -> 108 us
  Pallas kernels: 58.6 us -> 47.3 us
  local copies, waits for them, and re-layouts: 15.8 us -> 10.5 us
  other arithmetic: 7.38 us -> 3.36 us
    ppermute x27 -> x30, waiting for transfers between devices: 123 us -> 108 us  [send(): return lax.ppermute(array, AXES, moves(move))]
    pallas_call x7 -> x12, Pallas kernels: 35.5 us -> 31 us  [the longest x2 11.4 us: first_ratio(): call(kernel, out_shape, [SMEM] * 2 + [VMEM] * (7 + len(wides)), 'image_an...]
    pallas_call x2 -> x3, Pallas kernels: 14.2 us -> 10 us  [blur_x(): call(blur_x_kernel, (shape, shape), [VMEM] * 5, 'blur_x')]
    unnamed x44 -> x30, local copies, waits for them, and re-layouts: 11.1 us -> 9.24 us
    ppermute x27 -> x30, starting transfers between devices: 65.3 us -> 64.7 us  [send(): return lax.ppermute(array, AXES, moves(move))]
  transfers between devices with their start and end apart: 27 -> 30, of which waited for: 17 -> 19; matrix products, arithmetic and copies ran while one was open for 2% -> 2% of each run, Pallas kernels for 13% -> 16%
where the time goes in v3:
time: 237 us; the launch traced here: 234 us
  waiting for transfers between devices  108 us (46%)
  starting transfers between devices  64.7 us (27%)
  Pallas kernels  47.3 us (20%)
  local copies, waits for them, and re-layouts  10.5 us (4%)
  other arithmetic  3.36 us (1%)
    ppermute x30, waiting for transfers between devices, send(): return lax.ppermute(array, AXES, moves(move))  108 us
    ppermute x30, starting transfers between devices, send(): return lax.ppermute(array, AXES, moves(move))  64.7 us
    pallas_call x2, Pallas kernels, first_ratio(): call(kernel, out_shape, [SMEM] * 2 + [VMEM] * (7 + len(wides)), 'image_an...  11.4 us
    pallas_call x3, Pallas kernels, blur_x(): call(blur_x_kernel, (shape, shape), [VMEM] * 5, 'blur_x')  10 us
    unnamed x30, local copies, waits for them, and re-layouts  9.24 us
    pallas_call x5, Pallas kernels, log_factor(): call(kernel, shape, [VMEM] * 6, 'log_factor')(*tables[4:], before, *side)  8.42 us
    pallas_call x2, Pallas kernels, next_ratio(): call(kernel, ratio_shapes(wides, tables, radius), [VMEM] * (5 + len(wides...  7.06 us
  transfers between devices with their start and end apart: 30, of which 19 were waited for; matrix products, arithmetic and copies ran while one was open for 2% of the time, Pallas kernels for 16%

profile of v3, /device:TPU:17, one launch (start us, length us, event | category | flops | bytes accessed | tf_op | source)
XLA Modules:
  0.0 234.3 jit_solution(241117033996743000)
XLA Ops:
  5.5 4.2 %shift_recorded.1 = (f32[17,80,256]{2,1,0:T(8,128)}, f32[17,80,256]{2,1,0:T(8,128)S(1)}) custom-call(s32[3]{0:T(128)S(1)} %pad_add_fusion.2.scal_ref, f32[16,128,256]{2,1,0:T(8,128)S(1)} %bitcast.16, s32[16,128]{1,0:T(8,128)S(1)} %bitcast.17), custom_call_target="tpu_custom_call" | custom-call | tf_op jit(solution)/shard_map/shift_recorded/pallas_call | solution.py:237
  10.8 4.0 %collective-permute-done.1.refs_0_ = f32[8,96,256]{2,1,0:T(8,128)S(1)} collective-permute-done((f32[8,96,256]{2,1,0:T(8,128)S(1)}, f32[8,96,256]{2,1,0:T(8,128)S(1)}, u32[]{:S(2)}, u32[]{:S(2)}) %collective-permute-start.1) | collective-permute-done | bytes 786464 | tf_op jit(solution)/shard_map/ppermute | solution.py:33
  14.8 4.8 %collective-permute-start.3 = (f32[17,80,256]{2,1,0:T(8,128)}, f32[17,80,256]{2,1,0:T(8,128)}, u32[]{:S(2)}, u32[]{:S(2)}) collective-permute-start(f32[17,80,256]{2,1,0:T(8,128)} %get-tuple-element.58), channel_id=1, source_target_pairs={{1,8},{3,10},{5,12},{7,14},{8,1},{10,3},{12,5},{14,7},{17,24},{19,... | collective-permute-start | bytes 4177928 | tf_op jit(solution)/shard_map/ppermute | solution.py:33
  19.6 3.1 %collective-permute-start.2 = (f32[8,96,256]{2,1,0:T(8,128)S(1)}, f32[8,96,256]{2,1,0:T(8,128)S(1)}, u32[]{:S(2)}, u32[]{:S(2)}) collective-permute-start(f32[8,96,256]{2,1,0:T(8,128)S(1)} %collective-permute-done.1.refs_0_), channel_id=1, source_target_pairs={{1,17},{3,19},{5,21},{7,23},{8,24},{10,26},{12,28},{14,30},{17,1},... | collective-permute-start | bytes 2359304 | tf_op jit(solution)/shard_map/ppermute | solution.py:33
  23.7 8.6 %collective-permute-done.2.refs_1_ = f32[8,96,256]{2,1,0:T(8,128)S(1)} collective-permute-done((f32[8,96,256]{2,1,0:T(8,128)S(1)}, f32[8,96,256]{2,1,0:T(8,128)S(1)}, u32[]{:S(2)}, u32[]{:S(2)}) %collective-permute-start.2) | collective-permute-done | bytes 786464 | tf_op jit(solution)/shard_map/ppermute | solution.py:33
  35.5 2.0 estimate.1
  41.0 1.9 collective-permute-start.7
  44.4 2.5 %collective-permute-start.5 = (f32[17,80,256]{2,1,0:T(8,128)S(1)}, f32[17,80,256]{2,1,0:T(8,128)}, u32[]{:S(2)}, u32[]{:S(2)}) collective-permute-start(f32[17,80,256]{2,1,0:T(8,128)S(1)} %broadcast_select_fusion.own_ref), channel_id=1, source_target_pairs={{2,8},{3,9},{4,10},{5,11},{6,12},{7,13},{8,0},{9,1},{10,2},{11,3},... | collective-permute-start | bytes 4177928 | tf_op jit(solution)/shard_map/ppermute | solution.py:33
  46.9 3.1 %collective-permute-start.4 = (f32[17,80,256]{2,1,0:T(8,128)S(1)}, f32[17,80,256]{2,1,0:T(8,128)}, u32[]{:S(2)}, u32[]{:S(2)}) collective-permute-start(f32[17,80,256]{2,1,0:T(8,128)S(1)} %broadcast_select_fusion.own_ref), channel_id=1, source_target_pairs={{0,8},{1,9},{2,10},{3,11},{4,12},{5,13},{6,14},{7,15},{8,2},{9,3},... | collective-permute-start | bytes 4177928 | tf_op jit(solution)/shard_map/ppermute | solution.py:33
  50.0 8.1 %collective-permute-done.10.own_ref = f32[17,80,256]{2,1,0:T(8,128)} collective-permute-done((f32[17,80,256]{2,1,0:T(8,128)S(1)}, f32[17,80,256]{2,1,0:T(8,128)}, u32[]{:S(2)}, u32[]{:S(2)}) %collective-permute-start.10) | collective-permute-done | bytes 1392672 | tf_op jit(solution)/shard_map/ppermute | solution.py:33
  58.1 1.9 collective-permute-start.12
  61.2 3.6 %collective-permute-start.11 = (f32[17,80,256]{2,1,0:T(8,128)}, f32[17,80,256]{2,1,0:T(8,128)}, u32[]{:S(2)}, u32[]{:S(2)}) collective-permute-start(f32[17,80,256]{2,1,0:T(8,128)} %collective-permute-done.10.own_ref), channel_id=1, source_target_pairs={{0,8},{1,9},{2,10},{3,11},{4,12},{5,13},{6,14},{7,15},{8,2},{9,3},... | collective-permute-start | bytes 4177928 | tf_op jit(solution)/shard_map/ppermute | solution.py:33
  68.6 5.7 %blur_x.3 = (f32[16,96,256]{2,1,0:T(8,128)S(1)}, f32[16,96,256]{2,1,0:T(8,128)S(1)}) custom-call(bf16[2,256,384]{2,1,0:T(8,128)(2,1)S(1)} %get-tuple-element.50.hi_ref, bf16[2,256,384]{2,1,0:T(8,128)(2,1)S(1)} %get-tuple-element.51.lo_ref, f32[15,96,256]{2,1,0:T(8,128)S(1)} %copy-done.3, f32[16,96,256]{2,1,0:T(8,128)S(1)} %get-tuple-element.55.own_ref.before_ref, ...), custom_call_target="tpu_custom_call" | custom-call | tf_op jit(solution)/shard_map/blur_x/pallas_call | solution.py:269
  74.3 2.9 %collective-permute-done.5.high_ref = f32[17,80,256]{2,1,0:T(8,128)} collective-permute-done((f32[17,80,256]{2,1,0:T(8,128)S(1)}, f32[17,80,256]{2,1,0:T(8,128)}, u32[]{:S(2)}, u32[]{:S(2)}) %collective-permute-start.5) | collective-permute-done | bytes 1392672 | tf_op jit(solution)/shard_map/ppermute | solution.py:33
  77.2 5.5 %image_and_ratio.2 = (f32[16,64,256]{2,1,0:T(8,128)S(1)}, f32[15,64,256]{2,1,0:T(8,128)S(1)}, f32[15,64,256]{2,1,0:T(8,128)S(1)}, f32[16,80,256]{2,1,0:T(8,128)S(1)}) custom-call(s32[2,3]{1,0:T(2,128)S(1)} %slice_convert_fusion.shift_ref, s32[2]{0:T(128)S(1)} %pad_add_fusion.1.place_ref, f32[17,80,256]{2,1,0:T(8,128)} %collective-permute-done.4.low_ref, ...), custom_call_target="tpu_custom_call" | custom-call | tf_op jit(solution)/shard_map/image_and_ratio/pallas_call | solution.py:358
  82.7 1.9 collective-permute-start.8
  84.6 2.4 %collective-permute-start.9 = (f32[15,64,256]{2,1,0:T(8,128)S(1)}, f32[15,64,256]{2,1,0:T(8,128)S(1)}, u32[]{:S(2)}, u32[]{:S(2)}) collective-permute-start(f32[15,64,256]{2,1,0:T(8,128)S(1)} %get-tuple-element.70), channel_id=1, source_target_pairs={{2,8},{3,9},{4,10},{5,11},{6,12},{7,13},{8,0},{9,1},{10,2},{11,3},... | collective-permute-start | bytes 2949128 | tf_op jit(solution)/shard_map/ppermute | solution.py:33
  87.0 5.0 %collective-permute-done.12.high_ref = f32[17,80,256]{2,1,0:T(8,128)} collective-permute-done((f32[17,80,256]{2,1,0:T(8,128)}, f32[17,80,256]{2,1,0:T(8,128)}, u32[]{:S(2)}, u32[]{:S(2)}) %collective-permute-start.12) | collective-permute-done | bytes 1392672 | tf_op jit(solution)/shard_map/ppermute | solution.py:33
  92.0 5.9 %image_and_ratio.3 = (f32[16,64,256]{2,1,0:T(8,128)S(1)}, f32[15,64,256]{2,1,0:T(8,128)S(1)}, f32[15,64,256]{2,1,0:T(8,128)S(1)}, f32[16,80,256]{2,1,0:T(8,128)S(1)}) custom-call(s32[2,3]{1,0:T(2,128)S(1)} %slice_convert_fusion.shift_ref, s32[2]{0:T(128)S(1)} %pad_add_fusion.1.place_ref, f32[17,80,256]{2,1,0:T(8,128)} %collective-permute-done.11.low_ref, ...), custom_call_target="tpu_custom_call" | custom-call | tf_op jit(solution)/shard_map/image_and_ratio/pallas_call | solution.py:358
  97.9 1.9 collective-permute-start.13
  99.9 2.4 %collective-permute-start.14 = (f32[15,64,256]{2,1,0:T(8,128)S(1)}, f32[15,64,256]{2,1,0:T(8,128)S(1)}, u32[]{:S(2)}, u32[]{:S(2)}) collective-permute-start(f32[15,64,256]{2,1,0:T(8,128)S(1)} %get-tuple-element.75), channel_id=1, source_target_pairs={{2,8},{3,9},{4,10},{5,11},{6,12},{7,13},{8,0},{9,1},{10,2},{11,3},... | collective-permute-start | bytes 2949128 | tf_op jit(solution)/shard_map/ppermute | solution.py:33
  102.5 2.1 log_factor.5.before_ref
  104.6 6.2 %collective-permute-done.13.low_ref = f32[15,64,256]{2,1,0:T(8,128)S(1)} collective-permute-done((f32[15,64,256]{2,1,0:T(8,128)S(1)}, f32[15,64,256]{2,1,0:T(8,128)S(1)}, u32[]{:S(2)}, u32[]{:S(2)}) %collective-permute-start.13) | collective-permute-done | bytes 983072 | tf_op jit(solution)/shard_map/ppermute | solution.py:33
  110.9 4.4 %collective-permute-done.14.high_ref = f32[15,64,256]{2,1,0:T(8,128)S(1)} collective-permute-done((f32[15,64,256]{2,1,0:T(8,128)S(1)}, f32[15,64,256]{2,1,0:T(8,128)S(1)}, u32[]{:S(2)}, u32[]{:S(2)}) %collective-permute-start.14) | collective-permute-done | bytes 983072 | tf_op jit(solution)/shard_map/ppermute | solution.py:33
  119.0 11.3 %collective-permute-done.16 = f32[16,32,256]{2,1,0:T(8,128)S(1)} collective-permute-done((f32[16,32,256]{2,1,0:T(8,128)S(1)}, f32[16,32,256]{2,1,0:T(8,128)S(1)}, u32[]{:S(2)}, u32[]{:S(2)}) %collective-permute-start.16) | collective-permute-done | bytes 524320 | tf_op jit(solution)/shard_map/ppermute | solution.py:33
  131.9 8.8 %collective-permute-done.15.refs_1_ = f32[16,32,256]{2,1,0:T(8,128)S(1)} collective-permute-done((f32[16,32,256]{2,1,0:T(8,128)S(1)}, f32[16,32,256]{2,1,0:T(8,128)S(1)}, u32[]{:S(2)}, u32[]{:S(2)}) %collective-permute-start.15) | collective-permute-done | bytes 524320 | tf_op jit(solution)/shard_map/ppermute | solution.py:33
  140.9 1.9 collective-permute-start.17
  142.8 2.4 %collective-permute-start.18 = (f32[15,64,256]{2,1,0:T(8,128)S(1)}, f32[15,64,256]{2,1,0:T(8,128)S(1)}, u32[]{:S(2)}, u32[]{:S(2)}) collective-permute-start(f32[15,64,256]{2,1,0:T(8,128)S(1)} %get-tuple-element.79), channel_id=1, source_target_pairs={{2,8},{3,9},{4,10},{5,11},{6,12},{7,13},{8,0},{9,1},{10,2},{11,3},... | collective-permute-start | bytes 2949128 | tf_op jit(solution)/shard_map/ppermute | solution.py:33
  145.4 2.7 %collective-permute-start.21 = (f32[15,32,256]{2,1,0:T(8,128)S(1)}, f32[15,32,256]{2,1,0:T(8,128)S(1)}, u32[]{:S(2)}, u32[]{:S(2)}) collective-permute-start(f32[15,32,256]{2,1,0:T(8,128)S(1)} %get-tuple-element.91), channel_id=1, source_target_pairs={{2,8},{3,9},{4,10},{5,11},{6,12},{7,13},{8,0},{9,1},{10,2},{11,3},... | collective-permute-start | bytes 1474568 | tf_op jit(solution)/shard_map/ppermute | solution.py:33
  148.0 3.1 %collective-permute-start.20 = (f32[15,32,256]{2,1,0:T(8,128)S(1)}, f32[15,32,256]{2,1,0:T(8,128)S(1)}, u32[]{:S(2)}, u32[]{:S(2)}) collective-permute-start(f32[15,32,256]{2,1,0:T(8,128)S(1)} %get-tuple-element.92), channel_id=1, source_target_pairs={{0,8},{1,9},{2,10},{3,11},{4,12},{5,13},{6,14},{7,15},{8,2},{9,3},... | collective-permute-start | bytes 1474568 | tf_op jit(solution)/shard_map/ppermute | solution.py:33
  151.1 2.7 %collective-permute-done.17.low_ref = f32[15,64,256]{2,1,0:T(8,128)S(1)} collective-permute-done((f32[15,64,256]{2,1,0:T(8,128)S(1)}, f32[15,64,256]{2,1,0:T(8,128)S(1)}, u32[]{:S(2)}, u32[]{:S(2)}) %collective-permute-start.17) | collective-permute-done | bytes 983072 | tf_op jit(solution)/shard_map/ppermute | solution.py:33
  153.8 4.7 %collective-permute-done.18.high_ref = f32[15,64,256]{2,1,0:T(8,128)S(1)} collective-permute-done((f32[15,64,256]{2,1,0:T(8,128)S(1)}, f32[15,64,256]{2,1,0:T(8,128)S(1)}, u32[]{:S(2)}, u32[]{:S(2)}) %collective-permute-start.18) | collective-permute-done | bytes 983072 | tf_op jit(solution)/shard_map/ppermute | solution.py:33
  158.5 2.9 %blur_x.4 = (f32[16,64,256]{2,1,0:T(8,128)S(1)}, f32[16,64,256]{2,1,0:T(8,128)S(1)}) custom-call(bf16[2,256,384]{2,1,0:T(8,128)(2,1)S(1)} %get-tuple-element.50.hi_ref, bf16[2,256,384]{2,1,0:T(8,128)(2,1)S(1)} %get-tuple-element.51.lo_ref, f32[15,64,256]{2,1,0:T(8,128)S(1)} %collective-permute-done.17.low_ref, ...), custom_call_target="tpu_custom_call" | custom-call | tf_op jit(solution)/shard_map/blur_x/pallas_call | solution.py:269
  161.4 2.1 collective-permute-done.21.high_ref
  165.0 3.5 %ratio.2 = (f32[16,64,256]{2,1,0:T(8,128)S(1)}, f32[15,64,256]{2,1,0:T(8,128)S(1)}, f32[15,64,256]{2,1,0:T(8,128)S(1)}) custom-call(f32[16,80,256]{2,1,0:T(8,128)S(1)} %get-tuple-element.77.image_ref, f32[16,64,256]{2,1,0:T(8,128)S(1)} %get-tuple-element.80.refs_0_, f32[16,32,256]{2,1,0:T(8,128)S(1)} %get-tuple-element.81.refs_1_, ...), custom_call_target="tpu_custom_call" | custom-call | tf_op jit(solution)/shard_map/ratio/pallas_call | solution.py:365
  168.5 1.9 collective-permute-start.22
  170.4 2.4 %collective-permute-start.23 = (f32[15,64,256]{2,1,0:T(8,128)S(1)}, f32[15,64,256]{2,1,0:T(8,128)S(1)}, u32[]{:S(2)}, u32[]{:S(2)}) collective-permute-start(f32[15,64,256]{2,1,0:T(8,128)S(1)} %get-tuple-element.84), channel_id=1, source_target_pairs={{2,8},{3,9},{4,10},{5,11},{6,12},{7,13},{8,0},{9,1},{10,2},{11,3},... | collective-permute-start | bytes 2949128 | tf_op jit(solution)/shard_map/ppermute | solution.py:33
  172.8 3.5 %ratio.3 = (f32[16,64,256]{2,1,0:T(8,128)S(1)}, f32[15,64,256]{2,1,0:T(8,128)S(1)}, f32[15,64,256]{2,1,0:T(8,128)S(1)}) custom-call(f32[16,80,256]{2,1,0:T(8,128)S(1)} %get-tuple-element.85.image_ref, f32[16,64,256]{2,1,0:T(8,128)S(1)} %get-tuple-element.86.refs_0_, f32[16,32,256]{2,1,0:T(8,128)S(1)} %get-tuple-element.87.refs_1_, ...), custom_call_target="tpu_custom_call" | custom-call | tf_op jit(solution)/shard_map/ratio/pallas_call | solution.py:365
  176.4 3.2 %collective-permute-start.24 = (f32[15,64,256]{2,1,0:T(8,128)S(1)}, f32[15,64,256]{2,1,0:T(8,128)S(1)}, u32[]{:S(2)}, u32[]{:S(2)}) collective-permute-start(f32[15,64,256]{2,1,0:T(8,128)S(1)} %get-tuple-element.88), channel_id=1, source_target_pairs={{0,8},{1,9},{2,10},{3,11},{4,12},{5,13},{6,14},{7,15},{8,2},{9,3},... | collective-permute-start | bytes 2949128 | tf_op jit(solution)/shard_map/ppermute | solution.py:33
  179.6 1.9 collective-permute-start.25
  181.5 4.7 %collective-permute-done.23.high_ref = f32[15,64,256]{2,1,0:T(8,128)S(1)} collective-permute-done((f32[15,64,256]{2,1,0:T(8,128)S(1)}, f32[15,64,256]{2,1,0:T(8,128)S(1)}, u32[]{:S(2)}, u32[]{:S(2)}) %collective-permute-start.23) | collective-permute-done | bytes 983072 | tf_op jit(solution)/shard_map/ppermute | solution.py:33
  186.1 2.1 log_factor.8.before_ref
  188.3 3.7 %collective-permute-done.24.low_ref = f32[15,64,256]{2,1,0:T(8,128)S(1)} collective-permute-done((f32[15,64,256]{2,1,0:T(8,128)S(1)}, f32[15,64,256]{2,1,0:T(8,128)S(1)}, u32[]{:S(2)}, u32[]{:S(2)}) %collective-permute-start.24) | collective-permute-done | bytes 983072 | tf_op jit(solution)/shard_map/ppermute | solution.py:33
  192.0 4.4 %collective-permute-done.25.high_ref = f32[15,64,256]{2,1,0:T(8,128)S(1)} collective-permute-done((f32[15,64,256]{2,1,0:T(8,128)S(1)}, f32[15,64,256]{2,1,0:T(8,128)S(1)}, u32[]{:S(2)}, u32[]{:S(2)}) %collective-permute-start.25) | collective-permute-done | bytes 983072 | tf_op jit(solution)/shard_map/ppermute | solution.py:33
  196.4 2.1 log_factor.9.own_ref
  198.5 4.3 %collective-permute-start.28 = (f32[16,64,256]{2,1,0:T(8,128)S(1)}, f32[16,64,256]{2,1,0:T(8,128)S(1)}, u32[]{:S(2)}, u32[]{:S(2)}) collective-permute-start(f32[16,64,256]{2,1,0:T(8,128)S(1)} %log_factor.9.own_ref), channel_id=1, source_target_pairs={{1,16},{3,18},{5,20},{7,22},{8,25},{10,27},{12,29},{14,31},{17,0},... | collective-permute-start | bytes 3145736 | tf_op jit(solution)/shard_map/ppermute | solution.py:33
  204.9 19.5 %collective-permute-done.28.refs_2_ = f32[16,64,256]{2,1,0:T(8,128)S(1)} collective-permute-done((f32[16,64,256]{2,1,0:T(8,128)S(1)}, f32[16,64,256]{2,1,0:T(8,128)S(1)}, u32[]{:S(2)}, u32[]{:S(2)}) %collective-permute-start.28) | collective-permute-done | bytes 1048608 | tf_op jit(solution)/shard_map/ppermute | solution.py:33
  227.2 5.0 %collective-permute-done.29.other_ref = f32[16,128,256]{2,1,0:T(8,128)S(1)} collective-permute-done((f32[16,128,256]{2,1,0:T(8,128)S(1)}, f32[16,128,256]{2,1,0:T(8,128)S(1)}, u32[]{:S(2)}, u32[]{:S(2)}) %collective-permute-start.29) | collective-permute-done | bytes 2097184 | tf_op jit(solution)/shard_map/ppermute | solution.py:33
  (80 shorter events, 34.6 us)
Async XLA Ops:
  0.0 1.6 copy-start
  1.6 1.8 copy-start.11
  1.6 1.8 copy-start.12
  1.6 1.8 copy-start.13
  1.6 1.8 copy-start.14
  1.6 3.9 %copy-start.1 = (f32[1,16,128,256]{3,2,1,0:T(8,128)S(1)}, f32[1,16,128,256]{3,2,1,0:T(8,128)}, u32[]{:S(2)}) copy-start(f32[1,16,128,256]{3,2,1,0:T(8,128)} %param.7) | copy-start | bytes 6291460
  1.6 3.9 %copy-start.8 = (s32[1,16,128]{2,1,0:T(8,128)S(1)}, s32[1,16,128]{2,1,0:T(8,128)}, u32[]{:S(2)}) copy-start(s32[1,16,128]{2,1,0:T(8,128)} %param.10) | copy-start | bytes 24580
  1.9 12.9 %collective-permute-start.1 = (f32[8,96,256]{2,1,0:T(8,128)S(1)}, f32[8,96,256]{2,1,0:T(8,128)S(1)}, u32[]{:S(2)}, u32[]{:S(2)}) collective-permute-start(f32[8,96,256]{2,1,0:T(8,128)S(1)} %constant_dynamic-slice_fusion), channel_id=1, source_target_pairs={{0,1},{2,3},{4,5},{6,7},{9,8},{11,10},{13,12},{15,14},{16,17},{18,... | collective-permute-start | bytes 2359304 | tf_op jit(solution)/shard_map/ppermute | solution.py:33
  9.7 1.1 copy-start.9
  14.8 24.6 %collective-permute-start.3 = (f32[17,80,256]{2,1,0:T(8,128)}, f32[17,80,256]{2,1,0:T(8,128)}, u32[]{:S(2)}, u32[]{:S(2)}) collective-permute-start(f32[17,80,256]{2,1,0:T(8,128)} %get-tuple-element.58), channel_id=1, source_target_pairs={{1,8},{3,10},{5,12},{7,14},{8,1},{10,3},{12,5},{14,7},{17,24},{19,... | collective-permute-start | bytes 4177928 | tf_op jit(solution)/shard_map/ppermute | solution.py:33
  19.6 12.7 %collective-permute-start.2 = (f32[8,96,256]{2,1,0:T(8,128)S(1)}, f32[8,96,256]{2,1,0:T(8,128)S(1)}, u32[]{:S(2)}, u32[]{:S(2)}) collective-permute-start(f32[8,96,256]{2,1,0:T(8,128)S(1)} %collective-permute-done.1.refs_0_), channel_id=1, source_target_pairs={{1,17},{3,19},{5,21},{7,23},{8,24},{10,26},{12,28},{14,30},{17,1},... | collective-permute-start | bytes 2359304 | tf_op jit(solution)/shard_map/ppermute | solution.py:33
  22.8 0.9 copy-start.4
  32.4 0.9 copy-start.6
  33.2 1.1 copy-start.5
  34.4 1.1 copy-start.7
  35.5 3.9 %copy-start.10 = (f32[17,80,256]{2,1,0:T(8,128)S(1)}, f32[17,80,256]{2,1,0:T(8,128)}, u32[]{:S(2)}) copy-start(f32[17,80,256]{2,1,0:T(8,128)} %copy-done.9) | copy-start | bytes 4177924
  37.5 22.6 %collective-permute-start.6 = (f32[15,96,256]{2,1,0:T(8,128)S(1)}, f32[15,96,256]{2,1,0:T(8,128)S(1)}, u32[]{:S(2)}, u32[]{:S(2)}) collective-permute-start(f32[15,96,256]{2,1,0:T(8,128)S(1)} %get-tuple-element.61), channel_id=1, source_target_pairs={{0,8},{1,9},{2,10},{3,11},{4,12},{5,13},{6,14},{7,15},{8,2},{9,3},... | collective-permute-start | bytes 4423688 | tf_op jit(solution)/shard_map/ppermute | solution.py:33
  39.4 18.7 %collective-permute-start.10 = (f32[17,80,256]{2,1,0:T(8,128)S(1)}, f32[17,80,256]{2,1,0:T(8,128)}, u32[]{:S(2)}, u32[]{:S(2)}) collective-permute-start(f32[17,80,256]{2,1,0:T(8,128)S(1)} %copy-done.10), channel_id=1, source_target_pairs={{0,1},{1,9},{2,3},{3,11},{4,5},{5,13},{6,7},{7,15},{8,0},{9,8},{10... | collective-permute-start | bytes 4177928 | tf_op jit(solution)/shard_map/ppermute | solution.py:33
  39.9 7.0 %collective-permute-start = (f32[126]{0:T(128)S(1)}, f32[126]{0:T(128)S(1)}, u32[]{:S(2)}, u32[]{:S(2)}) collective-permute-start(f32[126]{0:T(128)S(1)} %pad_maximum_fusion.1), channel_id=1, source_target_pairs={{0,8},{1,9},{2,10},{3,11},{4,12},{5,13},{6,14},{7,15},{8,0},{9,1},... | collective-permute-start | bytes 1520 | tf_op jit(solution)/shard_map/ppermute | solution.py:33
  41.0 26.2 %collective-permute-start.7 = (f32[15,96,256]{2,1,0:T(8,128)}, f32[15,96,256]{2,1,0:T(8,128)}, u32[]{:S(2)}, u32[]{:S(2)}) collective-permute-start(f32[15,96,256]{2,1,0:T(8,128)} %get-tuple-element.62), channel_id=1, source_target_pairs={{2,8},{3,9},{4,10},{5,11},{6,12},{7,13},{8,0},{9,1},{10,2},{11,3},... | collective-permute-start | bytes 4423688 | tf_op jit(solution)/shard_map/ppermute | solution.py:33
  44.4 32.7 %collective-permute-start.5 = (f32[17,80,256]{2,1,0:T(8,128)S(1)}, f32[17,80,256]{2,1,0:T(8,128)}, u32[]{:S(2)}, u32[]{:S(2)}) collective-permute-start(f32[17,80,256]{2,1,0:T(8,128)S(1)} %broadcast_select_fusion.own_ref), channel_id=1, source_target_pairs={{2,8},{3,9},{4,10},{5,11},{6,12},{7,13},{8,0},{9,1},{10,2},{11,3},... | collective-permute-start | bytes 4177928 | tf_op jit(solution)/shard_map/ppermute | solution.py:33
  46.9 30.3 %collective-permute-start.4 = (f32[17,80,256]{2,1,0:T(8,128)S(1)}, f32[17,80,256]{2,1,0:T(8,128)}, u32[]{:S(2)}, u32[]{:S(2)}) collective-permute-start(f32[17,80,256]{2,1,0:T(8,128)S(1)} %broadcast_select_fusion.own_ref), channel_id=1, source_target_pairs={{0,8},{1,9},{2,10},{3,11},{4,12},{5,13},{6,14},{7,15},{8,2},{9,3},... | collective-permute-start | bytes 4177928 | tf_op jit(solution)/shard_map/ppermute | solution.py:33
  58.1 33.9 %collective-permute-start.12 = (f32[17,80,256]{2,1,0:T(8,128)}, f32[17,80,256]{2,1,0:T(8,128)}, u32[]{:S(2)}, u32[]{:S(2)}) collective-permute-start(f32[17,80,256]{2,1,0:T(8,128)} %collective-permute-done.10.own_ref), channel_id=1, source_target_pairs={{2,8},{3,9},{4,10},{5,11},{6,12},{7,13},{8,0},{9,1},{10,2},{11,3},... | collective-permute-start | bytes 4177928 | tf_op jit(solution)/shard_map/ppermute | solution.py:33
  60.1 1.1 copy-start.2
  61.2 30.8 %collective-permute-start.11 = (f32[17,80,256]{2,1,0:T(8,128)}, f32[17,80,256]{2,1,0:T(8,128)}, u32[]{:S(2)}, u32[]{:S(2)}) collective-permute-start(f32[17,80,256]{2,1,0:T(8,128)} %collective-permute-done.10.own_ref), channel_id=1, source_target_pairs={{0,8},{1,9},{2,10},{3,11},{4,12},{5,13},{6,14},{7,15},{8,2},{9,3},... | collective-permute-start | bytes 4177928 | tf_op jit(solution)/shard_map/ppermute | solution.py:33
  67.2 1.4 copy-start.3
  82.7 19.6 %collective-permute-start.8 = (f32[15,64,256]{2,1,0:T(8,128)S(1)}, f32[15,64,256]{2,1,0:T(8,128)S(1)}, u32[]{:S(2)}, u32[]{:S(2)}) collective-permute-start(f32[15,64,256]{2,1,0:T(8,128)S(1)} %get-tuple-element.68), channel_id=1, source_target_pairs={{0,8},{1,9},{2,10},{3,11},{4,12},{5,13},{6,14},{7,15},{8,2},{9,3},... | collective-permute-start | bytes 2949128 | tf_op jit(solution)/shard_map/ppermute | solution.py:33
  84.6 17.9 %collective-permute-start.9 = (f32[15,64,256]{2,1,0:T(8,128)S(1)}, f32[15,64,256]{2,1,0:T(8,128)S(1)}, u32[]{:S(2)}, u32[]{:S(2)}) collective-permute-start(f32[15,64,256]{2,1,0:T(8,128)S(1)} %get-tuple-element.70), channel_id=1, source_target_pairs={{2,8},{3,9},{4,10},{5,11},{6,12},{7,13},{8,0},{9,1},{10,2},{11,3},... | collective-permute-start | bytes 2949128 | tf_op jit(solution)/shard_map/ppermute | solution.py:33
  97.9 12.9 %collective-permute-start.13 = (f32[15,64,256]{2,1,0:T(8,128)S(1)}, f32[15,64,256]{2,1,0:T(8,128)S(1)}, u32[]{:S(2)}, u32[]{:S(2)}) collective-permute-start(f32[15,64,256]{2,1,0:T(8,128)S(1)} %get-tuple-element.73), channel_id=1, source_target_pairs={{0,8},{1,9},{2,10},{3,11},{4,12},{5,13},{6,14},{7,15},{8,2},{9,3},... | collective-permute-start | bytes 2949128 | tf_op jit(solution)/shard_map/ppermute | solution.py:33
  99.9 15.4 %collective-permute-start.14 = (f32[15,64,256]{2,1,0:T(8,128)S(1)}, f32[15,64,256]{2,1,0:T(8,128)S(1)}, u32[]{:S(2)}, u32[]{:S(2)}) collective-permute-start(f32[15,64,256]{2,1,0:T(8,128)S(1)} %get-tuple-element.75), channel_id=1, source_target_pairs={{2,8},{3,9},{4,10},{5,11},{6,12},{7,13},{8,0},{9,1},{10,2},{11,3},... | collective-permute-start | bytes 2949128 | tf_op jit(solution)/shard_map/ppermute | solution.py:33
  116.3 14.0 %collective-permute-start.16 = (f32[16,32,256]{2,1,0:T(8,128)S(1)}, f32[16,32,256]{2,1,0:T(8,128)S(1)}, u32[]{:S(2)}, u32[]{:S(2)}) collective-permute-start(f32[16,32,256]{2,1,0:T(8,128)S(1)} %log_factor.7), channel_id=1, source_target_pairs={{0,16},{1,17},{2,18},{3,19},{4,20},{5,21},{6,22},{7,23},{8,24},{9,... | collective-permute-start | bytes 1572872 | tf_op jit(solution)/shard_map/ppermute | solution.py:33
  118.6 22.1 %collective-permute-start.15 = (f32[16,32,256]{2,1,0:T(8,128)S(1)}, f32[16,32,256]{2,1,0:T(8,128)S(1)}, u32[]{:S(2)}, u32[]{:S(2)}) collective-permute-start(f32[16,32,256]{2,1,0:T(8,128)S(1)} %log_factor.6.refs_0_), channel_id=1, source_target_pairs={{0,16},{1,17},{2,18},{3,19},{4,20},{5,21},{6,22},{7,23},{8,24},{9,... | collective-permute-start | bytes 1572872 | tf_op jit(solution)/shard_map/ppermute | solution.py:33
  130.4 14.8 %collective-permute-start.19 = (f32[16,32,256]{2,1,0:T(8,128)S(1)}, f32[16,32,256]{2,1,0:T(8,128)S(1)}, u32[]{:S(2)}, u32[]{:S(2)}) collective-permute-start(f32[16,32,256]{2,1,0:T(8,128)S(1)} %add_exponential_fusion.refs_2_), channel_id=1, source_target_pairs={{0,1},{1,0},{2,3},{3,2},{4,5},{5,4},{6,7},{7,6},{8,9},{9,8},{10,11... | collective-permute-start | bytes 1572872 | tf_op jit(solution)/shard_map/ppermute | solution.py:33
  140.9 12.9 %collective-permute-start.17 = (f32[15,64,256]{2,1,0:T(8,128)S(1)}, f32[15,64,256]{2,1,0:T(8,128)S(1)}, u32[]{:S(2)}, u32[]{:S(2)}) collective-permute-start(f32[15,64,256]{2,1,0:T(8,128)S(1)} %get-tuple-element.78), channel_id=1, source_target_pairs={{0,8},{1,9},{2,10},{3,11},{4,12},{5,13},{6,14},{7,15},{8,2},{9,3},... | collective-permute-start | bytes 2949128 | tf_op jit(solution)/shard_map/ppermute | solution.py:33
  142.8 15.7 %collective-permute-start.18 = (f32[15,64,256]{2,1,0:T(8,128)S(1)}, f32[15,64,256]{2,1,0:T(8,128)S(1)}, u32[]{:S(2)}, u32[]{:S(2)}) collective-permute-start(f32[15,64,256]{2,1,0:T(8,128)S(1)} %get-tuple-element.79), channel_id=1, source_target_pairs={{2,8},{3,9},{4,10},{5,11},{6,12},{7,13},{8,0},{9,1},{10,2},{11,3},... | collective-permute-start | bytes 2949128 | tf_op jit(solution)/shard_map/ppermute | solution.py:33
  145.4 18.1 %collective-permute-start.21 = (f32[15,32,256]{2,1,0:T(8,128)S(1)}, f32[15,32,256]{2,1,0:T(8,128)S(1)}, u32[]{:S(2)}, u32[]{:S(2)}) collective-permute-start(f32[15,32,256]{2,1,0:T(8,128)S(1)} %get-tuple-element.91), channel_id=1, source_target_pairs={{2,8},{3,9},{4,10},{5,11},{6,12},{7,13},{8,0},{9,1},{10,2},{11,3},... | collective-permute-start | bytes 1474568 | tf_op jit(solution)/shard_map/ppermute | solution.py:33
  148.0 15.5 %collective-permute-start.20 = (f32[15,32,256]{2,1,0:T(8,128)S(1)}, f32[15,32,256]{2,1,0:T(8,128)S(1)}, u32[]{:S(2)}, u32[]{:S(2)}) collective-permute-start(f32[15,32,256]{2,1,0:T(8,128)S(1)} %get-tuple-element.92), channel_id=1, source_target_pairs={{0,8},{1,9},{2,10},{3,11},{4,12},{5,13},{6,14},{7,15},{8,2},{9,3},... | collective-permute-start | bytes 1474568 | tf_op jit(solution)/shard_map/ppermute | solution.py:33
  168.5 13.0 %collective-permute-start.22 = (f32[15,64,256]{2,1,0:T(8,128)S(1)}, f32[15,64,256]{2,1,0:T(8,128)S(1)}, u32[]{:S(2)}, u32[]{:S(2)}) collective-permute-start(f32[15,64,256]{2,1,0:T(8,128)S(1)} %get-tuple-element.82), channel_id=1, source_target_pairs={{0,8},{1,9},{2,10},{3,11},{4,12},{5,13},{6,14},{7,15},{8,2},{9,3},... | collective-permute-start | bytes 2949128 | tf_op jit(solution)/shard_map/ppermute | solution.py:33
  170.4 15.7 %collective-permute-start.23 = (f32[15,64,256]{2,1,0:T(8,128)S(1)}, f32[15,64,256]{2,1,0:T(8,128)S(1)}, u32[]{:S(2)}, u32[]{:S(2)}) collective-permute-start(f32[15,64,256]{2,1,0:T(8,128)S(1)} %get-tuple-element.84), channel_id=1, source_target_pairs={{2,8},{3,9},{4,10},{5,11},{6,12},{7,13},{8,0},{9,1},{10,2},{11,3},... | collective-permute-start | bytes 2949128 | tf_op jit(solution)/shard_map/ppermute | solution.py:33
  176.4 15.6 %collective-permute-start.24 = (f32[15,64,256]{2,1,0:T(8,128)S(1)}, f32[15,64,256]{2,1,0:T(8,128)S(1)}, u32[]{:S(2)}, u32[]{:S(2)}) collective-permute-start(f32[15,64,256]{2,1,0:T(8,128)S(1)} %get-tuple-element.88), channel_id=1, source_target_pairs={{0,8},{1,9},{2,10},{3,11},{4,12},{5,13},{6,14},{7,15},{8,2},{9,3},... | collective-permute-start | bytes 2949128 | tf_op jit(solution)/shard_map/ppermute | solution.py:33
  179.6 16.8 %collective-permute-start.25 = (f32[15,64,256]{2,1,0:T(8,128)S(1)}, f32[15,64,256]{2,1,0:T(8,128)S(1)}, u32[]{:S(2)}, u32[]{:S(2)}) collective-permute-start(f32[15,64,256]{2,1,0:T(8,128)S(1)} %get-tuple-element.90), channel_id=1, source_target_pairs={{2,8},{3,9},{4,10},{5,11},{6,12},{7,13},{8,0},{9,1},{10,2},{11,3},... | collective-permute-start | bytes 2949128 | tf_op jit(solution)/shard_map/ppermute | solution.py:33
  198.5 25.8 %collective-permute-start.28 = (f32[16,64,256]{2,1,0:T(8,128)S(1)}, f32[16,64,256]{2,1,0:T(8,128)S(1)}, u32[]{:S(2)}, u32[]{:S(2)}) collective-permute-start(f32[16,64,256]{2,1,0:T(8,128)S(1)} %log_factor.9.own_ref), channel_id=1, source_target_pairs={{1,16},{3,18},{5,20},{7,22},{8,25},{10,27},{12,29},{14,31},{17,0},... | collective-permute-start | bytes 3145736 | tf_op jit(solution)/shard_map/ppermute | solution.py:33
  202.8 22.9 %collective-permute-start.27 = (f32[16,64,256]{2,1,0:T(8,128)S(1)}, f32[16,64,256]{2,1,0:T(8,128)S(1)}, u32[]{:S(2)}, u32[]{:S(2)}) collective-permute-start(f32[16,64,256]{2,1,0:T(8,128)S(1)} %log_factor.9.own_ref), channel_id=1, source_target_pairs={{1,0},{3,2},{5,4},{7,6},{8,9},{10,11},{12,13},{14,15},{17,16},{19,... | collective-permute-start | bytes 3145736 | tf_op jit(solution)/shard_map/ppermute | solution.py:33
  204.1 21.5 %collective-permute-start.26 = (f32[16,64,256]{2,1,0:T(8,128)S(1)}, f32[16,64,256]{2,1,0:T(8,128)S(1)}, u32[]{:S(2)}, u32[]{:S(2)}) collective-permute-start(f32[16,64,256]{2,1,0:T(8,128)S(1)} %log_factor.9.own_ref), channel_id=1, source_target_pairs={{0,16},{2,18},{4,20},{6,22},{9,25},{11,27},{13,29},{15,31},{16,0},... | collective-permute-start | bytes 3145736 | tf_op jit(solution)/shard_map/ppermute | solution.py:33
  225.9 6.3 %collective-permute-start.29 = (f32[16,128,256]{2,1,0:T(8,128)S(1)}, f32[16,128,256]{2,1,0:T(8,128)S(1)}, u32[]{:S(2)}, u32[]{:S(2)}) collective-permute-start(f32[16,128,256]{2,1,0:T(8,128)S(1)} %last_update.1.one_ref), channel_id=1, source_target_pairs={{0,8},{2,10},{4,12},{6,14},{9,1},{11,3},{13,5},{15,7},{16,24},{18,... | collective-permute-start | bytes 6291464 | tf_op jit(solution)/shard_map/ppermute | solution.py:33

commit v4 on v3

v4 whole, which is shorter than its diff:
```python
import functools

import jax
import jax.numpy as jnp
from jax import lax
from jax.experimental import pallas as pl
from jax.experimental.pallas import tpu as pltpu
from jax.sharding import PartitionSpec as P

ITERS = 2
AXES = ("view", "tile")
F32 = jnp.float32
BF16 = jnp.bfloat16
VMEM = pl.BlockSpec(memory_space=pltpu.VMEM)
SMEM = pl.BlockSpec(memory_space=pltpu.SMEM)
PARAMS = pltpu.CompilerParams(vmem_limit_bytes=20 * 1024 * 1024)
GROUP = 16


def moves(move):
    views, tiles = lax.axis_size("view"), lax.axis_size("tile")
    pairs = []
    for view in range(views):
        for tile in range(tiles):
            target = move(view // 2, view % 2, tile // 2, tile % 2)
            if target is not None:
                g, c, q, r = target
                pairs.append((view * tiles + tile, (2 * g + c) * tiles + 2 * q + r))
    return pairs


def send(array, move):
    return lax.ppermute(array, AXES, moves(move))


def after(array, other):
    return lax.optimization_barrier((array, other))[0]


def to_far(g, c, q, r):
    s = 2 * q + c + (1 if c else -1)
    return (g, s % 2, s // 2, r) if 0 <= s < lax.axis_size("tile") else None


def to_row_partner(g, c, q, r):
    return (g, c, q, 1 - r)


def to_core_partner(g, c, q, r):
    return (g, 1 - c, q, r)


def core():
    return lax.rem(lax.axis_index("view"), 2)


def half():
    return lax.rem(lax.axis_index("tile"), 2)


def split(x):
    high = x.astype(BF16)
    return high, (x - high.astype(F32)).astype(BF16)


def dot(a, b):
    return jnp.dot(a, b, preferred_element_type=F32)


def iota(shape, dim):
    return lax.broadcasted_iota(jnp.int32, shape, dim)


def group_row(half, group, cells_y):
    return group * GROUP + half * (cells_y - GROUP - 2 * group * GROUP)


def global_row(half, local, cells_y):
    group = local // GROUP
    return group_row(half, group, cells_y) + (local - group * GROUP)


def wide_local(place, own, wide):
    group = (place - own) // GROUP
    return own + (wide - own) - GROUP - group * GROUP + (place - own - group * GROUP)


def wide_group(group, own_groups, groups):
    return group if group < own_groups else own_groups + groups - 1 - group


def pad_to(value, unit):
    return -(-value // unit) * unit


def call(kernel, out_shape, in_specs, name, scratch=()):
    return pl.pallas_call(
        kernel,
        out_shape=out_shape,
        in_specs=in_specs,
        out_specs=jax.tree.map(lambda _: VMEM, out_shape),
        scratch_shapes=list(scratch),
        compiler_params=PARAMS,
        name=name,
    )


def tables_kernel(
    ky_ref, tz_ref, tx_ref, yf_ref, ya_ref, zhi_ref, zlo_ref, xhi_ref, xlo_ref, *, sizes, cells_y, radius_x, radius_z
):
    taps = ky_ref.shape[1]
    radius = taps // 2
    side = half()
    own, near, wide = sizes
    for index in range(4):
        adjoint = index >= 2
        out_ref, rows, width = (ya_ref, own, near) if adjoint else (yf_ref, near, wide)
        lanes = out_ref.shape[2]
        row = global_row(side, iota((rows, lanes), 0), cells_y)
        lane = iota((rows, lanes), 1)
        turned = lane if adjoint else jnp.where(lane < own, lane, wide_local(lane, own, wide))
        col = global_row(side, turned, cells_y)
        delta = (row - col if adjoint else col - row) + radius
        delta = jnp.where(lane < width, delta, -1)
        band = jnp.zeros((rows, lanes), F32)
        for a in range(taps):
            band = jnp.where(delta == a, ky_ref[index % 2, a], band)
        high, low = split(band)
        high, low = high.astype(F32), low.astype(F32)
        out_ref[index % 2] = (high + pltpu.roll(high, width, 1) + pltpu.roll(low, 2 * width, 1)).astype(BF16)

    lanes = tz_ref.shape[1]
    near_z = jnp.abs(iota((lanes, lanes), 1) - iota((lanes, lanes), 0)) <= radius_z
    for index in range(4):
        base = pltpu.roll(tz_ref[index:index + 1, :], lanes - radius_z, 1)
        band = pltpu.roll(jnp.broadcast_to(base, (lanes, lanes)), 0, 1, stride=1, stride_axis=0)
        zhi_ref[index], zlo_ref[index] = split(jnp.where(near_z, band, jnp.zeros_like(band)))

    rows, lanes = xhi_ref.shape[1] // 2, tx_ref.shape[1]
    for index in range(4):
        base = jnp.broadcast_to(tx_ref[index:index + 1, :], (rows, lanes))
        band = pltpu.roll(base, 0, 1, stride=1, stride_axis=0)
        lane = iota((rows, lanes), 1)
        first, last = 8 * radius_x, 8 * radius_x + rows
        turned = jnp.where(
            lane < first, pltpu.roll(band, lanes - last, 1), jnp.where(lane < last, band, pltpu.roll(band, last, 1))
        )
        turned = jnp.where(lane < last + first, turned, jnp.zeros_like(turned))
        band = jnp.where(core() == 0, band, turned)[:, :xhi_ref.shape[2]]
        place = (index // 2, slice(index % 2 * rows, index % 2 * rows + rows))
        xhi_ref[place], xlo_ref[place] = split(band)


def make_tables(kx, ky, kz, planes, cells_y, cells_z, sizes):
    own, near, wide = sizes
    taps_x, taps_z = kx.shape[1], kz.shape[1]
    depth = 8 * pad_to(planes + taps_x - 1, 16)
    lanes = max(512, 1 << (depth - 1).bit_length())
    zero = jnp.zeros((), F32)
    tx = jnp.concatenate([kx, kx[:, ::-1]])
    tx = lax.pad(tx, zero, ((0, 0, 0), (0, lanes - 8 * taps_x + 7, 7)))
    tz = jnp.concatenate([kz[:, ::-1], kz])
    tz = lax.pad(tz, zero, ((0, 0, 0), (0, cells_z - taps_z, 0)))
    kernel = functools.partial(tables_kernel, sizes=sizes, cells_y=cells_y, radius_x=taps_x // 2, radius_z=taps_z // 2)
    shape = jax.ShapeDtypeStruct
    out_shape = (
        shape((2, near, pad_to(3 * wide, 128)), BF16),
        shape((2, own, pad_to(3 * near, 128)), BF16),
        shape((4, cells_z, cells_z), BF16),
        shape((4, cells_z, cells_z), BF16),
        shape((2, 2 * 8 * planes, depth), BF16),
        shape((2, 2 * 8 * planes, depth), BF16),
    )
    return call(kernel, out_shape, [SMEM, VMEM, VMEM], "band_matrices")(ky, tz, tx)


def window_kernel(estimate_ref, own_ref, other_ref):
    cells_y = estimate_ref.shape[1]
    groups = own_ref.shape[1] // GROUP
    for side, out_ref in ((half(), own_ref), (1 - half(), other_ref)):
        for group in range(groups):
            local = wide_group(group, cells_y // 2 // GROUP, groups)
            start = pl.multiple_of(group_row(side, local, cells_y), GROUP)
            out_ref[:, group * GROUP:(group + 1) * GROUP, :] = estimate_ref[:, pl.ds(start, GROUP), :]


def make_windows(estimate, wide):
    planes, _, cells_z = estimate.shape
    shape = jax.ShapeDtypeStruct((planes, wide, cells_z), F32)
    return call(window_kernel, (shape, shape), [VMEM], "estimate_windows")(estimate)


def put_edges(out_ref, far_ref, near_ref):
    radius = far_ref.shape[0]
    beyond = out_ref.shape[0] - radius
    for p in range(radius):
        far_ref[p] = out_ref[p + core() * beyond]
        near_ref[p] = out_ref[p + (1 - core()) * beyond]


def assemble_kernel(window_ref, *refs):
    pieces, (out_ref, far_ref, near_ref) = refs[:-3], refs[-3:]
    straight, group = core() == half(), lax.axis_index("view") // 2
    planes, share = out_ref.shape[0], pieces[0].shape[0]
    for p in range(planes):
        turn = lax.rem(group - p // share + len(pieces), len(pieces))
        value = pieces[0][p % share]
        for k in range(1, len(pieces)):
            value = jnp.where(turn == k, pieces[k][p % share], value)
        out_ref[p] = jnp.where(straight, window_ref[p], value)
    put_edges(out_ref, far_ref, near_ref)


def edge_shapes(shape, radius):
    edge = jax.ShapeDtypeStruct((radius,) + shape[1:], F32)
    return jax.ShapeDtypeStruct(shape, F32), edge, edge


def assemble(window, pieces, radius):
    out_shape = edge_shapes(window.shape, radius)
    return call(assemble_kernel, out_shape, [VMEM] * (1 + len(pieces)), "estimate")(window, *pieces)


def shift_kernel(offsets_ref, acq_ref, mask_ref, first_ref, second_ref, turned_ref):
    planes, cells_y, cells_z = acq_ref.shape
    near = first_ref.shape[1]
    shift_y, shift_z = offsets_ref[0, 1], offsets_ref[0, 2]
    row = iota((cells_y, cells_z), 0) + shift_y
    col = iota((cells_y, cells_z), 1) + shift_z
    inside = (row >= 0) & (row < cells_y) & (col >= 0) & (col < cells_z)
    turn_y = lax.rem(cells_y - shift_y, cells_y)
    turn_z = lax.rem(cells_z - shift_z, cells_z)

    def body(p, carry):
        x = pltpu.roll(pltpu.roll(acq_ref[p], turn_z, 1), turn_y, 0)
        turned_ref[...] = jnp.where(inside, x, jnp.zeros_like(x))
        for side, out_ref in ((core(), first_ref), (1 - core(), second_ref)):
            for group in range(near // GROUP):
                start = pl.multiple_of(group_row(side, group, cells_y), GROUP)
                out_ref[p, group * GROUP:(group + 1) * GROUP, :] = turned_ref[pl.ds(start, GROUP), :]
        return carry

    lax.fori_loop(0, planes, body, 0)
    mask = mask_ref[...].astype(F32)
    for out_ref in (first_ref, second_ref):
        out_ref[planes] = jnp.zeros((near, cells_z), F32)
        out_ref[planes, :planes, :cells_y] = mask


def shift_and_cut(offsets, acquired, mask, near):
    planes, cells_y, cells_z = acquired.shape
    shape = jax.ShapeDtypeStruct((planes + 1, near, cells_z), F32)
    scratch = [pltpu.VMEM((cells_y, cells_z), F32)]
    return call(shift_kernel, (shape, shape), [SMEM, VMEM, VMEM], "shift_recorded", scratch)(offsets, acquired, mask)


def spread_x(hi_ref, lo_ref, index, start, count, refs, row):
    lanes = refs[1].shape[2]
    depth = hi_ref.shape[2]
    parts = [ref[:, pl.ds(row, 8), :] for ref in refs]
    missing = depth // 8 - sum(part.shape[0] for part in parts)
    if missing:
        parts.append(jnp.zeros((missing, 8, lanes), F32))
    high, low = split(jnp.concatenate(parts, axis=0).reshape(depth, lanes))
    band = hi_ref[index, start:start + count, :]
    out = dot(band, high) + (dot(band, low) + dot(lo_ref[index, start:start + count, :], high))
    return out.reshape(count // 8, 8, lanes)


def blur_x_kernel(hi_ref, lo_ref, far_ref, own_ref, near_ref, first_ref, second_ref):
    planes, rows, lanes = own_ref.shape

    def body(step, carry):
        row = pl.multiple_of(step * 8, 8)
        out = spread_x(hi_ref, lo_ref, 0, 0, hi_ref.shape[1], (far_ref, own_ref, near_ref), row)
        first_ref[:, pl.ds(row, 8), :] = out[:planes]
        second_ref[:, pl.ds(row, 8), :] = out[planes:]
        return carry

    lax.fori_loop(0, rows // 8, body, 0)


def blur_x(tables, far, own, near):
    shape = jax.ShapeDtypeStruct(own.shape, F32)
    return call(blur_x_kernel, (shape, shape), [VMEM] * 5, "blur_x")(*tables[4:], far, own, near)


def spread_y(band, x):
    high, low = split(x)
    parts = [high, low, high]
    rest = band.shape[1] - 3 * x.shape[0]
    if rest:
        parts.append(jnp.zeros((rest, x.shape[1]), BF16))
    return dot(band, jnp.concatenate(parts, axis=0))


def spread_z(x, hi_ref, lo_ref, index):
    high, low = split(x)
    return dot(high, hi_ref[index]) + (dot(low, hi_ref[index]) + dot(high, lo_ref[index]))


def ratio_planes(wide_refs, fetch, yf_ref, ya_ref, zhi_ref, zlo_ref, order, outs):
    out_ref, far_ref, near_ref = outs
    planes, rows, _ = out_ref.shape
    near = yf_ref.shape[1]
    step = 4
    for start in range(0, planes, step):
        block = range(start, min(start + step, planes))
        blurred = jnp.concatenate(
            [spread_y(yf_ref[order], jnp.concatenate([ref[p] for ref in wide_refs], axis=0)) for p in block], axis=0
        )
        blurred = spread_z(blurred, zhi_ref, zlo_ref, order)
        image = jnp.concatenate([fetch(p) for p in block], axis=0)
        ratio = jnp.where(image >= 0, image / blurred, jnp.ones_like(image))
        spread = jnp.concatenate(
            [spread_y(ya_ref[order], ratio[k * near:(k + 1) * near]) for k in range(len(block))], axis=0
        )
        spread = spread_z(spread, zhi_ref, zlo_ref, 2 + order)
        for k, p in enumerate(block):
            out_ref[p] = spread[k * rows:(k + 1) * rows]
    put_edges(out_ref, far_ref, near_ref)


def first_ratio_kernel(shift_ref, far_ref, near_ref, own_ref, *refs, order, extent_x, cells_y):
    image_ref = refs[-1]
    planes, near, cells_z = image_ref.shape
    side = half()
    slab = lax.axis_index("tile") - side + core()
    shift_x, shift_y, shift_z = (shift_ref[order, i] for i in range(3))
    lanes = pad_to(cells_y, 128)
    pick = iota((near, lanes), 1) == global_row(side, iota((near, lanes), 0), cells_y)
    mask = own_ref[planes, :planes, :lanes].astype(BF16)
    columns = lax.dot_general(
        pick.astype(F32).astype(BF16), mask, (((1,), (1,)), ((), ())), preferred_element_type=F32
    )
    row = global_row(side, iota((near, cells_z), 0), cells_y) + shift_y
    col = iota((near, cells_z), 1) + shift_z
    inside = (row >= 0) & (row < cells_y) & (col >= 0) & (col < cells_z)

    def fetch(p):
        source = p + shift_x
        x = slab * planes + source
        beyond = jnp.clip(jnp.where(source < 0, source + planes, source - planes), 0, planes - 1)
        is_far = (source < 0) == (core() == 0)
        outer = jnp.where(is_far, far_ref[beyond], near_ref[beyond])
        is_own = (source >= 0) & (source < planes)
        value = jnp.where(is_own, own_ref[jnp.clip(source, 0, planes - 1)], outer)
        weight = jnp.broadcast_to(columns[:, p:p + 1], (near, cells_z))
        covered = inside & (weight > 0.5) & (x >= 0) & (x < extent_x)
        value = jnp.where(covered, value, jnp.full_like(value, -1.0))
        image_ref[p] = value
        return value

    ratio_planes(refs[:-8], fetch, *refs[-8:-4], order, refs[-4:-1])


def next_ratio_kernel(image_ref, *refs, order):
    ratio_planes(refs[:-7], lambda p: image_ref[p], *refs[-7:-3], order, refs[-3:])


def ratio_shapes(wides, tables, radius):
    planes, _, lanes = wides[0].shape
    return edge_shapes((planes, tables[1].shape[1], lanes), radius)


def first_ratio(shifts, blocks, wides, tables, order, radius, extent_x, cells_y):
    planes, _, lanes = wides[0].shape
    kernel = functools.partial(first_ratio_kernel, order=order, extent_x=extent_x, cells_y=cells_y)
    image = jax.ShapeDtypeStruct((planes, tables[0].shape[1], lanes), F32)
    out_shape = ratio_shapes(wides, tables, radius) + (image,)
    return call(kernel, out_shape, [SMEM] + [VMEM] * (7 + len(wides)), "image_and_ratio")(
        shifts, *blocks, *wides, *tables[:4]
    )


def next_ratio(image, wides, tables, order, radius):
    kernel = functools.partial(next_ratio_kernel, order=order)
    return call(kernel, ratio_shapes(wides, tables, radius), [VMEM] * (5 + len(wides)), "ratio")(
        image, *wides, *tables[:4]
    )


def factor_kernel(hi_ref, lo_ref, before_ref, far_ref, own_ref, near_ref, out_ref, *, order, start, share):
    planes, rows, _ = out_ref.shape

    def body(step, carry):
        row = pl.multiple_of(step * 8, 8)
        source = pl.multiple_of(start + row, 8)
        total = before_ref[:, pl.ds(source, 8), :]
        if share:
            total = share * jnp.log(total)
        factor = spread_x(hi_ref, lo_ref, 1, order * 8 * planes, 8 * planes, (far_ref, own_ref, near_ref), source)
        out_ref[:, pl.ds(row, 8), :] = total + jnp.log(factor)
        return carry

    lax.fori_loop(0, rows // 8, body, 0)


def log_factor(tables, before, side, order, start, rows, share):
    planes, _, lanes = side[1].shape
    kernel = functools.partial(factor_kernel, order=order, start=start, share=share)
    shape = jax.ShapeDtypeStruct((planes, rows, lanes), F32)
    return call(kernel, shape, [VMEM] * 6, "log_factor")(*tables[4:], before, *side)


def update_kernel(*refs):
    parts, edge_ref, (out_ref, far_ref, near_ref) = refs[:-4], refs[-4], refs[-3:]
    for p in range(out_ref.shape[0]):
        total = parts[0][p]
        for part in parts[1:]:
            total = total + part[p]
        out_ref[p] = jnp.concatenate([jnp.exp(total), edge_ref[p]], axis=0)
    put_edges(out_ref, far_ref, near_ref)


def update(parts, edge, radius):
    planes, rows, lanes = parts[0].shape
    out_shape = edge_shapes((planes, rows + edge.shape[1], lanes), radius)
    return call(update_kernel, out_shape, [VMEM] * (len(parts) + 1), "update")(*parts, edge)


def finish_kernel(*refs):
    own, other, out_ref = refs[:(len(refs) - 1) // 2], refs[(len(refs) - 1) // 2:-1], refs[-1]
    straight = core() == half()
    side = jnp.where(straight, half(), 1 - half())
    groups = out_ref.shape[1] // GROUP
    for group in range(groups):
        rows = slice(group * GROUP, (group + 1) * GROUP)
        own_total, other_total = own[0][:, rows, :], other[0][:, rows, :]
        for part in own[1:]:
            own_total = own_total + part[:, rows, :]
        for part in other[1:]:
            other_total = other_total + part[:, rows, :]
        start = jnp.where(side == 0, group, groups - 1 - group) * GROUP
        out_ref[:, pl.ds(pl.multiple_of(start, GROUP), GROUP), :] = jnp.exp(jnp.where(straight, own_total, other_total))


def finish(own_parts, other_parts):
    shape = jax.ShapeDtypeStruct(own_parts[0].shape, F32)
    return call(finish_kernel, shape, [VMEM] * (2 * len(own_parts)), "last_update")(*own_parts, *other_parts)


def join_kernel(mine_ref, theirs_ref, out_ref, semaphores):
    rows = mine_ref.shape[1]
    copies = []
    for index, (source_ref, side) in enumerate(((mine_ref, core()), (theirs_ref, 1 - core()))):
        target = out_ref.at[:, pl.ds(pl.multiple_of(side * rows, rows), rows), :]
        copies.append(pltpu.make_async_copy(source_ref, target, semaphores.at[index]))
    for copy in copies:
        copy.start()
    for copy in copies:
        copy.wait()


def join(mine, theirs):
    planes, rows, lanes = mine.shape
    anywhere = pl.BlockSpec(memory_space=pl.ANY)
    return pl.pallas_call(
        join_kernel,
        out_shape=jax.ShapeDtypeStruct((planes, 2 * rows, lanes), F32),
        in_specs=[anywhere, anywhere],
        out_specs=anywhere,
        scratch_shapes=[pltpu.SemaphoreType.DMA((2,))],
        compiler_params=PARAMS,
        name="join_halves",
    )(mine, theirs)


def shards(acquired, estimate, offsets, view_mask, kern_x, kern_y, kern_z):
    planes, cells_y, cells_z = estimate.shape
    views, slabs = lax.axis_size("view"), lax.axis_size("tile")
    groups = views // 2
    taps_x, taps_y, taps_z = kern_x.shape[1], kern_y.shape[1], kern_z.shape[1]
    radius = taps_x // 2
    own_rows = cells_y // 2
    near = own_rows + pad_to(taps_y // 2, GROUP)
    wide = own_rows + pad_to(2 * (taps_y // 2), GROUP)
    edge_rows = wide - own_rows
    inner_rows = own_rows - edge_rows
    group = lax.axis_index("view") // 2
    straight = core() == half()

    def across(turn, half_of=lambda r: r, core_of=lambda c: c, when=lambda c, r: True):
        return lambda g, c, q, r: ((g + turn) % groups, core_of(c), q, half_of(r)) if when(c, r) else None

    def neighbours(far, near):
        return send(far, to_far), send(near, to_core_partner)

    window, crossing = make_windows(estimate, wide)
    piece = lax.dynamic_slice_in_dim(crossing, group * (planes // groups), planes // groups, 0)
    piece = send(piece, across(0, lambda r: 1 - r, when=lambda c, r: c == r))

    acquired = after(acquired, window)
    first, second = shift_and_cut(offsets, acquired[0], view_mask[0], near)
    piece = after(piece, first)
    arrived = send(first, lambda g, c, q, r: (g, r, q, c) if c != r else None)

    mine = jnp.concatenate([kern_x[0], kern_y[0], kern_z[0], offsets[0].astype(F32)])
    mine = after(mine, first)
    other = send(mine, to_core_partner)
    both = jnp.where(straight, jnp.stack([mine, other]), jnp.stack([other, mine]))
    kx = both[:, :taps_x]
    ky = both[:, taps_x:taps_x + taps_y]
    kz = both[:, taps_x + taps_y:taps_x + taps_y + taps_z]
    shifts = both[:, taps_x + taps_y + taps_z:].astype(jnp.int32)
    tables = make_tables(kx, ky, kz, planes, cells_y, cells_z, (own_rows, near, wide))

    pieces = [piece] + [send(piece, across(turn, when=lambda c, r: c != r)) for turn in range(1, groups)]
    current, distant, close = assemble(window, pieces, radius)
    second = after(second, distant)
    distant, close = neighbours(distant, close)
    chunks = [(distant, current, close)]
    second = send(second, lambda g, c, q, r: (g, r, q, 1 - c))
    first = jnp.where(straight, first, arrived)
    blocks = [(*neighbours(first, first), first)]

    blocks.append((*neighbours(second, second), second))
    images = [None, None]

    for step in range(ITERS):
        wides = [blur_x(tables, *chunk) for chunk in chunks]
        sides = []
        for order in range(2):
            parts = [chunk[order] for chunk in wides]
            if step == 0:
                spread, distant, close, images[order] = first_ratio(
                    shifts, blocks[order], parts, tables, order, radius, planes * slabs, cells_y
                )
            else:
                spread, distant, close = next_ratio(images[order], parts, tables, order, radius)
            distant, close = neighbours(distant, close)
            sides.append((distant, spread, close))
        total = log_factor(tables, current, sides[0], 0, 0, own_rows, 1.0 / groups)
        if step < ITERS - 1:
            edge = log_factor(tables, total, sides[1], 1, inner_rows, edge_rows, 0)
            inner = log_factor(tables, total, sides[1], 1, 0, inner_rows, 0)
            edge_parts = [edge] + [send(edge, across(turn)) for turn in range(1, groups)]
            inner_parts = [inner] + [send(inner, across(turn)) for turn in range(1, groups)]
            edge = jnp.exp(sum(edge_parts[1:], edge_parts[0]))
            beyond = send(edge, to_row_partner)
            current, distant, close = update(inner_parts, edge, radius)
            distant, close = neighbours(distant, close)
            chunks = [(distant, current, close)]
            rest = planes - radius
            distant, close = neighbours(
                lax.dynamic_slice_in_dim(beyond, core() * rest, radius, 0),
                lax.dynamic_slice_in_dim(beyond, (1 - core()) * rest, radius, 0),
            )
            chunks.append((distant, beyond, close))

    own = log_factor(tables, total, sides[1], 1, 0, own_rows, 0)
    other_parts = [
        send(own, across(turn, lambda r: 1 - r, lambda c: 1 - c, lambda c, r: c != r)) for turn in reversed(range(groups))
    ]
    own_parts = [own] + [send(own, across(turn, when=lambda c, r: c == r)) for turn in range(1, groups)]
    mine = finish(own_parts, other_parts)
    return join(mine, send(mine, to_core_partner))


def solution(mesh):
    in_specs = (
        P("view", "tile", None, None),
        P("tile", None, None),
        P("view", None),
        P("view", "tile", None),
        P("view", None),
        P("view", None),
        P("view", None),
    )
    out_specs = P("tile", None, None)
    return jax.shard_map(shards, mesh=mesh, in_specs=in_specs, out_specs=out_specs, check_vma=False)
```

time: 237 us -> 227 us (0.958)
  starting transfers between devices: 64.7 us -> 56.1 us
  Pallas kernels: 47.3 us -> 52.5 us
  waiting for transfers between devices: 108 us -> 104 us
    ppermute x30, starting transfers between devices: 64.7 us -> 56.1 us  [send(): return lax.ppermute(array, AXES, moves(move))]
    ppermute x30, waiting for transfers between devices: 108 us -> 104 us  [send(): return lax.ppermute(array, AXES, moves(move))]
    unnamed x30 -> x38, local copies, waits for them, and re-layouts: 9.24 us -> 7.5 us
  transfers between devices with their start and end apart: 30 -> 30, of which waited for: 19 -> 16; matrix products, arithmetic and copies ran while one was open for 2% -> 2% of each run, Pallas kernels for 16% -> 19%
where the time goes in v4:
time: 227 us; the launch traced here: 226 us
  waiting for transfers between devices  104 us (46%)
  starting transfers between devices  56.1 us (25%)
  Pallas kernels  52.5 us (23%)
  local copies, waits for them, and re-layouts  9.24 us (4%)
  other arithmetic  3.73 us (2%)
    ppermute x30, waiting for transfers between devices, send(): return lax.ppermute(array, AXES, moves(move))  104 us
    ppermute x30, starting transfers between devices, send(): return lax.ppermute(array, AXES, moves(move))  56.1 us
    pallas_call x2, Pallas kernels, first_ratio(): call(kernel, out_shape, [SMEM] + [VMEM] * (7 + len(wides)), 'image_and_ra...  12.4 us
    pallas_call x3, Pallas kernels, blur_x(): call(blur_x_kernel, (shape, shape), [VMEM] * 5, 'blur_x')  11.5 us
    pallas_call x5, Pallas kernels, log_factor(): call(kernel, shape, [VMEM] * 6, 'log_factor')(*tables[4:], before, *side)  8.45 us
    unnamed x38, local copies, waits for them, and re-layouts  7.5 us
    pallas_call x2, Pallas kernels, next_ratio(): call(kernel, ratio_shapes(wides, tables, radius), [VMEM] * (5 + len(wides...  7.46 us
    pallas_call x1, Pallas kernels, shift_and_cut(): call(shift_kernel, (shape, shape), [SMEM, VMEM, VMEM], 'shift_recorded',...  4.58 us
  transfers between devices with their start and end apart: 30, of which 16 were waited for; matrix products, arithmetic and copies ran while one was open for 2% of the time, Pallas kernels for 19%

profile of v4, /device:TPU:17, one launch (start us, length us, event | category | flops | bytes accessed | tf_op | source)
XLA Modules:
  0.0 225.8 jit_solution(4667071218339473341)
XLA Ops:
  0.0 1.6 copy-done.1
  5.4 1.4 collective-permute-start.1
  6.8 4.6 %shift_recorded.1 = (f32[17,80,256]{2,1,0:T(8,128)}, f32[17,80,256]{2,1,0:T(8,128)}) custom-call(s32[1,3]{1,0:T(1,128)S(1)} %copy-done.14, f32[16,128,256]{2,1,0:T(8,128)S(1)} %bitcast.9, s32[16,128]{1,0:T(8,128)S(1)} %bitcast.10), custom_call_target="tpu_custom_call" | custom-call | tf_op jit(solution)/shard_map/shift_recorded/pallas_call | solution.py:254
  11.4 6.8 %collective-permute-done.1.refs_0_ = f32[8,96,256]{2,1,0:T(8,128)S(1)} collective-permute-done((f32[8,96,256]{2,1,0:T(8,128)S(1)}, f32[8,96,256]{2,1,0:T(8,128)S(1)}, u32[]{:S(2)}, u32[]{:S(2)}) %collective-permute-start.1) | collective-permute-done | bytes 786464 | tf_op jit(solution)/shard_map/ppermute | solution.py:33
  18.2 3.2 %collective-permute-start.2 = (f32[8,96,256]{2,1,0:T(8,128)S(1)}, f32[8,96,256]{2,1,0:T(8,128)S(1)}, u32[]{:S(2)}, u32[]{:S(2)}) collective-permute-start(f32[8,96,256]{2,1,0:T(8,128)S(1)} %collective-permute-done.1.refs_0_), channel_id=1, source_target_pairs={{1,17},{3,19},{5,21},{7,23},{8,24},{10,26},{12,28},{14,30},{17,1},... | collective-permute-start | bytes 2359304 | tf_op jit(solution)/shard_map/ppermute | solution.py:33
  21.5 5.1 %collective-permute-start.3 = (f32[17,80,256]{2,1,0:T(8,128)}, f32[17,80,256]{2,1,0:T(8,128)}, u32[]{:S(2)}, u32[]{:S(2)}) collective-permute-start(f32[17,80,256]{2,1,0:T(8,128)} %get-tuple-element.47), channel_id=1, source_target_pairs={{1,8},{3,10},{5,12},{7,14},{8,1},{10,3},{12,5},{14,7},{17,24},{19,... | collective-permute-start | bytes 4177928 | tf_op jit(solution)/shard_map/ppermute | solution.py:33
  26.6 4.5 %collective-permute-done.2.refs_1_ = f32[8,96,256]{2,1,0:T(8,128)S(1)} collective-permute-done((f32[8,96,256]{2,1,0:T(8,128)S(1)}, f32[8,96,256]{2,1,0:T(8,128)S(1)}, u32[]{:S(2)}, u32[]{:S(2)}) %collective-permute-start.2) | collective-permute-done | bytes 786464 | tf_op jit(solution)/shard_map/ppermute | solution.py:33
  31.1 1.5 estimate.1
  32.6 1.9 collective-permute-start.6
  35.2 3.9 %collective-permute-start = (f32[126]{0:T(128)S(1)}, f32[126]{0:T(128)S(1)}, u32[]{:S(2)}, u32[]{:S(2)}) collective-permute-start(f32[126]{0:T(128)S(1)} %pad_maximum_fusion.1), channel_id=1, source_target_pairs={{0,8},{1,9},{2,10},{3,11},{4,12},{5,13},{6,14},{7,15},{8,0},{9,1},... | collective-permute-start | bytes 1520 | tf_op jit(solution)/shard_map/ppermute | solution.py:33
  39.3 5.8 %collective-permute-done.3 = f32[17,80,256]{2,1,0:T(8,128)} collective-permute-done((f32[17,80,256]{2,1,0:T(8,128)}, f32[17,80,256]{2,1,0:T(8,128)}, u32[]{:S(2)}, u32[]{:S(2)}) %collective-permute-start.3) | collective-permute-done | bytes 1392672 | tf_op jit(solution)/shard_map/ppermute | solution.py:33
  45.1 2.7 %broadcast_select_fusion.own_ref = f32[17,80,256]{2,1,0:T(8,128)} fusion(f32[17,80,256]{2,1,0:T(8,128)} %get-tuple-element.47, f32[17,80,256]{2,1,0:T(8,128)} %collective-permute-done.3, pred[]{:T(512)S(6)} %eq.3), kind=kLoop, calls=%fused_computation | loop fusion | flops 348160 | bytes 4177921 | tf_op jit(solution)/shard_map/jit(_where)/select_n | solution.py:514
  47.7 1.9 collective-permute-start.4
  50.3 8.0 %collective-permute-done.10.own_ref = f32[17,80,256]{2,1,0:T(8,128)} collective-permute-done((f32[17,80,256]{2,1,0:T(8,128)}, f32[17,80,256]{2,1,0:T(8,128)}, u32[]{:S(2)}, u32[]{:S(2)}) %collective-permute-start.10) | collective-permute-done | bytes 1392672 | tf_op jit(solution)/shard_map/ppermute | solution.py:33
  58.3 2.4 %collective-permute-start.11 = (f32[17,80,256]{2,1,0:T(8,128)}, f32[17,80,256]{2,1,0:T(8,128)}, u32[]{:S(2)}, u32[]{:S(2)}) collective-permute-start(f32[17,80,256]{2,1,0:T(8,128)} %collective-permute-done.10.own_ref), channel_id=1, source_target_pairs={{2,8},{3,9},{4,10},{5,11},{6,12},{7,13},{8,2},{9,3},{10,4},{11,5},... | collective-permute-start | bytes 4177928 | tf_op jit(solution)/shard_map/ppermute | solution.py:33
  62.4 2.3 band_matrices.1
  64.7 1.4 copy-done.5
  66.1 5.7 %blur_x.3 = (f32[16,96,256]{2,1,0:T(8,128)S(1)}, f32[16,96,256]{2,1,0:T(8,128)S(1)}) custom-call(bf16[2,256,384]{2,1,0:T(8,128)(2,1)S(1)} %get-tuple-element.49.hi_ref, bf16[2,256,384]{2,1,0:T(8,128)(2,1)S(1)} %get-tuple-element.50.lo_ref, f32[15,96,256]{2,1,0:T(8,128)S(1)} %copy-done.5, f32[16,96,256]{2,1,0:T(8,128)S(1)} %get-tuple-element.53.own_ref.before_ref, ...), custom_call_target="tpu_custom_call" | custom-call | tf_op jit(solution)/shard_map/blur_x/pallas_call | solution.py:285
  71.9 6.2 %image_and_ratio.2 = (f32[16,64,256]{2,1,0:T(8,128)S(1)}, f32[15,64,256]{2,1,0:T(8,128)S(1)}, f32[15,64,256]{2,1,0:T(8,128)S(1)}, f32[16,80,256]{2,1,0:T(8,128)S(1)}) custom-call(s32[2,3]{1,0:T(2,128)S(1)} %slice_convert_fusion.shift_ref, f32[17,80,256]{2,1,0:T(8,128)} %collective-permute-done.4.far_ref, f32[17,80,256]{2,1,0:T(8,128)} %collective-permute-done.5.near_ref, ...), custom_call_target="tpu_custom_call" | custom-call | tf_op jit(solution)/shard_map/image_and_ratio/pallas_call | solution.py:371
  79.1 3.0 %collective-permute-start.8 = (f32[15,64,256]{2,1,0:T(8,128)S(1)}, f32[15,64,256]{2,1,0:T(8,128)S(1)}, u32[]{:S(2)}, u32[]{:S(2)}) collective-permute-start(f32[15,64,256]{2,1,0:T(8,128)S(1)} %get-tuple-element.61), channel_id=1, source_target_pairs={{2,8},{3,9},{4,10},{5,11},{6,12},{7,13},{8,2},{9,3},{10,4},{11,5},... | collective-permute-start | bytes 2949128 | tf_op jit(solution)/shard_map/ppermute | solution.py:33
  83.5 6.2 %image_and_ratio.3 = (f32[16,64,256]{2,1,0:T(8,128)S(1)}, f32[15,64,256]{2,1,0:T(8,128)S(1)}, f32[15,64,256]{2,1,0:T(8,128)S(1)}, f32[16,80,256]{2,1,0:T(8,128)S(1)}) custom-call(s32[2,3]{1,0:T(2,128)S(1)} %slice_convert_fusion.shift_ref, f32[17,80,256]{2,1,0:T(8,128)} %collective-permute-done.11.far_ref, f32[17,80,256]{2,1,0:T(8,128)} %collective-permute-done.12.near_ref, ...), custom_call_target="tpu_custom_call" | custom-call | tf_op jit(solution)/shard_map/image_and_ratio/pallas_call | solution.py:371
  89.7 2.1 collective-permute-start.13
  92.4 2.4 %collective-permute-done.8.far_ref = f32[15,64,256]{2,1,0:T(8,128)S(1)} collective-permute-done((f32[15,64,256]{2,1,0:T(8,128)S(1)}, f32[15,64,256]{2,1,0:T(8,128)S(1)}, u32[]{:S(2)}, u32[]{:S(2)}) %collective-permute-start.8) | collective-permute-done | bytes 983072 | tf_op jit(solution)/shard_map/ppermute | solution.py:33
  94.8 2.1 log_factor.5.before_ref
  97.0 8.1 %collective-permute-done.13.far_ref = f32[15,64,256]{2,1,0:T(8,128)S(1)} collective-permute-done((f32[15,64,256]{2,1,0:T(8,128)S(1)}, f32[15,64,256]{2,1,0:T(8,128)S(1)}, u32[]{:S(2)}, u32[]{:S(2)}) %collective-permute-start.13) | collective-permute-done | bytes 983072 | tf_op jit(solution)/shard_map/ppermute | solution.py:33
  106.2 1.5 collective-permute-start.16
  108.8 10.5 %collective-permute-done.16 = f32[16,32,256]{2,1,0:T(8,128)S(1)} collective-permute-done((f32[16,32,256]{2,1,0:T(8,128)S(1)}, f32[16,32,256]{2,1,0:T(8,128)S(1)}, u32[]{:S(2)}, u32[]{:S(2)}) %collective-permute-start.16) | collective-permute-done | bytes 524320 | tf_op jit(solution)/shard_map/ppermute | solution.py:33
  120.3 3.9 %collective-permute-start.19 = (f32[16,32,256]{2,1,0:T(8,128)}, f32[16,32,256]{2,1,0:T(8,128)S(1)}, u32[]{:S(2)}, u32[]{:S(2)}) collective-permute-start(f32[16,32,256]{2,1,0:T(8,128)} %add_exponential_fusion.refs_2_), channel_id=1, source_target_pairs={{0,1},{1,0},{2,3},{3,2},{4,5},{5,4},{6,7},{7,6},{8,9},{9,8},{10,11... | collective-permute-start | bytes 1572872 | tf_op jit(solution)/shard_map/ppermute | solution.py:33
  124.2 6.4 %collective-permute-done.15.refs_1_ = f32[16,32,256]{2,1,0:T(8,128)S(1)} collective-permute-done((f32[16,32,256]{2,1,0:T(8,128)S(1)}, f32[16,32,256]{2,1,0:T(8,128)S(1)}, u32[]{:S(2)}, u32[]{:S(2)}) %collective-permute-start.15) | collective-permute-done | bytes 524320 | tf_op jit(solution)/shard_map/ppermute | solution.py:33
  130.6 2.5 %update.1 = (f32[16,64,256]{2,1,0:T(8,128)S(1)}, f32[15,64,256]{2,1,0:T(8,128)}, f32[15,64,256]{2,1,0:T(8,128)}) custom-call(f32[16,32,256]{2,1,0:T(8,128)S(1)} %log_factor.6.refs_0_, f32[16,32,256]{2,1,0:T(8,128)S(1)} %collective-permute-done.15.refs_1_, f32[16,32,256]{2,1,0:T(8,128)} %add_exponential_fusion.refs_2_), custom_call_target="tpu_custom_call" | custom-call | tf_op jit(solution)/shard_map/update/pallas_call | solution.py:419
  133.1 1.9 collective-permute-start.17
  136.4 2.4 %collective-permute-start.20 = (f32[15,32,256]{2,1,0:T(8,128)S(1)}, f32[15,32,256]{2,1,0:T(8,128)S(1)}, u32[]{:S(2)}, u32[]{:S(2)}) collective-permute-start(f32[15,32,256]{2,1,0:T(8,128)S(1)} %get-tuple-element.86), channel_id=1, source_target_pairs={{2,8},{3,9},{4,10},{5,11},{6,12},{7,13},{8,2},{9,3},{10,4},{11,5},... | collective-permute-start | bytes 1474568 | tf_op jit(solution)/shard_map/ppermute | solution.py:33
  140.2 8.9 %collective-permute-done.17.far_ref = f32[15,64,256]{2,1,0:T(8,128)} collective-permute-done((f32[15,64,256]{2,1,0:T(8,128)}, f32[15,64,256]{2,1,0:T(8,128)}, u32[]{:S(2)}, u32[]{:S(2)}) %collective-permute-start.17) | collective-permute-done | bytes 983072 | tf_op jit(solution)/shard_map/ppermute | solution.py:33
  149.1 4.4 %blur_x.4 = (f32[16,64,256]{2,1,0:T(8,128)S(1)}, f32[16,64,256]{2,1,0:T(8,128)S(1)}) custom-call(bf16[2,256,384]{2,1,0:T(8,128)(2,1)S(1)} %get-tuple-element.49.hi_ref, bf16[2,256,384]{2,1,0:T(8,128)(2,1)S(1)} %get-tuple-element.50.lo_ref, f32[15,64,256]{2,1,0:T(8,128)} %collective-permute-done.17.far_ref, ...), custom_call_target="tpu_custom_call" | custom-call | tf_op jit(solution)/shard_map/blur_x/pallas_call | solution.py:285
  154.3 1.4 blur_x.5
  155.8 3.7 %ratio.2 = (f32[16,64,256]{2,1,0:T(8,128)S(1)}, f32[15,64,256]{2,1,0:T(8,128)S(1)}, f32[15,64,256]{2,1,0:T(8,128)S(1)}) custom-call(f32[16,80,256]{2,1,0:T(8,128)S(1)} %copy-done.7, f32[16,64,256]{2,1,0:T(8,128)S(1)} %get-tuple-element.74.refs_0_, f32[16,32,256]{2,1,0:T(8,128)S(1)} %get-tuple-element.75.refs_1_, ...), custom_call_target="tpu_custom_call" | custom-call | tf_op jit(solution)/shard_map/ratio/pallas_call | solution.py:378
  159.5 1.9 collective-permute-start.22
  162.6 3.7 %ratio.3 = (f32[16,64,256]{2,1,0:T(8,128)S(1)}, f32[15,64,256]{2,1,0:T(8,128)S(1)}, f32[15,64,256]{2,1,0:T(8,128)S(1)}) custom-call(f32[16,80,256]{2,1,0:T(8,128)S(1)} %copy-done.9, f32[16,64,256]{2,1,0:T(8,128)S(1)} %get-tuple-element.80.refs_0_, f32[16,32,256]{2,1,0:T(8,128)S(1)} %get-tuple-element.81.refs_1_, ...), custom_call_target="tpu_custom_call" | custom-call | tf_op jit(solution)/shard_map/ratio/pallas_call | solution.py:378
  166.3 2.5 %collective-permute-start.24 = (f32[15,64,256]{2,1,0:T(8,128)S(1)}, f32[15,64,256]{2,1,0:T(8,128)S(1)}, u32[]{:S(2)}, u32[]{:S(2)}) collective-permute-start(f32[15,64,256]{2,1,0:T(8,128)S(1)} %get-tuple-element.82), channel_id=1, source_target_pairs={{2,8},{3,9},{4,10},{5,11},{6,12},{7,13},{8,2},{9,3},{10,4},{11,5},... | collective-permute-start | bytes 2949128 | tf_op jit(solution)/shard_map/ppermute | solution.py:33
  169.9 5.3 %collective-permute-done.22.far_ref = f32[15,64,256]{2,1,0:T(8,128)S(1)} collective-permute-done((f32[15,64,256]{2,1,0:T(8,128)S(1)}, f32[15,64,256]{2,1,0:T(8,128)S(1)}, u32[]{:S(2)}, u32[]{:S(2)}) %collective-permute-start.22) | collective-permute-done | bytes 983072 | tf_op jit(solution)/shard_map/ppermute | solution.py:33
  175.2 2.1 log_factor.8.before_ref
  177.4 8.4 %collective-permute-done.24.far_ref = f32[15,64,256]{2,1,0:T(8,128)S(1)} collective-permute-done((f32[15,64,256]{2,1,0:T(8,128)S(1)}, f32[15,64,256]{2,1,0:T(8,128)S(1)}, u32[]{:S(2)}, u32[]{:S(2)}) %collective-permute-start.24) | collective-permute-done | bytes 983072 | tf_op jit(solution)/shard_map/ppermute | solution.py:33
  185.8 2.1 log_factor.9.refs_0_
  188.6 7.2 %collective-permute-start.27 = (f32[16,64,256]{2,1,0:T(8,128)S(1)}, f32[16,64,256]{2,1,0:T(8,128)S(1)}, u32[]{:S(2)}, u32[]{:S(2)}) collective-permute-start(f32[16,64,256]{2,1,0:T(8,128)S(1)} %log_factor.9.refs_0_), channel_id=1, source_target_pairs={{1,24},{3,26},{5,28},{7,30},{8,17},{10,19},{12,21},{14,23},{17,8},... | collective-permute-start | bytes 3145736 | tf_op jit(solution)/shard_map/ppermute | solution.py:33
  195.8 1.9 collective-permute-start.28
  197.8 20.7 %collective-permute-done.27.refs_2_ = f32[16,64,256]{2,1,0:T(8,128)S(1)} collective-permute-done((f32[16,64,256]{2,1,0:T(8,128)S(1)}, f32[16,64,256]{2,1,0:T(8,128)S(1)}, u32[]{:S(2)}, u32[]{:S(2)}) %collective-permute-start.27) | collective-permute-done | bytes 1048608 | tf_op jit(solution)/shard_map/ppermute | solution.py:33
  218.4 2.9 %collective-permute-done.28.refs_3_ = f32[16,64,256]{2,1,0:T(8,128)S(1)} collective-permute-done((f32[16,64,256]{2,1,0:T(8,128)S(1)}, f32[16,64,256]{2,1,0:T(8,128)S(1)}, u32[]{:S(2)}, u32[]{:S(2)}) %collective-permute-start.28) | collective-permute-done | bytes 1048608 | tf_op jit(solution)/shard_map/ppermute | solution.py:33
  221.6 2.6 %collective-permute-done.29.theirs_ref = f32[16,64,256]{2,1,0:T(8,128)S(1)} collective-permute-done((f32[16,64,256]{2,1,0:T(8,128)S(1)}, f32[16,64,256]{2,1,0:T(8,128)S(1)}, u32[]{:S(2)}, u32[]{:S(2)}) %collective-permute-start.29) | collective-permute-done | bytes 1048608 | tf_op jit(solution)/shard_map/ppermute | solution.py:33
  (84 shorter events, 20.9 us)
Async XLA Ops:
  0.0 1.6 copy-start.1
  1.6 5.2 %copy-start = (f32[1,16,128,256]{3,2,1,0:T(8,128)S(1)}, f32[1,16,128,256]{3,2,1,0:T(8,128)}, u32[]{:S(2)}) copy-start(f32[1,16,128,256]{3,2,1,0:T(8,128)} %param.7) | copy-start | bytes 6291460
  1.6 5.2 %copy-start.13 = (s32[1,16,128]{2,1,0:T(8,128)S(1)}, s32[1,16,128]{2,1,0:T(8,128)}, u32[]{:S(2)}) copy-start(s32[1,16,128]{2,1,0:T(8,128)} %param.10) | copy-start | bytes 24580
  1.6 5.2 %copy-start.14 = (s32[1,3]{1,0:T(1,128)S(1)}, s32[1,3]{1,0:T(1,128)}, u32[]{:S(2)}) copy-start(s32[1,3]{1,0:T(1,128)} %offsets_ref.1) | copy-start | bytes 40
  1.8 1.1 copy-start.2
  3.0 1.2 copy-start.12
  5.3 25.7 %copy-start.3 = (f32[16,96,256]{2,1,0:T(8,128)S(1)}, f32[16,96,256]{2,1,0:T(8,128)}, u32[]{:S(2)}) copy-start(f32[16,96,256]{2,1,0:T(8,128)} %copy-done.2) | copy-start | bytes 4718596
  5.4 12.9 %collective-permute-start.1 = (f32[8,96,256]{2,1,0:T(8,128)S(1)}, f32[8,96,256]{2,1,0:T(8,128)S(1)}, u32[]{:S(2)}, u32[]{:S(2)}) collective-permute-start(f32[8,96,256]{2,1,0:T(8,128)S(1)} %constant_dynamic-slice_fusion.2), channel_id=1, source_target_pairs={{0,1},{2,3},{4,5},{6,7},{9,8},{11,10},{13,12},{15,14},{16,17},{18,... | collective-permute-start | bytes 2359304 | tf_op jit(solution)/shard_map/ppermute | solution.py:33
  18.2 16.9 %copy-start.16 = (f32[1,61]{1,0:T(1,128)S(1)}, f32[1,61]{1,0:T(1,128)}, u32[]{:S(2)}) copy-start(f32[1,61]{1,0:T(1,128)} %param.13) | copy-start | bytes 736
  18.2 16.9 %copy-start.17 = (f32[1,31]{1,0:T(1,128)S(1)}, f32[1,31]{1,0:T(1,128)}, u32[]{:S(2)}) copy-start(f32[1,31]{1,0:T(1,128)} %param.12) | copy-start | bytes 376
  18.2 16.9 %copy-start.18 = (f32[1,31]{1,0:T(1,128)S(1)}, f32[1,31]{1,0:T(1,128)}, u32[]{:S(2)}) copy-start(f32[1,31]{1,0:T(1,128)} %param.11) | copy-start | bytes 376
  18.2 12.9 %collective-permute-start.2 = (f32[8,96,256]{2,1,0:T(8,128)S(1)}, f32[8,96,256]{2,1,0:T(8,128)S(1)}, u32[]{:S(2)}, u32[]{:S(2)}) collective-permute-start(f32[8,96,256]{2,1,0:T(8,128)S(1)} %collective-permute-done.1.refs_0_), channel_id=1, source_target_pairs={{1,17},{3,19},{5,21},{7,23},{8,24},{10,26},{12,28},{14,30},{17,1},... | collective-permute-start | bytes 2359304 | tf_op jit(solution)/shard_map/ppermute | solution.py:33
  21.5 23.6 %collective-permute-start.3 = (f32[17,80,256]{2,1,0:T(8,128)}, f32[17,80,256]{2,1,0:T(8,128)}, u32[]{:S(2)}, u32[]{:S(2)}) collective-permute-start(f32[17,80,256]{2,1,0:T(8,128)} %get-tuple-element.47), channel_id=1, source_target_pairs={{1,8},{3,10},{5,12},{7,14},{8,1},{10,3},{12,5},{14,7},{17,24},{19,... | collective-permute-start | bytes 4177928 | tf_op jit(solution)/shard_map/ppermute | solution.py:33
  32.6 2.5 %copy-start.15 = (f32[15,96,256]{2,1,0:T(8,128)}, f32[15,96,256]{2,1,0:T(8,128)S(1)}, u32[]{:S(2)}) copy-start(f32[15,96,256]{2,1,0:T(8,128)S(1)} %get-tuple-element.55) | copy-start | bytes 4423684
  32.6 28.1 %collective-permute-start.6 = (f32[15,96,256]{2,1,0:T(8,128)}, f32[15,96,256]{2,1,0:T(8,128)S(1)}, u32[]{:S(2)}, u32[]{:S(2)}) collective-permute-start(f32[15,96,256]{2,1,0:T(8,128)} %get-tuple-element.54), channel_id=1, source_target_pairs={{2,8},{3,9},{4,10},{5,11},{6,12},{7,13},{8,2},{9,3},{10,4},{11,5},... | collective-permute-start | bytes 4423688 | tf_op jit(solution)/shard_map/ppermute | solution.py:33
  34.6 23.8 %collective-permute-start.10 = (f32[17,80,256]{2,1,0:T(8,128)}, f32[17,80,256]{2,1,0:T(8,128)}, u32[]{:S(2)}, u32[]{:S(2)}) collective-permute-start(f32[17,80,256]{2,1,0:T(8,128)} %get-tuple-element.65), channel_id=1, source_target_pairs={{0,1},{1,9},{2,3},{3,11},{4,5},{5,13},{6,7},{7,15},{8,0},{9,8},{10... | collective-permute-start | bytes 4177928 | tf_op jit(solution)/shard_map/ppermute | solution.py:33
  35.2 14.4 %collective-permute-start = (f32[126]{0:T(128)S(1)}, f32[126]{0:T(128)S(1)}, u32[]{:S(2)}, u32[]{:S(2)}) collective-permute-start(f32[126]{0:T(128)S(1)} %pad_maximum_fusion.1), channel_id=1, source_target_pairs={{0,8},{1,9},{2,10},{3,11},{4,12},{5,13},{6,14},{7,15},{8,0},{9,1},... | collective-permute-start | bytes 1520 | tf_op jit(solution)/shard_map/ppermute | solution.py:33
  39.2 25.6 %collective-permute-start.7 = (f32[15,96,256]{2,1,0:T(8,128)}, f32[15,96,256]{2,1,0:T(8,128)}, u32[]{:S(2)}, u32[]{:S(2)}) collective-permute-start(f32[15,96,256]{2,1,0:T(8,128)} %copy-done.15), channel_id=1, source_target_pairs={{0,8},{1,9},{2,10},{3,11},{4,12},{5,13},{6,14},{7,15},{8,0},{9,1},... | collective-permute-start | bytes 4423688 | tf_op jit(solution)/shard_map/ppermute | solution.py:33
  47.7 24.1 %collective-permute-start.4 = (f32[17,80,256]{2,1,0:T(8,128)}, f32[17,80,256]{2,1,0:T(8,128)}, u32[]{:S(2)}, u32[]{:S(2)}) collective-permute-start(f32[17,80,256]{2,1,0:T(8,128)} %broadcast_select_fusion.own_ref), channel_id=1, source_target_pairs={{2,8},{3,9},{4,10},{5,11},{6,12},{7,13},{8,2},{9,3},{10,4},{11,5},... | collective-permute-start | bytes 4177928 | tf_op jit(solution)/shard_map/ppermute | solution.py:33
  49.7 22.2 %collective-permute-start.5 = (f32[17,80,256]{2,1,0:T(8,128)}, f32[17,80,256]{2,1,0:T(8,128)}, u32[]{:S(2)}, u32[]{:S(2)}) collective-permute-start(f32[17,80,256]{2,1,0:T(8,128)} %broadcast_select_fusion.own_ref), channel_id=1, source_target_pairs={{0,8},{1,9},{2,10},{3,11},{4,12},{5,13},{6,14},{7,15},{8,0},{9,1},... | collective-permute-start | bytes 4177928 | tf_op jit(solution)/shard_map/ppermute | solution.py:33
  58.3 25.2 %collective-permute-start.11 = (f32[17,80,256]{2,1,0:T(8,128)}, f32[17,80,256]{2,1,0:T(8,128)}, u32[]{:S(2)}, u32[]{:S(2)}) collective-permute-start(f32[17,80,256]{2,1,0:T(8,128)} %collective-permute-done.10.own_ref), channel_id=1, source_target_pairs={{2,8},{3,9},{4,10},{5,11},{6,12},{7,13},{8,2},{9,3},{10,4},{11,5},... | collective-permute-start | bytes 4177928 | tf_op jit(solution)/shard_map/ppermute | solution.py:33
  60.8 1.1 copy-start.4
  61.9 21.6 %collective-permute-start.12 = (f32[17,80,256]{2,1,0:T(8,128)}, f32[17,80,256]{2,1,0:T(8,128)}, u32[]{:S(2)}, u32[]{:S(2)}) collective-permute-start(f32[17,80,256]{2,1,0:T(8,128)} %collective-permute-done.10.own_ref), channel_id=1, source_target_pairs={{0,8},{1,9},{2,10},{3,11},{4,12},{5,13},{6,14},{7,15},{8,0},{9,1},... | collective-permute-start | bytes 4177928 | tf_op jit(solution)/shard_map/ppermute | solution.py:33
  64.7 18.8 %copy-start.10 = (bf16[2,64,256]{2,1,0:T(8,128)(2,1)}, bf16[2,64,256]{2,1,0:T(8,128)(2,1)S(1)}, u32[]{:S(2)}) copy-start(bf16[2,64,256]{2,1,0:T(8,128)(2,1)S(1)} %get-tuple-element.58.refs_2_.refs_3_) | copy-start | bytes 196612
  64.7 1.4 copy-start.5
  79.1 15.7 %collective-permute-start.8 = (f32[15,64,256]{2,1,0:T(8,128)S(1)}, f32[15,64,256]{2,1,0:T(8,128)S(1)}, u32[]{:S(2)}, u32[]{:S(2)}) collective-permute-start(f32[15,64,256]{2,1,0:T(8,128)S(1)} %get-tuple-element.61), channel_id=1, source_target_pairs={{2,8},{3,9},{4,10},{5,11},{6,12},{7,13},{8,2},{9,3},{10,4},{11,5},... | collective-permute-start | bytes 2949128 | tf_op jit(solution)/shard_map/ppermute | solution.py:33
  82.2 12.7 %collective-permute-start.9 = (f32[15,64,256]{2,1,0:T(8,128)S(1)}, f32[15,64,256]{2,1,0:T(8,128)S(1)}, u32[]{:S(2)}, u32[]{:S(2)}) collective-permute-start(f32[15,64,256]{2,1,0:T(8,128)S(1)} %get-tuple-element.63), channel_id=1, source_target_pairs={{0,8},{1,9},{2,10},{3,11},{4,12},{5,13},{6,14},{7,15},{8,0},{9,1},... | collective-permute-start | bytes 2949128 | tf_op jit(solution)/shard_map/ppermute | solution.py:33
  89.7 7.3 %copy-start.8 = (f32[16,80,256]{2,1,0:T(8,128)}, f32[16,80,256]{2,1,0:T(8,128)S(1)}, u32[]{:S(2)}) copy-start(f32[16,80,256]{2,1,0:T(8,128)S(1)} %get-tuple-element.79.image_ref) | copy-start | bytes 3932164
  89.7 15.4 %collective-permute-start.13 = (f32[15,64,256]{2,1,0:T(8,128)S(1)}, f32[15,64,256]{2,1,0:T(8,128)S(1)}, u32[]{:S(2)}, u32[]{:S(2)}) collective-permute-start(f32[15,64,256]{2,1,0:T(8,128)S(1)} %get-tuple-element.67), channel_id=1, source_target_pairs={{2,8},{3,9},{4,10},{5,11},{6,12},{7,13},{8,2},{9,3},{10,4},{11,5},... | collective-permute-start | bytes 2949128 | tf_op jit(solution)/shard_map/ppermute | solution.py:33
  91.8 13.3 %collective-permute-start.14 = (f32[15,64,256]{2,1,0:T(8,128)S(1)}, f32[15,64,256]{2,1,0:T(8,128)S(1)}, u32[]{:S(2)}, u32[]{:S(2)}) collective-permute-start(f32[15,64,256]{2,1,0:T(8,128)S(1)} %get-tuple-element.69), channel_id=1, source_target_pairs={{0,8},{1,9},{2,10},{3,11},{4,12},{5,13},{6,14},{7,15},{8,0},{9,1},... | collective-permute-start | bytes 2949128 | tf_op jit(solution)/shard_map/ppermute | solution.py:33
  106.2 13.2 %collective-permute-start.16 = (f32[16,32,256]{2,1,0:T(8,128)S(1)}, f32[16,32,256]{2,1,0:T(8,128)S(1)}, u32[]{:S(2)}, u32[]{:S(2)}) collective-permute-start(f32[16,32,256]{2,1,0:T(8,128)S(1)} %log_factor.7), channel_id=1, source_target_pairs={{0,16},{1,17},{2,18},{3,19},{4,20},{5,21},{6,22},{7,23},{8,24},{9,... | collective-permute-start | bytes 1572872 | tf_op jit(solution)/shard_map/ppermute | solution.py:33
  108.7 21.9 %collective-permute-start.15 = (f32[16,32,256]{2,1,0:T(8,128)S(1)}, f32[16,32,256]{2,1,0:T(8,128)S(1)}, u32[]{:S(2)}, u32[]{:S(2)}) collective-permute-start(f32[16,32,256]{2,1,0:T(8,128)S(1)} %log_factor.6.refs_0_), channel_id=1, source_target_pairs={{0,16},{1,17},{2,18},{3,19},{4,20},{5,21},{6,22},{7,23},{8,24},{9,... | collective-permute-start | bytes 1572872 | tf_op jit(solution)/shard_map/ppermute | solution.py:33
  120.3 16.1 %collective-permute-start.19 = (f32[16,32,256]{2,1,0:T(8,128)}, f32[16,32,256]{2,1,0:T(8,128)S(1)}, u32[]{:S(2)}, u32[]{:S(2)}) collective-permute-start(f32[16,32,256]{2,1,0:T(8,128)} %add_exponential_fusion.refs_2_), channel_id=1, source_target_pairs={{0,1},{1,0},{2,3},{3,2},{4,5},{5,4},{6,7},{7,6},{8,9},{9,8},{10,11... | collective-permute-start | bytes 1572872 | tf_op jit(solution)/shard_map/ppermute | solution.py:33
  133.1 16.0 %collective-permute-start.17 = (f32[15,64,256]{2,1,0:T(8,128)}, f32[15,64,256]{2,1,0:T(8,128)}, u32[]{:S(2)}, u32[]{:S(2)}) collective-permute-start(f32[15,64,256]{2,1,0:T(8,128)} %get-tuple-element.72), channel_id=1, source_target_pairs={{2,8},{3,9},{4,10},{5,11},{6,12},{7,13},{8,2},{9,3},{10,4},{11,5},... | collective-permute-start | bytes 2949128 | tf_op jit(solution)/shard_map/ppermute | solution.py:33
  135.0 14.1 %collective-permute-start.18 = (f32[15,64,256]{2,1,0:T(8,128)}, f32[15,64,256]{2,1,0:T(8,128)}, u32[]{:S(2)}, u32[]{:S(2)}) collective-permute-start(f32[15,64,256]{2,1,0:T(8,128)} %get-tuple-element.73), channel_id=1, source_target_pairs={{0,8},{1,9},{2,10},{3,11},{4,12},{5,13},{6,14},{7,15},{8,0},{9,1},... | collective-permute-start | bytes 2949128 | tf_op jit(solution)/shard_map/ppermute | solution.py:33
  136.4 17.9 %collective-permute-start.20 = (f32[15,32,256]{2,1,0:T(8,128)S(1)}, f32[15,32,256]{2,1,0:T(8,128)S(1)}, u32[]{:S(2)}, u32[]{:S(2)}) collective-permute-start(f32[15,32,256]{2,1,0:T(8,128)S(1)} %get-tuple-element.86), channel_id=1, source_target_pairs={{2,8},{3,9},{4,10},{5,11},{6,12},{7,13},{8,2},{9,3},{10,4},{11,5},... | collective-permute-start | bytes 1474568 | tf_op jit(solution)/shard_map/ppermute | solution.py:33
  138.9 15.4 %collective-permute-start.21 = (f32[15,32,256]{2,1,0:T(8,128)S(1)}, f32[15,32,256]{2,1,0:T(8,128)S(1)}, u32[]{:S(2)}, u32[]{:S(2)}) collective-permute-start(f32[15,32,256]{2,1,0:T(8,128)S(1)} %get-tuple-element.85), channel_id=1, source_target_pairs={{0,8},{1,9},{2,10},{3,11},{4,12},{5,13},{6,14},{7,15},{8,0},{9,1},... | collective-permute-start | bytes 1474568 | tf_op jit(solution)/shard_map/ppermute | solution.py:33
  153.5 2.2 copy-start.7
  153.5 2.2 copy-start.11
  155.8 6.8 %copy-start.9 = (f32[16,80,256]{2,1,0:T(8,128)S(1)}, f32[16,80,256]{2,1,0:T(8,128)}, u32[]{:S(2)}) copy-start(f32[16,80,256]{2,1,0:T(8,128)} %copy-done.8) | copy-start | bytes 3932164
  159.5 15.7 %collective-permute-start.22 = (f32[15,64,256]{2,1,0:T(8,128)S(1)}, f32[15,64,256]{2,1,0:T(8,128)S(1)}, u32[]{:S(2)}, u32[]{:S(2)}) collective-permute-start(f32[15,64,256]{2,1,0:T(8,128)S(1)} %get-tuple-element.76), channel_id=1, source_target_pairs={{2,8},{3,9},{4,10},{5,11},{6,12},{7,13},{8,2},{9,3},{10,4},{11,5},... | collective-permute-start | bytes 2949128 | tf_op jit(solution)/shard_map/ppermute | solution.py:33
  161.5 13.8 %collective-permute-start.23 = (f32[15,64,256]{2,1,0:T(8,128)S(1)}, f32[15,64,256]{2,1,0:T(8,128)S(1)}, u32[]{:S(2)}, u32[]{:S(2)}) collective-permute-start(f32[15,64,256]{2,1,0:T(8,128)S(1)} %get-tuple-element.78), channel_id=1, source_target_pairs={{0,8},{1,9},{2,10},{3,11},{4,12},{5,13},{6,14},{7,15},{8,0},{9,1},... | collective-permute-start | bytes 2949128 | tf_op jit(solution)/shard_map/ppermute | solution.py:33
  166.3 19.4 %collective-permute-start.24 = (f32[15,64,256]{2,1,0:T(8,128)S(1)}, f32[15,64,256]{2,1,0:T(8,128)S(1)}, u32[]{:S(2)}, u32[]{:S(2)}) collective-permute-start(f32[15,64,256]{2,1,0:T(8,128)S(1)} %get-tuple-element.82), channel_id=1, source_target_pairs={{2,8},{3,9},{4,10},{5,11},{6,12},{7,13},{8,2},{9,3},{10,4},{11,5},... | collective-permute-start | bytes 2949128 | tf_op jit(solution)/shard_map/ppermute | solution.py:33
  168.9 16.9 %collective-permute-start.25 = (f32[15,64,256]{2,1,0:T(8,128)S(1)}, f32[15,64,256]{2,1,0:T(8,128)S(1)}, u32[]{:S(2)}, u32[]{:S(2)}) collective-permute-start(f32[15,64,256]{2,1,0:T(8,128)S(1)} %get-tuple-element.84), channel_id=1, source_target_pairs={{0,8},{1,9},{2,10},{3,11},{4,12},{5,13},{6,14},{7,15},{8,0},{9,1},... | collective-permute-start | bytes 2949128 | tf_op jit(solution)/shard_map/ppermute | solution.py:33
  187.9 9.9 %collective-permute-start.26 = (f32[16,64,256]{2,1,0:T(8,128)S(1)}, f32[16,64,256]{2,1,0:T(8,128)S(1)}, u32[]{:S(2)}, u32[]{:S(2)}) collective-permute-start(f32[16,64,256]{2,1,0:T(8,128)S(1)} %log_factor.9.refs_0_), channel_id=1, source_target_pairs={{0,16},{2,18},{4,20},{6,22},{9,25},{11,27},{13,29},{15,31},{16,0},... | collective-permute-start | bytes 3145736 | tf_op jit(solution)/shard_map/ppermute | solution.py:33
  188.6 29.8 %collective-permute-start.27 = (f32[16,64,256]{2,1,0:T(8,128)S(1)}, f32[16,64,256]{2,1,0:T(8,128)S(1)}, u32[]{:S(2)}, u32[]{:S(2)}) collective-permute-start(f32[16,64,256]{2,1,0:T(8,128)S(1)} %log_factor.9.refs_0_), channel_id=1, source_target_pairs={{1,24},{3,26},{5,28},{7,30},{8,17},{10,19},{12,21},{14,23},{17,8},... | collective-permute-start | bytes 3145736 | tf_op jit(solution)/shard_map/ppermute | solution.py:33
  195.8 25.5 %collective-permute-start.28 = (f32[16,64,256]{2,1,0:T(8,128)S(1)}, f32[16,64,256]{2,1,0:T(8,128)S(1)}, u32[]{:S(2)}, u32[]{:S(2)}) collective-permute-start(f32[16,64,256]{2,1,0:T(8,128)S(1)} %log_factor.9.refs_0_), channel_id=1, source_target_pairs={{1,8},{3,10},{5,12},{7,14},{8,1},{10,3},{12,5},{14,7},{17,24},{19,... | collective-permute-start | bytes 3145736 | tf_op jit(solution)/shard_map/ppermute | solution.py:33
  221.6 2.7 %collective-permute-start.29 = (f32[16,64,256]{2,1,0:T(8,128)S(1)}, f32[16,64,256]{2,1,0:T(8,128)S(1)}, u32[]{:S(2)}, u32[]{:S(2)}) collective-permute-start(f32[16,64,256]{2,1,0:T(8,128)S(1)} %last_update.1.mine_ref), channel_id=1, source_target_pairs={{0,8},{1,9},{2,10},{3,11},{4,12},{5,13},{6,14},{7,15},{8,0},{9,1},... | collective-permute-start | bytes 3145736 | tf_op jit(solution)/shard_map/ppermute | solution.py:33
  (1 other events, 1.1 us)

commit v5 on v4

--- a/solution.py
+++ b/solution.py
@@ -13,7 +13,7 @@
 BF16 = jnp.bfloat16
 VMEM = pl.BlockSpec(memory_space=pltpu.VMEM)
 SMEM = pl.BlockSpec(memory_space=pltpu.SMEM)
-PARAMS = pltpu.CompilerParams(vmem_limit_bytes=20 * 1024 * 1024)
+PARAMS = pltpu.CompilerParams(vmem_limit_bytes=12 * 1024 * 1024)
 GROUP = 16
 
 
@@ -141,12 +141,16 @@
         base = jnp.broadcast_to(tx_ref[index:index + 1, :], (rows, lanes))
         band = pltpu.roll(base, 0, 1, stride=1, stride_axis=0)
         lane = iota((rows, lanes), 1)
-        first, last = 8 * radius_x, 8 * radius_x + rows
-        turned = jnp.where(
-            lane < first, pltpu.roll(band, lanes - last, 1), jnp.where(lane < last, band, pltpu.roll(band, last, 1))
-        )
-        turned = jnp.where(lane < last + first, turned, jnp.zeros_like(turned))
-        band = jnp.where(core() == 0, band, turned)[:, :xhi_ref.shape[2]]
+        edge = 8 * radius_x
+        far = pad_to(rows + edge, 128)
+        next_near = pltpu.roll(band, lanes - edge, 1)
+        next_far = pltpu.roll(band, far - rows - edge, 1)
+        near_part = jnp.where((lane < rows) | (core() == 0), next_near, pltpu.roll(band, rows, 1))
+        far_part = jnp.where(core() == 0, pltpu.roll(band, far, 1), next_far)
+        zero = jnp.zeros_like(band)
+        band = jnp.where(
+            lane < rows + edge, near_part, jnp.where((lane >= far) & (lane < far + edge), far_part, zero)
+        )[:, :xhi_ref.shape[2]]
         place = (index // 2, slice(index % 2 * rows, index % 2 * rows + rows))
         xhi_ref[place], xlo_ref[place] = split(band)
 
@@ -154,7 +158,7 @@
 def make_tables(kx, ky, kz, planes, cells_y, cells_z, sizes):
     own, near, wide = sizes
     taps_x, taps_z = kx.shape[1], kz.shape[1]
-    depth = 8 * pad_to(planes + taps_x - 1, 16)
+    depth = pad_to(8 * (planes + taps_x // 2), 128) + pad_to(8 * (taps_x // 2), 128)
     lanes = max(512, 1 << (depth - 1).bit_length())
     zero = jnp.zeros((), F32)
     tx = jnp.concatenate([kx, kx[:, ::-1]])
@@ -190,35 +194,49 @@
     return call(window_kernel, (shape, shape), [VMEM], "estimate_windows")(estimate)
 
 
-def put_edges(out_ref, far_ref, near_ref):
-    radius = far_ref.shape[0]
-    beyond = out_ref.shape[0] - radius
-    for p in range(radius):
-        far_ref[p] = out_ref[p + core() * beyond]
-        near_ref[p] = out_ref[p + (1 - core()) * beyond]
-
-
-def assemble_kernel(window_ref, *refs):
-    pieces, (out_ref, far_ref, near_ref) = refs[:-3], refs[-3:]
+def put_edges(out_ref, edge_refs):
+    start = 0
+    for far_ref, near_ref in zip(edge_refs[::2], edge_refs[1::2]):
+        radius, rows = far_ref.shape[0], slice(start, start + far_ref.shape[1])
+        beyond = out_ref.shape[0] - radius
+        for p in range(radius):
+            far_ref[p] = out_ref[p + core() * beyond, rows]
+            near_ref[p] = out_ref[p + (1 - core()) * beyond, rows]
+        start += far_ref.shape[1]
+
+
+def assemble_kernel(*refs, count):
+    pieces, window, out_ref, edge_refs = refs[:count], refs[count:-1], refs[-1], ()
+    if len(refs) > count + 1:
+        window, out_ref, edge_refs = refs[count], refs[count + 1], refs[count + 2:]
     straight, group = core() == half(), lax.axis_index("view") // 2
     planes, share = out_ref.shape[0], pieces[0].shape[0]
     for p in range(planes):
-        turn = lax.rem(group - p // share + len(pieces), len(pieces))
+        turn = lax.rem(group - p // share + count, count)
         value = pieces[0][p % share]
-        for k in range(1, len(pieces)):
+        for k in range(1, count):
             value = jnp.where(turn == k, pieces[k][p % share], value)
-        out_ref[p] = jnp.where(straight, window_ref[p], value)
-    put_edges(out_ref, far_ref, near_ref)
-
-
-def edge_shapes(shape, radius):
-    edge = jax.ShapeDtypeStruct((radius,) + shape[1:], F32)
-    return jax.ShapeDtypeStruct(shape, F32), edge, edge
+        out_ref[p] = jnp.where(straight, window[p], value) if edge_refs else value
+    put_edges(out_ref, edge_refs)
+
+
+def edge_shapes(shape, radius, chunks):
+    planes, _, lanes = shape
+    edges = [jax.ShapeDtypeStruct((radius, rows, lanes), F32) for rows in chunks for _ in range(2)]
+    return (jax.ShapeDtypeStruct(shape, F32), *edges)
 
 
 def assemble(window, pieces, radius):
-    out_shape = edge_shapes(window.shape, radius)
-    return call(assemble_kernel, out_shape, [VMEM] * (1 + len(pieces)), "estimate")(window, *pieces)
+    out_shape = edge_shapes(window.shape, radius, window.shape[1:2])
+    kernel = functools.partial(assemble_kernel, count=len(pieces))
+    return call(kernel, out_shape, [VMEM] * (1 + len(pieces)), "estimate")(*pieces, window)
+
+
+def assemble_far(pieces):
+    share, rows, lanes = pieces[0].shape
+    shape = jax.ShapeDtypeStruct((share * len(pieces), rows, lanes), F32)
+    kernel = functools.partial(assemble_kernel, count=len(pieces))
+    return call(kernel, (shape,), [VMEM] * len(pieces), "far_slab")(*pieces)[0]
 
 
 def shift_kernel(offsets_ref, acq_ref, mask_ref, first_ref, second_ref, turned_ref):
@@ -254,25 +272,37 @@
     return call(shift_kernel, (shape, shape), [SMEM, VMEM, VMEM], "shift_recorded", scratch)(offsets, acquired, mask)
 
 
-def spread_x(hi_ref, lo_ref, index, start, count, refs, row):
-    lanes = refs[1].shape[2]
-    depth = hi_ref.shape[2]
-    parts = [ref[:, pl.ds(row, 8), :] for ref in refs]
-    missing = depth // 8 - sum(part.shape[0] for part in parts)
-    if missing:
-        parts.append(jnp.zeros((missing, 8, lanes), F32))
-    high, low = split(jnp.concatenate(parts, axis=0).reshape(depth, lanes))
-    band = hi_ref[index, start:start + count, :]
-    out = dot(band, high) + (dot(band, low) + dot(lo_ref[index, start:start + count, :], high))
-    return out.reshape(count // 8, 8, lanes)
-
-
-def blur_x_kernel(hi_ref, lo_ref, far_ref, own_ref, near_ref, first_ref, second_ref):
-    planes, rows, lanes = own_ref.shape
+def gather(ref, row, radius=None):
+    if radius is None or ref.shape[0] == radius:
+        return ref[:, pl.ds(row, 8), :]
+    return ref[pl.ds((1 - core()) * (ref.shape[0] - radius), radius), pl.ds(row, 8), :]
+
+
+def spread_x(hi_ref, lo_ref, index, band_rows, band_lanes, blocks):
+    lanes = blocks[0][0].shape[2]
+    filled = []
+    for parts in blocks:
+        count = 8 * sum(part.shape[0] for part in parts)
+        missing = (pad_to(count, 128) - count) // 8
+        filled += list(parts) + ([jnp.zeros((missing, 8, lanes), F32)] if missing else [])
+    high, low = split(jnp.concatenate(filled, axis=0).reshape(-1, lanes))
+    band = hi_ref[index, band_rows, band_lanes]
+    out = dot(band, high) + (dot(band, low) + dot(lo_ref[index, band_rows, band_lanes], high))
+    return out.reshape(-1, 8, lanes)
+
+
+def near_lanes(planes, radius):
+    return pad_to(8 * (planes + radius), 128)
+
+
+def blur_near_kernel(hi_ref, lo_ref, own_ref, near_ref, first_ref, second_ref):
+    planes, rows, _ = own_ref.shape
+    lanes = slice(0, near_lanes(planes, near_ref.shape[0]))
 
     def body(step, carry):
         row = pl.multiple_of(step * 8, 8)
-        out = spread_x(hi_ref, lo_ref, 0, 0, hi_ref.shape[1], (far_ref, own_ref, near_ref), row)
+        block = [gather(own_ref, row), gather(near_ref, row)]
+        out = spread_x(hi_ref, lo_ref, 0, slice(None), lanes, [block])
         first_ref[:, pl.ds(row, 8), :] = out[:planes]
         second_ref[:, pl.ds(row, 8), :] = out[planes:]
         return carry
@@ -280,9 +310,27 @@
     lax.fori_loop(0, rows // 8, body, 0)
 
 
+def blur_far_kernel(hi_ref, lo_ref, far_ref, first_ref, second_ref, first_out, second_out, *, radius):
+    planes, rows, _ = first_ref.shape
+    lanes = slice(near_lanes(planes, radius), None)
+
+    def body(step, carry):
+        row = pl.multiple_of(step * 8, 8)
+        place = (slice(None), pl.ds(row, 8), slice(None))
+        out = spread_x(hi_ref, lo_ref, 0, slice(None), lanes, [[gather(far_ref, row, radius)]])
+        first_out[place] = first_ref[place] + out[:planes]
+        second_out[place] = second_ref[place] + out[planes:]
+        return carry
+
+    lax.fori_loop(0, rows // 8, body, 0)
+
+
 def blur_x(tables, far, own, near):
     shape = jax.ShapeDtypeStruct(own.shape, F32)
-    return call(blur_x_kernel, (shape, shape), [VMEM] * 5, "blur_x")(*tables[4:], far, own, near)
+    shapes = (shape, shape)
+    parts = call(blur_near_kernel, shapes, [VMEM] * 4, "blur_x_near")(*tables[4:], own, near)
+    kernel = functools.partial(blur_far_kernel, radius=near.shape[0])
+    return call(kernel, shapes, [VMEM] * 5, "blur_x_far")(*tables[4:], far, *parts)
 
 
 def spread_y(band, x):
@@ -300,7 +348,7 @@
 
 
 def ratio_planes(wide_refs, fetch, yf_ref, ya_ref, zhi_ref, zlo_ref, order, outs):
-    out_ref, far_ref, near_ref = outs
+    out_ref, edge_refs = outs[0], outs[1:]
     planes, rows, _ = out_ref.shape
     near = yf_ref.shape[1]
     step = 4
@@ -318,10 +366,10 @@
         spread = spread_z(spread, zhi_ref, zlo_ref, 2 + order)
         for k, p in enumerate(block):
             out_ref[p] = spread[k * rows:(k + 1) * rows]
-    put_edges(out_ref, far_ref, near_ref)
-
-
-def first_ratio_kernel(shift_ref, far_ref, near_ref, own_ref, *refs, order, extent_x, cells_y):
+    put_edges(out_ref, edge_refs)
+
+
+def first_ratio_kernel(shift_ref, far_ref, near_ref, own_ref, *refs, order, wides, extent_x, cells_y):
     image_ref = refs[-1]
     planes, near, cells_z = image_ref.shape
     side = half()
@@ -351,78 +399,83 @@
         image_ref[p] = value
         return value
 
-    ratio_planes(refs[:-8], fetch, *refs[-8:-4], order, refs[-4:-1])
-
-
-def next_ratio_kernel(image_ref, *refs, order):
-    ratio_planes(refs[:-7], lambda p: image_ref[p], *refs[-7:-3], order, refs[-3:])
-
-
-def ratio_shapes(wides, tables, radius):
+    ratio_planes(refs[:wides], fetch, *refs[wides:wides + 4], order, refs[wides + 4:-1])
+
+
+def next_ratio_kernel(image_ref, *refs, order, wides):
+    ratio_planes(refs[:wides], lambda p: image_ref[p], *refs[wides:wides + 4], order, refs[wides + 4:])
+
+
+def ratio_shapes(wides, tables, radius, chunks):
     planes, _, lanes = wides[0].shape
-    return edge_shapes((planes, tables[1].shape[1], lanes), radius)
-
-
-def first_ratio(shifts, blocks, wides, tables, order, radius, extent_x, cells_y):
+    return edge_shapes((planes, tables[1].shape[1], lanes), radius, chunks)
+
+
+def first_ratio(shifts, blocks, wides, tables, order, radius, chunks, extent_x, cells_y):
     planes, _, lanes = wides[0].shape
-    kernel = functools.partial(first_ratio_kernel, order=order, extent_x=extent_x, cells_y=cells_y)
+    kernel = functools.partial(
+        first_ratio_kernel, order=order, wides=len(wides), extent_x=extent_x, cells_y=cells_y
+    )
     image = jax.ShapeDtypeStruct((planes, tables[0].shape[1], lanes), F32)
-    out_shape = ratio_shapes(wides, tables, radius) + (image,)
+    out_shape = ratio_shapes(wides, tables, radius, chunks) + (image,)
     return call(kernel, out_shape, [SMEM] + [VMEM] * (7 + len(wides)), "image_and_ratio")(
         shifts, *blocks, *wides, *tables[:4]
     )
 
 
-def next_ratio(image, wides, tables, order, radius):
-    kernel = functools.partial(next_ratio_kernel, order=order)
-    return call(kernel, ratio_shapes(wides, tables, radius), [VMEM] * (5 + len(wides)), "ratio")(
+def next_ratio(image, wides, tables, order, radius, chunks):
+    kernel = functools.partial(next_ratio_kernel, order=order, wides=len(wides))
+    return call(kernel, ratio_shapes(wides, tables, radius, chunks), [VMEM] * (5 + len(wides)), "ratio")(
         image, *wides, *tables[:4]
     )
 
 
 def factor_kernel(hi_ref, lo_ref, before_ref, far_ref, own_ref, near_ref, out_ref, *, order, start, share):
     planes, rows, _ = out_ref.shape
+    band_rows = slice(order * 8 * planes, (order + 1) * 8 * planes)
 
     def body(step, carry):
         row = pl.multiple_of(step * 8, 8)
         source = pl.multiple_of(start + row, 8)
-        total = before_ref[:, pl.ds(source, 8), :]
         if share:
-            total = share * jnp.log(total)
-        factor = spread_x(hi_ref, lo_ref, 1, order * 8 * planes, 8 * planes, (far_ref, own_ref, near_ref), source)
+            total = share * jnp.log(before_ref[:, pl.ds(source, 8), :])
+        else:
+            total = before_ref[:, pl.ds(row, 8), :]
+        blocks = [[gather(own_ref, source), gather(near_ref, row)], [gather(far_ref, row)]]
+        factor = spread_x(hi_ref, lo_ref, 1, band_rows, slice(None), blocks)
         out_ref[:, pl.ds(row, 8), :] = total + jnp.log(factor)
         return carry
 
     lax.fori_loop(0, rows // 8, body, 0)
 
 
-def log_factor(tables, before, side, order, start, rows, share):
-    planes, _, lanes = side[1].shape
+def log_factor(tables, before, side, order, start, share):
+    far, own, near = side
     kernel = functools.partial(factor_kernel, order=order, start=start, share=share)
-    shape = jax.ShapeDtypeStruct((planes, rows, lanes), F32)
-    return call(kernel, shape, [VMEM] * 6, "log_factor")(*tables[4:], before, *side)
+    shape = jax.ShapeDtypeStruct((own.shape[0],) + far.shape[1:], F32)
+    return call(kernel, shape, [VMEM] * 6, "log_factor")(*tables[4:], before, far, own, near)
 
 
 def update_kernel(*refs):
-    parts, edge_ref, (out_ref, far_ref, near_ref) = refs[:-4], refs[-4], refs[-3:]
+    parts, edge_ref, out_ref, edge_refs = refs[:-4], refs[-4], refs[-3], refs[-2:]
     for p in range(out_ref.shape[0]):
         total = parts[0][p]
         for part in parts[1:]:
             total = total + part[p]
         out_ref[p] = jnp.concatenate([jnp.exp(total), edge_ref[p]], axis=0)
-    put_edges(out_ref, far_ref, near_ref)
+    put_edges(out_ref, edge_refs)
 
 
 def update(parts, edge, radius):
     planes, rows, lanes = parts[0].shape
-    out_shape = edge_shapes((planes, rows + edge.shape[1], lanes), radius)
+    rows += edge.shape[1]
+    out_shape = edge_shapes((planes, rows, lanes), radius, [rows])
     return call(update_kernel, out_shape, [VMEM] * (len(parts) + 1), "update")(*parts, edge)
 
 
 def finish_kernel(*refs):
     own, other, out_ref = refs[:(len(refs) - 1) // 2], refs[(len(refs) - 1) // 2:-1], refs[-1]
     straight = core() == half()
-    side = jnp.where(straight, half(), 1 - half())
     groups = out_ref.shape[1] // GROUP
     for group in range(groups):
         rows = slice(group * GROUP, (group + 1) * GROUP)
@@ -431,7 +484,7 @@
             own_total = own_total + part[:, rows, :]
         for part in other[1:]:
             other_total = other_total + part[:, rows, :]
-        start = jnp.where(side == 0, group, groups - 1 - group) * GROUP
+        start = jnp.where(core() == 0, group, groups - 1 - group) * GROUP
         out_ref[:, pl.ds(pl.multiple_of(start, GROUP), GROUP), :] = jnp.exp(jnp.where(straight, own_total, other_total))
 
 
@@ -440,11 +493,15 @@
     return call(finish_kernel, shape, [VMEM] * (2 * len(own_parts)), "last_update")(*own_parts, *other_parts)
 
 
-def join_kernel(mine_ref, theirs_ref, out_ref, semaphores):
-    rows = mine_ref.shape[1]
+def join_kernel(*refs, starts):
+    sources, out_ref, semaphores = refs[:-2], refs[-2], refs[-1]
+    cells_y = out_ref.shape[1]
     copies = []
-    for index, (source_ref, side) in enumerate(((mine_ref, core()), (theirs_ref, 1 - core()))):
-        target = out_ref.at[:, pl.ds(pl.multiple_of(side * rows, rows), rows), :]
+    for index, source_ref in enumerate(sources):
+        rows, start = source_ref.shape[1], starts[index // 2]
+        side = core() if index % 2 == 0 else 1 - core()
+        place = pl.multiple_of(jnp.where(side == 0, start, cells_y - start - rows), GROUP)
+        target = out_ref.at[:, pl.ds(place, rows), :]
         copies.append(pltpu.make_async_copy(source_ref, target, semaphores.at[index]))
     for copy in copies:
         copy.start()
@@ -452,18 +509,17 @@
         copy.wait()
 
 
-def join(mine, theirs):
-    planes, rows, lanes = mine.shape
+def join(pieces, starts, shape):
     anywhere = pl.BlockSpec(memory_space=pl.ANY)
     return pl.pallas_call(
-        join_kernel,
-        out_shape=jax.ShapeDtypeStruct((planes, 2 * rows, lanes), F32),
-        in_specs=[anywhere, anywhere],
+        functools.partial(join_kernel, starts=starts),
+        out_shape=jax.ShapeDtypeStruct(shape, F32),
+        in_specs=[anywhere] * len(pieces),
         out_specs=anywhere,
-        scratch_shapes=[pltpu.SemaphoreType.DMA((2,))],
+        scratch_shapes=[pltpu.SemaphoreType.DMA((len(pieces),))],
         compiler_params=PARAMS,
         name="join_halves",
-    )(mine, theirs)
+    )(*pieces)
 
 
 def shards(acquired, estimate, offsets, view_mask, kern_x, kern_y, kern_z):
@@ -505,35 +561,55 @@
     shifts = both[:, taps_x + taps_y + taps_z:].astype(jnp.int32)
     tables = make_tables(kx, ky, kz, planes, cells_y, cells_z, (own_rows, near, wide))
 
+    start = group * (planes // groups)
+    share = jnp.where(straight, lax.dynamic_slice_in_dim(window, start, planes // groups, 0), piece)
+    share = send(share, to_far)
     pieces = [piece] + [send(piece, across(turn, when=lambda c, r: c != r)) for turn in range(1, groups)]
-    current, distant, close = assemble(window, pieces, radius)
-    second = after(second, distant)
-    distant, close = neighbours(distant, close)
-    chunks = [(distant, current, close)]
+    current, _, close = assemble(window, pieces, radius)
+    second = after(second, current)
     second = send(second, lambda g, c, q, r: (g, r, q, 1 - c))
+    distant = assemble_far([share] + [send(share, across(turn)) for turn in range(1, groups)])
+    chunks = [(distant, current, send(close, to_core_partner))]
     first = jnp.where(straight, first, arrived)
-    blocks = [(*neighbours(first, first), first)]
-
-    blocks.append((*neighbours(second, second), second))
+    blocks = [(*neighbours(block, block), block) for block in (first, second)]
     images = [None, None]
 
+    row_chunks = [(0, inner_rows), (inner_rows, edge_rows)]
+    sizes = [size for _, size in row_chunks]
+
     for step in range(ITERS):
+        last = step == ITERS - 1
         wides = [blur_x(tables, *chunk) for chunk in chunks]
-        sides = []
+        spreads, edges = [], []
         for order in range(2):
             parts = [chunk[order] for chunk in wides]
             if step == 0:
-                spread, distant, close, images[order] = first_ratio(
-                    shifts, blocks[order], parts, tables, order, radius, planes * slabs, cells_y
+                spread, *edge, images[order] = first_ratio(
+                    shifts, blocks[order], parts, tables, order, radius, sizes, planes * slabs, cells_y
                 )
             else:
-                spread, distant, close = next_ratio(images[order], parts, tables, order, radius)
-            distant, close = neighbours(distant, close)
-            sides.append((distant, spread, close))
-        total = log_factor(tables, current, sides[0], 0, 0, own_rows, 1.0 / groups)
-        if step < ITERS - 1:
-            edge = log_factor(tables, total, sides[1], 1, inner_rows, edge_rows, 0)
-            inner = log_factor(tables, total, sides[1], 1, 0, inner_rows, 0)
+                spread, *edge = next_ratio(images[order], parts, tables, order, radius, sizes)
+            spreads.append(spread)
+            edges.append(edge)
+
+        totals = [None, None]
+        hook = None
+        for index in (1, 0):
+            total = current
+            for order in range(2):
+                distant, close = edges[order][2 * index:2 * index + 2]
+                if hook is not None:
+                    distant, close = after(distant, hook), after(close, hook)
+                distant, close = neighbours(distant, close)
+                side = (distant, spreads[order], close)
+                total = log_factor(tables, total, side, order, row_chunks[index][0], 0 if order else 1.0 / groups)
+                if index == 1 and order == 0:
+                    first_total = total
+            hook = first_total
+            totals[index] = total
+
+        if not last:
+            inner, edge = totals
             edge_parts = [edge] + [send(edge, across(turn)) for turn in range(1, groups)]
             inner_parts = [inner] + [send(inner, across(turn)) for turn in range(1, groups)]
             edge = jnp.exp(sum(edge_parts[1:], edge_parts[0]))
@@ -548,13 +624,17 @@
             )
             chunks.append((distant, beyond, close))
 
-    own = log_factor(tables, total, sides[1], 1, 0, own_rows, 0)
-    other_parts = [
-        send(own, across(turn, lambda r: 1 - r, lambda c: 1 - c, lambda c, r: c != r)) for turn in reversed(range(groups))
-    ]
-    own_parts = [own] + [send(own, across(turn, when=lambda c, r: c == r)) for turn in range(1, groups)]
-    mine = finish(own_parts, other_parts)
-    return join(mine, send(mine, to_core_partner))
+    pieces = []
+    for index in (1, 0):
+        own = totals[index]
+        other_parts = [
+            send(own, across(turn, lambda r: 1 - r, lambda c: 1 - c, lambda c, r: c != r))
+            for turn in reversed(range(groups))
+        ]
+        own_parts = [own] + [send(own, across(turn, when=lambda c, r: c == r)) for turn in range(1, groups)]
+        mine = finish(own_parts, other_parts)
+        pieces += [mine, send(mine, to_core_partner)]
+    return join(pieces, [row_chunks[1][0], row_chunks[0][0]], estimate.shape)
 
 
 def solution(mesh):

time: 227 us -> 218 us (0.960)
  waiting for transfers between devices: 104 us -> 71.8 us
  starting transfers between devices: 56.1 us -> 68.2 us
  Pallas kernels: 52.5 us -> 57.9 us
  local copies, waits for them, and re-layouts: 9.24 us -> 12.6 us
    ppermute x30 -> x43, waiting for transfers between devices: 104 us -> 71.8 us  [send(): return lax.ppermute(array, AXES, moves(move))]
    ppermute x30 -> x43, starting transfers between devices: 56.1 us -> 68.2 us  [send(): return lax.ppermute(array, AXES, moves(move))]
    pallas_call x12 -> x19, Pallas kernels: 30.3 us -> 36.3 us  [the longest x3 9.11 us: blur_x(): call(blur_near_kernel, shapes, [VMEM] * 4, 'blur_x_near')]
    unnamed x38 -> x46, local copies, waits for them, and re-layouts: 7.5 us -> 12 us
  transfers between devices with their start and end apart: 30 -> 43, of which waited for: 16 -> 19; matrix products, arithmetic and copies ran while one was open for 2% -> 2% of each run, Pallas kernels for 19% -> 23%
where the time goes in v5:
time: 218 us; the launch traced here: 215 us
  waiting for transfers between devices  71.8 us (33%)
  starting transfers between devices  68.2 us (31%)
  Pallas kernels  57.9 us (27%)
  local copies, waits for them, and re-layouts  12.6 us (6%)
  other arithmetic  3.8 us (2%)
    ppermute x43, waiting for transfers between devices, send(): return lax.ppermute(array, AXES, moves(move))  71.8 us
    ppermute x43, starting transfers between devices, send(): return lax.ppermute(array, AXES, moves(move))  68.2 us
    pallas_call x2, Pallas kernels, first_ratio(): call(kernel, out_shape, [SMEM] + [VMEM] * (7 + len(wides)), 'image_and_ra...  12.5 us
    unnamed x46, local copies, waits for them, and re-layouts  12 us
    pallas_call x3, Pallas kernels, blur_x(): call(blur_near_kernel, shapes, [VMEM] * 4, 'blur_x_near')  9.11 us
    pallas_call x8, Pallas kernels, log_factor(): call(kernel, shape, [VMEM] * 6, 'log_factor')  8.59 us
    pallas_call x2, Pallas kernels, next_ratio(): call(kernel, ratio_shapes(wides, tables, radius, chunks), [VMEM] * (5 + l...  7.51 us
    pallas_call x3, Pallas kernels, blur_x(): call(kernel, shapes, [VMEM] * 5, 'blur_x_far')(*tables[4:], far, *parts)  7.48 us
  transfers between devices with their start and end apart: 43, of which 19 were waited for; matrix products, arithmetic and copies ran while one was open for 2% of the time, Pallas kernels for 23%

profile of v5, /device:TPU:17, one launch (start us, length us, event | category | flops | bytes accessed | tf_op | source)
XLA Modules:
  0.0 215.2 jit_solution(15680976151169328884)
XLA Ops:
  4.8 4.1 %shift_recorded.1 = (f32[17,80,256]{2,1,0:T(8,128)}, f32[17,80,256]{2,1,0:T(8,128)S(1)}) custom-call(s32[1,3]{1,0:T(1,128)S(1)} %copy-done.17, f32[16,128,256]{2,1,0:T(8,128)S(1)} %bitcast.9, s32[16,128]{1,0:T(8,128)S(1)} %bitcast.10), custom_call_target="tpu_custom_call" | custom-call | tf_op jit(solution)/shard_map/shift_recorded/pallas_call | solution.py:272
  10.0 4.6 %collective-permute-done.1.refs_0_ = f32[8,96,256]{2,1,0:T(8,128)S(1)} collective-permute-done((f32[8,96,256]{2,1,0:T(8,128)S(1)}, f32[8,96,256]{2,1,0:T(8,128)S(1)}, u32[]{:S(2)}, u32[]{:S(2)}) %collective-permute-start.1) | collective-permute-done | bytes 786464 | tf_op jit(solution)/shard_map/ppermute | solution.py:33
  14.6 3.1 %collective-permute-start.2 = (f32[8,96,256]{2,1,0:T(8,128)S(1)}, f32[8,96,256]{2,1,0:T(8,128)S(1)}, u32[]{:S(2)}, u32[]{:S(2)}) collective-permute-start(f32[8,96,256]{2,1,0:T(8,128)S(1)} %collective-permute-done.1.refs_0_), channel_id=1, source_target_pairs={{1,17},{3,19},{5,21},{7,23},{8,24},{10,26},{12,28},{14,30},{17,1},... | collective-permute-start | bytes 2359304 | tf_op jit(solution)/shard_map/ppermute | solution.py:33
  17.8 5.1 %collective-permute-start.3 = (f32[17,80,256]{2,1,0:T(8,128)}, f32[17,80,256]{2,1,0:T(8,128)}, u32[]{:S(2)}, u32[]{:S(2)}) collective-permute-start(f32[17,80,256]{2,1,0:T(8,128)} %get-tuple-element.68), channel_id=1, source_target_pairs={{1,8},{3,10},{5,12},{7,14},{8,1},{10,3},{12,5},{14,7},{17,24},{19,... | collective-permute-start | bytes 4177928 | tf_op jit(solution)/shard_map/ppermute | solution.py:33
  23.1 2.1 collective-permute-start.6
  25.2 2.5 %collective-permute-done.2.refs_1_ = f32[8,96,256]{2,1,0:T(8,128)S(1)} collective-permute-done((f32[8,96,256]{2,1,0:T(8,128)S(1)}, f32[8,96,256]{2,1,0:T(8,128)S(1)}, u32[]{:S(2)}, u32[]{:S(2)}) %collective-permute-start.2) | collective-permute-done | bytes 786464 | tf_op jit(solution)/shard_map/ppermute | solution.py:33
  31.1 2.1 estimate.1
  33.2 3.4 %collective-permute-done.6.refs_0_ = f32[8,96,256]{2,1,0:T(8,128)S(1)} collective-permute-done((f32[8,96,256]{2,1,0:T(8,128)S(1)}, f32[8,96,256]{2,1,0:T(8,128)S(1)}, u32[]{:S(2)}, u32[]{:S(2)}) %collective-permute-start.6) | collective-permute-done | bytes 786464 | tf_op jit(solution)/shard_map/ppermute | solution.py:33
  36.9 2.1 collective-permute-start
  39.1 4.1 %collective-permute-done.3 = f32[17,80,256]{2,1,0:T(8,128)} collective-permute-done((f32[17,80,256]{2,1,0:T(8,128)}, f32[17,80,256]{2,1,0:T(8,128)}, u32[]{:S(2)}, u32[]{:S(2)}) %collective-permute-start.3) | collective-permute-done | bytes 1392672 | tf_op jit(solution)/shard_map/ppermute | solution.py:33
  43.2 2.6 %broadcast_select_fusion.own_ref = f32[17,80,256]{2,1,0:T(8,128)} fusion(f32[17,80,256]{2,1,0:T(8,128)} %get-tuple-element.68, f32[17,80,256]{2,1,0:T(8,128)} %collective-permute-done.3, pred[]{:T(512)S(6)} %eq.3), kind=kLoop, calls=%fused_computation.1 | loop fusion | flops 348160 | bytes 4177921 | tf_op jit(solution)/shard_map/jit(_where)/select_n | solution.py:573
  48.3 6.3 %collective-permute-done.13.own_ref = f32[17,80,256]{2,1,0:T(8,128)} collective-permute-done((f32[17,80,256]{2,1,0:T(8,128)S(1)}, f32[17,80,256]{2,1,0:T(8,128)}, u32[]{:S(2)}, u32[]{:S(2)}) %collective-permute-start.13) | collective-permute-done | bytes 1392672 | tf_op jit(solution)/shard_map/ppermute | solution.py:33
  54.6 2.3 %collective-permute-start.14 = (f32[17,80,256]{2,1,0:T(8,128)}, f32[17,80,256]{2,1,0:T(8,128)}, u32[]{:S(2)}, u32[]{:S(2)}) collective-permute-start(f32[17,80,256]{2,1,0:T(8,128)} %collective-permute-done.13.own_ref), channel_id=1, source_target_pairs={{2,8},{3,9},{4,10},{5,11},{6,12},{7,13},{8,2},{9,3},{10,4},{11,5},... | collective-permute-start | bytes 4177928 | tf_op jit(solution)/shard_map/ppermute | solution.py:33
  58.4 2.1 band_matrices.1
  63.1 4.6 %blur_x_near.3 = (f32[16,96,256]{2,1,0:T(8,128)S(1)}, f32[16,96,256]{2,1,0:T(8,128)S(1)}) custom-call(bf16[2,256,384]{2,1,0:T(8,128)(2,1)S(1)} %get-tuple-element.70.hi_ref, bf16[2,256,384]{2,1,0:T(8,128)(2,1)S(1)} %get-tuple-element.71.lo_ref, f32[16,96,256]{2,1,0:T(8,128)S(1)} %get-tuple-element.74.own_ref.before_ref, ...), custom_call_target="tpu_custom_call" | custom-call | tf_op jit(solution)/shard_map/blur_x_near/pallas_call | solution.py:331
  67.7 3.2 %blur_x_far.3 = (f32[16,96,256]{2,1,0:T(8,128)S(1)}, f32[16,96,256]{2,1,0:T(8,128)S(1)}) custom-call(bf16[2,256,384]{2,1,0:T(8,128)(2,1)S(1)} %get-tuple-element.70.hi_ref, bf16[2,256,384]{2,1,0:T(8,128)(2,1)S(1)} %get-tuple-element.71.lo_ref, f32[16,96,256]{2,1,0:T(8,128)S(1)} %far_slab.1.far_ref, f32[16,96,256]{2,1,0:T(8,128)S(1)} %get-tuple-element.76.first_ref, ...), custom_call_target="tpu_custom_call" | custom-call | tf_op jit(solution)/shard_map/blur_x_far/pallas_call | solution.py:333
  71.0 6.2 %image_and_ratio.2 = (f32[16,64,256]{2,1,0:T(8,128)S(1)}, f32[15,32,256]{2,1,0:T(8,128)S(1)}, f32[15,32,256]{2,1,0:T(8,128)S(1)}, f32[15,32,256]{2,1,0:T(8,128)S...) custom-call(s32[2,3]{1,0:T(2,128)S(1)} %slice_convert_fusion.shift_ref, ...), custom_call_target="tpu_custom_call" | custom-call | tf_op jit(solution)/shard_map/image_and_ratio/pallas_call | solution.py:421
  78.3 3.0 %collective-permute-start.9 = (f32[15,32,256]{2,1,0:T(8,128)S(1)}, f32[15,32,256]{2,1,0:T(8,128)S(1)}, u32[]{:S(2)}, u32[]{:S(2)}) collective-permute-start(f32[15,32,256]{2,1,0:T(8,128)S(1)} %get-tuple-element.84), channel_id=1, source_target_pairs={{2,8},{3,9},{4,10},{5,11},{6,12},{7,13},{8,2},{9,3},{10,4},{11,5},... | collective-permute-start | bytes 1474568 | tf_op jit(solution)/shard_map/ppermute | solution.py:33
  81.4 6.2 %image_and_ratio.3 = (f32[16,64,256]{2,1,0:T(8,128)S(1)}, f32[15,32,256]{2,1,0:T(8,128)S(1)}, f32[15,32,256]{2,1,0:T(8,128)S(1)}, f32[15,32,256]{2,1,0:T(8,128)S...) custom-call(s32[2,3]{1,0:T(2,128)S(1)} %slice_convert_fusion.shift_ref, ...), custom_call_target="tpu_custom_call" | custom-call | tf_op jit(solution)/shard_map/image_and_ratio/pallas_call | solution.py:421
  87.7 2.5 %collective-permute-start.19 = (f32[15,32,256]{2,1,0:T(8,128)S(1)}, f32[15,32,256]{2,1,0:T(8,128)S(1)}, u32[]{:S(2)}, u32[]{:S(2)}) collective-permute-start(f32[15,32,256]{2,1,0:T(8,128)S(1)} %get-tuple-element.98), channel_id=1, source_target_pairs={{2,8},{3,9},{4,10},{5,11},{6,12},{7,13},{8,2},{9,3},{10,4},{11,5},... | collective-permute-start | bytes 1474568 | tf_op jit(solution)/shard_map/ppermute | solution.py:33
  91.7 2.7 %collective-permute-start.11 = (f32[15,32,256]{2,1,0:T(8,128)S(1)}, f32[15,32,256]{2,1,0:T(8,128)S(1)}, u32[]{:S(2)}, u32[]{:S(2)}) collective-permute-start(f32[15,32,256]{2,1,0:T(8,128)S(1)} %get-tuple-element.87), channel_id=1, source_target_pairs={{2,8},{3,9},{4,10},{5,11},{6,12},{7,13},{8,2},{9,3},{10,4},{11,5},... | collective-permute-start | bytes 1474568 | tf_op jit(solution)/shard_map/ppermute | solution.py:33
  94.9 2.6 %collective-permute-start.16 = (f32[15,32,256]{2,1,0:T(8,128)S(1)}, f32[15,32,256]{2,1,0:T(8,128)S(1)}, u32[]{:S(2)}, u32[]{:S(2)}) collective-permute-start(f32[15,32,256]{2,1,0:T(8,128)S(1)} %get-tuple-element.94), channel_id=1, source_target_pairs={{2,8},{3,9},{4,10},{5,11},{6,12},{7,13},{8,2},{9,3},{10,4},{11,5},... | collective-permute-start | bytes 1474568 | tf_op jit(solution)/shard_map/ppermute | solution.py:33
  100.0 3.4 %collective-permute-done.11.far_ref = f32[15,32,256]{2,1,0:T(8,128)S(1)} collective-permute-done((f32[15,32,256]{2,1,0:T(8,128)S(1)}, f32[15,32,256]{2,1,0:T(8,128)S(1)}, u32[]{:S(2)}, u32[]{:S(2)}) %collective-permute-start.11) | collective-permute-done | bytes 491552 | tf_op jit(solution)/shard_map/ppermute | solution.py:33
  104.5 4.2 %collective-permute-done.16.far_ref = f32[15,32,256]{2,1,0:T(8,128)S(1)} collective-permute-done((f32[15,32,256]{2,1,0:T(8,128)S(1)}, f32[15,32,256]{2,1,0:T(8,128)S(1)}, u32[]{:S(2)}, u32[]{:S(2)}) %collective-permute-start.16) | collective-permute-done | bytes 491552 | tf_op jit(solution)/shard_map/ppermute | solution.py:33
  110.1 2.5 %collective-permute-done.21 = f32[16,32,256]{2,1,0:T(8,128)S(1)} collective-permute-done((f32[16,32,256]{2,1,0:T(8,128)S(1)}, f32[16,32,256]{2,1,0:T(8,128)S(1)}, u32[]{:S(2)}, u32[]{:S(2)}) %collective-permute-start.21) | collective-permute-done | bytes 524320 | tf_op jit(solution)/shard_map/ppermute | solution.py:33
  113.4 2.4 %collective-permute-start.24 = (f32[16,32,256]{2,1,0:T(8,128)}, f32[16,32,256]{2,1,0:T(8,128)S(1)}, u32[]{:S(2)}, u32[]{:S(2)}) collective-permute-start(f32[16,32,256]{2,1,0:T(8,128)} %add_exponential_fusion.refs_2_), channel_id=1, source_target_pairs={{0,1},{1,0},{2,3},{3,2},{4,5},{5,4},{6,7},{7,6},{8,9},{9,8},{10,11... | collective-permute-start | bytes 1572872 | tf_op jit(solution)/shard_map/ppermute | solution.py:33
  115.8 7.9 %collective-permute-done.18.refs_1_ = f32[16,32,256]{2,1,0:T(8,128)S(1)} collective-permute-done((f32[16,32,256]{2,1,0:T(8,128)S(1)}, f32[16,32,256]{2,1,0:T(8,128)S(1)}, u32[]{:S(2)}, u32[]{:S(2)}) %collective-permute-start.18) | collective-permute-done | bytes 524320 | tf_op jit(solution)/shard_map/ppermute | solution.py:33
  123.8 2.5 %update.1 = (f32[16,64,256]{2,1,0:T(8,128)S(1)}, f32[15,64,256]{2,1,0:T(8,128)}, f32[15,64,256]{2,1,0:T(8,128)}) custom-call(f32[16,32,256]{2,1,0:T(8,128)S(1)} %log_factor.10.refs_0_, f32[16,32,256]{2,1,0:T(8,128)S(1)} %collective-permute-done.18.refs_1_, f32[16,32,256]{2,1,0:T(8,128)} %add_exponential_fusion.refs_2_), custom_call_target="tpu_custom_call" | custom-call | tf_op jit(solution)/shard_map/update/pallas_call | solution.py:473
  127.5 2.5 %collective-permute-start.22 = (f32[15,64,256]{2,1,0:T(8,128)}, f32[15,64,256]{2,1,0:T(8,128)}, u32[]{:S(2)}, u32[]{:S(2)}) collective-permute-start(f32[15,64,256]{2,1,0:T(8,128)} %get-tuple-element.102), channel_id=1, source_target_pairs={{2,8},{3,9},{4,10},{5,11},{6,12},{7,13},{8,2},{9,3},{10,4},{11,5},... | collective-permute-start | bytes 2949128 | tf_op jit(solution)/shard_map/ppermute | solution.py:33
  130.7 2.6 %collective-permute-start.25 = (f32[15,32,256]{2,1,0:T(8,128)S(1)}, f32[15,32,256]{2,1,0:T(8,128)S(1)}, u32[]{:S(2)}, u32[]{:S(2)}) collective-permute-start(f32[15,32,256]{2,1,0:T(8,128)S(1)} %get-tuple-element.128), channel_id=1, source_target_pairs={{2,8},{3,9},{4,10},{5,11},{6,12},{7,13},{8,2},{9,3},{10,4},{11,5},... | collective-permute-start | bytes 1474568 | tf_op jit(solution)/shard_map/ppermute | solution.py:33
  133.3 3.4 %blur_x_near.4 = (f32[16,64,256]{2,1,0:T(8,128)S(1)}, f32[16,64,256]{2,1,0:T(8,128)S(1)}) custom-call(bf16[2,256,384]{2,1,0:T(8,128)(2,1)S(1)} %get-tuple-element.70.hi_ref, bf16[2,256,384]{2,1,0:T(8,128)(2,1)S(1)} %get-tuple-element.71.lo_ref, f32[16,64,256]{2,1,0:T(8,128)S(1)} %get-tuple-element.100.own_ref.before_ref, ...), custom_call_target="tpu_custom_call" | custom-call | tf_op jit(solution)/shard_map/blur_x_near/pallas_call | solution.py:331
  136.7 6.7 %collective-permute-done.22.far_ref = f32[15,64,256]{2,1,0:T(8,128)} collective-permute-done((f32[15,64,256]{2,1,0:T(8,128)}, f32[15,64,256]{2,1,0:T(8,128)}, u32[]{:S(2)}, u32[]{:S(2)}) %collective-permute-start.22) | collective-permute-done | bytes 983072 | tf_op jit(solution)/shard_map/ppermute | solution.py:33
  143.4 3.3 %blur_x_far.4 = (f32[16,64,256]{2,1,0:T(8,128)S(1)}, f32[16,64,256]{2,1,0:T(8,128)S(1)}) custom-call(bf16[2,256,384]{2,1,0:T(8,128)(2,1)S(1)} %get-tuple-element.70.hi_ref, bf16[2,256,384]{2,1,0:T(8,128)(2,1)S(1)} %get-tuple-element.71.lo_ref, f32[15,64,256]{2,1,0:T(8,128)} %collective-permute-done.22.far_ref, ...), custom_call_target="tpu_custom_call" | custom-call | tf_op jit(solution)/shard_map/blur_x_far/pallas_call | solution.py:333
  149.4 3.8 %ratio.2 = (f32[16,64,256]{2,1,0:T(8,128)S(1)}, f32[15,32,256]{2,1,0:T(8,128)S(1)}, f32[15,32,256]{2,1,0:T(8,128)S(1)}, f32[15,32,256]{2,1,0:T(8,128)S(1)}, f32[15,32,256]{2,1,0:T(8,128)S(1)}) custom-call(f32[16,80,256]{2,1,0:T(8,128)S(1)} %copy-done.5, f32[16,64,256]{2,1,0:T(8,128)S(1)} %get-tuple-element.106.refs_0_, ...), custom_call_target="tpu_custom_call" | custom-call | tf_op jit(solution)/shard_map/ratio/pallas_call | solution.py:428
  153.2 2.5 %collective-permute-start.27 = (f32[15,32,256]{2,1,0:T(8,128)S(1)}, f32[15,32,256]{2,1,0:T(8,128)S(1)}, u32[]{:S(2)}, u32[]{:S(2)}) collective-permute-start(f32[15,32,256]{2,1,0:T(8,128)S(1)} %get-tuple-element.110), channel_id=1, source_target_pairs={{2,8},{3,9},{4,10},{5,11},{6,12},{7,13},{8,2},{9,3},{10,4},{11,5},... | collective-permute-start | bytes 1474568 | tf_op jit(solution)/shard_map/ppermute | solution.py:33
  156.3 3.8 %ratio.3 = (f32[16,64,256]{2,1,0:T(8,128)S(1)}, f32[15,32,256]{2,1,0:T(8,128)S(1)}, f32[15,32,256]{2,1,0:T(8,128)S(1)}, f32[15,32,256]{2,1,0:T(8,128)S(1)}, f32[15,32,256]{2,1,0:T(8,128)S(1)}) custom-call(f32[16,80,256]{2,1,0:T(8,128)S(1)} %copy-done.7, f32[16,64,256]{2,1,0:T(8,128)S(1)} %get-tuple-element.114.refs_0_, ...), custom_call_target="tpu_custom_call" | custom-call | tf_op jit(solution)/shard_map/ratio/pallas_call | solution.py:428
  160.1 2.5 %collective-permute-start.29 = (f32[15,32,256]{2,1,0:T(8,128)S(1)}, f32[15,32,256]{2,1,0:T(8,128)S(1)}, u32[]{:S(2)}, u32[]{:S(2)}) collective-permute-start(f32[15,32,256]{2,1,0:T(8,128)S(1)} %get-tuple-element.116), channel_id=1, source_target_pairs={{2,8},{3,9},{4,10},{5,11},{6,12},{7,13},{8,2},{9,3},{10,4},{11,5},... | collective-permute-start | bytes 1474568 | tf_op jit(solution)/shard_map/ppermute | solution.py:33
  164.4 5.8 %collective-permute-done.29.far_ref = f32[15,32,256]{2,1,0:T(8,128)S(1)} collective-permute-done((f32[15,32,256]{2,1,0:T(8,128)S(1)}, f32[15,32,256]{2,1,0:T(8,128)S(1)}, u32[]{:S(2)}, u32[]{:S(2)}) %collective-permute-start.29) | collective-permute-done | bytes 491552 | tf_op jit(solution)/shard_map/ppermute | solution.py:33
  172.0 4.6 %collective-permute-start.35 = (f32[15,32,256]{2,1,0:T(8,128)S(1)}, f32[15,32,256]{2,1,0:T(8,128)S(1)}, u32[]{:S(2)}, u32[]{:S(2)}) collective-permute-start(f32[15,32,256]{2,1,0:T(8,128)S(1)} %get-tuple-element.120), channel_id=1, source_target_pairs={{2,8},{3,9},{4,10},{5,11},{6,12},{7,13},{8,2},{9,3},{10,4},{11,5},... | collective-permute-start | bytes 1474568 | tf_op jit(solution)/shard_map/ppermute | solution.py:33
  176.7 1.9 collective-permute-start.37
  179.8 3.6 %collective-permute-done.35.far_ref = f32[15,32,256]{2,1,0:T(8,128)S(1)} collective-permute-done((f32[15,32,256]{2,1,0:T(8,128)S(1)}, f32[15,32,256]{2,1,0:T(8,128)S(1)}, u32[]{:S(2)}, u32[]{:S(2)}) %collective-permute-start.35) | collective-permute-done | bytes 491552 | tf_op jit(solution)/shard_map/ppermute | solution.py:33
  183.4 4.0 %collective-permute-start.32 = (f32[16,32,256]{2,1,0:T(8,128)S(1)}, f32[16,32,256]{2,1,0:T(8,128)S(1)}, u32[]{:S(2)}, u32[]{:S(2)}) collective-permute-start(f32[16,32,256]{2,1,0:T(8,128)S(1)} %log_factor.13.refs_0_), channel_id=1, source_target_pairs={{1,24},{3,26},{5,28},{7,30},{8,17},{10,19},{12,21},{14,23},{17,8},... | collective-permute-start | bytes 1572872 | tf_op jit(solution)/shard_map/ppermute | solution.py:33
  187.4 2.1 collective-permute-start.33
  192.5 3.9 %collective-permute-start.40 = (f32[16,32,256]{2,1,0:T(8,128)S(1)}, f32[16,32,256]{2,1,0:T(8,128)S(1)}, u32[]{:S(2)}, u32[]{:S(2)}) collective-permute-start(f32[16,32,256]{2,1,0:T(8,128)S(1)} %log_factor.15.refs_0_), channel_id=1, source_target_pairs={{1,24},{3,26},{5,28},{7,30},{8,17},{10,19},{12,21},{14,23},{17,8},... | collective-permute-start | bytes 1572872 | tf_op jit(solution)/shard_map/ppermute | solution.py:33
  196.4 1.9 collective-permute-start.41
  198.4 4.4 %collective-permute-done.33.refs_3_ = f32[16,32,256]{2,1,0:T(8,128)S(1)} collective-permute-done((f32[16,32,256]{2,1,0:T(8,128)S(1)}, f32[16,32,256]{2,1,0:T(8,128)S(1)}, u32[]{:S(2)}, u32[]{:S(2)}) %collective-permute-start.33) | collective-permute-done | bytes 524320 | tf_op jit(solution)/shard_map/ppermute | solution.py:33
  203.0 5.3 %collective-permute-done.40.refs_2_ = f32[16,32,256]{2,1,0:T(8,128)S(1)} collective-permute-done((f32[16,32,256]{2,1,0:T(8,128)S(1)}, f32[16,32,256]{2,1,0:T(8,128)S(1)}, u32[]{:S(2)}, u32[]{:S(2)}) %collective-permute-start.40) | collective-permute-done | bytes 524320 | tf_op jit(solution)/shard_map/ppermute | solution.py:33
  208.3 3.4 %collective-permute-done.41.refs_3_ = f32[16,32,256]{2,1,0:T(8,128)S(1)} collective-permute-done((f32[16,32,256]{2,1,0:T(8,128)S(1)}, f32[16,32,256]{2,1,0:T(8,128)S(1)}, u32[]{:S(2)}, u32[]{:S(2)}) %collective-permute-start.41) | collective-permute-done | bytes 524320 | tf_op jit(solution)/shard_map/ppermute | solution.py:33
  (127 shorter events, 41.8 us)
Async XLA Ops:
  1.8 21.1 %copy-start = (f32[16,96,256]{2,1,0:T(8,128)}, f32[16,96,256]{2,1,0:T(8,128)S(1)}, u32[]{:S(2)}) copy-start(f32[16,96,256]{2,1,0:T(8,128)S(1)} %get-tuple-element.66.refs_2_) | copy-start | bytes 4718596
  1.9 12.7 %collective-permute-start.1 = (f32[8,96,256]{2,1,0:T(8,128)S(1)}, f32[8,96,256]{2,1,0:T(8,128)S(1)}, u32[]{:S(2)}, u32[]{:S(2)}) collective-permute-start(f32[8,96,256]{2,1,0:T(8,128)S(1)} %constant_dynamic-slice_fusion.2), channel_id=1, source_target_pairs={{0,1},{2,3},{4,5},{6,7},{9,8},{11,10},{13,12},{15,14},{16,17},{18,... | collective-permute-start | bytes 2359304 | tf_op jit(solution)/shard_map/ppermute | solution.py:33
  14.6 13.0 %collective-permute-start.2 = (f32[8,96,256]{2,1,0:T(8,128)S(1)}, f32[8,96,256]{2,1,0:T(8,128)S(1)}, u32[]{:S(2)}, u32[]{:S(2)}) collective-permute-start(f32[8,96,256]{2,1,0:T(8,128)S(1)} %collective-permute-done.1.refs_0_), channel_id=1, source_target_pairs={{1,17},{3,19},{5,21},{7,23},{8,24},{10,26},{12,28},{14,30},{17,1},... | collective-permute-start | bytes 2359304 | tf_op jit(solution)/shard_map/ppermute | solution.py:33
  17.8 25.4 %collective-permute-start.3 = (f32[17,80,256]{2,1,0:T(8,128)}, f32[17,80,256]{2,1,0:T(8,128)}, u32[]{:S(2)}, u32[]{:S(2)}) collective-permute-start(f32[17,80,256]{2,1,0:T(8,128)} %get-tuple-element.68), channel_id=1, source_target_pairs={{1,8},{3,10},{5,12},{7,14},{8,1},{10,3},{12,5},{14,7},{17,24},{19,... | collective-permute-start | bytes 4177928 | tf_op jit(solution)/shard_map/ppermute | solution.py:33
  22.9 13.9 %copy-start.20 = (f32[1,61]{1,0:T(1,128)S(1)}, f32[1,61]{1,0:T(1,128)}, u32[]{:S(2)}) copy-start(f32[1,61]{1,0:T(1,128)} %param.13) | copy-start | bytes 736
  22.9 13.9 %copy-start.21 = (f32[1,31]{1,0:T(1,128)S(1)}, f32[1,31]{1,0:T(1,128)}, u32[]{:S(2)}) copy-start(f32[1,31]{1,0:T(1,128)} %param.12) | copy-start | bytes 376
  23.0 13.9 %copy-start.22 = (f32[1,31]{1,0:T(1,128)S(1)}, f32[1,31]{1,0:T(1,128)}, u32[]{:S(2)}) copy-start(f32[1,31]{1,0:T(1,128)} %param.11) | copy-start | bytes 376
  23.1 13.4 %collective-permute-start.6 = (f32[8,96,256]{2,1,0:T(8,128)S(1)}, f32[8,96,256]{2,1,0:T(8,128)S(1)}, u32[]{:S(2)}, u32[]{:S(2)}) collective-permute-start(f32[8,96,256]{2,1,0:T(8,128)S(1)} %dynamic-slice_select_fusion), channel_id=1, source_target_pairs={{2,8},{3,9},{4,10},{5,11},{6,12},{7,13},{8,2},{9,3},{10,4},{11,5},... | collective-permute-start | bytes 2359304 | tf_op jit(solution)/shard_map/ppermute | solution.py:33
  33.2 21.4 %collective-permute-start.13 = (f32[17,80,256]{2,1,0:T(8,128)S(1)}, f32[17,80,256]{2,1,0:T(8,128)}, u32[]{:S(2)}, u32[]{:S(2)}) collective-permute-start(f32[17,80,256]{2,1,0:T(8,128)S(1)} %copy-done.19), channel_id=1, source_target_pairs={{0,1},{1,9},{2,3},{3,11},{4,5},{5,13},{6,7},{7,15},{8,0},{9,8},{10... | collective-permute-start | bytes 4177928 | tf_op jit(solution)/shard_map/ppermute | solution.py:33
  36.5 20.4 %collective-permute-start.7 = (f32[8,96,256]{2,1,0:T(8,128)S(1)}, f32[8,96,256]{2,1,0:T(8,128)S(1)}, u32[]{:S(2)}, u32[]{:S(2)}) collective-permute-start(f32[8,96,256]{2,1,0:T(8,128)S(1)} %collective-permute-done.6.refs_0_), channel_id=1, source_target_pairs={{0,16},{1,17},{2,18},{3,19},{4,20},{5,21},{6,22},{7,23},{8,24},{9,... | collective-permute-start | bytes 2359304 | tf_op jit(solution)/shard_map/ppermute | solution.py:33
  36.9 10.8 %collective-permute-start = (f32[126]{0:T(128)S(1)}, f32[126]{0:T(128)S(1)}, u32[]{:S(2)}, u32[]{:S(2)}) collective-permute-start(f32[126]{0:T(128)S(1)} %pad_maximum_fusion.1), channel_id=1, source_target_pairs={{0,8},{1,9},{2,10},{3,11},{4,12},{5,13},{6,14},{7,15},{8,0},{9,1},... | collective-permute-start | bytes 1520 | tf_op jit(solution)/shard_map/ppermute | solution.py:33
  39.0 24.1 %collective-permute-start.8 = (f32[15,96,256]{2,1,0:T(8,128)}, f32[15,96,256]{2,1,0:T(8,128)}, u32[]{:S(2)}, u32[]{:S(2)}) collective-permute-start(f32[15,96,256]{2,1,0:T(8,128)} %get-tuple-element.75), channel_id=1, source_target_pairs={{0,8},{1,9},{2,10},{3,11},{4,12},{5,13},{6,14},{7,15},{8,0},{9,1},... | collective-permute-start | bytes 4423688 | tf_op jit(solution)/shard_map/ppermute | solution.py:33
  45.8 25.2 %collective-permute-start.4 = (f32[17,80,256]{2,1,0:T(8,128)}, f32[17,80,256]{2,1,0:T(8,128)}, u32[]{:S(2)}, u32[]{:S(2)}) collective-permute-start(f32[17,80,256]{2,1,0:T(8,128)} %broadcast_select_fusion.own_ref), channel_id=1, source_target_pairs={{2,8},{3,9},{4,10},{5,11},{6,12},{7,13},{8,2},{9,3},{10,4},{11,5},... | collective-permute-start | bytes 4177928 | tf_op jit(solution)/shard_map/ppermute | solution.py:33
  47.7 23.3 %collective-permute-start.5 = (f32[17,80,256]{2,1,0:T(8,128)}, f32[17,80,256]{2,1,0:T(8,128)}, u32[]{:S(2)}, u32[]{:S(2)}) collective-permute-start(f32[17,80,256]{2,1,0:T(8,128)} %broadcast_select_fusion.own_ref), channel_id=1, source_target_pairs={{0,8},{1,9},{2,10},{3,11},{4,12},{5,13},{6,14},{7,15},{8,0},{9,1},... | collective-permute-start | bytes 4177928 | tf_op jit(solution)/shard_map/ppermute | solution.py:33
  54.6 26.8 %collective-permute-start.14 = (f32[17,80,256]{2,1,0:T(8,128)}, f32[17,80,256]{2,1,0:T(8,128)}, u32[]{:S(2)}, u32[]{:S(2)}) collective-permute-start(f32[17,80,256]{2,1,0:T(8,128)} %collective-permute-done.13.own_ref), channel_id=1, source_target_pairs={{2,8},{3,9},{4,10},{5,11},{6,12},{7,13},{8,2},{9,3},{10,4},{11,5},... | collective-permute-start | bytes 4177928 | tf_op jit(solution)/shard_map/ppermute | solution.py:33
  57.8 23.6 %collective-permute-start.15 = (f32[17,80,256]{2,1,0:T(8,128)}, f32[17,80,256]{2,1,0:T(8,128)}, u32[]{:S(2)}, u32[]{:S(2)}) collective-permute-start(f32[17,80,256]{2,1,0:T(8,128)} %collective-permute-done.13.own_ref), channel_id=1, source_target_pairs={{0,8},{1,9},{2,10},{3,11},{4,12},{5,13},{6,14},{7,15},{8,0},{9,1},... | collective-permute-start | bytes 4177928 | tf_op jit(solution)/shard_map/ppermute | solution.py:33
  60.6 20.8 %copy-start.8 = (bf16[2,64,256]{2,1,0:T(8,128)(2,1)}, bf16[2,64,256]{2,1,0:T(8,128)(2,1)S(1)}, u32[]{:S(2)}) copy-start(bf16[2,64,256]{2,1,0:T(8,128)(2,1)S(1)} %get-tuple-element.80.refs_2_.refs_3_) | copy-start | bytes 196612
  78.3 12.3 %collective-permute-start.9 = (f32[15,32,256]{2,1,0:T(8,128)S(1)}, f32[15,32,256]{2,1,0:T(8,128)S(1)}, u32[]{:S(2)}, u32[]{:S(2)}) collective-permute-start(f32[15,32,256]{2,1,0:T(8,128)S(1)} %get-tuple-element.84), channel_id=1, source_target_pairs={{2,8},{3,9},{4,10},{5,11},{6,12},{7,13},{8,2},{9,3},{10,4},{11,5},... | collective-permute-start | bytes 1474568 | tf_op jit(solution)/shard_map/ppermute | solution.py:33
  81.3 9.3 %collective-permute-start.10 = (f32[15,32,256]{2,1,0:T(8,128)S(1)}, f32[15,32,256]{2,1,0:T(8,128)S(1)}, u32[]{:S(2)}, u32[]{:S(2)}) collective-permute-start(f32[15,32,256]{2,1,0:T(8,128)S(1)} %get-tuple-element.86), channel_id=1, source_target_pairs={{0,8},{1,9},{2,10},{3,11},{4,12},{5,13},{6,14},{7,15},{8,0},{9,1},... | collective-permute-start | bytes 1474568 | tf_op jit(solution)/shard_map/ppermute | solution.py:33
  87.7 10.4 %collective-permute-start.19 = (f32[15,32,256]{2,1,0:T(8,128)S(1)}, f32[15,32,256]{2,1,0:T(8,128)S(1)}, u32[]{:S(2)}, u32[]{:S(2)}) collective-permute-start(f32[15,32,256]{2,1,0:T(8,128)S(1)} %get-tuple-element.98), channel_id=1, source_target_pairs={{2,8},{3,9},{4,10},{5,11},{6,12},{7,13},{8,2},{9,3},{10,4},{11,5},... | collective-permute-start | bytes 1474568 | tf_op jit(solution)/shard_map/ppermute | solution.py:33
  90.2 8.1 %collective-permute-start.20 = (f32[15,32,256]{2,1,0:T(8,128)S(1)}, f32[15,32,256]{2,1,0:T(8,128)S(1)}, u32[]{:S(2)}, u32[]{:S(2)}) collective-permute-start(f32[15,32,256]{2,1,0:T(8,128)S(1)} %get-tuple-element.99), channel_id=1, source_target_pairs={{0,8},{1,9},{2,10},{3,11},{4,12},{5,13},{6,14},{7,15},{8,0},{9,1},... | collective-permute-start | bytes 1474568 | tf_op jit(solution)/shard_map/ppermute | solution.py:33
  91.7 11.7 %collective-permute-start.11 = (f32[15,32,256]{2,1,0:T(8,128)S(1)}, f32[15,32,256]{2,1,0:T(8,128)S(1)}, u32[]{:S(2)}, u32[]{:S(2)}) collective-permute-start(f32[15,32,256]{2,1,0:T(8,128)S(1)} %get-tuple-element.87), channel_id=1, source_target_pairs={{2,8},{3,9},{4,10},{5,11},{6,12},{7,13},{8,2},{9,3},{10,4},{11,5},... | collective-permute-start | bytes 1474568 | tf_op jit(solution)/shard_map/ppermute | solution.py:33
  94.4 8.9 %collective-permute-start.12 = (f32[15,32,256]{2,1,0:T(8,128)S(1)}, f32[15,32,256]{2,1,0:T(8,128)S(1)}, u32[]{:S(2)}, u32[]{:S(2)}) collective-permute-start(f32[15,32,256]{2,1,0:T(8,128)S(1)} %get-tuple-element.89), channel_id=1, source_target_pairs={{0,8},{1,9},{2,10},{3,11},{4,12},{5,13},{6,14},{7,15},{8,0},{9,1},... | collective-permute-start | bytes 1474568 | tf_op jit(solution)/shard_map/ppermute | solution.py:33
  94.9 13.7 %collective-permute-start.16 = (f32[15,32,256]{2,1,0:T(8,128)S(1)}, f32[15,32,256]{2,1,0:T(8,128)S(1)}, u32[]{:S(2)}, u32[]{:S(2)}) collective-permute-start(f32[15,32,256]{2,1,0:T(8,128)S(1)} %get-tuple-element.94), channel_id=1, source_target_pairs={{2,8},{3,9},{4,10},{5,11},{6,12},{7,13},{8,2},{9,3},{10,4},{11,5},... | collective-permute-start | bytes 1474568 | tf_op jit(solution)/shard_map/ppermute | solution.py:33
  98.1 10.5 %collective-permute-start.17 = (f32[15,32,256]{2,1,0:T(8,128)S(1)}, f32[15,32,256]{2,1,0:T(8,128)S(1)}, u32[]{:S(2)}, u32[]{:S(2)}) collective-permute-start(f32[15,32,256]{2,1,0:T(8,128)S(1)} %get-tuple-element.97), channel_id=1, source_target_pairs={{0,8},{1,9},{2,10},{3,11},{4,12},{5,13},{6,14},{7,15},{8,0},{9,1},... | collective-permute-start | bytes 1474568 | tf_op jit(solution)/shard_map/ppermute | solution.py:33
  99.3 13.2 %collective-permute-start.21 = (f32[16,32,256]{2,1,0:T(8,128)S(1)}, f32[16,32,256]{2,1,0:T(8,128)S(1)}, u32[]{:S(2)}, u32[]{:S(2)}) collective-permute-start(f32[16,32,256]{2,1,0:T(8,128)S(1)} %log_factor.11), channel_id=1, source_target_pairs={{0,16},{1,17},{2,18},{3,19},{4,20},{5,21},{6,22},{7,23},{8,24},{9,... | collective-permute-start | bytes 1572872 | tf_op jit(solution)/shard_map/ppermute | solution.py:33
  109.7 14.0 %collective-permute-start.18 = (f32[16,32,256]{2,1,0:T(8,128)S(1)}, f32[16,32,256]{2,1,0:T(8,128)S(1)}, u32[]{:S(2)}, u32[]{:S(2)}) collective-permute-start(f32[16,32,256]{2,1,0:T(8,128)S(1)} %log_factor.10.refs_0_), channel_id=1, source_target_pairs={{0,16},{1,17},{2,18},{3,19},{4,20},{5,21},{6,22},{7,23},{8,24},{9,... | collective-permute-start | bytes 1572872 | tf_op jit(solution)/shard_map/ppermute | solution.py:33
  113.4 16.6 %collective-permute-start.24 = (f32[16,32,256]{2,1,0:T(8,128)}, f32[16,32,256]{2,1,0:T(8,128)S(1)}, u32[]{:S(2)}, u32[]{:S(2)}) collective-permute-start(f32[16,32,256]{2,1,0:T(8,128)} %add_exponential_fusion.refs_2_), channel_id=1, source_target_pairs={{0,1},{1,0},{2,3},{3,2},{4,5},{5,4},{6,7},{7,6},{8,9},{9,8},{10,11... | collective-permute-start | bytes 1572872 | tf_op jit(solution)/shard_map/ppermute | solution.py:33
  126.3 7.0 %collective-permute-start.23 = (f32[15,64,256]{2,1,0:T(8,128)}, f32[15,64,256]{2,1,0:T(8,128)}, u32[]{:S(2)}, u32[]{:S(2)}) collective-permute-start(f32[15,64,256]{2,1,0:T(8,128)} %get-tuple-element.103), channel_id=1, source_target_pairs={{0,8},{1,9},{2,10},{3,11},{4,12},{5,13},{6,14},{7,15},{8,0},{9,1},... | collective-permute-start | bytes 2949128 | tf_op jit(solution)/shard_map/ppermute | solution.py:33
  127.5 15.9 %collective-permute-start.22 = (f32[15,64,256]{2,1,0:T(8,128)}, f32[15,64,256]{2,1,0:T(8,128)}, u32[]{:S(2)}, u32[]{:S(2)}) collective-permute-start(f32[15,64,256]{2,1,0:T(8,128)} %get-tuple-element.102), channel_id=1, source_target_pairs={{2,8},{3,9},{4,10},{5,11},{6,12},{7,13},{8,2},{9,3},{10,4},{11,5},... | collective-permute-start | bytes 2949128 | tf_op jit(solution)/shard_map/ppermute | solution.py:33
  130.1 16.6 %collective-permute-start.26 = (f32[15,32,256]{2,1,0:T(8,128)S(1)}, f32[15,32,256]{2,1,0:T(8,128)S(1)}, u32[]{:S(2)}, u32[]{:S(2)}) collective-permute-start(f32[15,32,256]{2,1,0:T(8,128)S(1)} %get-tuple-element.127), channel_id=1, source_target_pairs={{0,8},{1,9},{2,10},{3,11},{4,12},{5,13},{6,14},{7,15},{8,0},{9,1},... | collective-permute-start | bytes 1474568 | tf_op jit(solution)/shard_map/ppermute | solution.py:33
  130.7 17.7 %collective-permute-start.25 = (f32[15,32,256]{2,1,0:T(8,128)S(1)}, f32[15,32,256]{2,1,0:T(8,128)S(1)}, u32[]{:S(2)}, u32[]{:S(2)}) collective-permute-start(f32[15,32,256]{2,1,0:T(8,128)S(1)} %get-tuple-element.128), channel_id=1, source_target_pairs={{2,8},{3,9},{4,10},{5,11},{6,12},{7,13},{8,2},{9,3},{10,4},{11,5},... | collective-permute-start | bytes 1474568 | tf_op jit(solution)/shard_map/ppermute | solution.py:33
  153.2 10.1 %collective-permute-start.27 = (f32[15,32,256]{2,1,0:T(8,128)S(1)}, f32[15,32,256]{2,1,0:T(8,128)S(1)}, u32[]{:S(2)}, u32[]{:S(2)}) collective-permute-start(f32[15,32,256]{2,1,0:T(8,128)S(1)} %get-tuple-element.110), channel_id=1, source_target_pairs={{2,8},{3,9},{4,10},{5,11},{6,12},{7,13},{8,2},{9,3},{10,4},{11,5},... | collective-permute-start | bytes 1474568 | tf_op jit(solution)/shard_map/ppermute | solution.py:33
  155.7 7.7 %collective-permute-start.28 = (f32[15,32,256]{2,1,0:T(8,128)S(1)}, f32[15,32,256]{2,1,0:T(8,128)S(1)}, u32[]{:S(2)}, u32[]{:S(2)}) collective-permute-start(f32[15,32,256]{2,1,0:T(8,128)S(1)} %get-tuple-element.112), channel_id=1, source_target_pairs={{0,8},{1,9},{2,10},{3,11},{4,12},{5,13},{6,14},{7,15},{8,0},{9,1},... | collective-permute-start | bytes 1474568 | tf_op jit(solution)/shard_map/ppermute | solution.py:33
  160.1 10.1 %collective-permute-start.29 = (f32[15,32,256]{2,1,0:T(8,128)S(1)}, f32[15,32,256]{2,1,0:T(8,128)S(1)}, u32[]{:S(2)}, u32[]{:S(2)}) collective-permute-start(f32[15,32,256]{2,1,0:T(8,128)S(1)} %get-tuple-element.116), channel_id=1, source_target_pairs={{2,8},{3,9},{4,10},{5,11},{6,12},{7,13},{8,2},{9,3},{10,4},{11,5},... | collective-permute-start | bytes 1474568 | tf_op jit(solution)/shard_map/ppermute | solution.py:33
  162.6 7.6 %collective-permute-start.30 = (f32[15,32,256]{2,1,0:T(8,128)S(1)}, f32[15,32,256]{2,1,0:T(8,128)S(1)}, u32[]{:S(2)}, u32[]{:S(2)}) collective-permute-start(f32[15,32,256]{2,1,0:T(8,128)S(1)} %get-tuple-element.118), channel_id=1, source_target_pairs={{0,8},{1,9},{2,10},{3,11},{4,12},{5,13},{6,14},{7,15},{8,0},{9,1},... | collective-permute-start | bytes 1474568 | tf_op jit(solution)/shard_map/ppermute | solution.py:33
  171.3 25.1 %collective-permute-start.31 = (f32[16,32,256]{2,1,0:T(8,128)S(1)}, f32[16,32,256]{2,1,0:T(8,128)S(1)}, u32[]{:S(2)}, u32[]{:S(2)}) collective-permute-start(f32[16,32,256]{2,1,0:T(8,128)S(1)} %log_factor.13.refs_0_), channel_id=1, source_target_pairs={{0,16},{2,18},{4,20},{6,22},{9,25},{11,27},{13,29},{15,31},{16,0},... | collective-permute-start | bytes 1572872 | tf_op jit(solution)/shard_map/ppermute | solution.py:33
  172.0 11.4 %collective-permute-start.35 = (f32[15,32,256]{2,1,0:T(8,128)S(1)}, f32[15,32,256]{2,1,0:T(8,128)S(1)}, u32[]{:S(2)}, u32[]{:S(2)}) collective-permute-start(f32[15,32,256]{2,1,0:T(8,128)S(1)} %get-tuple-element.120), channel_id=1, source_target_pairs={{2,8},{3,9},{4,10},{5,11},{6,12},{7,13},{8,2},{9,3},{10,4},{11,5},... | collective-permute-start | bytes 1474568 | tf_op jit(solution)/shard_map/ppermute | solution.py:33
  176.6 10.8 %collective-permute-start.36 = (f32[15,32,256]{2,1,0:T(8,128)S(1)}, f32[15,32,256]{2,1,0:T(8,128)S(1)}, u32[]{:S(2)}, u32[]{:S(2)}) collective-permute-start(f32[15,32,256]{2,1,0:T(8,128)S(1)} %get-tuple-element.122), channel_id=1, source_target_pairs={{0,8},{1,9},{2,10},{3,11},{4,12},{5,13},{6,14},{7,15},{8,0},{9,1},... | collective-permute-start | bytes 1474568 | tf_op jit(solution)/shard_map/ppermute | solution.py:33
  176.7 14.0 %collective-permute-start.37 = (f32[15,32,256]{2,1,0:T(8,128)S(1)}, f32[15,32,256]{2,1,0:T(8,128)S(1)}, u32[]{:S(2)}, u32[]{:S(2)}) collective-permute-start(f32[15,32,256]{2,1,0:T(8,128)S(1)} %get-tuple-element.124), channel_id=1, source_target_pairs={{2,8},{3,9},{4,10},{5,11},{6,12},{7,13},{8,2},{9,3},{10,4},{11,5},... | collective-permute-start | bytes 1474568 | tf_op jit(solution)/shard_map/ppermute | solution.py:33
  178.6 12.1 %collective-permute-start.38 = (f32[15,32,256]{2,1,0:T(8,128)S(1)}, f32[15,32,256]{2,1,0:T(8,128)S(1)}, u32[]{:S(2)}, u32[]{:S(2)}) collective-permute-start(f32[15,32,256]{2,1,0:T(8,128)S(1)} %get-tuple-element.126), channel_id=1, source_target_pairs={{0,8},{1,9},{2,10},{3,11},{4,12},{5,13},{6,14},{7,15},{8,0},{9,1},... | collective-permute-start | bytes 1474568 | tf_op jit(solution)/shard_map/ppermute | solution.py:33
  183.4 15.0 %collective-permute-start.32 = (f32[16,32,256]{2,1,0:T(8,128)S(1)}, f32[16,32,256]{2,1,0:T(8,128)S(1)}, u32[]{:S(2)}, u32[]{:S(2)}) collective-permute-start(f32[16,32,256]{2,1,0:T(8,128)S(1)} %log_factor.13.refs_0_), channel_id=1, source_target_pairs={{1,24},{3,26},{5,28},{7,30},{8,17},{10,19},{12,21},{14,23},{17,8},... | collective-permute-start | bytes 1572872 | tf_op jit(solution)/shard_map/ppermute | solution.py:33
  187.4 15.3 %collective-permute-start.33 = (f32[16,32,256]{2,1,0:T(8,128)S(1)}, f32[16,32,256]{2,1,0:T(8,128)S(1)}, u32[]{:S(2)}, u32[]{:S(2)}) collective-permute-start(f32[16,32,256]{2,1,0:T(8,128)S(1)} %log_factor.13.refs_0_), channel_id=1, source_target_pairs={{1,8},{3,10},{5,12},{7,14},{8,1},{10,3},{12,5},{14,7},{17,24},{19,... | collective-permute-start | bytes 1572872 | tf_op jit(solution)/shard_map/ppermute | solution.py:33
  191.8 11.2 %collective-permute-start.39 = (f32[16,32,256]{2,1,0:T(8,128)S(1)}, f32[16,32,256]{2,1,0:T(8,128)S(1)}, u32[]{:S(2)}, u32[]{:S(2)}) collective-permute-start(f32[16,32,256]{2,1,0:T(8,128)S(1)} %log_factor.15.refs_0_), channel_id=1, source_target_pairs={{0,16},{2,18},{4,20},{6,22},{9,25},{11,27},{13,29},{15,31},{16,0},... | collective-permute-start | bytes 1572872 | tf_op jit(solution)/shard_map/ppermute | solution.py:33
  192.5 15.8 %collective-permute-start.40 = (f32[16,32,256]{2,1,0:T(8,128)S(1)}, f32[16,32,256]{2,1,0:T(8,128)S(1)}, u32[]{:S(2)}, u32[]{:S(2)}) collective-permute-start(f32[16,32,256]{2,1,0:T(8,128)S(1)} %log_factor.15.refs_0_), channel_id=1, source_target_pairs={{1,24},{3,26},{5,28},{7,30},{8,17},{10,19},{12,21},{14,23},{17,8},... | collective-permute-start | bytes 1572872 | tf_op jit(solution)/shard_map/ppermute | solution.py:33
  196.4 15.2 %collective-permute-start.41 = (f32[16,32,256]{2,1,0:T(8,128)S(1)}, f32[16,32,256]{2,1,0:T(8,128)S(1)}, u32[]{:S(2)}, u32[]{:S(2)}) collective-permute-start(f32[16,32,256]{2,1,0:T(8,128)S(1)} %log_factor.15.refs_0_), channel_id=1, source_target_pairs={{1,8},{3,10},{5,12},{7,14},{8,1},{10,3},{12,5},{14,7},{17,24},{19,... | collective-permute-start | bytes 1572872 | tf_op jit(solution)/shard_map/ppermute | solution.py:33
  202.9 8.9 %collective-permute-start.34 = (f32[16,32,256]{2,1,0:T(8,128)S(1)}, f32[16,32,256]{2,1,0:T(8,128)S(1)}, u32[]{:S(2)}, u32[]{:S(2)}) collective-permute-start(f32[16,32,256]{2,1,0:T(8,128)S(1)} %last_update.2.refs_0_), channel_id=1, source_target_pairs={{0,8},{1,9},{2,10},{3,11},{4,12},{5,13},{6,14},{7,15},{8,0},{9,1},... | collective-permute-start | bytes 1572872 | tf_op jit(solution)/shard_map/ppermute | solution.py:33
  211.7 2.0 collective-permute-start.42
  (18 other events, 48.8 us)

commit v6 on v5

--- a/solution.py
+++ b/solution.py
@@ -105,11 +105,19 @@
     )
 
 
-def tables_kernel(
-    ky_ref, tz_ref, tx_ref, yf_ref, ya_ref, zhi_ref, zlo_ref, xhi_ref, xlo_ref, *, sizes, cells_y, radius_x, radius_z
-):
-    taps = ky_ref.shape[1]
-    radius = taps // 2
+def place(row, count, width, turned, spacing):
+    source, target = iota((row.shape[1], width), 0), iota((row.shape[1], width), 1)
+    index = count - 1 - source if turned else source
+    ones = (target == spacing * index) & (source < count)
+    return jnp.dot(row, ones.astype(F32), precision=lax.Precision.HIGHEST, preferred_element_type=F32)
+
+
+def tables_kernel(mine_ref, other_ref, yf_ref, ya_ref, zhi_ref, zlo_ref, xhi_ref, xlo_ref, *, sizes, cells_y, taps):
+    taps_x, taps_y, taps_z = taps
+    straight = core() == half()
+    mine, other = mine_ref[...], other_ref[...]
+    both = (jnp.where(straight, mine, other), jnp.where(straight, other, mine))
+    radius, radius_x, radius_z = taps_y // 2, taps_x // 2, taps_z // 2
     side = half()
     own, near, wide = sizes
     for index in range(4):
@@ -123,22 +131,26 @@
         delta = (row - col if adjoint else col - row) + radius
         delta = jnp.where(lane < width, delta, -1)
         band = jnp.zeros((rows, lanes), F32)
-        for a in range(taps):
-            band = jnp.where(delta == a, ky_ref[index % 2, a], band)
+        values = both[index % 2][:, 128:256]
+        for a in range(taps_y):
+            band = jnp.where(delta == a, jnp.broadcast_to(values[:, a:a + 1], (rows, lanes)), band)
         high, low = split(band)
         high, low = high.astype(F32), low.astype(F32)
         out_ref[index % 2] = (high + pltpu.roll(high, width, 1) + pltpu.roll(low, 2 * width, 1)).astype(BF16)
 
-    lanes = tz_ref.shape[1]
+    lanes = zhi_ref.shape[2]
     near_z = jnp.abs(iota((lanes, lanes), 1) - iota((lanes, lanes), 0)) <= radius_z
     for index in range(4):
-        base = pltpu.roll(tz_ref[index:index + 1, :], lanes - radius_z, 1)
+        base = place(both[index % 2][:, 256:384], taps_z, lanes, index < 2, 1)
+        base = pltpu.roll(base, lanes - radius_z, 1)
         band = pltpu.roll(jnp.broadcast_to(base, (lanes, lanes)), 0, 1, stride=1, stride_axis=0)
         zhi_ref[index], zlo_ref[index] = split(jnp.where(near_z, band, jnp.zeros_like(band)))
 
-    rows, lanes = xhi_ref.shape[1] // 2, tx_ref.shape[1]
+    rows = xhi_ref.shape[1] // 2
+    lanes = max(512, 1 << (xhi_ref.shape[2] - 1).bit_length())
     for index in range(4):
-        base = jnp.broadcast_to(tx_ref[index:index + 1, :], (rows, lanes))
+        base = place(both[index % 2][:, :128], taps_x, lanes, index >= 2, 8)
+        base = jnp.broadcast_to(base, (rows, lanes))
         band = pltpu.roll(base, 0, 1, stride=1, stride_axis=0)
         lane = iota((rows, lanes), 1)
         edge = 8 * radius_x
@@ -151,21 +163,15 @@
         band = jnp.where(
             lane < rows + edge, near_part, jnp.where((lane >= far) & (lane < far + edge), far_part, zero)
         )[:, :xhi_ref.shape[2]]
-        place = (index // 2, slice(index % 2 * rows, index % 2 * rows + rows))
-        xhi_ref[place], xlo_ref[place] = split(band)
-
-
-def make_tables(kx, ky, kz, planes, cells_y, cells_z, sizes):
+        block = (index // 2, slice(index % 2 * rows, index % 2 * rows + rows))
+        xhi_ref[block], xlo_ref[block] = split(band)
+
+
+def make_tables(mine, other, taps, planes, cells_y, cells_z, sizes):
     own, near, wide = sizes
-    taps_x, taps_z = kx.shape[1], kz.shape[1]
-    depth = pad_to(8 * (planes + taps_x // 2), 128) + pad_to(8 * (taps_x // 2), 128)
-    lanes = max(512, 1 << (depth - 1).bit_length())
-    zero = jnp.zeros((), F32)
-    tx = jnp.concatenate([kx, kx[:, ::-1]])
-    tx = lax.pad(tx, zero, ((0, 0, 0), (0, lanes - 8 * taps_x + 7, 7)))
-    tz = jnp.concatenate([kz[:, ::-1], kz])
-    tz = lax.pad(tz, zero, ((0, 0, 0), (0, cells_z - taps_z, 0)))
-    kernel = functools.partial(tables_kernel, sizes=sizes, cells_y=cells_y, radius_x=taps_x // 2, radius_z=taps_z // 2)
+    radius = taps[0] // 2
+    depth = pad_to(8 * (planes + radius), 128) + pad_to(8 * radius, 128)
+    kernel = functools.partial(tables_kernel, sizes=sizes, cells_y=cells_y, taps=taps)
     shape = jax.ShapeDtypeStruct
     out_shape = (
         shape((2, near, pad_to(3 * wide, 128)), BF16),
@@ -175,7 +181,7 @@
         shape((2, 2 * 8 * planes, depth), BF16),
         shape((2, 2 * 8 * planes, depth), BF16),
     )
-    return call(kernel, out_shape, [SMEM, VMEM, VMEM], "band_matrices")(ky, tz, tx)
+    return call(kernel, out_shape, [VMEM, VMEM], "band_matrices")(mine, other)
 
 
 def window_kernel(estimate_ref, own_ref, other_ref):
@@ -325,12 +331,15 @@
     lax.fori_loop(0, rows // 8, body, 0)
 
 
-def blur_x(tables, far, own, near):
+def blur_near(tables, own, near):
     shape = jax.ShapeDtypeStruct(own.shape, F32)
-    shapes = (shape, shape)
-    parts = call(blur_near_kernel, shapes, [VMEM] * 4, "blur_x_near")(*tables[4:], own, near)
-    kernel = functools.partial(blur_far_kernel, radius=near.shape[0])
-    return call(kernel, shapes, [VMEM] * 5, "blur_x_far")(*tables[4:], far, *parts)
+    return call(blur_near_kernel, (shape, shape), [VMEM] * 4, "blur_x_near")(*tables[4:], own, near)
+
+
+def blur_far(tables, far, parts, radius):
+    shape = jax.ShapeDtypeStruct(parts[0].shape, F32)
+    kernel = functools.partial(blur_far_kernel, radius=radius)
+    return call(kernel, (shape, shape), [VMEM] * 5, "blur_x_far")(*tables[4:], far, *parts)
 
 
 def spread_y(band, x):
@@ -370,14 +379,29 @@
 
 
 def first_ratio_kernel(shift_ref, far_ref, near_ref, own_ref, *refs, order, wides, extent_x, cells_y):
-    image_ref = refs[-1]
+    refs, image_ref, (planes_ref, mask_ref, semaphores) = refs[:-4], refs[-4], refs[-3:]
     planes, near, cells_z = image_ref.shape
     side = half()
     slab = lax.axis_index("tile") - side + core()
     shift_x, shift_y, shift_z = (shift_ref[order, i] for i in range(3))
     lanes = pad_to(cells_y, 128)
     pick = iota((near, lanes), 1) == global_row(side, iota((near, lanes), 0), cells_y)
-    mask = own_ref[planes, :planes, :lanes].astype(BF16)
+
+    def copy(ref, index, p):
+        return pltpu.make_async_copy(ref.at[index], planes_ref.at[p], semaphores.at[p])
+
+    mask_copy = pltpu.make_async_copy(own_ref.at[planes, pl.ds(0, planes)], mask_ref, semaphores.at[planes])
+    mask_copy.start()
+    for p in range(planes):
+        source = p + shift_x
+        is_own = (source >= 0) & (source < planes)
+        is_far = (source < 0) == (core() == 0)
+        beyond = jnp.clip(jnp.where(source < 0, source + planes, source - planes), 0, planes - 1)
+        pl.when(is_own)(copy(own_ref, jnp.clip(source, 0, planes - 1), p).start)
+        pl.when(jnp.logical_not(is_own) & is_far)(copy(far_ref, beyond, p).start)
+        pl.when(jnp.logical_not(is_own) & jnp.logical_not(is_far))(copy(near_ref, beyond, p).start)
+    mask_copy.wait()
+    mask = mask_ref[:, :lanes].astype(BF16)
     columns = lax.dot_general(
         pick.astype(F32).astype(BF16), mask, (((1,), (1,)), ((), ())), preferred_element_type=F32
     )
@@ -386,20 +410,16 @@
     inside = (row >= 0) & (row < cells_y) & (col >= 0) & (col < cells_z)
 
     def fetch(p):
-        source = p + shift_x
-        x = slab * planes + source
-        beyond = jnp.clip(jnp.where(source < 0, source + planes, source - planes), 0, planes - 1)
-        is_far = (source < 0) == (core() == 0)
-        outer = jnp.where(is_far, far_ref[beyond], near_ref[beyond])
-        is_own = (source >= 0) & (source < planes)
-        value = jnp.where(is_own, own_ref[jnp.clip(source, 0, planes - 1)], outer)
+        copy(own_ref, 0, p).wait()
+        x = slab * planes + p + shift_x
+        value = planes_ref[p]
         weight = jnp.broadcast_to(columns[:, p:p + 1], (near, cells_z))
         covered = inside & (weight > 0.5) & (x >= 0) & (x < extent_x)
         value = jnp.where(covered, value, jnp.full_like(value, -1.0))
         image_ref[p] = value
         return value
 
-    ratio_planes(refs[:wides], fetch, *refs[wides:wides + 4], order, refs[wides + 4:-1])
+    ratio_planes(refs[:wides], fetch, *refs[wides:wides + 4], order, refs[wides + 4:])
 
 
 def next_ratio_kernel(image_ref, *refs, order, wides):
@@ -418,9 +438,11 @@
     )
     image = jax.ShapeDtypeStruct((planes, tables[0].shape[1], lanes), F32)
     out_shape = ratio_shapes(wides, tables, radius, chunks) + (image,)
-    return call(kernel, out_shape, [SMEM] + [VMEM] * (7 + len(wides)), "image_and_ratio")(
-        shifts, *blocks, *wides, *tables[:4]
-    )
+    scratch = [
+        pltpu.VMEM(image.shape, F32), pltpu.VMEM((planes, lanes), F32), pltpu.SemaphoreType.DMA((planes + 1,))
+    ]
+    in_specs = [SMEM] + [pl.BlockSpec(memory_space=pl.ANY)] * 3 + [VMEM] * (4 + len(wides))
+    return call(kernel, out_shape, in_specs, "image_and_ratio", scratch)(shifts, *blocks, *wides, *tables[:4])
 
 
 def next_ratio(image, wides, tables, order, radius, chunks):
@@ -430,18 +452,17 @@
     )
 
 
-def factor_kernel(hi_ref, lo_ref, before_ref, far_ref, own_ref, near_ref, out_ref, *, order, start, share):
+def factor_kernel(hi_ref, lo_ref, before_ref, far_ref, near_ref, own_ref, out_ref, *, order, starts, share):
     planes, rows, _ = out_ref.shape
     band_rows = slice(order * 8 * planes, (order + 1) * 8 * planes)
 
     def body(step, carry):
         row = pl.multiple_of(step * 8, 8)
-        source = pl.multiple_of(start + row, 8)
+        total = before_ref[:, pl.ds(pl.multiple_of(starts[0] + row, 8), 8), :]
         if share:
-            total = share * jnp.log(before_ref[:, pl.ds(source, 8), :])
-        else:
-            total = before_ref[:, pl.ds(row, 8), :]
-        blocks = [[gather(own_ref, source), gather(near_ref, row)], [gather(far_ref, row)]]
+            total = share * jnp.log(total)
+        own = gather(own_ref, pl.multiple_of(starts[1] + row, 8))
+        blocks = [[own, gather(near_ref, row)], [gather(far_ref, row)]]
         factor = spread_x(hi_ref, lo_ref, 1, band_rows, slice(None), blocks)
         out_ref[:, pl.ds(row, 8), :] = total + jnp.log(factor)
         return carry
@@ -449,11 +470,11 @@
     lax.fori_loop(0, rows // 8, body, 0)
 
 
-def log_factor(tables, before, side, order, start, share):
-    far, own, near = side
-    kernel = functools.partial(factor_kernel, order=order, start=start, share=share)
+def log_factor(tables, before, side, order, before_start, own_start, share):
+    far, near, own = side
+    kernel = functools.partial(factor_kernel, order=order, starts=(before_start, own_start), share=share)
     shape = jax.ShapeDtypeStruct((own.shape[0],) + far.shape[1:], F32)
-    return call(kernel, shape, [VMEM] * 6, "log_factor")(*tables[4:], before, far, own, near)
+    return call(kernel, shape, [VMEM] * 6, "log_factor")(*tables[4:], before, far, near, own)
 
 
 def update_kernel(*refs):
@@ -526,8 +547,8 @@
     planes, cells_y, cells_z = estimate.shape
     views, slabs = lax.axis_size("view"), lax.axis_size("tile")
     groups = views // 2
-    taps_x, taps_y, taps_z = kern_x.shape[1], kern_y.shape[1], kern_z.shape[1]
-    radius = taps_x // 2
+    taps_y = kern_y.shape[1]
+    radius = kern_x.shape[1] // 2
     own_rows = cells_y // 2
     near = own_rows + pad_to(taps_y // 2, GROUP)
     wide = own_rows + pad_to(2 * (taps_y // 2), GROUP)
@@ -551,82 +572,68 @@
     piece = after(piece, first)
     arrived = send(first, lambda g, c, q, r: (g, r, q, c) if c != r else None)
 
-    mine = jnp.concatenate([kern_x[0], kern_y[0], kern_z[0], offsets[0].astype(F32)])
-    mine = after(mine, first)
+    mine = [jnp.pad(row, ((0, 0), (0, 128 - row.shape[1]))) for row in (kern_x, kern_y, kern_z, offsets.astype(F32))]
+    mine = jnp.concatenate(mine, axis=1)
     other = send(mine, to_core_partner)
-    both = jnp.where(straight, jnp.stack([mine, other]), jnp.stack([other, mine]))
-    kx = both[:, :taps_x]
-    ky = both[:, taps_x:taps_x + taps_y]
-    kz = both[:, taps_x + taps_y:taps_x + taps_y + taps_z]
-    shifts = both[:, taps_x + taps_y + taps_z:].astype(jnp.int32)
-    tables = make_tables(kx, ky, kz, planes, cells_y, cells_z, (own_rows, near, wide))
+    taps = kern_x.shape[1], taps_y, kern_z.shape[1]
+    tables = make_tables(mine, other, taps, planes, cells_y, cells_z, (own_rows, near, wide))
+    shifts = jnp.where(straight, jnp.concatenate([mine, other]), jnp.concatenate([other, mine]))
+    shifts = shifts[:, 384:384 + offsets.shape[1]].astype(jnp.int32)
 
     start = group * (planes // groups)
     share = jnp.where(straight, lax.dynamic_slice_in_dim(window, start, planes // groups, 0), piece)
+    later = after(after(piece, tables[0]), share)
     share = send(share, to_far)
-    pieces = [piece] + [send(piece, across(turn, when=lambda c, r: c != r)) for turn in range(1, groups)]
-    current, _, close = assemble(window, pieces, radius)
+    pieces = [piece] + [send(later, across(turn, when=lambda c, r: c != r)) for turn in range(1, groups)]
+    current, _, close = assemble(after(window, share), pieces, radius)
     second = after(second, current)
     second = send(second, lambda g, c, q, r: (g, r, q, 1 - c))
     distant = assemble_far([share] + [send(share, across(turn)) for turn in range(1, groups)])
-    chunks = [(distant, current, send(close, to_core_partner))]
+    chunks = [(distant, blur_near(tables, current, after(send(close, to_core_partner), distant)))]
     first = jnp.where(straight, first, arrived)
+    second = after(second, chunks[0][1][0])
     blocks = [(*neighbours(block, block), block) for block in (first, second)]
     images = [None, None]
 
-    row_chunks = [(0, inner_rows), (inner_rows, edge_rows)]
-    sizes = [size for _, size in row_chunks]
+    sizes = [[own_rows], [inner_rows, edge_rows]]
 
     for step in range(ITERS):
-        last = step == ITERS - 1
-        wides = [blur_x(tables, *chunk) for chunk in chunks]
-        spreads, edges = [], []
+        wides = []
+        for distant, parts in chunks:
+            distant = after(distant, wides[-1][0]) if wides else distant
+            wides.append(blur_far(tables, distant, parts, radius))
+        sides = []
         for order in range(2):
             parts = [chunk[order] for chunk in wides]
             if step == 0:
-                spread, *edge, images[order] = first_ratio(
-                    shifts, blocks[order], parts, tables, order, radius, sizes, planes * slabs, cells_y
+                spread, *edges, images[order] = first_ratio(
+                    shifts, blocks[order], parts, tables, order, radius, sizes[order], planes * slabs, cells_y
                 )
             else:
-                spread, *edge = next_ratio(images[order], parts, tables, order, radius, sizes)
-            spreads.append(spread)
-            edges.append(edge)
-
-        totals = [None, None]
-        hook = None
-        for index in (1, 0):
-            total = current
-            for order in range(2):
-                distant, close = edges[order][2 * index:2 * index + 2]
-                if hook is not None:
-                    distant, close = after(distant, hook), after(close, hook)
-                distant, close = neighbours(distant, close)
-                side = (distant, spreads[order], close)
-                total = log_factor(tables, total, side, order, row_chunks[index][0], 0 if order else 1.0 / groups)
-                if index == 1 and order == 0:
-                    first_total = total
-            hook = first_total
-            totals[index] = total
-
-        if not last:
-            inner, edge = totals
+                spread, *edges = next_ratio(images[order], parts, tables, order, radius, sizes[order])
+            sides += [(*neighbours(*edges[k:k + 2]), spread) for k in range(0, len(edges), 2)]
+
+        total = log_factor(tables, current, sides[0], 0, 0, 0, 1.0 / groups)
+        edge = log_factor(tables, after(total, sides[1][1]), sides[2], 1, inner_rows, inner_rows, 0)
+        inner = log_factor(tables, total, sides[1], 1, 0, 0, 0)
+
+        if step < ITERS - 1:
             edge_parts = [edge] + [send(edge, across(turn)) for turn in range(1, groups)]
             inner_parts = [inner] + [send(inner, across(turn)) for turn in range(1, groups)]
             edge = jnp.exp(sum(edge_parts[1:], edge_parts[0]))
             beyond = send(edge, to_row_partner)
             current, distant, close = update(inner_parts, edge, radius)
             distant, close = neighbours(distant, close)
-            chunks = [(distant, current, close)]
+            chunks = [(distant, blur_near(tables, current, close))]
             rest = planes - radius
             distant, close = neighbours(
                 lax.dynamic_slice_in_dim(beyond, core() * rest, radius, 0),
                 lax.dynamic_slice_in_dim(beyond, (1 - core()) * rest, radius, 0),
             )
-            chunks.append((distant, beyond, close))
+            chunks.append((distant, blur_near(tables, beyond, after(close, chunks[0][1][0]))))
 
     pieces = []
-    for index in (1, 0):
-        own = totals[index]
+    for own in (edge, inner):
         other_parts = [
             send(own, across(turn, lambda r: 1 - r, lambda c: 1 - c, lambda c, r: c != r))
             for turn in reversed(range(groups))
@@ -634,7 +641,7 @@
         own_parts = [own] + [send(own, across(turn, when=lambda c, r: c == r)) for turn in range(1, groups)]
         mine = finish(own_parts, other_parts)
         pieces += [mine, send(mine, to_core_partner)]
-    return join(pieces, [row_chunks[1][0], row_chunks[0][0]], estimate.shape)
+    return join(pieces, [inner_rows, 0], estimate.shape)
 
 
 def solution(mesh):

time: 218 us -> 218 us (level)
  local copies, waits for them, and re-layouts: 12.6 us -> 6.72 us
  starting transfers between devices: 68.2 us -> 71.6 us
    unnamed x46 -> x30, local copies, waits for them, and re-layouts: 12 us -> 5.63 us
    ppermute x43 -> x39, starting transfers between devices: 68.2 us -> 71.6 us  [send(): return lax.ppermute(array, AXES, moves(move))]
    ppermute x43 -> x39, waiting for transfers between devices: 71.8 us -> 73 us  [send(): return lax.ppermute(array, AXES, moves(move))]
    pallas_call x8 -> x6, Pallas kernels: 8.59 us -> 8.61 us  [log_factor(): call(kernel, shape, [VMEM] * 6, 'log_factor')]
  transfers between devices with their start and end apart: 43 -> 39, of which waited for: 19 -> 17; matrix products, arithmetic and copies ran while one was open for 2% -> 2% of each run, Pallas kernels for 23% -> 24%
where the time goes in v6:
time: 218 us; the launch traced here: 216 us
  waiting for transfers between devices  73 us (33%)
  starting transfers between devices  71.6 us (33%)
  Pallas kernels  60 us (28%)
  local copies, waits for them, and re-layouts  6.72 us (3%)
  other arithmetic  3.7 us (2%)
    ppermute x39, waiting for transfers between devices, send(): return lax.ppermute(array, AXES, moves(move))  73 us
    ppermute x39, starting transfers between devices, send(): return lax.ppermute(array, AXES, moves(move))  71.6 us
    pallas_call x2, Pallas kernels, first_ratio(): call(kernel, out_shape, in_specs, 'image_and_ratio', scratch)  15.8 us
    pallas_call x6, Pallas kernels, log_factor(): call(kernel, shape, [VMEM] * 6, 'log_factor')  8.61 us
    pallas_call x3, Pallas kernels, blur_near(): call(blur_near_kernel, (shape, shape), [VMEM] * 4, 'blur_x_near')  7.73 us
    pallas_call x2, Pallas kernels, next_ratio(): call(kernel, ratio_shapes(wides, tables, radius, chunks), [VMEM] * (5 + l...  7.5 us
    pallas_call x3, Pallas kernels, blur_far(): call(kernel, (shape, shape), [VMEM] * 5, 'blur_x_far')  7.49 us
    unnamed x30, local copies, waits for them, and re-layouts  5.63 us
  transfers between devices with their start and end apart: 39, of which 17 were waited for; matrix products, arithmetic and copies ran while one was open for 2% of the time, Pallas kernels for 24%

profile of v6, /device:TPU:17, one launch (start us, length us, event | category | flops | bytes accessed | tf_op | source)
XLA Modules:
  0.0 215.8 jit_solution(4601499903589021827)
XLA Ops:
  4.2 3.8 %collective-permute-start = (f32[1,512]{1,0:T(1,128)S(1)}, f32[1,512]{1,0:T(1,128)S(1)}, u32[]{:S(2)}, u32[]{:S(2)}) collective-permute-start(f32[1,512]{1,0:T(1,128)S(1)} %pad_maximum_fusion.mine_ref), channel_id=1, source_target_pairs={{0,8},{1,9},{2,10},{3,11},{4,12},{5,13},{6,14},{7,15},{8,0},{9,1},... | collective-permute-start | bytes 6152 | tf_op jit(solution)/shard_map/ppermute | solution.py:33
  8.0 1.6 copy-done
  9.6 4.1 %shift_recorded.1 = (f32[17,80,256]{2,1,0:T(8,128)}, f32[17,80,256]{2,1,0:T(8,128)S(1)}) custom-call(s32[1,3]{1,0:T(1,128)S(1)} %copy-done.9, f32[16,128,256]{2,1,0:T(8,128)S(1)} %bitcast.2, s32[16,128]{1,0:T(8,128)S(1)} %bitcast.3), custom_call_target="tpu_custom_call" | custom-call | tf_op jit(solution)/shard_map/shift_recorded/pallas_call | solution.py:278
  14.8 1.9 collective-permute-start.4
  19.6 1.9 collective-permute-start.3
  21.5 3.3 %collective-permute-start.2 = (f32[8,96,256]{2,1,0:T(8,128)}, f32[8,96,256]{2,1,0:T(8,128)S(1)}, u32[]{:S(2)}, u32[]{:S(2)}) collective-permute-start(f32[8,96,256]{2,1,0:T(8,128)} %collective-permute-done.1.refs_0_), channel_id=1, source_target_pairs={{1,17},{3,19},{5,21},{7,23},{8,24},{10,26},{12,28},{14,30},{17,1},... | collective-permute-start | bytes 2359304 | tf_op jit(solution)/shard_map/ppermute | solution.py:33
  24.8 8.1 %collective-permute-done.3.refs_0_ = f32[8,96,256]{2,1,0:T(8,128)S(1)} collective-permute-done((f32[8,96,256]{2,1,0:T(8,128)S(1)}, f32[8,96,256]{2,1,0:T(8,128)S(1)}, u32[]{:S(2)}, u32[]{:S(2)}) %collective-permute-start.3) | collective-permute-done | bytes 786464 | tf_op jit(solution)/shard_map/ppermute | solution.py:33
  32.9 1.7 collective-permute-done.2.refs_1_
  34.6 2.7 %estimate.1 = (f32[16,96,256]{2,1,0:T(8,128)S(1)}, f32[15,96,256]{2,1,0:T(8,128)}, f32[15,96,256]{2,1,0:T(8,128)S(1)}) custom-call(f32[8,96,256]{2,1,0:T(8,128)} %collective-permute-done.1.refs_0_, f32[8,96,256]{2,1,0:T(8,128)S(1)} %collective-permute-done.2.refs_1_, f32[16,96,256]{2,1,0:T(8,128)S(1)} %get-tuple-element.72.refs_2_), custom_call_target="tpu_custom_call" | custom-call | tf_op jit(solution)/shard_map/estimate/pallas_call | solution.py:238
  40.5 6.1 %collective-permute-start.5 = (f32[17,80,256]{2,1,0:T(8,128)S(1)}, f32[17,80,256]{2,1,0:T(8,128)S(1)}, u32[]{:S(2)}, u32[]{:S(2)}) collective-permute-start(f32[17,80,256]{2,1,0:T(8,128)S(1)} %broadcast_select_fusion.own_ref), channel_id=1, source_target_pairs={{2,8},{3,9},{4,10},{5,11},{6,12},{7,13},{8,2},{9,3},{10,4},{11,5},... | collective-permute-start | bytes 4177928 | tf_op jit(solution)/shard_map/ppermute | solution.py:33
  46.8 7.3 %collective-permute-done.7.refs_1_ = f32[8,96,256]{2,1,0:T(8,128)S(1)} collective-permute-done((f32[8,96,256]{2,1,0:T(8,128)S(1)}, f32[8,96,256]{2,1,0:T(8,128)S(1)}, u32[]{:S(2)}, u32[]{:S(2)}) %collective-permute-start.7) | collective-permute-done | bytes 786464 | tf_op jit(solution)/shard_map/ppermute | solution.py:33
  54.2 3.3 %blur_x_near.3 = (f32[16,96,256]{2,1,0:T(8,128)S(1)}, f32[16,96,256]{2,1,0:T(8,128)S(1)}) custom-call(bf16[2,256,384]{2,1,0:T(8,128)(2,1)S(1)} %get-tuple-element.62.hi_ref, bf16[2,256,384]{2,1,0:T(8,128)(2,1)S(1)} %get-tuple-element.63.lo_ref, f32[16,96,256]{2,1,0:T(8,128)S(1)} %get-tuple-element.73.own_ref.before_ref, ...), custom_call_target="tpu_custom_call" | custom-call | tf_op jit(solution)/shard_map/blur_x_near/pallas_call | solution.py:336
  57.5 5.6 %collective-permute-start.12 = (f32[17,80,256]{2,1,0:T(8,128)S(1)}, f32[17,80,256]{2,1,0:T(8,128)S(1)}, u32[]{:S(2)}, u32[]{:S(2)}) collective-permute-start(f32[17,80,256]{2,1,0:T(8,128)S(1)} %collective-permute-done.11.own_ref), channel_id=1, source_target_pairs={{2,8},{3,9},{4,10},{5,11},{6,12},{7,13},{8,2},{9,3},{10,4},{11,5},... | collective-permute-start | bytes 4177928 | tf_op jit(solution)/shard_map/ppermute | solution.py:33
  63.2 3.2 %blur_x_far.3 = (f32[16,96,256]{2,1,0:T(8,128)S(1)}, f32[16,96,256]{2,1,0:T(8,128)S(1)}) custom-call(bf16[2,256,384]{2,1,0:T(8,128)(2,1)S(1)} %get-tuple-element.62.hi_ref, bf16[2,256,384]{2,1,0:T(8,128)(2,1)S(1)} %get-tuple-element.63.lo_ref, f32[16,96,256]{2,1,0:T(8,128)S(1)} %far_slab.1.far_ref, f32[16,96,256]{2,1,0:T(8,128)S(1)} %get-tuple-element.76.first_ref, ...), custom_call_target="tpu_custom_call" | custom-call | tf_op jit(solution)/shard_map/blur_x_far/pallas_call | solution.py:342
  66.5 7.8 %image_and_ratio.2 = (f32[16,64,256]{2,1,0:T(8,128)S(1)}, f32[15,64,256]{2,1,0:T(8,128)S(1)}, f32[15,64,256]{2,1,0:T(8,128)S(1)}, f32[16,80,256]{2,1,0:T(8,128)S(1)}) custom-call(s32[2,3]{1,0:T(2,128)S(1)} %fusion.1.shift_ref, f32[17,80,256]{2,1,0:T(8,128)S(1)} %collective-permute-done.5.far_ref, f32[17,80,256]{2,1,0:T(8,128)S(1)} %collective-permute-done.6.near_ref, ...), custom_call_target="tpu_custom_call" | custom-call | tf_op jit(solution)/shard_map/image_and_ratio/pallas_call | solution.py:445
  75.8 1.9 collective-permute-start.9
  77.7 1.8 collective-permute-done.12.far_ref
  79.6 8.0 %image_and_ratio.3 = (f32[16,64,256]{2,1,0:T(8,128)S(1)}, f32[15,32,256]{2,1,0:T(8,128)S(1)}, f32[15,32,256]{2,1,0:T(8,128)S(1)}, f32[15,32,256]{2,1,0:T(8,128)S...) custom-call(s32[2,3]{1,0:T(2,128)S(1)} %fusion.1.shift_ref, ...), custom_call_target="tpu_custom_call" | custom-call | tf_op jit(solution)/shard_map/image_and_ratio/pallas_call | solution.py:445
  89.1 1.9 collective-permute-start.17
  91.6 3.1 %collective-permute-start.14 = (f32[15,32,256]{2,1,0:T(8,128)S(1)}, f32[15,32,256]{2,1,0:T(8,128)S(1)}, u32[]{:S(2)}, u32[]{:S(2)}) collective-permute-start(f32[15,32,256]{2,1,0:T(8,128)S(1)} %get-tuple-element.89), channel_id=1, source_target_pairs={{2,8},{3,9},{4,10},{5,11},{6,12},{7,13},{8,2},{9,3},{10,4},{11,5},... | collective-permute-start | bytes 1474568 | tf_op jit(solution)/shard_map/ppermute | solution.py:33
  94.8 2.1 log_factor.6.before_ref
  96.9 2.6 %collective-permute-done.17.far_ref = f32[15,32,256]{2,1,0:T(8,128)S(1)} collective-permute-done((f32[15,32,256]{2,1,0:T(8,128)S(1)}, f32[15,32,256]{2,1,0:T(8,128)S(1)}, u32[]{:S(2)}, u32[]{:S(2)}) %collective-permute-start.17) | collective-permute-done | bytes 491552 | tf_op jit(solution)/shard_map/ppermute | solution.py:33
  101.9 2.9 %collective-permute-done.14.far_ref = f32[15,32,256]{2,1,0:T(8,128)S(1)} collective-permute-done((f32[15,32,256]{2,1,0:T(8,128)S(1)}, f32[15,32,256]{2,1,0:T(8,128)S(1)}, u32[]{:S(2)}, u32[]{:S(2)}) %collective-permute-start.14) | collective-permute-done | bytes 491552 | tf_op jit(solution)/shard_map/ppermute | solution.py:33
  107.1 7.3 %collective-permute-done.19 = f32[16,32,256]{2,1,0:T(8,128)S(1)} collective-permute-done((f32[16,32,256]{2,1,0:T(8,128)S(1)}, f32[16,32,256]{2,1,0:T(8,128)S(1)}, u32[]{:S(2)}, u32[]{:S(2)}) %collective-permute-start.19) | collective-permute-done | bytes 524320 | tf_op jit(solution)/shard_map/ppermute | solution.py:33
  115.3 2.4 %collective-permute-start.22 = (f32[16,32,256]{2,1,0:T(8,128)}, f32[16,32,256]{2,1,0:T(8,128)S(1)}, u32[]{:S(2)}, u32[]{:S(2)}) collective-permute-start(f32[16,32,256]{2,1,0:T(8,128)} %add_exponential_fusion.refs_2_), channel_id=1, source_target_pairs={{0,1},{1,0},{2,3},{3,2},{4,5},{5,4},{6,7},{7,6},{8,9},{9,8},{10,11... | collective-permute-start | bytes 1572872 | tf_op jit(solution)/shard_map/ppermute | solution.py:33
  117.7 8.0 %collective-permute-done.16.refs_1_ = f32[16,32,256]{2,1,0:T(8,128)S(1)} collective-permute-done((f32[16,32,256]{2,1,0:T(8,128)S(1)}, f32[16,32,256]{2,1,0:T(8,128)S(1)}, u32[]{:S(2)}, u32[]{:S(2)}) %collective-permute-start.16) | collective-permute-done | bytes 524320 | tf_op jit(solution)/shard_map/ppermute | solution.py:33
  125.7 2.6 %update.1 = (f32[16,64,256]{2,1,0:T(8,128)S(1)}, f32[15,64,256]{2,1,0:T(8,128)}, f32[15,64,256]{2,1,0:T(8,128)}) custom-call(f32[16,32,256]{2,1,0:T(8,128)S(1)} %log_factor.7.refs_0_, f32[16,32,256]{2,1,0:T(8,128)S(1)} %collective-permute-done.16.refs_1_, f32[16,32,256]{2,1,0:T(8,128)} %add_exponential_fusion.refs_2_), custom_call_target="tpu_custom_call" | custom-call | tf_op jit(solution)/shard_map/update/pallas_call | solution.py:494
  128.8 1.9 collective-permute-start.20
  131.5 3.1 %collective-permute-start.23 = (f32[15,32,256]{2,1,0:T(8,128)S(1)}, f32[15,32,256]{2,1,0:T(8,128)S(1)}, u32[]{:S(2)}, u32[]{:S(2)}) collective-permute-start(f32[15,32,256]{2,1,0:T(8,128)S(1)} %get-tuple-element.120), channel_id=1, source_target_pairs={{2,8},{3,9},{4,10},{5,11},{6,12},{7,13},{8,2},{9,3},{10,4},{11,5},... | collective-permute-start | bytes 1474568 | tf_op jit(solution)/shard_map/ppermute | solution.py:33
  134.6 3.4 %blur_x_near.4 = (f32[16,64,256]{2,1,0:T(8,128)S(1)}, f32[16,64,256]{2,1,0:T(8,128)S(1)}) custom-call(bf16[2,256,384]{2,1,0:T(8,128)(2,1)S(1)} %get-tuple-element.62.hi_ref, bf16[2,256,384]{2,1,0:T(8,128)(2,1)S(1)} %get-tuple-element.63.lo_ref, f32[16,64,256]{2,1,0:T(8,128)S(1)} %get-tuple-element.95.own_ref.before_ref, ...), custom_call_target="tpu_custom_call" | custom-call | tf_op jit(solution)/shard_map/blur_x_near/pallas_call | solution.py:336
  138.0 6.7 %collective-permute-done.20.far_ref = f32[15,64,256]{2,1,0:T(8,128)} collective-permute-done((f32[15,64,256]{2,1,0:T(8,128)}, f32[15,64,256]{2,1,0:T(8,128)}, u32[]{:S(2)}, u32[]{:S(2)}) %collective-permute-start.20) | collective-permute-done | bytes 983072 | tf_op jit(solution)/shard_map/ppermute | solution.py:33
  144.7 3.3 %blur_x_far.4 = (f32[16,64,256]{2,1,0:T(8,128)S(1)}, f32[16,64,256]{2,1,0:T(8,128)S(1)}) custom-call(bf16[2,256,384]{2,1,0:T(8,128)(2,1)S(1)} %get-tuple-element.62.hi_ref, bf16[2,256,384]{2,1,0:T(8,128)(2,1)S(1)} %get-tuple-element.63.lo_ref, f32[15,64,256]{2,1,0:T(8,128)} %collective-permute-done.20.far_ref, ...), custom_call_target="tpu_custom_call" | custom-call | tf_op jit(solution)/shard_map/blur_x_far/pallas_call | solution.py:342
  148.0 1.7 collective-permute-done.23.far_ref
  152.1 3.8 %ratio.2 = (f32[16,64,256]{2,1,0:T(8,128)S(1)}, f32[15,64,256]{2,1,0:T(8,128)S(1)}, f32[15,64,256]{2,1,0:T(8,128)S(1)}) custom-call(f32[16,80,256]{2,1,0:T(8,128)S(1)} %copy-done.3, f32[16,64,256]{2,1,0:T(8,128)S(1)} %get-tuple-element.101.refs_0_, f32[16,32,256]{2,1,0:T(8,128)S(1)} %get-tuple-element.106.refs_1_, ...), custom_call_target="tpu_custom_call" | custom-call | tf_op jit(solution)/shard_map/ratio/pallas_call | solution.py:450
  155.8 1.9 collective-permute-start.25
  158.4 3.8 %ratio.3 = (f32[16,64,256]{2,1,0:T(8,128)S(1)}, f32[15,32,256]{2,1,0:T(8,128)S(1)}, f32[15,32,256]{2,1,0:T(8,128)S(1)}, f32[15,32,256]{2,1,0:T(8,128)S(1)}, f32[15,32,256]{2,1,0:T(8,128)S(1)}) custom-call(f32[16,80,256]{2,1,0:T(8,128)S(1)} %copy-done.5, f32[16,64,256]{2,1,0:T(8,128)S(1)} %get-tuple-element.111.refs_0_, ...), custom_call_target="tpu_custom_call" | custom-call | tf_op jit(solution)/shard_map/ratio/pallas_call | solution.py:450
  162.2 3.6 %collective-permute-start.34 = (f32[15,32,256]{2,1,0:T(8,128)S(1)}, f32[15,32,256]{2,1,0:T(8,128)S(1)}, u32[]{:S(2)}, u32[]{:S(2)}) collective-permute-start(f32[15,32,256]{2,1,0:T(8,128)S(1)} %get-tuple-element.118), channel_id=1, source_target_pairs={{2,8},{3,9},{4,10},{5,11},{6,12},{7,13},{8,2},{9,3},{10,4},{11,5},... | collective-permute-start | bytes 1474568 | tf_op jit(solution)/shard_map/ppermute | solution.py:33
  165.8 5.7 %collective-permute-done.25.far_ref = f32[15,64,256]{2,1,0:T(8,128)S(1)} collective-permute-done((f32[15,64,256]{2,1,0:T(8,128)S(1)}, f32[15,64,256]{2,1,0:T(8,128)S(1)}, u32[]{:S(2)}, u32[]{:S(2)}) %collective-permute-start.25) | collective-permute-done | bytes 983072 | tf_op jit(solution)/shard_map/ppermute | solution.py:33
  171.6 2.2 %log_factor.9.before_ref = f32[16,64,256]{2,1,0:T(8,128)S(1)} custom-call(bf16[2,256,384]{2,1,0:T(8,128)(2,1)S(1)} %get-tuple-element.62.hi_ref, bf16[2,256,384]{2,1,0:T(8,128)(2,1)S(1)} %get-tuple-element.63.lo_ref, f32[16,64,256]{2,1,0:T(8,128)S(1)} %get-tuple-element.95.own_ref.before_ref, f32[15,64,256]{2,1,0:T(8,128)S(1)} %collective-permute-done.25.far_ref, ...), custom_call_target="tpu_custom_call" | custom-call | tf_op jit(solution)/shard_map/log_factor/pallas_call | solution.py:477
  173.8 2.8 %collective-permute-done.34.far_ref = f32[15,32,256]{2,1,0:T(8,128)S(1)} collective-permute-done((f32[15,32,256]{2,1,0:T(8,128)S(1)}, f32[15,32,256]{2,1,0:T(8,128)S(1)}, u32[]{:S(2)}, u32[]{:S(2)}) %collective-permute-start.34) | collective-permute-done | bytes 491552 | tf_op jit(solution)/shard_map/ppermute | solution.py:33
  178.3 4.6 %collective-permute-start.28 = (f32[15,32,256]{2,1,0:T(8,128)S(1)}, f32[15,32,256]{2,1,0:T(8,128)S(1)}, u32[]{:S(2)}, u32[]{:S(2)}) collective-permute-start(f32[15,32,256]{2,1,0:T(8,128)S(1)} %get-tuple-element.115), channel_id=1, source_target_pairs={{2,8},{3,9},{4,10},{5,11},{6,12},{7,13},{8,2},{9,3},{10,4},{11,5},... | collective-permute-start | bytes 1474568 | tf_op jit(solution)/shard_map/ppermute | solution.py:33
  183.0 4.5 %collective-permute-start.36 = (f32[16,32,256]{2,1,0:T(8,128)S(1)}, f32[16,32,256]{2,1,0:T(8,128)S(1)}, u32[]{:S(2)}, u32[]{:S(2)}) collective-permute-start(f32[16,32,256]{2,1,0:T(8,128)S(1)} %log_factor.11.refs_0_), channel_id=1, source_target_pairs={{1,24},{3,26},{5,28},{7,30},{8,17},{10,19},{12,21},{14,23},{17,8},... | collective-permute-start | bytes 1572872 | tf_op jit(solution)/shard_map/ppermute | solution.py:33
  187.6 1.9 collective-permute-start.37
  191.5 4.3 %collective-permute-start.31 = (f32[16,32,256]{2,1,0:T(8,128)S(1)}, f32[16,32,256]{2,1,0:T(8,128)S(1)}, u32[]{:S(2)}, u32[]{:S(2)}) collective-permute-start(f32[16,32,256]{2,1,0:T(8,128)S(1)} %log_factor.10.refs_0_), channel_id=1, source_target_pairs={{1,24},{3,26},{5,28},{7,30},{8,17},{10,19},{12,21},{14,23},{17,8},... | collective-permute-start | bytes 1572872 | tf_op jit(solution)/shard_map/ppermute | solution.py:33
  195.9 1.9 collective-permute-start.32
  197.8 8.6 %collective-permute-done.37.refs_3_ = f32[16,32,256]{2,1,0:T(8,128)S(1)} collective-permute-done((f32[16,32,256]{2,1,0:T(8,128)S(1)}, f32[16,32,256]{2,1,0:T(8,128)S(1)}, u32[]{:S(2)}, u32[]{:S(2)}) %collective-permute-start.37) | collective-permute-done | bytes 524320 | tf_op jit(solution)/shard_map/ppermute | solution.py:33
  207.1 5.1 %collective-permute-done.32.refs_3_ = f32[16,32,256]{2,1,0:T(8,128)S(1)} collective-permute-done((f32[16,32,256]{2,1,0:T(8,128)S(1)}, f32[16,32,256]{2,1,0:T(8,128)S(1)}, u32[]{:S(2)}, u32[]{:S(2)}) %collective-permute-start.32) | collective-permute-done | bytes 524320 | tf_op jit(solution)/shard_map/ppermute | solution.py:33
  212.4 1.9 collective-permute-done.33.refs_1_
  (97 shorter events, 31.3 us)
Async XLA Ops:
  1.6 2.5 %copy-start.9 = (s32[1,3]{1,0:T(1,128)S(1)}, s32[1,3]{1,0:T(1,128)}, u32[]{:S(2)}) copy-start(s32[1,3]{1,0:T(1,128)} %offsets_ref.1) | copy-start | bytes 40
  1.6 2.5 %copy-start.12 = (f32[1,31]{1,0:T(1,128)S(1)}, f32[1,31]{1,0:T(1,128)}, u32[]{:S(2)}) copy-start(f32[1,31]{1,0:T(1,128)} %param.11) | copy-start | bytes 376
  1.6 2.6 %copy-start.13 = (f32[1,31]{1,0:T(1,128)S(1)}, f32[1,31]{1,0:T(1,128)}, u32[]{:S(2)}) copy-start(f32[1,31]{1,0:T(1,128)} %param.12) | copy-start | bytes 376
  1.6 2.6 %copy-start.14 = (f32[1,61]{1,0:T(1,128)S(1)}, f32[1,61]{1,0:T(1,128)}, u32[]{:S(2)}) copy-start(f32[1,61]{1,0:T(1,128)} %param.13) | copy-start | bytes 736
  1.6 6.4 %copy-start.8 = (s32[1,16,128]{2,1,0:T(8,128)S(1)}, s32[1,16,128]{2,1,0:T(8,128)}, u32[]{:S(2)}) copy-start(s32[1,16,128]{2,1,0:T(8,128)} %param.10) | copy-start | bytes 24580
  2.8 15.5 %collective-permute-start.1 = (f32[8,96,256]{2,1,0:T(8,128)}, f32[8,96,256]{2,1,0:T(8,128)}, u32[]{:S(2)}, u32[]{:S(2)}) collective-permute-start(f32[8,96,256]{2,1,0:T(8,128)} %constant_dynamic-slice_fusion.2), channel_id=1, source_target_pairs={{0,1},{2,3},{4,5},{6,7},{9,8},{11,10},{13,12},{15,14},{16,17},{18,... | collective-permute-start | bytes 2359304 | tf_op jit(solution)/shard_map/ppermute | solution.py:33
  4.2 12.5 %collective-permute-start = (f32[1,512]{1,0:T(1,128)S(1)}, f32[1,512]{1,0:T(1,128)S(1)}, u32[]{:S(2)}, u32[]{:S(2)}) collective-permute-start(f32[1,512]{1,0:T(1,128)S(1)} %pad_maximum_fusion.mine_ref), channel_id=1, source_target_pairs={{0,8},{1,9},{2,10},{3,11},{4,12},{5,13},{6,14},{7,15},{8,0},{9,1},... | collective-permute-start | bytes 6152 | tf_op jit(solution)/shard_map/ppermute | solution.py:33
  14.8 24.2 %collective-permute-start.4 = (f32[17,80,256]{2,1,0:T(8,128)}, f32[17,80,256]{2,1,0:T(8,128)}, u32[]{:S(2)}, u32[]{:S(2)}) collective-permute-start(f32[17,80,256]{2,1,0:T(8,128)} %get-tuple-element.67), channel_id=1, source_target_pairs={{1,8},{3,10},{5,12},{7,14},{8,1},{10,3},{12,5},{14,7},{17,24},{19,... | collective-permute-start | bytes 4177928 | tf_op jit(solution)/shard_map/ppermute | solution.py:33
  18.3 61.3 %copy-start.6 = (bf16[2,64,256]{2,1,0:T(8,128)(2,1)}, bf16[2,64,256]{2,1,0:T(8,128)(2,1)S(1)}, u32[]{:S(2)}) copy-start(bf16[2,64,256]{2,1,0:T(8,128)(2,1)S(1)} %get-tuple-element.79.refs_2_.refs_3_) | copy-start | bytes 196612
  19.6 13.3 %collective-permute-start.3 = (f32[8,96,256]{2,1,0:T(8,128)S(1)}, f32[8,96,256]{2,1,0:T(8,128)S(1)}, u32[]{:S(2)}, u32[]{:S(2)}) collective-permute-start(f32[8,96,256]{2,1,0:T(8,128)S(1)} %dynamic-slice_select_fusion), channel_id=1, source_target_pairs={{2,8},{3,9},{4,10},{5,11},{6,12},{7,13},{8,2},{9,3},{10,4},{11,5},... | collective-permute-start | bytes 2359304 | tf_op jit(solution)/shard_map/ppermute | solution.py:33
  21.5 15.8 %copy-start.11 = (f32[17,80,256]{2,1,0:T(8,128)S(1)}, f32[17,80,256]{2,1,0:T(8,128)}, u32[]{:S(2)}) copy-start(f32[17,80,256]{2,1,0:T(8,128)} %copy-done.10) | copy-start | bytes 4177924
  21.5 13.1 %collective-permute-start.2 = (f32[8,96,256]{2,1,0:T(8,128)}, f32[8,96,256]{2,1,0:T(8,128)S(1)}, u32[]{:S(2)}, u32[]{:S(2)}) collective-permute-start(f32[8,96,256]{2,1,0:T(8,128)} %collective-permute-done.1.refs_0_), channel_id=1, source_target_pairs={{1,17},{3,19},{5,21},{7,23},{8,24},{10,26},{12,28},{14,30},{17,1},... | collective-permute-start | bytes 2359304 | tf_op jit(solution)/shard_map/ppermute | solution.py:33
  37.3 17.0 %collective-permute-start.8 = (f32[15,96,256]{2,1,0:T(8,128)S(1)}, f32[15,96,256]{2,1,0:T(8,128)S(1)}, u32[]{:S(2)}, u32[]{:S(2)}) collective-permute-start(f32[15,96,256]{2,1,0:T(8,128)S(1)} %get-tuple-element.74), channel_id=1, source_target_pairs={{0,8},{1,9},{2,10},{3,11},{4,12},{5,13},{6,14},{7,15},{8,0},{9,1},... | collective-permute-start | bytes 4423688 | tf_op jit(solution)/shard_map/ppermute | solution.py:33
  37.3 20.2 %collective-permute-start.11 = (f32[17,80,256]{2,1,0:T(8,128)S(1)}, f32[17,80,256]{2,1,0:T(8,128)S(1)}, u32[]{:S(2)}, u32[]{:S(2)}) collective-permute-start(f32[17,80,256]{2,1,0:T(8,128)S(1)} %copy-done.11), channel_id=1, source_target_pairs={{0,1},{1,9},{2,3},{3,11},{4,5},{5,13},{6,7},{7,15},{8,0},{9,8},{10... | collective-permute-start | bytes 4177928 | tf_op jit(solution)/shard_map/ppermute | solution.py:33
  37.8 16.3 %collective-permute-start.7 = (f32[8,96,256]{2,1,0:T(8,128)S(1)}, f32[8,96,256]{2,1,0:T(8,128)S(1)}, u32[]{:S(2)}, u32[]{:S(2)}) collective-permute-start(f32[8,96,256]{2,1,0:T(8,128)S(1)} %collective-permute-done.3.refs_0_), channel_id=1, source_target_pairs={{0,16},{1,17},{2,18},{3,19},{4,20},{5,21},{6,22},{7,23},{8,24},{9,... | collective-permute-start | bytes 2359304 | tf_op jit(solution)/shard_map/ppermute | solution.py:33
  40.5 25.9 %collective-permute-start.5 = (f32[17,80,256]{2,1,0:T(8,128)S(1)}, f32[17,80,256]{2,1,0:T(8,128)S(1)}, u32[]{:S(2)}, u32[]{:S(2)}) collective-permute-start(f32[17,80,256]{2,1,0:T(8,128)S(1)} %broadcast_select_fusion.own_ref), channel_id=1, source_target_pairs={{2,8},{3,9},{4,10},{5,11},{6,12},{7,13},{8,2},{9,3},{10,4},{11,5},... | collective-permute-start | bytes 4177928 | tf_op jit(solution)/shard_map/ppermute | solution.py:33
  46.7 19.8 %collective-permute-start.6 = (f32[17,80,256]{2,1,0:T(8,128)S(1)}, f32[17,80,256]{2,1,0:T(8,128)S(1)}, u32[]{:S(2)}, u32[]{:S(2)}) collective-permute-start(f32[17,80,256]{2,1,0:T(8,128)S(1)} %broadcast_select_fusion.own_ref), channel_id=1, source_target_pairs={{0,8},{1,9},{2,10},{3,11},{4,12},{5,13},{6,14},{7,15},{8,0},{9,1},... | collective-permute-start | bytes 4177928 | tf_op jit(solution)/shard_map/ppermute | solution.py:33
  57.5 22.0 %collective-permute-start.12 = (f32[17,80,256]{2,1,0:T(8,128)S(1)}, f32[17,80,256]{2,1,0:T(8,128)S(1)}, u32[]{:S(2)}, u32[]{:S(2)}) collective-permute-start(f32[17,80,256]{2,1,0:T(8,128)S(1)} %collective-permute-done.11.own_ref), channel_id=1, source_target_pairs={{2,8},{3,9},{4,10},{5,11},{6,12},{7,13},{8,2},{9,3},{10,4},{11,5},... | collective-permute-start | bytes 4177928 | tf_op jit(solution)/shard_map/ppermute | solution.py:33
  63.1 16.5 %collective-permute-start.13 = (f32[17,80,256]{2,1,0:T(8,128)S(1)}, f32[17,80,256]{2,1,0:T(8,128)S(1)}, u32[]{:S(2)}, u32[]{:S(2)}) collective-permute-start(f32[17,80,256]{2,1,0:T(8,128)S(1)} %collective-permute-done.11.own_ref), channel_id=1, source_target_pairs={{0,8},{1,9},{2,10},{3,11},{4,12},{5,13},{6,14},{7,15},{8,0},{9,1},... | collective-permute-start | bytes 4177928 | tf_op jit(solution)/shard_map/ppermute | solution.py:33
  75.3 16.3 %collective-permute-start.10 = (f32[15,64,256]{2,1,0:T(8,128)S(1)}, f32[15,64,256]{2,1,0:T(8,128)S(1)}, u32[]{:S(2)}, u32[]{:S(2)}) collective-permute-start(f32[15,64,256]{2,1,0:T(8,128)S(1)} %get-tuple-element.83), channel_id=1, source_target_pairs={{0,8},{1,9},{2,10},{3,11},{4,12},{5,13},{6,14},{7,15},{8,0},{9,1},... | collective-permute-start | bytes 2949128 | tf_op jit(solution)/shard_map/ppermute | solution.py:33
  75.8 19.0 %collective-permute-start.9 = (f32[15,64,256]{2,1,0:T(8,128)S(1)}, f32[15,64,256]{2,1,0:T(8,128)S(1)}, u32[]{:S(2)}, u32[]{:S(2)}) collective-permute-start(f32[15,64,256]{2,1,0:T(8,128)S(1)} %get-tuple-element.82), channel_id=1, source_target_pairs={{2,8},{3,9},{4,10},{5,11},{6,12},{7,13},{8,2},{9,3},{10,4},{11,5},... | collective-permute-start | bytes 2949128 | tf_op jit(solution)/shard_map/ppermute | solution.py:33
  87.6 9.3 %copy-start.4 = (f32[16,80,256]{2,1,0:T(8,128)}, f32[16,80,256]{2,1,0:T(8,128)S(1)}, u32[]{:S(2)}) copy-start(f32[16,80,256]{2,1,0:T(8,128)S(1)} %get-tuple-element.110.image_ref) | copy-start | bytes 3932164
  87.6 9.3 %collective-permute-start.15 = (f32[15,32,256]{2,1,0:T(8,128)S(1)}, f32[15,32,256]{2,1,0:T(8,128)S(1)}, u32[]{:S(2)}, u32[]{:S(2)}) collective-permute-start(f32[15,32,256]{2,1,0:T(8,128)S(1)} %get-tuple-element.90), channel_id=1, source_target_pairs={{0,8},{1,9},{2,10},{3,11},{4,12},{5,13},{6,14},{7,15},{8,0},{9,1},... | collective-permute-start | bytes 1474568 | tf_op jit(solution)/shard_map/ppermute | solution.py:33
  89.1 10.4 %collective-permute-start.17 = (f32[15,32,256]{2,1,0:T(8,128)S(1)}, f32[15,32,256]{2,1,0:T(8,128)S(1)}, u32[]{:S(2)}, u32[]{:S(2)}) collective-permute-start(f32[15,32,256]{2,1,0:T(8,128)S(1)} %get-tuple-element.93), channel_id=1, source_target_pairs={{2,8},{3,9},{4,10},{5,11},{6,12},{7,13},{8,2},{9,3},{10,4},{11,5},... | collective-permute-start | bytes 1474568 | tf_op jit(solution)/shard_map/ppermute | solution.py:33
  91.0 8.5 %collective-permute-start.18 = (f32[15,32,256]{2,1,0:T(8,128)S(1)}, f32[15,32,256]{2,1,0:T(8,128)S(1)}, u32[]{:S(2)}, u32[]{:S(2)}) collective-permute-start(f32[15,32,256]{2,1,0:T(8,128)S(1)} %get-tuple-element.94), channel_id=1, source_target_pairs={{0,8},{1,9},{2,10},{3,11},{4,12},{5,13},{6,14},{7,15},{8,0},{9,1},... | collective-permute-start | bytes 1474568 | tf_op jit(solution)/shard_map/ppermute | solution.py:33
  91.6 13.2 %collective-permute-start.14 = (f32[15,32,256]{2,1,0:T(8,128)S(1)}, f32[15,32,256]{2,1,0:T(8,128)S(1)}, u32[]{:S(2)}, u32[]{:S(2)}) collective-permute-start(f32[15,32,256]{2,1,0:T(8,128)S(1)} %get-tuple-element.89), channel_id=1, source_target_pairs={{2,8},{3,9},{4,10},{5,11},{6,12},{7,13},{8,2},{9,3},{10,4},{11,5},... | collective-permute-start | bytes 1474568 | tf_op jit(solution)/shard_map/ppermute | solution.py:33
  100.6 13.8 %collective-permute-start.19 = (f32[16,32,256]{2,1,0:T(8,128)S(1)}, f32[16,32,256]{2,1,0:T(8,128)S(1)}, u32[]{:S(2)}, u32[]{:S(2)}) collective-permute-start(f32[16,32,256]{2,1,0:T(8,128)S(1)} %log_factor.8), channel_id=1, source_target_pairs={{0,16},{1,17},{2,18},{3,19},{4,20},{5,21},{6,22},{7,23},{8,24},{9,... | collective-permute-start | bytes 1572872 | tf_op jit(solution)/shard_map/ppermute | solution.py:33
  105.9 19.8 %collective-permute-start.16 = (f32[16,32,256]{2,1,0:T(8,128)S(1)}, f32[16,32,256]{2,1,0:T(8,128)S(1)}, u32[]{:S(2)}, u32[]{:S(2)}) collective-permute-start(f32[16,32,256]{2,1,0:T(8,128)S(1)} %log_factor.7.refs_0_), channel_id=1, source_target_pairs={{0,16},{1,17},{2,18},{3,19},{4,20},{5,21},{6,22},{7,23},{8,24},{9,... | collective-permute-start | bytes 1572872 | tf_op jit(solution)/shard_map/ppermute | solution.py:33
  115.3 15.4 %collective-permute-start.22 = (f32[16,32,256]{2,1,0:T(8,128)}, f32[16,32,256]{2,1,0:T(8,128)S(1)}, u32[]{:S(2)}, u32[]{:S(2)}) collective-permute-start(f32[16,32,256]{2,1,0:T(8,128)} %add_exponential_fusion.refs_2_), channel_id=1, source_target_pairs={{0,1},{1,0},{2,3},{3,2},{4,5},{5,4},{6,7},{7,6},{8,9},{9,8},{10,11... | collective-permute-start | bytes 1572872 | tf_op jit(solution)/shard_map/ppermute | solution.py:33
  128.2 6.4 %collective-permute-start.21 = (f32[15,64,256]{2,1,0:T(8,128)}, f32[15,64,256]{2,1,0:T(8,128)}, u32[]{:S(2)}, u32[]{:S(2)}) collective-permute-start(f32[15,64,256]{2,1,0:T(8,128)} %get-tuple-element.98), channel_id=1, source_target_pairs={{0,8},{1,9},{2,10},{3,11},{4,12},{5,13},{6,14},{7,15},{8,0},{9,1},... | collective-permute-start | bytes 2949128 | tf_op jit(solution)/shard_map/ppermute | solution.py:33
  128.8 15.9 %collective-permute-start.20 = (f32[15,64,256]{2,1,0:T(8,128)}, f32[15,64,256]{2,1,0:T(8,128)}, u32[]{:S(2)}, u32[]{:S(2)}) collective-permute-start(f32[15,64,256]{2,1,0:T(8,128)} %get-tuple-element.97), channel_id=1, source_target_pairs={{2,8},{3,9},{4,10},{5,11},{6,12},{7,13},{8,2},{9,3},{10,4},{11,5},... | collective-permute-start | bytes 2949128 | tf_op jit(solution)/shard_map/ppermute | solution.py:33
  130.8 17.1 %collective-permute-start.24 = (f32[15,32,256]{2,1,0:T(8,128)S(1)}, f32[15,32,256]{2,1,0:T(8,128)S(1)}, u32[]{:S(2)}, u32[]{:S(2)}) collective-permute-start(f32[15,32,256]{2,1,0:T(8,128)S(1)} %get-tuple-element.119), channel_id=1, source_target_pairs={{0,8},{1,9},{2,10},{3,11},{4,12},{5,13},{6,14},{7,15},{8,0},{9,1},... | collective-permute-start | bytes 1474568 | tf_op jit(solution)/shard_map/ppermute | solution.py:33
  131.5 18.2 %collective-permute-start.23 = (f32[15,32,256]{2,1,0:T(8,128)S(1)}, f32[15,32,256]{2,1,0:T(8,128)S(1)}, u32[]{:S(2)}, u32[]{:S(2)}) collective-permute-start(f32[15,32,256]{2,1,0:T(8,128)S(1)} %get-tuple-element.120), channel_id=1, source_target_pairs={{2,8},{3,9},{4,10},{5,11},{6,12},{7,13},{8,2},{9,3},{10,4},{11,5},... | collective-permute-start | bytes 1474568 | tf_op jit(solution)/shard_map/ppermute | solution.py:33
  152.1 6.3 %copy-start.5 = (f32[16,80,256]{2,1,0:T(8,128)S(1)}, f32[16,80,256]{2,1,0:T(8,128)}, u32[]{:S(2)}) copy-start(f32[16,80,256]{2,1,0:T(8,128)} %copy-done.4) | copy-start | bytes 3932164
  155.8 15.7 %collective-permute-start.25 = (f32[15,64,256]{2,1,0:T(8,128)S(1)}, f32[15,64,256]{2,1,0:T(8,128)S(1)}, u32[]{:S(2)}, u32[]{:S(2)}) collective-permute-start(f32[15,64,256]{2,1,0:T(8,128)S(1)} %get-tuple-element.107), channel_id=1, source_target_pairs={{2,8},{3,9},{4,10},{5,11},{6,12},{7,13},{8,2},{9,3},{10,4},{11,5},... | collective-permute-start | bytes 2949128 | tf_op jit(solution)/shard_map/ppermute | solution.py:33
  157.8 13.8 %collective-permute-start.26 = (f32[15,64,256]{2,1,0:T(8,128)S(1)}, f32[15,64,256]{2,1,0:T(8,128)S(1)}, u32[]{:S(2)}, u32[]{:S(2)}) collective-permute-start(f32[15,64,256]{2,1,0:T(8,128)S(1)} %get-tuple-element.108), channel_id=1, source_target_pairs={{0,8},{1,9},{2,10},{3,11},{4,12},{5,13},{6,14},{7,15},{8,0},{9,1},... | collective-permute-start | bytes 2949128 | tf_op jit(solution)/shard_map/ppermute | solution.py:33
  162.2 11.6 %collective-permute-start.27 = (f32[15,32,256]{2,1,0:T(8,128)S(1)}, f32[15,32,256]{2,1,0:T(8,128)S(1)}, u32[]{:S(2)}, u32[]{:S(2)}) collective-permute-start(f32[15,32,256]{2,1,0:T(8,128)S(1)} %get-tuple-element.113), channel_id=1, source_target_pairs={{0,8},{1,9},{2,10},{3,11},{4,12},{5,13},{6,14},{7,15},{8,0},{9,1},... | collective-permute-start | bytes 1474568 | tf_op jit(solution)/shard_map/ppermute | solution.py:33
  162.2 14.3 %collective-permute-start.34 = (f32[15,32,256]{2,1,0:T(8,128)S(1)}, f32[15,32,256]{2,1,0:T(8,128)S(1)}, u32[]{:S(2)}, u32[]{:S(2)}) collective-permute-start(f32[15,32,256]{2,1,0:T(8,128)S(1)} %get-tuple-element.118), channel_id=1, source_target_pairs={{2,8},{3,9},{4,10},{5,11},{6,12},{7,13},{8,2},{9,3},{10,4},{11,5},... | collective-permute-start | bytes 1474568 | tf_op jit(solution)/shard_map/ppermute | solution.py:33
  177.6 18.3 %collective-permute-start.35 = (f32[16,32,256]{2,1,0:T(8,128)S(1)}, f32[16,32,256]{2,1,0:T(8,128)S(1)}, u32[]{:S(2)}, u32[]{:S(2)}) collective-permute-start(f32[16,32,256]{2,1,0:T(8,128)S(1)} %log_factor.11.refs_0_), channel_id=1, source_target_pairs={{0,16},{2,18},{4,20},{6,22},{9,25},{11,27},{13,29},{15,31},{16,0},... | collective-permute-start | bytes 1572872 | tf_op jit(solution)/shard_map/ppermute | solution.py:33
  178.3 11.4 %collective-permute-start.28 = (f32[15,32,256]{2,1,0:T(8,128)S(1)}, f32[15,32,256]{2,1,0:T(8,128)S(1)}, u32[]{:S(2)}, u32[]{:S(2)}) collective-permute-start(f32[15,32,256]{2,1,0:T(8,128)S(1)} %get-tuple-element.115), channel_id=1, source_target_pairs={{2,8},{3,9},{4,10},{5,11},{6,12},{7,13},{8,2},{9,3},{10,4},{11,5},... | collective-permute-start | bytes 1474568 | tf_op jit(solution)/shard_map/ppermute | solution.py:33
  183.0 6.8 %collective-permute-start.29 = (f32[15,32,256]{2,1,0:T(8,128)S(1)}, f32[15,32,256]{2,1,0:T(8,128)S(1)}, u32[]{:S(2)}, u32[]{:S(2)}) collective-permute-start(f32[15,32,256]{2,1,0:T(8,128)S(1)} %get-tuple-element.116), channel_id=1, source_target_pairs={{0,8},{1,9},{2,10},{3,11},{4,12},{5,13},{6,14},{7,15},{8,0},{9,1},... | collective-permute-start | bytes 1474568 | tf_op jit(solution)/shard_map/ppermute | solution.py:33
  183.0 14.8 %collective-permute-start.36 = (f32[16,32,256]{2,1,0:T(8,128)S(1)}, f32[16,32,256]{2,1,0:T(8,128)S(1)}, u32[]{:S(2)}, u32[]{:S(2)}) collective-permute-start(f32[16,32,256]{2,1,0:T(8,128)S(1)} %log_factor.11.refs_0_), channel_id=1, source_target_pairs={{1,24},{3,26},{5,28},{7,30},{8,17},{10,19},{12,21},{14,23},{17,8},... | collective-permute-start | bytes 1572872 | tf_op jit(solution)/shard_map/ppermute | solution.py:33
  187.6 18.8 %collective-permute-start.37 = (f32[16,32,256]{2,1,0:T(8,128)S(1)}, f32[16,32,256]{2,1,0:T(8,128)S(1)}, u32[]{:S(2)}, u32[]{:S(2)}) collective-permute-start(f32[16,32,256]{2,1,0:T(8,128)S(1)} %log_factor.11.refs_0_), channel_id=1, source_target_pairs={{1,8},{3,10},{5,12},{7,14},{8,1},{10,3},{12,5},{14,7},{17,24},{19,... | collective-permute-start | bytes 1572872 | tf_op jit(solution)/shard_map/ppermute | solution.py:33
  190.8 15.8 %collective-permute-start.30 = (f32[16,32,256]{2,1,0:T(8,128)S(1)}, f32[16,32,256]{2,1,0:T(8,128)S(1)}, u32[]{:S(2)}, u32[]{:S(2)}) collective-permute-start(f32[16,32,256]{2,1,0:T(8,128)S(1)} %log_factor.10.refs_0_), channel_id=1, source_target_pairs={{0,16},{2,18},{4,20},{6,22},{9,25},{11,27},{13,29},{15,31},{16,0},... | collective-permute-start | bytes 1572872 | tf_op jit(solution)/shard_map/ppermute | solution.py:33
  191.5 15.6 %collective-permute-start.31 = (f32[16,32,256]{2,1,0:T(8,128)S(1)}, f32[16,32,256]{2,1,0:T(8,128)S(1)}, u32[]{:S(2)}, u32[]{:S(2)}) collective-permute-start(f32[16,32,256]{2,1,0:T(8,128)S(1)} %log_factor.10.refs_0_), channel_id=1, source_target_pairs={{1,24},{3,26},{5,28},{7,30},{8,17},{10,19},{12,21},{14,23},{17,8},... | collective-permute-start | bytes 1572872 | tf_op jit(solution)/shard_map/ppermute | solution.py:33
  195.9 16.3 %collective-permute-start.32 = (f32[16,32,256]{2,1,0:T(8,128)S(1)}, f32[16,32,256]{2,1,0:T(8,128)S(1)}, u32[]{:S(2)}, u32[]{:S(2)}) collective-permute-start(f32[16,32,256]{2,1,0:T(8,128)S(1)} %log_factor.10.refs_0_), channel_id=1, source_target_pairs={{1,8},{3,10},{5,12},{7,14},{8,1},{10,3},{12,5},{14,7},{17,24},{19,... | collective-permute-start | bytes 1572872 | tf_op jit(solution)/shard_map/ppermute | solution.py:33
  206.5 5.9 %collective-permute-start.38 = (f32[16,32,256]{2,1,0:T(8,128)S(1)}, f32[16,32,256]{2,1,0:T(8,128)S(1)}, u32[]{:S(2)}, u32[]{:S(2)}) collective-permute-start(f32[16,32,256]{2,1,0:T(8,128)S(1)} %last_update.3.refs_2_), channel_id=1, source_target_pairs={{0,8},{1,9},{2,10},{3,11},{4,12},{5,13},{6,14},{7,15},{8,0},{9,1},... | collective-permute-start | bytes 1572872 | tf_op jit(solution)/shard_map/ppermute | solution.py:33
  212.3 2.0 collective-permute-start.33
  (6 other events, 8.0 us)

commit v7 on v6

--- a/solution.py
+++ b/solution.py
@@ -211,18 +211,10 @@
         start += far_ref.shape[1]
 
 
-def assemble_kernel(*refs, count):
-    pieces, window, out_ref, edge_refs = refs[:count], refs[count:-1], refs[-1], ()
-    if len(refs) > count + 1:
-        window, out_ref, edge_refs = refs[count], refs[count + 1], refs[count + 2:]
-    straight, group = core() == half(), lax.axis_index("view") // 2
-    planes, share = out_ref.shape[0], pieces[0].shape[0]
-    for p in range(planes):
-        turn = lax.rem(group - p // share + count, count)
-        value = pieces[0][p % share]
-        for k in range(1, count):
-            value = jnp.where(turn == k, pieces[k][p % share], value)
-        out_ref[p] = jnp.where(straight, window[p], value) if edge_refs else value
+def choose_kernel(window_ref, crossed_ref, out_ref, *edge_refs):
+    straight = core() == half()
+    for p in range(out_ref.shape[0]):
+        out_ref[p] = jnp.where(straight, window_ref[p], crossed_ref[p])
     put_edges(out_ref, edge_refs)
 
 
@@ -232,17 +224,9 @@
     return (jax.ShapeDtypeStruct(shape, F32), *edges)
 
 
-def assemble(window, pieces, radius):
+def choose(window, crossed, radius):
     out_shape = edge_shapes(window.shape, radius, window.shape[1:2])
-    kernel = functools.partial(assemble_kernel, count=len(pieces))
-    return call(kernel, out_shape, [VMEM] * (1 + len(pieces)), "estimate")(*pieces, window)
-
-
-def assemble_far(pieces):
-    share, rows, lanes = pieces[0].shape
-    shape = jax.ShapeDtypeStruct((share * len(pieces), rows, lanes), F32)
-    kernel = functools.partial(assemble_kernel, count=len(pieces))
-    return call(kernel, (shape,), [VMEM] * len(pieces), "far_slab")(*pieces)[0]
+    return call(choose_kernel, out_shape, [VMEM] * 2, "estimate")(window, crossed)
 
 
 def shift_kernel(offsets_ref, acq_ref, mask_ref, first_ref, second_ref, turned_ref):
@@ -278,10 +262,8 @@
     return call(shift_kernel, (shape, shape), [SMEM, VMEM, VMEM], "shift_recorded", scratch)(offsets, acquired, mask)
 
 
-def gather(ref, row, radius=None):
-    if radius is None or ref.shape[0] == radius:
-        return ref[:, pl.ds(row, 8), :]
-    return ref[pl.ds((1 - core()) * (ref.shape[0] - radius), radius), pl.ds(row, 8), :]
+def gather(ref, row):
+    return ref[:, pl.ds(pl.multiple_of(row, 8), 8), :]
 
 
 def spread_x(hi_ref, lo_ref, index, band_rows, band_lanes, blocks):
@@ -316,14 +298,14 @@
     lax.fori_loop(0, rows // 8, body, 0)
 
 
-def blur_far_kernel(hi_ref, lo_ref, far_ref, first_ref, second_ref, first_out, second_out, *, radius):
+def blur_far_kernel(hi_ref, lo_ref, far_ref, first_ref, second_ref, first_out, second_out):
     planes, rows, _ = first_ref.shape
-    lanes = slice(near_lanes(planes, radius), None)
+    lanes = slice(near_lanes(planes, far_ref.shape[0]), None)
 
     def body(step, carry):
         row = pl.multiple_of(step * 8, 8)
         place = (slice(None), pl.ds(row, 8), slice(None))
-        out = spread_x(hi_ref, lo_ref, 0, slice(None), lanes, [[gather(far_ref, row, radius)]])
+        out = spread_x(hi_ref, lo_ref, 0, slice(None), lanes, [[gather(far_ref, row)]])
         first_out[place] = first_ref[place] + out[:planes]
         second_out[place] = second_ref[place] + out[planes:]
         return carry
@@ -336,10 +318,9 @@
     return call(blur_near_kernel, (shape, shape), [VMEM] * 4, "blur_x_near")(*tables[4:], own, near)
 
 
-def blur_far(tables, far, parts, radius):
+def blur_far(tables, far, parts):
     shape = jax.ShapeDtypeStruct(parts[0].shape, F32)
-    kernel = functools.partial(blur_far_kernel, radius=radius)
-    return call(kernel, (shape, shape), [VMEM] * 5, "blur_x_far")(*tables[4:], far, *parts)
+    return call(blur_far_kernel, (shape, shape), [VMEM] * 5, "blur_x_far")(*tables[4:], far, *parts)
 
 
 def spread_y(band, x):
@@ -356,19 +337,39 @@
     return dot(high, hi_ref[index]) + (dot(low, hi_ref[index]) + dot(high, lo_ref[index]))
 
 
-def ratio_planes(wide_refs, fetch, yf_ref, ya_ref, zhi_ref, zlo_ref, order, outs):
-    out_ref, edge_refs = outs[0], outs[1:]
+def blurred_planes(wide_refs, yf_ref, zhi_ref, zlo_ref, order, block):
+    wide = [jnp.concatenate([ref[p] for ref in wide_refs], axis=0) for p in block]
+    spread = jnp.concatenate([spread_y(yf_ref[order], rows) for rows in wide], axis=0)
+    return spread_z(spread, zhi_ref, zlo_ref, order)
+
+
+def plane_blocks(planes, step=4):
+    return [range(start, min(start + step, planes)) for start in range(0, planes, step)]
+
+
+def blur_yz_kernel(*refs, order):
+    wide_refs, (yf_ref, zhi_ref, zlo_ref, out_ref) = refs[:-4], refs[-4:]
+    near = yf_ref.shape[1]
+    for block in plane_blocks(out_ref.shape[0]):
+        blurred = blurred_planes(wide_refs, yf_ref, zhi_ref, zlo_ref, order, block)
+        for k, p in enumerate(block):
+            out_ref[p] = blurred[k * near:(k + 1) * near]
+
+
+def blur_yz(wides, tables, order):
+    planes, _, lanes = wides[0].shape
+    shape = jax.ShapeDtypeStruct((planes, tables[0].shape[1], lanes), F32)
+    kernel = functools.partial(blur_yz_kernel, order=order)
+    return call(kernel, shape, [VMEM] * (3 + len(wides)), "blur_yz")(*wides, tables[0], *tables[2:4])
+
+
+def adjoint_planes(blurred_of, image_of, ya_ref, zhi_ref, zlo_ref, order, out_ref, edge_refs):
     planes, rows, _ = out_ref.shape
-    near = yf_ref.shape[1]
-    step = 4
-    for start in range(0, planes, step):
-        block = range(start, min(start + step, planes))
-        blurred = jnp.concatenate(
-            [spread_y(yf_ref[order], jnp.concatenate([ref[p] for ref in wide_refs], axis=0)) for p in block], axis=0
-        )
-        blurred = spread_z(blurred, zhi_ref, zlo_ref, order)
-        image = jnp.concatenate([fetch(p) for p in block], axis=0)
+    for block in plane_blocks(planes):
+        blurred = blurred_of(block)
+        image = jnp.concatenate([image_of(p) for p in block], axis=0)
         ratio = jnp.where(image >= 0, image / blurred, jnp.ones_like(image))
+        near = ratio.shape[0] // len(block)
         spread = jnp.concatenate(
             [spread_y(ya_ref[order], ratio[k * near:(k + 1) * near]) for k in range(len(block))], axis=0
         )
@@ -378,30 +379,26 @@
     put_edges(out_ref, edge_refs)
 
 
-def first_ratio_kernel(shift_ref, far_ref, near_ref, own_ref, *refs, order, wides, extent_x, cells_y):
-    refs, image_ref, (planes_ref, mask_ref, semaphores) = refs[:-4], refs[-4], refs[-3:]
+def first_ratio_kernel(
+    shift_ref, far_ref, near_ref, own_ref, blurred_ref, ya_ref, zhi_ref, zlo_ref, out_ref, *refs, order, extent_x, cells_y
+):
+    edge_refs, image_ref, (mine_ref, beyond_ref, semaphores) = refs[:-4], refs[-4], refs[-3:]
     planes, near, cells_z = image_ref.shape
     side = half()
     slab = lax.axis_index("tile") - side + core()
     shift_x, shift_y, shift_z = (shift_ref[order, i] for i in range(3))
     lanes = pad_to(cells_y, 128)
     pick = iota((near, lanes), 1) == global_row(side, iota((near, lanes), 0), cells_y)
-
-    def copy(ref, index, p):
-        return pltpu.make_async_copy(ref.at[index], planes_ref.at[p], semaphores.at[p])
-
-    mask_copy = pltpu.make_async_copy(own_ref.at[planes, pl.ds(0, planes)], mask_ref, semaphores.at[planes])
-    mask_copy.start()
-    for p in range(planes):
-        source = p + shift_x
-        is_own = (source >= 0) & (source < planes)
-        is_far = (source < 0) == (core() == 0)
-        beyond = jnp.clip(jnp.where(source < 0, source + planes, source - planes), 0, planes - 1)
-        pl.when(is_own)(copy(own_ref, jnp.clip(source, 0, planes - 1), p).start)
-        pl.when(jnp.logical_not(is_own) & is_far)(copy(far_ref, beyond, p).start)
-        pl.when(jnp.logical_not(is_own) & jnp.logical_not(is_far))(copy(near_ref, beyond, p).start)
-    mask_copy.wait()
-    mask = mask_ref[:, :lanes].astype(BF16)
+    is_far = (shift_x > 0) == (core() == 1)
+    copy = pltpu.make_async_copy(own_ref, mine_ref, semaphores.at[0])
+    far_copy = pltpu.make_async_copy(far_ref.at[pl.ds(0, planes)], beyond_ref, semaphores.at[1])
+    near_copy = pltpu.make_async_copy(near_ref.at[pl.ds(0, planes)], beyond_ref, semaphores.at[1])
+    copy.start()
+    pl.when(is_far)(far_copy.start)
+    pl.when(jnp.logical_not(is_far))(near_copy.start)
+    copy.wait()
+    far_copy.wait()
+    mask = mine_ref[planes, :planes, :lanes].astype(BF16)
     columns = lax.dot_general(
         pick.astype(F32).astype(BF16), mask, (((1,), (1,)), ((), ())), preferred_element_type=F32
     )
@@ -410,46 +407,54 @@
     inside = (row >= 0) & (row < cells_y) & (col >= 0) & (col < cells_z)
 
     def fetch(p):
-        copy(own_ref, 0, p).wait()
-        x = slab * planes + p + shift_x
-        value = planes_ref[p]
+        source = p + shift_x
+        x = slab * planes + source
+        is_own = (source >= 0) & (source < planes)
+        beyond = jnp.clip(jnp.where(source < 0, source + planes, source - planes), 0, planes - 1)
+        value = jnp.where(is_own, mine_ref[jnp.clip(source, 0, planes - 1)], beyond_ref[beyond])
         weight = jnp.broadcast_to(columns[:, p:p + 1], (near, cells_z))
         covered = inside & (weight > 0.5) & (x >= 0) & (x < extent_x)
         value = jnp.where(covered, value, jnp.full_like(value, -1.0))
         image_ref[p] = value
         return value
 
-    ratio_planes(refs[:wides], fetch, *refs[wides:wides + 4], order, refs[wides + 4:])
+    def blurred_of(block):
+        return jnp.concatenate([blurred_ref[p] for p in block], axis=0)
+
+    adjoint_planes(blurred_of, fetch, ya_ref, zhi_ref, zlo_ref, order, out_ref, edge_refs)
 
 
 def next_ratio_kernel(image_ref, *refs, order, wides):
-    ratio_planes(refs[:wides], lambda p: image_ref[p], *refs[wides:wides + 4], order, refs[wides + 4:])
-
-
-def ratio_shapes(wides, tables, radius, chunks):
-    planes, _, lanes = wides[0].shape
+    wide_refs, (yf_ref, ya_ref, zhi_ref, zlo_ref, out_ref) = refs[:wides], refs[wides:wides + 5]
+
+    def blurred_of(block):
+        return blurred_planes(wide_refs, yf_ref, zhi_ref, zlo_ref, order, block)
+
+    adjoint_planes(
+        blurred_of, lambda p: image_ref[p], ya_ref, zhi_ref, zlo_ref, order, out_ref, refs[wides + 5:]
+    )
+
+
+def ratio_shapes(planes, lanes, tables, radius, chunks):
     return edge_shapes((planes, tables[1].shape[1], lanes), radius, chunks)
 
 
-def first_ratio(shifts, blocks, wides, tables, order, radius, chunks, extent_x, cells_y):
-    planes, _, lanes = wides[0].shape
-    kernel = functools.partial(
-        first_ratio_kernel, order=order, wides=len(wides), extent_x=extent_x, cells_y=cells_y
-    )
-    image = jax.ShapeDtypeStruct((planes, tables[0].shape[1], lanes), F32)
-    out_shape = ratio_shapes(wides, tables, radius, chunks) + (image,)
+def first_ratio(shifts, blocks, blurred, tables, order, radius, chunks, extent_x, cells_y):
+    planes, near, lanes = blurred.shape
+    kernel = functools.partial(first_ratio_kernel, order=order, extent_x=extent_x, cells_y=cells_y)
+    out_shape = ratio_shapes(planes, lanes, tables, radius, chunks) + (jax.ShapeDtypeStruct(blurred.shape, F32),)
     scratch = [
-        pltpu.VMEM(image.shape, F32), pltpu.VMEM((planes, lanes), F32), pltpu.SemaphoreType.DMA((planes + 1,))
+        pltpu.VMEM((planes + 1, near, lanes), F32), pltpu.VMEM(blurred.shape, F32), pltpu.SemaphoreType.DMA((2,))
     ]
-    in_specs = [SMEM] + [pl.BlockSpec(memory_space=pl.ANY)] * 3 + [VMEM] * (4 + len(wides))
-    return call(kernel, out_shape, in_specs, "image_and_ratio", scratch)(shifts, *blocks, *wides, *tables[:4])
+    in_specs = [SMEM] + [pl.BlockSpec(memory_space=pl.ANY)] * 3 + [VMEM] * 4
+    return call(kernel, out_shape, in_specs, "image_and_ratio", scratch)(shifts, *blocks, blurred, *tables[1:4])
 
 
 def next_ratio(image, wides, tables, order, radius, chunks):
+    planes, _, lanes = image.shape
     kernel = functools.partial(next_ratio_kernel, order=order, wides=len(wides))
-    return call(kernel, ratio_shapes(wides, tables, radius, chunks), [VMEM] * (5 + len(wides)), "ratio")(
-        image, *wides, *tables[:4]
-    )
+    out_shape = ratio_shapes(planes, lanes, tables, radius, chunks)
+    return call(kernel, out_shape, [VMEM] * (5 + len(wides)), "ratio")(image, *wides, *tables[:4])
 
 
 def factor_kernel(hi_ref, lo_ref, before_ref, far_ref, near_ref, own_ref, out_ref, *, order, starts, share):
@@ -458,11 +463,12 @@
 
     def body(step, carry):
         row = pl.multiple_of(step * 8, 8)
-        total = before_ref[:, pl.ds(pl.multiple_of(starts[0] + row, 8), 8), :]
+        total = gather(before_ref, starts[0] + row)
         if share:
             total = share * jnp.log(total)
-        own = gather(own_ref, pl.multiple_of(starts[1] + row, 8))
-        blocks = [[own, gather(near_ref, row)], [gather(far_ref, row)]]
+        own = gather(own_ref, starts[1] + row)
+        edge_row = starts[2] + row
+        blocks = [[own, gather(near_ref, edge_row)], [gather(far_ref, edge_row)]]
         factor = spread_x(hi_ref, lo_ref, 1, band_rows, slice(None), blocks)
         out_ref[:, pl.ds(row, 8), :] = total + jnp.log(factor)
         return carry
@@ -470,10 +476,10 @@
     lax.fori_loop(0, rows // 8, body, 0)
 
 
-def log_factor(tables, before, side, order, before_start, own_start, share):
+def log_factor(tables, before, side, order, rows, starts, share):
     far, near, own = side
-    kernel = functools.partial(factor_kernel, order=order, starts=(before_start, own_start), share=share)
-    shape = jax.ShapeDtypeStruct((own.shape[0],) + far.shape[1:], F32)
+    kernel = functools.partial(factor_kernel, order=order, starts=starts, share=share)
+    shape = jax.ShapeDtypeStruct((own.shape[0], rows, own.shape[2]), F32)
     return call(kernel, shape, [VMEM] * 6, "log_factor")(*tables[4:], before, far, near, own)
 
 
@@ -563,15 +569,11 @@
     def neighbours(far, near):
         return send(far, to_far), send(near, to_core_partner)
 
-    window, crossing = make_windows(estimate, wide)
-    piece = lax.dynamic_slice_in_dim(crossing, group * (planes // groups), planes // groups, 0)
-    piece = send(piece, across(0, lambda r: 1 - r, when=lambda c, r: c == r))
+    window, crossed = make_windows(estimate, wide)
+    crossed = send(crossed, across(0, lambda r: 1 - r, when=lambda c, r: c == r))
 
     acquired = after(acquired, window)
     first, second = shift_and_cut(offsets, acquired[0], view_mask[0], near)
-    piece = after(piece, first)
-    arrived = send(first, lambda g, c, q, r: (g, r, q, c) if c != r else None)
-
     mine = [jnp.pad(row, ((0, 0), (0, 128 - row.shape[1]))) for row in (kern_x, kern_y, kern_z, offsets.astype(F32))]
     mine = jnp.concatenate(mine, axis=1)
     other = send(mine, to_core_partner)
@@ -580,44 +582,44 @@
     shifts = jnp.where(straight, jnp.concatenate([mine, other]), jnp.concatenate([other, mine]))
     shifts = shifts[:, 384:384 + offsets.shape[1]].astype(jnp.int32)
 
-    start = group * (planes // groups)
-    share = jnp.where(straight, lax.dynamic_slice_in_dim(window, start, planes // groups, 0), piece)
-    later = after(after(piece, tables[0]), share)
-    share = send(share, to_far)
-    pieces = [piece] + [send(later, across(turn, when=lambda c, r: c != r)) for turn in range(1, groups)]
-    current, _, close = assemble(after(window, share), pieces, radius)
-    second = after(second, current)
-    second = send(second, lambda g, c, q, r: (g, r, q, 1 - c))
-    distant = assemble_far([share] + [send(share, across(turn)) for turn in range(1, groups)])
-    chunks = [(distant, blur_near(tables, current, after(send(close, to_core_partner), distant)))]
+    arrived = send(after(first, tables[0]), lambda g, c, q, r: (g, r, q, c) if c != r else None)
+    current, distant, close = choose(after(window, first), crossed, radius)
+    second = send(after(second, current), lambda g, c, q, r: (g, r, q, 1 - c))
+    distant, close = neighbours(distant, close)
+    chunks = [(distant, blur_near(tables, current, close))]
     first = jnp.where(straight, first, arrived)
-    second = after(second, chunks[0][1][0])
     blocks = [(*neighbours(block, block), block) for block in (first, second)]
     images = [None, None]
 
     sizes = [[own_rows], [inner_rows, edge_rows]]
 
     for step in range(ITERS):
+        last = step == ITERS - 1
+        if last:
+            sizes = [[own_rows], [own_rows]]
         wides = []
         for distant, parts in chunks:
             distant = after(distant, wides[-1][0]) if wides else distant
-            wides.append(blur_far(tables, distant, parts, radius))
+            wides.append(blur_far(tables, distant, parts))
         sides = []
+        if step == 0:
+            blurred = [blur_yz([chunk[order] for chunk in wides], tables, order) for order in range(2)]
         for order in range(2):
-            parts = [chunk[order] for chunk in wides]
             if step == 0:
                 spread, *edges, images[order] = first_ratio(
-                    shifts, blocks[order], parts, tables, order, radius, sizes[order], planes * slabs, cells_y
+                    shifts, blocks[order], blurred[order], tables, order, radius, sizes[order], planes * slabs, cells_y
                 )
             else:
+                parts = [chunk[order] for chunk in wides]
                 spread, *edges = next_ratio(images[order], parts, tables, order, radius, sizes[order])
             sides += [(*neighbours(*edges[k:k + 2]), spread) for k in range(0, len(edges), 2)]
 
-        total = log_factor(tables, current, sides[0], 0, 0, 0, 1.0 / groups)
-        edge = log_factor(tables, after(total, sides[1][1]), sides[2], 1, inner_rows, inner_rows, 0)
-        inner = log_factor(tables, total, sides[1], 1, 0, 0, 0)
-
-        if step < ITERS - 1:
+        total = log_factor(tables, current, sides[0], 0, own_rows, (0, 0, 0), 1.0 / groups)
+        starts = (inner_rows, inner_rows, inner_rows if last else 0)
+        edge = log_factor(tables, total, sides[-1], 1, edge_rows, starts, 0)
+        inner = log_factor(tables, total, sides[1], 1, inner_rows, (0, 0, 0), 0)
+
+        if not last:
             edge_parts = [edge] + [send(edge, across(turn)) for turn in range(1, groups)]
             inner_parts = [inner] + [send(inner, across(turn)) for turn in range(1, groups)]
             edge = jnp.exp(sum(edge_parts[1:], edge_parts[0]))

time: 218 us -> 220 us (level)
  waiting for transfers between devices: 73 us -> 95.1 us
  starting transfers between devices: 71.6 us -> 60.2 us
  Pallas kernels: 60 us -> 54 us
    ppermute x39 -> x35, waiting for transfers between devices: 73 us -> 95.1 us  [send(): return lax.ppermute(array, AXES, moves(move))]
    ppermute x39 -> x35, starting transfers between devices: 71.6 us -> 60.2 us  [send(): return lax.ppermute(array, AXES, moves(move))]
    pallas_call x2, Pallas kernels: 15.8 us -> 6.42 us  [first_ratio(): call(kernel, out_shape, in_specs, 'image_and_ratio', scratch)]
    unnamed x30 -> x26, local copies, waits for them, and re-layouts: 5.63 us -> 3.79 us
    pallas_call x7 -> x8, Pallas kernels: 17.8 us -> 19.4 us  [the longest x2 7.49 us: next_ratio(): call(kernel, out_shape, [VMEM] * (5 + len(wides)), 'ratio')]
  transfers between devices with their start and end apart: 39 -> 35, of which waited for: 17 -> 19; matrix products, arithmetic and copies ran while one was open for 2% -> 2% of each run, Pallas kernels for 24% -> 21%
where the time goes in v7:
time: 220 us; the launch traced here: 218 us
  waiting for transfers between devices  95.1 us (43%)
  starting transfers between devices  60.2 us (27%)
  Pallas kernels  54 us (25%)
  local copies, waits for them, and re-layouts  5.2 us (2%)
  other arithmetic  3.1 us (1%)
    ppermute x35, waiting for transfers between devices, send(): return lax.ppermute(array, AXES, moves(move))  95.1 us
    ppermute x35, starting transfers between devices, send(): return lax.ppermute(array, AXES, moves(move))  60.2 us
    pallas_call x3, Pallas kernels, blur_near(): call(blur_near_kernel, (shape, shape), [VMEM] * 4, 'blur_x_near')  9.1 us
    pallas_call x6, Pallas kernels, log_factor(): call(kernel, shape, [VMEM] * 6, 'log_factor')  8.65 us
    pallas_call x2, Pallas kernels, next_ratio(): call(kernel, out_shape, [VMEM] * (5 + len(wides)), 'ratio')  7.49 us
    pallas_call x3, Pallas kernels, blur_far(): call(blur_far_kernel, (shape, shape), [VMEM] * 5, 'blur_x_far')  7.36 us
    pallas_call x2, Pallas kernels, first_ratio(): call(kernel, out_shape, in_specs, 'image_and_ratio', scratch)  6.42 us
    pallas_call x1, Pallas kernels, shift_and_cut(): call(shift_kernel, (shape, shape), [SMEM, VMEM, VMEM], 'shift_recorded',...  4.54 us
  transfers between devices with their start and end apart: 35, of which 19 were waited for; matrix products, arithmetic and copies ran while one was open for 2% of the time, Pallas kernels for 21%

profile of v7, /device:TPU:17, one launch (start us, length us, event | category | flops | bytes accessed | tf_op | source)
XLA Modules:
  0.0 218.3 jit_solution(7819932556838775548)
XLA Ops:
  0.0 1.7 copy-done.1
  5.3 3.0 %collective-permute-start = (f32[1,512]{1,0:T(1,128)S(1)}, f32[1,512]{1,0:T(1,128)S(1)}, u32[]{:S(2)}, u32[]{:S(2)}) collective-permute-start(f32[1,512]{1,0:T(1,128)S(1)} %pad_maximum_fusion.mine_ref), channel_id=1, source_target_pairs={{0,8},{1,9},{2,10},{3,11},{4,12},{5,13},{6,14},{7,15},{8,0},{9,1},... | collective-permute-start | bytes 6152 | tf_op jit(solution)/shard_map/ppermute | solution.py:33
  8.2 4.5 %shift_recorded.1 = (f32[17,80,256]{2,1,0:T(8,128)}, f32[17,80,256]{2,1,0:T(8,128)}) custom-call(s32[1,3]{1,0:T(1,128)S(1)} %copy-done.10, f32[16,128,256]{2,1,0:T(8,128)S(1)} %bitcast.2, s32[16,128]{1,0:T(8,128)S(1)} %bitcast.3), custom_call_target="tpu_custom_call" | custom-call | tf_op jit(solution)/shard_map/shift_recorded/pallas_call | solution.py:262
  15.0 1.9 collective-permute-start.2
  16.9 9.3 %collective-permute-done.1.crossed_ref = f32[16,96,256]{2,1,0:T(8,128)S(1)} collective-permute-done((f32[16,96,256]{2,1,0:T(8,128)S(1)}, f32[16,96,256]{2,1,0:T(8,128)S(1)}, u32[]{:S(2)}, u32[]{:S(2)}) %collective-permute-start.1) | collective-permute-done | bytes 1572896 | tf_op jit(solution)/shard_map/ppermute | solution.py:33
  28.7 3.8 %collective-permute-start.6 = (f32[15,96,256]{2,1,0:T(8,128)}, f32[15,96,256]{2,1,0:T(8,128)}, u32[]{:S(2)}, u32[]{:S(2)}) collective-permute-start(f32[15,96,256]{2,1,0:T(8,128)} %get-tuple-element.66), channel_id=1, source_target_pairs={{0,8},{1,9},{2,10},{3,11},{4,12},{5,13},{6,14},{7,15},{8,0},{9,1},... | collective-permute-start | bytes 4423688 | tf_op jit(solution)/shard_map/ppermute | solution.py:33
  32.5 5.6 %collective-permute-start.5 = (f32[15,96,256]{2,1,0:T(8,128)}, f32[15,96,256]{2,1,0:T(8,128)S(1)}, u32[]{:S(2)}, u32[]{:S(2)}) collective-permute-start(f32[15,96,256]{2,1,0:T(8,128)} %copy-done.11), channel_id=1, source_target_pairs={{2,8},{3,9},{4,10},{5,11},{6,12},{7,13},{8,2},{9,3},{10,4},{11,5},... | collective-permute-start | bytes 4423688 | tf_op jit(solution)/shard_map/ppermute | solution.py:33
  38.1 3.0 %collective-permute-done.2 = f32[17,80,256]{2,1,0:T(8,128)} collective-permute-done((f32[17,80,256]{2,1,0:T(8,128)}, f32[17,80,256]{2,1,0:T(8,128)}, u32[]{:S(2)}, u32[]{:S(2)}) %collective-permute-start.2) | collective-permute-done | bytes 1392672 | tf_op jit(solution)/shard_map/ppermute | solution.py:33
  42.7 1.9 collective-permute-start.3
  45.2 8.0 %collective-permute-done.9.own_ref = f32[17,80,256]{2,1,0:T(8,128)} collective-permute-done((f32[17,80,256]{2,1,0:T(8,128)}, f32[17,80,256]{2,1,0:T(8,128)}, u32[]{:S(2)}, u32[]{:S(2)}) %collective-permute-start.9) | collective-permute-done | bytes 1392672 | tf_op jit(solution)/shard_map/ppermute | solution.py:33
  53.3 3.8 %collective-permute-start.10 = (f32[17,80,256]{2,1,0:T(8,128)}, f32[17,80,256]{2,1,0:T(8,128)S(1)}, u32[]{:S(2)}, u32[]{:S(2)}) collective-permute-start(f32[17,80,256]{2,1,0:T(8,128)} %collective-permute-done.9.own_ref), channel_id=1, source_target_pairs={{2,8},{3,9},{4,10},{5,11},{6,12},{7,13},{8,2},{9,3},{10,4},{11,5},... | collective-permute-start | bytes 4177928 | tf_op jit(solution)/shard_map/ppermute | solution.py:33
  57.1 4.6 %blur_x_near.3 = (f32[16,96,256]{2,1,0:T(8,128)S(1)}, f32[16,96,256]{2,1,0:T(8,128)S(1)}) custom-call(bf16[2,256,384]{2,1,0:T(8,128)(2,1)S(1)} %get-tuple-element.55.hi_ref, bf16[2,256,384]{2,1,0:T(8,128)(2,1)S(1)} %get-tuple-element.56.lo_ref, f32[16,96,256]{2,1,0:T(8,128)S(1)} %get-tuple-element.62.own_ref.before_ref, ...), custom_call_target="tpu_custom_call" | custom-call | tf_op jit(solution)/shard_map/blur_x_near/pallas_call | solution.py:318
  61.8 3.1 %blur_x_far.3 = (f32[16,96,256]{2,1,0:T(8,128)S(1)}, f32[16,96,256]{2,1,0:T(8,128)S(1)}) custom-call(bf16[2,256,384]{2,1,0:T(8,128)(2,1)S(1)} %get-tuple-element.55.hi_ref, bf16[2,256,384]{2,1,0:T(8,128)(2,1)S(1)} %get-tuple-element.56.lo_ref, f32[15,96,256]{2,1,0:T(8,128)S(1)} %collective-permute-done.5.far_ref, ...), custom_call_target="tpu_custom_call" | custom-call | tf_op jit(solution)/shard_map/blur_x_far/pallas_call | solution.py:323
  66.5 4.1 %collective-permute-done.3.far_ref = f32[17,80,256]{2,1,0:T(8,128)S(1)} collective-permute-done((f32[17,80,256]{2,1,0:T(8,128)S(1)}, f32[17,80,256]{2,1,0:T(8,128)S(1)}, u32[]{:S(2)}, u32[]{:S(2)}) %collective-permute-start.3) | collective-permute-done | bytes 1392672 | tf_op jit(solution)/shard_map/ppermute | solution.py:33
  70.6 2.7 %image_and_ratio.2 = (f32[16,64,256]{2,1,0:T(8,128)S(1)}, f32[15,64,256]{2,1,0:T(8,128)S(1)}, f32[15,64,256]{2,1,0:T(8,128)S(1)}, f32[16,80,256]{2,1,0:T(8,128)S(1)}) custom-call(s32[2,3]{1,0:T(2,128)S(1)} %fusion.1.shift_ref, f32[17,80,256]{2,1,0:T(8,128)S(1)} %collective-permute-done.3.far_ref, f32[17,80,256]{2,1,0:T(8,128)S(1)} %collective-permute-done.4.near_ref, ...), custom_call_target="tpu_custom_call" | custom-call | tf_op jit(solution)/shard_map/image_and_ratio/pallas_call | solution.py:450
  73.3 3.3 %collective-permute-start.7 = (f32[15,64,256]{2,1,0:T(8,128)S(1)}, f32[15,64,256]{2,1,0:T(8,128)S(1)}, u32[]{:S(2)}, u32[]{:S(2)}) collective-permute-start(f32[15,64,256]{2,1,0:T(8,128)S(1)} %get-tuple-element.73), channel_id=1, source_target_pairs={{2,8},{3,9},{4,10},{5,11},{6,12},{7,13},{8,2},{9,3},{10,4},{11,5},... | collective-permute-start | bytes 2949128 | tf_op jit(solution)/shard_map/ppermute | solution.py:33
  78.3 7.2 %collective-permute-done.10.far_ref = f32[17,80,256]{2,1,0:T(8,128)S(1)} collective-permute-done((f32[17,80,256]{2,1,0:T(8,128)}, f32[17,80,256]{2,1,0:T(8,128)S(1)}, u32[]{:S(2)}, u32[]{:S(2)}) %collective-permute-start.10) | collective-permute-done | bytes 1392672 | tf_op jit(solution)/shard_map/ppermute | solution.py:33
  85.5 3.7 %image_and_ratio.3 = (f32[16,64,256]{2,1,0:T(8,128)S(1)}, f32[15,32,256]{2,1,0:T(8,128)S(1)}, f32[15,32,256]{2,1,0:T(8,128)S(1)}, f32[15,32,256]{2,1,0:T(8,128)S...) custom-call(s32[2,3]{1,0:T(2,128)S(1)} %fusion.1.shift_ref, ...), custom_call_target="tpu_custom_call" | custom-call | tf_op jit(solution)/shard_map/image_and_ratio/pallas_call | solution.py:450
  89.2 3.3 %collective-permute-start.15 = (f32[15,32,256]{2,1,0:T(8,128)S(1)}, f32[15,32,256]{2,1,0:T(8,128)S(1)}, u32[]{:S(2)}, u32[]{:S(2)}) collective-permute-start(f32[15,32,256]{2,1,0:T(8,128)S(1)} %get-tuple-element.82), channel_id=1, source_target_pairs={{2,8},{3,9},{4,10},{5,11},{6,12},{7,13},{8,2},{9,3},{10,4},{11,5},... | collective-permute-start | bytes 1474568 | tf_op jit(solution)/shard_map/ppermute | solution.py:33
  92.7 2.2 %collective-permute-start.12 = (f32[15,32,256]{2,1,0:T(8,128)S(1)}, f32[15,32,256]{2,1,0:T(8,128)S(1)}, u32[]{:S(2)}, u32[]{:S(2)}) collective-permute-start(f32[15,32,256]{2,1,0:T(8,128)S(1)} %get-tuple-element.79), channel_id=1, source_target_pairs={{2,8},{3,9},{4,10},{5,11},{6,12},{7,13},{8,2},{9,3},{10,4},{11,5},... | collective-permute-start | bytes 1474568 | tf_op jit(solution)/shard_map/ppermute | solution.py:33
  96.3 2.2 log_factor.6.before_ref
  98.5 2.8 %collective-permute-done.15.far_ref = f32[15,32,256]{2,1,0:T(8,128)S(1)} collective-permute-done((f32[15,32,256]{2,1,0:T(8,128)S(1)}, f32[15,32,256]{2,1,0:T(8,128)S(1)}, u32[]{:S(2)}, u32[]{:S(2)}) %collective-permute-start.15) | collective-permute-done | bytes 491552 | tf_op jit(solution)/shard_map/ppermute | solution.py:33
  103.6 2.9 %collective-permute-done.12.far_ref = f32[15,32,256]{2,1,0:T(8,128)S(1)} collective-permute-done((f32[15,32,256]{2,1,0:T(8,128)S(1)}, f32[15,32,256]{2,1,0:T(8,128)S(1)}, u32[]{:S(2)}, u32[]{:S(2)}) %collective-permute-start.12) | collective-permute-done | bytes 491552 | tf_op jit(solution)/shard_map/ppermute | solution.py:33
  108.9 6.8 %collective-permute-done.17 = f32[16,32,256]{2,1,0:T(8,128)S(1)} collective-permute-done((f32[16,32,256]{2,1,0:T(8,128)S(1)}, f32[16,32,256]{2,1,0:T(8,128)S(1)}, u32[]{:S(2)}, u32[]{:S(2)}) %collective-permute-start.17) | collective-permute-done | bytes 524320 | tf_op jit(solution)/shard_map/ppermute | solution.py:33
  116.9 10.0 %collective-permute-done.14.refs_1_ = f32[16,32,256]{2,1,0:T(8,128)S(1)} collective-permute-done((f32[16,32,256]{2,1,0:T(8,128)S(1)}, f32[16,32,256]{2,1,0:T(8,128)S(1)}, u32[]{:S(2)}, u32[]{:S(2)}) %collective-permute-start.14) | collective-permute-done | bytes 524320 | tf_op jit(solution)/shard_map/ppermute | solution.py:33
  126.9 2.5 %update.1 = (f32[16,64,256]{2,1,0:T(8,128)S(1)}, f32[15,64,256]{2,1,0:T(8,128)}, f32[15,64,256]{2,1,0:T(8,128)}) custom-call(f32[16,32,256]{2,1,0:T(8,128)S(1)} %log_factor.7.refs_0_, f32[16,32,256]{2,1,0:T(8,128)S(1)} %collective-permute-done.14.refs_1_, f32[16,32,256]{2,1,0:T(8,128)} %add_exponential_fusion.refs_2_), custom_call_target="tpu_custom_call" | custom-call | tf_op jit(solution)/shard_map/update/pallas_call | solution.py:500
  130.6 1.9 collective-permute-start.18
  132.6 3.8 %collective-permute-start.21 = (f32[15,32,256]{2,1,0:T(8,128)S(1)}, f32[15,32,256]{2,1,0:T(8,128)S(1)}, u32[]{:S(2)}, u32[]{:S(2)}) collective-permute-start(f32[15,32,256]{2,1,0:T(8,128)S(1)} %get-tuple-element.106), channel_id=1, source_target_pairs={{2,8},{3,9},{4,10},{5,11},{6,12},{7,13},{8,2},{9,3},{10,4},{11,5},... | collective-permute-start | bytes 1474568 | tf_op jit(solution)/shard_map/ppermute | solution.py:33
  136.5 3.4 %blur_x_near.4 = (f32[16,64,256]{2,1,0:T(8,128)S(1)}, f32[16,64,256]{2,1,0:T(8,128)S(1)}) custom-call(bf16[2,256,384]{2,1,0:T(8,128)(2,1)S(1)} %get-tuple-element.55.hi_ref, bf16[2,256,384]{2,1,0:T(8,128)(2,1)S(1)} %get-tuple-element.56.lo_ref, f32[16,64,256]{2,1,0:T(8,128)S(1)} %get-tuple-element.84.own_ref.before_ref, ...), custom_call_target="tpu_custom_call" | custom-call | tf_op jit(solution)/shard_map/blur_x_near/pallas_call | solution.py:318
  139.9 6.6 %collective-permute-done.18.far_ref = f32[15,64,256]{2,1,0:T(8,128)} collective-permute-done((f32[15,64,256]{2,1,0:T(8,128)}, f32[15,64,256]{2,1,0:T(8,128)}, u32[]{:S(2)}, u32[]{:S(2)}) %collective-permute-start.18) | collective-permute-done | bytes 983072 | tf_op jit(solution)/shard_map/ppermute | solution.py:33
  146.5 3.2 %blur_x_far.4 = (f32[16,64,256]{2,1,0:T(8,128)S(1)}, f32[16,64,256]{2,1,0:T(8,128)S(1)}) custom-call(bf16[2,256,384]{2,1,0:T(8,128)(2,1)S(1)} %get-tuple-element.55.hi_ref, bf16[2,256,384]{2,1,0:T(8,128)(2,1)S(1)} %get-tuple-element.56.lo_ref, f32[15,64,256]{2,1,0:T(8,128)} %collective-permute-done.18.far_ref, ...), custom_call_target="tpu_custom_call" | custom-call | tf_op jit(solution)/shard_map/blur_x_far/pallas_call | solution.py:323
  149.7 1.7 collective-permute-done.21.far_ref
  153.9 3.7 %ratio.2 = (f32[16,64,256]{2,1,0:T(8,128)S(1)}, f32[15,64,256]{2,1,0:T(8,128)S(1)}, f32[15,64,256]{2,1,0:T(8,128)S(1)}) custom-call(f32[16,80,256]{2,1,0:T(8,128)S(1)} %copy-done.3, f32[16,64,256]{2,1,0:T(8,128)S(1)} %get-tuple-element.90.refs_0_, f32[16,32,256]{2,1,0:T(8,128)S(1)} %get-tuple-element.95.refs_1_, ...), custom_call_target="tpu_custom_call" | custom-call | tf_op jit(solution)/shard_map/ratio/pallas_call | solution.py:457
  157.6 1.9 collective-permute-start.23
  160.2 3.7 %ratio.3 = (f32[16,64,256]{2,1,0:T(8,128)S(1)}, f32[15,64,256]{2,1,0:T(8,128)S(1)}, f32[15,64,256]{2,1,0:T(8,128)S(1)}) custom-call(f32[16,80,256]{2,1,0:T(8,128)S(1)} %copy-done.5, f32[16,64,256]{2,1,0:T(8,128)S(1)} %get-tuple-element.100.refs_0_, f32[16,32,256]{2,1,0:T(8,128)S(1)} %get-tuple-element.101.refs_1_, ...), custom_call_target="tpu_custom_call" | custom-call | tf_op jit(solution)/shard_map/ratio/pallas_call | solution.py:457
  163.9 3.1 %collective-permute-start.25 = (f32[15,64,256]{2,1,0:T(8,128)S(1)}, f32[15,64,256]{2,1,0:T(8,128)S(1)}, u32[]{:S(2)}, u32[]{:S(2)}) collective-permute-start(f32[15,64,256]{2,1,0:T(8,128)S(1)} %get-tuple-element.102), channel_id=1, source_target_pairs={{2,8},{3,9},{4,10},{5,11},{6,12},{7,13},{8,2},{9,3},{10,4},{11,5},... | collective-permute-start | bytes 2949128 | tf_op jit(solution)/shard_map/ppermute | solution.py:33
  167.1 6.2 %collective-permute-done.23.far_ref = f32[15,64,256]{2,1,0:T(8,128)S(1)} collective-permute-done((f32[15,64,256]{2,1,0:T(8,128)S(1)}, f32[15,64,256]{2,1,0:T(8,128)S(1)}, u32[]{:S(2)}, u32[]{:S(2)}) %collective-permute-start.23) | collective-permute-done | bytes 983072 | tf_op jit(solution)/shard_map/ppermute | solution.py:33
  173.3 2.2 log_factor.9.before_ref
  175.5 8.1 %collective-permute-done.25.far_ref = f32[15,64,256]{2,1,0:T(8,128)S(1)} collective-permute-done((f32[15,64,256]{2,1,0:T(8,128)S(1)}, f32[15,64,256]{2,1,0:T(8,128)S(1)}, u32[]{:S(2)}, u32[]{:S(2)}) %collective-permute-start.25) | collective-permute-done | bytes 983072 | tf_op jit(solution)/shard_map/ppermute | solution.py:33
  185.3 3.0 %collective-permute-start.28 = (f32[16,32,256]{2,1,0:T(8,128)S(1)}, f32[16,32,256]{2,1,0:T(8,128)S(1)}, u32[]{:S(2)}, u32[]{:S(2)}) collective-permute-start(f32[16,32,256]{2,1,0:T(8,128)S(1)} %log_factor.10.refs_0_), channel_id=1, source_target_pairs={{1,24},{3,26},{5,28},{7,30},{8,17},{10,19},{12,21},{14,23},{17,8},... | collective-permute-start | bytes 1572872 | tf_op jit(solution)/shard_map/ppermute | solution.py:33
  188.3 3.5 %collective-permute-start.29 = (f32[16,32,256]{2,1,0:T(8,128)S(1)}, f32[16,32,256]{2,1,0:T(8,128)S(1)}, u32[]{:S(2)}, u32[]{:S(2)}) collective-permute-start(f32[16,32,256]{2,1,0:T(8,128)S(1)} %log_factor.10.refs_0_), channel_id=1, source_target_pairs={{1,8},{3,10},{5,12},{7,14},{8,1},{10,3},{12,5},{14,7},{17,24},{19,... | collective-permute-start | bytes 1572872 | tf_op jit(solution)/shard_map/ppermute | solution.py:33
  193.6 2.0 collective-permute-start.32
  195.7 3.5 %collective-permute-start.33 = (f32[16,32,256]{2,1,0:T(8,128)S(1)}, f32[16,32,256]{2,1,0:T(8,128)S(1)}, u32[]{:S(2)}, u32[]{:S(2)}) collective-permute-start(f32[16,32,256]{2,1,0:T(8,128)S(1)} %log_factor.11.refs_0_), channel_id=1, source_target_pairs={{1,8},{3,10},{5,12},{7,14},{8,1},{10,3},{12,5},{14,7},{17,24},{19,... | collective-permute-start | bytes 1572872 | tf_op jit(solution)/shard_map/ppermute | solution.py:33
  199.2 3.2 %collective-permute-done.28.refs_2_ = f32[16,32,256]{2,1,0:T(8,128)S(1)} collective-permute-done((f32[16,32,256]{2,1,0:T(8,128)S(1)}, f32[16,32,256]{2,1,0:T(8,128)S(1)}, u32[]{:S(2)}, u32[]{:S(2)}) %collective-permute-start.28) | collective-permute-done | bytes 524320 | tf_op jit(solution)/shard_map/ppermute | solution.py:33
  202.4 2.3 %collective-permute-done.29.refs_3_ = f32[16,32,256]{2,1,0:T(8,128)S(1)} collective-permute-done((f32[16,32,256]{2,1,0:T(8,128)S(1)}, f32[16,32,256]{2,1,0:T(8,128)S(1)}, u32[]{:S(2)}, u32[]{:S(2)}) %collective-permute-start.29) | collective-permute-done | bytes 524320 | tf_op jit(solution)/shard_map/ppermute | solution.py:33
  204.9 6.6 %collective-permute-done.32.refs_2_ = f32[16,32,256]{2,1,0:T(8,128)S(1)} collective-permute-done((f32[16,32,256]{2,1,0:T(8,128)S(1)}, f32[16,32,256]{2,1,0:T(8,128)S(1)}, u32[]{:S(2)}, u32[]{:S(2)}) %collective-permute-start.32) | collective-permute-done | bytes 524320 | tf_op jit(solution)/shard_map/ppermute | solution.py:33
  211.5 3.2 %collective-permute-done.33.refs_3_ = f32[16,32,256]{2,1,0:T(8,128)S(1)} collective-permute-done((f32[16,32,256]{2,1,0:T(8,128)S(1)}, f32[16,32,256]{2,1,0:T(8,128)S(1)}, u32[]{:S(2)}, u32[]{:S(2)}) %collective-permute-start.33) | collective-permute-done | bytes 524320 | tf_op jit(solution)/shard_map/ppermute | solution.py:33
  214.9 1.9 collective-permute-done.34.refs_3_
  (84 shorter events, 30.7 us)
Async XLA Ops:
  0.0 8.2 %copy-start = (f32[1,16,128,256]{3,2,1,0:T(8,128)S(1)}, f32[1,16,128,256]{3,2,1,0:T(8,128)}, u32[]{:S(2)}) copy-start(f32[1,16,128,256]{3,2,1,0:T(8,128)} %param.7) | copy-start | bytes 6291460
  0.0 1.7 copy-start.1
  1.7 3.5 %copy-start.12 = (f32[1,31]{1,0:T(1,128)S(1)}, f32[1,31]{1,0:T(1,128)}, u32[]{:S(2)}) copy-start(f32[1,31]{1,0:T(1,128)} %param.11) | copy-start | bytes 376
  1.7 6.5 %copy-start.9 = (s32[1,16,128]{2,1,0:T(8,128)S(1)}, s32[1,16,128]{2,1,0:T(8,128)}, u32[]{:S(2)}) copy-start(s32[1,16,128]{2,1,0:T(8,128)} %param.10) | copy-start | bytes 24580
  1.7 6.5 %copy-start.10 = (s32[1,3]{1,0:T(1,128)S(1)}, s32[1,3]{1,0:T(1,128)}, u32[]{:S(2)}) copy-start(s32[1,3]{1,0:T(1,128)} %offsets_ref.1) | copy-start | bytes 40
  2.0 24.2 %collective-permute-start.1 = (f32[16,96,256]{2,1,0:T(8,128)S(1)}, f32[16,96,256]{2,1,0:T(8,128)S(1)}, u32[]{:S(2)}, u32[]{:S(2)}) collective-permute-start(f32[16,96,256]{2,1,0:T(8,128)S(1)} %get-tuple-element.61), channel_id=1, source_target_pairs={{0,1},{2,3},{4,5},{6,7},{9,8},{11,10},{13,12},{15,14},{16,17},{18,... | collective-permute-start | bytes 4718600 | tf_op jit(solution)/shard_map/ppermute | solution.py:33
  5.3 7.5 %collective-permute-start = (f32[1,512]{1,0:T(1,128)S(1)}, f32[1,512]{1,0:T(1,128)S(1)}, u32[]{:S(2)}, u32[]{:S(2)}) collective-permute-start(f32[1,512]{1,0:T(1,128)S(1)} %pad_maximum_fusion.mine_ref), channel_id=1, source_target_pairs={{0,8},{1,9},{2,10},{3,11},{4,12},{5,13},{6,14},{7,15},{8,0},{9,1},... | collective-permute-start | bytes 6152 | tf_op jit(solution)/shard_map/ppermute | solution.py:33
  14.3 0.6 copy-start.6
  15.0 26.2 %collective-permute-start.2 = (f32[17,80,256]{2,1,0:T(8,128)}, f32[17,80,256]{2,1,0:T(8,128)}, u32[]{:S(2)}, u32[]{:S(2)}) collective-permute-start(f32[17,80,256]{2,1,0:T(8,128)} %get-tuple-element.64), channel_id=1, source_target_pairs={{1,8},{3,10},{5,12},{7,14},{8,1},{10,3},{12,5},{14,7},{17,24},{19,... | collective-permute-start | bytes 4177928 | tf_op jit(solution)/shard_map/ppermute | solution.py:33
  27.6 1.1 copy-start.11
  28.7 28.3 %collective-permute-start.6 = (f32[15,96,256]{2,1,0:T(8,128)}, f32[15,96,256]{2,1,0:T(8,128)}, u32[]{:S(2)}, u32[]{:S(2)}) collective-permute-start(f32[15,96,256]{2,1,0:T(8,128)} %get-tuple-element.66), channel_id=1, source_target_pairs={{0,8},{1,9},{2,10},{3,11},{4,12},{5,13},{6,14},{7,15},{8,0},{9,1},... | collective-permute-start | bytes 4423688 | tf_op jit(solution)/shard_map/ppermute | solution.py:33
  32.5 20.7 %collective-permute-start.9 = (f32[17,80,256]{2,1,0:T(8,128)}, f32[17,80,256]{2,1,0:T(8,128)}, u32[]{:S(2)}, u32[]{:S(2)}) collective-permute-start(f32[17,80,256]{2,1,0:T(8,128)} %get-tuple-element.77), channel_id=1, source_target_pairs={{0,1},{1,9},{2,3},{3,11},{4,5},{5,13},{6,7},{7,15},{8,0},{9,8},{10... | collective-permute-start | bytes 4177928 | tf_op jit(solution)/shard_map/ppermute | solution.py:33
  32.5 29.2 %collective-permute-start.5 = (f32[15,96,256]{2,1,0:T(8,128)}, f32[15,96,256]{2,1,0:T(8,128)S(1)}, u32[]{:S(2)}, u32[]{:S(2)}) collective-permute-start(f32[15,96,256]{2,1,0:T(8,128)} %copy-done.11), channel_id=1, source_target_pairs={{2,8},{3,9},{4,10},{5,11},{6,12},{7,13},{8,2},{9,3},{10,4},{11,5},... | collective-permute-start | bytes 4423688 | tf_op jit(solution)/shard_map/ppermute | solution.py:33
  42.7 27.9 %collective-permute-start.3 = (f32[17,80,256]{2,1,0:T(8,128)S(1)}, f32[17,80,256]{2,1,0:T(8,128)S(1)}, u32[]{:S(2)}, u32[]{:S(2)}) collective-permute-start(f32[17,80,256]{2,1,0:T(8,128)S(1)} %broadcast_select_fusion.own_ref), channel_id=1, source_target_pairs={{2,8},{3,9},{4,10},{5,11},{6,12},{7,13},{8,2},{9,3},{10,4},{11,5},... | collective-permute-start | bytes 4177928 | tf_op jit(solution)/shard_map/ppermute | solution.py:33
  44.6 26.0 %collective-permute-start.4 = (f32[17,80,256]{2,1,0:T(8,128)S(1)}, f32[17,80,256]{2,1,0:T(8,128)S(1)}, u32[]{:S(2)}, u32[]{:S(2)}) collective-permute-start(f32[17,80,256]{2,1,0:T(8,128)S(1)} %broadcast_select_fusion.own_ref), channel_id=1, source_target_pairs={{0,8},{1,9},{2,10},{3,11},{4,12},{5,13},{6,14},{7,15},{8,0},{9,1},... | collective-permute-start | bytes 4177928 | tf_op jit(solution)/shard_map/ppermute | solution.py:33
  53.3 32.2 %collective-permute-start.10 = (f32[17,80,256]{2,1,0:T(8,128)}, f32[17,80,256]{2,1,0:T(8,128)S(1)}, u32[]{:S(2)}, u32[]{:S(2)}) collective-permute-start(f32[17,80,256]{2,1,0:T(8,128)} %collective-permute-done.9.own_ref), channel_id=1, source_target_pairs={{2,8},{3,9},{4,10},{5,11},{6,12},{7,13},{8,2},{9,3},{10,4},{11,5},... | collective-permute-start | bytes 4177928 | tf_op jit(solution)/shard_map/ppermute | solution.py:33
  57.0 28.5 %collective-permute-start.11 = (f32[17,80,256]{2,1,0:T(8,128)}, f32[17,80,256]{2,1,0:T(8,128)S(1)}, u32[]{:S(2)}, u32[]{:S(2)}) collective-permute-start(f32[17,80,256]{2,1,0:T(8,128)} %collective-permute-done.9.own_ref), channel_id=1, source_target_pairs={{0,8},{1,9},{2,10},{3,11},{4,12},{5,13},{6,14},{7,15},{8,0},{9,1},... | collective-permute-start | bytes 4177928 | tf_op jit(solution)/shard_map/ppermute | solution.py:33
  64.9 5.7 %copy-start.7 = (bf16[2,64,256]{2,1,0:T(8,128)(2,1)S(1)}, bf16[2,64,256]{2,1,0:T(8,128)(2,1)}, u32[]{:S(2)}) copy-start(bf16[2,64,256]{2,1,0:T(8,128)(2,1)} %copy-done.6) | copy-start | bytes 196612
  73.3 5.0 %copy-start.2 = (f32[16,80,256]{2,1,0:T(8,128)}, f32[16,80,256]{2,1,0:T(8,128)S(1)}, u32[]{:S(2)}) copy-start(f32[16,80,256]{2,1,0:T(8,128)S(1)} %get-tuple-element.85.image_ref) | copy-start | bytes 3932164
  73.3 22.7 %collective-permute-start.7 = (f32[15,64,256]{2,1,0:T(8,128)S(1)}, f32[15,64,256]{2,1,0:T(8,128)S(1)}, u32[]{:S(2)}, u32[]{:S(2)}) collective-permute-start(f32[15,64,256]{2,1,0:T(8,128)S(1)} %get-tuple-element.73), channel_id=1, source_target_pairs={{2,8},{3,9},{4,10},{5,11},{6,12},{7,13},{8,2},{9,3},{10,4},{11,5},... | collective-permute-start | bytes 2949128 | tf_op jit(solution)/shard_map/ppermute | solution.py:33
  76.6 19.7 %collective-permute-start.8 = (f32[15,64,256]{2,1,0:T(8,128)S(1)}, f32[15,64,256]{2,1,0:T(8,128)S(1)}, u32[]{:S(2)}, u32[]{:S(2)}) collective-permute-start(f32[15,64,256]{2,1,0:T(8,128)S(1)} %get-tuple-element.74), channel_id=1, source_target_pairs={{0,8},{1,9},{2,10},{3,11},{4,12},{5,13},{6,14},{7,15},{8,0},{9,1},... | collective-permute-start | bytes 2949128 | tf_op jit(solution)/shard_map/ppermute | solution.py:33
  89.2 9.2 %copy-start.4 = (f32[16,80,256]{2,1,0:T(8,128)}, f32[16,80,256]{2,1,0:T(8,128)S(1)}, u32[]{:S(2)}) copy-start(f32[16,80,256]{2,1,0:T(8,128)S(1)} %get-tuple-element.99.image_ref) | copy-start | bytes 3932164
  89.2 12.0 %collective-permute-start.15 = (f32[15,32,256]{2,1,0:T(8,128)S(1)}, f32[15,32,256]{2,1,0:T(8,128)S(1)}, u32[]{:S(2)}, u32[]{:S(2)}) collective-permute-start(f32[15,32,256]{2,1,0:T(8,128)S(1)} %get-tuple-element.82), channel_id=1, source_target_pairs={{2,8},{3,9},{4,10},{5,11},{6,12},{7,13},{8,2},{9,3},{10,4},{11,5},... | collective-permute-start | bytes 1474568 | tf_op jit(solution)/shard_map/ppermute | solution.py:33
  92.6 8.7 %collective-permute-start.16 = (f32[15,32,256]{2,1,0:T(8,128)S(1)}, f32[15,32,256]{2,1,0:T(8,128)S(1)}, u32[]{:S(2)}, u32[]{:S(2)}) collective-permute-start(f32[15,32,256]{2,1,0:T(8,128)S(1)} %get-tuple-element.83), channel_id=1, source_target_pairs={{0,8},{1,9},{2,10},{3,11},{4,12},{5,13},{6,14},{7,15},{8,0},{9,1},... | collective-permute-start | bytes 1474568 | tf_op jit(solution)/shard_map/ppermute | solution.py:33
  92.7 13.9 %collective-permute-start.12 = (f32[15,32,256]{2,1,0:T(8,128)S(1)}, f32[15,32,256]{2,1,0:T(8,128)S(1)}, u32[]{:S(2)}, u32[]{:S(2)}) collective-permute-start(f32[15,32,256]{2,1,0:T(8,128)S(1)} %get-tuple-element.79), channel_id=1, source_target_pairs={{2,8},{3,9},{4,10},{5,11},{6,12},{7,13},{8,2},{9,3},{10,4},{11,5},... | collective-permute-start | bytes 1474568 | tf_op jit(solution)/shard_map/ppermute | solution.py:33
  96.0 10.5 %collective-permute-start.13 = (f32[15,32,256]{2,1,0:T(8,128)S(1)}, f32[15,32,256]{2,1,0:T(8,128)S(1)}, u32[]{:S(2)}, u32[]{:S(2)}) collective-permute-start(f32[15,32,256]{2,1,0:T(8,128)S(1)} %get-tuple-element.80), channel_id=1, source_target_pairs={{0,8},{1,9},{2,10},{3,11},{4,12},{5,13},{6,14},{7,15},{8,0},{9,1},... | collective-permute-start | bytes 1474568 | tf_op jit(solution)/shard_map/ppermute | solution.py:33
  102.4 13.3 %collective-permute-start.17 = (f32[16,32,256]{2,1,0:T(8,128)S(1)}, f32[16,32,256]{2,1,0:T(8,128)S(1)}, u32[]{:S(2)}, u32[]{:S(2)}) collective-permute-start(f32[16,32,256]{2,1,0:T(8,128)S(1)} %log_factor.8), channel_id=1, source_target_pairs={{0,16},{1,17},{2,18},{3,19},{4,20},{5,21},{6,22},{7,23},{8,24},{9,... | collective-permute-start | bytes 1572872 | tf_op jit(solution)/shard_map/ppermute | solution.py:33
  107.7 19.3 %collective-permute-start.14 = (f32[16,32,256]{2,1,0:T(8,128)S(1)}, f32[16,32,256]{2,1,0:T(8,128)S(1)}, u32[]{:S(2)}, u32[]{:S(2)}) collective-permute-start(f32[16,32,256]{2,1,0:T(8,128)S(1)} %log_factor.7.refs_0_), channel_id=1, source_target_pairs={{0,16},{1,17},{2,18},{3,19},{4,20},{5,21},{6,22},{7,23},{8,24},{9,... | collective-permute-start | bytes 1572872 | tf_op jit(solution)/shard_map/ppermute | solution.py:33
  116.6 15.9 %collective-permute-start.20 = (f32[16,32,256]{2,1,0:T(8,128)}, f32[16,32,256]{2,1,0:T(8,128)S(1)}, u32[]{:S(2)}, u32[]{:S(2)}) collective-permute-start(f32[16,32,256]{2,1,0:T(8,128)} %add_exponential_fusion.refs_2_), channel_id=1, source_target_pairs={{0,1},{1,0},{2,3},{3,2},{4,5},{5,4},{6,7},{7,6},{8,9},{9,8},{10,11... | collective-permute-start | bytes 1572872 | tf_op jit(solution)/shard_map/ppermute | solution.py:33
  129.5 7.0 %collective-permute-start.19 = (f32[15,64,256]{2,1,0:T(8,128)}, f32[15,64,256]{2,1,0:T(8,128)}, u32[]{:S(2)}, u32[]{:S(2)}) collective-permute-start(f32[15,64,256]{2,1,0:T(8,128)} %get-tuple-element.87), channel_id=1, source_target_pairs={{0,8},{1,9},{2,10},{3,11},{4,12},{5,13},{6,14},{7,15},{8,0},{9,1},... | collective-permute-start | bytes 2949128 | tf_op jit(solution)/shard_map/ppermute | solution.py:33
  130.6 15.9 %collective-permute-start.18 = (f32[15,64,256]{2,1,0:T(8,128)}, f32[15,64,256]{2,1,0:T(8,128)}, u32[]{:S(2)}, u32[]{:S(2)}) collective-permute-start(f32[15,64,256]{2,1,0:T(8,128)} %get-tuple-element.86), channel_id=1, source_target_pairs={{2,8},{3,9},{4,10},{5,11},{6,12},{7,13},{8,2},{9,3},{10,4},{11,5},... | collective-permute-start | bytes 2949128 | tf_op jit(solution)/shard_map/ppermute | solution.py:33
  132.6 18.9 %collective-permute-start.21 = (f32[15,32,256]{2,1,0:T(8,128)S(1)}, f32[15,32,256]{2,1,0:T(8,128)S(1)}, u32[]{:S(2)}, u32[]{:S(2)}) collective-permute-start(f32[15,32,256]{2,1,0:T(8,128)S(1)} %get-tuple-element.106), channel_id=1, source_target_pairs={{2,8},{3,9},{4,10},{5,11},{6,12},{7,13},{8,2},{9,3},{10,4},{11,5},... | collective-permute-start | bytes 1474568 | tf_op jit(solution)/shard_map/ppermute | solution.py:33
  136.4 15.0 %collective-permute-start.22 = (f32[15,32,256]{2,1,0:T(8,128)S(1)}, f32[15,32,256]{2,1,0:T(8,128)S(1)}, u32[]{:S(2)}, u32[]{:S(2)}) collective-permute-start(f32[15,32,256]{2,1,0:T(8,128)S(1)} %get-tuple-element.105), channel_id=1, source_target_pairs={{0,8},{1,9},{2,10},{3,11},{4,12},{5,13},{6,14},{7,15},{8,0},{9,1},... | collective-permute-start | bytes 1474568 | tf_op jit(solution)/shard_map/ppermute | solution.py:33
  152.5 1.3 copy-start.3
  152.5 1.3 copy-start.8
  153.9 6.3 %copy-start.5 = (f32[16,80,256]{2,1,0:T(8,128)S(1)}, f32[16,80,256]{2,1,0:T(8,128)}, u32[]{:S(2)}) copy-start(f32[16,80,256]{2,1,0:T(8,128)} %copy-done.4) | copy-start | bytes 3932164
  157.6 15.7 %collective-permute-start.23 = (f32[15,64,256]{2,1,0:T(8,128)S(1)}, f32[15,64,256]{2,1,0:T(8,128)S(1)}, u32[]{:S(2)}, u32[]{:S(2)}) collective-permute-start(f32[15,64,256]{2,1,0:T(8,128)S(1)} %get-tuple-element.96), channel_id=1, source_target_pairs={{2,8},{3,9},{4,10},{5,11},{6,12},{7,13},{8,2},{9,3},{10,4},{11,5},... | collective-permute-start | bytes 2949128 | tf_op jit(solution)/shard_map/ppermute | solution.py:33
  159.5 13.8 %collective-permute-start.24 = (f32[15,64,256]{2,1,0:T(8,128)S(1)}, f32[15,64,256]{2,1,0:T(8,128)S(1)}, u32[]{:S(2)}, u32[]{:S(2)}) collective-permute-start(f32[15,64,256]{2,1,0:T(8,128)S(1)} %get-tuple-element.97), channel_id=1, source_target_pairs={{0,8},{1,9},{2,10},{3,11},{4,12},{5,13},{6,14},{7,15},{8,0},{9,1},... | collective-permute-start | bytes 2949128 | tf_op jit(solution)/shard_map/ppermute | solution.py:33
  163.9 19.6 %collective-permute-start.25 = (f32[15,64,256]{2,1,0:T(8,128)S(1)}, f32[15,64,256]{2,1,0:T(8,128)S(1)}, u32[]{:S(2)}, u32[]{:S(2)}) collective-permute-start(f32[15,64,256]{2,1,0:T(8,128)S(1)} %get-tuple-element.102), channel_id=1, source_target_pairs={{2,8},{3,9},{4,10},{5,11},{6,12},{7,13},{8,2},{9,3},{10,4},{11,5},... | collective-permute-start | bytes 2949128 | tf_op jit(solution)/shard_map/ppermute | solution.py:33
  167.0 16.6 %collective-permute-start.26 = (f32[15,64,256]{2,1,0:T(8,128)S(1)}, f32[15,64,256]{2,1,0:T(8,128)S(1)}, u32[]{:S(2)}, u32[]{:S(2)}) collective-permute-start(f32[15,64,256]{2,1,0:T(8,128)S(1)} %get-tuple-element.103), channel_id=1, source_target_pairs={{0,8},{1,9},{2,10},{3,11},{4,12},{5,13},{6,14},{7,15},{8,0},{9,1},... | collective-permute-start | bytes 2949128 | tf_op jit(solution)/shard_map/ppermute | solution.py:33
  184.6 11.0 %collective-permute-start.27 = (f32[16,32,256]{2,1,0:T(8,128)S(1)}, f32[16,32,256]{2,1,0:T(8,128)S(1)}, u32[]{:S(2)}, u32[]{:S(2)}) collective-permute-start(f32[16,32,256]{2,1,0:T(8,128)S(1)} %log_factor.10.refs_0_), channel_id=1, source_target_pairs={{0,16},{2,18},{4,20},{6,22},{9,25},{11,27},{13,29},{15,31},{16,0},... | collective-permute-start | bytes 1572872 | tf_op jit(solution)/shard_map/ppermute | solution.py:33
  185.3 17.1 %collective-permute-start.28 = (f32[16,32,256]{2,1,0:T(8,128)S(1)}, f32[16,32,256]{2,1,0:T(8,128)S(1)}, u32[]{:S(2)}, u32[]{:S(2)}) collective-permute-start(f32[16,32,256]{2,1,0:T(8,128)S(1)} %log_factor.10.refs_0_), channel_id=1, source_target_pairs={{1,24},{3,26},{5,28},{7,30},{8,17},{10,19},{12,21},{14,23},{17,8},... | collective-permute-start | bytes 1572872 | tf_op jit(solution)/shard_map/ppermute | solution.py:33
  188.3 16.4 %collective-permute-start.29 = (f32[16,32,256]{2,1,0:T(8,128)S(1)}, f32[16,32,256]{2,1,0:T(8,128)S(1)}, u32[]{:S(2)}, u32[]{:S(2)}) collective-permute-start(f32[16,32,256]{2,1,0:T(8,128)S(1)} %log_factor.10.refs_0_), channel_id=1, source_target_pairs={{1,8},{3,10},{5,12},{7,14},{8,1},{10,3},{12,5},{14,7},{17,24},{19,... | collective-permute-start | bytes 1572872 | tf_op jit(solution)/shard_map/ppermute | solution.py:33
  192.9 12.0 %collective-permute-start.31 = (f32[16,32,256]{2,1,0:T(8,128)S(1)}, f32[16,32,256]{2,1,0:T(8,128)S(1)}, u32[]{:S(2)}, u32[]{:S(2)}) collective-permute-start(f32[16,32,256]{2,1,0:T(8,128)S(1)} %log_factor.11.refs_0_), channel_id=1, source_target_pairs={{0,16},{2,18},{4,20},{6,22},{9,25},{11,27},{13,29},{15,31},{16,0},... | collective-permute-start | bytes 1572872 | tf_op jit(solution)/shard_map/ppermute | solution.py:33
  193.6 17.9 %collective-permute-start.32 = (f32[16,32,256]{2,1,0:T(8,128)S(1)}, f32[16,32,256]{2,1,0:T(8,128)S(1)}, u32[]{:S(2)}, u32[]{:S(2)}) collective-permute-start(f32[16,32,256]{2,1,0:T(8,128)S(1)} %log_factor.11.refs_0_), channel_id=1, source_target_pairs={{1,24},{3,26},{5,28},{7,30},{8,17},{10,19},{12,21},{14,23},{17,8},... | collective-permute-start | bytes 1572872 | tf_op jit(solution)/shard_map/ppermute | solution.py:33
  195.7 19.0 %collective-permute-start.33 = (f32[16,32,256]{2,1,0:T(8,128)S(1)}, f32[16,32,256]{2,1,0:T(8,128)S(1)}, u32[]{:S(2)}, u32[]{:S(2)}) collective-permute-start(f32[16,32,256]{2,1,0:T(8,128)S(1)} %log_factor.11.refs_0_), channel_id=1, source_target_pairs={{1,8},{3,10},{5,12},{7,14},{8,1},{10,3},{12,5},{14,7},{17,24},{19,... | collective-permute-start | bytes 1572872 | tf_op jit(solution)/shard_map/ppermute | solution.py:33
  204.8 10.1 %collective-permute-start.30 = (f32[16,32,256]{2,1,0:T(8,128)S(1)}, f32[16,32,256]{2,1,0:T(8,128)S(1)}, u32[]{:S(2)}, u32[]{:S(2)}) collective-permute-start(f32[16,32,256]{2,1,0:T(8,128)S(1)} %last_update.2.refs_0_), channel_id=1, source_target_pairs={{0,8},{1,9},{2,10},{3,11},{4,12},{5,13},{6,14},{7,15},{8,0},{9,1},... | collective-permute-start | bytes 1572872 | tf_op jit(solution)/shard_map/ppermute | solution.py:33
  214.8 2.0 collective-permute-start.34

commit v8 on v7

--- a/solution.py
+++ b/solution.py
@@ -201,20 +201,28 @@
 
 
 def put_edges(out_ref, edge_refs):
-    start = 0
+    end = out_ref.shape[1]
     for far_ref, near_ref in zip(edge_refs[::2], edge_refs[1::2]):
-        radius, rows = far_ref.shape[0], slice(start, start + far_ref.shape[1])
+        radius, rows = far_ref.shape[0], slice(end - far_ref.shape[1], end)
         beyond = out_ref.shape[0] - radius
         for p in range(radius):
             far_ref[p] = out_ref[p + core() * beyond, rows]
             near_ref[p] = out_ref[p + (1 - core()) * beyond, rows]
-        start += far_ref.shape[1]
-
-
-def choose_kernel(window_ref, crossed_ref, out_ref, *edge_refs):
-    straight = core() == half()
-    for p in range(out_ref.shape[0]):
-        out_ref[p] = jnp.where(straight, window_ref[p], crossed_ref[p])
+        end -= far_ref.shape[1]
+
+
+def assemble_kernel(*refs, count):
+    pieces, window, out_ref, edge_refs = refs[:count], refs[count:-1], refs[-1], ()
+    if len(refs) > count + 1:
+        window, out_ref, edge_refs = refs[count], refs[count + 1], refs[count + 2:]
+    straight, group = core() == half(), lax.axis_index("view") // 2
+    planes, share = out_ref.shape[0], pieces[0].shape[0]
+    for p in range(planes):
+        turn = lax.rem(group - p // share + count, count)
+        value = pieces[0][p % share]
+        for k in range(1, count):
+            value = jnp.where(turn == k, pieces[k][p % share], value)
+        out_ref[p] = jnp.where(straight, window[p], value) if edge_refs else value
     put_edges(out_ref, edge_refs)
 
 
@@ -224,9 +232,17 @@
     return (jax.ShapeDtypeStruct(shape, F32), *edges)
 
 
-def choose(window, crossed, radius):
+def assemble(window, pieces, radius):
     out_shape = edge_shapes(window.shape, radius, window.shape[1:2])
-    return call(choose_kernel, out_shape, [VMEM] * 2, "estimate")(window, crossed)
+    kernel = functools.partial(assemble_kernel, count=len(pieces))
+    return call(kernel, out_shape, [VMEM] * (1 + len(pieces)), "estimate")(*pieces, window)
+
+
+def assemble_far(pieces):
+    share, rows, lanes = pieces[0].shape
+    shape = jax.ShapeDtypeStruct((share * len(pieces), rows, lanes), F32)
+    kernel = functools.partial(assemble_kernel, count=len(pieces))
+    return call(kernel, (shape,), [VMEM] * len(pieces), "far_slab")(*pieces)[0]
 
 
 def shift_kernel(offsets_ref, acq_ref, mask_ref, first_ref, second_ref, turned_ref):
@@ -262,8 +278,11 @@
     return call(shift_kernel, (shape, shape), [SMEM, VMEM, VMEM], "shift_recorded", scratch)(offsets, acquired, mask)
 
 
-def gather(ref, row):
-    return ref[:, pl.ds(pl.multiple_of(row, 8), 8), :]
+def gather(ref, row, radius=None):
+    rows = pl.ds(pl.multiple_of(row, 8), 8)
+    if radius is None or ref.shape[0] == radius:
+        return ref[:, rows, :]
+    return ref[pl.ds((1 - core()) * (ref.shape[0] - radius), radius), rows, :]
 
 
 def spread_x(hi_ref, lo_ref, index, band_rows, band_lanes, blocks):
@@ -298,14 +317,14 @@
     lax.fori_loop(0, rows // 8, body, 0)
 
 
-def blur_far_kernel(hi_ref, lo_ref, far_ref, first_ref, second_ref, first_out, second_out):
+def blur_far_kernel(hi_ref, lo_ref, far_ref, first_ref, second_ref, first_out, second_out, *, radius):
     planes, rows, _ = first_ref.shape
-    lanes = slice(near_lanes(planes, far_ref.shape[0]), None)
+    lanes = slice(near_lanes(planes, radius), None)
 
     def body(step, carry):
         row = pl.multiple_of(step * 8, 8)
         place = (slice(None), pl.ds(row, 8), slice(None))
-        out = spread_x(hi_ref, lo_ref, 0, slice(None), lanes, [[gather(far_ref, row)]])
+        out = spread_x(hi_ref, lo_ref, 0, slice(None), lanes, [[gather(far_ref, row, radius)]])
         first_out[place] = first_ref[place] + out[:planes]
         second_out[place] = second_ref[place] + out[planes:]
         return carry
@@ -318,9 +337,10 @@
     return call(blur_near_kernel, (shape, shape), [VMEM] * 4, "blur_x_near")(*tables[4:], own, near)
 
 
-def blur_far(tables, far, parts):
+def blur_far(tables, far, parts, radius):
     shape = jax.ShapeDtypeStruct(parts[0].shape, F32)
-    return call(blur_far_kernel, (shape, shape), [VMEM] * 5, "blur_x_far")(*tables[4:], far, *parts)
+    kernel = functools.partial(blur_far_kernel, radius=radius)
+    return call(kernel, (shape, shape), [VMEM] * 5, "blur_x_far")(*tables[4:], far, *parts)
 
 
 def spread_y(band, x):
@@ -424,15 +444,20 @@
     adjoint_planes(blurred_of, fetch, ya_ref, zhi_ref, zlo_ref, order, out_ref, edge_refs)
 
 
-def next_ratio_kernel(image_ref, *refs, order, wides):
-    wide_refs, (yf_ref, ya_ref, zhi_ref, zlo_ref, out_ref) = refs[:wides], refs[wides:wides + 5]
-
-    def blurred_of(block):
-        return blurred_planes(wide_refs, yf_ref, zhi_ref, zlo_ref, order, block)
-
-    adjoint_planes(
-        blurred_of, lambda p: image_ref[p], ya_ref, zhi_ref, zlo_ref, order, out_ref, refs[wides + 5:]
-    )
+def next_ratio_kernel(*refs, wides):
+    image_refs, refs = refs[:2], refs[2:]
+    wide_refs, refs = (refs[:wides], refs[wides:2 * wides]), refs[2 * wides:]
+    (yf_ref, ya_ref, zhi_ref, zlo_ref), out_refs, edge_refs = refs[:4], refs[4:6], refs[6:]
+    for order in range(2):
+
+        def blurred_of(block, order=order):
+            return blurred_planes(wide_refs[order], yf_ref, zhi_ref, zlo_ref, order, block)
+
+        def image_of(p, order=order):
+            return image_refs[order][p]
+
+        edges = [ref.at[order] for ref in edge_refs]
+        adjoint_planes(blurred_of, image_of, ya_ref, zhi_ref, zlo_ref, order, out_refs[order], edges)
 
 
 def ratio_shapes(planes, lanes, tables, radius, chunks):
@@ -450,54 +475,61 @@
     return call(kernel, out_shape, in_specs, "image_and_ratio", scratch)(shifts, *blocks, blurred, *tables[1:4])
 
 
-def next_ratio(image, wides, tables, order, radius, chunks):
-    planes, _, lanes = image.shape
-    kernel = functools.partial(next_ratio_kernel, order=order, wides=len(wides))
-    out_shape = ratio_shapes(planes, lanes, tables, radius, chunks)
-    return call(kernel, out_shape, [VMEM] * (5 + len(wides)), "ratio")(image, *wides, *tables[:4])
-
-
-def factor_kernel(hi_ref, lo_ref, before_ref, far_ref, near_ref, own_ref, out_ref, *, order, starts, share):
+def next_ratio(images, wides, tables, radius, chunks):
+    planes, _, lanes = images[0].shape
+    kernel = functools.partial(next_ratio_kernel, wides=len(wides[0]))
+    whole, *edges = ratio_shapes(planes, lanes, tables, radius, chunks)
+    edges = [jax.ShapeDtypeStruct((2,) + edge.shape, F32) for edge in edges]
+    return call(kernel, (whole, whole, *edges), [VMEM] * (6 + 2 * len(wides[0])), "ratio")(
+        *images, *wides[0], *wides[1], *tables[:4]
+    )
+
+
+def factor_kernel(hi_ref, lo_ref, before_ref, *refs, orders, starts, share):
+    out_ref = refs[-1]
     planes, rows, _ = out_ref.shape
-    band_rows = slice(order * 8 * planes, (order + 1) * 8 * planes)
 
     def body(step, carry):
         row = pl.multiple_of(step * 8, 8)
         total = gather(before_ref, starts[0] + row)
         if share:
             total = share * jnp.log(total)
-        own = gather(own_ref, starts[1] + row)
-        edge_row = starts[2] + row
-        blocks = [[own, gather(near_ref, edge_row)], [gather(far_ref, edge_row)]]
-        factor = spread_x(hi_ref, lo_ref, 1, band_rows, slice(None), blocks)
-        out_ref[:, pl.ds(row, 8), :] = total + jnp.log(factor)
+        for index, order in enumerate(orders):
+            far_ref, near_ref, own_ref = refs[3 * index:3 * index + 3]
+            if len(far_ref.shape) == 4:
+                far_ref, near_ref = far_ref.at[order], near_ref.at[order]
+            own = gather(own_ref, starts[1] + row)
+            blocks = [[own, gather(near_ref, row)], [gather(far_ref, row)]]
+            band_rows = slice(order * 8 * planes, (order + 1) * 8 * planes)
+            total = total + jnp.log(spread_x(hi_ref, lo_ref, 1, band_rows, slice(None), blocks))
+        out_ref[:, pl.ds(row, 8), :] = total
         return carry
 
     lax.fori_loop(0, rows // 8, body, 0)
 
 
-def log_factor(tables, before, side, order, rows, starts, share):
-    far, near, own = side
-    kernel = functools.partial(factor_kernel, order=order, starts=starts, share=share)
-    shape = jax.ShapeDtypeStruct((own.shape[0], rows, own.shape[2]), F32)
-    return call(kernel, shape, [VMEM] * 6, "log_factor")(*tables[4:], before, far, near, own)
-
-
-def update_kernel(*refs):
-    parts, edge_ref, out_ref, edge_refs = refs[:-4], refs[-4], refs[-3], refs[-2:]
+def log_factor(tables, before, sides, orders, rows, starts, share):
+    kernel = functools.partial(factor_kernel, orders=orders, starts=starts, share=share)
+    planes, _, lanes = sides[0][2].shape
+    shape = jax.ShapeDtypeStruct((planes, rows, lanes), F32)
+    parts = [part for side in sides for part in side]
+    return call(kernel, shape, [VMEM] * (3 + len(parts)), "log_factor")(*tables[4:], before, *parts)
+
+
+def update_kernel(*refs, count):
+    parts, out_ref, edge_refs = refs[:count], refs[count], refs[count + 1:]
     for p in range(out_ref.shape[0]):
         total = parts[0][p]
         for part in parts[1:]:
             total = total + part[p]
-        out_ref[p] = jnp.concatenate([jnp.exp(total), edge_ref[p]], axis=0)
+        out_ref[p] = jnp.exp(total)
     put_edges(out_ref, edge_refs)
 
 
-def update(parts, edge, radius):
-    planes, rows, lanes = parts[0].shape
-    rows += edge.shape[1]
-    out_shape = edge_shapes((planes, rows, lanes), radius, [rows])
-    return call(update_kernel, out_shape, [VMEM] * (len(parts) + 1), "update")(*parts, edge)
+def update(parts, radius):
+    kernel = functools.partial(update_kernel, count=len(parts))
+    out_shape = edge_shapes(parts[0].shape, radius, parts[0].shape[1:2])
+    return call(kernel, out_shape, [VMEM] * len(parts), "update")(*parts)
 
 
 def finish_kernel(*refs):
@@ -569,11 +601,14 @@
     def neighbours(far, near):
         return send(far, to_far), send(near, to_core_partner)
 
-    window, crossed = make_windows(estimate, wide)
-    crossed = send(crossed, across(0, lambda r: 1 - r, when=lambda c, r: c == r))
+    window, crossing = make_windows(estimate, wide)
+    piece = lax.dynamic_slice_in_dim(crossing, group * (planes // groups), planes // groups, 0)
+    piece = send(piece, across(0, lambda r: 1 - r, when=lambda c, r: c == r))
 
     acquired = after(acquired, window)
     first, second = shift_and_cut(offsets, acquired[0], view_mask[0], near)
+    piece = after(piece, first)
+
     mine = [jnp.pad(row, ((0, 0), (0, 128 - row.shape[1]))) for row in (kern_x, kern_y, kern_z, offsets.astype(F32))]
     mine = jnp.concatenate(mine, axis=1)
     other = send(mine, to_core_partner)
@@ -582,60 +617,66 @@
     shifts = jnp.where(straight, jnp.concatenate([mine, other]), jnp.concatenate([other, mine]))
     shifts = shifts[:, 384:384 + offsets.shape[1]].astype(jnp.int32)
 
-    arrived = send(after(first, tables[0]), lambda g, c, q, r: (g, r, q, c) if c != r else None)
-    current, distant, close = choose(after(window, first), crossed, radius)
-    second = send(after(second, current), lambda g, c, q, r: (g, r, q, 1 - c))
-    distant, close = neighbours(distant, close)
-    chunks = [(distant, blur_near(tables, current, close))]
+    arrived = send(first, lambda g, c, q, r: (g, r, q, c) if c != r else None)
+    start = group * (planes // groups)
+    share = jnp.where(straight, lax.dynamic_slice_in_dim(window, start, planes // groups, 0), piece)
+    later = after(after(piece, tables[0]), share)
+    pieces = [piece] + [send(later, across(turn, when=lambda c, r: c != r)) for turn in range(1, groups)]
+    share = send(share, to_far)
+    shares = [share] + [send(share, across(turn)) for turn in range(1, groups)]
+    second = send(after(second, share), lambda g, c, q, r: (g, r, q, 1 - c))
+    current, _, close = assemble(after(window, shares[-1]), pieces, radius)
+    chunks = [(assemble_far(shares), blur_near(tables, current, send(close, to_core_partner)))]
     first = jnp.where(straight, first, arrived)
     blocks = [(*neighbours(block, block), block) for block in (first, second)]
     images = [None, None]
 
-    sizes = [[own_rows], [inner_rows, edge_rows]]
-
-    for step in range(ITERS):
-        last = step == ITERS - 1
-        if last:
-            sizes = [[own_rows], [own_rows]]
-        wides = []
-        for distant, parts in chunks:
-            distant = after(distant, wides[-1][0]) if wides else distant
-            wides.append(blur_far(tables, distant, parts))
-        sides = []
-        if step == 0:
-            blurred = [blur_yz([chunk[order] for chunk in wides], tables, order) for order in range(2)]
-        for order in range(2):
-            if step == 0:
-                spread, *edges, images[order] = first_ratio(
-                    shifts, blocks[order], blurred[order], tables, order, radius, sizes[order], planes * slabs, cells_y
-                )
-            else:
-                parts = [chunk[order] for chunk in wides]
-                spread, *edges = next_ratio(images[order], parts, tables, order, radius, sizes[order])
-            sides += [(*neighbours(*edges[k:k + 2]), spread) for k in range(0, len(edges), 2)]
-
-        total = log_factor(tables, current, sides[0], 0, own_rows, (0, 0, 0), 1.0 / groups)
-        starts = (inner_rows, inner_rows, inner_rows if last else 0)
-        edge = log_factor(tables, total, sides[-1], 1, edge_rows, starts, 0)
-        inner = log_factor(tables, total, sides[1], 1, inner_rows, (0, 0, 0), 0)
-
-        if not last:
-            edge_parts = [edge] + [send(edge, across(turn)) for turn in range(1, groups)]
-            inner_parts = [inner] + [send(inner, across(turn)) for turn in range(1, groups)]
-            edge = jnp.exp(sum(edge_parts[1:], edge_parts[0]))
-            beyond = send(edge, to_row_partner)
-            current, distant, close = update(inner_parts, edge, radius)
+    row_chunks = [(inner_rows, edge_rows), (0, inner_rows)]
+    share = 1.0 / groups
+    wide_parts = [blur_far(tables, *chunk, radius) for chunk in chunks]
+    blurred = [blur_yz([parts[order] for parts in wide_parts], tables, order) for order in range(2)]
+    images, sides = [], []
+    for order, chunk_sizes in enumerate(([own_rows], [edge_rows, inner_rows])):
+        spread, *edges, image = first_ratio(
+            shifts, blocks[order], blurred[order], tables, order, radius, chunk_sizes, planes * slabs, cells_y
+        )
+        images.append(image)
+        sides.append([(*neighbours(*edges[k:k + 2]), spread) for k in range(0, len(edges), 2)])
+    total = log_factor(tables, current, sides[0], [0], own_rows, (0, 0), share)
+    totals = [
+        log_factor(tables, total, [side], [1], rows, (start, start), 0)
+        for (start, rows), side in zip(row_chunks, sides[1])
+    ]
+
+    for step in range(1, ITERS):
+        chunks, before = [], []
+        for total in totals:
+            parts = [total] + [send(total, across(turn)) for turn in range(1, groups)]
+            rows, distant, close = update(parts, radius)
+            if total is totals[0]:
+                beyond = send(rows, to_row_partner)
             distant, close = neighbours(distant, close)
-            chunks = [(distant, blur_near(tables, current, close))]
-            rest = planes - radius
-            distant, close = neighbours(
-                lax.dynamic_slice_in_dim(beyond, core() * rest, radius, 0),
-                lax.dynamic_slice_in_dim(beyond, (1 - core()) * rest, radius, 0),
-            )
-            chunks.append((distant, blur_near(tables, beyond, after(close, chunks[0][1][0]))))
+            chunks.append((distant, blur_near(tables, rows, close)))
+            before.append(rows)
+        rest = planes - radius
+        distant, close = neighbours(
+            lax.dynamic_slice_in_dim(beyond, core() * rest, radius, 0),
+            lax.dynamic_slice_in_dim(beyond, (1 - core()) * rest, radius, 0),
+        )
+        chunks.append((distant, blur_near(tables, beyond, close)))
+        edge_parts, inner_parts, halo_parts = [blur_far(tables, *chunk, radius) for chunk in chunks]
+        wides = [[parts[order] for parts in (inner_parts, edge_parts, halo_parts)] for order in range(2)]
+        *spreads, edge_far, edge_near, inner_far, inner_near = next_ratio(
+            images, wides, tables, radius, [edge_rows, inner_rows]
+        )
+        sides = [neighbours(edge_far, edge_near), neighbours(inner_far, inner_near)]
+        totals = [
+            log_factor(tables, estimate_rows, [(*side, spread) for spread in spreads], [0, 1], rows, (0, start), share)
+            for (start, rows), side, estimate_rows in zip(row_chunks, sides, before)
+        ]
 
     pieces = []
-    for own in (edge, inner):
+    for own in totals:
         other_parts = [
             send(own, across(turn, lambda r: 1 - r, lambda c: 1 - c, lambda c, r: c != r))
             for turn in reversed(range(groups))
@@ -643,7 +684,7 @@
         own_parts = [own] + [send(own, across(turn, when=lambda c, r: c == r)) for turn in range(1, groups)]
         mine = finish(own_parts, other_parts)
         pieces += [mine, send(mine, to_core_partner)]
-    return join(pieces, [inner_rows, 0], estimate.shape)
+    return join(pieces, [start for start, _ in row_chunks], estimate.shape)
 
 
 def solution(mesh):

time: 220 us -> 218 us (level)
  Pallas kernels: 54 us -> 48.8 us
  waiting for transfers between devices: 95.1 us -> 98.3 us
    ppermute x35 -> x39, waiting for transfers between devices: 95.1 us -> 98.3 us  [send(): return lax.ppermute(array, AXES, moves(move))]
    pallas_call x3 -> x4, Pallas kernels: 9.1 us -> 7.56 us  [blur_near(): call(blur_near_kernel, (shape, shape), [VMEM] * 4, 'blur_x_near')]
    unnamed x26 -> x28, local copies, waits for them, and re-layouts: 3.79 us -> 5.06 us
    ppermute x35 -> x39, starting transfers between devices: 60.2 us -> 61.3 us  [send(): return lax.ppermute(array, AXES, moves(move))]
    pallas_call x13 -> x14, Pallas kernels: 27.5 us -> 26.4 us  [the longest x5 7.68 us: log_factor(): call(kernel, shape, [VMEM] * (3 + len(parts)), 'log_factor')]
  transfers between devices with their start and end apart: 35 -> 39, of which waited for: 19 -> 19; matrix products, arithmetic and copies ran while one was open for 2% -> 0% of each run, Pallas kernels for 21% -> 17%
where the time goes in v8:
time: 218 us; the launch traced here: 217 us
  waiting for transfers between devices  98.3 us (45%)
  starting transfers between devices  61.3 us (28%)
  Pallas kernels  48.8 us (22%)
  local copies, waits for them, and re-layouts  6.1 us (3%)
    ppermute x39, waiting for transfers between devices, send(): return lax.ppermute(array, AXES, moves(move))  98.3 us
    ppermute x39, starting transfers between devices, send(): return lax.ppermute(array, AXES, moves(move))  61.3 us
    pallas_call x5, Pallas kernels, log_factor(): call(kernel, shape, [VMEM] * (3 + len(parts)), 'log_factor')  7.68 us
    pallas_call x4, Pallas kernels, blur_near(): call(blur_near_kernel, (shape, shape), [VMEM] * 4, 'blur_x_near')  7.56 us
    pallas_call x1, Pallas kernels, next_ratio(): call(kernel, (whole, whole, *edges), [VMEM] * (6 + 2 * len(wides[0])), 'r...  7.36 us
    pallas_call x4, Pallas kernels, blur_far(): call(kernel, (shape, shape), [VMEM] * 5, 'blur_x_far')  6.28 us
    pallas_call x2, Pallas kernels, first_ratio(): call(kernel, out_shape, in_specs, 'image_and_ratio', scratch)  5.38 us
    unnamed x28, local copies, waits for them, and re-layouts  5.06 us
  transfers between devices with their start and end apart: 39, of which 19 were waited for; matrix products, arithmetic and copies ran while one was open for 0% of the time, Pallas kernels for 17%

profile of v8, /device:TPU:17, one launch (start us, length us, event | category | flops | bytes accessed | tf_op | source)
XLA Modules:
  0.0 216.9 jit_solution(10124583225260784264)
XLA Ops:
  0.0 1.6 copy-done.1
  4.1 1.6 copy-done
  5.7 3.0 %shift_recorded.1 = (f32[17,80,256]{2,1,0:T(8,128)S(1)}, f32[17,80,256]{2,1,0:T(8,128)S(1)}) custom-call(s32[1,3]{1,0:T(1,128)S(1)} %copy-done.9, f32[16,128,256]{2,1,0:T(8,128)S(1)} %bitcast.2, s32[16,128]{1,0:T(8,128)S(1)} %bitcast.3), custom_call_target="tpu_custom_call" | custom-call | tf_op jit(solution)/shard_map/shift_recorded/pallas_call | solution.py:278
  8.7 7.1 %collective-permute-done.1.refs_0_ = f32[8,96,256]{2,1,0:T(8,128)} collective-permute-done((f32[8,96,256]{2,1,0:T(8,128)}, f32[8,96,256]{2,1,0:T(8,128)}, u32[]{:S(2)}, u32[]{:S(2)}) %collective-permute-start.1) | collective-permute-done | bytes 786464 | tf_op jit(solution)/shard_map/ppermute | solution.py:33
  17.1 2.8 %collective-permute-start.3 = (f32[8,96,256]{2,1,0:T(8,128)S(1)}, f32[8,96,256]{2,1,0:T(8,128)S(1)}, u32[]{:S(2)}, u32[]{:S(2)}) collective-permute-start(f32[8,96,256]{2,1,0:T(8,128)S(1)} %dynamic-slice_select_fusion), channel_id=1, source_target_pairs={{2,8},{3,9},{4,10},{5,11},{6,12},{7,13},{8,2},{9,3},{10,4},{11,5},... | collective-permute-start | bytes 2359304 | tf_op jit(solution)/shard_map/ppermute | solution.py:33
  19.9 4.0 %collective-permute-start.5 = (f32[17,80,256]{2,1,0:T(8,128)S(1)}, f32[17,80,256]{2,1,0:T(8,128)S(1)}, u32[]{:S(2)}, u32[]{:S(2)}) collective-permute-start(f32[17,80,256]{2,1,0:T(8,128)S(1)} %get-tuple-element.66), channel_id=1, source_target_pairs={{1,8},{3,10},{5,12},{7,14},{8,1},{10,3},{12,5},{14,7},{17,24},{19,... | collective-permute-start | bytes 4177928 | tf_op jit(solution)/shard_map/ppermute | solution.py:33
  26.8 3.6 %collective-permute-done.3.refs_0_ = f32[8,96,256]{2,1,0:T(8,128)S(1)} collective-permute-done((f32[8,96,256]{2,1,0:T(8,128)S(1)}, f32[8,96,256]{2,1,0:T(8,128)S(1)}, u32[]{:S(2)}, u32[]{:S(2)}) %collective-permute-start.3) | collective-permute-done | bytes 786464 | tf_op jit(solution)/shard_map/ppermute | solution.py:33
  31.6 2.2 collective-permute-start.2
  33.8 16.0 %collective-permute-done.4.refs_1_ = f32[8,96,256]{2,1,0:T(8,128)S(1)} collective-permute-done((f32[8,96,256]{2,1,0:T(8,128)S(1)}, f32[8,96,256]{2,1,0:T(8,128)S(1)}, u32[]{:S(2)}, u32[]{:S(2)}) %collective-permute-start.4) | collective-permute-done | bytes 786464 | tf_op jit(solution)/shard_map/ppermute | solution.py:33
  49.8 8.3 %collective-permute-done.2.refs_1_ = f32[8,96,256]{2,1,0:T(8,128)S(1)} collective-permute-done((f32[8,96,256]{2,1,0:T(8,128)}, f32[8,96,256]{2,1,0:T(8,128)S(1)}, u32[]{:S(2)}, u32[]{:S(2)}) %collective-permute-start.2) | collective-permute-done | bytes 786464 | tf_op jit(solution)/shard_map/ppermute | solution.py:33
  58.1 2.7 %estimate.1 = (f32[16,96,256]{2,1,0:T(8,128)S(1)}, f32[15,96,256]{2,1,0:T(8,128)}, f32[15,96,256]{2,1,0:T(8,128)S(1)}) custom-call(f32[8,96,256]{2,1,0:T(8,128)} %collective-permute-done.1.refs_0_, f32[8,96,256]{2,1,0:T(8,128)S(1)} %collective-permute-done.2.refs_1_, f32[16,96,256]{2,1,0:T(8,128)S(1)} %get-tuple-element.71.refs_2_), custom_call_target="tpu_custom_call" | custom-call | tf_op jit(solution)/shard_map/estimate/pallas_call | solution.py:238
  61.0 1.9 collective-permute-start.6
  63.6 3.1 %collective-permute-start.12 = (f32[17,80,256]{2,1,0:T(8,128)S(1)}, f32[17,80,256]{2,1,0:T(8,128)S(1)}, u32[]{:S(2)}, u32[]{:S(2)}) collective-permute-start(f32[17,80,256]{2,1,0:T(8,128)S(1)} %collective-permute-done.11.own_ref), channel_id=1, source_target_pairs={{2,8},{3,9},{4,10},{5,11},{6,12},{7,13},{8,2},{9,3},{10,4},{11,5},... | collective-permute-start | bytes 4177928 | tf_op jit(solution)/shard_map/ppermute | solution.py:33
  67.5 3.3 %blur_x_near.4 = (f32[16,96,256]{2,1,0:T(8,128)S(1)}, f32[16,96,256]{2,1,0:T(8,128)S(1)}) custom-call(bf16[2,256,384]{2,1,0:T(8,128)(2,1)S(1)} %get-tuple-element.61.hi_ref, bf16[2,256,384]{2,1,0:T(8,128)(2,1)S(1)} %get-tuple-element.62.lo_ref, f32[16,96,256]{2,1,0:T(8,128)S(1)} %get-tuple-element.72.own_ref.before_ref, ...), custom_call_target="tpu_custom_call" | custom-call | tf_op jit(solution)/shard_map/blur_x_near/pallas_call | solution.py:337
  70.8 3.2 %blur_x_far.4 = (f32[16,96,256]{2,1,0:T(8,128)S(1)}, f32[16,96,256]{2,1,0:T(8,128)S(1)}) custom-call(bf16[2,256,384]{2,1,0:T(8,128)(2,1)S(1)} %get-tuple-element.61.hi_ref, bf16[2,256,384]{2,1,0:T(8,128)(2,1)S(1)} %get-tuple-element.62.lo_ref, f32[16,96,256]{2,1,0:T(8,128)S(1)} %far_slab.1.far_ref, f32[16,96,256]{2,1,0:T(8,128)S(1)} %get-tuple-element.74.first_ref, ...), custom_call_target="tpu_custom_call" | custom-call | tf_op jit(solution)/shard_map/blur_x_far/pallas_call | solution.py:343
  75.6 5.6 %collective-permute-done.6.far_ref = f32[17,80,256]{2,1,0:T(8,128)S(1)} collective-permute-done((f32[17,80,256]{2,1,0:T(8,128)S(1)}, f32[17,80,256]{2,1,0:T(8,128)S(1)}, u32[]{:S(2)}, u32[]{:S(2)}) %collective-permute-start.6) | collective-permute-done | bytes 1392672 | tf_op jit(solution)/shard_map/ppermute | solution.py:33
  81.1 2.7 %image_and_ratio.2 = (f32[16,64,256]{2,1,0:T(8,128)S(1)}, f32[15,64,256]{2,1,0:T(8,128)S(1)}, f32[15,64,256]{2,1,0:T(8,128)S(1)}, f32[16,80,256]{2,1,0:T(8,128)S(1)}) custom-call(s32[2,3]{1,0:T(2,128)S(1)} %fusion.1.shift_ref, f32[17,80,256]{2,1,0:T(8,128)S(1)} %collective-permute-done.6.far_ref, f32[17,80,256]{2,1,0:T(8,128)S(1)} %collective-permute-done.7.near_ref, ...), custom_call_target="tpu_custom_call" | custom-call | tf_op jit(solution)/shard_map/image_and_ratio/pallas_call | solution.py:475
  85.1 1.9 collective-permute-start.9
  87.0 1.6 blur_yz.3.blurred_ref
  88.6 7.5 %collective-permute-done.12.far_ref = f32[17,80,256]{2,1,0:T(8,128)S(1)} collective-permute-done((f32[17,80,256]{2,1,0:T(8,128)S(1)}, f32[17,80,256]{2,1,0:T(8,128)S(1)}, u32[]{:S(2)}, u32[]{:S(2)}) %collective-permute-start.12) | collective-permute-done | bytes 1392672 | tf_op jit(solution)/shard_map/ppermute | solution.py:33
  96.0 2.7 %image_and_ratio.3 = (f32[16,64,256]{2,1,0:T(8,128)S(1)}, f32[15,32,256]{2,1,0:T(8,128)S(1)}, f32[15,32,256]{2,1,0:T(8,128)S(1)}, f32[15,32,256]{2,1,0:T(8,128)S...) custom-call(s32[2,3]{1,0:T(2,128)S(1)} %fusion.1.shift_ref, ...), custom_call_target="tpu_custom_call" | custom-call | tf_op jit(solution)/shard_map/image_and_ratio/pallas_call | solution.py:475
  98.8 1.9 collective-permute-start.14
  101.3 5.3 %collective-permute-done.9.refs_0_ = f32[15,64,256]{2,1,0:T(8,128)S(1)} collective-permute-done((f32[15,64,256]{2,1,0:T(8,128)S(1)}, f32[15,64,256]{2,1,0:T(8,128)S(1)}, u32[]{:S(2)}, u32[]{:S(2)}) %collective-permute-start.9) | collective-permute-done | bytes 983072 | tf_op jit(solution)/shard_map/ppermute | solution.py:33
  106.6 2.1 log_factor.5.before_ref
  108.7 2.9 %collective-permute-done.14.refs_0_ = f32[15,32,256]{2,1,0:T(8,128)S(1)} collective-permute-done((f32[15,32,256]{2,1,0:T(8,128)S(1)}, f32[15,32,256]{2,1,0:T(8,128)S(1)}, u32[]{:S(2)}, u32[]{:S(2)}) %collective-permute-start.14) | collective-permute-done | bytes 491552 | tf_op jit(solution)/shard_map/ppermute | solution.py:33
  114.0 2.3 %collective-permute-start.17 = (f32[15,32,256]{2,1,0:T(8,128)S(1)}, f32[15,32,256]{2,1,0:T(8,128)S(1)}, u32[]{:S(2)}, u32[]{:S(2)}) collective-permute-start(f32[15,32,256]{2,1,0:T(8,128)S(1)} %get-tuple-element.92), channel_id=1, source_target_pairs={{2,8},{3,9},{4,10},{5,11},{6,12},{7,13},{8,2},{9,3},{10,4},{11,5},... | collective-permute-start | bytes 1474568 | tf_op jit(solution)/shard_map/ppermute | solution.py:33
  116.9 7.6 %collective-permute-done.17.refs_0_ = f32[15,32,256]{2,1,0:T(8,128)S(1)} collective-permute-done((f32[15,32,256]{2,1,0:T(8,128)S(1)}, f32[15,32,256]{2,1,0:T(8,128)S(1)}, u32[]{:S(2)}, u32[]{:S(2)}) %collective-permute-start.17) | collective-permute-done | bytes 491552 | tf_op jit(solution)/shard_map/ppermute | solution.py:33
  127.7 3.8 %collective-permute-start.24 = (f32[16,32,256]{2,1,0:T(8,128)S(1)}, f32[16,32,256]{2,1,0:T(8,128)S(1)}, u32[]{:S(2)}, u32[]{:S(2)}) collective-permute-start(f32[16,32,256]{2,1,0:T(8,128)S(1)} %get-tuple-element.89.own_ref.before_ref), channel_id=1, source_target_pairs={{0,1},{1,0},{2,3},{3,2},{4,5},{5,4},{6,7},{7,6},{8,9},{9,8},{10,11... | collective-permute-start | bytes 1572872 | tf_op jit(solution)/shard_map/ppermute | solution.py:33
  132.6 1.9 collective-permute-start.22
  134.5 4.4 %collective-permute-done.19.refs_1_ = f32[16,32,256]{2,1,0:T(8,128)} collective-permute-done((f32[16,32,256]{2,1,0:T(8,128)S(1)}, f32[16,32,256]{2,1,0:T(8,128)}, u32[]{:S(2)}, u32[]{:S(2)}) %collective-permute-start.19) | collective-permute-done | bytes 524320 | tf_op jit(solution)/shard_map/ppermute | solution.py:33
  141.3 1.9 collective-permute-start.20
  144.5 2.6 %collective-permute-start.25 = (f32[15,32,256]{2,1,0:T(8,128)S(1)}, f32[15,32,256]{2,1,0:T(8,128)S(1)}, u32[]{:S(2)}, u32[]{:S(2)}) collective-permute-start(f32[15,32,256]{2,1,0:T(8,128)S(1)} %get-tuple-element.118), channel_id=1, source_target_pairs={{2,8},{3,9},{4,10},{5,11},{6,12},{7,13},{8,2},{9,3},{10,4},{11,5},... | collective-permute-start | bytes 1474568 | tf_op jit(solution)/shard_map/ppermute | solution.py:33
  147.1 2.1 blur_x_near.6
  153.9 2.8 %collective-permute-done.25.far_ref = f32[15,32,256]{2,1,0:T(8,128)S(1)} collective-permute-done((f32[15,32,256]{2,1,0:T(8,128)S(1)}, f32[15,32,256]{2,1,0:T(8,128)S(1)}, u32[]{:S(2)}, u32[]{:S(2)}) %collective-permute-start.25) | collective-permute-done | bytes 491552 | tf_op jit(solution)/shard_map/ppermute | solution.py:33
  157.8 7.4 %ratio.1 = (f32[16,64,256]{2,1,0:T(8,128)S(1)}, f32[16,64,256]{2,1,0:T(8,128)S(1)}, f32[2,15,32,256]{3,2,1,0:T(8,128)S(1)}, f32[2,15,32,256]{3,2,1,0:T(8,128)S(1...) custom-call(f32[16,80,256]{2,1,0:T(8,128)S(1)} %copy-done.3, f32[16,80,256]{2,1,0:T(8,128)S(1)} %copy-done.5, ...), custom_call_target="tpu_custom_call" | custom-call | tf_op jit(solution)/shard_map/ratio/pallas_call | solution.py:483
  165.2 1.9 collective-permute-start.33
  167.9 3.0 %collective-permute-start.27 = (f32[2,15,32,256]{3,2,1,0:T(8,128)S(1)}, f32[2,15,32,256]{3,2,1,0:T(8,128)S(1)}, u32[]{:S(2)}, u32[]{:S(2)}) collective-permute-start(f32[2,15,32,256]{3,2,1,0:T(8,128)S(1)} %get-tuple-element.111), channel_id=1, source_target_pairs={{2,8},{3,9},{4,10},{5,11},{6,12},{7,13},{8,2},{9,3},{10,4},{11,5},... | collective-permute-start | bytes 2949128 | tf_op jit(solution)/shard_map/ppermute | solution.py:33
  170.9 10.0 %collective-permute-done.33.refs_0_.refs_3_ = f32[2,15,32,256]{3,2,1,0:T(8,128)S(1)} collective-permute-done((f32[2,15,32,256]{3,2,1,0:T(8,128)S(1)}, f32[2,15,32,256]{3,2,1,0:T(8,128)S(1)}, u32[]{:S(2)}, u32[]{:S(2)}) %collective-permute-start.33) | collective-permute-done | bytes 983072 | tf_op jit(solution)/shard_map/ppermute | solution.py:33
  180.9 1.7 log_factor.9.refs_0_
  183.3 4.8 %collective-permute-start.36 = (f32[16,32,256]{2,1,0:T(8,128)S(1)}, f32[16,32,256]{2,1,0:T(8,128)S(1)}, u32[]{:S(2)}, u32[]{:S(2)}) collective-permute-start(f32[16,32,256]{2,1,0:T(8,128)S(1)} %log_factor.9.refs_0_), channel_id=1, source_target_pairs={{1,24},{3,26},{5,28},{7,30},{8,17},{10,19},{12,21},{14,23},{17,8},... | collective-permute-start | bytes 1572872 | tf_op jit(solution)/shard_map/ppermute | solution.py:33
  188.1 1.9 collective-permute-start.37
  191.4 1.7 log_factor.8.refs_0_
  193.8 4.8 %collective-permute-start.30 = (f32[16,32,256]{2,1,0:T(8,128)S(1)}, f32[16,32,256]{2,1,0:T(8,128)S(1)}, u32[]{:S(2)}, u32[]{:S(2)}) collective-permute-start(f32[16,32,256]{2,1,0:T(8,128)S(1)} %log_factor.8.refs_0_), channel_id=1, source_target_pairs={{1,24},{3,26},{5,28},{7,30},{8,17},{10,19},{12,21},{14,23},{17,8},... | collective-permute-start | bytes 1572872 | tf_op jit(solution)/shard_map/ppermute | solution.py:33
  198.7 1.9 collective-permute-start.31
  200.6 3.9 %collective-permute-done.37.refs_3_ = f32[16,32,256]{2,1,0:T(8,128)S(1)} collective-permute-done((f32[16,32,256]{2,1,0:T(8,128)S(1)}, f32[16,32,256]{2,1,0:T(8,128)S(1)}, u32[]{:S(2)}, u32[]{:S(2)}) %collective-permute-start.37) | collective-permute-done | bytes 524320 | tf_op jit(solution)/shard_map/ppermute | solution.py:33
  204.7 6.5 %collective-permute-done.30.refs_2_ = f32[16,32,256]{2,1,0:T(8,128)S(1)} collective-permute-done((f32[16,32,256]{2,1,0:T(8,128)S(1)}, f32[16,32,256]{2,1,0:T(8,128)S(1)}, u32[]{:S(2)}, u32[]{:S(2)}) %collective-permute-start.30) | collective-permute-done | bytes 524320 | tf_op jit(solution)/shard_map/ppermute | solution.py:33
  211.2 2.1 collective-permute-done.31.refs_3_
  213.5 1.9 collective-permute-done.32.refs_1_
  (97 shorter events, 34.7 us)
Async XLA Ops:
  1.6 2.5 %copy-start.9 = (s32[1,3]{1,0:T(1,128)S(1)}, s32[1,3]{1,0:T(1,128)}, u32[]{:S(2)}) copy-start(s32[1,3]{1,0:T(1,128)} %offsets_ref.1) | copy-start | bytes 40
  2.7 13.0 %collective-permute-start.1 = (f32[8,96,256]{2,1,0:T(8,128)}, f32[8,96,256]{2,1,0:T(8,128)}, u32[]{:S(2)}, u32[]{:S(2)}) collective-permute-start(f32[8,96,256]{2,1,0:T(8,128)} %constant_dynamic-slice_fusion.2), channel_id=1, source_target_pairs={{0,1},{2,3},{4,5},{6,7},{9,8},{11,10},{13,12},{15,14},{16,17},{18,... | collective-permute-start | bytes 2359304 | tf_op jit(solution)/shard_map/ppermute | solution.py:33
  8.7 15.2 %copy-start.11 = (f32[1,31]{1,0:T(1,128)S(1)}, f32[1,31]{1,0:T(1,128)}, u32[]{:S(2)}) copy-start(f32[1,31]{1,0:T(1,128)} %param.11) | copy-start | bytes 376
  8.7 15.3 %copy-start.12 = (f32[1,31]{1,0:T(1,128)S(1)}, f32[1,31]{1,0:T(1,128)}, u32[]{:S(2)}) copy-start(f32[1,31]{1,0:T(1,128)} %param.12) | copy-start | bytes 376
  8.7 15.3 %copy-start.13 = (f32[1,61]{1,0:T(1,128)S(1)}, f32[1,61]{1,0:T(1,128)}, u32[]{:S(2)}) copy-start(f32[1,61]{1,0:T(1,128)} %param.13) | copy-start | bytes 736
  17.1 13.3 %collective-permute-start.3 = (f32[8,96,256]{2,1,0:T(8,128)S(1)}, f32[8,96,256]{2,1,0:T(8,128)S(1)}, u32[]{:S(2)}, u32[]{:S(2)}) collective-permute-start(f32[8,96,256]{2,1,0:T(8,128)S(1)} %dynamic-slice_select_fusion), channel_id=1, source_target_pairs={{2,8},{3,9},{4,10},{5,11},{6,12},{7,13},{8,2},{9,3},{10,4},{11,5},... | collective-permute-start | bytes 2359304 | tf_op jit(solution)/shard_map/ppermute | solution.py:33
  19.9 40.9 %collective-permute-start.5 = (f32[17,80,256]{2,1,0:T(8,128)S(1)}, f32[17,80,256]{2,1,0:T(8,128)S(1)}, u32[]{:S(2)}, u32[]{:S(2)}) collective-permute-start(f32[17,80,256]{2,1,0:T(8,128)S(1)} %get-tuple-element.66), channel_id=1, source_target_pairs={{1,8},{3,10},{5,12},{7,14},{8,1},{10,3},{12,5},{14,7},{17,24},{19,... | collective-permute-start | bytes 4177928 | tf_op jit(solution)/shard_map/ppermute | solution.py:33
  24.0 1.2 collective-permute-start
  26.8 69.3 %copy-start.6 = (bf16[2,64,256]{2,1,0:T(8,128)(2,1)}, bf16[2,64,256]{2,1,0:T(8,128)(2,1)S(1)}, u32[]{:S(2)}) copy-start(bf16[2,64,256]{2,1,0:T(8,128)(2,1)S(1)} %get-tuple-element.79.ya_ref.refs_9_) | copy-start | bytes 196612
  30.4 19.4 %collective-permute-start.4 = (f32[8,96,256]{2,1,0:T(8,128)S(1)}, f32[8,96,256]{2,1,0:T(8,128)S(1)}, u32[]{:S(2)}, u32[]{:S(2)}) collective-permute-start(f32[8,96,256]{2,1,0:T(8,128)S(1)} %collective-permute-done.3.refs_0_), channel_id=1, source_target_pairs={{0,16},{1,17},{2,18},{3,19},{4,20},{5,21},{6,22},{7,23},{8,24},{9,... | collective-permute-start | bytes 2359304 | tf_op jit(solution)/shard_map/ppermute | solution.py:33
  31.6 26.5 %collective-permute-start.2 = (f32[8,96,256]{2,1,0:T(8,128)}, f32[8,96,256]{2,1,0:T(8,128)S(1)}, u32[]{:S(2)}, u32[]{:S(2)}) collective-permute-start(f32[8,96,256]{2,1,0:T(8,128)} %collective-permute-done.1.refs_0_), channel_id=1, source_target_pairs={{1,17},{3,19},{5,21},{7,23},{8,24},{10,26},{12,28},{14,30},{17,1},... | collective-permute-start | bytes 2359304 | tf_op jit(solution)/shard_map/ppermute | solution.py:33
  33.8 29.8 %collective-permute-start.11 = (f32[17,80,256]{2,1,0:T(8,128)S(1)}, f32[17,80,256]{2,1,0:T(8,128)S(1)}, u32[]{:S(2)}, u32[]{:S(2)}) collective-permute-start(f32[17,80,256]{2,1,0:T(8,128)S(1)} %get-tuple-element.84), channel_id=1, source_target_pairs={{0,1},{1,9},{2,3},{3,11},{4,5},{5,13},{6,7},{7,15},{8,0},{9,8},{10... | collective-permute-start | bytes 4177928 | tf_op jit(solution)/shard_map/ppermute | solution.py:33
  60.8 6.7 %collective-permute-start.8 = (f32[15,96,256]{2,1,0:T(8,128)S(1)}, f32[15,96,256]{2,1,0:T(8,128)S(1)}, u32[]{:S(2)}, u32[]{:S(2)}) collective-permute-start(f32[15,96,256]{2,1,0:T(8,128)S(1)} %get-tuple-element.73), channel_id=1, source_target_pairs={{0,8},{1,9},{2,10},{3,11},{4,12},{5,13},{6,14},{7,15},{8,0},{9,1},... | collective-permute-start | bytes 4423688 | tf_op jit(solution)/shard_map/ppermute | solution.py:33
  61.0 20.1 %collective-permute-start.6 = (f32[17,80,256]{2,1,0:T(8,128)S(1)}, f32[17,80,256]{2,1,0:T(8,128)S(1)}, u32[]{:S(2)}, u32[]{:S(2)}) collective-permute-start(f32[17,80,256]{2,1,0:T(8,128)S(1)} %broadcast_select_fusion.own_ref), channel_id=1, source_target_pairs={{2,8},{3,9},{4,10},{5,11},{6,12},{7,13},{8,2},{9,3},{10,4},{11,5},... | collective-permute-start | bytes 4177928 | tf_op jit(solution)/shard_map/ppermute | solution.py:33
  62.9 18.2 %collective-permute-start.7 = (f32[17,80,256]{2,1,0:T(8,128)S(1)}, f32[17,80,256]{2,1,0:T(8,128)S(1)}, u32[]{:S(2)}, u32[]{:S(2)}) collective-permute-start(f32[17,80,256]{2,1,0:T(8,128)S(1)} %broadcast_select_fusion.own_ref), channel_id=1, source_target_pairs={{0,8},{1,9},{2,10},{3,11},{4,12},{5,13},{6,14},{7,15},{8,0},{9,1},... | collective-permute-start | bytes 4177928 | tf_op jit(solution)/shard_map/ppermute | solution.py:33
  63.6 32.5 %collective-permute-start.12 = (f32[17,80,256]{2,1,0:T(8,128)S(1)}, f32[17,80,256]{2,1,0:T(8,128)S(1)}, u32[]{:S(2)}, u32[]{:S(2)}) collective-permute-start(f32[17,80,256]{2,1,0:T(8,128)S(1)} %collective-permute-done.11.own_ref), channel_id=1, source_target_pairs={{2,8},{3,9},{4,10},{5,11},{6,12},{7,13},{8,2},{9,3},{10,4},{11,5},... | collective-permute-start | bytes 4177928 | tf_op jit(solution)/shard_map/ppermute | solution.py:33
  66.7 29.4 %collective-permute-start.13 = (f32[17,80,256]{2,1,0:T(8,128)S(1)}, f32[17,80,256]{2,1,0:T(8,128)S(1)}, u32[]{:S(2)}, u32[]{:S(2)}) collective-permute-start(f32[17,80,256]{2,1,0:T(8,128)S(1)} %collective-permute-done.11.own_ref), channel_id=1, source_target_pairs={{0,8},{1,9},{2,10},{3,11},{4,12},{5,13},{6,14},{7,15},{8,0},{9,1},... | collective-permute-start | bytes 4177928 | tf_op jit(solution)/shard_map/ppermute | solution.py:33
  84.9 16.4 %collective-permute-start.10 = (f32[15,64,256]{2,1,0:T(8,128)S(1)}, f32[15,64,256]{2,1,0:T(8,128)S(1)}, u32[]{:S(2)}, u32[]{:S(2)}) collective-permute-start(f32[15,64,256]{2,1,0:T(8,128)S(1)} %get-tuple-element.81), channel_id=1, source_target_pairs={{0,8},{1,9},{2,10},{3,11},{4,12},{5,13},{6,14},{7,15},{8,0},{9,1},... | collective-permute-start | bytes 2949128 | tf_op jit(solution)/shard_map/ppermute | solution.py:33
  85.1 21.5 %collective-permute-start.9 = (f32[15,64,256]{2,1,0:T(8,128)S(1)}, f32[15,64,256]{2,1,0:T(8,128)S(1)}, u32[]{:S(2)}, u32[]{:S(2)}) collective-permute-start(f32[15,64,256]{2,1,0:T(8,128)S(1)} %get-tuple-element.80), channel_id=1, source_target_pairs={{2,8},{3,9},{4,10},{5,11},{6,12},{7,13},{8,2},{9,3},{10,4},{11,5},... | collective-permute-start | bytes 2949128 | tf_op jit(solution)/shard_map/ppermute | solution.py:33
  98.7 10.0 %copy-start.4 = (f32[16,80,256]{2,1,0:T(8,128)}, f32[16,80,256]{2,1,0:T(8,128)S(1)}, u32[]{:S(2)}) copy-start(f32[16,80,256]{2,1,0:T(8,128)S(1)} %get-tuple-element.91.refs_1_) | copy-start | bytes 3932164
  98.8 12.9 %collective-permute-start.14 = (f32[15,32,256]{2,1,0:T(8,128)S(1)}, f32[15,32,256]{2,1,0:T(8,128)S(1)}, u32[]{:S(2)}, u32[]{:S(2)}) collective-permute-start(f32[15,32,256]{2,1,0:T(8,128)S(1)} %get-tuple-element.86), channel_id=1, source_target_pairs={{2,8},{3,9},{4,10},{5,11},{6,12},{7,13},{8,2},{9,3},{10,4},{11,5},... | collective-permute-start | bytes 1474568 | tf_op jit(solution)/shard_map/ppermute | solution.py:33
  100.7 11.0 %collective-permute-start.15 = (f32[15,32,256]{2,1,0:T(8,128)S(1)}, f32[15,32,256]{2,1,0:T(8,128)S(1)}, u32[]{:S(2)}, u32[]{:S(2)}) collective-permute-start(f32[15,32,256]{2,1,0:T(8,128)S(1)} %get-tuple-element.87), channel_id=1, source_target_pairs={{0,8},{1,9},{2,10},{3,11},{4,12},{5,13},{6,14},{7,15},{8,0},{9,1},... | collective-permute-start | bytes 1474568 | tf_op jit(solution)/shard_map/ppermute | solution.py:33
  112.7 13.2 %collective-permute-start.16 = (f32[16,32,256]{2,1,0:T(8,128)S(1)}, f32[16,32,256]{2,1,0:T(8,128)S(1)}, u32[]{:S(2)}, u32[]{:S(2)}) collective-permute-start(f32[16,32,256]{2,1,0:T(8,128)S(1)} %log_factor.6.refs_0_), channel_id=1, source_target_pairs={{0,16},{1,17},{2,18},{3,19},{4,20},{5,21},{6,22},{7,23},{8,24},{9,... | collective-permute-start | bytes 1572872 | tf_op jit(solution)/shard_map/ppermute | solution.py:33
  114.0 10.4 %collective-permute-start.17 = (f32[15,32,256]{2,1,0:T(8,128)S(1)}, f32[15,32,256]{2,1,0:T(8,128)S(1)}, u32[]{:S(2)}, u32[]{:S(2)}) collective-permute-start(f32[15,32,256]{2,1,0:T(8,128)S(1)} %get-tuple-element.92), channel_id=1, source_target_pairs={{2,8},{3,9},{4,10},{5,11},{6,12},{7,13},{8,2},{9,3},{10,4},{11,5},... | collective-permute-start | bytes 1474568 | tf_op jit(solution)/shard_map/ppermute | solution.py:33
  116.3 8.2 %collective-permute-start.18 = (f32[15,32,256]{2,1,0:T(8,128)S(1)}, f32[15,32,256]{2,1,0:T(8,128)S(1)}, u32[]{:S(2)}, u32[]{:S(2)}) collective-permute-start(f32[15,32,256]{2,1,0:T(8,128)S(1)} %get-tuple-element.93), channel_id=1, source_target_pairs={{0,8},{1,9},{2,10},{3,11},{4,12},{5,13},{6,14},{7,15},{8,0},{9,1},... | collective-permute-start | bytes 1474568 | tf_op jit(solution)/shard_map/ppermute | solution.py:33
  125.5 13.3 %collective-permute-start.19 = (f32[16,32,256]{2,1,0:T(8,128)S(1)}, f32[16,32,256]{2,1,0:T(8,128)}, u32[]{:S(2)}, u32[]{:S(2)}) collective-permute-start(f32[16,32,256]{2,1,0:T(8,128)S(1)} %log_factor.7.refs_0_), channel_id=1, source_target_pairs={{0,16},{1,17},{2,18},{3,19},{4,20},{5,21},{6,22},{7,23},{8,24},{9,... | collective-permute-start | bytes 1572872 | tf_op jit(solution)/shard_map/ppermute | solution.py:33
  127.7 15.6 %collective-permute-start.24 = (f32[16,32,256]{2,1,0:T(8,128)S(1)}, f32[16,32,256]{2,1,0:T(8,128)S(1)}, u32[]{:S(2)}, u32[]{:S(2)}) collective-permute-start(f32[16,32,256]{2,1,0:T(8,128)S(1)} %get-tuple-element.89.own_ref.before_ref), channel_id=1, source_target_pairs={{0,1},{1,0},{2,3},{3,2},{4,5},{5,4},{6,7},{7,6},{8,9},{9,8},{10,11... | collective-permute-start | bytes 1572872 | tf_op jit(solution)/shard_map/ppermute | solution.py:33
  131.5 13.0 %collective-permute-start.23 = (f32[15,32,256]{2,1,0:T(8,128)}, f32[15,32,256]{2,1,0:T(8,128)}, u32[]{:S(2)}, u32[]{:S(2)}) collective-permute-start(f32[15,32,256]{2,1,0:T(8,128)} %get-tuple-element.101), channel_id=1, source_target_pairs={{0,8},{1,9},{2,10},{3,11},{4,12},{5,13},{6,14},{7,15},{8,0},{9,1},... | collective-permute-start | bytes 1474568 | tf_op jit(solution)/shard_map/ppermute | solution.py:33
  132.6 17.8 %collective-permute-start.22 = (f32[15,32,256]{2,1,0:T(8,128)}, f32[15,32,256]{2,1,0:T(8,128)S(1)}, u32[]{:S(2)}, u32[]{:S(2)}) collective-permute-start(f32[15,32,256]{2,1,0:T(8,128)} %copy-done.10), channel_id=1, source_target_pairs={{2,8},{3,9},{4,10},{5,11},{6,12},{7,13},{8,2},{9,3},{10,4},{11,5},... | collective-permute-start | bytes 1474568 | tf_op jit(solution)/shard_map/ppermute | solution.py:33
  140.1 9.2 %collective-permute-start.21 = (f32[15,32,256]{2,1,0:T(8,128)S(1)}, f32[15,32,256]{2,1,0:T(8,128)S(1)}, u32[]{:S(2)}, u32[]{:S(2)}) collective-permute-start(f32[15,32,256]{2,1,0:T(8,128)S(1)} %get-tuple-element.96), channel_id=1, source_target_pairs={{0,8},{1,9},{2,10},{3,11},{4,12},{5,13},{6,14},{7,15},{8,0},{9,1},... | collective-permute-start | bytes 1474568 | tf_op jit(solution)/shard_map/ppermute | solution.py:33
  141.3 10.4 %collective-permute-start.20 = (f32[15,32,256]{2,1,0:T(8,128)S(1)}, f32[15,32,256]{2,1,0:T(8,128)S(1)}, u32[]{:S(2)}, u32[]{:S(2)}) collective-permute-start(f32[15,32,256]{2,1,0:T(8,128)S(1)} %get-tuple-element.94), channel_id=1, source_target_pairs={{2,8},{3,9},{4,10},{5,11},{6,12},{7,13},{8,2},{9,3},{10,4},{11,5},... | collective-permute-start | bytes 1474568 | tf_op jit(solution)/shard_map/ppermute | solution.py:33
  143.4 9.5 %collective-permute-start.26 = (f32[15,32,256]{2,1,0:T(8,128)S(1)}, f32[15,32,256]{2,1,0:T(8,128)S(1)}, u32[]{:S(2)}, u32[]{:S(2)}) collective-permute-start(f32[15,32,256]{2,1,0:T(8,128)S(1)} %get-tuple-element.117), channel_id=1, source_target_pairs={{0,8},{1,9},{2,10},{3,11},{4,12},{5,13},{6,14},{7,15},{8,0},{9,1},... | collective-permute-start | bytes 1474568 | tf_op jit(solution)/shard_map/ppermute | solution.py:33
  144.5 12.2 %collective-permute-start.25 = (f32[15,32,256]{2,1,0:T(8,128)S(1)}, f32[15,32,256]{2,1,0:T(8,128)S(1)}, u32[]{:S(2)}, u32[]{:S(2)}) collective-permute-start(f32[15,32,256]{2,1,0:T(8,128)S(1)} %get-tuple-element.118), channel_id=1, source_target_pairs={{2,8},{3,9},{4,10},{5,11},{6,12},{7,13},{8,2},{9,3},{10,4},{11,5},... | collective-permute-start | bytes 1474568 | tf_op jit(solution)/shard_map/ppermute | solution.py:33
  152.8 5.0 %copy-start.5 = (f32[16,80,256]{2,1,0:T(8,128)S(1)}, f32[16,80,256]{2,1,0:T(8,128)}, u32[]{:S(2)}) copy-start(f32[16,80,256]{2,1,0:T(8,128)} %copy-done.4) | copy-start | bytes 3932164
  153.9 3.9 %copy-start.3 = (f32[16,80,256]{2,1,0:T(8,128)S(1)}, f32[16,80,256]{2,1,0:T(8,128)}, u32[]{:S(2)}) copy-start(f32[16,80,256]{2,1,0:T(8,128)} %copy-done.2) | copy-start | bytes 3932164
  153.9 3.9 %copy-start.7 = (bf16[2,64,256]{2,1,0:T(8,128)(2,1)S(1)}, bf16[2,64,256]{2,1,0:T(8,128)(2,1)}, u32[]{:S(2)}) copy-start(bf16[2,64,256]{2,1,0:T(8,128)(2,1)} %copy-done.6) | copy-start | bytes 196612
  165.2 15.7 %collective-permute-start.33 = (f32[2,15,32,256]{3,2,1,0:T(8,128)S(1)}, f32[2,15,32,256]{3,2,1,0:T(8,128)S(1)}, u32[]{:S(2)}, u32[]{:S(2)}) collective-permute-start(f32[2,15,32,256]{3,2,1,0:T(8,128)S(1)} %get-tuple-element.115), channel_id=1, source_target_pairs={{2,8},{3,9},{4,10},{5,11},{6,12},{7,13},{8,2},{9,3},{10,4},{11,5},... | collective-permute-start | bytes 2949128 | tf_op jit(solution)/shard_map/ppermute | solution.py:33
  167.1 13.8 %collective-permute-start.34 = (f32[2,15,32,256]{3,2,1,0:T(8,128)S(1)}, f32[2,15,32,256]{3,2,1,0:T(8,128)S(1)}, u32[]{:S(2)}, u32[]{:S(2)}) collective-permute-start(f32[2,15,32,256]{3,2,1,0:T(8,128)S(1)} %get-tuple-element.116), channel_id=1, source_target_pairs={{0,8},{1,9},{2,10},{3,11},{4,12},{5,13},{6,14},{7,15},{8,0},{9,1},... | collective-permute-start | bytes 2949128 | tf_op jit(solution)/shard_map/ppermute | solution.py:33
  167.9 23.6 %collective-permute-start.27 = (f32[2,15,32,256]{3,2,1,0:T(8,128)S(1)}, f32[2,15,32,256]{3,2,1,0:T(8,128)S(1)}, u32[]{:S(2)}, u32[]{:S(2)}) collective-permute-start(f32[2,15,32,256]{3,2,1,0:T(8,128)S(1)} %get-tuple-element.111), channel_id=1, source_target_pairs={{2,8},{3,9},{4,10},{5,11},{6,12},{7,13},{8,2},{9,3},{10,4},{11,5},... | collective-permute-start | bytes 2949128 | tf_op jit(solution)/shard_map/ppermute | solution.py:33
  170.8 20.6 %collective-permute-start.28 = (f32[2,15,32,256]{3,2,1,0:T(8,128)S(1)}, f32[2,15,32,256]{3,2,1,0:T(8,128)S(1)}, u32[]{:S(2)}, u32[]{:S(2)}) collective-permute-start(f32[2,15,32,256]{3,2,1,0:T(8,128)S(1)} %get-tuple-element.112), channel_id=1, source_target_pairs={{0,8},{1,9},{2,10},{3,11},{4,12},{5,13},{6,14},{7,15},{8,0},{9,1},... | collective-permute-start | bytes 2949128 | tf_op jit(solution)/shard_map/ppermute | solution.py:33
  182.6 16.1 %collective-permute-start.35 = (f32[16,32,256]{2,1,0:T(8,128)S(1)}, f32[16,32,256]{2,1,0:T(8,128)S(1)}, u32[]{:S(2)}, u32[]{:S(2)}) collective-permute-start(f32[16,32,256]{2,1,0:T(8,128)S(1)} %log_factor.9.refs_0_), channel_id=1, source_target_pairs={{0,16},{2,18},{4,20},{6,22},{9,25},{11,27},{13,29},{15,31},{16,0},... | collective-permute-start | bytes 1572872 | tf_op jit(solution)/shard_map/ppermute | solution.py:33
  183.3 17.3 %collective-permute-start.36 = (f32[16,32,256]{2,1,0:T(8,128)S(1)}, f32[16,32,256]{2,1,0:T(8,128)S(1)}, u32[]{:S(2)}, u32[]{:S(2)}) collective-permute-start(f32[16,32,256]{2,1,0:T(8,128)S(1)} %log_factor.9.refs_0_), channel_id=1, source_target_pairs={{1,24},{3,26},{5,28},{7,30},{8,17},{10,19},{12,21},{14,23},{17,8},... | collective-permute-start | bytes 1572872 | tf_op jit(solution)/shard_map/ppermute | solution.py:33
  188.1 16.4 %collective-permute-start.37 = (f32[16,32,256]{2,1,0:T(8,128)S(1)}, f32[16,32,256]{2,1,0:T(8,128)S(1)}, u32[]{:S(2)}, u32[]{:S(2)}) collective-permute-start(f32[16,32,256]{2,1,0:T(8,128)S(1)} %log_factor.9.refs_0_), channel_id=1, source_target_pairs={{1,8},{3,10},{5,12},{7,14},{8,1},{10,3},{12,5},{14,7},{17,24},{19,... | collective-permute-start | bytes 1572872 | tf_op jit(solution)/shard_map/ppermute | solution.py:33
  193.1 11.6 %collective-permute-start.29 = (f32[16,32,256]{2,1,0:T(8,128)S(1)}, f32[16,32,256]{2,1,0:T(8,128)S(1)}, u32[]{:S(2)}, u32[]{:S(2)}) collective-permute-start(f32[16,32,256]{2,1,0:T(8,128)S(1)} %log_factor.8.refs_0_), channel_id=1, source_target_pairs={{0,16},{2,18},{4,20},{6,22},{9,25},{11,27},{13,29},{15,31},{16,0},... | collective-permute-start | bytes 1572872 | tf_op jit(solution)/shard_map/ppermute | solution.py:33
  193.8 17.4 %collective-permute-start.30 = (f32[16,32,256]{2,1,0:T(8,128)S(1)}, f32[16,32,256]{2,1,0:T(8,128)S(1)}, u32[]{:S(2)}, u32[]{:S(2)}) collective-permute-start(f32[16,32,256]{2,1,0:T(8,128)S(1)} %log_factor.8.refs_0_), channel_id=1, source_target_pairs={{1,24},{3,26},{5,28},{7,30},{8,17},{10,19},{12,21},{14,23},{17,8},... | collective-permute-start | bytes 1572872 | tf_op jit(solution)/shard_map/ppermute | solution.py:33
  198.7 14.7 %collective-permute-start.31 = (f32[16,32,256]{2,1,0:T(8,128)S(1)}, f32[16,32,256]{2,1,0:T(8,128)S(1)}, u32[]{:S(2)}, u32[]{:S(2)}) collective-permute-start(f32[16,32,256]{2,1,0:T(8,128)S(1)} %log_factor.8.refs_0_), channel_id=1, source_target_pairs={{1,8},{3,10},{5,12},{7,14},{8,1},{10,3},{12,5},{14,7},{17,24},{19,... | collective-permute-start | bytes 1572872 | tf_op jit(solution)/shard_map/ppermute | solution.py:33
  204.6 8.9 %collective-permute-start.38 = (f32[16,32,256]{2,1,0:T(8,128)S(1)}, f32[16,32,256]{2,1,0:T(8,128)S(1)}, u32[]{:S(2)}, u32[]{:S(2)}) collective-permute-start(f32[16,32,256]{2,1,0:T(8,128)S(1)} %last_update.3.refs_2_), channel_id=1, source_target_pairs={{0,8},{1,9},{2,10},{3,11},{4,12},{5,13},{6,14},{7,15},{8,0},{9,1},... | collective-permute-start | bytes 1572872 | tf_op jit(solution)/shard_map/ppermute | solution.py:33
  213.5 2.0 collective-permute-start.32
  (5 other events, 7.5 us)

commit v9 on v8

--- a/solution.py
+++ b/solution.py
@@ -1,4 +1,5 @@
 import functools
+import typing
 
 import jax
 import jax.numpy as jnp
@@ -105,6 +106,14 @@
     )
 
 
+class Tables(typing.NamedTuple):
+    whole: tuple
+    inner: tuple
+    edge: tuple
+    z: tuple
+    x: tuple
+
+
 def place(row, count, width, turned, spacing):
     source, target = iota((row.shape[1], width), 0), iota((row.shape[1], width), 1)
     index = count - 1 - source if turned else source
@@ -112,31 +121,32 @@
     return jnp.dot(row, ones.astype(F32), precision=lax.Precision.HIGHEST, preferred_element_type=F32)
 
 
-def tables_kernel(mine_ref, other_ref, yf_ref, ya_ref, zhi_ref, zlo_ref, xhi_ref, xlo_ref, *, sizes, cells_y, taps):
+def tables_kernel(mine_ref, other_ref, *refs, blocks, sizes, cells_y, taps):
+    y_refs, (zhi_ref, zlo_ref, xhi_ref, xlo_ref) = refs[:-4], refs[-4:]
     taps_x, taps_y, taps_z = taps
     straight = core() == half()
     mine, other = mine_ref[...], other_ref[...]
     both = (jnp.where(straight, mine, other), jnp.where(straight, other, mine))
     radius, radius_x, radius_z = taps_y // 2, taps_x // 2, taps_z // 2
     side = half()
-    own, near, wide = sizes
-    for index in range(4):
-        adjoint = index >= 2
-        out_ref, rows, width = (ya_ref, own, near) if adjoint else (yf_ref, near, wide)
-        lanes = out_ref.shape[2]
-        row = global_row(side, iota((rows, lanes), 0), cells_y)
+    own, wide = sizes
+    for out_ref, adjoint, first_row, first_col, width in zip(y_refs, *zip(*blocks)):
+        _, rows, lanes = out_ref.shape
+        row = global_row(side, first_row + iota((rows, lanes), 0), cells_y)
         lane = iota((rows, lanes), 1)
-        turned = lane if adjoint else jnp.where(lane < own, lane, wide_local(lane, own, wide))
+        place_of = lane + first_col
+        turned = place_of if adjoint else jnp.where(place_of < own, place_of, wide_local(place_of, own, wide))
         col = global_row(side, turned, cells_y)
         delta = (row - col if adjoint else col - row) + radius
         delta = jnp.where(lane < width, delta, -1)
-        band = jnp.zeros((rows, lanes), F32)
-        values = both[index % 2][:, 128:256]
-        for a in range(taps_y):
-            band = jnp.where(delta == a, jnp.broadcast_to(values[:, a:a + 1], (rows, lanes)), band)
-        high, low = split(band)
-        high, low = high.astype(F32), low.astype(F32)
-        out_ref[index % 2] = (high + pltpu.roll(high, width, 1) + pltpu.roll(low, 2 * width, 1)).astype(BF16)
+        for order in range(2):
+            band = jnp.zeros((rows, lanes), F32)
+            values = both[order][:, 128:256]
+            for a in range(taps_y):
+                band = jnp.where(delta == a, jnp.broadcast_to(values[:, a:a + 1], (rows, lanes)), band)
+            high, low = split(band)
+            high, low = high.astype(F32), low.astype(F32)
+            out_ref[order] = (high + pltpu.roll(high, width, 1) + pltpu.roll(low, 2 * width, 1)).astype(BF16)
 
     lanes = zhi_ref.shape[2]
     near_z = jnp.abs(iota((lanes, lanes), 1) - iota((lanes, lanes), 0)) <= radius_z
@@ -169,19 +179,28 @@
 
 def make_tables(mine, other, taps, planes, cells_y, cells_z, sizes):
     own, near, wide = sizes
+    inner, beyond = 2 * own - wide, near - own
     radius = taps[0] // 2
     depth = pad_to(8 * (planes + radius), 128) + pad_to(8 * radius, 128)
-    kernel = functools.partial(tables_kernel, sizes=sizes, cells_y=cells_y, taps=taps)
+    blocks = [
+        (False, near, 0, 0, wide), (True, own, 0, 0, near),
+        (False, inner + beyond, 0, 0, own), (True, inner, 0, 0, inner + beyond),
+        (False, near - inner - beyond, inner + beyond, inner, wide - inner),
+        (True, own - inner, inner, inner - beyond, near - inner + beyond),
+    ]
+    kernel = functools.partial(
+        tables_kernel, blocks=[block[:1] + block[2:] for block in blocks], sizes=(own, wide), cells_y=cells_y, taps=taps
+    )
     shape = jax.ShapeDtypeStruct
-    out_shape = (
-        shape((2, near, pad_to(3 * wide, 128)), BF16),
-        shape((2, own, pad_to(3 * near, 128)), BF16),
+    out_shape = tuple(shape((2, block[1], pad_to(3 * block[4], 128)), BF16) for block in blocks) + (
         shape((4, cells_z, cells_z), BF16),
         shape((4, cells_z, cells_z), BF16),
         shape((2, 2 * 8 * planes, depth), BF16),
         shape((2, 2 * 8 * planes, depth), BF16),
     )
-    return call(kernel, out_shape, [VMEM, VMEM], "band_matrices")(mine, other)
+    tables = call(kernel, out_shape, [VMEM, VMEM], "band_matrices")(mine, other)
+    whole, inner_rows, edge_rows = tables[0:2], tables[2:4], tables[4:6]
+    return Tables(whole, inner_rows, edge_rows, tables[6:8], tables[8:10])
 
 
 def window_kernel(estimate_ref, own_ref, other_ref):
@@ -211,18 +230,10 @@
         end -= far_ref.shape[1]
 
 
-def assemble_kernel(*refs, count):
-    pieces, window, out_ref, edge_refs = refs[:count], refs[count:-1], refs[-1], ()
-    if len(refs) > count + 1:
-        window, out_ref, edge_refs = refs[count], refs[count + 1], refs[count + 2:]
-    straight, group = core() == half(), lax.axis_index("view") // 2
-    planes, share = out_ref.shape[0], pieces[0].shape[0]
-    for p in range(planes):
-        turn = lax.rem(group - p // share + count, count)
-        value = pieces[0][p % share]
-        for k in range(1, count):
-            value = jnp.where(turn == k, pieces[k][p % share], value)
-        out_ref[p] = jnp.where(straight, window[p], value) if edge_refs else value
+def choose_kernel(window_ref, crossed_ref, out_ref, *edge_refs):
+    straight = core() == half()
+    for p in range(out_ref.shape[0]):
+        out_ref[p] = jnp.where(straight, window_ref[p], crossed_ref[p])
     put_edges(out_ref, edge_refs)
 
 
@@ -232,17 +243,9 @@
     return (jax.ShapeDtypeStruct(shape, F32), *edges)
 
 
-def assemble(window, pieces, radius):
+def choose(window, crossed, radius):
     out_shape = edge_shapes(window.shape, radius, window.shape[1:2])
-    kernel = functools.partial(assemble_kernel, count=len(pieces))
-    return call(kernel, out_shape, [VMEM] * (1 + len(pieces)), "estimate")(*pieces, window)
-
-
-def assemble_far(pieces):
-    share, rows, lanes = pieces[0].shape
-    shape = jax.ShapeDtypeStruct((share * len(pieces), rows, lanes), F32)
-    kernel = functools.partial(assemble_kernel, count=len(pieces))
-    return call(kernel, (shape,), [VMEM] * len(pieces), "far_slab")(*pieces)[0]
+    return call(choose_kernel, out_shape, [VMEM] * 2, "estimate")(window, crossed)
 
 
 def shift_kernel(offsets_ref, acq_ref, mask_ref, first_ref, second_ref, turned_ref):
@@ -278,11 +281,8 @@
     return call(shift_kernel, (shape, shape), [SMEM, VMEM, VMEM], "shift_recorded", scratch)(offsets, acquired, mask)
 
 
-def gather(ref, row, radius=None):
-    rows = pl.ds(pl.multiple_of(row, 8), 8)
-    if radius is None or ref.shape[0] == radius:
-        return ref[:, rows, :]
-    return ref[pl.ds((1 - core()) * (ref.shape[0] - radius), radius), rows, :]
+def gather(ref, row):
+    return ref[:, pl.ds(pl.multiple_of(row, 8), 8), :]
 
 
 def spread_x(hi_ref, lo_ref, index, band_rows, band_lanes, blocks):
@@ -317,14 +317,14 @@
     lax.fori_loop(0, rows // 8, body, 0)
 
 
-def blur_far_kernel(hi_ref, lo_ref, far_ref, first_ref, second_ref, first_out, second_out, *, radius):
+def blur_far_kernel(hi_ref, lo_ref, far_ref, first_ref, second_ref, first_out, second_out):
     planes, rows, _ = first_ref.shape
-    lanes = slice(near_lanes(planes, radius), None)
+    lanes = slice(near_lanes(planes, far_ref.shape[0]), None)
 
     def body(step, carry):
         row = pl.multiple_of(step * 8, 8)
         place = (slice(None), pl.ds(row, 8), slice(None))
-        out = spread_x(hi_ref, lo_ref, 0, slice(None), lanes, [[gather(far_ref, row, radius)]])
+        out = spread_x(hi_ref, lo_ref, 0, slice(None), lanes, [[gather(far_ref, row)]])
         first_out[place] = first_ref[place] + out[:planes]
         second_out[place] = second_ref[place] + out[planes:]
         return carry
@@ -334,13 +334,12 @@
 
 def blur_near(tables, own, near):
     shape = jax.ShapeDtypeStruct(own.shape, F32)
-    return call(blur_near_kernel, (shape, shape), [VMEM] * 4, "blur_x_near")(*tables[4:], own, near)
-
-
-def blur_far(tables, far, parts, radius):
+    return call(blur_near_kernel, (shape, shape), [VMEM] * 4, "blur_x_near")(*tables.x, own, near)
+
+
+def blur_far(tables, far, parts):
     shape = jax.ShapeDtypeStruct(parts[0].shape, F32)
-    kernel = functools.partial(blur_far_kernel, radius=radius)
-    return call(kernel, (shape, shape), [VMEM] * 5, "blur_x_far")(*tables[4:], far, *parts)
+    return call(blur_far_kernel, (shape, shape), [VMEM] * 5, "blur_x_far")(*tables.x, far, *parts)
 
 
 def spread_y(band, x):
@@ -378,21 +377,22 @@
 
 def blur_yz(wides, tables, order):
     planes, _, lanes = wides[0].shape
-    shape = jax.ShapeDtypeStruct((planes, tables[0].shape[1], lanes), F32)
+    shape = jax.ShapeDtypeStruct((planes, tables.whole[0].shape[1], lanes), F32)
     kernel = functools.partial(blur_yz_kernel, order=order)
-    return call(kernel, shape, [VMEM] * (3 + len(wides)), "blur_yz")(*wides, tables[0], *tables[2:4])
-
-
-def adjoint_planes(blurred_of, image_of, ya_ref, zhi_ref, zlo_ref, order, out_ref, edge_refs):
+    return call(kernel, shape, [VMEM] * (3 + len(wides)), "blur_yz")(*wides, tables.whole[0], *tables.z)
+
+
+def adjoint_planes(blurred_of, image_of, ya_ref, zhi_ref, zlo_ref, order, out_ref, edge_refs, complete=None):
     planes, rows, _ = out_ref.shape
     for block in plane_blocks(planes):
         blurred = blurred_of(block)
         image = jnp.concatenate([image_of(p) for p in block], axis=0)
         ratio = jnp.where(image >= 0, image / blurred, jnp.ones_like(image))
         near = ratio.shape[0] // len(block)
-        spread = jnp.concatenate(
-            [spread_y(ya_ref[order], ratio[k * near:(k + 1) * near]) for k in range(len(block))], axis=0
-        )
+        ratios = [ratio[k * near:(k + 1) * near] for k in range(len(block))]
+        if complete:
+            ratios = [complete(p, rows_of) for p, rows_of in zip(block, ratios)]
+        spread = jnp.concatenate([spread_y(ya_ref[order], rows_of) for rows_of in ratios], axis=0)
         spread = spread_z(spread, zhi_ref, zlo_ref, 2 + order)
         for k, p in enumerate(block):
             out_ref[p] = spread[k * rows:(k + 1) * rows]
@@ -444,44 +444,54 @@
     adjoint_planes(blurred_of, fetch, ya_ref, zhi_ref, zlo_ref, order, out_ref, edge_refs)
 
 
-def next_ratio_kernel(*refs, wides):
-    image_refs, refs = refs[:2], refs[2:]
-    wide_refs, refs = (refs[:wides], refs[wides:2 * wides]), refs[2 * wides:]
-    (yf_ref, ya_ref, zhi_ref, zlo_ref), out_refs, edge_refs = refs[:4], refs[4:6], refs[6:]
+def next_ratio_kernel(*refs, inner, count, first_row):
+    image_refs, wide_refs, refs = refs[:2], (refs[2:4], refs[4:6]), refs[6:]
+    passed_ref, refs = (None, refs) if inner else (refs[0], refs[1:])
+    (yf_ref, ya_ref, zhi_ref, zlo_ref), out_refs, (far_ref, near_ref), refs = refs[:4], refs[4:6], refs[6:8], refs[8:]
+    planes = out_refs[0].shape[0]
+    rows = yf_ref.shape[1]
     for order in range(2):
 
-        def blurred_of(block, order=order):
+        def blurred_of(block):
             return blurred_planes(wide_refs[order], yf_ref, zhi_ref, zlo_ref, order, block)
 
-        def image_of(p, order=order):
-            return image_refs[order][p]
-
-        edges = [ref.at[order] for ref in edge_refs]
-        adjoint_planes(blurred_of, image_of, ya_ref, zhi_ref, zlo_ref, order, out_refs[order], edges)
-
-
-def ratio_shapes(planes, lanes, tables, radius, chunks):
-    return edge_shapes((planes, tables[1].shape[1], lanes), radius, chunks)
+        def image_of(p):
+            return image_refs[order][p, first_row:first_row + rows]
+
+        def complete(p, ratio):
+            if inner:
+                refs[0][order, p] = ratio[rows - count:]
+                return ratio
+            return jnp.concatenate([passed_ref[order, p], ratio], axis=0)
+
+        edges = (far_ref.at[order], near_ref.at[order])
+        adjoint_planes(blurred_of, image_of, ya_ref, zhi_ref, zlo_ref, order, out_refs[order], edges, complete)
+
+
+def next_ratio(images, wides, passed, y_tables, z_tables, radius, count, first_row):
+    planes, _, lanes = images[0].shape
+    rows = y_tables[1].shape[1]
+    kernel = functools.partial(next_ratio_kernel, inner=passed is None, count=count, first_row=first_row)
+    shape = jax.ShapeDtypeStruct
+    whole, edge = shape((planes, rows, lanes), F32), shape((2, radius, rows, lanes), F32)
+    out_shape = (whole, whole, edge, edge)
+    if passed is None:
+        out_shape += (shape((2, planes, count, lanes), F32),)
+    operands = [*images, *wides[0], *wides[1]] + ([] if passed is None else [passed]) + [*y_tables, *z_tables]
+    return call(kernel, out_shape, [VMEM] * len(operands), "ratio")(*operands)
 
 
 def first_ratio(shifts, blocks, blurred, tables, order, radius, chunks, extent_x, cells_y):
     planes, near, lanes = blurred.shape
     kernel = functools.partial(first_ratio_kernel, order=order, extent_x=extent_x, cells_y=cells_y)
-    out_shape = ratio_shapes(planes, lanes, tables, radius, chunks) + (jax.ShapeDtypeStruct(blurred.shape, F32),)
+    rows = tables.whole[1].shape[1]
+    out_shape = edge_shapes((planes, rows, lanes), radius, chunks) + (jax.ShapeDtypeStruct(blurred.shape, F32),)
     scratch = [
         pltpu.VMEM((planes + 1, near, lanes), F32), pltpu.VMEM(blurred.shape, F32), pltpu.SemaphoreType.DMA((2,))
     ]
     in_specs = [SMEM] + [pl.BlockSpec(memory_space=pl.ANY)] * 3 + [VMEM] * 4
-    return call(kernel, out_shape, in_specs, "image_and_ratio", scratch)(shifts, *blocks, blurred, *tables[1:4])
-
-
-def next_ratio(images, wides, tables, radius, chunks):
-    planes, _, lanes = images[0].shape
-    kernel = functools.partial(next_ratio_kernel, wides=len(wides[0]))
-    whole, *edges = ratio_shapes(planes, lanes, tables, radius, chunks)
-    edges = [jax.ShapeDtypeStruct((2,) + edge.shape, F32) for edge in edges]
-    return call(kernel, (whole, whole, *edges), [VMEM] * (6 + 2 * len(wides[0])), "ratio")(
-        *images, *wides[0], *wides[1], *tables[:4]
+    return call(kernel, out_shape, in_specs, "image_and_ratio", scratch)(
+        shifts, *blocks, blurred, tables.whole[1], *tables.z
     )
 
 
@@ -513,7 +523,7 @@
     planes, _, lanes = sides[0][2].shape
     shape = jax.ShapeDtypeStruct((planes, rows, lanes), F32)
     parts = [part for side in sides for part in side]
-    return call(kernel, shape, [VMEM] * (3 + len(parts)), "log_factor")(*tables[4:], before, *parts)
+    return call(kernel, shape, [VMEM] * (3 + len(parts)), "log_factor")(*tables.x, before, *parts)
 
 
 def update_kernel(*refs, count):
@@ -601,13 +611,11 @@
     def neighbours(far, near):
         return send(far, to_far), send(near, to_core_partner)
 
-    window, crossing = make_windows(estimate, wide)
-    piece = lax.dynamic_slice_in_dim(crossing, group * (planes // groups), planes // groups, 0)
-    piece = send(piece, across(0, lambda r: 1 - r, when=lambda c, r: c == r))
+    window, crossed = make_windows(estimate, wide)
+    crossed = send(crossed, across(0, lambda r: 1 - r, when=lambda c, r: c == r))
 
     acquired = after(acquired, window)
     first, second = shift_and_cut(offsets, acquired[0], view_mask[0], near)
-    piece = after(piece, first)
 
     mine = [jnp.pad(row, ((0, 0), (0, 128 - row.shape[1]))) for row in (kern_x, kern_y, kern_z, offsets.astype(F32))]
     mine = jnp.concatenate(mine, axis=1)
@@ -618,23 +626,17 @@
     shifts = shifts[:, 384:384 + offsets.shape[1]].astype(jnp.int32)
 
     arrived = send(first, lambda g, c, q, r: (g, r, q, c) if c != r else None)
-    start = group * (planes // groups)
-    share = jnp.where(straight, lax.dynamic_slice_in_dim(window, start, planes // groups, 0), piece)
-    later = after(after(piece, tables[0]), share)
-    pieces = [piece] + [send(later, across(turn, when=lambda c, r: c != r)) for turn in range(1, groups)]
-    share = send(share, to_far)
-    shares = [share] + [send(share, across(turn)) for turn in range(1, groups)]
-    second = send(after(second, share), lambda g, c, q, r: (g, r, q, 1 - c))
-    current, _, close = assemble(after(window, shares[-1]), pieces, radius)
-    chunks = [(assemble_far(shares), blur_near(tables, current, send(close, to_core_partner)))]
+    current, distant, close = choose(after(after(window, first), tables.whole[0]), crossed, radius)
+    distant = send(distant, to_far)
+    second = send(after(second, current), lambda g, c, q, r: (g, r, q, 1 - c))
     first = jnp.where(straight, first, arrived)
+    close = send(after(close, distant), to_core_partner)
     blocks = [(*neighbours(block, block), block) for block in (first, second)]
-    images = [None, None]
+    wide_parts = blur_far(tables, distant, blur_near(tables, current, close))
+    blurred = [blur_yz([part], tables, order) for order, part in enumerate(wide_parts)]
 
     row_chunks = [(inner_rows, edge_rows), (0, inner_rows)]
     share = 1.0 / groups
-    wide_parts = [blur_far(tables, *chunk, radius) for chunk in chunks]
-    blurred = [blur_yz([parts[order] for parts in wide_parts], tables, order) for order in range(2)]
     images, sides = [], []
     for order, chunk_sizes in enumerate(([own_rows], [edge_rows, inner_rows])):
         spread, *edges, image = first_ratio(
@@ -652,6 +654,8 @@
         chunks, before = [], []
         for total in totals:
             parts = [total] + [send(total, across(turn)) for turn in range(1, groups)]
+            if chunks:
+                parts[-1] = after(parts[-1], chunks[0][0])
             rows, distant, close = update(parts, radius)
             if total is totals[0]:
                 beyond = send(rows, to_row_partner)
@@ -663,20 +667,26 @@
             lax.dynamic_slice_in_dim(beyond, core() * rest, radius, 0),
             lax.dynamic_slice_in_dim(beyond, (1 - core()) * rest, radius, 0),
         )
-        chunks.append((distant, blur_near(tables, beyond, close)))
-        edge_parts, inner_parts, halo_parts = [blur_far(tables, *chunk, radius) for chunk in chunks]
-        wides = [[parts[order] for parts in (inner_parts, edge_parts, halo_parts)] for order in range(2)]
-        *spreads, edge_far, edge_near, inner_far, inner_near = next_ratio(
-            images, wides, tables, radius, [edge_rows, inner_rows]
+        edge_parts, inner_parts = [blur_far(tables, *chunk) for chunk in chunks]
+        *inner_spreads, distant_inner, close_inner, passed = next_ratio(
+            images, list(zip([after(after(part, distant), close) for part in inner_parts], edge_parts)), None, tables.inner, tables.z, radius, 2 * (near - own_rows), 0
         )
-        sides = [neighbours(edge_far, edge_near), neighbours(inner_far, inner_near)]
+        halo_parts = blur_far(tables, distant, blur_near(tables, beyond, close))
+        inner_side = neighbours(distant_inner, close_inner)
+        *edge_spreads, distant, close = next_ratio(
+            images, list(zip(edge_parts, halo_parts)), passed, tables.edge, tables.z, radius, 0,
+            inner_rows + near - own_rows,
+        )
+        edge_side = neighbours(distant, close)
         totals = [
-            log_factor(tables, estimate_rows, [(*side, spread) for spread in spreads], [0, 1], rows, (0, start), share)
-            for (start, rows), side, estimate_rows in zip(row_chunks, sides, before)
+            log_factor(tables, rows_of, [(*side, spread) for spread in spreads], [0, 1], rows, (0, 0), share)
+            for rows_of, side, spreads, rows in (
+                (before[0], edge_side, edge_spreads, edge_rows), (before[1], inner_side, inner_spreads, inner_rows)
+            )
         ]
 
     pieces = []
-    for own in totals:
+    for own in totals[::-1]:
         other_parts = [
             send(own, across(turn, lambda r: 1 - r, lambda c: 1 - c, lambda c, r: c != r))
             for turn in reversed(range(groups))
@@ -684,7 +694,7 @@
         own_parts = [own] + [send(own, across(turn, when=lambda c, r: c == r)) for turn in range(1, groups)]
         mine = finish(own_parts, other_parts)
         pieces += [mine, send(mine, to_core_partner)]
-    return join(pieces, [start for start, _ in row_chunks], estimate.shape)
+    return join(pieces, [start for start, _ in row_chunks[::-1]], estimate.shape)
 
 
 def solution(mesh):

time: 218 us -> 218 us (level)
  Pallas kernels: 48.8 us -> 53.6 us
  starting transfers between devices: 61.3 us -> 57.8 us
    ppermute x39 -> x37, starting transfers between devices: 61.3 us -> 57.8 us  [send(): return lax.ppermute(array, AXES, moves(move))]
    pallas_call x8, Pallas kernels: 18.1 us -> 21.4 us  [the longest x2 9.35 us: next_ratio(): return call(kernel, out_shape, [VMEM] * len(operands), 'ratio')(*operands)]
    ppermute x39 -> x37, waiting for transfers between devices: 98.3 us -> 96.4 us  [send(): return lax.ppermute(array, AXES, moves(move))]
    unnamed x28 -> x42, local copies, waits for them, and re-layouts: 5.06 us -> 4.78 us
  transfers between devices with their start and end apart: 39 -> 37, of which waited for: 19 -> 17; matrix products, arithmetic and copies ran while one was open for 0% -> 2% of each run, Pallas kernels for 17% -> 20%
where the time goes in v9:
time: 218 us; the launch traced here: 217 us
  waiting for transfers between devices  96.4 us (44%)
  starting transfers between devices  57.8 us (27%)
  Pallas kernels  53.6 us (25%)
  local copies, waits for them, and re-layouts  6.18 us (3%)
  other arithmetic  2.21 us (1%)
    ppermute x37, waiting for transfers between devices, send(): return lax.ppermute(array, AXES, moves(move))  96.4 us
    ppermute x37, starting transfers between devices, send(): return lax.ppermute(array, AXES, moves(move))  57.8 us
    pallas_call x2, Pallas kernels, next_ratio(): return call(kernel, out_shape, [VMEM] * len(operands), 'ratio')(*operands)  9.35 us
    pallas_call x4, Pallas kernels, blur_far(): call(blur_far_kernel, (shape, shape), [VMEM] * 5, 'blur_x_far')  8.57 us
    pallas_call x5, Pallas kernels, log_factor(): call(kernel, shape, [VMEM] * (3 + len(parts)), 'log_factor')  7.67 us
    pallas_call x4, Pallas kernels, blur_near(): call(blur_near_kernel, (shape, shape), [VMEM] * 4, 'blur_x_near')  6.55 us
    pallas_call x2, Pallas kernels, first_ratio(): call(kernel, out_shape, in_specs, 'image_and_ratio', scratch)  6.36 us
    unnamed x42, local copies, waits for them, and re-layouts  4.78 us
  transfers between devices with their start and end apart: 37, of which 17 were waited for; matrix products, arithmetic and copies ran while one was open for 2% of the time, Pallas kernels for 20%

profile of v9, /device:TPU:17, one launch (start us, length us, event | category | flops | bytes accessed | tf_op | source)
XLA Modules:
  0.0 217.0 jit_solution(8525775845721457095)
XLA Ops:
  0.0 1.7 copy-done.5
  5.3 3.0 %collective-permute-start = (f32[1,512]{1,0:T(1,128)S(1)}, f32[1,512]{1,0:T(1,128)S(1)}, u32[]{:S(2)}, u32[]{:S(2)}) collective-permute-start(f32[1,512]{1,0:T(1,128)S(1)} %pad_maximum_fusion.mine_ref), channel_id=1, source_target_pairs={{0,8},{1,9},{2,10},{3,11},{4,12},{5,13},{6,14},{7,15},{8,0},{9,1},... | collective-permute-start | bytes 6152 | tf_op jit(solution)/shard_map/ppermute | solution.py:34
  8.2 4.6 %shift_recorded.1 = (f32[17,80,256]{2,1,0:T(8,128)}, f32[17,80,256]{2,1,0:T(8,128)}) custom-call(s32[1,3]{1,0:T(1,128)S(1)} %copy-done.17, f32[16,128,256]{2,1,0:T(8,128)S(1)} %bitcast.2, s32[16,128]{1,0:T(8,128)S(1)} %bitcast.3), custom_call_target="tpu_custom_call" | custom-call | tf_op jit(solution)/shard_map/shift_recorded/pallas_call | solution.py:281
  12.8 2.0 band_matrices.1
  14.9 8.2 %collective-permute-done.1.crossed_ref = f32[16,96,256]{2,1,0:T(8,128)S(1)} collective-permute-done((f32[16,96,256]{2,1,0:T(8,128)S(1)}, f32[16,96,256]{2,1,0:T(8,128)S(1)}, u32[]{:S(2)}, u32[]{:S(2)}) %collective-permute-start.1) | collective-permute-done | bytes 1572896 | tf_op jit(solution)/shard_map/ppermute | solution.py:34
  25.7 3.9 %collective-permute-start.5 = (f32[15,96,256]{2,1,0:T(8,128)}, f32[15,96,256]{2,1,0:T(8,128)}, u32[]{:S(2)}, u32[]{:S(2)}) collective-permute-start(f32[15,96,256]{2,1,0:T(8,128)} %get-tuple-element.83), channel_id=1, source_target_pairs={{2,8},{3,9},{4,10},{5,11},{6,12},{7,13},{8,2},{9,3},{10,4},{11,5},... | collective-permute-start | bytes 4423688 | tf_op jit(solution)/shard_map/ppermute | solution.py:34
  29.7 2.8 %collective-permute-start.2 = (f32[17,80,256]{2,1,0:T(8,128)}, f32[17,80,256]{2,1,0:T(8,128)}, u32[]{:S(2)}, u32[]{:S(2)}) collective-permute-start(f32[17,80,256]{2,1,0:T(8,128)} %get-tuple-element.77), channel_id=1, source_target_pairs={{1,8},{3,10},{5,12},{7,14},{8,1},{10,3},{12,5},{14,7},{17,24},{19,... | collective-permute-start | bytes 4177928 | tf_op jit(solution)/shard_map/ppermute | solution.py:34
  32.5 14.6 %collective-permute-done.5.far_ref = f32[15,96,256]{2,1,0:T(8,128)} collective-permute-done((f32[15,96,256]{2,1,0:T(8,128)}, f32[15,96,256]{2,1,0:T(8,128)}, u32[]{:S(2)}, u32[]{:S(2)}) %collective-permute-start.5) | collective-permute-done | bytes 1474592 | tf_op jit(solution)/shard_map/ppermute | solution.py:34
  47.6 16.8 %collective-permute-done.2 = f32[17,80,256]{2,1,0:T(8,128)} collective-permute-done((f32[17,80,256]{2,1,0:T(8,128)}, f32[17,80,256]{2,1,0:T(8,128)}, u32[]{:S(2)}, u32[]{:S(2)}) %collective-permute-start.2) | collective-permute-done | bytes 1392672 | tf_op jit(solution)/shard_map/ppermute | solution.py:34
  65.9 1.9 collective-permute-start.3
  68.5 3.1 %collective-permute-start.10 = (f32[17,80,256]{2,1,0:T(8,128)}, f32[17,80,256]{2,1,0:T(8,128)S(1)}, u32[]{:S(2)}, u32[]{:S(2)}) collective-permute-start(f32[17,80,256]{2,1,0:T(8,128)} %collective-permute-done.9.own_ref), channel_id=1, source_target_pairs={{2,8},{3,9},{4,10},{5,11},{6,12},{7,13},{8,2},{9,3},{10,4},{11,5},... | collective-permute-start | bytes 4177928 | tf_op jit(solution)/shard_map/ppermute | solution.py:34
  71.7 3.3 %blur_x_near.4 = (f32[16,96,256]{2,1,0:T(8,128)S(1)}, f32[16,96,256]{2,1,0:T(8,128)S(1)}) custom-call(bf16[2,256,384]{2,1,0:T(8,128)(2,1)S(1)} %get-tuple-element.73.hi_ref, bf16[2,256,384]{2,1,0:T(8,128)(2,1)S(1)} %get-tuple-element.74.lo_ref, f32[16,96,256]{2,1,0:T(8,128)S(1)} %get-tuple-element.82.own_ref.before_ref, ...), custom_call_target="tpu_custom_call" | custom-call | tf_op jit(solution)/shard_map/blur_x_near/pallas_call | solution.py:337
  75.0 4.5 %blur_x_far.4 = (f32[16,96,256]{2,1,0:T(8,128)S(1)}, f32[16,96,256]{2,1,0:T(8,128)S(1)}) custom-call(bf16[2,256,384]{2,1,0:T(8,128)(2,1)S(1)} %get-tuple-element.73.hi_ref, bf16[2,256,384]{2,1,0:T(8,128)(2,1)S(1)} %get-tuple-element.74.lo_ref, f32[15,96,256]{2,1,0:T(8,128)} %collective-permute-done.5.far_ref, ...), custom_call_target="tpu_custom_call" | custom-call | tf_op jit(solution)/shard_map/blur_x_far/pallas_call | solution.py:342
  79.5 1.6 blur_yz.2.blurred_ref
  81.1 5.0 %collective-permute-done.3.far_ref = f32[17,80,256]{2,1,0:T(8,128)S(1)} collective-permute-done((f32[17,80,256]{2,1,0:T(8,128)S(1)}, f32[17,80,256]{2,1,0:T(8,128)S(1)}, u32[]{:S(2)}, u32[]{:S(2)}) %collective-permute-start.3) | collective-permute-done | bytes 1392672 | tf_op jit(solution)/shard_map/ppermute | solution.py:34
  86.1 2.7 %image_and_ratio.2 = (f32[16,64,256]{2,1,0:T(8,128)S(1)}, f32[15,64,256]{2,1,0:T(8,128)S(1)}, f32[15,64,256]{2,1,0:T(8,128)S(1)}, f32[16,80,256]{2,1,0:T(8,128)S(1)}) custom-call(s32[2,3]{1,0:T(2,128)S(1)} %fusion.1.shift_ref, f32[17,80,256]{2,1,0:T(8,128)S(1)} %collective-permute-done.3.far_ref, f32[17,80,256]{2,1,0:T(8,128)S(1)} %collective-permute-done.4.near_ref, ...), custom_call_target="tpu_custom_call" | custom-call | tf_op jit(solution)/shard_map/image_and_ratio/pallas_call | solution.py:493
  88.7 1.9 collective-permute-start.7
  91.3 1.6 blur_yz.3.blurred_ref
  92.9 8.1 %collective-permute-done.10.far_ref = f32[17,80,256]{2,1,0:T(8,128)S(1)} collective-permute-done((f32[17,80,256]{2,1,0:T(8,128)}, f32[17,80,256]{2,1,0:T(8,128)S(1)}, u32[]{:S(2)}, u32[]{:S(2)}) %collective-permute-start.10) | collective-permute-done | bytes 1392672 | tf_op jit(solution)/shard_map/ppermute | solution.py:34
  101.0 3.7 %image_and_ratio.3 = (f32[16,64,256]{2,1,0:T(8,128)S(1)}, f32[15,32,256]{2,1,0:T(8,128)S(1)}, f32[15,32,256]{2,1,0:T(8,128)S(1)}, f32[15,32,256]{2,1,0:T(8,128)S...) custom-call(s32[2,3]{1,0:T(2,128)S(1)} %fusion.1.shift_ref, ...), custom_call_target="tpu_custom_call" | custom-call | tf_op jit(solution)/shard_map/image_and_ratio/pallas_call | solution.py:493
  105.8 1.9 collective-permute-start.15
  108.3 3.2 %collective-permute-done.7.refs_0_ = f32[15,64,256]{2,1,0:T(8,128)S(1)} collective-permute-done((f32[15,64,256]{2,1,0:T(8,128)S(1)}, f32[15,64,256]{2,1,0:T(8,128)S(1)}, u32[]{:S(2)}, u32[]{:S(2)}) %collective-permute-start.7) | collective-permute-done | bytes 983072 | tf_op jit(solution)/shard_map/ppermute | solution.py:34
  111.5 2.1 log_factor.5.before_ref
  113.7 2.8 %collective-permute-done.15.refs_0_ = f32[15,32,256]{2,1,0:T(8,128)S(1)} collective-permute-done((f32[15,32,256]{2,1,0:T(8,128)S(1)}, f32[15,32,256]{2,1,0:T(8,128)S(1)}, u32[]{:S(2)}, u32[]{:S(2)}) %collective-permute-start.15) | collective-permute-done | bytes 491552 | tf_op jit(solution)/shard_map/ppermute | solution.py:34
  118.8 2.2 %collective-permute-start.12 = (f32[15,32,256]{2,1,0:T(8,128)S(1)}, f32[15,32,256]{2,1,0:T(8,128)S(1)}, u32[]{:S(2)}, u32[]{:S(2)}) collective-permute-start(f32[15,32,256]{2,1,0:T(8,128)S(1)} %get-tuple-element.98), channel_id=1, source_target_pairs={{2,8},{3,9},{4,10},{5,11},{6,12},{7,13},{8,2},{9,3},{10,4},{11,5},... | collective-permute-start | bytes 1474568 | tf_op jit(solution)/shard_map/ppermute | solution.py:34
  121.4 7.9 %collective-permute-done.12.refs_0_ = f32[15,32,256]{2,1,0:T(8,128)S(1)} collective-permute-done((f32[15,32,256]{2,1,0:T(8,128)S(1)}, f32[15,32,256]{2,1,0:T(8,128)S(1)}, u32[]{:S(2)}, u32[]{:S(2)}) %collective-permute-start.12) | collective-permute-done | bytes 491552 | tf_op jit(solution)/shard_map/ppermute | solution.py:34
  133.3 3.7 %collective-permute-start.18 = (f32[15,32,256]{2,1,0:T(8,128)}, f32[15,32,256]{2,1,0:T(8,128)}, u32[]{:S(2)}, u32[]{:S(2)}) collective-permute-start(f32[15,32,256]{2,1,0:T(8,128)} %get-tuple-element.103), channel_id=1, source_target_pairs={{2,8},{3,9},{4,10},{5,11},{6,12},{7,13},{8,2},{9,3},{10,4},{11,5},... | collective-permute-start | bytes 1474568 | tf_op jit(solution)/shard_map/ppermute | solution.py:34
  137.1 6.7 %collective-permute-done.14.refs_1_ = f32[16,32,256]{2,1,0:T(8,128)} collective-permute-done((f32[16,32,256]{2,1,0:T(8,128)S(1)}, f32[16,32,256]{2,1,0:T(8,128)}, u32[]{:S(2)}, u32[]{:S(2)}) %collective-permute-start.14) | collective-permute-done | bytes 524320 | tf_op jit(solution)/shard_map/ppermute | solution.py:34
  145.3 3.2 %collective-permute-start.19 = (f32[15,32,256]{2,1,0:T(8,128)S(1)}, f32[15,32,256]{2,1,0:T(8,128)S(1)}, u32[]{:S(2)}, u32[]{:S(2)}) collective-permute-start(f32[15,32,256]{2,1,0:T(8,128)S(1)} %get-tuple-element.108), channel_id=1, source_target_pairs={{2,8},{3,9},{4,10},{5,11},{6,12},{7,13},{8,2},{9,3},{10,4},{11,5},... | collective-permute-start | bytes 1474568 | tf_op jit(solution)/shard_map/ppermute | solution.py:34
  148.7 2.4 %collective-permute-start.22 = (f32[15,32,256]{2,1,0:T(8,128)S(1)}, f32[15,32,256]{2,1,0:T(8,128)S(1)}, u32[]{:S(2)}, u32[]{:S(2)}) collective-permute-start(f32[15,32,256]{2,1,0:T(8,128)S(1)} %get-tuple-element.142), channel_id=1, source_target_pairs={{2,8},{3,9},{4,10},{5,11},{6,12},{7,13},{8,2},{9,3},{10,4},{11,5},... | collective-permute-start | bytes 1474568 | tf_op jit(solution)/shard_map/ppermute | solution.py:34
  152.8 2.1 blur_x_far.6
  157.0 3.8 %collective-permute-done.22.far_ref = f32[15,32,256]{2,1,0:T(8,128)S(1)} collective-permute-done((f32[15,32,256]{2,1,0:T(8,128)S(1)}, f32[15,32,256]{2,1,0:T(8,128)S(1)}, u32[]{:S(2)}, u32[]{:S(2)}) %collective-permute-start.22) | collective-permute-done | bytes 491552 | tf_op jit(solution)/shard_map/ppermute | solution.py:34
  160.9 5.2 %ratio.2 = (f32[16,32,256]{2,1,0:T(8,128)S(1)}, f32[16,32,256]{2,1,0:T(8,128)S(1)}, f32[2,15,32,256]{3,2,1,0:T(8,128)S(1)}, f32[2,15,32,256]{3,2,1,0:T(8,128)S(1)}, f32[2,16,32,256]{3,2,1,0:T(8,128)S(1)}) custom-call(f32[16,80,256]{2,1,0:T(8,128)S(1)} %copy-done.1, f32[16,80,256]{2,1,0:T(8,128)S(1)} %copy-done.3, ...), custom_call_target="tpu_custom_call" | custom-call | tf_op jit(solution)/shard_map/ratio/pallas_call | solution.py:481
  166.1 2.9 %collective-permute-start.25 = (f32[2,15,32,256]{3,2,1,0:T(8,128)S(1)}, f32[2,15,32,256]{3,2,1,0:T(8,128)S(1)}, u32[]{:S(2)}, u32[]{:S(2)}) collective-permute-start(f32[2,15,32,256]{3,2,1,0:T(8,128)S(1)} %get-tuple-element.126), channel_id=1, source_target_pairs={{2,8},{3,9},{4,10},{5,11},{6,12},{7,13},{8,2},{9,3},{10,4},{11,5},... | collective-permute-start | bytes 2949128 | tf_op jit(solution)/shard_map/ppermute | solution.py:34
  171.2 4.2 %ratio.3 = (f32[16,32,256]{2,1,0:T(8,128)S(1)}, f32[16,32,256]{2,1,0:T(8,128)S(1)}, f32[2,15,32,256]{3,2,1,0:T(8,128)S(1)}, f32[2,15,32,256]{3,2,1,0:T(8,128)S(1)}) custom-call(f32[16,80,256]{2,1,0:T(8,128)S(1)} %copy-done.1, f32[16,80,256]{2,1,0:T(8,128)S(1)} %copy-done.3, f32[16,32,256]{2,1,0:T(8,128)S(1)} %get-tuple-element.119.refs_3_.refs_2_, ...), custom_call_target="tpu_custom_call" | custom-call | tf_op jit(solution)/shard_map/ratio/pallas_call | solution.py:481
  175.4 2.6 %collective-permute-start.31 = (f32[2,15,32,256]{3,2,1,0:T(8,128)S(1)}, f32[2,15,32,256]{3,2,1,0:T(8,128)S(1)}, u32[]{:S(2)}, u32[]{:S(2)}) collective-permute-start(f32[2,15,32,256]{3,2,1,0:T(8,128)S(1)} %get-tuple-element.137), channel_id=1, source_target_pairs={{2,8},{3,9},{4,10},{5,11},{6,12},{7,13},{8,2},{9,3},{10,4},{11,5},... | collective-permute-start | bytes 2949128 | tf_op jit(solution)/shard_map/ppermute | solution.py:34
  178.5 3.3 %collective-permute-done.25.refs_0_.refs_3_ = f32[2,15,32,256]{3,2,1,0:T(8,128)S(1)} collective-permute-done((f32[2,15,32,256]{3,2,1,0:T(8,128)S(1)}, f32[2,15,32,256]{3,2,1,0:T(8,128)S(1)}, u32[]{:S(2)}, u32[]{:S(2)}) %collective-permute-start.25) | collective-permute-done | bytes 983072 | tf_op jit(solution)/shard_map/ppermute | solution.py:34
  181.8 1.7 log_factor.8.refs_0_
  184.2 2.6 %collective-permute-start.28 = (f32[16,32,256]{2,1,0:T(8,128)S(1)}, f32[16,32,256]{2,1,0:T(8,128)S(1)}, u32[]{:S(2)}, u32[]{:S(2)}) collective-permute-start(f32[16,32,256]{2,1,0:T(8,128)S(1)} %log_factor.8.refs_0_), channel_id=1, source_target_pairs={{1,24},{3,26},{5,28},{7,30},{8,17},{10,19},{12,21},{14,23},{17,8},... | collective-permute-start | bytes 1572872 | tf_op jit(solution)/shard_map/ppermute | solution.py:34
  186.8 3.9 %collective-permute-start.29 = (f32[16,32,256]{2,1,0:T(8,128)S(1)}, f32[16,32,256]{2,1,0:T(8,128)S(1)}, u32[]{:S(2)}, u32[]{:S(2)}) collective-permute-start(f32[16,32,256]{2,1,0:T(8,128)S(1)} %log_factor.8.refs_0_), channel_id=1, source_target_pairs={{1,8},{3,10},{5,12},{7,14},{8,1},{10,3},{12,5},{14,7},{17,24},{19,... | collective-permute-start | bytes 1572872 | tf_op jit(solution)/shard_map/ppermute | solution.py:34
  190.7 1.6 collective-permute-done.31.refs_0_.refs_3_
  192.3 1.7 log_factor.9.refs_0_
  194.7 2.6 %collective-permute-start.34 = (f32[16,32,256]{2,1,0:T(8,128)S(1)}, f32[16,32,256]{2,1,0:T(8,128)S(1)}, u32[]{:S(2)}, u32[]{:S(2)}) collective-permute-start(f32[16,32,256]{2,1,0:T(8,128)S(1)} %log_factor.9.refs_0_), channel_id=1, source_target_pairs={{1,24},{3,26},{5,28},{7,30},{8,17},{10,19},{12,21},{14,23},{17,8},... | collective-permute-start | bytes 1572872 | tf_op jit(solution)/shard_map/ppermute | solution.py:34
  197.3 3.9 %collective-permute-start.35 = (f32[16,32,256]{2,1,0:T(8,128)S(1)}, f32[16,32,256]{2,1,0:T(8,128)S(1)}, u32[]{:S(2)}, u32[]{:S(2)}) collective-permute-start(f32[16,32,256]{2,1,0:T(8,128)S(1)} %log_factor.9.refs_0_), channel_id=1, source_target_pairs={{1,8},{3,10},{5,12},{7,14},{8,1},{10,3},{12,5},{14,7},{17,24},{19,... | collective-permute-start | bytes 1572872 | tf_op jit(solution)/shard_map/ppermute | solution.py:34
  201.2 2.9 %collective-permute-done.29.refs_3_ = f32[16,32,256]{2,1,0:T(8,128)S(1)} collective-permute-done((f32[16,32,256]{2,1,0:T(8,128)S(1)}, f32[16,32,256]{2,1,0:T(8,128)S(1)}, u32[]{:S(2)}, u32[]{:S(2)}) %collective-permute-start.29) | collective-permute-done | bytes 524320 | tf_op jit(solution)/shard_map/ppermute | solution.py:34
  204.3 6.3 %collective-permute-done.34.refs_2_ = f32[16,32,256]{2,1,0:T(8,128)S(1)} collective-permute-done((f32[16,32,256]{2,1,0:T(8,128)S(1)}, f32[16,32,256]{2,1,0:T(8,128)S(1)}, u32[]{:S(2)}, u32[]{:S(2)}) %collective-permute-start.34) | collective-permute-done | bytes 524320 | tf_op jit(solution)/shard_map/ppermute | solution.py:34
  210.6 2.8 %collective-permute-done.35.refs_3_ = f32[16,32,256]{2,1,0:T(8,128)S(1)} collective-permute-done((f32[16,32,256]{2,1,0:T(8,128)S(1)}, f32[16,32,256]{2,1,0:T(8,128)S(1)}, u32[]{:S(2)}, u32[]{:S(2)}) %collective-permute-start.35) | collective-permute-done | bytes 524320 | tf_op jit(solution)/shard_map/ppermute | solution.py:34
  213.6 1.9 collective-permute-done.36.refs_3_
  (105 shorter events, 29.1 us)
Async XLA Ops:
  0.0 8.2 %copy-start.4 = (f32[1,16,128,256]{3,2,1,0:T(8,128)S(1)}, f32[1,16,128,256]{3,2,1,0:T(8,128)}, u32[]{:S(2)}) copy-start(f32[1,16,128,256]{3,2,1,0:T(8,128)} %param.7) | copy-start | bytes 6291460
  1.7 6.5 %copy-start.16 = (s32[1,16,128]{2,1,0:T(8,128)S(1)}, s32[1,16,128]{2,1,0:T(8,128)}, u32[]{:S(2)}) copy-start(s32[1,16,128]{2,1,0:T(8,128)} %param.10) | copy-start | bytes 24580
  1.7 6.5 %copy-start.17 = (s32[1,3]{1,0:T(1,128)S(1)}, s32[1,3]{1,0:T(1,128)}, u32[]{:S(2)}) copy-start(s32[1,3]{1,0:T(1,128)} %offsets_ref.1) | copy-start | bytes 40
  2.0 21.2 %collective-permute-start.1 = (f32[16,96,256]{2,1,0:T(8,128)S(1)}, f32[16,96,256]{2,1,0:T(8,128)S(1)}, u32[]{:S(2)}, u32[]{:S(2)}) collective-permute-start(f32[16,96,256]{2,1,0:T(8,128)S(1)} %get-tuple-element.81), channel_id=1, source_target_pairs={{0,1},{2,3},{4,5},{6,7},{9,8},{11,10},{13,12},{15,14},{16,17},{18,... | collective-permute-start | bytes 4718600 | tf_op jit(solution)/shard_map/ppermute | solution.py:34
  5.3 7.5 %collective-permute-start = (f32[1,512]{1,0:T(1,128)S(1)}, f32[1,512]{1,0:T(1,128)S(1)}, u32[]{:S(2)}, u32[]{:S(2)}) collective-permute-start(f32[1,512]{1,0:T(1,128)S(1)} %pad_maximum_fusion.mine_ref), channel_id=1, source_target_pairs={{0,8},{1,9},{2,10},{3,11},{4,12},{5,13},{6,14},{7,15},{8,0},{9,1},... | collective-permute-start | bytes 6152 | tf_op jit(solution)/shard_map/ppermute | solution.py:34
  14.8 9.7 %copy-start.6 = (bf16[2,64,256]{2,1,0:T(8,128)(2,1)}, bf16[2,64,256]{2,1,0:T(8,128)(2,1)S(1)}, u32[]{:S(2)}) copy-start(bf16[2,64,256]{2,1,0:T(8,128)(2,1)S(1)} %get-tuple-element.91.ya_ref) | copy-start | bytes 196612
  14.8 9.7 %copy-start.8 = (bf16[2,48,256]{2,1,0:T(8,128)(2,1)}, bf16[2,48,256]{2,1,0:T(8,128)(2,1)S(1)}, u32[]{:S(2)}) copy-start(bf16[2,48,256]{2,1,0:T(8,128)(2,1)S(1)} %get-tuple-element.124.refs_6_) | copy-start | bytes 147460
  14.9 9.7 %copy-start.10 = (bf16[2,32,256]{2,1,0:T(8,128)(2,1)}, bf16[2,32,256]{2,1,0:T(8,128)(2,1)S(1)}, u32[]{:S(2)}) copy-start(bf16[2,32,256]{2,1,0:T(8,128)(2,1)S(1)} %get-tuple-element.135.refs_7_) | copy-start | bytes 98308
  14.9 9.7 %copy-start.12 = (bf16[2,32,256]{2,1,0:T(8,128)(2,1)}, bf16[2,32,256]{2,1,0:T(8,128)(2,1)S(1)}, u32[]{:S(2)}) copy-start(bf16[2,32,256]{2,1,0:T(8,128)(2,1)S(1)} %get-tuple-element.136.refs_8_) | copy-start | bytes 98308
  14.9 9.7 %copy-start.14 = (bf16[2,32,256]{2,1,0:T(8,128)(2,1)}, bf16[2,32,256]{2,1,0:T(8,128)(2,1)S(1)}, u32[]{:S(2)}) copy-start(bf16[2,32,256]{2,1,0:T(8,128)(2,1)S(1)} %get-tuple-element.125.refs_7_) | copy-start | bytes 98308
  25.7 21.5 %collective-permute-start.5 = (f32[15,96,256]{2,1,0:T(8,128)}, f32[15,96,256]{2,1,0:T(8,128)}, u32[]{:S(2)}, u32[]{:S(2)}) collective-permute-start(f32[15,96,256]{2,1,0:T(8,128)} %get-tuple-element.83), channel_id=1, source_target_pairs={{2,8},{3,9},{4,10},{5,11},{6,12},{7,13},{8,2},{9,3},{10,4},{11,5},... | collective-permute-start | bytes 4423688 | tf_op jit(solution)/shard_map/ppermute | solution.py:34
  29.7 34.7 %collective-permute-start.2 = (f32[17,80,256]{2,1,0:T(8,128)}, f32[17,80,256]{2,1,0:T(8,128)}, u32[]{:S(2)}, u32[]{:S(2)}) collective-permute-start(f32[17,80,256]{2,1,0:T(8,128)} %get-tuple-element.77), channel_id=1, source_target_pairs={{1,8},{3,10},{5,12},{7,14},{8,1},{10,3},{12,5},{14,7},{17,24},{19,... | collective-permute-start | bytes 4177928 | tf_op jit(solution)/shard_map/ppermute | solution.py:34
  32.5 36.0 %collective-permute-start.9 = (f32[17,80,256]{2,1,0:T(8,128)}, f32[17,80,256]{2,1,0:T(8,128)}, u32[]{:S(2)}, u32[]{:S(2)}) collective-permute-start(f32[17,80,256]{2,1,0:T(8,128)} %get-tuple-element.96), channel_id=1, source_target_pairs={{0,1},{1,9},{2,3},{3,11},{4,5},{5,13},{6,7},{7,15},{8,0},{9,8},{10... | collective-permute-start | bytes 4177928 | tf_op jit(solution)/shard_map/ppermute | solution.py:34
  47.2 24.5 %collective-permute-start.6 = (f32[15,96,256]{2,1,0:T(8,128)}, f32[15,96,256]{2,1,0:T(8,128)S(1)}, u32[]{:S(2)}, u32[]{:S(2)}) collective-permute-start(f32[15,96,256]{2,1,0:T(8,128)} %copy-done.18), channel_id=1, source_target_pairs={{0,8},{1,9},{2,10},{3,11},{4,12},{5,13},{6,14},{7,15},{8,0},{9,1},... | collective-permute-start | bytes 4423688 | tf_op jit(solution)/shard_map/ppermute | solution.py:34
  65.9 20.1 %collective-permute-start.3 = (f32[17,80,256]{2,1,0:T(8,128)S(1)}, f32[17,80,256]{2,1,0:T(8,128)S(1)}, u32[]{:S(2)}, u32[]{:S(2)}) collective-permute-start(f32[17,80,256]{2,1,0:T(8,128)S(1)} %broadcast_select_fusion.own_ref), channel_id=1, source_target_pairs={{2,8},{3,9},{4,10},{5,11},{6,12},{7,13},{8,2},{9,3},{10,4},{11,5},... | collective-permute-start | bytes 4177928 | tf_op jit(solution)/shard_map/ppermute | solution.py:34
  67.9 18.2 %collective-permute-start.4 = (f32[17,80,256]{2,1,0:T(8,128)S(1)}, f32[17,80,256]{2,1,0:T(8,128)S(1)}, u32[]{:S(2)}, u32[]{:S(2)}) collective-permute-start(f32[17,80,256]{2,1,0:T(8,128)S(1)} %broadcast_select_fusion.own_ref), channel_id=1, source_target_pairs={{0,8},{1,9},{2,10},{3,11},{4,12},{5,13},{6,14},{7,15},{8,0},{9,1},... | collective-permute-start | bytes 4177928 | tf_op jit(solution)/shard_map/ppermute | solution.py:34
  68.5 32.5 %collective-permute-start.10 = (f32[17,80,256]{2,1,0:T(8,128)}, f32[17,80,256]{2,1,0:T(8,128)S(1)}, u32[]{:S(2)}, u32[]{:S(2)}) collective-permute-start(f32[17,80,256]{2,1,0:T(8,128)} %collective-permute-done.9.own_ref), channel_id=1, source_target_pairs={{2,8},{3,9},{4,10},{5,11},{6,12},{7,13},{8,2},{9,3},{10,4},{11,5},... | collective-permute-start | bytes 4177928 | tf_op jit(solution)/shard_map/ppermute | solution.py:34
  71.6 29.4 %collective-permute-start.11 = (f32[17,80,256]{2,1,0:T(8,128)}, f32[17,80,256]{2,1,0:T(8,128)S(1)}, u32[]{:S(2)}, u32[]{:S(2)}) collective-permute-start(f32[17,80,256]{2,1,0:T(8,128)} %collective-permute-done.9.own_ref), channel_id=1, source_target_pairs={{0,8},{1,9},{2,10},{3,11},{4,12},{5,13},{6,14},{7,15},{8,0},{9,1},... | collective-permute-start | bytes 4177928 | tf_op jit(solution)/shard_map/ppermute | solution.py:34
  79.5 6.6 %copy-start.7 = (bf16[2,64,256]{2,1,0:T(8,128)(2,1)S(1)}, bf16[2,64,256]{2,1,0:T(8,128)(2,1)}, u32[]{:S(2)}) copy-start(bf16[2,64,256]{2,1,0:T(8,128)(2,1)} %copy-done.6) | copy-start | bytes 196612
  88.7 22.8 %collective-permute-start.7 = (f32[15,64,256]{2,1,0:T(8,128)S(1)}, f32[15,64,256]{2,1,0:T(8,128)S(1)}, u32[]{:S(2)}, u32[]{:S(2)}) collective-permute-start(f32[15,64,256]{2,1,0:T(8,128)S(1)} %get-tuple-element.92), channel_id=1, source_target_pairs={{2,8},{3,9},{4,10},{5,11},{6,12},{7,13},{8,2},{9,3},{10,4},{11,5},... | collective-permute-start | bytes 2949128 | tf_op jit(solution)/shard_map/ppermute | solution.py:34
  90.7 20.8 %collective-permute-start.8 = (f32[15,64,256]{2,1,0:T(8,128)S(1)}, f32[15,64,256]{2,1,0:T(8,128)S(1)}, u32[]{:S(2)}, u32[]{:S(2)}) collective-permute-start(f32[15,64,256]{2,1,0:T(8,128)S(1)} %get-tuple-element.93), channel_id=1, source_target_pairs={{0,8},{1,9},{2,10},{3,11},{4,12},{5,13},{6,14},{7,15},{8,0},{9,1},... | collective-permute-start | bytes 2949128 | tf_op jit(solution)/shard_map/ppermute | solution.py:34
  105.8 10.7 %collective-permute-start.15 = (f32[15,32,256]{2,1,0:T(8,128)S(1)}, f32[15,32,256]{2,1,0:T(8,128)S(1)}, u32[]{:S(2)}, u32[]{:S(2)}) collective-permute-start(f32[15,32,256]{2,1,0:T(8,128)S(1)} %get-tuple-element.101), channel_id=1, source_target_pairs={{2,8},{3,9},{4,10},{5,11},{6,12},{7,13},{8,2},{9,3},{10,4},{11,5},... | collective-permute-start | bytes 1474568 | tf_op jit(solution)/shard_map/ppermute | solution.py:34
  107.7 8.8 %collective-permute-start.16 = (f32[15,32,256]{2,1,0:T(8,128)S(1)}, f32[15,32,256]{2,1,0:T(8,128)S(1)}, u32[]{:S(2)}, u32[]{:S(2)}) collective-permute-start(f32[15,32,256]{2,1,0:T(8,128)S(1)} %get-tuple-element.102), channel_id=1, source_target_pairs={{0,8},{1,9},{2,10},{3,11},{4,12},{5,13},{6,14},{7,15},{8,0},{9,1},... | collective-permute-start | bytes 1474568 | tf_op jit(solution)/shard_map/ppermute | solution.py:34
  117.6 13.1 %collective-permute-start.17 = (f32[16,32,256]{2,1,0:T(8,128)S(1)}, f32[16,32,256]{2,1,0:T(8,128)S(1)}, u32[]{:S(2)}, u32[]{:S(2)}) collective-permute-start(f32[16,32,256]{2,1,0:T(8,128)S(1)} %log_factor.7.refs_0_), channel_id=1, source_target_pairs={{0,16},{1,17},{2,18},{3,19},{4,20},{5,21},{6,22},{7,23},{8,24},{9,... | collective-permute-start | bytes 1572872 | tf_op jit(solution)/shard_map/ppermute | solution.py:34
  118.8 10.4 %collective-permute-start.12 = (f32[15,32,256]{2,1,0:T(8,128)S(1)}, f32[15,32,256]{2,1,0:T(8,128)S(1)}, u32[]{:S(2)}, u32[]{:S(2)}) collective-permute-start(f32[15,32,256]{2,1,0:T(8,128)S(1)} %get-tuple-element.98), channel_id=1, source_target_pairs={{2,8},{3,9},{4,10},{5,11},{6,12},{7,13},{8,2},{9,3},{10,4},{11,5},... | collective-permute-start | bytes 1474568 | tf_op jit(solution)/shard_map/ppermute | solution.py:34
  121.0 8.2 %collective-permute-start.13 = (f32[15,32,256]{2,1,0:T(8,128)S(1)}, f32[15,32,256]{2,1,0:T(8,128)S(1)}, u32[]{:S(2)}, u32[]{:S(2)}) collective-permute-start(f32[15,32,256]{2,1,0:T(8,128)S(1)} %get-tuple-element.99), channel_id=1, source_target_pairs={{0,8},{1,9},{2,10},{3,11},{4,12},{5,13},{6,14},{7,15},{8,0},{9,1},... | collective-permute-start | bytes 1474568 | tf_op jit(solution)/shard_map/ppermute | solution.py:34
  130.4 13.4 %collective-permute-start.14 = (f32[16,32,256]{2,1,0:T(8,128)S(1)}, f32[16,32,256]{2,1,0:T(8,128)}, u32[]{:S(2)}, u32[]{:S(2)}) collective-permute-start(f32[16,32,256]{2,1,0:T(8,128)S(1)} %log_factor.6.refs_0_), channel_id=1, source_target_pairs={{0,16},{1,17},{2,18},{3,19},{4,20},{5,21},{6,22},{7,23},{8,24},{9,... | collective-permute-start | bytes 1572872 | tf_op jit(solution)/shard_map/ppermute | solution.py:34
  132.4 16.1 %collective-permute-start.21 = (f32[16,32,256]{2,1,0:T(8,128)S(1)}, f32[16,32,256]{2,1,0:T(8,128)S(1)}, u32[]{:S(2)}, u32[]{:S(2)}) collective-permute-start(f32[16,32,256]{2,1,0:T(8,128)S(1)} %get-tuple-element.113.own_ref.before_ref), channel_id=1, source_target_pairs={{0,1},{1,0},{2,3},{3,2},{4,5},{5,4},{6,7},{7,6},{8,9},{9,8},{10,11... | collective-permute-start | bytes 1572872 | tf_op jit(solution)/shard_map/ppermute | solution.py:34
  133.3 10.7 %collective-permute-start.18 = (f32[15,32,256]{2,1,0:T(8,128)}, f32[15,32,256]{2,1,0:T(8,128)}, u32[]{:S(2)}, u32[]{:S(2)}) collective-permute-start(f32[15,32,256]{2,1,0:T(8,128)} %get-tuple-element.103), channel_id=1, source_target_pairs={{2,8},{3,9},{4,10},{5,11},{6,12},{7,13},{8,2},{9,3},{10,4},{11,5},... | collective-permute-start | bytes 1474568 | tf_op jit(solution)/shard_map/ppermute | solution.py:34
  137.0 14.7 %collective-permute-start.24 = (f32[15,32,256]{2,1,0:T(8,128)}, f32[15,32,256]{2,1,0:T(8,128)S(1)}, u32[]{:S(2)}, u32[]{:S(2)}) collective-permute-start(f32[15,32,256]{2,1,0:T(8,128)} %copy-done.19), channel_id=1, source_target_pairs={{0,8},{1,9},{2,10},{3,11},{4,12},{5,13},{6,14},{7,15},{8,0},{9,1},... | collective-permute-start | bytes 1474568 | tf_op jit(solution)/shard_map/ppermute | solution.py:34
  145.3 10.7 %collective-permute-start.19 = (f32[15,32,256]{2,1,0:T(8,128)S(1)}, f32[15,32,256]{2,1,0:T(8,128)S(1)}, u32[]{:S(2)}, u32[]{:S(2)}) collective-permute-start(f32[15,32,256]{2,1,0:T(8,128)S(1)} %get-tuple-element.108), channel_id=1, source_target_pairs={{2,8},{3,9},{4,10},{5,11},{6,12},{7,13},{8,2},{9,3},{10,4},{11,5},... | collective-permute-start | bytes 1474568 | tf_op jit(solution)/shard_map/ppermute | solution.py:34
  148.5 6.4 %collective-permute-start.20 = (f32[15,32,256]{2,1,0:T(8,128)S(1)}, f32[15,32,256]{2,1,0:T(8,128)S(1)}, u32[]{:S(2)}, u32[]{:S(2)}) collective-permute-start(f32[15,32,256]{2,1,0:T(8,128)S(1)} %get-tuple-element.109), channel_id=1, source_target_pairs={{0,8},{1,9},{2,10},{3,11},{4,12},{5,13},{6,14},{7,15},{8,0},{9,1},... | collective-permute-start | bytes 1474568 | tf_op jit(solution)/shard_map/ppermute | solution.py:34
  148.7 12.2 %collective-permute-start.22 = (f32[15,32,256]{2,1,0:T(8,128)S(1)}, f32[15,32,256]{2,1,0:T(8,128)S(1)}, u32[]{:S(2)}, u32[]{:S(2)}) collective-permute-start(f32[15,32,256]{2,1,0:T(8,128)S(1)} %get-tuple-element.142), channel_id=1, source_target_pairs={{2,8},{3,9},{4,10},{5,11},{6,12},{7,13},{8,2},{9,3},{10,4},{11,5},... | collective-permute-start | bytes 1474568 | tf_op jit(solution)/shard_map/ppermute | solution.py:34
  151.0 9.9 %collective-permute-start.23 = (f32[15,32,256]{2,1,0:T(8,128)S(1)}, f32[15,32,256]{2,1,0:T(8,128)S(1)}, u32[]{:S(2)}, u32[]{:S(2)}) collective-permute-start(f32[15,32,256]{2,1,0:T(8,128)S(1)} %get-tuple-element.141), channel_id=1, source_target_pairs={{0,8},{1,9},{2,10},{3,11},{4,12},{5,13},{6,14},{7,15},{8,0},{9,1},... | collective-permute-start | bytes 1474568 | tf_op jit(solution)/shard_map/ppermute | solution.py:34
  154.8 6.0 %copy-start.3 = (f32[16,80,256]{2,1,0:T(8,128)S(1)}, f32[16,80,256]{2,1,0:T(8,128)}, u32[]{:S(2)}) copy-start(f32[16,80,256]{2,1,0:T(8,128)} %copy-done.2) | copy-start | bytes 3932164
  155.9 4.9 %copy-start.1 = (f32[16,80,256]{2,1,0:T(8,128)S(1)}, f32[16,80,256]{2,1,0:T(8,128)}, u32[]{:S(2)}) copy-start(f32[16,80,256]{2,1,0:T(8,128)} %copy-done) | copy-start | bytes 3932164
  166.1 15.7 %collective-permute-start.25 = (f32[2,15,32,256]{3,2,1,0:T(8,128)S(1)}, f32[2,15,32,256]{3,2,1,0:T(8,128)S(1)}, u32[]{:S(2)}, u32[]{:S(2)}) collective-permute-start(f32[2,15,32,256]{3,2,1,0:T(8,128)S(1)} %get-tuple-element.126), channel_id=1, source_target_pairs={{2,8},{3,9},{4,10},{5,11},{6,12},{7,13},{8,2},{9,3},{10,4},{11,5},... | collective-permute-start | bytes 2949128 | tf_op jit(solution)/shard_map/ppermute | solution.py:34
  169.0 12.8 %collective-permute-start.26 = (f32[2,15,32,256]{3,2,1,0:T(8,128)S(1)}, f32[2,15,32,256]{3,2,1,0:T(8,128)S(1)}, u32[]{:S(2)}, u32[]{:S(2)}) collective-permute-start(f32[2,15,32,256]{3,2,1,0:T(8,128)S(1)} %get-tuple-element.127), channel_id=1, source_target_pairs={{0,8},{1,9},{2,10},{3,11},{4,12},{5,13},{6,14},{7,15},{8,0},{9,1},... | collective-permute-start | bytes 2949128 | tf_op jit(solution)/shard_map/ppermute | solution.py:34
  175.4 16.9 %collective-permute-start.31 = (f32[2,15,32,256]{3,2,1,0:T(8,128)S(1)}, f32[2,15,32,256]{3,2,1,0:T(8,128)S(1)}, u32[]{:S(2)}, u32[]{:S(2)}) collective-permute-start(f32[2,15,32,256]{3,2,1,0:T(8,128)S(1)} %get-tuple-element.137), channel_id=1, source_target_pairs={{2,8},{3,9},{4,10},{5,11},{6,12},{7,13},{8,2},{9,3},{10,4},{11,5},... | collective-permute-start | bytes 2949128 | tf_op jit(solution)/shard_map/ppermute | solution.py:34
  178.1 14.2 %collective-permute-start.32 = (f32[2,15,32,256]{3,2,1,0:T(8,128)S(1)}, f32[2,15,32,256]{3,2,1,0:T(8,128)S(1)}, u32[]{:S(2)}, u32[]{:S(2)}) collective-permute-start(f32[2,15,32,256]{3,2,1,0:T(8,128)S(1)} %get-tuple-element.138), channel_id=1, source_target_pairs={{0,8},{1,9},{2,10},{3,11},{4,12},{5,13},{6,14},{7,15},{8,0},{9,1},... | collective-permute-start | bytes 2949128 | tf_op jit(solution)/shard_map/ppermute | solution.py:34
  183.5 13.9 %collective-permute-start.27 = (f32[16,32,256]{2,1,0:T(8,128)S(1)}, f32[16,32,256]{2,1,0:T(8,128)S(1)}, u32[]{:S(2)}, u32[]{:S(2)}) collective-permute-start(f32[16,32,256]{2,1,0:T(8,128)S(1)} %log_factor.8.refs_0_), channel_id=1, source_target_pairs={{0,16},{2,18},{4,20},{6,22},{9,25},{11,27},{13,29},{15,31},{16,0},... | collective-permute-start | bytes 1572872 | tf_op jit(solution)/shard_map/ppermute | solution.py:34
  184.2 17.1 %collective-permute-start.28 = (f32[16,32,256]{2,1,0:T(8,128)S(1)}, f32[16,32,256]{2,1,0:T(8,128)S(1)}, u32[]{:S(2)}, u32[]{:S(2)}) collective-permute-start(f32[16,32,256]{2,1,0:T(8,128)S(1)} %log_factor.8.refs_0_), channel_id=1, source_target_pairs={{1,24},{3,26},{5,28},{7,30},{8,17},{10,19},{12,21},{14,23},{17,8},... | collective-permute-start | bytes 1572872 | tf_op jit(solution)/shard_map/ppermute | solution.py:34
  186.8 17.3 %collective-permute-start.29 = (f32[16,32,256]{2,1,0:T(8,128)S(1)}, f32[16,32,256]{2,1,0:T(8,128)S(1)}, u32[]{:S(2)}, u32[]{:S(2)}) collective-permute-start(f32[16,32,256]{2,1,0:T(8,128)S(1)} %log_factor.8.refs_0_), channel_id=1, source_target_pairs={{1,8},{3,10},{5,12},{7,14},{8,1},{10,3},{12,5},{14,7},{17,24},{19,... | collective-permute-start | bytes 1572872 | tf_op jit(solution)/shard_map/ppermute | solution.py:34
  194.0 10.3 %collective-permute-start.33 = (f32[16,32,256]{2,1,0:T(8,128)S(1)}, f32[16,32,256]{2,1,0:T(8,128)S(1)}, u32[]{:S(2)}, u32[]{:S(2)}) collective-permute-start(f32[16,32,256]{2,1,0:T(8,128)S(1)} %log_factor.9.refs_0_), channel_id=1, source_target_pairs={{0,16},{2,18},{4,20},{6,22},{9,25},{11,27},{13,29},{15,31},{16,0},... | collective-permute-start | bytes 1572872 | tf_op jit(solution)/shard_map/ppermute | solution.py:34
  194.7 15.9 %collective-permute-start.34 = (f32[16,32,256]{2,1,0:T(8,128)S(1)}, f32[16,32,256]{2,1,0:T(8,128)S(1)}, u32[]{:S(2)}, u32[]{:S(2)}) collective-permute-start(f32[16,32,256]{2,1,0:T(8,128)S(1)} %log_factor.9.refs_0_), channel_id=1, source_target_pairs={{1,24},{3,26},{5,28},{7,30},{8,17},{10,19},{12,21},{14,23},{17,8},... | collective-permute-start | bytes 1572872 | tf_op jit(solution)/shard_map/ppermute | solution.py:34
  197.3 16.1 %collective-permute-start.35 = (f32[16,32,256]{2,1,0:T(8,128)S(1)}, f32[16,32,256]{2,1,0:T(8,128)S(1)}, u32[]{:S(2)}, u32[]{:S(2)}) collective-permute-start(f32[16,32,256]{2,1,0:T(8,128)S(1)} %log_factor.9.refs_0_), channel_id=1, source_target_pairs={{1,8},{3,10},{5,12},{7,14},{8,1},{10,3},{12,5},{14,7},{17,24},{19,... | collective-permute-start | bytes 1572872 | tf_op jit(solution)/shard_map/ppermute | solution.py:34
  204.3 9.4 %collective-permute-start.30 = (f32[16,32,256]{2,1,0:T(8,128)S(1)}, f32[16,32,256]{2,1,0:T(8,128)S(1)}, u32[]{:S(2)}, u32[]{:S(2)}) collective-permute-start(f32[16,32,256]{2,1,0:T(8,128)S(1)} %last_update.2.refs_0_), channel_id=1, source_target_pairs={{0,8},{1,9},{2,10},{3,11},{4,12},{5,13},{6,14},{7,15},{8,0},{9,1},... | collective-permute-start | bytes 1572872 | tf_op jit(solution)/shard_map/ppermute | solution.py:34
  213.6 2.0 collective-permute-start.36
  (10 other events, 24.3 us)

commit v10 on v9

--- a/solution.py
+++ b/solution.py
@@ -302,44 +302,39 @@
     return pad_to(8 * (planes + radius), 128)
 
 
-def blur_near_kernel(hi_ref, lo_ref, own_ref, near_ref, first_ref, second_ref):
-    planes, rows, _ = own_ref.shape
-    lanes = slice(0, near_lanes(planes, near_ref.shape[0]))
-
-    def body(step, carry):
-        row = pl.multiple_of(step * 8, 8)
-        block = [gather(own_ref, row), gather(near_ref, row)]
-        out = spread_x(hi_ref, lo_ref, 0, slice(None), lanes, [block])
-        first_ref[:, pl.ds(row, 8), :] = out[:planes]
-        second_ref[:, pl.ds(row, 8), :] = out[planes:]
-        return carry
-
-    lax.fori_loop(0, rows // 8, body, 0)
-
-
-def blur_far_kernel(hi_ref, lo_ref, far_ref, first_ref, second_ref, first_out, second_out):
+def blur_x_kernel(hi_ref, lo_ref, *refs, far, radius):
+    planes_of, before, (first_ref, second_ref) = refs[:2 - far], refs[2 - far:-2], refs[-2:]
     planes, rows, _ = first_ref.shape
-    lanes = slice(near_lanes(planes, far_ref.shape[0]), None)
+    split_at = near_lanes(planes, radius)
+    lanes = slice(split_at, None) if far else slice(0, split_at)
 
     def body(step, carry):
         row = pl.multiple_of(step * 8, 8)
         place = (slice(None), pl.ds(row, 8), slice(None))
-        out = spread_x(hi_ref, lo_ref, 0, slice(None), lanes, [[gather(far_ref, row)]])
-        first_out[place] = first_ref[place] + out[:planes]
-        second_out[place] = second_ref[place] + out[planes:]
+        out = spread_x(hi_ref, lo_ref, 0, slice(None), lanes, [[gather(ref, row) for ref in planes_of]])
+        out = [out[:planes], out[planes:]]
+        if before:
+            out = [ref[place] + part for ref, part in zip(before, out)]
+        first_ref[place], second_ref[place] = out
         return carry
 
     lax.fori_loop(0, rows // 8, body, 0)
 
 
+def blur_x(tables, planes_of, before, planes):
+    far, (radius, rows, lanes) = len(planes_of) == 1, planes_of[-1].shape
+    shape = jax.ShapeDtypeStruct((planes, rows, lanes), F32)
+    kernel = functools.partial(blur_x_kernel, far=far, radius=radius)
+    operands = [*tables.x, *planes_of, *before]
+    return call(kernel, (shape, shape), [VMEM] * len(operands), "blur_x_far" if far else "blur_x_near")(*operands)
+
+
 def blur_near(tables, own, near):
-    shape = jax.ShapeDtypeStruct(own.shape, F32)
-    return call(blur_near_kernel, (shape, shape), [VMEM] * 4, "blur_x_near")(*tables.x, own, near)
+    return blur_x(tables, (own, near), (), own.shape[0])
 
 
 def blur_far(tables, far, parts):
-    shape = jax.ShapeDtypeStruct(parts[0].shape, F32)
-    return call(blur_far_kernel, (shape, shape), [VMEM] * 5, "blur_x_far")(*tables.x, far, *parts)
+    return blur_x(tables, (far,), parts, parts[0].shape[0])
 
 
 def spread_y(band, x):
@@ -625,14 +620,13 @@
     shifts = jnp.where(straight, jnp.concatenate([mine, other]), jnp.concatenate([other, mine]))
     shifts = shifts[:, 384:384 + offsets.shape[1]].astype(jnp.int32)
 
-    arrived = send(first, lambda g, c, q, r: (g, r, q, c) if c != r else None)
-    current, distant, close = choose(after(after(window, first), tables.whole[0]), crossed, radius)
-    distant = send(distant, to_far)
+    arrived = send(after(first, tables.whole[0]), lambda g, c, q, r: (g, r, q, c) if c != r else None)
+    current, distant, close = choose(after(window, first), crossed, radius)
     second = send(after(second, current), lambda g, c, q, r: (g, r, q, 1 - c))
+    distant, close = neighbours(distant, close)
     first = jnp.where(straight, first, arrived)
-    close = send(after(close, distant), to_core_partner)
     blocks = [(*neighbours(block, block), block) for block in (first, second)]
-    wide_parts = blur_far(tables, distant, blur_near(tables, current, close))
+    wide_parts = blur_x(tables, (current, close), blur_x(tables, (distant,), (), planes), planes)
     blurred = [blur_yz([part], tables, order) for order, part in enumerate(wide_parts)]
 
     row_chunks = [(inner_rows, edge_rows), (0, inner_rows)]

time: 218 us -> 203 us (0.931)
  waiting for transfers between devices: 96.4 us -> 72.7 us
  starting transfers between devices: 57.8 us -> 65.5 us
    ppermute x37, waiting for transfers between devices: 96.4 us -> 72.7 us  [send(): return lax.ppermute(array, AXES, moves(move))]
    ppermute x37, starting transfers between devices: 57.8 us -> 65.5 us  [send(): return lax.ppermute(array, AXES, moves(move))]
  transfers between devices with their start and end apart: 37 -> 37, of which waited for: 17 -> 17; matrix products, arithmetic and copies ran while one was open for 2% -> 2% of each run, Pallas kernels for 20% -> 23%
where the time goes in v10:
time: 203 us; the launch traced here: 201 us
  waiting for transfers between devices  72.7 us (36%)
  starting transfers between devices  65.5 us (32%)
  Pallas kernels  53.6 us (26%)
  local copies, waits for them, and re-layouts  6.23 us (3%)
  other arithmetic  2.21 us (1%)
    ppermute x37, waiting for transfers between devices, send(): return lax.ppermute(array, AXES, moves(move))  72.7 us
    ppermute x37, starting transfers between devices, send(): return lax.ppermute(array, AXES, moves(move))  65.5 us
    pallas_call x8, Pallas kernels, blur_x(): call(kernel, (shape, shape), [VMEM] * len(operands), 'blur_x_far' if far...  15.1 us
    pallas_call x2, Pallas kernels, next_ratio(): return call(kernel, out_shape, [VMEM] * len(operands), 'ratio')(*operands)  9.34 us
    pallas_call x5, Pallas kernels, log_factor(): call(kernel, shape, [VMEM] * (3 + len(parts)), 'log_factor')  7.67 us
    pallas_call x2, Pallas kernels, first_ratio(): call(kernel, out_shape, in_specs, 'image_and_ratio', scratch)  6.37 us
    unnamed x42, local copies, waits for them, and re-layouts  4.82 us
    pallas_call x1, Pallas kernels, shift_and_cut(): call(shift_kernel, (shape, shape), [SMEM, VMEM, VMEM], 'shift_recorded',...  4.55 us
  transfers between devices with their start and end apart: 37, of which 17 were waited for; matrix products, arithmetic and copies ran while one was open for 2% of the time, Pallas kernels for 23%

profile of v10, /device:TPU:17, one launch (start us, length us, event | category | flops | bytes accessed | tf_op | source)
XLA Modules:
  0.0 201.1 jit_solution(14219592465470423826)
XLA Ops:
  0.0 1.7 copy-done.5
  5.3 3.0 %collective-permute-start = (f32[1,512]{1,0:T(1,128)S(1)}, f32[1,512]{1,0:T(1,128)S(1)}, u32[]{:S(2)}, u32[]{:S(2)}) collective-permute-start(f32[1,512]{1,0:T(1,128)S(1)} %pad_maximum_fusion.mine_ref), channel_id=1, source_target_pairs={{0,8},{1,9},{2,10},{3,11},{4,12},{5,13},{6,14},{7,15},{8,0},{9,1},... | collective-permute-start | bytes 6152 | tf_op jit(solution)/shard_map/ppermute | solution.py:34
  8.2 4.6 %shift_recorded.1 = (f32[17,80,256]{2,1,0:T(8,128)}, f32[17,80,256]{2,1,0:T(8,128)}) custom-call(s32[1,3]{1,0:T(1,128)S(1)} %copy-done.17, f32[16,128,256]{2,1,0:T(8,128)S(1)} %bitcast.2, s32[16,128]{1,0:T(8,128)S(1)} %bitcast.3), custom_call_target="tpu_custom_call" | custom-call | tf_op jit(solution)/shard_map/shift_recorded/pallas_call | solution.py:281
  12.8 2.0 %band_matrices.1 = (bf16[2,80,384]{2,1,0:T(8,128)(2,1)S(1)}, bf16[2,64,256]{2,1,0:T(8,128)(2,1)S(1)}, bf16[2,48,256]{2,1,0:T(8,128)(2,1)S(1)}, bf16[2,32,256]{2,...) custom-call(f32[1,512]{1,0:T(1,128)S(1)} %pad_maximum_fusion.mine_re, ...), custom_call_target="tpu_custom_call" | custom-call | tf_op jit(solution)/shard_map/band_matrices/pallas_call | solution.py:201
  14.9 1.9 collective-permute-start.2
  16.8 9.4 %collective-permute-done.1.crossed_ref = f32[16,96,256]{2,1,0:T(8,128)S(1)} collective-permute-done((f32[16,96,256]{2,1,0:T(8,128)S(1)}, f32[16,96,256]{2,1,0:T(8,128)S(1)}, u32[]{:S(2)}, u32[]{:S(2)}) %collective-permute-start.1) | collective-permute-done | bytes 1572896 | tf_op jit(solution)/shard_map/ppermute | solution.py:34
  28.8 6.9 %collective-permute-start.6 = (f32[15,96,256]{2,1,0:T(8,128)}, f32[15,96,256]{2,1,0:T(8,128)}, u32[]{:S(2)}, u32[]{:S(2)}) collective-permute-start(f32[15,96,256]{2,1,0:T(8,128)} %get-tuple-element.83), channel_id=1, source_target_pairs={{2,8},{3,9},{4,10},{5,11},{6,12},{7,13},{8,2},{9,3},{10,4},{11,5},... | collective-permute-start | bytes 4423688 | tf_op jit(solution)/shard_map/ppermute | solution.py:34
  37.0 2.1 %collective-permute-done.2 = f32[17,80,256]{2,1,0:T(8,128)} collective-permute-done((f32[17,80,256]{2,1,0:T(8,128)}, f32[17,80,256]{2,1,0:T(8,128)}, u32[]{:S(2)}, u32[]{:S(2)}) %collective-permute-start.2) | collective-permute-done | bytes 1392672 | tf_op jit(solution)/shard_map/ppermute | solution.py:34
  40.6 1.9 collective-permute-start.3
  43.2 11.1 %collective-permute-done.9.own_ref = f32[17,80,256]{2,1,0:T(8,128)} collective-permute-done((f32[17,80,256]{2,1,0:T(8,128)}, f32[17,80,256]{2,1,0:T(8,128)}, u32[]{:S(2)}, u32[]{:S(2)}) %collective-permute-start.9) | collective-permute-done | bytes 1392672 | tf_op jit(solution)/shard_map/ppermute | solution.py:34
  54.3 2.7 %collective-permute-start.10 = (f32[17,80,256]{2,1,0:T(8,128)}, f32[17,80,256]{2,1,0:T(8,128)S(1)}, u32[]{:S(2)}, u32[]{:S(2)}) collective-permute-start(f32[17,80,256]{2,1,0:T(8,128)} %collective-permute-done.9.own_ref), channel_id=1, source_target_pairs={{2,8},{3,9},{4,10},{5,11},{6,12},{7,13},{8,2},{9,3},{10,4},{11,5},... | collective-permute-start | bytes 4177928 | tf_op jit(solution)/shard_map/ppermute | solution.py:34
  57.1 4.4 %blur_x_far.4 = (f32[16,96,256]{2,1,0:T(8,128)S(1)}, f32[16,96,256]{2,1,0:T(8,128)S(1)}) custom-call(bf16[2,256,384]{2,1,0:T(8,128)(2,1)S(1)} %get-tuple-element.72.hi_ref, bf16[2,256,384]{2,1,0:T(8,128)(2,1)S(1)} %get-tuple-element.73.lo_ref, f32[15,96,256]{2,1,0:T(8,128)} %collective-permute-done.6.refs_0_), custom_call_target="tpu_custom_call" | custom-call | tf_op jit(solution)/shard_map/blur_x_far/pallas_call | solution.py:329
  61.6 3.3 %blur_x_near.4 = (f32[16,96,256]{2,1,0:T(8,128)S(1)}, f32[16,96,256]{2,1,0:T(8,128)S(1)}) custom-call(bf16[2,256,384]{2,1,0:T(8,128)(2,1)S(1)} %get-tuple-element.72.hi_ref, bf16[2,256,384]{2,1,0:T(8,128)(2,1)S(1)} %get-tuple-element.73.lo_ref, f32[16,96,256]{2,1,0:T(8,128)S(1)} %get-tuple-element.79.refs_0_.before_ref, ...), custom_call_target="tpu_custom_call" | custom-call | tf_op jit(solution)/shard_map/blur_x_near/pallas_call | solution.py:329
  66.5 1.7 collective-permute-done.3.far_ref
  68.2 2.7 %image_and_ratio.2 = (f32[16,64,256]{2,1,0:T(8,128)S(1)}, f32[15,64,256]{2,1,0:T(8,128)S(1)}, f32[15,64,256]{2,1,0:T(8,128)S(1)}, f32[16,80,256]{2,1,0:T(8,128)S(1)}) custom-call(s32[2,3]{1,0:T(2,128)S(1)} %fusion.1.shift_ref, f32[17,80,256]{2,1,0:T(8,128)S(1)} %collective-permute-done.3.far_ref, f32[17,80,256]{2,1,0:T(8,128)S(1)} %collective-permute-done.4.near_ref, ...), custom_call_target="tpu_custom_call" | custom-call | tf_op jit(solution)/shard_map/image_and_ratio/pallas_call | solution.py:488
  70.9 3.3 %collective-permute-start.7 = (f32[15,64,256]{2,1,0:T(8,128)S(1)}, f32[15,64,256]{2,1,0:T(8,128)S(1)}, u32[]{:S(2)}, u32[]{:S(2)}) collective-permute-start(f32[15,64,256]{2,1,0:T(8,128)S(1)} %get-tuple-element.90), channel_id=1, source_target_pairs={{2,8},{3,9},{4,10},{5,11},{6,12},{7,13},{8,2},{9,3},{10,4},{11,5},... | collective-permute-start | bytes 2949128 | tf_op jit(solution)/shard_map/ppermute | solution.py:34
  75.9 7.2 %collective-permute-done.10.far_ref = f32[17,80,256]{2,1,0:T(8,128)S(1)} collective-permute-done((f32[17,80,256]{2,1,0:T(8,128)}, f32[17,80,256]{2,1,0:T(8,128)S(1)}, u32[]{:S(2)}, u32[]{:S(2)}) %collective-permute-start.10) | collective-permute-done | bytes 1392672 | tf_op jit(solution)/shard_map/ppermute | solution.py:34
  83.1 3.7 %image_and_ratio.3 = (f32[16,64,256]{2,1,0:T(8,128)S(1)}, f32[15,32,256]{2,1,0:T(8,128)S(1)}, f32[15,32,256]{2,1,0:T(8,128)S(1)}, f32[15,32,256]{2,1,0:T(8,128)S...) custom-call(s32[2,3]{1,0:T(2,128)S(1)} %fusion.1.shift_ref, ...), custom_call_target="tpu_custom_call" | custom-call | tf_op jit(solution)/shard_map/image_and_ratio/pallas_call | solution.py:488
  87.9 3.3 %collective-permute-start.15 = (f32[15,32,256]{2,1,0:T(8,128)S(1)}, f32[15,32,256]{2,1,0:T(8,128)S(1)}, u32[]{:S(2)}, u32[]{:S(2)}) collective-permute-start(f32[15,32,256]{2,1,0:T(8,128)S(1)} %get-tuple-element.99), channel_id=1, source_target_pairs={{2,8},{3,9},{4,10},{5,11},{6,12},{7,13},{8,2},{9,3},{10,4},{11,5},... | collective-permute-start | bytes 1474568 | tf_op jit(solution)/shard_map/ppermute | solution.py:34
  91.3 2.3 %collective-permute-done.7.refs_0_ = f32[15,64,256]{2,1,0:T(8,128)S(1)} collective-permute-done((f32[15,64,256]{2,1,0:T(8,128)S(1)}, f32[15,64,256]{2,1,0:T(8,128)S(1)}, u32[]{:S(2)}, u32[]{:S(2)}) %collective-permute-start.7) | collective-permute-done | bytes 983072 | tf_op jit(solution)/shard_map/ppermute | solution.py:34
  93.6 2.1 %log_factor.5.before_ref = f32[16,64,256]{2,1,0:T(8,128)S(1)} custom-call(bf16[2,256,384]{2,1,0:T(8,128)(2,1)S(1)} %get-tuple-element.72.hi_ref, bf16[2,256,384]{2,1,0:T(8,128)(2,1)S(1)} %get-tuple-element.73.lo_ref, f32[16,96,256]{2,1,0:T(8,128)S(1)} %get-tuple-element.79.refs_0_.before_ref, f32[15,64,256]{2,1,0:T(8,128)S(1)} %collective-permute-done.7.refs_0_, ...), custom_call_target="tpu_custom_call" | custom-call | tf_op jit(solution)/shard_map/log_factor/pallas_call | solution.py:521
  95.8 3.0 %collective-permute-done.15.refs_0_ = f32[15,32,256]{2,1,0:T(8,128)S(1)} collective-permute-done((f32[15,32,256]{2,1,0:T(8,128)S(1)}, f32[15,32,256]{2,1,0:T(8,128)S(1)}, u32[]{:S(2)}, u32[]{:S(2)}) %collective-permute-start.15) | collective-permute-done | bytes 491552 | tf_op jit(solution)/shard_map/ppermute | solution.py:34
  101.1 3.7 %collective-permute-start.12 = (f32[15,32,256]{2,1,0:T(8,128)S(1)}, f32[15,32,256]{2,1,0:T(8,128)S(1)}, u32[]{:S(2)}, u32[]{:S(2)}) collective-permute-start(f32[15,32,256]{2,1,0:T(8,128)S(1)} %get-tuple-element.96), channel_id=1, source_target_pairs={{2,8},{3,9},{4,10},{5,11},{6,12},{7,13},{8,2},{9,3},{10,4},{11,5},... | collective-permute-start | bytes 1474568 | tf_op jit(solution)/shard_map/ppermute | solution.py:34
  105.0 6.7 %collective-permute-done.12.refs_0_ = f32[15,32,256]{2,1,0:T(8,128)S(1)} collective-permute-done((f32[15,32,256]{2,1,0:T(8,128)S(1)}, f32[15,32,256]{2,1,0:T(8,128)S(1)}, u32[]{:S(2)}, u32[]{:S(2)}) %collective-permute-start.12) | collective-permute-done | bytes 491552 | tf_op jit(solution)/shard_map/ppermute | solution.py:34
  114.8 2.2 %collective-permute-start.21 = (f32[16,32,256]{2,1,0:T(8,128)S(1)}, f32[16,32,256]{2,1,0:T(8,128)S(1)}, u32[]{:S(2)}, u32[]{:S(2)}) collective-permute-start(f32[16,32,256]{2,1,0:T(8,128)S(1)} %get-tuple-element.111.refs_0_.before_ref), channel_id=1, source_target_pairs={{0,1},{1,0},{2,3},{3,2},{4,5},{5,4},{6,7},{7,6},{8,9},{9,8},{10,11... | collective-permute-start | bytes 1572872 | tf_op jit(solution)/shard_map/ppermute | solution.py:34
  117.0 4.1 %collective-permute-start.18 = (f32[15,32,256]{2,1,0:T(8,128)}, f32[15,32,256]{2,1,0:T(8,128)}, u32[]{:S(2)}, u32[]{:S(2)}) collective-permute-start(f32[15,32,256]{2,1,0:T(8,128)} %get-tuple-element.101), channel_id=1, source_target_pairs={{2,8},{3,9},{4,10},{5,11},{6,12},{7,13},{8,2},{9,3},{10,4},{11,5},... | collective-permute-start | bytes 1474568 | tf_op jit(solution)/shard_map/ppermute | solution.py:34
  121.2 5.0 %collective-permute-done.14.refs_1_ = f32[16,32,256]{2,1,0:T(8,128)} collective-permute-done((f32[16,32,256]{2,1,0:T(8,128)S(1)}, f32[16,32,256]{2,1,0:T(8,128)}, u32[]{:S(2)}, u32[]{:S(2)}) %collective-permute-start.14) | collective-permute-done | bytes 524320 | tf_op jit(solution)/shard_map/ppermute | solution.py:34
  126.2 1.8 collective-permute-done.18.refs_0_
  129.2 3.3 %collective-permute-start.19 = (f32[15,32,256]{2,1,0:T(8,128)S(1)}, f32[15,32,256]{2,1,0:T(8,128)S(1)}, u32[]{:S(2)}, u32[]{:S(2)}) collective-permute-start(f32[15,32,256]{2,1,0:T(8,128)S(1)} %get-tuple-element.106), channel_id=1, source_target_pairs={{2,8},{3,9},{4,10},{5,11},{6,12},{7,13},{8,2},{9,3},{10,4},{11,5},... | collective-permute-start | bytes 1474568 | tf_op jit(solution)/shard_map/ppermute | solution.py:34
  132.8 2.2 %collective-permute-start.22 = (f32[15,32,256]{2,1,0:T(8,128)S(1)}, f32[15,32,256]{2,1,0:T(8,128)S(1)}, u32[]{:S(2)}, u32[]{:S(2)}) collective-permute-start(f32[15,32,256]{2,1,0:T(8,128)S(1)} %get-tuple-element.140), channel_id=1, source_target_pairs={{2,8},{3,9},{4,10},{5,11},{6,12},{7,13},{8,2},{9,3},{10,4},{11,5},... | collective-permute-start | bytes 1474568 | tf_op jit(solution)/shard_map/ppermute | solution.py:34
  137.0 2.1 %blur_x_far.6 = (f32[16,32,256]{2,1,0:T(8,128)S(1)}, f32[16,32,256]{2,1,0:T(8,128)S(1)}) custom-call(bf16[2,256,384]{2,1,0:T(8,128)(2,1)S(1)} %get-tuple-element.72.hi_ref, bf16[2,256,384]{2,1,0:T(8,128)(2,1)S(1)} %get-tuple-element.73.lo_ref, f32[15,32,256]{2,1,0:T(8,128)} %collective-permute-done.18.refs_0_, ...), custom_call_target="tpu_custom_call" | custom-call | tf_op jit(solution)/shard_map/blur_x_far/pallas_call | solution.py:329
  141.3 3.7 %collective-permute-done.22.refs_0_ = f32[15,32,256]{2,1,0:T(8,128)S(1)} collective-permute-done((f32[15,32,256]{2,1,0:T(8,128)S(1)}, f32[15,32,256]{2,1,0:T(8,128)S(1)}, u32[]{:S(2)}, u32[]{:S(2)}) %collective-permute-start.22) | collective-permute-done | bytes 491552 | tf_op jit(solution)/shard_map/ppermute | solution.py:34
  145.0 5.2 %ratio.2 = (f32[16,32,256]{2,1,0:T(8,128)S(1)}, f32[16,32,256]{2,1,0:T(8,128)S(1)}, f32[2,15,32,256]{3,2,1,0:T(8,128)S(1)}, f32[2,15,32,256]{3,2,1,0:T(8,128)S(1)}, f32[2,16,32,256]{3,2,1,0:T(8,128)S(1)}) custom-call(f32[16,80,256]{2,1,0:T(8,128)S(1)} %copy-done.1, f32[16,80,256]{2,1,0:T(8,128)S(1)} %copy-done.3, ...), custom_call_target="tpu_custom_call" | custom-call | tf_op jit(solution)/shard_map/ratio/pallas_call | solution.py:476
  150.2 3.0 %collective-permute-start.25 = (f32[2,15,32,256]{3,2,1,0:T(8,128)S(1)}, f32[2,15,32,256]{3,2,1,0:T(8,128)S(1)}, u32[]{:S(2)}, u32[]{:S(2)}) collective-permute-start(f32[2,15,32,256]{3,2,1,0:T(8,128)S(1)} %get-tuple-element.124), channel_id=1, source_target_pairs={{2,8},{3,9},{4,10},{5,11},{6,12},{7,13},{8,2},{9,3},{10,4},{11,5},... | collective-permute-start | bytes 2949128 | tf_op jit(solution)/shard_map/ppermute | solution.py:34
  155.4 4.2 %ratio.3 = (f32[16,32,256]{2,1,0:T(8,128)S(1)}, f32[16,32,256]{2,1,0:T(8,128)S(1)}, f32[2,15,32,256]{3,2,1,0:T(8,128)S(1)}, f32[2,15,32,256]{3,2,1,0:T(8,128)S(1)}) custom-call(f32[16,80,256]{2,1,0:T(8,128)S(1)} %copy-done.1, f32[16,80,256]{2,1,0:T(8,128)S(1)} %copy-done.3, f32[16,32,256]{2,1,0:T(8,128)S(1)} %get-tuple-element.117.refs_3_.refs_2_, ...), custom_call_target="tpu_custom_call" | custom-call | tf_op jit(solution)/shard_map/ratio/pallas_call | solution.py:476
  159.6 2.6 %collective-permute-start.31 = (f32[2,15,32,256]{3,2,1,0:T(8,128)S(1)}, f32[2,15,32,256]{3,2,1,0:T(8,128)S(1)}, u32[]{:S(2)}, u32[]{:S(2)}) collective-permute-start(f32[2,15,32,256]{3,2,1,0:T(8,128)S(1)} %get-tuple-element.135), channel_id=1, source_target_pairs={{2,8},{3,9},{4,10},{5,11},{6,12},{7,13},{8,2},{9,3},{10,4},{11,5},... | collective-permute-start | bytes 2949128 | tf_op jit(solution)/shard_map/ppermute | solution.py:34
  162.7 3.1 %collective-permute-done.25.refs_0_.refs_3_ = f32[2,15,32,256]{3,2,1,0:T(8,128)S(1)} collective-permute-done((f32[2,15,32,256]{3,2,1,0:T(8,128)S(1)}, f32[2,15,32,256]{3,2,1,0:T(8,128)S(1)}, u32[]{:S(2)}, u32[]{:S(2)}) %collective-permute-start.25) | collective-permute-done | bytes 983072 | tf_op jit(solution)/shard_map/ppermute | solution.py:34
  165.9 1.7 log_factor.8.refs_0_
  168.3 2.6 %collective-permute-start.28 = (f32[16,32,256]{2,1,0:T(8,128)S(1)}, f32[16,32,256]{2,1,0:T(8,128)S(1)}, u32[]{:S(2)}, u32[]{:S(2)}) collective-permute-start(f32[16,32,256]{2,1,0:T(8,128)S(1)} %log_factor.8.refs_0_), channel_id=1, source_target_pairs={{1,24},{3,26},{5,28},{7,30},{8,17},{10,19},{12,21},{14,23},{17,8},... | collective-permute-start | bytes 1572872 | tf_op jit(solution)/shard_map/ppermute | solution.py:34
  170.9 3.9 %collective-permute-start.29 = (f32[16,32,256]{2,1,0:T(8,128)S(1)}, f32[16,32,256]{2,1,0:T(8,128)S(1)}, u32[]{:S(2)}, u32[]{:S(2)}) collective-permute-start(f32[16,32,256]{2,1,0:T(8,128)S(1)} %log_factor.8.refs_0_), channel_id=1, source_target_pairs={{1,8},{3,10},{5,12},{7,14},{8,1},{10,3},{12,5},{14,7},{17,24},{19,... | collective-permute-start | bytes 1572872 | tf_op jit(solution)/shard_map/ppermute | solution.py:34
  174.8 1.6 collective-permute-done.31.refs_0_.refs_3_
  176.4 1.7 log_factor.9.refs_0_
  178.8 2.6 %collective-permute-start.34 = (f32[16,32,256]{2,1,0:T(8,128)S(1)}, f32[16,32,256]{2,1,0:T(8,128)S(1)}, u32[]{:S(2)}, u32[]{:S(2)}) collective-permute-start(f32[16,32,256]{2,1,0:T(8,128)S(1)} %log_factor.9.refs_0_), channel_id=1, source_target_pairs={{1,24},{3,26},{5,28},{7,30},{8,17},{10,19},{12,21},{14,23},{17,8},... | collective-permute-start | bytes 1572872 | tf_op jit(solution)/shard_map/ppermute | solution.py:34
  181.5 3.9 %collective-permute-start.35 = (f32[16,32,256]{2,1,0:T(8,128)S(1)}, f32[16,32,256]{2,1,0:T(8,128)S(1)}, u32[]{:S(2)}, u32[]{:S(2)}) collective-permute-start(f32[16,32,256]{2,1,0:T(8,128)S(1)} %log_factor.9.refs_0_), channel_id=1, source_target_pairs={{1,8},{3,10},{5,12},{7,14},{8,1},{10,3},{12,5},{14,7},{17,24},{19,... | collective-permute-start | bytes 1572872 | tf_op jit(solution)/shard_map/ppermute | solution.py:34
  185.3 2.9 %collective-permute-done.29.refs_3_ = f32[16,32,256]{2,1,0:T(8,128)S(1)} collective-permute-done((f32[16,32,256]{2,1,0:T(8,128)S(1)}, f32[16,32,256]{2,1,0:T(8,128)S(1)}, u32[]{:S(2)}, u32[]{:S(2)}) %collective-permute-start.29) | collective-permute-done | bytes 524320 | tf_op jit(solution)/shard_map/ppermute | solution.py:34
  188.4 6.2 %collective-permute-done.34.refs_2_ = f32[16,32,256]{2,1,0:T(8,128)S(1)} collective-permute-done((f32[16,32,256]{2,1,0:T(8,128)S(1)}, f32[16,32,256]{2,1,0:T(8,128)S(1)}, u32[]{:S(2)}, u32[]{:S(2)}) %collective-permute-start.34) | collective-permute-done | bytes 524320 | tf_op jit(solution)/shard_map/ppermute | solution.py:34
  194.6 3.0 %collective-permute-done.35.refs_3_ = f32[16,32,256]{2,1,0:T(8,128)S(1)} collective-permute-done((f32[16,32,256]{2,1,0:T(8,128)S(1)}, f32[16,32,256]{2,1,0:T(8,128)S(1)}, u32[]{:S(2)}, u32[]{:S(2)}) %collective-permute-start.35) | collective-permute-done | bytes 524320 | tf_op jit(solution)/shard_map/ppermute | solution.py:34
  197.7 1.9 collective-permute-done.36.refs_3_
  (105 shorter events, 31.1 us)
Async XLA Ops:
  0.0 8.2 %copy-start.4 = (f32[1,16,128,256]{3,2,1,0:T(8,128)S(1)}, f32[1,16,128,256]{3,2,1,0:T(8,128)}, u32[]{:S(2)}) copy-start(f32[1,16,128,256]{3,2,1,0:T(8,128)} %param.7) | copy-start | bytes 6291460
  1.7 6.5 %copy-start.16 = (s32[1,16,128]{2,1,0:T(8,128)S(1)}, s32[1,16,128]{2,1,0:T(8,128)}, u32[]{:S(2)}) copy-start(s32[1,16,128]{2,1,0:T(8,128)} %param.10) | copy-start | bytes 24580
  1.7 6.5 %copy-start.17 = (s32[1,3]{1,0:T(1,128)S(1)}, s32[1,3]{1,0:T(1,128)}, u32[]{:S(2)}) copy-start(s32[1,3]{1,0:T(1,128)} %offsets_ref.1) | copy-start | bytes 40
  2.0 24.2 %collective-permute-start.1 = (f32[16,96,256]{2,1,0:T(8,128)S(1)}, f32[16,96,256]{2,1,0:T(8,128)S(1)}, u32[]{:S(2)}, u32[]{:S(2)}) collective-permute-start(f32[16,96,256]{2,1,0:T(8,128)S(1)} %get-tuple-element.78), channel_id=1, source_target_pairs={{0,1},{2,3},{4,5},{6,7},{9,8},{11,10},{13,12},{15,14},{16,17},{18,... | collective-permute-start | bytes 4718600 | tf_op jit(solution)/shard_map/ppermute | solution.py:34
  5.3 7.5 %collective-permute-start = (f32[1,512]{1,0:T(1,128)S(1)}, f32[1,512]{1,0:T(1,128)S(1)}, u32[]{:S(2)}, u32[]{:S(2)}) collective-permute-start(f32[1,512]{1,0:T(1,128)S(1)} %pad_maximum_fusion.mine_ref), channel_id=1, source_target_pairs={{0,8},{1,9},{2,10},{3,11},{4,12},{5,13},{6,14},{7,15},{8,0},{9,1},... | collective-permute-start | bytes 6152 | tf_op jit(solution)/shard_map/ppermute | solution.py:34
  14.8 12.8 %copy-start.6 = (bf16[2,64,256]{2,1,0:T(8,128)(2,1)}, bf16[2,64,256]{2,1,0:T(8,128)(2,1)S(1)}, u32[]{:S(2)}) copy-start(bf16[2,64,256]{2,1,0:T(8,128)(2,1)S(1)} %get-tuple-element.89.ya_ref) | copy-start | bytes 196612
  14.8 12.8 %copy-start.8 = (bf16[2,48,256]{2,1,0:T(8,128)(2,1)}, bf16[2,48,256]{2,1,0:T(8,128)(2,1)S(1)}, u32[]{:S(2)}) copy-start(bf16[2,48,256]{2,1,0:T(8,128)(2,1)S(1)} %get-tuple-element.122.refs_6_) | copy-start | bytes 147460
  14.9 12.8 %copy-start.10 = (bf16[2,32,256]{2,1,0:T(8,128)(2,1)}, bf16[2,32,256]{2,1,0:T(8,128)(2,1)S(1)}, u32[]{:S(2)}) copy-start(bf16[2,32,256]{2,1,0:T(8,128)(2,1)S(1)} %get-tuple-element.133.refs_7_) | copy-start | bytes 98308
  14.9 12.8 %copy-start.12 = (bf16[2,32,256]{2,1,0:T(8,128)(2,1)}, bf16[2,32,256]{2,1,0:T(8,128)(2,1)S(1)}, u32[]{:S(2)}) copy-start(bf16[2,32,256]{2,1,0:T(8,128)(2,1)S(1)} %get-tuple-element.134.refs_8_) | copy-start | bytes 98308
  14.9 12.8 %copy-start.14 = (bf16[2,32,256]{2,1,0:T(8,128)(2,1)}, bf16[2,32,256]{2,1,0:T(8,128)(2,1)S(1)}, u32[]{:S(2)}) copy-start(bf16[2,32,256]{2,1,0:T(8,128)(2,1)S(1)} %get-tuple-element.123.refs_7_) | copy-start | bytes 98308
  14.9 24.2 %collective-permute-start.2 = (f32[17,80,256]{2,1,0:T(8,128)}, f32[17,80,256]{2,1,0:T(8,128)}, u32[]{:S(2)}, u32[]{:S(2)}) collective-permute-start(f32[17,80,256]{2,1,0:T(8,128)} %get-tuple-element.81), channel_id=1, source_target_pairs={{1,8},{3,10},{5,12},{7,14},{8,1},{10,3},{12,5},{14,7},{17,24},{19,... | collective-permute-start | bytes 4177928 | tf_op jit(solution)/shard_map/ppermute | solution.py:34
  28.8 28.2 %collective-permute-start.6 = (f32[15,96,256]{2,1,0:T(8,128)}, f32[15,96,256]{2,1,0:T(8,128)}, u32[]{:S(2)}, u32[]{:S(2)}) collective-permute-start(f32[15,96,256]{2,1,0:T(8,128)} %get-tuple-element.83), channel_id=1, source_target_pairs={{2,8},{3,9},{4,10},{5,11},{6,12},{7,13},{8,2},{9,3},{10,4},{11,5},... | collective-permute-start | bytes 4423688 | tf_op jit(solution)/shard_map/ppermute | solution.py:34
  35.7 18.6 %collective-permute-start.9 = (f32[17,80,256]{2,1,0:T(8,128)}, f32[17,80,256]{2,1,0:T(8,128)}, u32[]{:S(2)}, u32[]{:S(2)}) collective-permute-start(f32[17,80,256]{2,1,0:T(8,128)} %get-tuple-element.94), channel_id=1, source_target_pairs={{0,1},{1,9},{2,3},{3,11},{4,5},{5,13},{6,7},{7,15},{8,0},{9,8},{10... | collective-permute-start | bytes 4177928 | tf_op jit(solution)/shard_map/ppermute | solution.py:34
  35.8 25.8 %collective-permute-start.5 = (f32[15,96,256]{2,1,0:T(8,128)}, f32[15,96,256]{2,1,0:T(8,128)S(1)}, u32[]{:S(2)}, u32[]{:S(2)}) collective-permute-start(f32[15,96,256]{2,1,0:T(8,128)} %copy-done.18), channel_id=1, source_target_pairs={{0,8},{1,9},{2,10},{3,11},{4,12},{5,13},{6,14},{7,15},{8,0},{9,1},... | collective-permute-start | bytes 4423688 | tf_op jit(solution)/shard_map/ppermute | solution.py:34
  40.6 27.5 %collective-permute-start.3 = (f32[17,80,256]{2,1,0:T(8,128)S(1)}, f32[17,80,256]{2,1,0:T(8,128)S(1)}, u32[]{:S(2)}, u32[]{:S(2)}) collective-permute-start(f32[17,80,256]{2,1,0:T(8,128)S(1)} %broadcast_select_fusion.own_ref), channel_id=1, source_target_pairs={{2,8},{3,9},{4,10},{5,11},{6,12},{7,13},{8,2},{9,3},{10,4},{11,5},... | collective-permute-start | bytes 4177928 | tf_op jit(solution)/shard_map/ppermute | solution.py:34
  42.6 25.6 %collective-permute-start.4 = (f32[17,80,256]{2,1,0:T(8,128)S(1)}, f32[17,80,256]{2,1,0:T(8,128)S(1)}, u32[]{:S(2)}, u32[]{:S(2)}) collective-permute-start(f32[17,80,256]{2,1,0:T(8,128)S(1)} %broadcast_select_fusion.own_ref), channel_id=1, source_target_pairs={{0,8},{1,9},{2,10},{3,11},{4,12},{5,13},{6,14},{7,15},{8,0},{9,1},... | collective-permute-start | bytes 4177928 | tf_op jit(solution)/shard_map/ppermute | solution.py:34
  54.3 28.8 %collective-permute-start.10 = (f32[17,80,256]{2,1,0:T(8,128)}, f32[17,80,256]{2,1,0:T(8,128)S(1)}, u32[]{:S(2)}, u32[]{:S(2)}) collective-permute-start(f32[17,80,256]{2,1,0:T(8,128)} %collective-permute-done.9.own_ref), channel_id=1, source_target_pairs={{2,8},{3,9},{4,10},{5,11},{6,12},{7,13},{8,2},{9,3},{10,4},{11,5},... | collective-permute-start | bytes 4177928 | tf_op jit(solution)/shard_map/ppermute | solution.py:34
  57.0 26.1 %collective-permute-start.11 = (f32[17,80,256]{2,1,0:T(8,128)}, f32[17,80,256]{2,1,0:T(8,128)S(1)}, u32[]{:S(2)}, u32[]{:S(2)}) collective-permute-start(f32[17,80,256]{2,1,0:T(8,128)} %collective-permute-done.9.own_ref), channel_id=1, source_target_pairs={{0,8},{1,9},{2,10},{3,11},{4,12},{5,13},{6,14},{7,15},{8,0},{9,1},... | collective-permute-start | bytes 4177928 | tf_op jit(solution)/shard_map/ppermute | solution.py:34
  70.9 5.0 %copy-start = (f32[16,80,256]{2,1,0:T(8,128)}, f32[16,80,256]{2,1,0:T(8,128)S(1)}, u32[]{:S(2)}) copy-start(f32[16,80,256]{2,1,0:T(8,128)S(1)} %get-tuple-element.104.refs_0_) | copy-start | bytes 3932164
  70.9 22.8 %collective-permute-start.7 = (f32[15,64,256]{2,1,0:T(8,128)S(1)}, f32[15,64,256]{2,1,0:T(8,128)S(1)}, u32[]{:S(2)}, u32[]{:S(2)}) collective-permute-start(f32[15,64,256]{2,1,0:T(8,128)S(1)} %get-tuple-element.90), channel_id=1, source_target_pairs={{2,8},{3,9},{4,10},{5,11},{6,12},{7,13},{8,2},{9,3},{10,4},{11,5},... | collective-permute-start | bytes 2949128 | tf_op jit(solution)/shard_map/ppermute | solution.py:34
  74.2 19.4 %collective-permute-start.8 = (f32[15,64,256]{2,1,0:T(8,128)S(1)}, f32[15,64,256]{2,1,0:T(8,128)S(1)}, u32[]{:S(2)}, u32[]{:S(2)}) collective-permute-start(f32[15,64,256]{2,1,0:T(8,128)S(1)} %get-tuple-element.91), channel_id=1, source_target_pairs={{0,8},{1,9},{2,10},{3,11},{4,12},{5,13},{6,14},{7,15},{8,0},{9,1},... | collective-permute-start | bytes 2949128 | tf_op jit(solution)/shard_map/ppermute | solution.py:34
  87.9 10.9 %collective-permute-start.15 = (f32[15,32,256]{2,1,0:T(8,128)S(1)}, f32[15,32,256]{2,1,0:T(8,128)S(1)}, u32[]{:S(2)}, u32[]{:S(2)}) collective-permute-start(f32[15,32,256]{2,1,0:T(8,128)S(1)} %get-tuple-element.99), channel_id=1, source_target_pairs={{2,8},{3,9},{4,10},{5,11},{6,12},{7,13},{8,2},{9,3},{10,4},{11,5},... | collective-permute-start | bytes 1474568 | tf_op jit(solution)/shard_map/ppermute | solution.py:34
  91.2 7.5 %collective-permute-start.16 = (f32[15,32,256]{2,1,0:T(8,128)S(1)}, f32[15,32,256]{2,1,0:T(8,128)S(1)}, u32[]{:S(2)}, u32[]{:S(2)}) collective-permute-start(f32[15,32,256]{2,1,0:T(8,128)S(1)} %get-tuple-element.100), channel_id=1, source_target_pairs={{0,8},{1,9},{2,10},{3,11},{4,12},{5,13},{6,14},{7,15},{8,0},{9,1},... | collective-permute-start | bytes 1474568 | tf_op jit(solution)/shard_map/ppermute | solution.py:34
  99.8 13.2 %collective-permute-start.17 = (f32[16,32,256]{2,1,0:T(8,128)S(1)}, f32[16,32,256]{2,1,0:T(8,128)S(1)}, u32[]{:S(2)}, u32[]{:S(2)}) collective-permute-start(f32[16,32,256]{2,1,0:T(8,128)S(1)} %log_factor.7.refs_0_), channel_id=1, source_target_pairs={{0,16},{1,17},{2,18},{3,19},{4,20},{5,21},{6,22},{7,23},{8,24},{9,... | collective-permute-start | bytes 1572872 | tf_op jit(solution)/shard_map/ppermute | solution.py:34
  101.1 10.5 %collective-permute-start.12 = (f32[15,32,256]{2,1,0:T(8,128)S(1)}, f32[15,32,256]{2,1,0:T(8,128)S(1)}, u32[]{:S(2)}, u32[]{:S(2)}) collective-permute-start(f32[15,32,256]{2,1,0:T(8,128)S(1)} %get-tuple-element.96), channel_id=1, source_target_pairs={{2,8},{3,9},{4,10},{5,11},{6,12},{7,13},{8,2},{9,3},{10,4},{11,5},... | collective-permute-start | bytes 1474568 | tf_op jit(solution)/shard_map/ppermute | solution.py:34
  104.9 6.8 %collective-permute-start.13 = (f32[15,32,256]{2,1,0:T(8,128)S(1)}, f32[15,32,256]{2,1,0:T(8,128)S(1)}, u32[]{:S(2)}, u32[]{:S(2)}) collective-permute-start(f32[15,32,256]{2,1,0:T(8,128)S(1)} %get-tuple-element.97), channel_id=1, source_target_pairs={{0,8},{1,9},{2,10},{3,11},{4,12},{5,13},{6,14},{7,15},{8,0},{9,1},... | collective-permute-start | bytes 1474568 | tf_op jit(solution)/shard_map/ppermute | solution.py:34
  112.8 13.4 %collective-permute-start.14 = (f32[16,32,256]{2,1,0:T(8,128)S(1)}, f32[16,32,256]{2,1,0:T(8,128)}, u32[]{:S(2)}, u32[]{:S(2)}) collective-permute-start(f32[16,32,256]{2,1,0:T(8,128)S(1)} %log_factor.6.refs_0_), channel_id=1, source_target_pairs={{0,16},{1,17},{2,18},{3,19},{4,20},{5,21},{6,22},{7,23},{8,24},{9,... | collective-permute-start | bytes 1572872 | tf_op jit(solution)/shard_map/ppermute | solution.py:34
  114.8 17.9 %collective-permute-start.21 = (f32[16,32,256]{2,1,0:T(8,128)S(1)}, f32[16,32,256]{2,1,0:T(8,128)S(1)}, u32[]{:S(2)}, u32[]{:S(2)}) collective-permute-start(f32[16,32,256]{2,1,0:T(8,128)S(1)} %get-tuple-element.111.refs_0_.before_ref), channel_id=1, source_target_pairs={{0,1},{1,0},{2,3},{3,2},{4,5},{5,4},{6,7},{7,6},{8,9},{9,8},{10,11... | collective-permute-start | bytes 1572872 | tf_op jit(solution)/shard_map/ppermute | solution.py:34
  117.0 11.0 %collective-permute-start.18 = (f32[15,32,256]{2,1,0:T(8,128)}, f32[15,32,256]{2,1,0:T(8,128)}, u32[]{:S(2)}, u32[]{:S(2)}) collective-permute-start(f32[15,32,256]{2,1,0:T(8,128)} %get-tuple-element.101), channel_id=1, source_target_pairs={{2,8},{3,9},{4,10},{5,11},{6,12},{7,13},{8,2},{9,3},{10,4},{11,5},... | collective-permute-start | bytes 1474568 | tf_op jit(solution)/shard_map/ppermute | solution.py:34
  121.1 14.8 %collective-permute-start.24 = (f32[15,32,256]{2,1,0:T(8,128)}, f32[15,32,256]{2,1,0:T(8,128)S(1)}, u32[]{:S(2)}, u32[]{:S(2)}) collective-permute-start(f32[15,32,256]{2,1,0:T(8,128)} %copy-done.19), channel_id=1, source_target_pairs={{0,8},{1,9},{2,10},{3,11},{4,12},{5,13},{6,14},{7,15},{8,0},{9,1},... | collective-permute-start | bytes 1474568 | tf_op jit(solution)/shard_map/ppermute | solution.py:34
  129.2 11.0 %collective-permute-start.19 = (f32[15,32,256]{2,1,0:T(8,128)S(1)}, f32[15,32,256]{2,1,0:T(8,128)S(1)}, u32[]{:S(2)}, u32[]{:S(2)}) collective-permute-start(f32[15,32,256]{2,1,0:T(8,128)S(1)} %get-tuple-element.106), channel_id=1, source_target_pairs={{2,8},{3,9},{4,10},{5,11},{6,12},{7,13},{8,2},{9,3},{10,4},{11,5},... | collective-permute-start | bytes 1474568 | tf_op jit(solution)/shard_map/ppermute | solution.py:34
  132.6 6.5 %collective-permute-start.20 = (f32[15,32,256]{2,1,0:T(8,128)S(1)}, f32[15,32,256]{2,1,0:T(8,128)S(1)}, u32[]{:S(2)}, u32[]{:S(2)}) collective-permute-start(f32[15,32,256]{2,1,0:T(8,128)S(1)} %get-tuple-element.107), channel_id=1, source_target_pairs={{0,8},{1,9},{2,10},{3,11},{4,12},{5,13},{6,14},{7,15},{8,0},{9,1},... | collective-permute-start | bytes 1474568 | tf_op jit(solution)/shard_map/ppermute | solution.py:34
  132.8 12.2 %collective-permute-start.22 = (f32[15,32,256]{2,1,0:T(8,128)S(1)}, f32[15,32,256]{2,1,0:T(8,128)S(1)}, u32[]{:S(2)}, u32[]{:S(2)}) collective-permute-start(f32[15,32,256]{2,1,0:T(8,128)S(1)} %get-tuple-element.140), channel_id=1, source_target_pairs={{2,8},{3,9},{4,10},{5,11},{6,12},{7,13},{8,2},{9,3},{10,4},{11,5},... | collective-permute-start | bytes 1474568 | tf_op jit(solution)/shard_map/ppermute | solution.py:34
  135.0 10.0 %collective-permute-start.23 = (f32[15,32,256]{2,1,0:T(8,128)S(1)}, f32[15,32,256]{2,1,0:T(8,128)S(1)}, u32[]{:S(2)}, u32[]{:S(2)}) collective-permute-start(f32[15,32,256]{2,1,0:T(8,128)S(1)} %get-tuple-element.139), channel_id=1, source_target_pairs={{0,8},{1,9},{2,10},{3,11},{4,12},{5,13},{6,14},{7,15},{8,0},{9,1},... | collective-permute-start | bytes 1474568 | tf_op jit(solution)/shard_map/ppermute | solution.py:34
  139.1 5.8 %copy-start.3 = (f32[16,80,256]{2,1,0:T(8,128)S(1)}, f32[16,80,256]{2,1,0:T(8,128)}, u32[]{:S(2)}) copy-start(f32[16,80,256]{2,1,0:T(8,128)} %copy-done.2) | copy-start | bytes 3932164
  140.2 4.7 %copy-start.1 = (f32[16,80,256]{2,1,0:T(8,128)S(1)}, f32[16,80,256]{2,1,0:T(8,128)}, u32[]{:S(2)}) copy-start(f32[16,80,256]{2,1,0:T(8,128)} %copy-done) | copy-start | bytes 3932164
  150.2 15.7 %collective-permute-start.25 = (f32[2,15,32,256]{3,2,1,0:T(8,128)S(1)}, f32[2,15,32,256]{3,2,1,0:T(8,128)S(1)}, u32[]{:S(2)}, u32[]{:S(2)}) collective-permute-start(f32[2,15,32,256]{3,2,1,0:T(8,128)S(1)} %get-tuple-element.124), channel_id=1, source_target_pairs={{2,8},{3,9},{4,10},{5,11},{6,12},{7,13},{8,2},{9,3},{10,4},{11,5},... | collective-permute-start | bytes 2949128 | tf_op jit(solution)/shard_map/ppermute | solution.py:34
  153.1 12.8 %collective-permute-start.26 = (f32[2,15,32,256]{3,2,1,0:T(8,128)S(1)}, f32[2,15,32,256]{3,2,1,0:T(8,128)S(1)}, u32[]{:S(2)}, u32[]{:S(2)}) collective-permute-start(f32[2,15,32,256]{3,2,1,0:T(8,128)S(1)} %get-tuple-element.125), channel_id=1, source_target_pairs={{0,8},{1,9},{2,10},{3,11},{4,12},{5,13},{6,14},{7,15},{8,0},{9,1},... | collective-permute-start | bytes 2949128 | tf_op jit(solution)/shard_map/ppermute | solution.py:34
  159.6 16.8 %collective-permute-start.31 = (f32[2,15,32,256]{3,2,1,0:T(8,128)S(1)}, f32[2,15,32,256]{3,2,1,0:T(8,128)S(1)}, u32[]{:S(2)}, u32[]{:S(2)}) collective-permute-start(f32[2,15,32,256]{3,2,1,0:T(8,128)S(1)} %get-tuple-element.135), channel_id=1, source_target_pairs={{2,8},{3,9},{4,10},{5,11},{6,12},{7,13},{8,2},{9,3},{10,4},{11,5},... | collective-permute-start | bytes 2949128 | tf_op jit(solution)/shard_map/ppermute | solution.py:34
  162.2 14.2 %collective-permute-start.32 = (f32[2,15,32,256]{3,2,1,0:T(8,128)S(1)}, f32[2,15,32,256]{3,2,1,0:T(8,128)S(1)}, u32[]{:S(2)}, u32[]{:S(2)}) collective-permute-start(f32[2,15,32,256]{3,2,1,0:T(8,128)S(1)} %get-tuple-element.136), channel_id=1, source_target_pairs={{0,8},{1,9},{2,10},{3,11},{4,12},{5,13},{6,14},{7,15},{8,0},{9,1},... | collective-permute-start | bytes 2949128 | tf_op jit(solution)/shard_map/ppermute | solution.py:34
  167.6 13.9 %collective-permute-start.27 = (f32[16,32,256]{2,1,0:T(8,128)S(1)}, f32[16,32,256]{2,1,0:T(8,128)S(1)}, u32[]{:S(2)}, u32[]{:S(2)}) collective-permute-start(f32[16,32,256]{2,1,0:T(8,128)S(1)} %log_factor.8.refs_0_), channel_id=1, source_target_pairs={{0,16},{2,18},{4,20},{6,22},{9,25},{11,27},{13,29},{15,31},{16,0},... | collective-permute-start | bytes 1572872 | tf_op jit(solution)/shard_map/ppermute | solution.py:34
  168.3 17.1 %collective-permute-start.28 = (f32[16,32,256]{2,1,0:T(8,128)S(1)}, f32[16,32,256]{2,1,0:T(8,128)S(1)}, u32[]{:S(2)}, u32[]{:S(2)}) collective-permute-start(f32[16,32,256]{2,1,0:T(8,128)S(1)} %log_factor.8.refs_0_), channel_id=1, source_target_pairs={{1,24},{3,26},{5,28},{7,30},{8,17},{10,19},{12,21},{14,23},{17,8},... | collective-permute-start | bytes 1572872 | tf_op jit(solution)/shard_map/ppermute | solution.py:34
  170.9 17.3 %collective-permute-start.29 = (f32[16,32,256]{2,1,0:T(8,128)S(1)}, f32[16,32,256]{2,1,0:T(8,128)S(1)}, u32[]{:S(2)}, u32[]{:S(2)}) collective-permute-start(f32[16,32,256]{2,1,0:T(8,128)S(1)} %log_factor.8.refs_0_), channel_id=1, source_target_pairs={{1,8},{3,10},{5,12},{7,14},{8,1},{10,3},{12,5},{14,7},{17,24},{19,... | collective-permute-start | bytes 1572872 | tf_op jit(solution)/shard_map/ppermute | solution.py:34
  178.1 10.3 %collective-permute-start.33 = (f32[16,32,256]{2,1,0:T(8,128)S(1)}, f32[16,32,256]{2,1,0:T(8,128)S(1)}, u32[]{:S(2)}, u32[]{:S(2)}) collective-permute-start(f32[16,32,256]{2,1,0:T(8,128)S(1)} %log_factor.9.refs_0_), channel_id=1, source_target_pairs={{0,16},{2,18},{4,20},{6,22},{9,25},{11,27},{13,29},{15,31},{16,0},... | collective-permute-start | bytes 1572872 | tf_op jit(solution)/shard_map/ppermute | solution.py:34
  178.8 15.8 %collective-permute-start.34 = (f32[16,32,256]{2,1,0:T(8,128)S(1)}, f32[16,32,256]{2,1,0:T(8,128)S(1)}, u32[]{:S(2)}, u32[]{:S(2)}) collective-permute-start(f32[16,32,256]{2,1,0:T(8,128)S(1)} %log_factor.9.refs_0_), channel_id=1, source_target_pairs={{1,24},{3,26},{5,28},{7,30},{8,17},{10,19},{12,21},{14,23},{17,8},... | collective-permute-start | bytes 1572872 | tf_op jit(solution)/shard_map/ppermute | solution.py:34
  181.5 16.1 %collective-permute-start.35 = (f32[16,32,256]{2,1,0:T(8,128)S(1)}, f32[16,32,256]{2,1,0:T(8,128)S(1)}, u32[]{:S(2)}, u32[]{:S(2)}) collective-permute-start(f32[16,32,256]{2,1,0:T(8,128)S(1)} %log_factor.9.refs_0_), channel_id=1, source_target_pairs={{1,8},{3,10},{5,12},{7,14},{8,1},{10,3},{12,5},{14,7},{17,24},{19,... | collective-permute-start | bytes 1572872 | tf_op jit(solution)/shard_map/ppermute | solution.py:34
  188.3 9.4 %collective-permute-start.30 = (f32[16,32,256]{2,1,0:T(8,128)S(1)}, f32[16,32,256]{2,1,0:T(8,128)S(1)}, u32[]{:S(2)}, u32[]{:S(2)}) collective-permute-start(f32[16,32,256]{2,1,0:T(8,128)S(1)} %last_update.2.refs_0_), channel_id=1, source_target_pairs={{0,8},{1,9},{2,10},{3,11},{4,12},{5,13},{6,14},{7,15},{8,0},{9,1},... | collective-permute-start | bytes 1572872 | tf_op jit(solution)/shard_map/ppermute | solution.py:34
  197.6 2.0 collective-permute-start.36
  (10 other events, 23.1 us)

commit v11 on v10

--- a/solution.py
+++ b/solution.py
@@ -612,15 +612,16 @@
     acquired = after(acquired, window)
     first, second = shift_and_cut(offsets, acquired[0], view_mask[0], near)
 
-    mine = [jnp.pad(row, ((0, 0), (0, 128 - row.shape[1]))) for row in (kern_x, kern_y, kern_z, offsets.astype(F32))]
+    mine = [jnp.pad(row, ((0, 0), (0, 128 - row.shape[1]))) for row in (kern_x, kern_y, kern_z)]
     mine = jnp.concatenate(mine, axis=1)
     other = send(mine, to_core_partner)
     taps = kern_x.shape[1], taps_y, kern_z.shape[1]
     tables = make_tables(mine, other, taps, planes, cells_y, cells_z, (own_rows, near, wide))
-    shifts = jnp.where(straight, jnp.concatenate([mine, other]), jnp.concatenate([other, mine]))
-    shifts = shifts[:, 384:384 + offsets.shape[1]].astype(jnp.int32)
-
-    arrived = send(after(first, tables.whole[0]), lambda g, c, q, r: (g, r, q, c) if c != r else None)
+    mine = after(offsets.astype(F32), tables.whole[0])
+    other = send(mine, to_core_partner)
+    shifts = jnp.where(straight, jnp.concatenate([mine, other]), jnp.concatenate([other, mine])).astype(jnp.int32)
+
+    arrived = send(after(first, other), lambda g, c, q, r: (g, r, q, c) if c != r else None)
     current, distant, close = choose(after(window, first), crossed, radius)
     second = send(after(second, current), lambda g, c, q, r: (g, r, q, 1 - c))
     distant, close = neighbours(distant, close)
@@ -648,11 +649,10 @@
         chunks, before = [], []
         for total in totals:
             parts = [total] + [send(total, across(turn)) for turn in range(1, groups)]
-            if chunks:
-                parts[-1] = after(parts[-1], chunks[0][0])
             rows, distant, close = update(parts, radius)
             if total is totals[0]:
                 beyond = send(rows, to_row_partner)
+            distant = after(distant, chunks[0][0]) if chunks else distant
             distant, close = neighbours(distant, close)
             chunks.append((distant, blur_near(tables, rows, close)))
             before.append(rows)
@@ -662,10 +662,11 @@
             lax.dynamic_slice_in_dim(beyond, (1 - core()) * rest, radius, 0),
         )
         edge_parts, inner_parts = [blur_far(tables, *chunk) for chunk in chunks]
+        halo_parts = blur_near(tables, beyond, close)
         *inner_spreads, distant_inner, close_inner, passed = next_ratio(
-            images, list(zip([after(after(part, distant), close) for part in inner_parts], edge_parts)), None, tables.inner, tables.z, radius, 2 * (near - own_rows), 0
+            images, list(zip([after(after(part, distant), halo_parts[0]) for part in inner_parts], edge_parts)), None, tables.inner, tables.z, radius, 2 * (near - own_rows), 0
         )
-        halo_parts = blur_far(tables, distant, blur_near(tables, beyond, close))
+        halo_parts = blur_far(tables, distant, halo_parts)
         inner_side = neighbours(distant_inner, close_inner)
         *edge_spreads, distant, close = next_ratio(
             images, list(zip(edge_parts, halo_parts)), passed, tables.edge, tables.z, radius, 0,

time: 203 us -> 202 us (level)
    ppermute x37 -> x38, waiting for transfers between devices: 72.7 us -> 73.3 us  [send(): return lax.ppermute(array, AXES, moves(move))]
    ppermute x37 -> x38, starting transfers between devices: 65.5 us -> 66 us  [send(): return lax.ppermute(array, AXES, moves(move))]
    unnamed x42 -> x40, local copies, waits for them, and re-layouts: 4.82 us -> 4.82 us
  transfers between devices with their start and end apart: 37 -> 38, of which waited for: 17 -> 18; matrix products, arithmetic and copies ran while one was open for 2% -> 1% of each run, Pallas kernels for 23% -> 22%
where the time goes in v11:
time: 202 us
  waiting for transfers between devices  73.3 us (36%)
  starting transfers between devices  66 us (33%)
  Pallas kernels  53.6 us (27%)
  local copies, waits for them, and re-layouts  4.9 us (2%)
  other arithmetic  2.89 us (1%)
    ppermute x38, waiting for transfers between devices, send(): return lax.ppermute(array, AXES, moves(move))  73.3 us
    ppermute x38, starting transfers between devices, send(): return lax.ppermute(array, AXES, moves(move))  66 us
    pallas_call x8, Pallas kernels, blur_x(): call(kernel, (shape, shape), [VMEM] * len(operands), 'blur_x_far' if far...  15.1 us
    pallas_call x2, Pallas kernels, next_ratio(): return call(kernel, out_shape, [VMEM] * len(operands), 'ratio')(*operands)  9.34 us
    pallas_call x5, Pallas kernels, log_factor(): call(kernel, shape, [VMEM] * (3 + len(parts)), 'log_factor')  7.67 us
    pallas_call x2, Pallas kernels, first_ratio(): call(kernel, out_shape, in_specs, 'image_and_ratio', scratch)  6.36 us
    unnamed x40, local copies, waits for them, and re-layouts  4.82 us
    pallas_call x1, Pallas kernels, shift_and_cut(): call(shift_kernel, (shape, shape), [SMEM, VMEM, VMEM], 'shift_recorded',...  4.55 us
  transfers between devices with their start and end apart: 38, of which 18 were waited for; matrix products, arithmetic and copies ran while one was open for 1% of the time, Pallas kernels for 22%

profile of v11, /device:TPU:17, one launch (start us, length us, event | category | flops | bytes accessed | tf_op | source)
XLA Modules:
  0.0 201.6 jit_solution(9420959088744020711)
XLA Ops:
  0.0 1.7 copy-done.5
  4.0 2.9 %collective-permute-start = (f32[1,384]{1,0:T(1,128)S(1)}, f32[1,384]{1,0:T(1,128)S(1)}, u32[]{:S(2)}, u32[]{:S(2)}) collective-permute-start(f32[1,384]{1,0:T(1,128)S(1)} %fusion.1.mine_ref), channel_id=1, source_target_pairs={{0,8},{1,9},{2,10},{3,11},{4,12},{5,13},{6,14},{7,15},{8,0},{9,1},... | collective-permute-start | bytes 4616 | tf_op jit(solution)/shard_map/ppermute | solution.py:34
  7.5 4.6 %shift_recorded.1 = (f32[17,80,256]{2,1,0:T(8,128)}, f32[17,80,256]{2,1,0:T(8,128)}) custom-call(s32[1,3]{1,0:T(1,128)S(1)} %copy-done.17, f32[16,128,256]{2,1,0:T(8,128)S(1)} %bitcast.2, s32[16,128]{1,0:T(8,128)S(1)} %bitcast.3), custom_call_target="tpu_custom_call" | custom-call | tf_op jit(solution)/shard_map/shift_recorded/pallas_call | solution.py:281
  12.1 2.0 %band_matrices.1 = (bf16[2,80,384]{2,1,0:T(8,128)(2,1)S(1)}, bf16[2,64,256]{2,1,0:T(8,128)(2,1)S(1)}, bf16[2,48,256]{2,1,0:T(8,128)(2,1)S(1)}, bf16[2,32,256]{2,...) custom-call(f32[1,384]{1,0:T(1,128)S(1)} %fusion.1.mine_ref, ...), custom_call_target="tpu_custom_call" | custom-call | tf_op jit(solution)/shard_map/band_matrices/pallas_call | solution.py:201
  15.3 1.9 collective-permute-start.3
  17.3 8.5 %collective-permute-done.1.crossed_ref = f32[16,96,256]{2,1,0:T(8,128)S(1)} collective-permute-done((f32[16,96,256]{2,1,0:T(8,128)S(1)}, f32[16,96,256]{2,1,0:T(8,128)S(1)}, u32[]{:S(2)}, u32[]{:S(2)}) %collective-permute-start.1) | collective-permute-done | bytes 1572896 | tf_op jit(solution)/shard_map/ppermute | solution.py:34
  28.4 6.9 %collective-permute-start.7 = (f32[15,96,256]{2,1,0:T(8,128)}, f32[15,96,256]{2,1,0:T(8,128)}, u32[]{:S(2)}, u32[]{:S(2)}) collective-permute-start(f32[15,96,256]{2,1,0:T(8,128)} %get-tuple-element.85), channel_id=1, source_target_pairs={{2,8},{3,9},{4,10},{5,11},{6,12},{7,13},{8,2},{9,3},{10,4},{11,5},... | collective-permute-start | bytes 4423688 | tf_op jit(solution)/shard_map/ppermute | solution.py:34
  36.6 3.0 %collective-permute-done.3 = f32[17,80,256]{2,1,0:T(8,128)} collective-permute-done((f32[17,80,256]{2,1,0:T(8,128)}, f32[17,80,256]{2,1,0:T(8,128)}, u32[]{:S(2)}, u32[]{:S(2)}) %collective-permute-start.3) | collective-permute-done | bytes 1392672 | tf_op jit(solution)/shard_map/ppermute | solution.py:34
  41.1 1.9 collective-permute-start.4
  43.6 10.2 %collective-permute-done.10.own_ref = f32[17,80,256]{2,1,0:T(8,128)} collective-permute-done((f32[17,80,256]{2,1,0:T(8,128)}, f32[17,80,256]{2,1,0:T(8,128)}, u32[]{:S(2)}, u32[]{:S(2)}) %collective-permute-start.10) | collective-permute-done | bytes 1392672 | tf_op jit(solution)/shard_map/ppermute | solution.py:34
  53.9 3.1 %collective-permute-start.11 = (f32[17,80,256]{2,1,0:T(8,128)}, f32[17,80,256]{2,1,0:T(8,128)S(1)}, u32[]{:S(2)}, u32[]{:S(2)}) collective-permute-start(f32[17,80,256]{2,1,0:T(8,128)} %collective-permute-done.10.own_ref), channel_id=1, source_target_pairs={{2,8},{3,9},{4,10},{5,11},{6,12},{7,13},{8,2},{9,3},{10,4},{11,5},... | collective-permute-start | bytes 4177928 | tf_op jit(solution)/shard_map/ppermute | solution.py:34
  57.1 4.5 %blur_x_far.4 = (f32[16,96,256]{2,1,0:T(8,128)S(1)}, f32[16,96,256]{2,1,0:T(8,128)S(1)}) custom-call(bf16[2,256,384]{2,1,0:T(8,128)(2,1)S(1)} %get-tuple-element.73.hi_ref, bf16[2,256,384]{2,1,0:T(8,128)(2,1)S(1)} %get-tuple-element.74.lo_ref, f32[15,96,256]{2,1,0:T(8,128)} %collective-permute-done.7.refs_0_), custom_call_target="tpu_custom_call" | custom-call | tf_op jit(solution)/shard_map/blur_x_far/pallas_call | solution.py:329
  61.6 3.3 %blur_x_near.4 = (f32[16,96,256]{2,1,0:T(8,128)S(1)}, f32[16,96,256]{2,1,0:T(8,128)S(1)}) custom-call(bf16[2,256,384]{2,1,0:T(8,128)(2,1)S(1)} %get-tuple-element.73.hi_ref, bf16[2,256,384]{2,1,0:T(8,128)(2,1)S(1)} %get-tuple-element.74.lo_ref, f32[16,96,256]{2,1,0:T(8,128)S(1)} %get-tuple-element.80.refs_0_.before_ref, ...), custom_call_target="tpu_custom_call" | custom-call | tf_op jit(solution)/shard_map/blur_x_near/pallas_call | solution.py:329
  64.9 1.6 blur_yz.2.blurred_ref
  67.7 2.7 %image_and_ratio.2 = (f32[16,64,256]{2,1,0:T(8,128)S(1)}, f32[15,64,256]{2,1,0:T(8,128)S(1)}, f32[15,64,256]{2,1,0:T(8,128)S(1)}, f32[16,80,256]{2,1,0:T(8,128)S(1)}) custom-call(s32[2,3]{1,0:T(2,128)S(1)} %fusion.2.shift_ref, f32[17,80,256]{2,1,0:T(8,128)S(1)} %collective-permute-done.4.far_ref, f32[17,80,256]{2,1,0:T(8,128)S(1)} %collective-permute-done.5.near_ref, ...), custom_call_target="tpu_custom_call" | custom-call | tf_op jit(solution)/shard_map/image_and_ratio/pallas_call | solution.py:488
  70.4 3.3 %collective-permute-start.8 = (f32[15,64,256]{2,1,0:T(8,128)S(1)}, f32[15,64,256]{2,1,0:T(8,128)S(1)}, u32[]{:S(2)}, u32[]{:S(2)}) collective-permute-start(f32[15,64,256]{2,1,0:T(8,128)S(1)} %get-tuple-element.92), channel_id=1, source_target_pairs={{2,8},{3,9},{4,10},{5,11},{6,12},{7,13},{8,2},{9,3},{10,4},{11,5},... | collective-permute-start | bytes 2949128 | tf_op jit(solution)/shard_map/ppermute | solution.py:34
  73.8 1.6 blur_yz.3.blurred_ref
  75.4 7.2 %collective-permute-done.11.far_ref = f32[17,80,256]{2,1,0:T(8,128)S(1)} collective-permute-done((f32[17,80,256]{2,1,0:T(8,128)}, f32[17,80,256]{2,1,0:T(8,128)S(1)}, u32[]{:S(2)}, u32[]{:S(2)}) %collective-permute-start.11) | collective-permute-done | bytes 1392672 | tf_op jit(solution)/shard_map/ppermute | solution.py:34
  82.6 3.7 %image_and_ratio.3 = (f32[16,64,256]{2,1,0:T(8,128)S(1)}, f32[15,32,256]{2,1,0:T(8,128)S(1)}, f32[15,32,256]{2,1,0:T(8,128)S(1)}, f32[15,32,256]{2,1,0:T(8,128)S...) custom-call(s32[2,3]{1,0:T(2,128)S(1)} %fusion.2.shift_ref, ...), custom_call_target="tpu_custom_call" | custom-call | tf_op jit(solution)/shard_map/image_and_ratio/pallas_call | solution.py:488
  87.4 3.3 %collective-permute-start.16 = (f32[15,32,256]{2,1,0:T(8,128)S(1)}, f32[15,32,256]{2,1,0:T(8,128)S(1)}, u32[]{:S(2)}, u32[]{:S(2)}) collective-permute-start(f32[15,32,256]{2,1,0:T(8,128)S(1)} %get-tuple-element.105), channel_id=1, source_target_pairs={{2,8},{3,9},{4,10},{5,11},{6,12},{7,13},{8,2},{9,3},{10,4},{11,5},... | collective-permute-start | bytes 1474568 | tf_op jit(solution)/shard_map/ppermute | solution.py:34
  90.9 2.3 %collective-permute-done.8.refs_0_ = f32[15,64,256]{2,1,0:T(8,128)S(1)} collective-permute-done((f32[15,64,256]{2,1,0:T(8,128)S(1)}, f32[15,64,256]{2,1,0:T(8,128)S(1)}, u32[]{:S(2)}, u32[]{:S(2)}) %collective-permute-start.8) | collective-permute-done | bytes 983072 | tf_op jit(solution)/shard_map/ppermute | solution.py:34
  93.2 2.1 %log_factor.5.before_ref = f32[16,64,256]{2,1,0:T(8,128)S(1)} custom-call(bf16[2,256,384]{2,1,0:T(8,128)(2,1)S(1)} %get-tuple-element.73.hi_ref, bf16[2,256,384]{2,1,0:T(8,128)(2,1)S(1)} %get-tuple-element.74.lo_ref, f32[16,96,256]{2,1,0:T(8,128)S(1)} %get-tuple-element.80.refs_0_.before_ref, f32[15,64,256]{2,1,0:T(8,128)S(1)} %collective-permute-done.8.refs_0_, ...), custom_call_target="tpu_custom_call" | custom-call | tf_op jit(solution)/shard_map/log_factor/pallas_call | solution.py:521
  95.3 3.0 %collective-permute-done.16.refs_0_ = f32[15,32,256]{2,1,0:T(8,128)S(1)} collective-permute-done((f32[15,32,256]{2,1,0:T(8,128)S(1)}, f32[15,32,256]{2,1,0:T(8,128)S(1)}, u32[]{:S(2)}, u32[]{:S(2)}) %collective-permute-start.16) | collective-permute-done | bytes 491552 | tf_op jit(solution)/shard_map/ppermute | solution.py:34
  100.7 3.8 %collective-permute-start.13 = (f32[15,32,256]{2,1,0:T(8,128)S(1)}, f32[15,32,256]{2,1,0:T(8,128)S(1)}, u32[]{:S(2)}, u32[]{:S(2)}) collective-permute-start(f32[15,32,256]{2,1,0:T(8,128)S(1)} %get-tuple-element.98), channel_id=1, source_target_pairs={{2,8},{3,9},{4,10},{5,11},{6,12},{7,13},{8,2},{9,3},{10,4},{11,5},... | collective-permute-start | bytes 1474568 | tf_op jit(solution)/shard_map/ppermute | solution.py:34
  104.5 6.7 %collective-permute-done.13.refs_0_ = f32[15,32,256]{2,1,0:T(8,128)S(1)} collective-permute-done((f32[15,32,256]{2,1,0:T(8,128)S(1)}, f32[15,32,256]{2,1,0:T(8,128)S(1)}, u32[]{:S(2)}, u32[]{:S(2)}) %collective-permute-start.13) | collective-permute-done | bytes 491552 | tf_op jit(solution)/shard_map/ppermute | solution.py:34
  114.4 2.2 %collective-permute-start.22 = (f32[16,32,256]{2,1,0:T(8,128)S(1)}, f32[16,32,256]{2,1,0:T(8,128)S(1)}, u32[]{:S(2)}, u32[]{:S(2)}) collective-permute-start(f32[16,32,256]{2,1,0:T(8,128)S(1)} %get-tuple-element.113.refs_0_.before_ref), channel_id=1, source_target_pairs={{0,1},{1,0},{2,3},{3,2},{4,5},{5,4},{6,7},{7,6},{8,9},{9,8},{10,11... | collective-permute-start | bytes 1572872 | tf_op jit(solution)/shard_map/ppermute | solution.py:34
  116.6 4.1 %collective-permute-start.19 = (f32[15,32,256]{2,1,0:T(8,128)}, f32[15,32,256]{2,1,0:T(8,128)}, u32[]{:S(2)}, u32[]{:S(2)}) collective-permute-start(f32[15,32,256]{2,1,0:T(8,128)} %get-tuple-element.107), channel_id=1, source_target_pairs={{2,8},{3,9},{4,10},{5,11},{6,12},{7,13},{8,2},{9,3},{10,4},{11,5},... | collective-permute-start | bytes 1474568 | tf_op jit(solution)/shard_map/ppermute | solution.py:34
  120.7 5.0 %collective-permute-done.15.refs_1_ = f32[16,32,256]{2,1,0:T(8,128)} collective-permute-done((f32[16,32,256]{2,1,0:T(8,128)S(1)}, f32[16,32,256]{2,1,0:T(8,128)}, u32[]{:S(2)}, u32[]{:S(2)}) %collective-permute-start.15) | collective-permute-done | bytes 524320 | tf_op jit(solution)/shard_map/ppermute | solution.py:34
  128.2 2.8 %collective-permute-start.20 = (f32[15,32,256]{2,1,0:T(8,128)S(1)}, f32[15,32,256]{2,1,0:T(8,128)S(1)}, u32[]{:S(2)}, u32[]{:S(2)}) collective-permute-start(f32[15,32,256]{2,1,0:T(8,128)S(1)} %get-tuple-element.108), channel_id=1, source_target_pairs={{2,8},{3,9},{4,10},{5,11},{6,12},{7,13},{8,2},{9,3},{10,4},{11,5},... | collective-permute-start | bytes 1474568 | tf_op jit(solution)/shard_map/ppermute | solution.py:34
  131.0 2.8 %collective-permute-start.23 = (f32[15,32,256]{2,1,0:T(8,128)S(1)}, f32[15,32,256]{2,1,0:T(8,128)S(1)}, u32[]{:S(2)}, u32[]{:S(2)}) collective-permute-start(f32[15,32,256]{2,1,0:T(8,128)S(1)} %get-tuple-element.142), channel_id=1, source_target_pairs={{2,8},{3,9},{4,10},{5,11},{6,12},{7,13},{8,2},{9,3},{10,4},{11,5},... | collective-permute-start | bytes 1474568 | tf_op jit(solution)/shard_map/ppermute | solution.py:34
  136.5 2.1 %blur_x_far.6 = (f32[16,32,256]{2,1,0:T(8,128)S(1)}, f32[16,32,256]{2,1,0:T(8,128)S(1)}) custom-call(bf16[2,256,384]{2,1,0:T(8,128)(2,1)S(1)} %get-tuple-element.73.hi_ref, bf16[2,256,384]{2,1,0:T(8,128)(2,1)S(1)} %get-tuple-element.74.lo_ref, f32[15,32,256]{2,1,0:T(8,128)} %collective-permute-done.19.refs_0_, ...), custom_call_target="tpu_custom_call" | custom-call | tf_op jit(solution)/shard_map/blur_x_far/pallas_call | solution.py:329
  139.7 3.9 %collective-permute-done.23.refs_0_ = f32[15,32,256]{2,1,0:T(8,128)S(1)} collective-permute-done((f32[15,32,256]{2,1,0:T(8,128)S(1)}, f32[15,32,256]{2,1,0:T(8,128)S(1)}, u32[]{:S(2)}, u32[]{:S(2)}) %collective-permute-start.23) | collective-permute-done | bytes 491552 | tf_op jit(solution)/shard_map/ppermute | solution.py:34
  144.7 5.2 %ratio.2 = (f32[16,32,256]{2,1,0:T(8,128)S(1)}, f32[16,32,256]{2,1,0:T(8,128)S(1)}, f32[2,15,32,256]{3,2,1,0:T(8,128)S(1)}, f32[2,15,32,256]{3,2,1,0:T(8,128)S(1)}, f32[2,16,32,256]{3,2,1,0:T(8,128)S(1)}) custom-call(f32[16,80,256]{2,1,0:T(8,128)S(1)} %copy-done.1, f32[16,80,256]{2,1,0:T(8,128)S(1)} %copy-done.3, ...), custom_call_target="tpu_custom_call" | custom-call | tf_op jit(solution)/shard_map/ratio/pallas_call | solution.py:476
  149.9 2.8 %collective-permute-start.26 = (f32[2,15,32,256]{3,2,1,0:T(8,128)S(1)}, f32[2,15,32,256]{3,2,1,0:T(8,128)S(1)}, u32[]{:S(2)}, u32[]{:S(2)}) collective-permute-start(f32[2,15,32,256]{3,2,1,0:T(8,128)S(1)} %get-tuple-element.127), channel_id=1, source_target_pairs={{2,8},{3,9},{4,10},{5,11},{6,12},{7,13},{8,2},{9,3},{10,4},{11,5},... | collective-permute-start | bytes 2949128 | tf_op jit(solution)/shard_map/ppermute | solution.py:34
  153.9 4.2 %ratio.3 = (f32[16,32,256]{2,1,0:T(8,128)S(1)}, f32[16,32,256]{2,1,0:T(8,128)S(1)}, f32[2,15,32,256]{3,2,1,0:T(8,128)S(1)}, f32[2,15,32,256]{3,2,1,0:T(8,128)S(1)}) custom-call(f32[16,80,256]{2,1,0:T(8,128)S(1)} %copy-done.1, f32[16,80,256]{2,1,0:T(8,128)S(1)} %copy-done.3, f32[16,32,256]{2,1,0:T(8,128)S(1)} %get-tuple-element.120.refs_3_.refs_2_, ...), custom_call_target="tpu_custom_call" | custom-call | tf_op jit(solution)/shard_map/ratio/pallas_call | solution.py:476
  158.1 2.9 %collective-permute-start.32 = (f32[2,15,32,256]{3,2,1,0:T(8,128)S(1)}, f32[2,15,32,256]{3,2,1,0:T(8,128)S(1)}, u32[]{:S(2)}, u32[]{:S(2)}) collective-permute-start(f32[2,15,32,256]{3,2,1,0:T(8,128)S(1)} %get-tuple-element.137), channel_id=1, source_target_pairs={{2,8},{3,9},{4,10},{5,11},{6,12},{7,13},{8,2},{9,3},{10,4},{11,5},... | collective-permute-start | bytes 2949128 | tf_op jit(solution)/shard_map/ppermute | solution.py:34
  161.3 4.4 %collective-permute-done.26.refs_0_.refs_3_ = f32[2,15,32,256]{3,2,1,0:T(8,128)S(1)} collective-permute-done((f32[2,15,32,256]{3,2,1,0:T(8,128)S(1)}, f32[2,15,32,256]{3,2,1,0:T(8,128)S(1)}, u32[]{:S(2)}, u32[]{:S(2)}) %collective-permute-start.26) | collective-permute-done | bytes 983072 | tf_op jit(solution)/shard_map/ppermute | solution.py:34
  165.8 1.7 log_factor.8.refs_0_
  168.2 4.0 %collective-permute-start.29 = (f32[16,32,256]{2,1,0:T(8,128)S(1)}, f32[16,32,256]{2,1,0:T(8,128)S(1)}, u32[]{:S(2)}, u32[]{:S(2)}) collective-permute-start(f32[16,32,256]{2,1,0:T(8,128)S(1)} %log_factor.8.refs_0_), channel_id=1, source_target_pairs={{1,24},{3,26},{5,28},{7,30},{8,17},{10,19},{12,21},{14,23},{17,8},... | collective-permute-start | bytes 1572872 | tf_op jit(solution)/shard_map/ppermute | solution.py:34
  172.2 2.2 %collective-permute-start.30 = (f32[16,32,256]{2,1,0:T(8,128)S(1)}, f32[16,32,256]{2,1,0:T(8,128)S(1)}, u32[]{:S(2)}, u32[]{:S(2)}) collective-permute-start(f32[16,32,256]{2,1,0:T(8,128)S(1)} %log_factor.8.refs_0_), channel_id=1, source_target_pairs={{1,8},{3,10},{5,12},{7,14},{8,1},{10,3},{12,5},{14,7},{17,24},{19,... | collective-permute-start | bytes 1572872 | tf_op jit(solution)/shard_map/ppermute | solution.py:34
  174.4 1.9 collective-permute-done.32.refs_0_.refs_3_
  176.3 1.7 log_factor.9.refs_0_
  178.7 4.0 %collective-permute-start.35 = (f32[16,32,256]{2,1,0:T(8,128)S(1)}, f32[16,32,256]{2,1,0:T(8,128)S(1)}, u32[]{:S(2)}, u32[]{:S(2)}) collective-permute-start(f32[16,32,256]{2,1,0:T(8,128)S(1)} %log_factor.9.refs_0_), channel_id=1, source_target_pairs={{1,24},{3,26},{5,28},{7,30},{8,17},{10,19},{12,21},{14,23},{17,8},... | collective-permute-start | bytes 1572872 | tf_op jit(solution)/shard_map/ppermute | solution.py:34
  182.7 2.2 %collective-permute-start.36 = (f32[16,32,256]{2,1,0:T(8,128)S(1)}, f32[16,32,256]{2,1,0:T(8,128)S(1)}, u32[]{:S(2)}, u32[]{:S(2)}) collective-permute-start(f32[16,32,256]{2,1,0:T(8,128)S(1)} %log_factor.9.refs_0_), channel_id=1, source_target_pairs={{1,8},{3,10},{5,12},{7,14},{8,1},{10,3},{12,5},{14,7},{17,24},{19,... | collective-permute-start | bytes 1572872 | tf_op jit(solution)/shard_map/ppermute | solution.py:34
  185.2 3.4 %collective-permute-done.30.refs_3_ = f32[16,32,256]{2,1,0:T(8,128)S(1)} collective-permute-done((f32[16,32,256]{2,1,0:T(8,128)S(1)}, f32[16,32,256]{2,1,0:T(8,128)S(1)}, u32[]{:S(2)}, u32[]{:S(2)}) %collective-permute-start.30) | collective-permute-done | bytes 524320 | tf_op jit(solution)/shard_map/ppermute | solution.py:34
  188.8 7.5 %collective-permute-done.35.refs_2_ = f32[16,32,256]{2,1,0:T(8,128)S(1)} collective-permute-done((f32[16,32,256]{2,1,0:T(8,128)S(1)}, f32[16,32,256]{2,1,0:T(8,128)S(1)}, u32[]{:S(2)}, u32[]{:S(2)}) %collective-permute-start.35) | collective-permute-done | bytes 524320 | tf_op jit(solution)/shard_map/ppermute | solution.py:34
  196.3 1.7 collective-permute-done.36.refs_3_
  198.2 1.9 collective-permute-done.37.refs_3_
  (101 shorter events, 30.4 us)
Async XLA Ops:
  0.0 7.5 %copy-start.4 = (f32[1,16,128,256]{3,2,1,0:T(8,128)S(1)}, f32[1,16,128,256]{3,2,1,0:T(8,128)}, u32[]{:S(2)}) copy-start(f32[1,16,128,256]{3,2,1,0:T(8,128)} %param.7) | copy-start | bytes 6291460
  1.7 5.8 %copy-start.16 = (s32[1,16,128]{2,1,0:T(8,128)S(1)}, s32[1,16,128]{2,1,0:T(8,128)}, u32[]{:S(2)}) copy-start(s32[1,16,128]{2,1,0:T(8,128)} %param.10) | copy-start | bytes 24580
  1.7 5.8 %copy-start.17 = (s32[1,3]{1,0:T(1,128)S(1)}, s32[1,3]{1,0:T(1,128)}, u32[]{:S(2)}) copy-start(s32[1,3]{1,0:T(1,128)} %offsets_ref.1) | copy-start | bytes 40
  2.0 23.8 %collective-permute-start.1 = (f32[16,96,256]{2,1,0:T(8,128)S(1)}, f32[16,96,256]{2,1,0:T(8,128)S(1)}, u32[]{:S(2)}, u32[]{:S(2)}) collective-permute-start(f32[16,96,256]{2,1,0:T(8,128)S(1)} %get-tuple-element.79), channel_id=1, source_target_pairs={{0,1},{2,3},{4,5},{6,7},{9,8},{11,10},{13,12},{15,14},{16,17},{18,... | collective-permute-start | bytes 4718600 | tf_op jit(solution)/shard_map/ppermute | solution.py:34
  4.0 8.1 %collective-permute-start = (f32[1,384]{1,0:T(1,128)S(1)}, f32[1,384]{1,0:T(1,128)S(1)}, u32[]{:S(2)}, u32[]{:S(2)}) collective-permute-start(f32[1,384]{1,0:T(1,128)S(1)} %fusion.1.mine_ref), channel_id=1, source_target_pairs={{0,8},{1,9},{2,10},{3,11},{4,12},{5,13},{6,14},{7,15},{8,0},{9,1},... | collective-permute-start | bytes 4616 | tf_op jit(solution)/shard_map/ppermute | solution.py:34
  14.1 13.1 %copy-start.6 = (bf16[2,64,256]{2,1,0:T(8,128)(2,1)}, bf16[2,64,256]{2,1,0:T(8,128)(2,1)S(1)}, u32[]{:S(2)}) copy-start(bf16[2,64,256]{2,1,0:T(8,128)(2,1)S(1)} %get-tuple-element.91.ya_ref) | copy-start | bytes 196612
  14.1 13.1 %copy-start.8 = (bf16[2,48,256]{2,1,0:T(8,128)(2,1)}, bf16[2,48,256]{2,1,0:T(8,128)(2,1)S(1)}, u32[]{:S(2)}) copy-start(bf16[2,48,256]{2,1,0:T(8,128)(2,1)S(1)} %get-tuple-element.125.refs_6_) | copy-start | bytes 147460
  14.1 13.1 %copy-start.10 = (bf16[2,32,256]{2,1,0:T(8,128)(2,1)}, bf16[2,32,256]{2,1,0:T(8,128)(2,1)S(1)}, u32[]{:S(2)}) copy-start(bf16[2,32,256]{2,1,0:T(8,128)(2,1)S(1)} %get-tuple-element.135.refs_7_) | copy-start | bytes 98308
  14.1 13.1 %copy-start.12 = (bf16[2,32,256]{2,1,0:T(8,128)(2,1)}, bf16[2,32,256]{2,1,0:T(8,128)(2,1)S(1)}, u32[]{:S(2)}) copy-start(bf16[2,32,256]{2,1,0:T(8,128)(2,1)S(1)} %get-tuple-element.136.refs_8_) | copy-start | bytes 98308
  14.2 13.1 %copy-start.14 = (bf16[2,32,256]{2,1,0:T(8,128)(2,1)}, bf16[2,32,256]{2,1,0:T(8,128)(2,1)S(1)}, u32[]{:S(2)}) copy-start(bf16[2,32,256]{2,1,0:T(8,128)(2,1)S(1)} %get-tuple-element.126.refs_7_) | copy-start | bytes 98308
  14.2 1.2 collective-permute-start.2
  15.3 24.2 %collective-permute-start.3 = (f32[17,80,256]{2,1,0:T(8,128)}, f32[17,80,256]{2,1,0:T(8,128)}, u32[]{:S(2)}, u32[]{:S(2)}) collective-permute-start(f32[17,80,256]{2,1,0:T(8,128)} %get-tuple-element.83), channel_id=1, source_target_pairs={{1,8},{3,10},{5,12},{7,14},{8,1},{10,3},{12,5},{14,7},{17,24},{19,... | collective-permute-start | bytes 4177928 | tf_op jit(solution)/shard_map/ppermute | solution.py:34
  28.4 28.6 %collective-permute-start.7 = (f32[15,96,256]{2,1,0:T(8,128)}, f32[15,96,256]{2,1,0:T(8,128)}, u32[]{:S(2)}, u32[]{:S(2)}) collective-permute-start(f32[15,96,256]{2,1,0:T(8,128)} %get-tuple-element.85), channel_id=1, source_target_pairs={{2,8},{3,9},{4,10},{5,11},{6,12},{7,13},{8,2},{9,3},{10,4},{11,5},... | collective-permute-start | bytes 4423688 | tf_op jit(solution)/shard_map/ppermute | solution.py:34
  35.3 18.6 %collective-permute-start.10 = (f32[17,80,256]{2,1,0:T(8,128)}, f32[17,80,256]{2,1,0:T(8,128)}, u32[]{:S(2)}, u32[]{:S(2)}) collective-permute-start(f32[17,80,256]{2,1,0:T(8,128)} %get-tuple-element.96), channel_id=1, source_target_pairs={{0,1},{1,9},{2,3},{3,11},{4,5},{5,13},{6,7},{7,15},{8,0},{9,8},{10... | collective-permute-start | bytes 4177928 | tf_op jit(solution)/shard_map/ppermute | solution.py:34
  35.3 26.3 %collective-permute-start.6 = (f32[15,96,256]{2,1,0:T(8,128)}, f32[15,96,256]{2,1,0:T(8,128)S(1)}, u32[]{:S(2)}, u32[]{:S(2)}) collective-permute-start(f32[15,96,256]{2,1,0:T(8,128)} %copy-done.18), channel_id=1, source_target_pairs={{0,8},{1,9},{2,10},{3,11},{4,12},{5,13},{6,14},{7,15},{8,0},{9,1},... | collective-permute-start | bytes 4423688 | tf_op jit(solution)/shard_map/ppermute | solution.py:34
  41.1 26.6 %collective-permute-start.4 = (f32[17,80,256]{2,1,0:T(8,128)S(1)}, f32[17,80,256]{2,1,0:T(8,128)S(1)}, u32[]{:S(2)}, u32[]{:S(2)}) collective-permute-start(f32[17,80,256]{2,1,0:T(8,128)S(1)} %broadcast_select_fusion.own_ref), channel_id=1, source_target_pairs={{2,8},{3,9},{4,10},{5,11},{6,12},{7,13},{8,2},{9,3},{10,4},{11,5},... | collective-permute-start | bytes 4177928 | tf_op jit(solution)/shard_map/ppermute | solution.py:34
  43.0 24.7 %collective-permute-start.5 = (f32[17,80,256]{2,1,0:T(8,128)S(1)}, f32[17,80,256]{2,1,0:T(8,128)S(1)}, u32[]{:S(2)}, u32[]{:S(2)}) collective-permute-start(f32[17,80,256]{2,1,0:T(8,128)S(1)} %broadcast_select_fusion.own_ref), channel_id=1, source_target_pairs={{0,8},{1,9},{2,10},{3,11},{4,12},{5,13},{6,14},{7,15},{8,0},{9,1},... | collective-permute-start | bytes 4177928 | tf_op jit(solution)/shard_map/ppermute | solution.py:34
  53.9 28.8 %collective-permute-start.11 = (f32[17,80,256]{2,1,0:T(8,128)}, f32[17,80,256]{2,1,0:T(8,128)S(1)}, u32[]{:S(2)}, u32[]{:S(2)}) collective-permute-start(f32[17,80,256]{2,1,0:T(8,128)} %collective-permute-done.10.own_ref), channel_id=1, source_target_pairs={{2,8},{3,9},{4,10},{5,11},{6,12},{7,13},{8,2},{9,3},{10,4},{11,5},... | collective-permute-start | bytes 4177928 | tf_op jit(solution)/shard_map/ppermute | solution.py:34
  57.0 25.6 %collective-permute-start.12 = (f32[17,80,256]{2,1,0:T(8,128)}, f32[17,80,256]{2,1,0:T(8,128)S(1)}, u32[]{:S(2)}, u32[]{:S(2)}) collective-permute-start(f32[17,80,256]{2,1,0:T(8,128)} %collective-permute-done.10.own_ref), channel_id=1, source_target_pairs={{0,8},{1,9},{2,10},{3,11},{4,12},{5,13},{6,14},{7,15},{8,0},{9,1},... | collective-permute-start | bytes 4177928 | tf_op jit(solution)/shard_map/ppermute | solution.py:34
  70.4 22.8 %collective-permute-start.8 = (f32[15,64,256]{2,1,0:T(8,128)S(1)}, f32[15,64,256]{2,1,0:T(8,128)S(1)}, u32[]{:S(2)}, u32[]{:S(2)}) collective-permute-start(f32[15,64,256]{2,1,0:T(8,128)S(1)} %get-tuple-element.92), channel_id=1, source_target_pairs={{2,8},{3,9},{4,10},{5,11},{6,12},{7,13},{8,2},{9,3},{10,4},{11,5},... | collective-permute-start | bytes 2949128 | tf_op jit(solution)/shard_map/ppermute | solution.py:34
  73.8 19.4 %collective-permute-start.9 = (f32[15,64,256]{2,1,0:T(8,128)S(1)}, f32[15,64,256]{2,1,0:T(8,128)S(1)}, u32[]{:S(2)}, u32[]{:S(2)}) collective-permute-start(f32[15,64,256]{2,1,0:T(8,128)S(1)} %get-tuple-element.93), channel_id=1, source_target_pairs={{0,8},{1,9},{2,10},{3,11},{4,12},{5,13},{6,14},{7,15},{8,0},{9,1},... | collective-permute-start | bytes 2949128 | tf_op jit(solution)/shard_map/ppermute | solution.py:34
  87.4 10.9 %collective-permute-start.16 = (f32[15,32,256]{2,1,0:T(8,128)S(1)}, f32[15,32,256]{2,1,0:T(8,128)S(1)}, u32[]{:S(2)}, u32[]{:S(2)}) collective-permute-start(f32[15,32,256]{2,1,0:T(8,128)S(1)} %get-tuple-element.105), channel_id=1, source_target_pairs={{2,8},{3,9},{4,10},{5,11},{6,12},{7,13},{8,2},{9,3},{10,4},{11,5},... | collective-permute-start | bytes 1474568 | tf_op jit(solution)/shard_map/ppermute | solution.py:34
  90.8 7.5 %collective-permute-start.17 = (f32[15,32,256]{2,1,0:T(8,128)S(1)}, f32[15,32,256]{2,1,0:T(8,128)S(1)}, u32[]{:S(2)}, u32[]{:S(2)}) collective-permute-start(f32[15,32,256]{2,1,0:T(8,128)S(1)} %get-tuple-element.106), channel_id=1, source_target_pairs={{0,8},{1,9},{2,10},{3,11},{4,12},{5,13},{6,14},{7,15},{8,0},{9,1},... | collective-permute-start | bytes 1474568 | tf_op jit(solution)/shard_map/ppermute | solution.py:34
  99.4 13.2 %collective-permute-start.18 = (f32[16,32,256]{2,1,0:T(8,128)S(1)}, f32[16,32,256]{2,1,0:T(8,128)S(1)}, u32[]{:S(2)}, u32[]{:S(2)}) collective-permute-start(f32[16,32,256]{2,1,0:T(8,128)S(1)} %log_factor.7.refs_0_), channel_id=1, source_target_pairs={{0,16},{1,17},{2,18},{3,19},{4,20},{5,21},{6,22},{7,23},{8,24},{9,... | collective-permute-start | bytes 1572872 | tf_op jit(solution)/shard_map/ppermute | solution.py:34
  100.7 10.6 %collective-permute-start.13 = (f32[15,32,256]{2,1,0:T(8,128)S(1)}, f32[15,32,256]{2,1,0:T(8,128)S(1)}, u32[]{:S(2)}, u32[]{:S(2)}) collective-permute-start(f32[15,32,256]{2,1,0:T(8,128)S(1)} %get-tuple-element.98), channel_id=1, source_target_pairs={{2,8},{3,9},{4,10},{5,11},{6,12},{7,13},{8,2},{9,3},{10,4},{11,5},... | collective-permute-start | bytes 1474568 | tf_op jit(solution)/shard_map/ppermute | solution.py:34
  104.4 6.8 %collective-permute-start.14 = (f32[15,32,256]{2,1,0:T(8,128)S(1)}, f32[15,32,256]{2,1,0:T(8,128)S(1)}, u32[]{:S(2)}, u32[]{:S(2)}) collective-permute-start(f32[15,32,256]{2,1,0:T(8,128)S(1)} %get-tuple-element.99), channel_id=1, source_target_pairs={{0,8},{1,9},{2,10},{3,11},{4,12},{5,13},{6,14},{7,15},{8,0},{9,1},... | collective-permute-start | bytes 1474568 | tf_op jit(solution)/shard_map/ppermute | solution.py:34
  112.3 13.4 %collective-permute-start.15 = (f32[16,32,256]{2,1,0:T(8,128)S(1)}, f32[16,32,256]{2,1,0:T(8,128)}, u32[]{:S(2)}, u32[]{:S(2)}) collective-permute-start(f32[16,32,256]{2,1,0:T(8,128)S(1)} %log_factor.6.refs_0_), channel_id=1, source_target_pairs={{0,16},{1,17},{2,18},{3,19},{4,20},{5,21},{6,22},{7,23},{8,24},{9,... | collective-permute-start | bytes 1572872 | tf_op jit(solution)/shard_map/ppermute | solution.py:34
  114.4 16.6 %collective-permute-start.22 = (f32[16,32,256]{2,1,0:T(8,128)S(1)}, f32[16,32,256]{2,1,0:T(8,128)S(1)}, u32[]{:S(2)}, u32[]{:S(2)}) collective-permute-start(f32[16,32,256]{2,1,0:T(8,128)S(1)} %get-tuple-element.113.refs_0_.before_ref), channel_id=1, source_target_pairs={{0,1},{1,0},{2,3},{3,2},{4,5},{5,4},{6,7},{7,6},{8,9},{9,8},{10,11... | collective-permute-start | bytes 1572872 | tf_op jit(solution)/shard_map/ppermute | solution.py:34
  116.6 11.6 %collective-permute-start.19 = (f32[15,32,256]{2,1,0:T(8,128)}, f32[15,32,256]{2,1,0:T(8,128)}, u32[]{:S(2)}, u32[]{:S(2)}) collective-permute-start(f32[15,32,256]{2,1,0:T(8,128)} %get-tuple-element.107), channel_id=1, source_target_pairs={{2,8},{3,9},{4,10},{5,11},{6,12},{7,13},{8,2},{9,3},{10,4},{11,5},... | collective-permute-start | bytes 1474568 | tf_op jit(solution)/shard_map/ppermute | solution.py:34
  126.9 8.5 %collective-permute-start.21 = (f32[15,32,256]{2,1,0:T(8,128)S(1)}, f32[15,32,256]{2,1,0:T(8,128)S(1)}, u32[]{:S(2)}, u32[]{:S(2)}) collective-permute-start(f32[15,32,256]{2,1,0:T(8,128)S(1)} %get-tuple-element.109), channel_id=1, source_target_pairs={{0,8},{1,9},{2,10},{3,11},{4,12},{5,13},{6,14},{7,15},{8,0},{9,1},... | collective-permute-start | bytes 1474568 | tf_op jit(solution)/shard_map/ppermute | solution.py:34
  128.1 6.2 %collective-permute-start.25 = (f32[15,32,256]{2,1,0:T(8,128)}, f32[15,32,256]{2,1,0:T(8,128)S(1)}, u32[]{:S(2)}, u32[]{:S(2)}) collective-permute-start(f32[15,32,256]{2,1,0:T(8,128)} %copy-done.19), channel_id=1, source_target_pairs={{0,8},{1,9},{2,10},{3,11},{4,12},{5,13},{6,14},{7,15},{8,0},{9,1},... | collective-permute-start | bytes 1474568 | tf_op jit(solution)/shard_map/ppermute | solution.py:34
  128.2 10.4 %collective-permute-start.20 = (f32[15,32,256]{2,1,0:T(8,128)S(1)}, f32[15,32,256]{2,1,0:T(8,128)S(1)}, u32[]{:S(2)}, u32[]{:S(2)}) collective-permute-start(f32[15,32,256]{2,1,0:T(8,128)S(1)} %get-tuple-element.108), channel_id=1, source_target_pairs={{2,8},{3,9},{4,10},{5,11},{6,12},{7,13},{8,2},{9,3},{10,4},{11,5},... | collective-permute-start | bytes 1474568 | tf_op jit(solution)/shard_map/ppermute | solution.py:34
  131.0 12.6 %collective-permute-start.23 = (f32[15,32,256]{2,1,0:T(8,128)S(1)}, f32[15,32,256]{2,1,0:T(8,128)S(1)}, u32[]{:S(2)}, u32[]{:S(2)}) collective-permute-start(f32[15,32,256]{2,1,0:T(8,128)S(1)} %get-tuple-element.142), channel_id=1, source_target_pairs={{2,8},{3,9},{4,10},{5,11},{6,12},{7,13},{8,2},{9,3},{10,4},{11,5},... | collective-permute-start | bytes 1474568 | tf_op jit(solution)/shard_map/ppermute | solution.py:34
  133.8 9.8 %collective-permute-start.24 = (f32[15,32,256]{2,1,0:T(8,128)S(1)}, f32[15,32,256]{2,1,0:T(8,128)S(1)}, u32[]{:S(2)}, u32[]{:S(2)}) collective-permute-start(f32[15,32,256]{2,1,0:T(8,128)S(1)} %get-tuple-element.141), channel_id=1, source_target_pairs={{0,8},{1,9},{2,10},{3,11},{4,12},{5,13},{6,14},{7,15},{8,0},{9,1},... | collective-permute-start | bytes 1474568 | tf_op jit(solution)/shard_map/ppermute | solution.py:34
  138.6 6.1 %copy-start.3 = (f32[16,80,256]{2,1,0:T(8,128)S(1)}, f32[16,80,256]{2,1,0:T(8,128)}, u32[]{:S(2)}) copy-start(f32[16,80,256]{2,1,0:T(8,128)} %copy-done.2) | copy-start | bytes 3932164
  139.7 5.1 %copy-start.1 = (f32[16,80,256]{2,1,0:T(8,128)S(1)}, f32[16,80,256]{2,1,0:T(8,128)}, u32[]{:S(2)}) copy-start(f32[16,80,256]{2,1,0:T(8,128)} %copy-done) | copy-start | bytes 3932164
  149.9 15.8 %collective-permute-start.26 = (f32[2,15,32,256]{3,2,1,0:T(8,128)S(1)}, f32[2,15,32,256]{3,2,1,0:T(8,128)S(1)}, u32[]{:S(2)}, u32[]{:S(2)}) collective-permute-start(f32[2,15,32,256]{3,2,1,0:T(8,128)S(1)} %get-tuple-element.127), channel_id=1, source_target_pairs={{2,8},{3,9},{4,10},{5,11},{6,12},{7,13},{8,2},{9,3},{10,4},{11,5},... | collective-permute-start | bytes 2949128 | tf_op jit(solution)/shard_map/ppermute | solution.py:34
  152.7 13.0 %collective-permute-start.27 = (f32[2,15,32,256]{3,2,1,0:T(8,128)S(1)}, f32[2,15,32,256]{3,2,1,0:T(8,128)S(1)}, u32[]{:S(2)}, u32[]{:S(2)}) collective-permute-start(f32[2,15,32,256]{3,2,1,0:T(8,128)S(1)} %get-tuple-element.128), channel_id=1, source_target_pairs={{0,8},{1,9},{2,10},{3,11},{4,12},{5,13},{6,14},{7,15},{8,0},{9,1},... | collective-permute-start | bytes 2949128 | tf_op jit(solution)/shard_map/ppermute | solution.py:34
  158.1 18.2 %collective-permute-start.32 = (f32[2,15,32,256]{3,2,1,0:T(8,128)S(1)}, f32[2,15,32,256]{3,2,1,0:T(8,128)S(1)}, u32[]{:S(2)}, u32[]{:S(2)}) collective-permute-start(f32[2,15,32,256]{3,2,1,0:T(8,128)S(1)} %get-tuple-element.137), channel_id=1, source_target_pairs={{2,8},{3,9},{4,10},{5,11},{6,12},{7,13},{8,2},{9,3},{10,4},{11,5},... | collective-permute-start | bytes 2949128 | tf_op jit(solution)/shard_map/ppermute | solution.py:34
  161.0 15.3 %collective-permute-start.33 = (f32[2,15,32,256]{3,2,1,0:T(8,128)S(1)}, f32[2,15,32,256]{3,2,1,0:T(8,128)S(1)}, u32[]{:S(2)}, u32[]{:S(2)}) collective-permute-start(f32[2,15,32,256]{3,2,1,0:T(8,128)S(1)} %get-tuple-element.138), channel_id=1, source_target_pairs={{0,8},{1,9},{2,10},{3,11},{4,12},{5,13},{6,14},{7,15},{8,0},{9,1},... | collective-permute-start | bytes 2949128 | tf_op jit(solution)/shard_map/ppermute | solution.py:34
  167.5 15.2 %collective-permute-start.28 = (f32[16,32,256]{2,1,0:T(8,128)S(1)}, f32[16,32,256]{2,1,0:T(8,128)S(1)}, u32[]{:S(2)}, u32[]{:S(2)}) collective-permute-start(f32[16,32,256]{2,1,0:T(8,128)S(1)} %log_factor.8.refs_0_), channel_id=1, source_target_pairs={{0,16},{2,18},{4,20},{6,22},{9,25},{11,27},{13,29},{15,31},{16,0},... | collective-permute-start | bytes 1572872 | tf_op jit(solution)/shard_map/ppermute | solution.py:34
  168.2 17.0 %collective-permute-start.29 = (f32[16,32,256]{2,1,0:T(8,128)S(1)}, f32[16,32,256]{2,1,0:T(8,128)S(1)}, u32[]{:S(2)}, u32[]{:S(2)}) collective-permute-start(f32[16,32,256]{2,1,0:T(8,128)S(1)} %log_factor.8.refs_0_), channel_id=1, source_target_pairs={{1,24},{3,26},{5,28},{7,30},{8,17},{10,19},{12,21},{14,23},{17,8},... | collective-permute-start | bytes 1572872 | tf_op jit(solution)/shard_map/ppermute | solution.py:34
  172.2 16.4 %collective-permute-start.30 = (f32[16,32,256]{2,1,0:T(8,128)S(1)}, f32[16,32,256]{2,1,0:T(8,128)S(1)}, u32[]{:S(2)}, u32[]{:S(2)}) collective-permute-start(f32[16,32,256]{2,1,0:T(8,128)S(1)} %log_factor.8.refs_0_), channel_id=1, source_target_pairs={{1,8},{3,10},{5,12},{7,14},{8,1},{10,3},{12,5},{14,7},{17,24},{19,... | collective-permute-start | bytes 1572872 | tf_op jit(solution)/shard_map/ppermute | solution.py:34
  178.0 10.7 %collective-permute-start.34 = (f32[16,32,256]{2,1,0:T(8,128)S(1)}, f32[16,32,256]{2,1,0:T(8,128)S(1)}, u32[]{:S(2)}, u32[]{:S(2)}) collective-permute-start(f32[16,32,256]{2,1,0:T(8,128)S(1)} %log_factor.9.refs_0_), channel_id=1, source_target_pairs={{0,16},{2,18},{4,20},{6,22},{9,25},{11,27},{13,29},{15,31},{16,0},... | collective-permute-start | bytes 1572872 | tf_op jit(solution)/shard_map/ppermute | solution.py:34
  178.7 17.6 %collective-permute-start.35 = (f32[16,32,256]{2,1,0:T(8,128)S(1)}, f32[16,32,256]{2,1,0:T(8,128)S(1)}, u32[]{:S(2)}, u32[]{:S(2)}) collective-permute-start(f32[16,32,256]{2,1,0:T(8,128)S(1)} %log_factor.9.refs_0_), channel_id=1, source_target_pairs={{1,24},{3,26},{5,28},{7,30},{8,17},{10,19},{12,21},{14,23},{17,8},... | collective-permute-start | bytes 1572872 | tf_op jit(solution)/shard_map/ppermute | solution.py:34
  182.7 15.3 %collective-permute-start.36 = (f32[16,32,256]{2,1,0:T(8,128)S(1)}, f32[16,32,256]{2,1,0:T(8,128)S(1)}, u32[]{:S(2)}, u32[]{:S(2)}) collective-permute-start(f32[16,32,256]{2,1,0:T(8,128)S(1)} %log_factor.9.refs_0_), channel_id=1, source_target_pairs={{1,8},{3,10},{5,12},{7,14},{8,1},{10,3},{12,5},{14,7},{17,24},{19,... | collective-permute-start | bytes 1572872 | tf_op jit(solution)/shard_map/ppermute | solution.py:34
  188.7 9.5 %collective-permute-start.31 = (f32[16,32,256]{2,1,0:T(8,128)S(1)}, f32[16,32,256]{2,1,0:T(8,128)S(1)}, u32[]{:S(2)}, u32[]{:S(2)}) collective-permute-start(f32[16,32,256]{2,1,0:T(8,128)S(1)} %last_update.2.refs_0_), channel_id=1, source_target_pairs={{0,8},{1,9},{2,10},{3,11},{4,12},{5,13},{6,14},{7,15},{8,0},{9,1},... | collective-permute-start | bytes 1572872 | tf_op jit(solution)/shard_map/ppermute | solution.py:34
  198.1 2.0 collective-permute-start.37
  (10 other events, 30.6 us)

commit v12 on v11

--- a/solution.py
+++ b/solution.py
@@ -248,7 +248,7 @@
     return call(choose_kernel, out_shape, [VMEM] * 2, "estimate")(window, crossed)
 
 
-def shift_kernel(offsets_ref, acq_ref, mask_ref, first_ref, second_ref, turned_ref):
+def shift_kernel(offsets_ref, acq_ref, first_ref, second_ref, turned_ref):
     planes, cells_y, cells_z = acq_ref.shape
     near = first_ref.shape[1]
     shift_y, shift_z = offsets_ref[0, 1], offsets_ref[0, 2]
@@ -268,17 +268,13 @@
         return carry
 
     lax.fori_loop(0, planes, body, 0)
-    mask = mask_ref[...].astype(F32)
-    for out_ref in (first_ref, second_ref):
-        out_ref[planes] = jnp.zeros((near, cells_z), F32)
-        out_ref[planes, :planes, :cells_y] = mask
-
-
-def shift_and_cut(offsets, acquired, mask, near):
+
+
+def shift_and_cut(offsets, acquired, near):
     planes, cells_y, cells_z = acquired.shape
-    shape = jax.ShapeDtypeStruct((planes + 1, near, cells_z), F32)
+    shape = jax.ShapeDtypeStruct((planes, near, cells_z), F32)
     scratch = [pltpu.VMEM((cells_y, cells_z), F32)]
-    return call(shift_kernel, (shape, shape), [SMEM, VMEM, VMEM], "shift_recorded", scratch)(offsets, acquired, mask)
+    return call(shift_kernel, (shape, shape), [SMEM, VMEM], "shift_recorded", scratch)(offsets, acquired)
 
 
 def gather(ref, row):
@@ -339,11 +335,7 @@
 
 def spread_y(band, x):
     high, low = split(x)
-    parts = [high, low, high]
-    rest = band.shape[1] - 3 * x.shape[0]
-    if rest:
-        parts.append(jnp.zeros((rest, x.shape[1]), BF16))
-    return dot(band, jnp.concatenate(parts, axis=0))
+    return dot(band[:, :3 * x.shape[0]], jnp.concatenate([high, low, high], axis=0))
 
 
 def spread_z(x, hi_ref, lo_ref, index):
@@ -395,25 +387,25 @@
 
 
 def first_ratio_kernel(
-    shift_ref, far_ref, near_ref, own_ref, blurred_ref, ya_ref, zhi_ref, zlo_ref, out_ref, *refs, order, extent_x, cells_y
+    shift_ref, far_ref, near_ref, own_ref, masks_ref, blurred_ref, ya_ref, zhi_ref, zlo_ref, out_ref, *refs, order, extent_x, cells_y
 ):
     edge_refs, image_ref, (mine_ref, beyond_ref, semaphores) = refs[:-4], refs[-4], refs[-3:]
     planes, near, cells_z = image_ref.shape
     side = half()
     slab = lax.axis_index("tile") - side + core()
     shift_x, shift_y, shift_z = (shift_ref[order, i] for i in range(3))
-    lanes = pad_to(cells_y, 128)
+    lanes = masks_ref.shape[2]
     pick = iota((near, lanes), 1) == global_row(side, iota((near, lanes), 0), cells_y)
     is_far = (shift_x > 0) == (core() == 1)
     copy = pltpu.make_async_copy(own_ref, mine_ref, semaphores.at[0])
-    far_copy = pltpu.make_async_copy(far_ref.at[pl.ds(0, planes)], beyond_ref, semaphores.at[1])
-    near_copy = pltpu.make_async_copy(near_ref.at[pl.ds(0, planes)], beyond_ref, semaphores.at[1])
+    far_copy = pltpu.make_async_copy(far_ref, beyond_ref, semaphores.at[1])
+    near_copy = pltpu.make_async_copy(near_ref, beyond_ref, semaphores.at[1])
     copy.start()
     pl.when(is_far)(far_copy.start)
     pl.when(jnp.logical_not(is_far))(near_copy.start)
     copy.wait()
     far_copy.wait()
-    mask = mine_ref[planes, :planes, :lanes].astype(BF16)
+    mask = masks_ref[half() if order == 0 else 1 - half()].astype(BF16)
     columns = lax.dot_general(
         pick.astype(F32).astype(BF16), mask, (((1,), (1,)), ((), ())), preferred_element_type=F32
     )
@@ -476,17 +468,17 @@
     return call(kernel, out_shape, [VMEM] * len(operands), "ratio")(*operands)
 
 
-def first_ratio(shifts, blocks, blurred, tables, order, radius, chunks, extent_x, cells_y):
+def first_ratio(shifts, blocks, masks, blurred, tables, order, radius, chunks, extent_x, cells_y):
     planes, near, lanes = blurred.shape
     kernel = functools.partial(first_ratio_kernel, order=order, extent_x=extent_x, cells_y=cells_y)
     rows = tables.whole[1].shape[1]
     out_shape = edge_shapes((planes, rows, lanes), radius, chunks) + (jax.ShapeDtypeStruct(blurred.shape, F32),)
     scratch = [
-        pltpu.VMEM((planes + 1, near, lanes), F32), pltpu.VMEM(blurred.shape, F32), pltpu.SemaphoreType.DMA((2,))
+        pltpu.VMEM(blurred.shape, F32), pltpu.VMEM(blurred.shape, F32), pltpu.SemaphoreType.DMA((2,))
     ]
-    in_specs = [SMEM] + [pl.BlockSpec(memory_space=pl.ANY)] * 3 + [VMEM] * 4
+    in_specs = [SMEM] + [pl.BlockSpec(memory_space=pl.ANY)] * 3 + [VMEM] * 5
     return call(kernel, out_shape, in_specs, "image_and_ratio", scratch)(
-        shifts, *blocks, blurred, tables.whole[1], *tables.z
+        shifts, *blocks, masks, blurred, tables.whole[1], *tables.z
     )
 
 
@@ -610,18 +602,24 @@
     crossed = send(crossed, across(0, lambda r: 1 - r, when=lambda c, r: c == r))
 
     acquired = after(acquired, window)
-    first, second = shift_and_cut(offsets, acquired[0], view_mask[0], near)
+    first, second = shift_and_cut(offsets, acquired[0], near)
 
     mine = [jnp.pad(row, ((0, 0), (0, 128 - row.shape[1]))) for row in (kern_x, kern_y, kern_z)]
     mine = jnp.concatenate(mine, axis=1)
     other = send(mine, to_core_partner)
     taps = kern_x.shape[1], taps_y, kern_z.shape[1]
     tables = make_tables(mine, other, taps, planes, cells_y, cells_z, (own_rows, near, wide))
-    mine = after(offsets.astype(F32), tables.whole[0])
-    other = send(mine, to_core_partner)
-    shifts = jnp.where(straight, jnp.concatenate([mine, other]), jnp.concatenate([other, mine])).astype(jnp.int32)
-
-    arrived = send(after(first, other), lambda g, c, q, r: (g, r, q, c) if c != r else None)
+    offset = offsets.astype(F32)
+    other = send(offset, to_core_partner)
+    shifts = jnp.where(straight, jnp.concatenate([offset, other]), jnp.concatenate([other, offset])).astype(jnp.int32)
+
+    mask = view_mask.astype(F32)
+    other = send(mask, to_core_partner)
+    masks = jnp.where(core() == 0, jnp.concatenate([mask, other]), jnp.concatenate([other, mask]))
+    beyond = send(after(masks, tables.whole[0]), to_row_partner)
+    masks = jnp.where(straight, masks, beyond)
+
+    arrived = send(after(first, masks), lambda g, c, q, r: (g, r, q, c) if c != r else None)
     current, distant, close = choose(after(window, first), crossed, radius)
     second = send(after(second, current), lambda g, c, q, r: (g, r, q, 1 - c))
     distant, close = neighbours(distant, close)
@@ -635,7 +633,7 @@
     images, sides = [], []
     for order, chunk_sizes in enumerate(([own_rows], [edge_rows, inner_rows])):
         spread, *edges, image = first_ratio(
-            shifts, blocks[order], blurred[order], tables, order, radius, chunk_sizes, planes * slabs, cells_y
+            shifts, blocks[order], masks, blurred[order], tables, order, radius, chunk_sizes, planes * slabs, cells_y
         )
         images.append(image)
         sides.append([(*neighbours(*edges[k:k + 2]), spread) for k in range(0, len(edges), 2)])

time: 202 us -> 210 us (1.040)
  waiting for transfers between devices: 73.3 us -> 81.2 us
  starting transfers between devices: 66 us -> 59.9 us
  local copies, waits for them, and re-layouts: 4.9 us -> 9.33 us
    ppermute x38 -> x40, waiting for transfers between devices: 73.3 us -> 81.2 us  [send(): return lax.ppermute(array, AXES, moves(move))]
    ppermute x38 -> x40, starting transfers between devices: 66 us -> 59.9 us  [send(): return lax.ppermute(array, AXES, moves(move))]
    unnamed x40, local copies, waits for them, and re-layouts: 4.82 us -> 8.08 us
    select_n x0 -> x2, other arithmetic: none -> 2.15 us  [the longest x1 1.37 us: shards(): jnp.where(core() == 0, jnp.concatenate([mask, other]), jnp.concatenate([o...]
  transfers between devices with their start and end apart: 38 -> 40, of which waited for: 18 -> 17; matrix products, arithmetic and copies ran while one was open for 1% -> 2% of each run, Pallas kernels for 22% -> 21%
where the time goes in v12:
time: 210 us; the launch traced here: 209 us
  waiting for transfers between devices  81.2 us (39%)
  starting transfers between devices  59.9 us (29%)
  Pallas kernels  55.1 us (26%)
  local copies, waits for them, and re-layouts  9.33 us (4%)
  other arithmetic  2.34 us (1%)
    ppermute x40, waiting for transfers between devices, send(): return lax.ppermute(array, AXES, moves(move))  81.2 us
    ppermute x40, starting transfers between devices, send(): return lax.ppermute(array, AXES, moves(move))  59.9 us
    pallas_call x8, Pallas kernels, blur_x(): call(kernel, (shape, shape), [VMEM] * len(operands), 'blur_x_far' if far...  15.8 us
    pallas_call x5, Pallas kernels, log_factor(): call(kernel, shape, [VMEM] * (3 + len(parts)), 'log_factor')  9.5 us
    pallas_call x2, Pallas kernels, next_ratio(): return call(kernel, out_shape, [VMEM] * len(operands), 'ratio')(*operands)  9.34 us
    unnamed x40, local copies, waits for them, and re-layouts  8.08 us
    pallas_call x2, Pallas kernels, first_ratio(): call(kernel, out_shape, in_specs, 'image_and_ratio', scratch)  5.11 us
  transfers between devices with their start and end apart: 40, of which 17 were waited for; matrix products, arithmetic and copies ran while one was open for 2% of the time, Pallas kernels for 21%

profile of v12, /device:TPU:17, one launch (start us, length us, event | category | flops | bytes accessed | tf_op | source)
XLA Modules:
  0.0 208.7 jit_solution(17343484715667319136)
XLA Ops:
  4.3 4.0 %collective-permute-start.3 = (f32[1,16,128]{2,1,0:T(8,128)S(1)}, f32[1,16,128]{2,1,0:T(8,128)}, u32[]{:S(2)}, u32[]{:S(2)}) collective-permute-start(f32[1,16,128]{2,1,0:T(8,128)S(1)} %convert_element_type.16), channel_id=1, source_target_pairs={{0,8},{1,9},{2,10},{3,11},{4,12},{5,13},{6,14},{7,15},{8,0},{9,1},... | collective-permute-start | bytes 24584 | tf_op jit(solution)/shard_map/ppermute | solution.py:34
  9.5 2.0 band_matrices.1
  17.5 3.0 %shift_recorded.1 = (f32[16,80,256]{2,1,0:T(8,128)S(1)}, f32[16,80,256]{2,1,0:T(8,128)S(1)}) custom-call(s32[1,3]{1,0:T(1,128)S(1)} %copy-done.14, f32[16,128,256]{2,1,0:T(8,128)S(1)} %bitcast.1), custom_call_target="tpu_custom_call" | custom-call | tf_op jit(solution)/shard_map/shift_recorded/pallas_call | solution.py:277
  20.5 4.3 %collective-permute-done.4 = f32[2,16,128]{2,1,0:T(8,128)} collective-permute-done((f32[2,16,128]{2,1,0:T(8,128)}, f32[2,16,128]{2,1,0:T(8,128)}, u32[]{:S(2)}, u32[]{:S(2)}) %collective-permute-start.4) | collective-permute-done | bytes 16416 | tf_op jit(solution)/shard_map/ppermute | solution.py:34
  25.6 4.8 %collective-permute-start.5 = (f32[16,80,256]{2,1,0:T(8,128)S(1)}, f32[16,80,256]{2,1,0:T(8,128)S(1)}, u32[]{:S(2)}, u32[]{:S(2)}) collective-permute-start(f32[16,80,256]{2,1,0:T(8,128)S(1)} %get-tuple-element.83), channel_id=1, source_target_pairs={{1,8},{3,10},{5,12},{7,14},{8,1},{10,3},{12,5},{14,7},{17,24},{19,... | collective-permute-start | bytes 3932168 | tf_op jit(solution)/shard_map/ppermute | solution.py:34
  30.4 1.8 estimate.1
  32.2 1.9 collective-permute-start.9
  35.2 19.6 %collective-permute-done.5 = f32[16,80,256]{2,1,0:T(8,128)S(1)} collective-permute-done((f32[16,80,256]{2,1,0:T(8,128)S(1)}, f32[16,80,256]{2,1,0:T(8,128)S(1)}, u32[]{:S(2)}, u32[]{:S(2)}) %collective-permute-start.5) | collective-permute-done | bytes 1310752 | tf_op jit(solution)/shard_map/ppermute | solution.py:34
  54.9 1.9 collective-permute-start.6
  57.5 2.5 %collective-permute-done.12.own_ref = f32[16,80,256]{2,1,0:T(8,128)S(1)} collective-permute-done((f32[16,80,256]{2,1,0:T(8,128)S(1)}, f32[16,80,256]{2,1,0:T(8,128)S(1)}, u32[]{:S(2)}, u32[]{:S(2)}) %collective-permute-start.12) | collective-permute-done | bytes 1310752 | tf_op jit(solution)/shard_map/ppermute | solution.py:34
  60.0 2.4 %collective-permute-start.13 = (f32[16,80,256]{2,1,0:T(8,128)S(1)}, f32[16,80,256]{2,1,0:T(8,128)S(1)}, u32[]{:S(2)}, u32[]{:S(2)}) collective-permute-start(f32[16,80,256]{2,1,0:T(8,128)S(1)} %collective-permute-done.12.own_ref), channel_id=1, source_target_pairs={{2,8},{3,9},{4,10},{5,11},{6,12},{7,13},{8,2},{9,3},{10,4},{11,5},... | collective-permute-start | bytes 3932168 | tf_op jit(solution)/shard_map/ppermute | solution.py:34
  62.6 3.1 %blur_x_far.4 = (f32[16,96,256]{2,1,0:T(8,128)S(1)}, f32[16,96,256]{2,1,0:T(8,128)S(1)}) custom-call(bf16[2,256,384]{2,1,0:T(8,128)(2,1)S(1)} %get-tuple-element.73.hi_ref, bf16[2,256,384]{2,1,0:T(8,128)(2,1)S(1)} %get-tuple-element.74.lo_ref, f32[15,96,256]{2,1,0:T(8,128)S(1)} %collective-permute-done.9.refs_0_), custom_call_target="tpu_custom_call" | custom-call | tf_op jit(solution)/shard_map/blur_x_far/pallas_call | solution.py:325
  65.7 3.3 %blur_x_near.4 = (f32[16,96,256]{2,1,0:T(8,128)S(1)}, f32[16,96,256]{2,1,0:T(8,128)S(1)}) custom-call(bf16[2,256,384]{2,1,0:T(8,128)(2,1)S(1)} %get-tuple-element.73.hi_ref, bf16[2,256,384]{2,1,0:T(8,128)(2,1)S(1)} %get-tuple-element.74.lo_ref, f32[16,96,256]{2,1,0:T(8,128)S(1)} %get-tuple-element.80.refs_0_.before_ref, ...), custom_call_target="tpu_custom_call" | custom-call | tf_op jit(solution)/shard_map/blur_x_near/pallas_call | solution.py:325
  70.6 3.6 %collective-permute-done.6.far_ref = f32[16,80,256]{2,1,0:T(8,128)S(1)} collective-permute-done((f32[16,80,256]{2,1,0:T(8,128)S(1)}, f32[16,80,256]{2,1,0:T(8,128)S(1)}, u32[]{:S(2)}, u32[]{:S(2)}) %collective-permute-start.6) | collective-permute-done | bytes 1310752 | tf_op jit(solution)/shard_map/ppermute | solution.py:34
  74.2 2.6 %image_and_ratio.2 = (f32[16,64,256]{2,1,0:T(8,128)S(1)}, f32[15,64,256]{2,1,0:T(8,128)S(1)}, f32[15,64,256]{2,1,0:T(8,128)S(1)}, f32[16,80,256]{2,1,0:T(8,128)S(1)}) custom-call(s32[2,3]{1,0:T(2,128)S(1)} %fusion.2.shift_ref, f32[16,80,256]{2,1,0:T(8,128)S(1)} %collective-permute-done.6.far_ref, f32[16,80,256]{2,1,0:T(8,128)S(1)} %collective-permute-done.7.near_ref, ...), custom_call_target="tpu_custom_call" | custom-call | tf_op jit(solution)/shard_map/image_and_ratio/pallas_call | solution.py:480
  76.7 1.9 collective-permute-start.10
  80.9 7.3 %collective-permute-done.13.far_ref = f32[16,80,256]{2,1,0:T(8,128)S(1)} collective-permute-done((f32[16,80,256]{2,1,0:T(8,128)S(1)}, f32[16,80,256]{2,1,0:T(8,128)S(1)}, u32[]{:S(2)}, u32[]{:S(2)}) %collective-permute-start.13) | collective-permute-done | bytes 1310752 | tf_op jit(solution)/shard_map/ppermute | solution.py:34
  88.2 2.6 %image_and_ratio.3 = (f32[16,64,256]{2,1,0:T(8,128)S(1)}, f32[15,32,256]{2,1,0:T(8,128)S(1)}, f32[15,32,256]{2,1,0:T(8,128)S(1)}, f32[15,32,256]{2,1,0:T(8,128)S...) custom-call(s32[2,3]{1,0:T(2,128)S(1)} %fusion.2.shift_ref, ...), custom_call_target="tpu_custom_call" | custom-call | tf_op jit(solution)/shard_map/image_and_ratio/pallas_call | solution.py:480
  91.8 1.9 collective-permute-start.18
  94.4 4.4 %collective-permute-done.10.refs_0_ = f32[15,64,256]{2,1,0:T(8,128)S(1)} collective-permute-done((f32[15,64,256]{2,1,0:T(8,128)S(1)}, f32[15,64,256]{2,1,0:T(8,128)S(1)}, u32[]{:S(2)}, u32[]{:S(2)}) %collective-permute-start.10) | collective-permute-done | bytes 983072 | tf_op jit(solution)/shard_map/ppermute | solution.py:34
  98.7 2.1 %log_factor.5.before_ref = f32[16,64,256]{2,1,0:T(8,128)S(1)} custom-call(bf16[2,256,384]{2,1,0:T(8,128)(2,1)S(1)} %get-tuple-element.73.hi_ref, bf16[2,256,384]{2,1,0:T(8,128)(2,1)S(1)} %get-tuple-element.74.lo_ref, f32[16,96,256]{2,1,0:T(8,128)S(1)} %get-tuple-element.80.refs_0_.before_ref, f32[15,64,256]{2,1,0:T(8,128)S(1)} %collective-permute-done.10.refs_0_, ...), custom_call_target="tpu_custom_call" | custom-call | tf_op jit(solution)/shard_map/log_factor/pallas_call | solution.py:513
  100.9 2.8 %collective-permute-done.18.refs_0_ = f32[15,32,256]{2,1,0:T(8,128)S(1)} collective-permute-done((f32[15,32,256]{2,1,0:T(8,128)S(1)}, f32[15,32,256]{2,1,0:T(8,128)S(1)}, u32[]{:S(2)}, u32[]{:S(2)}) %collective-permute-start.18) | collective-permute-done | bytes 491552 | tf_op jit(solution)/shard_map/ppermute | solution.py:34
  106.1 2.4 %collective-permute-start.15 = (f32[15,32,256]{2,1,0:T(8,128)S(1)}, f32[15,32,256]{2,1,0:T(8,128)S(1)}, u32[]{:S(2)}, u32[]{:S(2)}) collective-permute-start(f32[15,32,256]{2,1,0:T(8,128)S(1)} %get-tuple-element.98), channel_id=1, source_target_pairs={{2,8},{3,9},{4,10},{5,11},{6,12},{7,13},{8,2},{9,3},{10,4},{11,5},... | collective-permute-start | bytes 1474568 | tf_op jit(solution)/shard_map/ppermute | solution.py:34
  108.8 7.7 %collective-permute-done.15.refs_0_ = f32[15,32,256]{2,1,0:T(8,128)S(1)} collective-permute-done((f32[15,32,256]{2,1,0:T(8,128)S(1)}, f32[15,32,256]{2,1,0:T(8,128)S(1)}, u32[]{:S(2)}, u32[]{:S(2)}) %collective-permute-start.15) | collective-permute-done | bytes 491552 | tf_op jit(solution)/shard_map/ppermute | solution.py:34
  116.5 1.9 log_factor.6.refs_0_
  120.6 2.0 collective-permute-start.24
  122.6 3.9 %collective-permute-start.21 = (f32[15,32,256]{2,1,0:T(8,128)}, f32[15,32,256]{2,1,0:T(8,128)}, u32[]{:S(2)}, u32[]{:S(2)}) collective-permute-start(f32[15,32,256]{2,1,0:T(8,128)} %get-tuple-element.107), channel_id=1, source_target_pairs={{2,8},{3,9},{4,10},{5,11},{6,12},{7,13},{8,2},{9,3},{10,4},{11,5},... | collective-permute-start | bytes 1474568 | tf_op jit(solution)/shard_map/ppermute | solution.py:34
  126.5 5.4 %collective-permute-done.17.refs_1_ = f32[16,32,256]{2,1,0:T(8,128)} collective-permute-done((f32[16,32,256]{2,1,0:T(8,128)}, f32[16,32,256]{2,1,0:T(8,128)}, u32[]{:S(2)}, u32[]{:S(2)}) %collective-permute-start.17) | collective-permute-done | bytes 524320 | tf_op jit(solution)/shard_map/ppermute | solution.py:34
  133.9 3.1 %collective-permute-start.22 = (f32[15,32,256]{2,1,0:T(8,128)S(1)}, f32[15,32,256]{2,1,0:T(8,128)S(1)}, u32[]{:S(2)}, u32[]{:S(2)}) collective-permute-start(f32[15,32,256]{2,1,0:T(8,128)S(1)} %get-tuple-element.108), channel_id=1, source_target_pairs={{2,8},{3,9},{4,10},{5,11},{6,12},{7,13},{8,2},{9,3},{10,4},{11,5},... | collective-permute-start | bytes 1474568 | tf_op jit(solution)/shard_map/ppermute | solution.py:34
  138.2 2.5 %collective-permute-start.25 = (f32[15,32,256]{2,1,0:T(8,128)S(1)}, f32[15,32,256]{2,1,0:T(8,128)S(1)}, u32[]{:S(2)}, u32[]{:S(2)}) collective-permute-start(f32[15,32,256]{2,1,0:T(8,128)S(1)} %get-tuple-element.142), channel_id=1, source_target_pairs={{2,8},{3,9},{4,10},{5,11},{6,12},{7,13},{8,2},{9,3},{10,4},{11,5},... | collective-permute-start | bytes 1474568 | tf_op jit(solution)/shard_map/ppermute | solution.py:34
  140.8 2.1 %blur_x_near.7 = (f32[16,32,256]{2,1,0:T(8,128)S(1)}, f32[16,32,256]{2,1,0:T(8,128)S(1)}) custom-call(bf16[2,256,384]{2,1,0:T(8,128)(2,1)S(1)} %get-tuple-element.73.hi_ref, bf16[2,256,384]{2,1,0:T(8,128)(2,1)S(1)} %get-tuple-element.74.lo_ref, f32[16,32,256]{2,1,0:T(8,128)} %get-tuple-element.113.refs_0_.before_ref, ...), custom_call_target="tpu_custom_call" | custom-call | tf_op jit(solution)/shard_map/blur_x_near/pallas_call | solution.py:325
  144.1 2.1 blur_x_far.6
  147.2 2.0 collective-permute-done.25.refs_0_
  149.3 2.1 %blur_x_near.6 = (f32[16,32,256]{2,1,0:T(8,128)S(1)}, f32[16,32,256]{2,1,0:T(8,128)S(1)}) custom-call(bf16[2,256,384]{2,1,0:T(8,128)(2,1)S(1)} %get-tuple-element.73.hi_ref, bf16[2,256,384]{2,1,0:T(8,128)(2,1)S(1)} %get-tuple-element.74.lo_ref, f32[16,32,256]{2,1,0:T(8,128)} %collective-permute-done.24.refs_0_, ...), custom_call_target="tpu_custom_call" | custom-call | tf_op jit(solution)/shard_map/blur_x_near/pallas_call | solution.py:325
  151.4 5.2 %ratio.2 = (f32[16,32,256]{2,1,0:T(8,128)S(1)}, f32[16,32,256]{2,1,0:T(8,128)S(1)}, f32[2,15,32,256]{3,2,1,0:T(8,128)S(1)}, f32[2,15,32,256]{3,2,1,0:T(8,128)S(1)}, f32[2,16,32,256]{3,2,1,0:T(8,128)S(1)}) custom-call(f32[16,80,256]{2,1,0:T(8,128)S(1)} %get-tuple-element.102.refs_0_, f32[16,80,256]{2,1,0:T(8,128)S(1)} %copy-done.1, ...), custom_call_target="tpu_custom_call" | custom-call | tf_op jit(solution)/shard_map/ratio/pallas_call | solution.py:468
  156.6 3.1 %collective-permute-start.28 = (f32[2,15,32,256]{3,2,1,0:T(8,128)S(1)}, f32[2,15,32,256]{3,2,1,0:T(8,128)S(1)}, u32[]{:S(2)}, u32[]{:S(2)}) collective-permute-start(f32[2,15,32,256]{3,2,1,0:T(8,128)S(1)} %get-tuple-element.127), channel_id=1, source_target_pairs={{2,8},{3,9},{4,10},{5,11},{6,12},{7,13},{8,2},{9,3},{10,4},{11,5},... | collective-permute-start | bytes 2949128 | tf_op jit(solution)/shard_map/ppermute | solution.py:34
  161.1 4.2 %ratio.3 = (f32[16,32,256]{2,1,0:T(8,128)S(1)}, f32[16,32,256]{2,1,0:T(8,128)S(1)}, f32[2,15,32,256]{3,2,1,0:T(8,128)S(1)}, f32[2,15,32,256]{3,2,1,0:T(8,128)S(1)}) custom-call(f32[16,80,256]{2,1,0:T(8,128)S(1)} %get-tuple-element.102.refs_0_, f32[16,80,256]{2,1,0:T(8,128)S(1)} %copy-done.1, f32[16,32,256]{2,1,0:T(8,128)S(1)} %get-tuple-element.120.refs_3_.refs_2_, ...), custom_call_target="tpu_custom_call" | custom-call | tf_op jit(solution)/shard_map/ratio/pallas_call | solution.py:468
  165.3 2.4 %collective-permute-start.34 = (f32[2,15,32,256]{3,2,1,0:T(8,128)S(1)}, f32[2,15,32,256]{3,2,1,0:T(8,128)S(1)}, u32[]{:S(2)}, u32[]{:S(2)}) collective-permute-start(f32[2,15,32,256]{3,2,1,0:T(8,128)S(1)} %get-tuple-element.137), channel_id=1, source_target_pairs={{2,8},{3,9},{4,10},{5,11},{6,12},{7,13},{8,2},{9,3},{10,4},{11,5},... | collective-permute-start | bytes 2949128 | tf_op jit(solution)/shard_map/ppermute | solution.py:34
  167.7 4.7 %collective-permute-done.28.refs_0_.refs_3_ = f32[2,15,32,256]{3,2,1,0:T(8,128)S(1)} collective-permute-done((f32[2,15,32,256]{3,2,1,0:T(8,128)S(1)}, f32[2,15,32,256]{3,2,1,0:T(8,128)S(1)}, u32[]{:S(2)}, u32[]{:S(2)}) %collective-permute-start.28) | collective-permute-done | bytes 983072 | tf_op jit(solution)/shard_map/ppermute | solution.py:34
  174.9 4.5 %collective-permute-start.31 = (f32[16,32,256]{2,1,0:T(8,128)S(1)}, f32[16,32,256]{2,1,0:T(8,128)S(1)}, u32[]{:S(2)}, u32[]{:S(2)}) collective-permute-start(f32[16,32,256]{2,1,0:T(8,128)S(1)} %log_factor.8.refs_0_), channel_id=1, source_target_pairs={{1,24},{3,26},{5,28},{7,30},{8,17},{10,19},{12,21},{14,23},{17,8},... | collective-permute-start | bytes 1572872 | tf_op jit(solution)/shard_map/ppermute | solution.py:34
  179.4 1.9 collective-permute-start.32
  183.0 2.7 %log_factor.9.refs_0_ = f32[16,32,256]{2,1,0:T(8,128)S(1)} custom-call(bf16[2,256,384]{2,1,0:T(8,128)(2,1)S(1)} %get-tuple-element.73.hi_ref, bf16[2,256,384]{2,1,0:T(8,128)(2,1)S(1)} %get-tuple-element.74.lo_ref, f32[16,32,256]{2,1,0:T(8,128)} %get-tuple-element.113.refs_0_.before_ref, f32[2,15,32,256]{3,2,1,0:T(8,128)S(1)} %collective-permute-done.34.refs_0_.refs_3_, ...), custom_call_target="tpu_custom_call" | custom-call | tf_op jit(solution)/shard_map/log_factor/pallas_call | solution.py:513
  186.4 4.5 %collective-permute-start.37 = (f32[16,32,256]{2,1,0:T(8,128)S(1)}, f32[16,32,256]{2,1,0:T(8,128)S(1)}, u32[]{:S(2)}, u32[]{:S(2)}) collective-permute-start(f32[16,32,256]{2,1,0:T(8,128)S(1)} %log_factor.9.refs_0_), channel_id=1, source_target_pairs={{1,24},{3,26},{5,28},{7,30},{8,17},{10,19},{12,21},{14,23},{17,8},... | collective-permute-start | bytes 1572872 | tf_op jit(solution)/shard_map/ppermute | solution.py:34
  190.9 1.9 collective-permute-start.38
  192.9 2.5 %collective-permute-done.32.refs_3_ = f32[16,32,256]{2,1,0:T(8,128)S(1)} collective-permute-done((f32[16,32,256]{2,1,0:T(8,128)S(1)}, f32[16,32,256]{2,1,0:T(8,128)S(1)}, u32[]{:S(2)}, u32[]{:S(2)}) %collective-permute-start.32) | collective-permute-done | bytes 524320 | tf_op jit(solution)/shard_map/ppermute | solution.py:34
  195.6 7.6 %collective-permute-done.37.refs_2_ = f32[16,32,256]{2,1,0:T(8,128)S(1)} collective-permute-done((f32[16,32,256]{2,1,0:T(8,128)S(1)}, f32[16,32,256]{2,1,0:T(8,128)S(1)}, u32[]{:S(2)}, u32[]{:S(2)}) %collective-permute-start.37) | collective-permute-done | bytes 524320 | tf_op jit(solution)/shard_map/ppermute | solution.py:34
  203.2 1.9 collective-permute-done.38.refs_3_
  205.3 1.9 collective-permute-done.39.refs_3_
  (108 shorter events, 37.9 us)
Async XLA Ops:
  1.6 6.6 %copy-start.17 = (f32[1,61]{1,0:T(1,128)S(1)}, f32[1,61]{1,0:T(1,128)}, u32[]{:S(2)}) copy-start(f32[1,61]{1,0:T(1,128)} %param.13) | copy-start | bytes 736
  1.6 6.6 %copy-start.18 = (f32[1,31]{1,0:T(1,128)S(1)}, f32[1,31]{1,0:T(1,128)}, u32[]{:S(2)}) copy-start(f32[1,31]{1,0:T(1,128)} %param.12) | copy-start | bytes 376
  1.6 6.6 %copy-start.19 = (f32[1,31]{1,0:T(1,128)S(1)}, f32[1,31]{1,0:T(1,128)}, u32[]{:S(2)}) copy-start(f32[1,31]{1,0:T(1,128)} %param.11) | copy-start | bytes 376
  1.6 14.3 %copy-start.14 = (s32[1,3]{1,0:T(1,128)S(1)}, s32[1,3]{1,0:T(1,128)}, u32[]{:S(2)}) copy-start(s32[1,3]{1,0:T(1,128)} %offsets_ref.1) | copy-start | bytes 40
  3.0 27.5 %collective-permute-start.1 = (f32[16,96,256]{2,1,0:T(8,128)}, f32[16,96,256]{2,1,0:T(8,128)}, u32[]{:S(2)}, u32[]{:S(2)}) collective-permute-start(f32[16,96,256]{2,1,0:T(8,128)} %get-tuple-element.79), channel_id=1, source_target_pairs={{0,1},{2,3},{4,5},{6,7},{9,8},{11,10},{13,12},{15,14},{16,17},{18,... | collective-permute-start | bytes 4718600 | tf_op jit(solution)/shard_map/ppermute | solution.py:34
  4.3 10.3 %collective-permute-start.3 = (f32[1,16,128]{2,1,0:T(8,128)S(1)}, f32[1,16,128]{2,1,0:T(8,128)}, u32[]{:S(2)}, u32[]{:S(2)}) collective-permute-start(f32[1,16,128]{2,1,0:T(8,128)S(1)} %convert_element_type.16), channel_id=1, source_target_pairs={{0,8},{1,9},{2,10},{3,11},{4,12},{5,13},{6,14},{7,15},{8,0},{9,1},... | collective-permute-start | bytes 24584 | tf_op jit(solution)/shard_map/ppermute | solution.py:34
  8.3 1.2 collective-permute-start
  15.9 8.9 %collective-permute-start.4 = (f32[2,16,128]{2,1,0:T(8,128)}, f32[2,16,128]{2,1,0:T(8,128)}, u32[]{:S(2)}, u32[]{:S(2)}) collective-permute-start(f32[2,16,128]{2,1,0:T(8,128)} %maximum_select_fusion), channel_id=1, source_target_pairs={{0,1},{1,0},{2,3},{3,2},{4,5},{5,4},{6,7},{7,6},{8,9},{9,8},{10,11... | collective-permute-start | bytes 49160 | tf_op jit(solution)/shard_map/ppermute | solution.py:34
  25.6 29.2 %collective-permute-start.5 = (f32[16,80,256]{2,1,0:T(8,128)S(1)}, f32[16,80,256]{2,1,0:T(8,128)S(1)}, u32[]{:S(2)}, u32[]{:S(2)}) collective-permute-start(f32[16,80,256]{2,1,0:T(8,128)S(1)} %get-tuple-element.83), channel_id=1, source_target_pairs={{1,8},{3,10},{5,12},{7,14},{8,1},{10,3},{12,5},{14,7},{17,24},{19,... | collective-permute-start | bytes 3932168 | tf_op jit(solution)/shard_map/ppermute | solution.py:34
  32.2 30.3 %collective-permute-start.9 = (f32[15,96,256]{2,1,0:T(8,128)S(1)}, f32[15,96,256]{2,1,0:T(8,128)S(1)}, u32[]{:S(2)}, u32[]{:S(2)}) collective-permute-start(f32[15,96,256]{2,1,0:T(8,128)S(1)} %get-tuple-element.85), channel_id=1, source_target_pairs={{2,8},{3,9},{4,10},{5,11},{6,12},{7,13},{8,2},{9,3},{10,4},{11,5},... | collective-permute-start | bytes 4423688 | tf_op jit(solution)/shard_map/ppermute | solution.py:34
  34.1 25.9 %collective-permute-start.12 = (f32[16,80,256]{2,1,0:T(8,128)S(1)}, f32[16,80,256]{2,1,0:T(8,128)S(1)}, u32[]{:S(2)}, u32[]{:S(2)}) collective-permute-start(f32[16,80,256]{2,1,0:T(8,128)S(1)} %get-tuple-element.96), channel_id=1, source_target_pairs={{0,1},{1,9},{2,3},{3,11},{4,5},{5,13},{6,7},{7,15},{8,0},{9,8},{10... | collective-permute-start | bytes 3932168 | tf_op jit(solution)/shard_map/ppermute | solution.py:34
  34.7 22.2 %collective-permute-start.2 = (f32[1,3]{1,0:T(1,128)S(1)}, f32[1,3]{1,0:T(1,128)S(1)}, u32[]{:S(2)}, u32[]{:S(2)}) collective-permute-start(f32[1,3]{1,0:T(1,128)S(1)} %convert_element_type.14), channel_id=1, source_target_pairs={{0,8},{1,9},{2,10},{3,11},{4,12},{5,13},{6,14},{7,15},{8,0},{9,1},... | collective-permute-start | bytes 44 | tf_op jit(solution)/shard_map/ppermute | solution.py:34
  34.8 30.9 %collective-permute-start.8 = (f32[15,96,256]{2,1,0:T(8,128)S(1)}, f32[15,96,256]{2,1,0:T(8,128)S(1)}, u32[]{:S(2)}, u32[]{:S(2)}) collective-permute-start(f32[15,96,256]{2,1,0:T(8,128)S(1)} %get-tuple-element.84), channel_id=1, source_target_pairs={{0,8},{1,9},{2,10},{3,11},{4,12},{5,13},{6,14},{7,15},{8,0},{9,1},... | collective-permute-start | bytes 4423688 | tf_op jit(solution)/shard_map/ppermute | solution.py:34
  54.9 19.2 %collective-permute-start.6 = (f32[16,80,256]{2,1,0:T(8,128)S(1)}, f32[16,80,256]{2,1,0:T(8,128)S(1)}, u32[]{:S(2)}, u32[]{:S(2)}) collective-permute-start(f32[16,80,256]{2,1,0:T(8,128)S(1)} %broadcast_select_fusion.own_ref), channel_id=1, source_target_pairs={{2,8},{3,9},{4,10},{5,11},{6,12},{7,13},{8,2},{9,3},{10,4},{11,5},... | collective-permute-start | bytes 3932168 | tf_op jit(solution)/shard_map/ppermute | solution.py:34
  56.9 17.3 %collective-permute-start.7 = (f32[16,80,256]{2,1,0:T(8,128)S(1)}, f32[16,80,256]{2,1,0:T(8,128)S(1)}, u32[]{:S(2)}, u32[]{:S(2)}) collective-permute-start(f32[16,80,256]{2,1,0:T(8,128)S(1)} %broadcast_select_fusion.own_ref), channel_id=1, source_target_pairs={{0,8},{1,9},{2,10},{3,11},{4,12},{5,13},{6,14},{7,15},{8,0},{9,1},... | collective-permute-start | bytes 3932168 | tf_op jit(solution)/shard_map/ppermute | solution.py:34
  60.0 28.2 %collective-permute-start.13 = (f32[16,80,256]{2,1,0:T(8,128)S(1)}, f32[16,80,256]{2,1,0:T(8,128)S(1)}, u32[]{:S(2)}, u32[]{:S(2)}) collective-permute-start(f32[16,80,256]{2,1,0:T(8,128)S(1)} %collective-permute-done.12.own_ref), channel_id=1, source_target_pairs={{2,8},{3,9},{4,10},{5,11},{6,12},{7,13},{8,2},{9,3},{10,4},{11,5},... | collective-permute-start | bytes 3932168 | tf_op jit(solution)/shard_map/ppermute | solution.py:34
  62.5 25.7 %collective-permute-start.14 = (f32[16,80,256]{2,1,0:T(8,128)S(1)}, f32[16,80,256]{2,1,0:T(8,128)S(1)}, u32[]{:S(2)}, u32[]{:S(2)}) collective-permute-start(f32[16,80,256]{2,1,0:T(8,128)S(1)} %collective-permute-done.12.own_ref), channel_id=1, source_target_pairs={{0,8},{1,9},{2,10},{3,11},{4,12},{5,13},{6,14},{7,15},{8,0},{9,1},... | collective-permute-start | bytes 3932168 | tf_op jit(solution)/shard_map/ppermute | solution.py:34
  69.0 5.2 %copy-start.5 = (bf16[2,64,256]{2,1,0:T(8,128)(2,1)S(1)}, bf16[2,64,256]{2,1,0:T(8,128)(2,1)}, u32[]{:S(2)}) copy-start(bf16[2,64,256]{2,1,0:T(8,128)(2,1)} %copy-done.4) | copy-start | bytes 196612
  76.7 22.0 %collective-permute-start.10 = (f32[15,64,256]{2,1,0:T(8,128)S(1)}, f32[15,64,256]{2,1,0:T(8,128)S(1)}, u32[]{:S(2)}, u32[]{:S(2)}) collective-permute-start(f32[15,64,256]{2,1,0:T(8,128)S(1)} %get-tuple-element.92), channel_id=1, source_target_pairs={{2,8},{3,9},{4,10},{5,11},{6,12},{7,13},{8,2},{9,3},{10,4},{11,5},... | collective-permute-start | bytes 2949128 | tf_op jit(solution)/shard_map/ppermute | solution.py:34
  78.7 20.1 %collective-permute-start.11 = (f32[15,64,256]{2,1,0:T(8,128)S(1)}, f32[15,64,256]{2,1,0:T(8,128)S(1)}, u32[]{:S(2)}, u32[]{:S(2)}) collective-permute-start(f32[15,64,256]{2,1,0:T(8,128)S(1)} %get-tuple-element.93), channel_id=1, source_target_pairs={{0,8},{1,9},{2,10},{3,11},{4,12},{5,13},{6,14},{7,15},{8,0},{9,1},... | collective-permute-start | bytes 2949128 | tf_op jit(solution)/shard_map/ppermute | solution.py:34
  91.8 11.9 %collective-permute-start.18 = (f32[15,32,256]{2,1,0:T(8,128)S(1)}, f32[15,32,256]{2,1,0:T(8,128)S(1)}, u32[]{:S(2)}, u32[]{:S(2)}) collective-permute-start(f32[15,32,256]{2,1,0:T(8,128)S(1)} %get-tuple-element.105), channel_id=1, source_target_pairs={{2,8},{3,9},{4,10},{5,11},{6,12},{7,13},{8,2},{9,3},{10,4},{11,5},... | collective-permute-start | bytes 1474568 | tf_op jit(solution)/shard_map/ppermute | solution.py:34
  93.8 10.0 %collective-permute-start.19 = (f32[15,32,256]{2,1,0:T(8,128)S(1)}, f32[15,32,256]{2,1,0:T(8,128)S(1)}, u32[]{:S(2)}, u32[]{:S(2)}) collective-permute-start(f32[15,32,256]{2,1,0:T(8,128)S(1)} %get-tuple-element.106), channel_id=1, source_target_pairs={{0,8},{1,9},{2,10},{3,11},{4,12},{5,13},{6,14},{7,15},{8,0},{9,1},... | collective-permute-start | bytes 1474568 | tf_op jit(solution)/shard_map/ppermute | solution.py:34
  104.8 13.9 %collective-permute-start.20 = (f32[16,32,256]{2,1,0:T(8,128)S(1)}, f32[16,32,256]{2,1,0:T(8,128)S(1)}, u32[]{:S(2)}, u32[]{:S(2)}) collective-permute-start(f32[16,32,256]{2,1,0:T(8,128)S(1)} %log_factor.7.refs_0_), channel_id=1, source_target_pairs={{0,16},{1,17},{2,18},{3,19},{4,20},{5,21},{6,22},{7,23},{8,24},{9,... | collective-permute-start | bytes 1572872 | tf_op jit(solution)/shard_map/ppermute | solution.py:34
  106.1 10.4 %collective-permute-start.15 = (f32[15,32,256]{2,1,0:T(8,128)S(1)}, f32[15,32,256]{2,1,0:T(8,128)S(1)}, u32[]{:S(2)}, u32[]{:S(2)}) collective-permute-start(f32[15,32,256]{2,1,0:T(8,128)S(1)} %get-tuple-element.98), channel_id=1, source_target_pairs={{2,8},{3,9},{4,10},{5,11},{6,12},{7,13},{8,2},{9,3},{10,4},{11,5},... | collective-permute-start | bytes 1474568 | tf_op jit(solution)/shard_map/ppermute | solution.py:34
  108.5 8.1 %collective-permute-start.16 = (f32[15,32,256]{2,1,0:T(8,128)S(1)}, f32[15,32,256]{2,1,0:T(8,128)S(1)}, u32[]{:S(2)}, u32[]{:S(2)}) collective-permute-start(f32[15,32,256]{2,1,0:T(8,128)S(1)} %get-tuple-element.99), channel_id=1, source_target_pairs={{0,8},{1,9},{2,10},{3,11},{4,12},{5,13},{6,14},{7,15},{8,0},{9,1},... | collective-permute-start | bytes 1474568 | tf_op jit(solution)/shard_map/ppermute | solution.py:34
  118.4 13.5 %collective-permute-start.17 = (f32[16,32,256]{2,1,0:T(8,128)}, f32[16,32,256]{2,1,0:T(8,128)}, u32[]{:S(2)}, u32[]{:S(2)}) collective-permute-start(f32[16,32,256]{2,1,0:T(8,128)} %log_factor.6.refs_0_), channel_id=1, source_target_pairs={{0,16},{1,17},{2,18},{3,19},{4,20},{5,21},{6,22},{7,23},{8,24},{9,... | collective-permute-start | bytes 1572872 | tf_op jit(solution)/shard_map/ppermute | solution.py:34
  120.6 16.4 %collective-permute-start.24 = (f32[16,32,256]{2,1,0:T(8,128)}, f32[16,32,256]{2,1,0:T(8,128)}, u32[]{:S(2)}, u32[]{:S(2)}) collective-permute-start(f32[16,32,256]{2,1,0:T(8,128)} %get-tuple-element.113.refs_0_.before_ref), channel_id=1, source_target_pairs={{0,1},{1,0},{2,3},{3,2},{4,5},{5,4},{6,7},{7,6},{8,9},{9,8},{10,11... | collective-permute-start | bytes 1572872 | tf_op jit(solution)/shard_map/ppermute | solution.py:34
  122.6 11.3 %collective-permute-start.21 = (f32[15,32,256]{2,1,0:T(8,128)}, f32[15,32,256]{2,1,0:T(8,128)}, u32[]{:S(2)}, u32[]{:S(2)}) collective-permute-start(f32[15,32,256]{2,1,0:T(8,128)} %get-tuple-element.107), channel_id=1, source_target_pairs={{2,8},{3,9},{4,10},{5,11},{6,12},{7,13},{8,2},{9,3},{10,4},{11,5},... | collective-permute-start | bytes 1474568 | tf_op jit(solution)/shard_map/ppermute | solution.py:34
  133.3 9.7 %collective-permute-start.23 = (f32[15,32,256]{2,1,0:T(8,128)S(1)}, f32[15,32,256]{2,1,0:T(8,128)S(1)}, u32[]{:S(2)}, u32[]{:S(2)}) collective-permute-start(f32[15,32,256]{2,1,0:T(8,128)S(1)} %get-tuple-element.109), channel_id=1, source_target_pairs={{0,8},{1,9},{2,10},{3,11},{4,12},{5,13},{6,14},{7,15},{8,0},{9,1},... | collective-permute-start | bytes 1474568 | tf_op jit(solution)/shard_map/ppermute | solution.py:34
  133.4 7.5 %collective-permute-start.27 = (f32[15,32,256]{2,1,0:T(8,128)}, f32[15,32,256]{2,1,0:T(8,128)S(1)}, u32[]{:S(2)}, u32[]{:S(2)}) collective-permute-start(f32[15,32,256]{2,1,0:T(8,128)} %copy-done.15), channel_id=1, source_target_pairs={{0,8},{1,9},{2,10},{3,11},{4,12},{5,13},{6,14},{7,15},{8,0},{9,1},... | collective-permute-start | bytes 1474568 | tf_op jit(solution)/shard_map/ppermute | solution.py:34
  133.9 12.3 %collective-permute-start.22 = (f32[15,32,256]{2,1,0:T(8,128)S(1)}, f32[15,32,256]{2,1,0:T(8,128)S(1)}, u32[]{:S(2)}, u32[]{:S(2)}) collective-permute-start(f32[15,32,256]{2,1,0:T(8,128)S(1)} %get-tuple-element.108), channel_id=1, source_target_pairs={{2,8},{3,9},{4,10},{5,11},{6,12},{7,13},{8,2},{9,3},{10,4},{11,5},... | collective-permute-start | bytes 1474568 | tf_op jit(solution)/shard_map/ppermute | solution.py:34
  138.2 11.1 %collective-permute-start.25 = (f32[15,32,256]{2,1,0:T(8,128)S(1)}, f32[15,32,256]{2,1,0:T(8,128)S(1)}, u32[]{:S(2)}, u32[]{:S(2)}) collective-permute-start(f32[15,32,256]{2,1,0:T(8,128)S(1)} %get-tuple-element.142), channel_id=1, source_target_pairs={{2,8},{3,9},{4,10},{5,11},{6,12},{7,13},{8,2},{9,3},{10,4},{11,5},... | collective-permute-start | bytes 1474568 | tf_op jit(solution)/shard_map/ppermute | solution.py:34
  140.7 8.6 %collective-permute-start.26 = (f32[15,32,256]{2,1,0:T(8,128)S(1)}, f32[15,32,256]{2,1,0:T(8,128)S(1)}, u32[]{:S(2)}, u32[]{:S(2)}) collective-permute-start(f32[15,32,256]{2,1,0:T(8,128)S(1)} %get-tuple-element.141), channel_id=1, source_target_pairs={{0,8},{1,9},{2,10},{3,11},{4,12},{5,13},{6,14},{7,15},{8,0},{9,1},... | collective-permute-start | bytes 1474568 | tf_op jit(solution)/shard_map/ppermute | solution.py:34
  147.2 4.2 %copy-start.1 = (f32[16,80,256]{2,1,0:T(8,128)S(1)}, f32[16,80,256]{2,1,0:T(8,128)}, u32[]{:S(2)}) copy-start(f32[16,80,256]{2,1,0:T(8,128)} %copy-done) | copy-start | bytes 3932164
  156.6 4.5 %copy-start.9 = (bf16[2,32,256]{2,1,0:T(8,128)(2,1)S(1)}, bf16[2,32,256]{2,1,0:T(8,128)(2,1)}, u32[]{:S(2)}) copy-start(bf16[2,32,256]{2,1,0:T(8,128)(2,1)} %copy-done.8) | copy-start | bytes 98308
  156.6 4.5 %copy-start.11 = (bf16[2,32,256]{2,1,0:T(8,128)(2,1)S(1)}, bf16[2,32,256]{2,1,0:T(8,128)(2,1)}, u32[]{:S(2)}) copy-start(bf16[2,32,256]{2,1,0:T(8,128)(2,1)} %copy-done.10) | copy-start | bytes 98308
  156.6 15.8 %collective-permute-start.28 = (f32[2,15,32,256]{3,2,1,0:T(8,128)S(1)}, f32[2,15,32,256]{3,2,1,0:T(8,128)S(1)}, u32[]{:S(2)}, u32[]{:S(2)}) collective-permute-start(f32[2,15,32,256]{3,2,1,0:T(8,128)S(1)} %get-tuple-element.127), channel_id=1, source_target_pairs={{2,8},{3,9},{4,10},{5,11},{6,12},{7,13},{8,2},{9,3},{10,4},{11,5},... | collective-permute-start | bytes 2949128 | tf_op jit(solution)/shard_map/ppermute | solution.py:34
  159.7 12.7 %collective-permute-start.29 = (f32[2,15,32,256]{3,2,1,0:T(8,128)S(1)}, f32[2,15,32,256]{3,2,1,0:T(8,128)S(1)}, u32[]{:S(2)}, u32[]{:S(2)}) collective-permute-start(f32[2,15,32,256]{3,2,1,0:T(8,128)S(1)} %get-tuple-element.128), channel_id=1, source_target_pairs={{0,8},{1,9},{2,10},{3,11},{4,12},{5,13},{6,14},{7,15},{8,0},{9,1},... | collective-permute-start | bytes 2949128 | tf_op jit(solution)/shard_map/ppermute | solution.py:34
  165.3 17.7 %collective-permute-start.34 = (f32[2,15,32,256]{3,2,1,0:T(8,128)S(1)}, f32[2,15,32,256]{3,2,1,0:T(8,128)S(1)}, u32[]{:S(2)}, u32[]{:S(2)}) collective-permute-start(f32[2,15,32,256]{3,2,1,0:T(8,128)S(1)} %get-tuple-element.137), channel_id=1, source_target_pairs={{2,8},{3,9},{4,10},{5,11},{6,12},{7,13},{8,2},{9,3},{10,4},{11,5},... | collective-permute-start | bytes 2949128 | tf_op jit(solution)/shard_map/ppermute | solution.py:34
  167.6 15.3 %collective-permute-start.35 = (f32[2,15,32,256]{3,2,1,0:T(8,128)S(1)}, f32[2,15,32,256]{3,2,1,0:T(8,128)S(1)}, u32[]{:S(2)}, u32[]{:S(2)}) collective-permute-start(f32[2,15,32,256]{3,2,1,0:T(8,128)S(1)} %get-tuple-element.138), channel_id=1, source_target_pairs={{0,8},{1,9},{2,10},{3,11},{4,12},{5,13},{6,14},{7,15},{8,0},{9,1},... | collective-permute-start | bytes 2949128 | tf_op jit(solution)/shard_map/ppermute | solution.py:34
  174.2 16.8 %collective-permute-start.30 = (f32[16,32,256]{2,1,0:T(8,128)S(1)}, f32[16,32,256]{2,1,0:T(8,128)S(1)}, u32[]{:S(2)}, u32[]{:S(2)}) collective-permute-start(f32[16,32,256]{2,1,0:T(8,128)S(1)} %log_factor.8.refs_0_), channel_id=1, source_target_pairs={{0,16},{2,18},{4,20},{6,22},{9,25},{11,27},{13,29},{15,31},{16,0},... | collective-permute-start | bytes 1572872 | tf_op jit(solution)/shard_map/ppermute | solution.py:34
  174.9 18.0 %collective-permute-start.31 = (f32[16,32,256]{2,1,0:T(8,128)S(1)}, f32[16,32,256]{2,1,0:T(8,128)S(1)}, u32[]{:S(2)}, u32[]{:S(2)}) collective-permute-start(f32[16,32,256]{2,1,0:T(8,128)S(1)} %log_factor.8.refs_0_), channel_id=1, source_target_pairs={{1,24},{3,26},{5,28},{7,30},{8,17},{10,19},{12,21},{14,23},{17,8},... | collective-permute-start | bytes 1572872 | tf_op jit(solution)/shard_map/ppermute | solution.py:34
  179.4 16.1 %collective-permute-start.32 = (f32[16,32,256]{2,1,0:T(8,128)S(1)}, f32[16,32,256]{2,1,0:T(8,128)S(1)}, u32[]{:S(2)}, u32[]{:S(2)}) collective-permute-start(f32[16,32,256]{2,1,0:T(8,128)S(1)} %log_factor.8.refs_0_), channel_id=1, source_target_pairs={{1,8},{3,10},{5,12},{7,14},{8,1},{10,3},{12,5},{14,7},{17,24},{19,... | collective-permute-start | bytes 1572872 | tf_op jit(solution)/shard_map/ppermute | solution.py:34
  185.7 9.9 %collective-permute-start.36 = (f32[16,32,256]{2,1,0:T(8,128)S(1)}, f32[16,32,256]{2,1,0:T(8,128)S(1)}, u32[]{:S(2)}, u32[]{:S(2)}) collective-permute-start(f32[16,32,256]{2,1,0:T(8,128)S(1)} %log_factor.9.refs_0_), channel_id=1, source_target_pairs={{0,16},{2,18},{4,20},{6,22},{9,25},{11,27},{13,29},{15,31},{16,0},... | collective-permute-start | bytes 1572872 | tf_op jit(solution)/shard_map/ppermute | solution.py:34
  186.4 16.7 %collective-permute-start.37 = (f32[16,32,256]{2,1,0:T(8,128)S(1)}, f32[16,32,256]{2,1,0:T(8,128)S(1)}, u32[]{:S(2)}, u32[]{:S(2)}) collective-permute-start(f32[16,32,256]{2,1,0:T(8,128)S(1)} %log_factor.9.refs_0_), channel_id=1, source_target_pairs={{1,24},{3,26},{5,28},{7,30},{8,17},{10,19},{12,21},{14,23},{17,8},... | collective-permute-start | bytes 1572872 | tf_op jit(solution)/shard_map/ppermute | solution.py:34
  190.9 14.2 %collective-permute-start.38 = (f32[16,32,256]{2,1,0:T(8,128)S(1)}, f32[16,32,256]{2,1,0:T(8,128)S(1)}, u32[]{:S(2)}, u32[]{:S(2)}) collective-permute-start(f32[16,32,256]{2,1,0:T(8,128)S(1)} %log_factor.9.refs_0_), channel_id=1, source_target_pairs={{1,8},{3,10},{5,12},{7,14},{8,1},{10,3},{12,5},{14,7},{17,24},{19,... | collective-permute-start | bytes 1572872 | tf_op jit(solution)/shard_map/ppermute | solution.py:34
  195.5 9.8 %collective-permute-start.33 = (f32[16,32,256]{2,1,0:T(8,128)S(1)}, f32[16,32,256]{2,1,0:T(8,128)S(1)}, u32[]{:S(2)}, u32[]{:S(2)}) collective-permute-start(f32[16,32,256]{2,1,0:T(8,128)S(1)} %last_update.2.refs_0_), channel_id=1, source_target_pairs={{0,8},{1,9},{2,10},{3,11},{4,12},{5,13},{6,14},{7,15},{8,0},{9,1},... | collective-permute-start | bytes 1572872 | tf_op jit(solution)/shard_map/ppermute | solution.py:34
  205.2 2.0 collective-permute-start.39
  (12 other events, 19.1 us)

commit v13 on v12

--- a/solution.py
+++ b/solution.py
@@ -609,21 +609,21 @@
     other = send(mine, to_core_partner)
     taps = kern_x.shape[1], taps_y, kern_z.shape[1]
     tables = make_tables(mine, other, taps, planes, cells_y, cells_z, (own_rows, near, wide))
-    offset = offsets.astype(F32)
+    offset = after(offsets.astype(F32), tables.whole[0])
     other = send(offset, to_core_partner)
     shifts = jnp.where(straight, jnp.concatenate([offset, other]), jnp.concatenate([other, offset])).astype(jnp.int32)
 
-    mask = view_mask.astype(F32)
-    other = send(mask, to_core_partner)
-    masks = jnp.where(core() == 0, jnp.concatenate([mask, other]), jnp.concatenate([other, mask]))
-    beyond = send(after(masks, tables.whole[0]), to_row_partner)
-    masks = jnp.where(straight, masks, beyond)
-
-    arrived = send(after(first, masks), lambda g, c, q, r: (g, r, q, c) if c != r else None)
+    arrived = send(after(first, tables.whole[0]), lambda g, c, q, r: (g, r, q, c) if c != r else None)
     current, distant, close = choose(after(window, first), crossed, radius)
     second = send(after(second, current), lambda g, c, q, r: (g, r, q, 1 - c))
     distant, close = neighbours(distant, close)
     first = jnp.where(straight, first, arrived)
+
+    mask = after(view_mask.astype(F32), current)
+    other = send(mask, to_core_partner)
+    masks = jnp.where(core() == 0, jnp.concatenate([mask, other]), jnp.concatenate([other, mask]))
+    masks = jnp.where(straight, masks, send(masks, to_row_partner))
+
     blocks = [(*neighbours(block, block), block) for block in (first, second)]
     wide_parts = blur_x(tables, (current, close), blur_x(tables, (distant,), (), planes), planes)
     blurred = [blur_yz([part], tables, order) for order, part in enumerate(wide_parts)]

time: 210 us -> 202 us (0.962)
  waiting for transfers between devices: 81.2 us -> 73.6 us
  starting transfers between devices: 59.9 us -> 66.6 us
  local copies, waits for them, and re-layouts: 9.33 us -> 4.9 us
    ppermute x40, waiting for transfers between devices: 81.2 us -> 73.6 us  [send(): return lax.ppermute(array, AXES, moves(move))]
    ppermute x40, starting transfers between devices: 59.9 us -> 66.6 us  [send(): return lax.ppermute(array, AXES, moves(move))]
    unnamed x40 -> x44, local copies, waits for them, and re-layouts: 8.08 us -> 4.82 us
  transfers between devices with their start and end apart: 40 -> 40, of which waited for: 17 -> 17; matrix products, arithmetic and copies ran while one was open for 2% -> 1% of each run, Pallas kernels for 21% -> 22%
where the time goes in v13:
time: 202 us
  waiting for transfers between devices  73.6 us (36%)
  starting transfers between devices  66.6 us (33%)
  Pallas kernels  53.3 us (26%)
  local copies, waits for them, and re-layouts  4.9 us (2%)
  other arithmetic  2.18 us (1%)
    ppermute x40, waiting for transfers between devices, send(): return lax.ppermute(array, AXES, moves(move))  73.6 us
    ppermute x40, starting transfers between devices, send(): return lax.ppermute(array, AXES, moves(move))  66.6 us
    pallas_call x8, Pallas kernels, blur_x(): call(kernel, (shape, shape), [VMEM] * len(operands), 'blur_x_far' if far...  15.1 us
    pallas_call x2, Pallas kernels, next_ratio(): return call(kernel, out_shape, [VMEM] * len(operands), 'ratio')(*operands)  9.35 us
    pallas_call x5, Pallas kernels, log_factor(): call(kernel, shape, [VMEM] * (3 + len(parts)), 'log_factor')  7.67 us
    pallas_call x2, Pallas kernels, first_ratio(): call(kernel, out_shape, in_specs, 'image_and_ratio', scratch)  6.22 us
    unnamed x44, local copies, waits for them, and re-layouts  4.82 us
    pallas_call x1, Pallas kernels, shift_and_cut(): call(shift_kernel, (shape, shape), [SMEM, VMEM], 'shift_recorded', scratch)  4.48 us
  transfers between devices with their start and end apart: 40, of which 17 were waited for; matrix products, arithmetic and copies ran while one was open for 1% of the time, Pallas kernels for 22%

profile of v13, /device:TPU:17, one launch (start us, length us, event | category | flops | bytes accessed | tf_op | source)
XLA Modules:
  0.0 201.6 jit_solution(15107723409710651226)
XLA Ops:
  0.0 1.7 copy-done.5
  3.9 2.9 %collective-permute-start = (f32[1,384]{1,0:T(1,128)S(1)}, f32[1,384]{1,0:T(1,128)S(1)}, u32[]{:S(2)}, u32[]{:S(2)}) collective-permute-start(f32[1,384]{1,0:T(1,128)S(1)} %fusion.1.mine_ref), channel_id=1, source_target_pairs={{0,8},{1,9},{2,10},{3,11},{4,12},{5,13},{6,14},{7,15},{8,0},{9,1},... | collective-permute-start | bytes 4616 | tf_op jit(solution)/shard_map/ppermute | solution.py:34
  6.9 4.5 %shift_recorded.1 = (f32[16,80,256]{2,1,0:T(8,128)}, f32[16,80,256]{2,1,0:T(8,128)}) custom-call(s32[1,3]{1,0:T(1,128)S(1)} %copy-done.16, f32[16,128,256]{2,1,0:T(8,128)S(1)} %bitcast.1), custom_call_target="tpu_custom_call" | custom-call | tf_op jit(solution)/shard_map/shift_recorded/pallas_call | solution.py:277
  11.3 2.0 %band_matrices.1 = (bf16[2,80,384]{2,1,0:T(8,128)(2,1)S(1)}, bf16[2,64,256]{2,1,0:T(8,128)(2,1)S(1)}, bf16[2,48,256]{2,1,0:T(8,128)(2,1)S(1)}, bf16[2,32,256]{2,...) custom-call(f32[1,384]{1,0:T(1,128)S(1)} %fusion.1.mine_ref, ...), custom_call_target="tpu_custom_call" | custom-call | tf_op jit(solution)/shard_map/band_matrices/pallas_call | solution.py:201
  13.4 2.1 %collective-permute-start.3 = (f32[16,80,256]{2,1,0:T(8,128)}, f32[16,80,256]{2,1,0:T(8,128)}, u32[]{:S(2)}, u32[]{:S(2)}) collective-permute-start(f32[16,80,256]{2,1,0:T(8,128)} %get-tuple-element.84), channel_id=1, source_target_pairs={{1,8},{3,10},{5,12},{7,14},{8,1},{10,3},{12,5},{14,7},{17,24},{19,... | collective-permute-start | bytes 3932168 | tf_op jit(solution)/shard_map/ppermute | solution.py:34
  15.5 12.0 %collective-permute-done.1.crossed_ref = f32[16,96,256]{2,1,0:T(8,128)S(1)} collective-permute-done((f32[16,96,256]{2,1,0:T(8,128)S(1)}, f32[16,96,256]{2,1,0:T(8,128)S(1)}, u32[]{:S(2)}, u32[]{:S(2)}) %collective-permute-start.1) | collective-permute-done | bytes 1572896 | tf_op jit(solution)/shard_map/ppermute | solution.py:34
  30.1 6.9 %collective-permute-start.9 = (f32[15,96,256]{2,1,0:T(8,128)}, f32[15,96,256]{2,1,0:T(8,128)}, u32[]{:S(2)}, u32[]{:S(2)}) collective-permute-start(f32[15,96,256]{2,1,0:T(8,128)} %get-tuple-element.87), channel_id=1, source_target_pairs={{2,8},{3,9},{4,10},{5,11},{6,12},{7,13},{8,2},{9,3},{10,4},{11,5},... | collective-permute-start | bytes 4423688 | tf_op jit(solution)/shard_map/ppermute | solution.py:34
  43.1 2.1 %collective-permute-start.4 = (f32[16,80,256]{2,1,0:T(8,128)S(1)}, f32[16,80,256]{2,1,0:T(8,128)S(1)}, u32[]{:S(2)}, u32[]{:S(2)}) collective-permute-start(f32[16,80,256]{2,1,0:T(8,128)S(1)} %broadcast_select_fusion.own_ref), channel_id=1, source_target_pairs={{2,8},{3,9},{4,10},{5,11},{6,12},{7,13},{8,2},{9,3},{10,4},{11,5},... | collective-permute-start | bytes 3932168 | tf_op jit(solution)/shard_map/ppermute | solution.py:34
  45.2 9.9 %collective-permute-done.7 = f32[2,16,128]{2,1,0:T(8,128)S(1)} collective-permute-done((f32[2,16,128]{2,1,0:T(8,128)S(1)}, f32[2,16,128]{2,1,0:T(8,128)S(1)}, u32[]{:S(2)}, u32[]{:S(2)}) %collective-permute-start.7) | collective-permute-done | bytes 16416 | tf_op jit(solution)/shard_map/ppermute | solution.py:34
  55.1 2.0 %collective-permute-start.13 = (f32[16,80,256]{2,1,0:T(8,128)}, f32[16,80,256]{2,1,0:T(8,128)S(1)}, u32[]{:S(2)}, u32[]{:S(2)}) collective-permute-start(f32[16,80,256]{2,1,0:T(8,128)} %collective-permute-done.12.own_ref), channel_id=1, source_target_pairs={{2,8},{3,9},{4,10},{5,11},{6,12},{7,13},{8,2},{9,3},{10,4},{11,5},... | collective-permute-start | bytes 3932168 | tf_op jit(solution)/shard_map/ppermute | solution.py:34
  57.7 4.4 %blur_x_far.4 = (f32[16,96,256]{2,1,0:T(8,128)S(1)}, f32[16,96,256]{2,1,0:T(8,128)S(1)}) custom-call(bf16[2,256,384]{2,1,0:T(8,128)(2,1)S(1)} %get-tuple-element.74.hi_ref, bf16[2,256,384]{2,1,0:T(8,128)(2,1)S(1)} %get-tuple-element.75.lo_ref, f32[15,96,256]{2,1,0:T(8,128)} %collective-permute-done.9.refs_0_), custom_call_target="tpu_custom_call" | custom-call | tf_op jit(solution)/shard_map/blur_x_far/pallas_call | solution.py:325
  62.1 3.3 %blur_x_near.4 = (f32[16,96,256]{2,1,0:T(8,128)S(1)}, f32[16,96,256]{2,1,0:T(8,128)S(1)}) custom-call(bf16[2,256,384]{2,1,0:T(8,128)(2,1)S(1)} %get-tuple-element.74.hi_ref, bf16[2,256,384]{2,1,0:T(8,128)(2,1)S(1)} %get-tuple-element.75.lo_ref, f32[16,96,256]{2,1,0:T(8,128)S(1)} %get-tuple-element.81.refs_0_.before_ref, ...), custom_call_target="tpu_custom_call" | custom-call | tf_op jit(solution)/shard_map/blur_x_near/pallas_call | solution.py:325
  65.5 1.6 blur_yz.2.blurred_ref
  67.0 1.6 collective-permute-done.4.far_ref
  68.6 2.5 %image_and_ratio.2 = (f32[16,64,256]{2,1,0:T(8,128)S(1)}, f32[15,64,256]{2,1,0:T(8,128)S(1)}, f32[15,64,256]{2,1,0:T(8,128)S(1)}, f32[16,80,256]{2,1,0:T(8,128)S(1)}) custom-call(s32[2,3]{1,0:T(2,128)S(1)} %fusion.2.shift_ref, f32[16,80,256]{2,1,0:T(8,128)S(1)} %collective-permute-done.4.far_ref, f32[16,80,256]{2,1,0:T(8,128)S(1)} %collective-permute-done.5.near_ref, ...), custom_call_target="tpu_custom_call" | custom-call | tf_op jit(solution)/shard_map/image_and_ratio/pallas_call | solution.py:480
  71.2 3.3 %collective-permute-start.10 = (f32[15,64,256]{2,1,0:T(8,128)S(1)}, f32[15,64,256]{2,1,0:T(8,128)S(1)}, u32[]{:S(2)}, u32[]{:S(2)}) collective-permute-start(f32[15,64,256]{2,1,0:T(8,128)S(1)} %get-tuple-element.94), channel_id=1, source_target_pairs={{2,8},{3,9},{4,10},{5,11},{6,12},{7,13},{8,2},{9,3},{10,4},{11,5},... | collective-permute-start | bytes 2949128 | tf_op jit(solution)/shard_map/ppermute | solution.py:34
  74.6 1.6 blur_yz.3.blurred_ref
  76.2 6.5 %collective-permute-done.13.far_ref = f32[16,80,256]{2,1,0:T(8,128)S(1)} collective-permute-done((f32[16,80,256]{2,1,0:T(8,128)}, f32[16,80,256]{2,1,0:T(8,128)S(1)}, u32[]{:S(2)}, u32[]{:S(2)}) %collective-permute-start.13) | collective-permute-done | bytes 1310752 | tf_op jit(solution)/shard_map/ppermute | solution.py:34
  82.7 3.7 %image_and_ratio.3 = (f32[16,64,256]{2,1,0:T(8,128)S(1)}, f32[15,32,256]{2,1,0:T(8,128)S(1)}, f32[15,32,256]{2,1,0:T(8,128)S(1)}, f32[15,32,256]{2,1,0:T(8,128)S...) custom-call(s32[2,3]{1,0:T(2,128)S(1)} %fusion.2.shift_ref, ...), custom_call_target="tpu_custom_call" | custom-call | tf_op jit(solution)/shard_map/image_and_ratio/pallas_call | solution.py:480
  87.4 3.3 %collective-permute-start.18 = (f32[15,32,256]{2,1,0:T(8,128)S(1)}, f32[15,32,256]{2,1,0:T(8,128)S(1)}, u32[]{:S(2)}, u32[]{:S(2)}) collective-permute-start(f32[15,32,256]{2,1,0:T(8,128)S(1)} %get-tuple-element.107), channel_id=1, source_target_pairs={{2,8},{3,9},{4,10},{5,11},{6,12},{7,13},{8,2},{9,3},{10,4},{11,5},... | collective-permute-start | bytes 1474568 | tf_op jit(solution)/shard_map/ppermute | solution.py:34
  90.8 2.4 %collective-permute-done.10.refs_0_ = f32[15,64,256]{2,1,0:T(8,128)S(1)} collective-permute-done((f32[15,64,256]{2,1,0:T(8,128)S(1)}, f32[15,64,256]{2,1,0:T(8,128)S(1)}, u32[]{:S(2)}, u32[]{:S(2)}) %collective-permute-start.10) | collective-permute-done | bytes 983072 | tf_op jit(solution)/shard_map/ppermute | solution.py:34
  93.2 2.1 %log_factor.5.before_ref = f32[16,64,256]{2,1,0:T(8,128)S(1)} custom-call(bf16[2,256,384]{2,1,0:T(8,128)(2,1)S(1)} %get-tuple-element.74.hi_ref, bf16[2,256,384]{2,1,0:T(8,128)(2,1)S(1)} %get-tuple-element.75.lo_ref, f32[16,96,256]{2,1,0:T(8,128)S(1)} %get-tuple-element.81.refs_0_.before_ref, f32[15,64,256]{2,1,0:T(8,128)S(1)} %collective-permute-done.10.refs_0_, ...), custom_call_target="tpu_custom_call" | custom-call | tf_op jit(solution)/shard_map/log_factor/pallas_call | solution.py:513
  95.3 3.0 %collective-permute-done.18.refs_0_ = f32[15,32,256]{2,1,0:T(8,128)S(1)} collective-permute-done((f32[15,32,256]{2,1,0:T(8,128)S(1)}, f32[15,32,256]{2,1,0:T(8,128)S(1)}, u32[]{:S(2)}, u32[]{:S(2)}) %collective-permute-start.18) | collective-permute-done | bytes 491552 | tf_op jit(solution)/shard_map/ppermute | solution.py:34
  100.7 3.9 %collective-permute-start.15 = (f32[15,32,256]{2,1,0:T(8,128)S(1)}, f32[15,32,256]{2,1,0:T(8,128)S(1)}, u32[]{:S(2)}, u32[]{:S(2)}) collective-permute-start(f32[15,32,256]{2,1,0:T(8,128)S(1)} %get-tuple-element.100), channel_id=1, source_target_pairs={{2,8},{3,9},{4,10},{5,11},{6,12},{7,13},{8,2},{9,3},{10,4},{11,5},... | collective-permute-start | bytes 1474568 | tf_op jit(solution)/shard_map/ppermute | solution.py:34
  104.7 6.5 %collective-permute-done.15.refs_0_ = f32[15,32,256]{2,1,0:T(8,128)S(1)} collective-permute-done((f32[15,32,256]{2,1,0:T(8,128)S(1)}, f32[15,32,256]{2,1,0:T(8,128)S(1)}, u32[]{:S(2)}, u32[]{:S(2)}) %collective-permute-start.15) | collective-permute-done | bytes 491552 | tf_op jit(solution)/shard_map/ppermute | solution.py:34
  114.3 2.2 %collective-permute-start.24 = (f32[16,32,256]{2,1,0:T(8,128)S(1)}, f32[16,32,256]{2,1,0:T(8,128)S(1)}, u32[]{:S(2)}, u32[]{:S(2)}) collective-permute-start(f32[16,32,256]{2,1,0:T(8,128)S(1)} %get-tuple-element.115.refs_0_.before_ref), channel_id=1, source_target_pairs={{0,1},{1,0},{2,3},{3,2},{4,5},{5,4},{6,7},{7,6},{8,9},{9,8},{10,11... | collective-permute-start | bytes 1572872 | tf_op jit(solution)/shard_map/ppermute | solution.py:34
  116.5 3.9 %collective-permute-start.21 = (f32[15,32,256]{2,1,0:T(8,128)}, f32[15,32,256]{2,1,0:T(8,128)}, u32[]{:S(2)}, u32[]{:S(2)}) collective-permute-start(f32[15,32,256]{2,1,0:T(8,128)} %get-tuple-element.109), channel_id=1, source_target_pairs={{2,8},{3,9},{4,10},{5,11},{6,12},{7,13},{8,2},{9,3},{10,4},{11,5},... | collective-permute-start | bytes 1474568 | tf_op jit(solution)/shard_map/ppermute | solution.py:34
  120.5 5.3 %collective-permute-done.17.refs_1_ = f32[16,32,256]{2,1,0:T(8,128)} collective-permute-done((f32[16,32,256]{2,1,0:T(8,128)S(1)}, f32[16,32,256]{2,1,0:T(8,128)}, u32[]{:S(2)}, u32[]{:S(2)}) %collective-permute-start.17) | collective-permute-done | bytes 524320 | tf_op jit(solution)/shard_map/ppermute | solution.py:34
  128.2 2.7 %collective-permute-start.22 = (f32[15,32,256]{2,1,0:T(8,128)S(1)}, f32[15,32,256]{2,1,0:T(8,128)S(1)}, u32[]{:S(2)}, u32[]{:S(2)}) collective-permute-start(f32[15,32,256]{2,1,0:T(8,128)S(1)} %get-tuple-element.110), channel_id=1, source_target_pairs={{2,8},{3,9},{4,10},{5,11},{6,12},{7,13},{8,2},{9,3},{10,4},{11,5},... | collective-permute-start | bytes 1474568 | tf_op jit(solution)/shard_map/ppermute | solution.py:34
  131.0 2.8 %collective-permute-start.25 = (f32[15,32,256]{2,1,0:T(8,128)S(1)}, f32[15,32,256]{2,1,0:T(8,128)S(1)}, u32[]{:S(2)}, u32[]{:S(2)}) collective-permute-start(f32[15,32,256]{2,1,0:T(8,128)S(1)} %get-tuple-element.144), channel_id=1, source_target_pairs={{2,8},{3,9},{4,10},{5,11},{6,12},{7,13},{8,2},{9,3},{10,4},{11,5},... | collective-permute-start | bytes 1474568 | tf_op jit(solution)/shard_map/ppermute | solution.py:34
  136.5 2.1 %blur_x_far.6 = (f32[16,32,256]{2,1,0:T(8,128)S(1)}, f32[16,32,256]{2,1,0:T(8,128)S(1)}) custom-call(bf16[2,256,384]{2,1,0:T(8,128)(2,1)S(1)} %get-tuple-element.74.hi_ref, bf16[2,256,384]{2,1,0:T(8,128)(2,1)S(1)} %get-tuple-element.75.lo_ref, f32[15,32,256]{2,1,0:T(8,128)} %collective-permute-done.21.refs_0_, ...), custom_call_target="tpu_custom_call" | custom-call | tf_op jit(solution)/shard_map/blur_x_far/pallas_call | solution.py:325
  139.7 3.9 %collective-permute-done.25.refs_0_ = f32[15,32,256]{2,1,0:T(8,128)S(1)} collective-permute-done((f32[15,32,256]{2,1,0:T(8,128)S(1)}, f32[15,32,256]{2,1,0:T(8,128)S(1)}, u32[]{:S(2)}, u32[]{:S(2)}) %collective-permute-start.25) | collective-permute-done | bytes 491552 | tf_op jit(solution)/shard_map/ppermute | solution.py:34
  144.8 5.2 %ratio.2 = (f32[16,32,256]{2,1,0:T(8,128)S(1)}, f32[16,32,256]{2,1,0:T(8,128)S(1)}, f32[2,15,32,256]{3,2,1,0:T(8,128)S(1)}, f32[2,15,32,256]{3,2,1,0:T(8,128)S(1)}, f32[2,16,32,256]{3,2,1,0:T(8,128)S(1)}) custom-call(f32[16,80,256]{2,1,0:T(8,128)S(1)} %copy-done.1, f32[16,80,256]{2,1,0:T(8,128)S(1)} %copy-done.3, ...), custom_call_target="tpu_custom_call" | custom-call | tf_op jit(solution)/shard_map/ratio/pallas_call | solution.py:468
  150.0 2.7 %collective-permute-start.28 = (f32[2,15,32,256]{3,2,1,0:T(8,128)S(1)}, f32[2,15,32,256]{3,2,1,0:T(8,128)S(1)}, u32[]{:S(2)}, u32[]{:S(2)}) collective-permute-start(f32[2,15,32,256]{3,2,1,0:T(8,128)S(1)} %get-tuple-element.129), channel_id=1, source_target_pairs={{2,8},{3,9},{4,10},{5,11},{6,12},{7,13},{8,2},{9,3},{10,4},{11,5},... | collective-permute-start | bytes 2949128 | tf_op jit(solution)/shard_map/ppermute | solution.py:34
  153.8 4.2 %ratio.3 = (f32[16,32,256]{2,1,0:T(8,128)S(1)}, f32[16,32,256]{2,1,0:T(8,128)S(1)}, f32[2,15,32,256]{3,2,1,0:T(8,128)S(1)}, f32[2,15,32,256]{3,2,1,0:T(8,128)S(1)}) custom-call(f32[16,80,256]{2,1,0:T(8,128)S(1)} %copy-done.1, f32[16,80,256]{2,1,0:T(8,128)S(1)} %copy-done.3, f32[16,32,256]{2,1,0:T(8,128)S(1)} %get-tuple-element.122.refs_3_.refs_2_, ...), custom_call_target="tpu_custom_call" | custom-call | tf_op jit(solution)/shard_map/ratio/pallas_call | solution.py:468
  158.0 3.0 %collective-permute-start.34 = (f32[2,15,32,256]{3,2,1,0:T(8,128)S(1)}, f32[2,15,32,256]{3,2,1,0:T(8,128)S(1)}, u32[]{:S(2)}, u32[]{:S(2)}) collective-permute-start(f32[2,15,32,256]{3,2,1,0:T(8,128)S(1)} %get-tuple-element.139), channel_id=1, source_target_pairs={{2,8},{3,9},{4,10},{5,11},{6,12},{7,13},{8,2},{9,3},{10,4},{11,5},... | collective-permute-start | bytes 2949128 | tf_op jit(solution)/shard_map/ppermute | solution.py:34
  161.4 4.4 %collective-permute-done.28.refs_0_.refs_3_ = f32[2,15,32,256]{3,2,1,0:T(8,128)S(1)} collective-permute-done((f32[2,15,32,256]{3,2,1,0:T(8,128)S(1)}, f32[2,15,32,256]{3,2,1,0:T(8,128)S(1)}, u32[]{:S(2)}, u32[]{:S(2)}) %collective-permute-start.28) | collective-permute-done | bytes 983072 | tf_op jit(solution)/shard_map/ppermute | solution.py:34
  165.8 1.7 log_factor.8.refs_0_
  168.2 3.9 %collective-permute-start.31 = (f32[16,32,256]{2,1,0:T(8,128)S(1)}, f32[16,32,256]{2,1,0:T(8,128)S(1)}, u32[]{:S(2)}, u32[]{:S(2)}) collective-permute-start(f32[16,32,256]{2,1,0:T(8,128)S(1)} %log_factor.8.refs_0_), channel_id=1, source_target_pairs={{1,24},{3,26},{5,28},{7,30},{8,17},{10,19},{12,21},{14,23},{17,8},... | collective-permute-start | bytes 1572872 | tf_op jit(solution)/shard_map/ppermute | solution.py:34
  172.2 2.2 %collective-permute-start.32 = (f32[16,32,256]{2,1,0:T(8,128)S(1)}, f32[16,32,256]{2,1,0:T(8,128)S(1)}, u32[]{:S(2)}, u32[]{:S(2)}) collective-permute-start(f32[16,32,256]{2,1,0:T(8,128)S(1)} %log_factor.8.refs_0_), channel_id=1, source_target_pairs={{1,8},{3,10},{5,12},{7,14},{8,1},{10,3},{12,5},{14,7},{17,24},{19,... | collective-permute-start | bytes 1572872 | tf_op jit(solution)/shard_map/ppermute | solution.py:34
  174.3 2.0 collective-permute-done.34.refs_0_.refs_3_
  176.3 1.7 log_factor.9.refs_0_
  178.7 3.9 %collective-permute-start.37 = (f32[16,32,256]{2,1,0:T(8,128)S(1)}, f32[16,32,256]{2,1,0:T(8,128)S(1)}, u32[]{:S(2)}, u32[]{:S(2)}) collective-permute-start(f32[16,32,256]{2,1,0:T(8,128)S(1)} %log_factor.9.refs_0_), channel_id=1, source_target_pairs={{1,24},{3,26},{5,28},{7,30},{8,17},{10,19},{12,21},{14,23},{17,8},... | collective-permute-start | bytes 1572872 | tf_op jit(solution)/shard_map/ppermute | solution.py:34
  182.7 2.2 %collective-permute-start.38 = (f32[16,32,256]{2,1,0:T(8,128)S(1)}, f32[16,32,256]{2,1,0:T(8,128)S(1)}, u32[]{:S(2)}, u32[]{:S(2)}) collective-permute-start(f32[16,32,256]{2,1,0:T(8,128)S(1)} %log_factor.9.refs_0_), channel_id=1, source_target_pairs={{1,8},{3,10},{5,12},{7,14},{8,1},{10,3},{12,5},{14,7},{17,24},{19,... | collective-permute-start | bytes 1572872 | tf_op jit(solution)/shard_map/ppermute | solution.py:34
  185.2 3.4 %collective-permute-done.32.refs_3_ = f32[16,32,256]{2,1,0:T(8,128)S(1)} collective-permute-done((f32[16,32,256]{2,1,0:T(8,128)S(1)}, f32[16,32,256]{2,1,0:T(8,128)S(1)}, u32[]{:S(2)}, u32[]{:S(2)}) %collective-permute-start.32) | collective-permute-done | bytes 524320 | tf_op jit(solution)/shard_map/ppermute | solution.py:34
  188.8 7.5 %collective-permute-done.37.refs_2_ = f32[16,32,256]{2,1,0:T(8,128)S(1)} collective-permute-done((f32[16,32,256]{2,1,0:T(8,128)S(1)}, f32[16,32,256]{2,1,0:T(8,128)S(1)}, u32[]{:S(2)}, u32[]{:S(2)}) %collective-permute-start.37) | collective-permute-done | bytes 524320 | tf_op jit(solution)/shard_map/ppermute | solution.py:34
  196.3 1.7 collective-permute-done.38.refs_3_
  198.2 1.9 collective-permute-done.39.refs_3_
  (112 shorter events, 30.4 us)
Async XLA Ops:
  0.0 6.8 %copy-start.4 = (f32[1,16,128,256]{3,2,1,0:T(8,128)S(1)}, f32[1,16,128,256]{3,2,1,0:T(8,128)}, u32[]{:S(2)}) copy-start(f32[1,16,128,256]{3,2,1,0:T(8,128)} %param.7) | copy-start | bytes 6291460
  2.0 25.6 %collective-permute-start.1 = (f32[16,96,256]{2,1,0:T(8,128)S(1)}, f32[16,96,256]{2,1,0:T(8,128)S(1)}, u32[]{:S(2)}, u32[]{:S(2)}) collective-permute-start(f32[16,96,256]{2,1,0:T(8,128)S(1)} %get-tuple-element.80), channel_id=1, source_target_pairs={{0,1},{2,3},{4,5},{6,7},{9,8},{11,10},{13,12},{15,14},{16,17},{18,... | collective-permute-start | bytes 4718600 | tf_op jit(solution)/shard_map/ppermute | solution.py:34
  3.9 7.4 %collective-permute-start = (f32[1,384]{1,0:T(1,128)S(1)}, f32[1,384]{1,0:T(1,128)S(1)}, u32[]{:S(2)}, u32[]{:S(2)}) collective-permute-start(f32[1,384]{1,0:T(1,128)S(1)} %fusion.1.mine_ref), channel_id=1, source_target_pairs={{0,8},{1,9},{2,10},{3,11},{4,12},{5,13},{6,14},{7,15},{8,0},{9,1},... | collective-permute-start | bytes 4616 | tf_op jit(solution)/shard_map/ppermute | solution.py:34
  13.4 15.6 %copy-start.6 = (bf16[2,64,256]{2,1,0:T(8,128)(2,1)}, bf16[2,64,256]{2,1,0:T(8,128)(2,1)S(1)}, u32[]{:S(2)}) copy-start(bf16[2,64,256]{2,1,0:T(8,128)(2,1)S(1)} %get-tuple-element.93.ya_ref) | copy-start | bytes 196612
  13.4 15.6 %copy-start.8 = (bf16[2,48,256]{2,1,0:T(8,128)(2,1)}, bf16[2,48,256]{2,1,0:T(8,128)(2,1)S(1)}, u32[]{:S(2)}) copy-start(bf16[2,48,256]{2,1,0:T(8,128)(2,1)S(1)} %get-tuple-element.127.refs_6_) | copy-start | bytes 147460
  13.4 15.6 %copy-start.10 = (bf16[2,32,256]{2,1,0:T(8,128)(2,1)}, bf16[2,32,256]{2,1,0:T(8,128)(2,1)S(1)}, u32[]{:S(2)}) copy-start(bf16[2,32,256]{2,1,0:T(8,128)(2,1)S(1)} %get-tuple-element.137.refs_7_) | copy-start | bytes 98308
  13.4 15.6 %copy-start.12 = (bf16[2,32,256]{2,1,0:T(8,128)(2,1)}, bf16[2,32,256]{2,1,0:T(8,128)(2,1)S(1)}, u32[]{:S(2)}) copy-start(bf16[2,32,256]{2,1,0:T(8,128)(2,1)S(1)} %get-tuple-element.138.refs_8_) | copy-start | bytes 98308
  13.4 15.6 %copy-start.14 = (bf16[2,32,256]{2,1,0:T(8,128)(2,1)}, bf16[2,32,256]{2,1,0:T(8,128)(2,1)S(1)}, u32[]{:S(2)}) copy-start(bf16[2,32,256]{2,1,0:T(8,128)(2,1)S(1)} %get-tuple-element.128.refs_7_) | copy-start | bytes 98308
  13.4 23.6 %copy-start.19 = (s32[1,16,128]{2,1,0:T(8,128)S(1)}, s32[1,16,128]{2,1,0:T(8,128)}, u32[]{:S(2)}) copy-start(s32[1,16,128]{2,1,0:T(8,128)} %param.10) | copy-start | bytes 24580
  13.4 26.7 %collective-permute-start.3 = (f32[16,80,256]{2,1,0:T(8,128)}, f32[16,80,256]{2,1,0:T(8,128)}, u32[]{:S(2)}, u32[]{:S(2)}) collective-permute-start(f32[16,80,256]{2,1,0:T(8,128)} %get-tuple-element.84), channel_id=1, source_target_pairs={{1,8},{3,10},{5,12},{7,14},{8,1},{10,3},{12,5},{14,7},{17,24},{19,... | collective-permute-start | bytes 3932168 | tf_op jit(solution)/shard_map/ppermute | solution.py:34
  30.1 27.0 %collective-permute-start.9 = (f32[15,96,256]{2,1,0:T(8,128)}, f32[15,96,256]{2,1,0:T(8,128)}, u32[]{:S(2)}, u32[]{:S(2)}) collective-permute-start(f32[15,96,256]{2,1,0:T(8,128)} %get-tuple-element.87), channel_id=1, source_target_pairs={{2,8},{3,9},{4,10},{5,11},{6,12},{7,13},{8,2},{9,3},{10,4},{11,5},... | collective-permute-start | bytes 4423688 | tf_op jit(solution)/shard_map/ppermute | solution.py:34
  37.0 18.1 %collective-permute-start.12 = (f32[16,80,256]{2,1,0:T(8,128)}, f32[16,80,256]{2,1,0:T(8,128)}, u32[]{:S(2)}, u32[]{:S(2)}) collective-permute-start(f32[16,80,256]{2,1,0:T(8,128)} %get-tuple-element.98), channel_id=1, source_target_pairs={{0,1},{1,9},{2,3},{3,11},{4,5},{5,13},{6,7},{7,15},{8,0},{9,8},{10... | collective-permute-start | bytes 3932168 | tf_op jit(solution)/shard_map/ppermute | solution.py:34
  37.1 2.6 %collective-permute-start.6 = (f32[1,16,128]{2,1,0:T(8,128)S(1)}, f32[1,16,128]{2,1,0:T(8,128)S(1)}, u32[]{:S(2)}, u32[]{:S(2)}) collective-permute-start(f32[1,16,128]{2,1,0:T(8,128)S(1)} %convert_element_type.16), channel_id=1, source_target_pairs={{0,8},{1,9},{2,10},{3,11},{4,12},{5,13},{6,14},{7,15},{8,0},{9,1},... | collective-permute-start | bytes 24584 | tf_op jit(solution)/shard_map/ppermute | solution.py:34
  38.4 4.7 %collective-permute-start.2 = (f32[1,3]{1,0:T(1,128)S(1)}, f32[1,3]{1,0:T(1,128)S(1)}, u32[]{:S(2)}, u32[]{:S(2)}) collective-permute-start(f32[1,3]{1,0:T(1,128)S(1)} %convert_element_type.14), channel_id=1, source_target_pairs={{0,8},{1,9},{2,10},{3,11},{4,12},{5,13},{6,14},{7,15},{8,0},{9,1},... | collective-permute-start | bytes 44 | tf_op jit(solution)/shard_map/ppermute | solution.py:34
  39.7 22.4 %collective-permute-start.8 = (f32[15,96,256]{2,1,0:T(8,128)}, f32[15,96,256]{2,1,0:T(8,128)S(1)}, u32[]{:S(2)}, u32[]{:S(2)}) collective-permute-start(f32[15,96,256]{2,1,0:T(8,128)} %copy-done.17), channel_id=1, source_target_pairs={{0,8},{1,9},{2,10},{3,11},{4,12},{5,13},{6,14},{7,15},{8,0},{9,1},... | collective-permute-start | bytes 4423688 | tf_op jit(solution)/shard_map/ppermute | solution.py:34
  40.1 15.0 %collective-permute-start.7 = (f32[2,16,128]{2,1,0:T(8,128)S(1)}, f32[2,16,128]{2,1,0:T(8,128)S(1)}, u32[]{:S(2)}, u32[]{:S(2)}) collective-permute-start(f32[2,16,128]{2,1,0:T(8,128)S(1)} %maximum_select_fusion), channel_id=1, source_target_pairs={{0,1},{1,0},{2,3},{3,2},{4,5},{5,4},{6,7},{7,6},{8,9},{9,8},{10,11... | collective-permute-start | bytes 49160 | tf_op jit(solution)/shard_map/ppermute | solution.py:34
  43.1 25.5 %collective-permute-start.4 = (f32[16,80,256]{2,1,0:T(8,128)S(1)}, f32[16,80,256]{2,1,0:T(8,128)S(1)}, u32[]{:S(2)}, u32[]{:S(2)}) collective-permute-start(f32[16,80,256]{2,1,0:T(8,128)S(1)} %broadcast_select_fusion.own_ref), channel_id=1, source_target_pairs={{2,8},{3,9},{4,10},{5,11},{6,12},{7,13},{8,2},{9,3},{10,4},{11,5},... | collective-permute-start | bytes 3932168 | tf_op jit(solution)/shard_map/ppermute | solution.py:34
  55.1 13.5 %collective-permute-start.5 = (f32[16,80,256]{2,1,0:T(8,128)S(1)}, f32[16,80,256]{2,1,0:T(8,128)S(1)}, u32[]{:S(2)}, u32[]{:S(2)}) collective-permute-start(f32[16,80,256]{2,1,0:T(8,128)S(1)} %broadcast_select_fusion.own_ref), channel_id=1, source_target_pairs={{0,8},{1,9},{2,10},{3,11},{4,12},{5,13},{6,14},{7,15},{8,0},{9,1},... | collective-permute-start | bytes 3932168 | tf_op jit(solution)/shard_map/ppermute | solution.py:34
  55.1 27.5 %collective-permute-start.13 = (f32[16,80,256]{2,1,0:T(8,128)}, f32[16,80,256]{2,1,0:T(8,128)S(1)}, u32[]{:S(2)}, u32[]{:S(2)}) collective-permute-start(f32[16,80,256]{2,1,0:T(8,128)} %collective-permute-done.12.own_ref), channel_id=1, source_target_pairs={{2,8},{3,9},{4,10},{5,11},{6,12},{7,13},{8,2},{9,3},{10,4},{11,5},... | collective-permute-start | bytes 3932168 | tf_op jit(solution)/shard_map/ppermute | solution.py:34
  57.2 25.5 %collective-permute-start.14 = (f32[16,80,256]{2,1,0:T(8,128)}, f32[16,80,256]{2,1,0:T(8,128)S(1)}, u32[]{:S(2)}, u32[]{:S(2)}) collective-permute-start(f32[16,80,256]{2,1,0:T(8,128)} %collective-permute-done.12.own_ref), channel_id=1, source_target_pairs={{0,8},{1,9},{2,10},{3,11},{4,12},{5,13},{6,14},{7,15},{8,0},{9,1},... | collective-permute-start | bytes 3932168 | tf_op jit(solution)/shard_map/ppermute | solution.py:34
  71.2 22.0 %collective-permute-start.10 = (f32[15,64,256]{2,1,0:T(8,128)S(1)}, f32[15,64,256]{2,1,0:T(8,128)S(1)}, u32[]{:S(2)}, u32[]{:S(2)}) collective-permute-start(f32[15,64,256]{2,1,0:T(8,128)S(1)} %get-tuple-element.94), channel_id=1, source_target_pairs={{2,8},{3,9},{4,10},{5,11},{6,12},{7,13},{8,2},{9,3},{10,4},{11,5},... | collective-permute-start | bytes 2949128 | tf_op jit(solution)/shard_map/ppermute | solution.py:34
  74.5 18.7 %collective-permute-start.11 = (f32[15,64,256]{2,1,0:T(8,128)S(1)}, f32[15,64,256]{2,1,0:T(8,128)S(1)}, u32[]{:S(2)}, u32[]{:S(2)}) collective-permute-start(f32[15,64,256]{2,1,0:T(8,128)S(1)} %get-tuple-element.95), channel_id=1, source_target_pairs={{0,8},{1,9},{2,10},{3,11},{4,12},{5,13},{6,14},{7,15},{8,0},{9,1},... | collective-permute-start | bytes 2949128 | tf_op jit(solution)/shard_map/ppermute | solution.py:34
  87.4 10.9 %collective-permute-start.18 = (f32[15,32,256]{2,1,0:T(8,128)S(1)}, f32[15,32,256]{2,1,0:T(8,128)S(1)}, u32[]{:S(2)}, u32[]{:S(2)}) collective-permute-start(f32[15,32,256]{2,1,0:T(8,128)S(1)} %get-tuple-element.107), channel_id=1, source_target_pairs={{2,8},{3,9},{4,10},{5,11},{6,12},{7,13},{8,2},{9,3},{10,4},{11,5},... | collective-permute-start | bytes 1474568 | tf_op jit(solution)/shard_map/ppermute | solution.py:34
  90.8 7.6 %collective-permute-start.19 = (f32[15,32,256]{2,1,0:T(8,128)S(1)}, f32[15,32,256]{2,1,0:T(8,128)S(1)}, u32[]{:S(2)}, u32[]{:S(2)}) collective-permute-start(f32[15,32,256]{2,1,0:T(8,128)S(1)} %get-tuple-element.108), channel_id=1, source_target_pairs={{0,8},{1,9},{2,10},{3,11},{4,12},{5,13},{6,14},{7,15},{8,0},{9,1},... | collective-permute-start | bytes 1474568 | tf_op jit(solution)/shard_map/ppermute | solution.py:34
  99.4 13.2 %collective-permute-start.20 = (f32[16,32,256]{2,1,0:T(8,128)S(1)}, f32[16,32,256]{2,1,0:T(8,128)S(1)}, u32[]{:S(2)}, u32[]{:S(2)}) collective-permute-start(f32[16,32,256]{2,1,0:T(8,128)S(1)} %log_factor.7.refs_0_), channel_id=1, source_target_pairs={{0,16},{1,17},{2,18},{3,19},{4,20},{5,21},{6,22},{7,23},{8,24},{9,... | collective-permute-start | bytes 1572872 | tf_op jit(solution)/shard_map/ppermute | solution.py:34
  100.7 10.6 %collective-permute-start.15 = (f32[15,32,256]{2,1,0:T(8,128)S(1)}, f32[15,32,256]{2,1,0:T(8,128)S(1)}, u32[]{:S(2)}, u32[]{:S(2)}) collective-permute-start(f32[15,32,256]{2,1,0:T(8,128)S(1)} %get-tuple-element.100), channel_id=1, source_target_pairs={{2,8},{3,9},{4,10},{5,11},{6,12},{7,13},{8,2},{9,3},{10,4},{11,5},... | collective-permute-start | bytes 1474568 | tf_op jit(solution)/shard_map/ppermute | solution.py:34
  104.6 6.6 %collective-permute-start.16 = (f32[15,32,256]{2,1,0:T(8,128)S(1)}, f32[15,32,256]{2,1,0:T(8,128)S(1)}, u32[]{:S(2)}, u32[]{:S(2)}) collective-permute-start(f32[15,32,256]{2,1,0:T(8,128)S(1)} %get-tuple-element.101), channel_id=1, source_target_pairs={{0,8},{1,9},{2,10},{3,11},{4,12},{5,13},{6,14},{7,15},{8,0},{9,1},... | collective-permute-start | bytes 1474568 | tf_op jit(solution)/shard_map/ppermute | solution.py:34
  112.3 13.4 %collective-permute-start.17 = (f32[16,32,256]{2,1,0:T(8,128)S(1)}, f32[16,32,256]{2,1,0:T(8,128)}, u32[]{:S(2)}, u32[]{:S(2)}) collective-permute-start(f32[16,32,256]{2,1,0:T(8,128)S(1)} %log_factor.6.refs_0_), channel_id=1, source_target_pairs={{0,16},{1,17},{2,18},{3,19},{4,20},{5,21},{6,22},{7,23},{8,24},{9,... | collective-permute-start | bytes 1572872 | tf_op jit(solution)/shard_map/ppermute | solution.py:34
  114.3 16.6 %collective-permute-start.24 = (f32[16,32,256]{2,1,0:T(8,128)S(1)}, f32[16,32,256]{2,1,0:T(8,128)S(1)}, u32[]{:S(2)}, u32[]{:S(2)}) collective-permute-start(f32[16,32,256]{2,1,0:T(8,128)S(1)} %get-tuple-element.115.refs_0_.before_ref), channel_id=1, source_target_pairs={{0,1},{1,0},{2,3},{3,2},{4,5},{5,4},{6,7},{7,6},{8,9},{9,8},{10,11... | collective-permute-start | bytes 1572872 | tf_op jit(solution)/shard_map/ppermute | solution.py:34
  116.5 11.6 %collective-permute-start.21 = (f32[15,32,256]{2,1,0:T(8,128)}, f32[15,32,256]{2,1,0:T(8,128)}, u32[]{:S(2)}, u32[]{:S(2)}) collective-permute-start(f32[15,32,256]{2,1,0:T(8,128)} %get-tuple-element.109), channel_id=1, source_target_pairs={{2,8},{3,9},{4,10},{5,11},{6,12},{7,13},{8,2},{9,3},{10,4},{11,5},... | collective-permute-start | bytes 1474568 | tf_op jit(solution)/shard_map/ppermute | solution.py:34
  127.0 8.5 %collective-permute-start.23 = (f32[15,32,256]{2,1,0:T(8,128)S(1)}, f32[15,32,256]{2,1,0:T(8,128)S(1)}, u32[]{:S(2)}, u32[]{:S(2)}) collective-permute-start(f32[15,32,256]{2,1,0:T(8,128)S(1)} %get-tuple-element.111), channel_id=1, source_target_pairs={{0,8},{1,9},{2,10},{3,11},{4,12},{5,13},{6,14},{7,15},{8,0},{9,1},... | collective-permute-start | bytes 1474568 | tf_op jit(solution)/shard_map/ppermute | solution.py:34
  128.1 6.2 %collective-permute-start.27 = (f32[15,32,256]{2,1,0:T(8,128)}, f32[15,32,256]{2,1,0:T(8,128)S(1)}, u32[]{:S(2)}, u32[]{:S(2)}) collective-permute-start(f32[15,32,256]{2,1,0:T(8,128)} %copy-done.18), channel_id=1, source_target_pairs={{0,8},{1,9},{2,10},{3,11},{4,12},{5,13},{6,14},{7,15},{8,0},{9,1},... | collective-permute-start | bytes 1474568 | tf_op jit(solution)/shard_map/ppermute | solution.py:34
  128.2 10.4 %collective-permute-start.22 = (f32[15,32,256]{2,1,0:T(8,128)S(1)}, f32[15,32,256]{2,1,0:T(8,128)S(1)}, u32[]{:S(2)}, u32[]{:S(2)}) collective-permute-start(f32[15,32,256]{2,1,0:T(8,128)S(1)} %get-tuple-element.110), channel_id=1, source_target_pairs={{2,8},{3,9},{4,10},{5,11},{6,12},{7,13},{8,2},{9,3},{10,4},{11,5},... | collective-permute-start | bytes 1474568 | tf_op jit(solution)/shard_map/ppermute | solution.py:34
  131.0 12.6 %collective-permute-start.25 = (f32[15,32,256]{2,1,0:T(8,128)S(1)}, f32[15,32,256]{2,1,0:T(8,128)S(1)}, u32[]{:S(2)}, u32[]{:S(2)}) collective-permute-start(f32[15,32,256]{2,1,0:T(8,128)S(1)} %get-tuple-element.144), channel_id=1, source_target_pairs={{2,8},{3,9},{4,10},{5,11},{6,12},{7,13},{8,2},{9,3},{10,4},{11,5},... | collective-permute-start | bytes 1474568 | tf_op jit(solution)/shard_map/ppermute | solution.py:34
  133.8 9.8 %collective-permute-start.26 = (f32[15,32,256]{2,1,0:T(8,128)S(1)}, f32[15,32,256]{2,1,0:T(8,128)S(1)}, u32[]{:S(2)}, u32[]{:S(2)}) collective-permute-start(f32[15,32,256]{2,1,0:T(8,128)S(1)} %get-tuple-element.143), channel_id=1, source_target_pairs={{0,8},{1,9},{2,10},{3,11},{4,12},{5,13},{6,14},{7,15},{8,0},{9,1},... | collective-permute-start | bytes 1474568 | tf_op jit(solution)/shard_map/ppermute | solution.py:34
  138.6 6.1 %copy-start.3 = (f32[16,80,256]{2,1,0:T(8,128)S(1)}, f32[16,80,256]{2,1,0:T(8,128)}, u32[]{:S(2)}) copy-start(f32[16,80,256]{2,1,0:T(8,128)} %copy-done.2) | copy-start | bytes 3932164
  150.0 15.8 %collective-permute-start.28 = (f32[2,15,32,256]{3,2,1,0:T(8,128)S(1)}, f32[2,15,32,256]{3,2,1,0:T(8,128)S(1)}, u32[]{:S(2)}, u32[]{:S(2)}) collective-permute-start(f32[2,15,32,256]{3,2,1,0:T(8,128)S(1)} %get-tuple-element.129), channel_id=1, source_target_pairs={{2,8},{3,9},{4,10},{5,11},{6,12},{7,13},{8,2},{9,3},{10,4},{11,5},... | collective-permute-start | bytes 2949128 | tf_op jit(solution)/shard_map/ppermute | solution.py:34
  152.7 13.1 %collective-permute-start.29 = (f32[2,15,32,256]{3,2,1,0:T(8,128)S(1)}, f32[2,15,32,256]{3,2,1,0:T(8,128)S(1)}, u32[]{:S(2)}, u32[]{:S(2)}) collective-permute-start(f32[2,15,32,256]{3,2,1,0:T(8,128)S(1)} %get-tuple-element.130), channel_id=1, source_target_pairs={{0,8},{1,9},{2,10},{3,11},{4,12},{5,13},{6,14},{7,15},{8,0},{9,1},... | collective-permute-start | bytes 2949128 | tf_op jit(solution)/shard_map/ppermute | solution.py:34
  158.0 18.3 %collective-permute-start.34 = (f32[2,15,32,256]{3,2,1,0:T(8,128)S(1)}, f32[2,15,32,256]{3,2,1,0:T(8,128)S(1)}, u32[]{:S(2)}, u32[]{:S(2)}) collective-permute-start(f32[2,15,32,256]{3,2,1,0:T(8,128)S(1)} %get-tuple-element.139), channel_id=1, source_target_pairs={{2,8},{3,9},{4,10},{5,11},{6,12},{7,13},{8,2},{9,3},{10,4},{11,5},... | collective-permute-start | bytes 2949128 | tf_op jit(solution)/shard_map/ppermute | solution.py:34
  161.0 15.3 %collective-permute-start.35 = (f32[2,15,32,256]{3,2,1,0:T(8,128)S(1)}, f32[2,15,32,256]{3,2,1,0:T(8,128)S(1)}, u32[]{:S(2)}, u32[]{:S(2)}) collective-permute-start(f32[2,15,32,256]{3,2,1,0:T(8,128)S(1)} %get-tuple-element.140), channel_id=1, source_target_pairs={{0,8},{1,9},{2,10},{3,11},{4,12},{5,13},{6,14},{7,15},{8,0},{9,1},... | collective-permute-start | bytes 2949128 | tf_op jit(solution)/shard_map/ppermute | solution.py:34
  167.5 15.2 %collective-permute-start.30 = (f32[16,32,256]{2,1,0:T(8,128)S(1)}, f32[16,32,256]{2,1,0:T(8,128)S(1)}, u32[]{:S(2)}, u32[]{:S(2)}) collective-permute-start(f32[16,32,256]{2,1,0:T(8,128)S(1)} %log_factor.8.refs_0_), channel_id=1, source_target_pairs={{0,16},{2,18},{4,20},{6,22},{9,25},{11,27},{13,29},{15,31},{16,0},... | collective-permute-start | bytes 1572872 | tf_op jit(solution)/shard_map/ppermute | solution.py:34
  168.2 17.0 %collective-permute-start.31 = (f32[16,32,256]{2,1,0:T(8,128)S(1)}, f32[16,32,256]{2,1,0:T(8,128)S(1)}, u32[]{:S(2)}, u32[]{:S(2)}) collective-permute-start(f32[16,32,256]{2,1,0:T(8,128)S(1)} %log_factor.8.refs_0_), channel_id=1, source_target_pairs={{1,24},{3,26},{5,28},{7,30},{8,17},{10,19},{12,21},{14,23},{17,8},... | collective-permute-start | bytes 1572872 | tf_op jit(solution)/shard_map/ppermute | solution.py:34
  172.2 16.4 %collective-permute-start.32 = (f32[16,32,256]{2,1,0:T(8,128)S(1)}, f32[16,32,256]{2,1,0:T(8,128)S(1)}, u32[]{:S(2)}, u32[]{:S(2)}) collective-permute-start(f32[16,32,256]{2,1,0:T(8,128)S(1)} %log_factor.8.refs_0_), channel_id=1, source_target_pairs={{1,8},{3,10},{5,12},{7,14},{8,1},{10,3},{12,5},{14,7},{17,24},{19,... | collective-permute-start | bytes 1572872 | tf_op jit(solution)/shard_map/ppermute | solution.py:34
  178.0 10.7 %collective-permute-start.36 = (f32[16,32,256]{2,1,0:T(8,128)S(1)}, f32[16,32,256]{2,1,0:T(8,128)S(1)}, u32[]{:S(2)}, u32[]{:S(2)}) collective-permute-start(f32[16,32,256]{2,1,0:T(8,128)S(1)} %log_factor.9.refs_0_), channel_id=1, source_target_pairs={{0,16},{2,18},{4,20},{6,22},{9,25},{11,27},{13,29},{15,31},{16,0},... | collective-permute-start | bytes 1572872 | tf_op jit(solution)/shard_map/ppermute | solution.py:34
  178.7 17.6 %collective-permute-start.37 = (f32[16,32,256]{2,1,0:T(8,128)S(1)}, f32[16,32,256]{2,1,0:T(8,128)S(1)}, u32[]{:S(2)}, u32[]{:S(2)}) collective-permute-start(f32[16,32,256]{2,1,0:T(8,128)S(1)} %log_factor.9.refs_0_), channel_id=1, source_target_pairs={{1,24},{3,26},{5,28},{7,30},{8,17},{10,19},{12,21},{14,23},{17,8},... | collective-permute-start | bytes 1572872 | tf_op jit(solution)/shard_map/ppermute | solution.py:34
  182.7 15.3 %collective-permute-start.38 = (f32[16,32,256]{2,1,0:T(8,128)S(1)}, f32[16,32,256]{2,1,0:T(8,128)S(1)}, u32[]{:S(2)}, u32[]{:S(2)}) collective-permute-start(f32[16,32,256]{2,1,0:T(8,128)S(1)} %log_factor.9.refs_0_), channel_id=1, source_target_pairs={{1,8},{3,10},{5,12},{7,14},{8,1},{10,3},{12,5},{14,7},{17,24},{19,... | collective-permute-start | bytes 1572872 | tf_op jit(solution)/shard_map/ppermute | solution.py:34
  188.7 9.5 %collective-permute-start.33 = (f32[16,32,256]{2,1,0:T(8,128)S(1)}, f32[16,32,256]{2,1,0:T(8,128)S(1)}, u32[]{:S(2)}, u32[]{:S(2)}) collective-permute-start(f32[16,32,256]{2,1,0:T(8,128)S(1)} %last_update.2.refs_0_), channel_id=1, source_target_pairs={{0,8},{1,9},{2,10},{3,11},{4,12},{5,13},{6,14},{7,15},{8,0},{9,1},... | collective-permute-start | bytes 1572872 | tf_op jit(solution)/shard_map/ppermute | solution.py:34
  198.1 2.0 collective-permute-start.39
  (14 other events, 44.0 us)

commit v14 on v12

--- a/solution.py
+++ b/solution.py
@@ -601,29 +601,30 @@
     window, crossed = make_windows(estimate, wide)
     crossed = send(crossed, across(0, lambda r: 1 - r, when=lambda c, r: c == r))
 
-    acquired = after(acquired, window)
-    first, second = shift_and_cut(offsets, acquired[0], near)
-
     mine = [jnp.pad(row, ((0, 0), (0, 128 - row.shape[1]))) for row in (kern_x, kern_y, kern_z)]
-    mine = jnp.concatenate(mine, axis=1)
+    mine = after(jnp.concatenate(mine, axis=1), window)
     other = send(mine, to_core_partner)
     taps = kern_x.shape[1], taps_y, kern_z.shape[1]
     tables = make_tables(mine, other, taps, planes, cells_y, cells_z, (own_rows, near, wide))
-    offset = offsets.astype(F32)
+    offset = after(offsets.astype(F32), tables.whole[0])
     other = send(offset, to_core_partner)
     shifts = jnp.where(straight, jnp.concatenate([offset, other]), jnp.concatenate([other, offset])).astype(jnp.int32)
 
     mask = view_mask.astype(F32)
     other = send(mask, to_core_partner)
     masks = jnp.where(core() == 0, jnp.concatenate([mask, other]), jnp.concatenate([other, mask]))
-    beyond = send(after(masks, tables.whole[0]), to_row_partner)
-    masks = jnp.where(straight, masks, beyond)
-
-    arrived = send(after(first, masks), lambda g, c, q, r: (g, r, q, c) if c != r else None)
+
+    acquired = after(after(acquired, tables.whole[0]), masks)
+    first, second = shift_and_cut(offsets, acquired[0], near)
+
+    arrived = send(after(first, tables.whole[0]), lambda g, c, q, r: (g, r, q, c) if c != r else None)
     current, distant, close = choose(after(window, first), crossed, radius)
     second = send(after(second, current), lambda g, c, q, r: (g, r, q, 1 - c))
     distant, close = neighbours(distant, close)
     first = jnp.where(straight, first, arrived)
+
+    masks = jnp.where(straight, masks, send(after(masks, current), to_row_partner))
+
     blocks = [(*neighbours(block, block), block) for block in (first, second)]
     wide_parts = blur_x(tables, (current, close), blur_x(tables, (distant,), (), planes), planes)
     blurred = [blur_yz([part], tables, order) for order, part in enumerate(wide_parts)]

time: 210 us -> 202 us (0.962)
  waiting for transfers between devices: 81.2 us -> 58.3 us
  starting transfers between devices: 59.9 us -> 71 us
  local copies, waits for them, and re-layouts: 9.33 us -> 12.4 us
    ppermute x40, waiting for transfers between devices: 81.2 us -> 58.3 us  [send(): return lax.ppermute(array, AXES, moves(move))]
    ppermute x40, starting transfers between devices: 59.9 us -> 71 us  [send(): return lax.ppermute(array, AXES, moves(move))]
    unnamed x40 -> x54, local copies, waits for them, and re-layouts: 8.08 us -> 12.3 us
  transfers between devices with their start and end apart: 40 -> 40, of which waited for: 17 -> 17; matrix products, arithmetic and copies ran while one was open for 2% -> 2% of each run, Pallas kernels for 21% -> 22%
where the time goes in v14:
time: 202 us; the launch traced here: 201 us
  starting transfers between devices  71 us (35%)
  waiting for transfers between devices  58.3 us (29%)
  Pallas kernels  54.5 us (27%)
  local copies, waits for them, and re-layouts  12.4 us (6%)
  other arithmetic  3.67 us (2%)
    ppermute x40, starting transfers between devices, send(): return lax.ppermute(array, AXES, moves(move))  71 us
    ppermute x40, waiting for transfers between devices, send(): return lax.ppermute(array, AXES, moves(move))  58.3 us
    pallas_call x8, Pallas kernels, blur_x(): call(kernel, (shape, shape), [VMEM] * len(operands), 'blur_x_far' if far...  15.1 us
    unnamed x54, local copies, waits for them, and re-layouts  12.3 us
    pallas_call x2, Pallas kernels, next_ratio(): return call(kernel, out_shape, [VMEM] * len(operands), 'ratio')(*operands)  9.35 us
    pallas_call x5, Pallas kernels, log_factor(): call(kernel, shape, [VMEM] * (3 + len(parts)), 'log_factor')  7.66 us
    pallas_call x2, Pallas kernels, first_ratio(): call(kernel, out_shape, in_specs, 'image_and_ratio', scratch)  6.22 us
    pallas_call x1, Pallas kernels, shift_and_cut(): call(shift_kernel, (shape, shape), [SMEM, VMEM], 'shift_recorded', scratch)  4.48 us
  transfers between devices with their start and end apart: 40, of which 17 were waited for; matrix products, arithmetic and copies ran while one was open for 2% of the time, Pallas kernels for 22%

profile of v14, /device:TPU:17, one launch (start us, length us, event | category | flops | bytes accessed | tf_op | source)
XLA Modules:
  0.0 200.8 jit_solution(5082229278358721509)
XLA Ops:
  0.0 1.6 copy-done.5
  5.4 3.0 %collective-permute-start.1 = (f32[1,16,128]{2,1,0:T(8,128)S(1)}, f32[1,16,128]{2,1,0:T(8,128)}, u32[]{:S(2)}, u32[]{:S(2)}) collective-permute-start(f32[1,16,128]{2,1,0:T(8,128)S(1)} %convert_element_type.14), channel_id=1, source_target_pairs={{0,8},{1,9},{2,10},{3,11},{4,12},{5,13},{6,14},{7,15},{8,0},{9,1},... | collective-permute-start | bytes 24584 | tf_op jit(solution)/shard_map/ppermute | solution.py:34
  9.6 2.0 %band_matrices.1 = (bf16[2,80,384]{2,1,0:T(8,128)(2,1)S(1)}, bf16[2,64,256]{2,1,0:T(8,128)(2,1)S(1)}, bf16[2,48,256]{2,1,0:T(8,128)(2,1)S(1)}, bf16[2,32,256]{2,...) custom-call(f32[1,384]{1,0:T(1,128)S(1)} %fusion.1.mine_ref, ...), custom_call_target="tpu_custom_call" | custom-call | tf_op jit(solution)/shard_map/band_matrices/pallas_call | solution.py:201
  15.5 1.6 copy-done.4
  17.1 4.5 %shift_recorded.1 = (f32[16,80,256]{2,1,0:T(8,128)}, f32[16,80,256]{2,1,0:T(8,128)}) custom-call(s32[1,3]{1,0:T(1,128)S(1)} %copy-done.20, f32[16,128,256]{2,1,0:T(8,128)S(1)} %bitcast.1), custom_call_target="tpu_custom_call" | custom-call | tf_op jit(solution)/shard_map/shift_recorded/pallas_call | solution.py:277
  21.6 1.9 collective-permute-start.4
  23.5 2.0 collective-permute-done.2.crossed_ref
  30.6 5.7 %collective-permute-start.9 = (f32[15,96,256]{2,1,0:T(8,128)}, f32[15,96,256]{2,1,0:T(8,128)}, u32[]{:S(2)}, u32[]{:S(2)}) collective-permute-start(f32[15,96,256]{2,1,0:T(8,128)} %get-tuple-element.91), channel_id=1, source_target_pairs={{2,8},{3,9},{4,10},{5,11},{6,12},{7,13},{8,2},{9,3},{10,4},{11,5},... | collective-permute-start | bytes 4423688 | tf_op jit(solution)/shard_map/ppermute | solution.py:34
  39.0 3.2 %collective-permute-done.4 = f32[16,80,256]{2,1,0:T(8,128)} collective-permute-done((f32[16,80,256]{2,1,0:T(8,128)}, f32[16,80,256]{2,1,0:T(8,128)}, u32[]{:S(2)}, u32[]{:S(2)}) %collective-permute-start.4) | collective-permute-done | bytes 1310752 | tf_op jit(solution)/shard_map/ppermute | solution.py:34
  43.6 8.2 %collective-permute-start.5 = (f32[16,80,256]{2,1,0:T(8,128)S(1)}, f32[16,80,256]{2,1,0:T(8,128)S(1)}, u32[]{:S(2)}, u32[]{:S(2)}) collective-permute-start(f32[16,80,256]{2,1,0:T(8,128)S(1)} %broadcast_select_fusion.own_ref), channel_id=1, source_target_pairs={{2,8},{3,9},{4,10},{5,11},{6,12},{7,13},{8,2},{9,3},{10,4},{11,5},... | collective-permute-start | bytes 3932168 | tf_op jit(solution)/shard_map/ppermute | solution.py:34
  51.8 3.5 %collective-permute-done.7 = f32[2,16,128]{2,1,0:T(8,128)S(1)} collective-permute-done((f32[2,16,128]{2,1,0:T(8,128)}, f32[2,16,128]{2,1,0:T(8,128)S(1)}, u32[]{:S(2)}, u32[]{:S(2)}) %collective-permute-start.7) | collective-permute-done | bytes 16416 | tf_op jit(solution)/shard_map/ppermute | solution.py:34
  55.4 3.6 %collective-permute-start.13 = (f32[16,80,256]{2,1,0:T(8,128)}, f32[16,80,256]{2,1,0:T(8,128)S(1)}, u32[]{:S(2)}, u32[]{:S(2)}) collective-permute-start(f32[16,80,256]{2,1,0:T(8,128)} %collective-permute-done.12.own_ref), channel_id=1, source_target_pairs={{2,8},{3,9},{4,10},{5,11},{6,12},{7,13},{8,2},{9,3},{10,4},{11,5},... | collective-permute-start | bytes 3932168 | tf_op jit(solution)/shard_map/ppermute | solution.py:34
  59.9 4.4 %blur_x_far.4 = (f32[16,96,256]{2,1,0:T(8,128)S(1)}, f32[16,96,256]{2,1,0:T(8,128)S(1)}) custom-call(bf16[2,256,384]{2,1,0:T(8,128)(2,1)S(1)} %get-tuple-element.78.hi_ref, bf16[2,256,384]{2,1,0:T(8,128)(2,1)S(1)} %get-tuple-element.79.lo_ref, f32[15,96,256]{2,1,0:T(8,128)} %collective-permute-done.9.refs_0_), custom_call_target="tpu_custom_call" | custom-call | tf_op jit(solution)/shard_map/blur_x_far/pallas_call | solution.py:325
  64.3 3.3 %blur_x_near.4 = (f32[16,96,256]{2,1,0:T(8,128)S(1)}, f32[16,96,256]{2,1,0:T(8,128)S(1)}) custom-call(bf16[2,256,384]{2,1,0:T(8,128)(2,1)S(1)} %get-tuple-element.78.hi_ref, bf16[2,256,384]{2,1,0:T(8,128)(2,1)S(1)} %get-tuple-element.79.lo_ref, f32[16,96,256]{2,1,0:T(8,128)S(1)} %get-tuple-element.86.refs_0_.before_ref, ...), custom_call_target="tpu_custom_call" | custom-call | tf_op jit(solution)/shard_map/blur_x_near/pallas_call | solution.py:325
  69.3 2.6 %image_and_ratio.2 = (f32[16,64,256]{2,1,0:T(8,128)S(1)}, f32[15,64,256]{2,1,0:T(8,128)S(1)}, f32[15,64,256]{2,1,0:T(8,128)S(1)}, f32[16,80,256]{2,1,0:T(8,128)S(1)}) custom-call(s32[2,3]{1,0:T(2,128)S(1)} %fusion.2.shift_ref, f32[16,80,256]{2,1,0:T(8,128)S(1)} %collective-permute-done.5.far_ref, f32[16,80,256]{2,1,0:T(8,128)S(1)} %collective-permute-done.6.near_ref, ...), custom_call_target="tpu_custom_call" | custom-call | tf_op jit(solution)/shard_map/image_and_ratio/pallas_call | solution.py:480
  71.8 2.0 collective-permute-start.10
  74.4 1.6 blur_yz.3.blurred_ref
  76.0 6.0 %collective-permute-done.13.far_ref = f32[16,80,256]{2,1,0:T(8,128)S(1)} collective-permute-done((f32[16,80,256]{2,1,0:T(8,128)}, f32[16,80,256]{2,1,0:T(8,128)S(1)}, u32[]{:S(2)}, u32[]{:S(2)}) %collective-permute-start.13) | collective-permute-done | bytes 1310752 | tf_op jit(solution)/shard_map/ppermute | solution.py:34
  82.0 3.7 %image_and_ratio.3 = (f32[16,64,256]{2,1,0:T(8,128)S(1)}, f32[15,32,256]{2,1,0:T(8,128)S(1)}, f32[15,32,256]{2,1,0:T(8,128)S(1)}, f32[15,32,256]{2,1,0:T(8,128)S...) custom-call(s32[2,3]{1,0:T(2,128)S(1)} %fusion.2.shift_ref, ...), custom_call_target="tpu_custom_call" | custom-call | tf_op jit(solution)/shard_map/image_and_ratio/pallas_call | solution.py:480
  86.7 3.3 %collective-permute-start.18 = (f32[15,32,256]{2,1,0:T(8,128)S(1)}, f32[15,32,256]{2,1,0:T(8,128)S(1)}, u32[]{:S(2)}, u32[]{:S(2)}) collective-permute-start(f32[15,32,256]{2,1,0:T(8,128)S(1)} %get-tuple-element.111), channel_id=1, source_target_pairs={{2,8},{3,9},{4,10},{5,11},{6,12},{7,13},{8,2},{9,3},{10,4},{11,5},... | collective-permute-start | bytes 1474568 | tf_op jit(solution)/shard_map/ppermute | solution.py:34
  90.1 2.4 %collective-permute-done.10.refs_0_ = f32[15,64,256]{2,1,0:T(8,128)S(1)} collective-permute-done((f32[15,64,256]{2,1,0:T(8,128)S(1)}, f32[15,64,256]{2,1,0:T(8,128)S(1)}, u32[]{:S(2)}, u32[]{:S(2)}) %collective-permute-start.10) | collective-permute-done | bytes 983072 | tf_op jit(solution)/shard_map/ppermute | solution.py:34
  92.5 2.1 %log_factor.5.before_ref = f32[16,64,256]{2,1,0:T(8,128)S(1)} custom-call(bf16[2,256,384]{2,1,0:T(8,128)(2,1)S(1)} %get-tuple-element.78.hi_ref, bf16[2,256,384]{2,1,0:T(8,128)(2,1)S(1)} %get-tuple-element.79.lo_ref, f32[16,96,256]{2,1,0:T(8,128)S(1)} %get-tuple-element.86.refs_0_.before_ref, f32[15,64,256]{2,1,0:T(8,128)S(1)} %collective-permute-done.10.refs_0_, ...), custom_call_target="tpu_custom_call" | custom-call | tf_op jit(solution)/shard_map/log_factor/pallas_call | solution.py:513
  94.6 3.0 %collective-permute-done.18.refs_0_ = f32[15,32,256]{2,1,0:T(8,128)S(1)} collective-permute-done((f32[15,32,256]{2,1,0:T(8,128)S(1)}, f32[15,32,256]{2,1,0:T(8,128)S(1)}, u32[]{:S(2)}, u32[]{:S(2)}) %collective-permute-start.18) | collective-permute-done | bytes 491552 | tf_op jit(solution)/shard_map/ppermute | solution.py:34
  100.0 3.9 %collective-permute-start.15 = (f32[15,32,256]{2,1,0:T(8,128)S(1)}, f32[15,32,256]{2,1,0:T(8,128)S(1)}, u32[]{:S(2)}, u32[]{:S(2)}) collective-permute-start(f32[15,32,256]{2,1,0:T(8,128)S(1)} %get-tuple-element.104), channel_id=1, source_target_pairs={{2,8},{3,9},{4,10},{5,11},{6,12},{7,13},{8,2},{9,3},{10,4},{11,5},... | collective-permute-start | bytes 1474568 | tf_op jit(solution)/shard_map/ppermute | solution.py:34
  104.0 6.5 %collective-permute-done.15.refs_0_ = f32[15,32,256]{2,1,0:T(8,128)S(1)} collective-permute-done((f32[15,32,256]{2,1,0:T(8,128)S(1)}, f32[15,32,256]{2,1,0:T(8,128)S(1)}, u32[]{:S(2)}, u32[]{:S(2)}) %collective-permute-start.15) | collective-permute-done | bytes 491552 | tf_op jit(solution)/shard_map/ppermute | solution.py:34
  113.6 2.1 %collective-permute-start.24 = (f32[16,32,256]{2,1,0:T(8,128)S(1)}, f32[16,32,256]{2,1,0:T(8,128)S(1)}, u32[]{:S(2)}, u32[]{:S(2)}) collective-permute-start(f32[16,32,256]{2,1,0:T(8,128)S(1)} %get-tuple-element.119.refs_0_.before_ref), channel_id=1, source_target_pairs={{0,1},{1,0},{2,3},{3,2},{4,5},{5,4},{6,7},{7,6},{8,9},{9,8},{10,11... | collective-permute-start | bytes 1572872 | tf_op jit(solution)/shard_map/ppermute | solution.py:34
  115.7 3.9 %collective-permute-start.21 = (f32[15,32,256]{2,1,0:T(8,128)}, f32[15,32,256]{2,1,0:T(8,128)}, u32[]{:S(2)}, u32[]{:S(2)}) collective-permute-start(f32[15,32,256]{2,1,0:T(8,128)} %get-tuple-element.113), channel_id=1, source_target_pairs={{2,8},{3,9},{4,10},{5,11},{6,12},{7,13},{8,2},{9,3},{10,4},{11,5},... | collective-permute-start | bytes 1474568 | tf_op jit(solution)/shard_map/ppermute | solution.py:34
  119.7 5.4 %collective-permute-done.17.refs_1_ = f32[16,32,256]{2,1,0:T(8,128)} collective-permute-done((f32[16,32,256]{2,1,0:T(8,128)S(1)}, f32[16,32,256]{2,1,0:T(8,128)}, u32[]{:S(2)}, u32[]{:S(2)}) %collective-permute-start.17) | collective-permute-done | bytes 524320 | tf_op jit(solution)/shard_map/ppermute | solution.py:34
  127.5 2.6 %collective-permute-start.22 = (f32[15,32,256]{2,1,0:T(8,128)S(1)}, f32[15,32,256]{2,1,0:T(8,128)S(1)}, u32[]{:S(2)}, u32[]{:S(2)}) collective-permute-start(f32[15,32,256]{2,1,0:T(8,128)S(1)} %get-tuple-element.114), channel_id=1, source_target_pairs={{2,8},{3,9},{4,10},{5,11},{6,12},{7,13},{8,2},{9,3},{10,4},{11,5},... | collective-permute-start | bytes 1474568 | tf_op jit(solution)/shard_map/ppermute | solution.py:34
  130.2 2.9 %collective-permute-start.25 = (f32[15,32,256]{2,1,0:T(8,128)S(1)}, f32[15,32,256]{2,1,0:T(8,128)S(1)}, u32[]{:S(2)}, u32[]{:S(2)}) collective-permute-start(f32[15,32,256]{2,1,0:T(8,128)S(1)} %get-tuple-element.148), channel_id=1, source_target_pairs={{2,8},{3,9},{4,10},{5,11},{6,12},{7,13},{8,2},{9,3},{10,4},{11,5},... | collective-permute-start | bytes 1474568 | tf_op jit(solution)/shard_map/ppermute | solution.py:34
  135.8 2.1 %blur_x_far.6 = (f32[16,32,256]{2,1,0:T(8,128)S(1)}, f32[16,32,256]{2,1,0:T(8,128)S(1)}) custom-call(bf16[2,256,384]{2,1,0:T(8,128)(2,1)S(1)} %get-tuple-element.78.hi_ref, bf16[2,256,384]{2,1,0:T(8,128)(2,1)S(1)} %get-tuple-element.79.lo_ref, f32[15,32,256]{2,1,0:T(8,128)} %collective-permute-done.21.refs_0_, ...), custom_call_target="tpu_custom_call" | custom-call | tf_op jit(solution)/shard_map/blur_x_far/pallas_call | solution.py:325
  139.0 3.9 %collective-permute-done.25.refs_0_ = f32[15,32,256]{2,1,0:T(8,128)S(1)} collective-permute-done((f32[15,32,256]{2,1,0:T(8,128)S(1)}, f32[15,32,256]{2,1,0:T(8,128)S(1)}, u32[]{:S(2)}, u32[]{:S(2)}) %collective-permute-start.25) | collective-permute-done | bytes 491552 | tf_op jit(solution)/shard_map/ppermute | solution.py:34
  144.1 5.2 %ratio.2 = (f32[16,32,256]{2,1,0:T(8,128)S(1)}, f32[16,32,256]{2,1,0:T(8,128)S(1)}, f32[2,15,32,256]{3,2,1,0:T(8,128)S(1)}, f32[2,15,32,256]{3,2,1,0:T(8,128)S(1)}, f32[2,16,32,256]{3,2,1,0:T(8,128)S(1)}) custom-call(f32[16,80,256]{2,1,0:T(8,128)S(1)} %copy-done.1, f32[16,80,256]{2,1,0:T(8,128)S(1)} %copy-done.3, ...), custom_call_target="tpu_custom_call" | custom-call | tf_op jit(solution)/shard_map/ratio/pallas_call | solution.py:468
  149.2 2.6 %collective-permute-start.28 = (f32[2,15,32,256]{3,2,1,0:T(8,128)S(1)}, f32[2,15,32,256]{3,2,1,0:T(8,128)S(1)}, u32[]{:S(2)}, u32[]{:S(2)}) collective-permute-start(f32[2,15,32,256]{3,2,1,0:T(8,128)S(1)} %get-tuple-element.133), channel_id=1, source_target_pairs={{2,8},{3,9},{4,10},{5,11},{6,12},{7,13},{8,2},{9,3},{10,4},{11,5},... | collective-permute-start | bytes 2949128 | tf_op jit(solution)/shard_map/ppermute | solution.py:34
  153.0 4.2 %ratio.3 = (f32[16,32,256]{2,1,0:T(8,128)S(1)}, f32[16,32,256]{2,1,0:T(8,128)S(1)}, f32[2,15,32,256]{3,2,1,0:T(8,128)S(1)}, f32[2,15,32,256]{3,2,1,0:T(8,128)S(1)}) custom-call(f32[16,80,256]{2,1,0:T(8,128)S(1)} %copy-done.1, f32[16,80,256]{2,1,0:T(8,128)S(1)} %copy-done.3, f32[16,32,256]{2,1,0:T(8,128)S(1)} %get-tuple-element.126.refs_3_.refs_2_, ...), custom_call_target="tpu_custom_call" | custom-call | tf_op jit(solution)/shard_map/ratio/pallas_call | solution.py:468
  157.2 3.1 %collective-permute-start.34 = (f32[2,15,32,256]{3,2,1,0:T(8,128)S(1)}, f32[2,15,32,256]{3,2,1,0:T(8,128)S(1)}, u32[]{:S(2)}, u32[]{:S(2)}) collective-permute-start(f32[2,15,32,256]{3,2,1,0:T(8,128)S(1)} %get-tuple-element.143), channel_id=1, source_target_pairs={{2,8},{3,9},{4,10},{5,11},{6,12},{7,13},{8,2},{9,3},{10,4},{11,5},... | collective-permute-start | bytes 2949128 | tf_op jit(solution)/shard_map/ppermute | solution.py:34
  160.6 4.4 %collective-permute-done.28.refs_0_.refs_3_ = f32[2,15,32,256]{3,2,1,0:T(8,128)S(1)} collective-permute-done((f32[2,15,32,256]{3,2,1,0:T(8,128)S(1)}, f32[2,15,32,256]{3,2,1,0:T(8,128)S(1)}, u32[]{:S(2)}, u32[]{:S(2)}) %collective-permute-start.28) | collective-permute-done | bytes 983072 | tf_op jit(solution)/shard_map/ppermute | solution.py:34
  165.1 1.7 log_factor.8.refs_0_
  167.5 3.9 %collective-permute-start.31 = (f32[16,32,256]{2,1,0:T(8,128)S(1)}, f32[16,32,256]{2,1,0:T(8,128)S(1)}, u32[]{:S(2)}, u32[]{:S(2)}) collective-permute-start(f32[16,32,256]{2,1,0:T(8,128)S(1)} %log_factor.8.refs_0_), channel_id=1, source_target_pairs={{1,24},{3,26},{5,28},{7,30},{8,17},{10,19},{12,21},{14,23},{17,8},... | collective-permute-start | bytes 1572872 | tf_op jit(solution)/shard_map/ppermute | solution.py:34
  171.3 2.2 %collective-permute-start.32 = (f32[16,32,256]{2,1,0:T(8,128)S(1)}, f32[16,32,256]{2,1,0:T(8,128)S(1)}, u32[]{:S(2)}, u32[]{:S(2)}) collective-permute-start(f32[16,32,256]{2,1,0:T(8,128)S(1)} %log_factor.8.refs_0_), channel_id=1, source_target_pairs={{1,8},{3,10},{5,12},{7,14},{8,1},{10,3},{12,5},{14,7},{17,24},{19,... | collective-permute-start | bytes 1572872 | tf_op jit(solution)/shard_map/ppermute | solution.py:34
  173.5 2.1 %collective-permute-done.34.refs_0_.refs_3_ = f32[2,15,32,256]{3,2,1,0:T(8,128)S(1)} collective-permute-done((f32[2,15,32,256]{3,2,1,0:T(8,128)S(1)}, f32[2,15,32,256]{3,2,1,0:T(8,128)S(1)}, u32[]{:S(2)}, u32[]{:S(2)}) %collective-permute-start.34) | collective-permute-done | bytes 983072 | tf_op jit(solution)/shard_map/ppermute | solution.py:34
  175.6 1.7 log_factor.9.refs_0_
  178.0 3.9 %collective-permute-start.37 = (f32[16,32,256]{2,1,0:T(8,128)S(1)}, f32[16,32,256]{2,1,0:T(8,128)S(1)}, u32[]{:S(2)}, u32[]{:S(2)}) collective-permute-start(f32[16,32,256]{2,1,0:T(8,128)S(1)} %log_factor.9.refs_0_), channel_id=1, source_target_pairs={{1,24},{3,26},{5,28},{7,30},{8,17},{10,19},{12,21},{14,23},{17,8},... | collective-permute-start | bytes 1572872 | tf_op jit(solution)/shard_map/ppermute | solution.py:34
  181.9 2.2 %collective-permute-start.38 = (f32[16,32,256]{2,1,0:T(8,128)S(1)}, f32[16,32,256]{2,1,0:T(8,128)S(1)}, u32[]{:S(2)}, u32[]{:S(2)}) collective-permute-start(f32[16,32,256]{2,1,0:T(8,128)S(1)} %log_factor.9.refs_0_), channel_id=1, source_target_pairs={{1,8},{3,10},{5,12},{7,14},{8,1},{10,3},{12,5},{14,7},{17,24},{19,... | collective-permute-start | bytes 1572872 | tf_op jit(solution)/shard_map/ppermute | solution.py:34
  184.4 3.3 %collective-permute-done.32.refs_3_ = f32[16,32,256]{2,1,0:T(8,128)S(1)} collective-permute-done((f32[16,32,256]{2,1,0:T(8,128)S(1)}, f32[16,32,256]{2,1,0:T(8,128)S(1)}, u32[]{:S(2)}, u32[]{:S(2)}) %collective-permute-start.32) | collective-permute-done | bytes 524320 | tf_op jit(solution)/shard_map/ppermute | solution.py:34
  188.0 7.5 %collective-permute-done.37.refs_2_ = f32[16,32,256]{2,1,0:T(8,128)S(1)} collective-permute-done((f32[16,32,256]{2,1,0:T(8,128)S(1)}, f32[16,32,256]{2,1,0:T(8,128)S(1)}, u32[]{:S(2)}, u32[]{:S(2)}) %collective-permute-start.37) | collective-permute-done | bytes 524320 | tf_op jit(solution)/shard_map/ppermute | solution.py:34
  195.5 1.7 collective-permute-done.38.refs_3_
  197.4 1.9 collective-permute-done.39.refs_3_
  (122 shorter events, 40.0 us)
Async XLA Ops:
  1.6 6.8 %copy-start.24 = (f32[1,61]{1,0:T(1,128)S(1)}, f32[1,61]{1,0:T(1,128)}, u32[]{:S(2)}) copy-start(f32[1,61]{1,0:T(1,128)} %param.13) | copy-start | bytes 736
  1.6 6.8 %copy-start.25 = (f32[1,31]{1,0:T(1,128)S(1)}, f32[1,31]{1,0:T(1,128)}, u32[]{:S(2)}) copy-start(f32[1,31]{1,0:T(1,128)} %param.12) | copy-start | bytes 376
  1.6 6.8 %copy-start.26 = (f32[1,31]{1,0:T(1,128)S(1)}, f32[1,31]{1,0:T(1,128)}, u32[]{:S(2)}) copy-start(f32[1,31]{1,0:T(1,128)} %param.11) | copy-start | bytes 376
  1.6 13.9 %copy-start.20 = (s32[1,3]{1,0:T(1,128)S(1)}, s32[1,3]{1,0:T(1,128)}, u32[]{:S(2)}) copy-start(s32[1,3]{1,0:T(1,128)} %offsets_ref.1) | copy-start | bytes 40
  4.1 21.4 %collective-permute-start.2 = (f32[16,96,256]{2,1,0:T(8,128)}, f32[16,96,256]{2,1,0:T(8,128)S(1)}, u32[]{:S(2)}, u32[]{:S(2)}) collective-permute-start(f32[16,96,256]{2,1,0:T(8,128)} %get-tuple-element.85), channel_id=1, source_target_pairs={{0,1},{2,3},{4,5},{6,7},{9,8},{11,10},{13,12},{15,14},{16,17},{18,... | collective-permute-start | bytes 4718600 | tf_op jit(solution)/shard_map/ppermute | solution.py:34
  5.4 8.7 %collective-permute-start.1 = (f32[1,16,128]{2,1,0:T(8,128)S(1)}, f32[1,16,128]{2,1,0:T(8,128)}, u32[]{:S(2)}, u32[]{:S(2)}) collective-permute-start(f32[1,16,128]{2,1,0:T(8,128)S(1)} %convert_element_type.14), channel_id=1, source_target_pairs={{0,8},{1,9},{2,10},{3,11},{4,12},{5,13},{6,14},{7,15},{8,0},{9,1},... | collective-permute-start | bytes 24584 | tf_op jit(solution)/shard_map/ppermute | solution.py:34
  8.4 1.2 collective-permute-start
  17.1 9.5 %copy-start.7 = (f32[16,96,256]{2,1,0:T(8,128)S(1)}, f32[16,96,256]{2,1,0:T(8,128)}, u32[]{:S(2)}) copy-start(f32[16,96,256]{2,1,0:T(8,128)} %copy-done.6) | copy-start | bytes 4718596
  21.6 20.6 %collective-permute-start.4 = (f32[16,80,256]{2,1,0:T(8,128)}, f32[16,80,256]{2,1,0:T(8,128)}, u32[]{:S(2)}, u32[]{:S(2)}) collective-permute-start(f32[16,80,256]{2,1,0:T(8,128)} %get-tuple-element.88), channel_id=1, source_target_pairs={{1,8},{3,10},{5,12},{7,14},{8,1},{10,3},{12,5},{14,7},{17,24},{19,... | collective-permute-start | bytes 3932168 | tf_op jit(solution)/shard_map/ppermute | solution.py:34
  30.6 28.4 %collective-permute-start.9 = (f32[15,96,256]{2,1,0:T(8,128)}, f32[15,96,256]{2,1,0:T(8,128)}, u32[]{:S(2)}, u32[]{:S(2)}) collective-permute-start(f32[15,96,256]{2,1,0:T(8,128)} %get-tuple-element.91), channel_id=1, source_target_pairs={{2,8},{3,9},{4,10},{5,11},{6,12},{7,13},{8,2},{9,3},{10,4},{11,5},... | collective-permute-start | bytes 4423688 | tf_op jit(solution)/shard_map/ppermute | solution.py:34
  36.3 19.1 %collective-permute-start.12 = (f32[16,80,256]{2,1,0:T(8,128)}, f32[16,80,256]{2,1,0:T(8,128)}, u32[]{:S(2)}, u32[]{:S(2)}) collective-permute-start(f32[16,80,256]{2,1,0:T(8,128)} %get-tuple-element.102), channel_id=1, source_target_pairs={{0,1},{1,9},{2,3},{3,11},{4,5},{5,13},{6,7},{7,15},{8,0},{9,8},{10... | collective-permute-start | bytes 3932168 | tf_op jit(solution)/shard_map/ppermute | solution.py:34
  36.4 7.2 %collective-permute-start.3 = (f32[1,3]{1,0:T(1,128)S(1)}, f32[1,3]{1,0:T(1,128)S(1)}, u32[]{:S(2)}, u32[]{:S(2)}) collective-permute-start(f32[1,3]{1,0:T(1,128)S(1)} %convert_element_type.15), channel_id=1, source_target_pairs={{0,8},{1,9},{2,10},{3,11},{4,12},{5,13},{6,14},{7,15},{8,0},{9,1},... | collective-permute-start | bytes 44 | tf_op jit(solution)/shard_map/ppermute | solution.py:34
  37.6 17.8 %collective-permute-start.7 = (f32[2,16,128]{2,1,0:T(8,128)}, f32[2,16,128]{2,1,0:T(8,128)S(1)}, u32[]{:S(2)}, u32[]{:S(2)}) collective-permute-start(f32[2,16,128]{2,1,0:T(8,128)} %maximum_select_fusion), channel_id=1, source_target_pairs={{0,1},{1,0},{2,3},{3,2},{4,5},{5,4},{6,7},{7,6},{8,9},{9,8},{10,11... | collective-permute-start | bytes 49160 | tf_op jit(solution)/shard_map/ppermute | solution.py:34
  42.1 22.2 %collective-permute-start.8 = (f32[15,96,256]{2,1,0:T(8,128)}, f32[15,96,256]{2,1,0:T(8,128)S(1)}, u32[]{:S(2)}, u32[]{:S(2)}) collective-permute-start(f32[15,96,256]{2,1,0:T(8,128)} %copy-done.21), channel_id=1, source_target_pairs={{0,8},{1,9},{2,10},{3,11},{4,12},{5,13},{6,14},{7,15},{8,0},{9,1},... | collective-permute-start | bytes 4423688 | tf_op jit(solution)/shard_map/ppermute | solution.py:34
  43.6 25.6 %collective-permute-start.5 = (f32[16,80,256]{2,1,0:T(8,128)S(1)}, f32[16,80,256]{2,1,0:T(8,128)S(1)}, u32[]{:S(2)}, u32[]{:S(2)}) collective-permute-start(f32[16,80,256]{2,1,0:T(8,128)S(1)} %broadcast_select_fusion.own_ref), channel_id=1, source_target_pairs={{2,8},{3,9},{4,10},{5,11},{6,12},{7,13},{8,2},{9,3},{10,4},{11,5},... | collective-permute-start | bytes 3932168 | tf_op jit(solution)/shard_map/ppermute | solution.py:34
  55.4 13.9 %collective-permute-start.6 = (f32[16,80,256]{2,1,0:T(8,128)S(1)}, f32[16,80,256]{2,1,0:T(8,128)S(1)}, u32[]{:S(2)}, u32[]{:S(2)}) collective-permute-start(f32[16,80,256]{2,1,0:T(8,128)S(1)} %broadcast_select_fusion.own_ref), channel_id=1, source_target_pairs={{0,8},{1,9},{2,10},{3,11},{4,12},{5,13},{6,14},{7,15},{8,0},{9,1},... | collective-permute-start | bytes 3932168 | tf_op jit(solution)/shard_map/ppermute | solution.py:34
  55.4 26.6 %collective-permute-start.13 = (f32[16,80,256]{2,1,0:T(8,128)}, f32[16,80,256]{2,1,0:T(8,128)S(1)}, u32[]{:S(2)}, u32[]{:S(2)}) collective-permute-start(f32[16,80,256]{2,1,0:T(8,128)} %collective-permute-done.12.own_ref), channel_id=1, source_target_pairs={{2,8},{3,9},{4,10},{5,11},{6,12},{7,13},{8,2},{9,3},{10,4},{11,5},... | collective-permute-start | bytes 3932168 | tf_op jit(solution)/shard_map/ppermute | solution.py:34
  59.0 23.0 %collective-permute-start.14 = (f32[16,80,256]{2,1,0:T(8,128)}, f32[16,80,256]{2,1,0:T(8,128)S(1)}, u32[]{:S(2)}, u32[]{:S(2)}) collective-permute-start(f32[16,80,256]{2,1,0:T(8,128)} %collective-permute-done.12.own_ref), channel_id=1, source_target_pairs={{0,8},{1,9},{2,10},{3,11},{4,12},{5,13},{6,14},{7,15},{8,0},{9,1},... | collective-permute-start | bytes 3932168 | tf_op jit(solution)/shard_map/ppermute | solution.py:34
  71.8 20.6 %collective-permute-start.10 = (f32[15,64,256]{2,1,0:T(8,128)S(1)}, f32[15,64,256]{2,1,0:T(8,128)S(1)}, u32[]{:S(2)}, u32[]{:S(2)}) collective-permute-start(f32[15,64,256]{2,1,0:T(8,128)S(1)} %get-tuple-element.98), channel_id=1, source_target_pairs={{2,8},{3,9},{4,10},{5,11},{6,12},{7,13},{8,2},{9,3},{10,4},{11,5},... | collective-permute-start | bytes 2949128 | tf_op jit(solution)/shard_map/ppermute | solution.py:34
  73.8 18.7 %collective-permute-start.11 = (f32[15,64,256]{2,1,0:T(8,128)S(1)}, f32[15,64,256]{2,1,0:T(8,128)S(1)}, u32[]{:S(2)}, u32[]{:S(2)}) collective-permute-start(f32[15,64,256]{2,1,0:T(8,128)S(1)} %get-tuple-element.99), channel_id=1, source_target_pairs={{0,8},{1,9},{2,10},{3,11},{4,12},{5,13},{6,14},{7,15},{8,0},{9,1},... | collective-permute-start | bytes 2949128 | tf_op jit(solution)/shard_map/ppermute | solution.py:34
  86.7 10.9 %collective-permute-start.18 = (f32[15,32,256]{2,1,0:T(8,128)S(1)}, f32[15,32,256]{2,1,0:T(8,128)S(1)}, u32[]{:S(2)}, u32[]{:S(2)}) collective-permute-start(f32[15,32,256]{2,1,0:T(8,128)S(1)} %get-tuple-element.111), channel_id=1, source_target_pairs={{2,8},{3,9},{4,10},{5,11},{6,12},{7,13},{8,2},{9,3},{10,4},{11,5},... | collective-permute-start | bytes 1474568 | tf_op jit(solution)/shard_map/ppermute | solution.py:34
  90.0 7.6 %collective-permute-start.19 = (f32[15,32,256]{2,1,0:T(8,128)S(1)}, f32[15,32,256]{2,1,0:T(8,128)S(1)}, u32[]{:S(2)}, u32[]{:S(2)}) collective-permute-start(f32[15,32,256]{2,1,0:T(8,128)S(1)} %get-tuple-element.112), channel_id=1, source_target_pairs={{0,8},{1,9},{2,10},{3,11},{4,12},{5,13},{6,14},{7,15},{8,0},{9,1},... | collective-permute-start | bytes 1474568 | tf_op jit(solution)/shard_map/ppermute | solution.py:34
  98.7 13.2 %collective-permute-start.20 = (f32[16,32,256]{2,1,0:T(8,128)S(1)}, f32[16,32,256]{2,1,0:T(8,128)S(1)}, u32[]{:S(2)}, u32[]{:S(2)}) collective-permute-start(f32[16,32,256]{2,1,0:T(8,128)S(1)} %log_factor.7.refs_0_), channel_id=1, source_target_pairs={{0,16},{1,17},{2,18},{3,19},{4,20},{5,21},{6,22},{7,23},{8,24},{9,... | collective-permute-start | bytes 1572872 | tf_op jit(solution)/shard_map/ppermute | solution.py:34
  100.0 10.6 %collective-permute-start.15 = (f32[15,32,256]{2,1,0:T(8,128)S(1)}, f32[15,32,256]{2,1,0:T(8,128)S(1)}, u32[]{:S(2)}, u32[]{:S(2)}) collective-permute-start(f32[15,32,256]{2,1,0:T(8,128)S(1)} %get-tuple-element.104), channel_id=1, source_target_pairs={{2,8},{3,9},{4,10},{5,11},{6,12},{7,13},{8,2},{9,3},{10,4},{11,5},... | collective-permute-start | bytes 1474568 | tf_op jit(solution)/shard_map/ppermute | solution.py:34
  103.9 6.6 %collective-permute-start.16 = (f32[15,32,256]{2,1,0:T(8,128)S(1)}, f32[15,32,256]{2,1,0:T(8,128)S(1)}, u32[]{:S(2)}, u32[]{:S(2)}) collective-permute-start(f32[15,32,256]{2,1,0:T(8,128)S(1)} %get-tuple-element.105), channel_id=1, source_target_pairs={{0,8},{1,9},{2,10},{3,11},{4,12},{5,13},{6,14},{7,15},{8,0},{9,1},... | collective-permute-start | bytes 1474568 | tf_op jit(solution)/shard_map/ppermute | solution.py:34
  111.6 13.4 %collective-permute-start.17 = (f32[16,32,256]{2,1,0:T(8,128)S(1)}, f32[16,32,256]{2,1,0:T(8,128)}, u32[]{:S(2)}, u32[]{:S(2)}) collective-permute-start(f32[16,32,256]{2,1,0:T(8,128)S(1)} %log_factor.6.refs_0_), channel_id=1, source_target_pairs={{0,16},{1,17},{2,18},{3,19},{4,20},{5,21},{6,22},{7,23},{8,24},{9,... | collective-permute-start | bytes 1572872 | tf_op jit(solution)/shard_map/ppermute | solution.py:34
  113.6 16.5 %collective-permute-start.24 = (f32[16,32,256]{2,1,0:T(8,128)S(1)}, f32[16,32,256]{2,1,0:T(8,128)S(1)}, u32[]{:S(2)}, u32[]{:S(2)}) collective-permute-start(f32[16,32,256]{2,1,0:T(8,128)S(1)} %get-tuple-element.119.refs_0_.before_ref), channel_id=1, source_target_pairs={{0,1},{1,0},{2,3},{3,2},{4,5},{5,4},{6,7},{7,6},{8,9},{9,8},{10,11... | collective-permute-start | bytes 1572872 | tf_op jit(solution)/shard_map/ppermute | solution.py:34
  115.7 11.7 %collective-permute-start.21 = (f32[15,32,256]{2,1,0:T(8,128)}, f32[15,32,256]{2,1,0:T(8,128)}, u32[]{:S(2)}, u32[]{:S(2)}) collective-permute-start(f32[15,32,256]{2,1,0:T(8,128)} %get-tuple-element.113), channel_id=1, source_target_pairs={{2,8},{3,9},{4,10},{5,11},{6,12},{7,13},{8,2},{9,3},{10,4},{11,5},... | collective-permute-start | bytes 1474568 | tf_op jit(solution)/shard_map/ppermute | solution.py:34
  126.3 8.5 %collective-permute-start.23 = (f32[15,32,256]{2,1,0:T(8,128)S(1)}, f32[15,32,256]{2,1,0:T(8,128)S(1)}, u32[]{:S(2)}, u32[]{:S(2)}) collective-permute-start(f32[15,32,256]{2,1,0:T(8,128)S(1)} %get-tuple-element.115), channel_id=1, source_target_pairs={{0,8},{1,9},{2,10},{3,11},{4,12},{5,13},{6,14},{7,15},{8,0},{9,1},... | collective-permute-start | bytes 1474568 | tf_op jit(solution)/shard_map/ppermute | solution.py:34
  127.4 6.2 %collective-permute-start.27 = (f32[15,32,256]{2,1,0:T(8,128)}, f32[15,32,256]{2,1,0:T(8,128)S(1)}, u32[]{:S(2)}, u32[]{:S(2)}) collective-permute-start(f32[15,32,256]{2,1,0:T(8,128)} %copy-done.22), channel_id=1, source_target_pairs={{0,8},{1,9},{2,10},{3,11},{4,12},{5,13},{6,14},{7,15},{8,0},{9,1},... | collective-permute-start | bytes 1474568 | tf_op jit(solution)/shard_map/ppermute | solution.py:34
  127.5 10.4 %collective-permute-start.22 = (f32[15,32,256]{2,1,0:T(8,128)S(1)}, f32[15,32,256]{2,1,0:T(8,128)S(1)}, u32[]{:S(2)}, u32[]{:S(2)}) collective-permute-start(f32[15,32,256]{2,1,0:T(8,128)S(1)} %get-tuple-element.114), channel_id=1, source_target_pairs={{2,8},{3,9},{4,10},{5,11},{6,12},{7,13},{8,2},{9,3},{10,4},{11,5},... | collective-permute-start | bytes 1474568 | tf_op jit(solution)/shard_map/ppermute | solution.py:34
  130.2 12.7 %collective-permute-start.25 = (f32[15,32,256]{2,1,0:T(8,128)S(1)}, f32[15,32,256]{2,1,0:T(8,128)S(1)}, u32[]{:S(2)}, u32[]{:S(2)}) collective-permute-start(f32[15,32,256]{2,1,0:T(8,128)S(1)} %get-tuple-element.148), channel_id=1, source_target_pairs={{2,8},{3,9},{4,10},{5,11},{6,12},{7,13},{8,2},{9,3},{10,4},{11,5},... | collective-permute-start | bytes 1474568 | tf_op jit(solution)/shard_map/ppermute | solution.py:34
  133.1 9.8 %collective-permute-start.26 = (f32[15,32,256]{2,1,0:T(8,128)S(1)}, f32[15,32,256]{2,1,0:T(8,128)S(1)}, u32[]{:S(2)}, u32[]{:S(2)}) collective-permute-start(f32[15,32,256]{2,1,0:T(8,128)S(1)} %get-tuple-element.147), channel_id=1, source_target_pairs={{0,8},{1,9},{2,10},{3,11},{4,12},{5,13},{6,14},{7,15},{8,0},{9,1},... | collective-permute-start | bytes 1474568 | tf_op jit(solution)/shard_map/ppermute | solution.py:34
  137.9 6.1 %copy-start.3 = (f32[16,80,256]{2,1,0:T(8,128)S(1)}, f32[16,80,256]{2,1,0:T(8,128)}, u32[]{:S(2)}) copy-start(f32[16,80,256]{2,1,0:T(8,128)} %copy-done.2) | copy-start | bytes 3932164
  139.0 5.1 %copy-start.1 = (f32[16,80,256]{2,1,0:T(8,128)S(1)}, f32[16,80,256]{2,1,0:T(8,128)}, u32[]{:S(2)}) copy-start(f32[16,80,256]{2,1,0:T(8,128)} %copy-done) | copy-start | bytes 3932164
  139.0 5.1 %copy-start.13 = (bf16[2,48,256]{2,1,0:T(8,128)(2,1)S(1)}, bf16[2,48,256]{2,1,0:T(8,128)(2,1)}, u32[]{:S(2)}) copy-start(bf16[2,48,256]{2,1,0:T(8,128)(2,1)} %copy-done.12) | copy-start | bytes 147460
  149.2 15.8 %collective-permute-start.28 = (f32[2,15,32,256]{3,2,1,0:T(8,128)S(1)}, f32[2,15,32,256]{3,2,1,0:T(8,128)S(1)}, u32[]{:S(2)}, u32[]{:S(2)}) collective-permute-start(f32[2,15,32,256]{3,2,1,0:T(8,128)S(1)} %get-tuple-element.133), channel_id=1, source_target_pairs={{2,8},{3,9},{4,10},{5,11},{6,12},{7,13},{8,2},{9,3},{10,4},{11,5},... | collective-permute-start | bytes 2949128 | tf_op jit(solution)/shard_map/ppermute | solution.py:34
  151.9 13.2 %collective-permute-start.29 = (f32[2,15,32,256]{3,2,1,0:T(8,128)S(1)}, f32[2,15,32,256]{3,2,1,0:T(8,128)S(1)}, u32[]{:S(2)}, u32[]{:S(2)}) collective-permute-start(f32[2,15,32,256]{3,2,1,0:T(8,128)S(1)} %get-tuple-element.134), channel_id=1, source_target_pairs={{0,8},{1,9},{2,10},{3,11},{4,12},{5,13},{6,14},{7,15},{8,0},{9,1},... | collective-permute-start | bytes 2949128 | tf_op jit(solution)/shard_map/ppermute | solution.py:34
  157.2 18.4 %collective-permute-start.34 = (f32[2,15,32,256]{3,2,1,0:T(8,128)S(1)}, f32[2,15,32,256]{3,2,1,0:T(8,128)S(1)}, u32[]{:S(2)}, u32[]{:S(2)}) collective-permute-start(f32[2,15,32,256]{3,2,1,0:T(8,128)S(1)} %get-tuple-element.143), channel_id=1, source_target_pairs={{2,8},{3,9},{4,10},{5,11},{6,12},{7,13},{8,2},{9,3},{10,4},{11,5},... | collective-permute-start | bytes 2949128 | tf_op jit(solution)/shard_map/ppermute | solution.py:34
  160.3 15.3 %collective-permute-start.35 = (f32[2,15,32,256]{3,2,1,0:T(8,128)S(1)}, f32[2,15,32,256]{3,2,1,0:T(8,128)S(1)}, u32[]{:S(2)}, u32[]{:S(2)}) collective-permute-start(f32[2,15,32,256]{3,2,1,0:T(8,128)S(1)} %get-tuple-element.144), channel_id=1, source_target_pairs={{0,8},{1,9},{2,10},{3,11},{4,12},{5,13},{6,14},{7,15},{8,0},{9,1},... | collective-permute-start | bytes 2949128 | tf_op jit(solution)/shard_map/ppermute | solution.py:34
  166.8 15.1 %collective-permute-start.30 = (f32[16,32,256]{2,1,0:T(8,128)S(1)}, f32[16,32,256]{2,1,0:T(8,128)S(1)}, u32[]{:S(2)}, u32[]{:S(2)}) collective-permute-start(f32[16,32,256]{2,1,0:T(8,128)S(1)} %log_factor.8.refs_0_), channel_id=1, source_target_pairs={{0,16},{2,18},{4,20},{6,22},{9,25},{11,27},{13,29},{15,31},{16,0},... | collective-permute-start | bytes 1572872 | tf_op jit(solution)/shard_map/ppermute | solution.py:34
  167.5 16.9 %collective-permute-start.31 = (f32[16,32,256]{2,1,0:T(8,128)S(1)}, f32[16,32,256]{2,1,0:T(8,128)S(1)}, u32[]{:S(2)}, u32[]{:S(2)}) collective-permute-start(f32[16,32,256]{2,1,0:T(8,128)S(1)} %log_factor.8.refs_0_), channel_id=1, source_target_pairs={{1,24},{3,26},{5,28},{7,30},{8,17},{10,19},{12,21},{14,23},{17,8},... | collective-permute-start | bytes 1572872 | tf_op jit(solution)/shard_map/ppermute | solution.py:34
  171.3 16.4 %collective-permute-start.32 = (f32[16,32,256]{2,1,0:T(8,128)S(1)}, f32[16,32,256]{2,1,0:T(8,128)S(1)}, u32[]{:S(2)}, u32[]{:S(2)}) collective-permute-start(f32[16,32,256]{2,1,0:T(8,128)S(1)} %log_factor.8.refs_0_), channel_id=1, source_target_pairs={{1,8},{3,10},{5,12},{7,14},{8,1},{10,3},{12,5},{14,7},{17,24},{19,... | collective-permute-start | bytes 1572872 | tf_op jit(solution)/shard_map/ppermute | solution.py:34
  177.3 10.6 %collective-permute-start.36 = (f32[16,32,256]{2,1,0:T(8,128)S(1)}, f32[16,32,256]{2,1,0:T(8,128)S(1)}, u32[]{:S(2)}, u32[]{:S(2)}) collective-permute-start(f32[16,32,256]{2,1,0:T(8,128)S(1)} %log_factor.9.refs_0_), channel_id=1, source_target_pairs={{0,16},{2,18},{4,20},{6,22},{9,25},{11,27},{13,29},{15,31},{16,0},... | collective-permute-start | bytes 1572872 | tf_op jit(solution)/shard_map/ppermute | solution.py:34
  178.0 17.5 %collective-permute-start.37 = (f32[16,32,256]{2,1,0:T(8,128)S(1)}, f32[16,32,256]{2,1,0:T(8,128)S(1)}, u32[]{:S(2)}, u32[]{:S(2)}) collective-permute-start(f32[16,32,256]{2,1,0:T(8,128)S(1)} %log_factor.9.refs_0_), channel_id=1, source_target_pairs={{1,24},{3,26},{5,28},{7,30},{8,17},{10,19},{12,21},{14,23},{17,8},... | collective-permute-start | bytes 1572872 | tf_op jit(solution)/shard_map/ppermute | solution.py:34
  181.9 15.3 %collective-permute-start.38 = (f32[16,32,256]{2,1,0:T(8,128)S(1)}, f32[16,32,256]{2,1,0:T(8,128)S(1)}, u32[]{:S(2)}, u32[]{:S(2)}) collective-permute-start(f32[16,32,256]{2,1,0:T(8,128)S(1)} %log_factor.9.refs_0_), channel_id=1, source_target_pairs={{1,8},{3,10},{5,12},{7,14},{8,1},{10,3},{12,5},{14,7},{17,24},{19,... | collective-permute-start | bytes 1572872 | tf_op jit(solution)/shard_map/ppermute | solution.py:34
  187.9 9.5 %collective-permute-start.33 = (f32[16,32,256]{2,1,0:T(8,128)S(1)}, f32[16,32,256]{2,1,0:T(8,128)S(1)}, u32[]{:S(2)}, u32[]{:S(2)}) collective-permute-start(f32[16,32,256]{2,1,0:T(8,128)S(1)} %last_update.2.refs_0_), channel_id=1, source_target_pairs={{0,8},{1,9},{2,10},{3,11},{4,12},{5,13},{6,14},{7,15},{8,0},{9,1},... | collective-permute-start | bytes 1572872 | tf_op jit(solution)/shard_map/ppermute | solution.py:34
  197.3 2.0 collective-permute-start.39
  (19 other events, 35.9 us)

commit v15 on v14

--- a/solution.py
+++ b/solution.py
@@ -94,12 +94,14 @@
     return -(-value // unit) * unit
 
 
-def call(kernel, out_shape, in_specs, name, scratch=()):
+def call(kernel, out_shape, in_specs, name, scratch=(), hbm=()):
+    if hbm:
+        out_shape = tuple(pltpu.HBM(o.shape, o.dtype) if index in hbm else o for index, o in enumerate(out_shape))
     return pl.pallas_call(
         kernel,
         out_shape=out_shape,
         in_specs=in_specs,
-        out_specs=jax.tree.map(lambda _: VMEM, out_shape),
+        out_specs=(VMEM,) * len(out_shape) if isinstance(out_shape, tuple) else VMEM,
         scratch_shapes=list(scratch),
         compiler_params=PARAMS,
         name=name,
@@ -198,7 +200,7 @@
         shape((2, 2 * 8 * planes, depth), BF16),
         shape((2, 2 * 8 * planes, depth), BF16),
     )
-    tables = call(kernel, out_shape, [VMEM, VMEM], "band_matrices")(mine, other)
+    tables = call(kernel, out_shape, [VMEM, VMEM], "band_matrices", hbm=range(1, 6))(mine, other)
     whole, inner_rows, edge_rows = tables[0:2], tables[2:4], tables[4:6]
     return Tables(whole, inner_rows, edge_rows, tables[6:8], tables[8:10])
 
@@ -216,7 +218,7 @@
 def make_windows(estimate, wide):
     planes, _, cells_z = estimate.shape
     shape = jax.ShapeDtypeStruct((planes, wide, cells_z), F32)
-    return call(window_kernel, (shape, shape), [VMEM], "estimate_windows")(estimate)
+    return call(window_kernel, (shape, shape), [VMEM], "estimate_windows", hbm=(0, 1))(estimate)
 
 
 def put_edges(out_ref, edge_refs):
@@ -245,7 +247,9 @@
 
 def choose(window, crossed, radius):
     out_shape = edge_shapes(window.shape, radius, window.shape[1:2])
-    return call(choose_kernel, out_shape, [VMEM] * 2, "estimate")(window, crossed)
+    return call(choose_kernel, out_shape, [VMEM] * 2, "estimate", hbm=(2,))(
+        pltpu.with_memory_space_constraint(window, pltpu.HBM), crossed
+    )
 
 
 def shift_kernel(offsets_ref, acq_ref, first_ref, second_ref, turned_ref):
@@ -477,7 +481,7 @@
         pltpu.VMEM(blurred.shape, F32), pltpu.VMEM(blurred.shape, F32), pltpu.SemaphoreType.DMA((2,))
     ]
     in_specs = [SMEM] + [pl.BlockSpec(memory_space=pl.ANY)] * 3 + [VMEM] * 5
-    return call(kernel, out_shape, in_specs, "image_and_ratio", scratch)(
+    return call(kernel, out_shape, in_specs, "image_and_ratio", scratch, hbm=(len(out_shape) - 1,))(
         shifts, *blocks, masks, blurred, tables.whole[1], *tables.z
     )
 

time: 202 us -> 204 us (level)
  waiting for transfers between devices: 58.3 us -> 64.6 us
  local copies, waits for them, and re-layouts: 12.4 us -> 6.67 us
  Pallas kernels: 54.5 us -> 58.7 us
  starting transfers between devices: 71 us -> 68.5 us
    ppermute x40, waiting for transfers between devices: 58.3 us -> 64.6 us  [send(): return lax.ppermute(array, AXES, moves(move))]
    unnamed x54 -> x34, local copies, waits for them, and re-layouts: 12.3 us -> 6.59 us
    pallas_call x5, Pallas kernels: 11.1 us -> 15.2 us  [the longest x2 7.36 us: first_ratio(): call(kernel, out_shape, in_specs, 'image_and_ratio', scratch, hbm=(len(ou...]
    ppermute x40, starting transfers between devices: 71 us -> 68.5 us  [send(): return lax.ppermute(array, AXES, moves(move))]
  transfers between devices with their start and end apart: 40 -> 40, of which waited for: 17 -> 17; matrix products, arithmetic and copies ran while one was open for 2% -> 2% of each run, Pallas kernels for 22% -> 24%
where the time goes in v15:
time: 204 us; the launch traced here: 203 us
  starting transfers between devices  68.5 us (34%)
  waiting for transfers between devices  64.6 us (32%)
  Pallas kernels  58.7 us (29%)
  local copies, waits for them, and re-layouts  6.67 us (3%)
  other arithmetic  3.68 us (2%)
    ppermute x40, starting transfers between devices, send(): return lax.ppermute(array, AXES, moves(move))  68.5 us
    ppermute x40, waiting for transfers between devices, send(): return lax.ppermute(array, AXES, moves(move))  64.6 us
    pallas_call x8, Pallas kernels, blur_x(): call(kernel, (shape, shape), [VMEM] * len(operands), 'blur_x_far' if far...  15.1 us
    pallas_call x2, Pallas kernels, next_ratio(): return call(kernel, out_shape, [VMEM] * len(operands), 'ratio')(*operands)  9.35 us
    pallas_call x5, Pallas kernels, log_factor(): call(kernel, shape, [VMEM] * (3 + len(parts)), 'log_factor')  7.67 us
    pallas_call x2, Pallas kernels, first_ratio(): call(kernel, out_shape, in_specs, 'image_and_ratio', scratch, hbm=(len(ou...  7.36 us
    unnamed x34, local copies, waits for them, and re-layouts  6.59 us
    pallas_call x1, Pallas kernels, shift_and_cut(): call(shift_kernel, (shape, shape), [SMEM, VMEM], 'shift_recorded', scratch)  4.55 us
  transfers between devices with their start and end apart: 40, of which 17 were waited for; matrix products, arithmetic and copies ran while one was open for 2% of the time, Pallas kernels for 24%

profile of v15, /device:TPU:17, one launch (start us, length us, event | category | flops | bytes accessed | tf_op | source)
XLA Modules:
  0.0 202.9 jit_solution(16828017526860819584)
XLA Ops:
  0.0 1.6 copy-done.3
  1.6 1.9 estimate_windows.1
  4.8 3.0 %collective-permute-start.1 = (f32[1,16,128]{2,1,0:T(8,128)S(1)}, f32[1,16,128]{2,1,0:T(8,128)}, u32[]{:S(2)}, u32[]{:S(2)}) collective-permute-start(f32[1,16,128]{2,1,0:T(8,128)S(1)} %convert_element_type.14), channel_id=1, source_target_pairs={{0,8},{1,9},{2,10},{3,11},{4,12},{5,13},{6,14},{7,15},{8,0},{9,1},... | collective-permute-start | bytes 24584 | tf_op jit(solution)/shard_map/ppermute | solution.py:34
  9.0 2.5 %band_matrices.1 = (bf16[2,80,384]{2,1,0:T(8,128)(2,1)S(1)}, bf16[2,64,256]{2,1,0:T(8,128)(2,1)}, bf16[2,48,256]{2,1,0:T(8,128)(2,1)}, bf16[2,32,256]{2,1,0:T(8,...) custom-call(f32[1,384]{1,0:T(1,128)S(1)} %fusion.1.mine_ref, ...), custom_call_target="tpu_custom_call" | custom-call | tf_op jit(solution)/shard_map/band_matrices/pallas_call | solution.py:203
  12.9 1.6 copy-done.2
  14.5 4.5 %shift_recorded.1 = (f32[16,80,256]{2,1,0:T(8,128)}, f32[16,80,256]{2,1,0:T(8,128)}) custom-call(s32[1,3]{1,0:T(1,128)S(1)} %copy-done.11, f32[16,128,256]{2,1,0:T(8,128)S(1)} %bitcast.1), custom_call_target="tpu_custom_call" | custom-call | tf_op jit(solution)/shard_map/shift_recorded/pallas_call | solution.py:281
  19.1 1.9 collective-permute-start.4
  21.0 4.5 %collective-permute-done.2.crossed_ref = f32[16,96,256]{2,1,0:T(8,128)S(1)} collective-permute-done((f32[16,96,256]{2,1,0:T(8,128)}, f32[16,96,256]{2,1,0:T(8,128)S(1)}, u32[]{:S(2)}, u32[]{:S(2)}) %collective-permute-start.2) | collective-permute-done | bytes 1572896 | tf_op jit(solution)/shard_map/ppermute | solution.py:34
  28.1 3.4 %estimate.1 = (f32[16,96,256]{2,1,0:T(8,128)S(1)}, f32[15,96,256]{2,1,0:T(8,128)}, f32[15,96,256]{2,1,0:T(8,128)}) custom-call(f32[16,96,256]{2,1,0:T(8,128)} %get-tuple-element.84.window_ref, f32[16,96,256]{2,1,0:T(8,128)S(1)} %copy-done.5), custom_call_target="tpu_custom_call" | custom-call | tf_op jit(solution)/shard_map/estimate/pallas_call | solution.py:250
  31.5 7.0 %collective-permute-start.9 = (f32[15,96,256]{2,1,0:T(8,128)}, f32[15,96,256]{2,1,0:T(8,128)}, u32[]{:S(2)}, u32[]{:S(2)}) collective-permute-start(f32[15,96,256]{2,1,0:T(8,128)} %get-tuple-element.91), channel_id=1, source_target_pairs={{2,8},{3,9},{4,10},{5,11},{6,12},{7,13},{8,2},{9,3},{10,4},{11,5},... | collective-permute-start | bytes 4423688 | tf_op jit(solution)/shard_map/ppermute | solution.py:34
  43.0 4.4 %collective-permute-start.5 = (f32[16,80,256]{2,1,0:T(8,128)S(1)}, f32[16,80,256]{2,1,0:T(8,128)S(1)}, u32[]{:S(2)}, u32[]{:S(2)}) collective-permute-start(f32[16,80,256]{2,1,0:T(8,128)S(1)} %broadcast_select_fusion.own_ref), channel_id=1, source_target_pairs={{2,8},{3,9},{4,10},{5,11},{6,12},{7,13},{8,2},{9,3},{10,4},{11,5},... | collective-permute-start | bytes 3932168 | tf_op jit(solution)/shard_map/ppermute | solution.py:34
  47.4 9.1 %collective-permute-done.7 = f32[2,16,128]{2,1,0:T(8,128)S(1)} collective-permute-done((f32[2,16,128]{2,1,0:T(8,128)}, f32[2,16,128]{2,1,0:T(8,128)S(1)}, u32[]{:S(2)}, u32[]{:S(2)}) %collective-permute-start.7) | collective-permute-done | bytes 16416 | tf_op jit(solution)/shard_map/ppermute | solution.py:34
  56.5 1.9 collective-permute-start.13
  59.8 4.4 %blur_x_far.4 = (f32[16,96,256]{2,1,0:T(8,128)S(1)}, f32[16,96,256]{2,1,0:T(8,128)S(1)}) custom-call(bf16[2,256,384]{2,1,0:T(8,128)(2,1)S(1)} %get-tuple-element.78.hi_ref, bf16[2,256,384]{2,1,0:T(8,128)(2,1)S(1)} %get-tuple-element.79.lo_ref, f32[15,96,256]{2,1,0:T(8,128)} %collective-permute-done.9.refs_0_), custom_call_target="tpu_custom_call" | custom-call | tf_op jit(solution)/shard_map/blur_x_far/pallas_call | solution.py:329
  64.3 3.3 %blur_x_near.4 = (f32[16,96,256]{2,1,0:T(8,128)S(1)}, f32[16,96,256]{2,1,0:T(8,128)S(1)}) custom-call(bf16[2,256,384]{2,1,0:T(8,128)(2,1)S(1)} %get-tuple-element.78.hi_ref, bf16[2,256,384]{2,1,0:T(8,128)(2,1)S(1)} %get-tuple-element.79.lo_ref, f32[16,96,256]{2,1,0:T(8,128)S(1)} %get-tuple-element.86.refs_0_.before_ref, ...), custom_call_target="tpu_custom_call" | custom-call | tf_op jit(solution)/shard_map/blur_x_near/pallas_call | solution.py:329
  70.1 3.1 %image_and_ratio.2 = (f32[16,64,256]{2,1,0:T(8,128)S(1)}, f32[15,64,256]{2,1,0:T(8,128)S(1)}, f32[15,64,256]{2,1,0:T(8,128)S(1)}, f32[16,80,256]{2,1,0:T(8,128)}) custom-call(s32[2,3]{1,0:T(2,128)S(1)} %fusion.2.shift_ref, f32[16,80,256]{2,1,0:T(8,128)S(1)} %collective-permute-done.5.far_ref, f32[16,80,256]{2,1,0:T(8,128)S(1)} %collective-permute-done.6.near_ref, ...), custom_call_target="tpu_custom_call" | custom-call | tf_op jit(solution)/shard_map/image_and_ratio/pallas_call | solution.py:484
  73.2 3.3 %collective-permute-start.10 = (f32[15,64,256]{2,1,0:T(8,128)S(1)}, f32[15,64,256]{2,1,0:T(8,128)S(1)}, u32[]{:S(2)}, u32[]{:S(2)}) collective-permute-start(f32[15,64,256]{2,1,0:T(8,128)S(1)} %get-tuple-element.98), channel_id=1, source_target_pairs={{2,8},{3,9},{4,10},{5,11},{6,12},{7,13},{8,2},{9,3},{10,4},{11,5},... | collective-permute-start | bytes 2949128 | tf_op jit(solution)/shard_map/ppermute | solution.py:34
  78.2 5.9 %collective-permute-done.13.far_ref = f32[16,80,256]{2,1,0:T(8,128)S(1)} collective-permute-done((f32[16,80,256]{2,1,0:T(8,128)}, f32[16,80,256]{2,1,0:T(8,128)S(1)}, u32[]{:S(2)}, u32[]{:S(2)}) %collective-permute-start.13) | collective-permute-done | bytes 1310752 | tf_op jit(solution)/shard_map/ppermute | solution.py:34
  84.1 4.3 %image_and_ratio.3 = (f32[16,64,256]{2,1,0:T(8,128)S(1)}, f32[15,32,256]{2,1,0:T(8,128)S(1)}, f32[15,32,256]{2,1,0:T(8,128)S(1)}, f32[15,32,256]{2,1,0:T(8,128)S...) custom-call(s32[2,3]{1,0:T(2,128)S(1)} %fusion.2.shift_ref, f32[16,80,256]{2,1,0:T(8,128)S(1)} %collective-permute-done.13.far_ref, ...), custom_call_target="tpu_custom_call" | custom-call | tf_op jit(solution)/shard_map/image_and_ratio/pallas_call | solution.py:484
  88.4 3.3 %collective-permute-start.18 = (f32[15,32,256]{2,1,0:T(8,128)S(1)}, f32[15,32,256]{2,1,0:T(8,128)S(1)}, u32[]{:S(2)}, u32[]{:S(2)}) collective-permute-start(f32[15,32,256]{2,1,0:T(8,128)S(1)} %get-tuple-element.111), channel_id=1, source_target_pairs={{2,8},{3,9},{4,10},{5,11},{6,12},{7,13},{8,2},{9,3},{10,4},{11,5},... | collective-permute-start | bytes 1474568 | tf_op jit(solution)/shard_map/ppermute | solution.py:34
  91.8 2.8 %collective-permute-done.10.refs_0_ = f32[15,64,256]{2,1,0:T(8,128)S(1)} collective-permute-done((f32[15,64,256]{2,1,0:T(8,128)S(1)}, f32[15,64,256]{2,1,0:T(8,128)S(1)}, u32[]{:S(2)}, u32[]{:S(2)}) %collective-permute-start.10) | collective-permute-done | bytes 983072 | tf_op jit(solution)/shard_map/ppermute | solution.py:34
  94.7 2.1 %log_factor.5.before_ref = f32[16,64,256]{2,1,0:T(8,128)S(1)} custom-call(bf16[2,256,384]{2,1,0:T(8,128)(2,1)S(1)} %get-tuple-element.78.hi_ref, bf16[2,256,384]{2,1,0:T(8,128)(2,1)S(1)} %get-tuple-element.79.lo_ref, f32[16,96,256]{2,1,0:T(8,128)S(1)} %get-tuple-element.86.refs_0_.before_ref, f32[15,64,256]{2,1,0:T(8,128)S(1)} %collective-permute-done.10.refs_0_, ...), custom_call_target="tpu_custom_call" | custom-call | tf_op jit(solution)/shard_map/log_factor/pallas_call | solution.py:517
  96.8 3.0 %collective-permute-done.18.refs_0_ = f32[15,32,256]{2,1,0:T(8,128)S(1)} collective-permute-done((f32[15,32,256]{2,1,0:T(8,128)S(1)}, f32[15,32,256]{2,1,0:T(8,128)S(1)}, u32[]{:S(2)}, u32[]{:S(2)}) %collective-permute-start.18) | collective-permute-done | bytes 491552 | tf_op jit(solution)/shard_map/ppermute | solution.py:34
  102.1 3.8 %collective-permute-start.15 = (f32[15,32,256]{2,1,0:T(8,128)S(1)}, f32[15,32,256]{2,1,0:T(8,128)S(1)}, u32[]{:S(2)}, u32[]{:S(2)}) collective-permute-start(f32[15,32,256]{2,1,0:T(8,128)S(1)} %get-tuple-element.104), channel_id=1, source_target_pairs={{2,8},{3,9},{4,10},{5,11},{6,12},{7,13},{8,2},{9,3},{10,4},{11,5},... | collective-permute-start | bytes 1474568 | tf_op jit(solution)/shard_map/ppermute | solution.py:34
  106.0 6.7 %collective-permute-done.15.refs_0_ = f32[15,32,256]{2,1,0:T(8,128)S(1)} collective-permute-done((f32[15,32,256]{2,1,0:T(8,128)S(1)}, f32[15,32,256]{2,1,0:T(8,128)S(1)}, u32[]{:S(2)}, u32[]{:S(2)}) %collective-permute-start.15) | collective-permute-done | bytes 491552 | tf_op jit(solution)/shard_map/ppermute | solution.py:34
  115.8 2.1 %collective-permute-start.24 = (f32[16,32,256]{2,1,0:T(8,128)S(1)}, f32[16,32,256]{2,1,0:T(8,128)S(1)}, u32[]{:S(2)}, u32[]{:S(2)}) collective-permute-start(f32[16,32,256]{2,1,0:T(8,128)S(1)} %get-tuple-element.119.refs_0_.before_ref), channel_id=1, source_target_pairs={{0,1},{1,0},{2,3},{3,2},{4,5},{5,4},{6,7},{7,6},{8,9},{9,8},{10,11... | collective-permute-start | bytes 1572872 | tf_op jit(solution)/shard_map/ppermute | solution.py:34
  117.9 4.1 %collective-permute-start.21 = (f32[15,32,256]{2,1,0:T(8,128)}, f32[15,32,256]{2,1,0:T(8,128)}, u32[]{:S(2)}, u32[]{:S(2)}) collective-permute-start(f32[15,32,256]{2,1,0:T(8,128)} %get-tuple-element.113), channel_id=1, source_target_pairs={{2,8},{3,9},{4,10},{5,11},{6,12},{7,13},{8,2},{9,3},{10,4},{11,5},... | collective-permute-start | bytes 1474568 | tf_op jit(solution)/shard_map/ppermute | solution.py:34
  122.0 5.2 %collective-permute-done.17.refs_1_ = f32[16,32,256]{2,1,0:T(8,128)} collective-permute-done((f32[16,32,256]{2,1,0:T(8,128)S(1)}, f32[16,32,256]{2,1,0:T(8,128)}, u32[]{:S(2)}, u32[]{:S(2)}) %collective-permute-start.17) | collective-permute-done | bytes 524320 | tf_op jit(solution)/shard_map/ppermute | solution.py:34
  129.6 2.6 %collective-permute-start.22 = (f32[15,32,256]{2,1,0:T(8,128)S(1)}, f32[15,32,256]{2,1,0:T(8,128)S(1)}, u32[]{:S(2)}, u32[]{:S(2)}) collective-permute-start(f32[15,32,256]{2,1,0:T(8,128)S(1)} %get-tuple-element.114), channel_id=1, source_target_pairs={{2,8},{3,9},{4,10},{5,11},{6,12},{7,13},{8,2},{9,3},{10,4},{11,5},... | collective-permute-start | bytes 1474568 | tf_op jit(solution)/shard_map/ppermute | solution.py:34
  132.4 2.9 %collective-permute-start.25 = (f32[15,32,256]{2,1,0:T(8,128)S(1)}, f32[15,32,256]{2,1,0:T(8,128)S(1)}, u32[]{:S(2)}, u32[]{:S(2)}) collective-permute-start(f32[15,32,256]{2,1,0:T(8,128)S(1)} %get-tuple-element.148), channel_id=1, source_target_pairs={{2,8},{3,9},{4,10},{5,11},{6,12},{7,13},{8,2},{9,3},{10,4},{11,5},... | collective-permute-start | bytes 1474568 | tf_op jit(solution)/shard_map/ppermute | solution.py:34
  138.0 2.1 %blur_x_far.6 = (f32[16,32,256]{2,1,0:T(8,128)S(1)}, f32[16,32,256]{2,1,0:T(8,128)S(1)}) custom-call(bf16[2,256,384]{2,1,0:T(8,128)(2,1)S(1)} %get-tuple-element.78.hi_ref, bf16[2,256,384]{2,1,0:T(8,128)(2,1)S(1)} %get-tuple-element.79.lo_ref, f32[15,32,256]{2,1,0:T(8,128)} %collective-permute-done.21.refs_0_, ...), custom_call_target="tpu_custom_call" | custom-call | tf_op jit(solution)/shard_map/blur_x_far/pallas_call | solution.py:329
  141.2 3.9 %collective-permute-done.25.refs_0_ = f32[15,32,256]{2,1,0:T(8,128)S(1)} collective-permute-done((f32[15,32,256]{2,1,0:T(8,128)S(1)}, f32[15,32,256]{2,1,0:T(8,128)S(1)}, u32[]{:S(2)}, u32[]{:S(2)}) %collective-permute-start.25) | collective-permute-done | bytes 491552 | tf_op jit(solution)/shard_map/ppermute | solution.py:34
  146.2 5.2 %ratio.2 = (f32[16,32,256]{2,1,0:T(8,128)S(1)}, f32[16,32,256]{2,1,0:T(8,128)S(1)}, f32[2,15,32,256]{3,2,1,0:T(8,128)S(1)}, f32[2,15,32,256]{3,2,1,0:T(8,128)S(1)}, f32[2,16,32,256]{3,2,1,0:T(8,128)S(1)}) custom-call(f32[16,80,256]{2,1,0:T(8,128)S(1)} %copy-done, f32[16,80,256]{2,1,0:T(8,128)S(1)} %copy-done.1, ...), custom_call_target="tpu_custom_call" | custom-call | tf_op jit(solution)/shard_map/ratio/pallas_call | solution.py:472
  151.4 2.6 %collective-permute-start.28 = (f32[2,15,32,256]{3,2,1,0:T(8,128)S(1)}, f32[2,15,32,256]{3,2,1,0:T(8,128)S(1)}, u32[]{:S(2)}, u32[]{:S(2)}) collective-permute-start(f32[2,15,32,256]{3,2,1,0:T(8,128)S(1)} %get-tuple-element.133), channel_id=1, source_target_pairs={{2,8},{3,9},{4,10},{5,11},{6,12},{7,13},{8,2},{9,3},{10,4},{11,5},... | collective-permute-start | bytes 2949128 | tf_op jit(solution)/shard_map/ppermute | solution.py:34
  155.2 4.2 %ratio.3 = (f32[16,32,256]{2,1,0:T(8,128)S(1)}, f32[16,32,256]{2,1,0:T(8,128)S(1)}, f32[2,15,32,256]{3,2,1,0:T(8,128)S(1)}, f32[2,15,32,256]{3,2,1,0:T(8,128)S(1)}) custom-call(f32[16,80,256]{2,1,0:T(8,128)S(1)} %copy-done, f32[16,80,256]{2,1,0:T(8,128)S(1)} %copy-done.1, f32[16,32,256]{2,1,0:T(8,128)S(1)} %get-tuple-element.126.refs_3_.refs_2_, ...), custom_call_target="tpu_custom_call" | custom-call | tf_op jit(solution)/shard_map/ratio/pallas_call | solution.py:472
  159.4 3.1 %collective-permute-start.34 = (f32[2,15,32,256]{3,2,1,0:T(8,128)S(1)}, f32[2,15,32,256]{3,2,1,0:T(8,128)S(1)}, u32[]{:S(2)}, u32[]{:S(2)}) collective-permute-start(f32[2,15,32,256]{3,2,1,0:T(8,128)S(1)} %get-tuple-element.143), channel_id=1, source_target_pairs={{2,8},{3,9},{4,10},{5,11},{6,12},{7,13},{8,2},{9,3},{10,4},{11,5},... | collective-permute-start | bytes 2949128 | tf_op jit(solution)/shard_map/ppermute | solution.py:34
  162.8 4.4 %collective-permute-done.28.refs_0_.refs_3_ = f32[2,15,32,256]{3,2,1,0:T(8,128)S(1)} collective-permute-done((f32[2,15,32,256]{3,2,1,0:T(8,128)S(1)}, f32[2,15,32,256]{3,2,1,0:T(8,128)S(1)}, u32[]{:S(2)}, u32[]{:S(2)}) %collective-permute-start.28) | collective-permute-done | bytes 983072 | tf_op jit(solution)/shard_map/ppermute | solution.py:34
  167.3 1.7 log_factor.8.refs_0_
  169.7 3.8 %collective-permute-start.31 = (f32[16,32,256]{2,1,0:T(8,128)S(1)}, f32[16,32,256]{2,1,0:T(8,128)S(1)}, u32[]{:S(2)}, u32[]{:S(2)}) collective-permute-start(f32[16,32,256]{2,1,0:T(8,128)S(1)} %log_factor.8.refs_0_), channel_id=1, source_target_pairs={{1,24},{3,26},{5,28},{7,30},{8,17},{10,19},{12,21},{14,23},{17,8},... | collective-permute-start | bytes 1572872 | tf_op jit(solution)/shard_map/ppermute | solution.py:34
  173.5 2.2 %collective-permute-start.32 = (f32[16,32,256]{2,1,0:T(8,128)S(1)}, f32[16,32,256]{2,1,0:T(8,128)S(1)}, u32[]{:S(2)}, u32[]{:S(2)}) collective-permute-start(f32[16,32,256]{2,1,0:T(8,128)S(1)} %log_factor.8.refs_0_), channel_id=1, source_target_pairs={{1,8},{3,10},{5,12},{7,14},{8,1},{10,3},{12,5},{14,7},{17,24},{19,... | collective-permute-start | bytes 1572872 | tf_op jit(solution)/shard_map/ppermute | solution.py:34
  175.7 2.1 %collective-permute-done.34.refs_0_.refs_3_ = f32[2,15,32,256]{3,2,1,0:T(8,128)S(1)} collective-permute-done((f32[2,15,32,256]{3,2,1,0:T(8,128)S(1)}, f32[2,15,32,256]{3,2,1,0:T(8,128)S(1)}, u32[]{:S(2)}, u32[]{:S(2)}) %collective-permute-start.34) | collective-permute-done | bytes 983072 | tf_op jit(solution)/shard_map/ppermute | solution.py:34
  177.8 1.7 log_factor.9.refs_0_
  180.2 3.8 %collective-permute-start.37 = (f32[16,32,256]{2,1,0:T(8,128)S(1)}, f32[16,32,256]{2,1,0:T(8,128)S(1)}, u32[]{:S(2)}, u32[]{:S(2)}) collective-permute-start(f32[16,32,256]{2,1,0:T(8,128)S(1)} %log_factor.9.refs_0_), channel_id=1, source_target_pairs={{1,24},{3,26},{5,28},{7,30},{8,17},{10,19},{12,21},{14,23},{17,8},... | collective-permute-start | bytes 1572872 | tf_op jit(solution)/shard_map/ppermute | solution.py:34
  184.1 2.2 %collective-permute-start.38 = (f32[16,32,256]{2,1,0:T(8,128)S(1)}, f32[16,32,256]{2,1,0:T(8,128)S(1)}, u32[]{:S(2)}, u32[]{:S(2)}) collective-permute-start(f32[16,32,256]{2,1,0:T(8,128)S(1)} %log_factor.9.refs_0_), channel_id=1, source_target_pairs={{1,8},{3,10},{5,12},{7,14},{8,1},{10,3},{12,5},{14,7},{17,24},{19,... | collective-permute-start | bytes 1572872 | tf_op jit(solution)/shard_map/ppermute | solution.py:34
  186.6 3.3 %collective-permute-done.32.refs_3_ = f32[16,32,256]{2,1,0:T(8,128)S(1)} collective-permute-done((f32[16,32,256]{2,1,0:T(8,128)S(1)}, f32[16,32,256]{2,1,0:T(8,128)S(1)}, u32[]{:S(2)}, u32[]{:S(2)}) %collective-permute-start.32) | collective-permute-done | bytes 524320 | tf_op jit(solution)/shard_map/ppermute | solution.py:34
  190.1 7.5 %collective-permute-done.37.refs_2_ = f32[16,32,256]{2,1,0:T(8,128)S(1)} collective-permute-done((f32[16,32,256]{2,1,0:T(8,128)S(1)}, f32[16,32,256]{2,1,0:T(8,128)S(1)}, u32[]{:S(2)}, u32[]{:S(2)}) %collective-permute-start.37) | collective-permute-done | bytes 524320 | tf_op jit(solution)/shard_map/ppermute | solution.py:34
  197.6 1.7 collective-permute-done.38.refs_3_
  199.5 1.9 collective-permute-done.39.refs_3_
  (102 shorter events, 34.3 us)
Async XLA Ops:
  1.6 6.2 %copy-start.14 = (f32[1,61]{1,0:T(1,128)S(1)}, f32[1,61]{1,0:T(1,128)}, u32[]{:S(2)}) copy-start(f32[1,61]{1,0:T(1,128)} %param.13) | copy-start | bytes 736
  1.6 6.2 %copy-start.15 = (f32[1,31]{1,0:T(1,128)S(1)}, f32[1,31]{1,0:T(1,128)}, u32[]{:S(2)}) copy-start(f32[1,31]{1,0:T(1,128)} %param.12) | copy-start | bytes 376
  1.6 6.2 %copy-start.16 = (f32[1,31]{1,0:T(1,128)S(1)}, f32[1,31]{1,0:T(1,128)}, u32[]{:S(2)}) copy-start(f32[1,31]{1,0:T(1,128)} %param.11) | copy-start | bytes 376
  1.6 11.3 %copy-start.11 = (s32[1,3]{1,0:T(1,128)S(1)}, s32[1,3]{1,0:T(1,128)}, u32[]{:S(2)}) copy-start(s32[1,3]{1,0:T(1,128)} %offsets_ref.1) | copy-start | bytes 40
  3.5 22.0 %collective-permute-start.2 = (f32[16,96,256]{2,1,0:T(8,128)}, f32[16,96,256]{2,1,0:T(8,128)S(1)}, u32[]{:S(2)}, u32[]{:S(2)}) collective-permute-start(f32[16,96,256]{2,1,0:T(8,128)} %get-tuple-element.85), channel_id=1, source_target_pairs={{0,1},{2,3},{4,5},{6,7},{9,8},{11,10},{13,12},{15,14},{16,17},{18,... | collective-permute-start | bytes 4718600 | tf_op jit(solution)/shard_map/ppermute | solution.py:34
  4.8 6.7 %collective-permute-start.1 = (f32[1,16,128]{2,1,0:T(8,128)S(1)}, f32[1,16,128]{2,1,0:T(8,128)}, u32[]{:S(2)}, u32[]{:S(2)}) collective-permute-start(f32[1,16,128]{2,1,0:T(8,128)S(1)} %convert_element_type.14), channel_id=1, source_target_pairs={{0,8},{1,9},{2,10},{3,11},{4,12},{5,13},{6,14},{7,15},{8,0},{9,1},... | collective-permute-start | bytes 24584 | tf_op jit(solution)/shard_map/ppermute | solution.py:34
  7.8 1.2 collective-permute-start
  19.1 22.1 %collective-permute-start.4 = (f32[16,80,256]{2,1,0:T(8,128)}, f32[16,80,256]{2,1,0:T(8,128)}, u32[]{:S(2)}, u32[]{:S(2)}) collective-permute-start(f32[16,80,256]{2,1,0:T(8,128)} %get-tuple-element.88), channel_id=1, source_target_pairs={{1,8},{3,10},{5,12},{7,14},{8,1},{10,3},{12,5},{14,7},{17,24},{19,... | collective-permute-start | bytes 3932168 | tf_op jit(solution)/shard_map/ppermute | solution.py:34
  31.5 26.9 %collective-permute-start.9 = (f32[15,96,256]{2,1,0:T(8,128)}, f32[15,96,256]{2,1,0:T(8,128)}, u32[]{:S(2)}, u32[]{:S(2)}) collective-permute-start(f32[15,96,256]{2,1,0:T(8,128)} %get-tuple-element.91), channel_id=1, source_target_pairs={{2,8},{3,9},{4,10},{5,11},{6,12},{7,13},{8,2},{9,3},{10,4},{11,5},... | collective-permute-start | bytes 4423688 | tf_op jit(solution)/shard_map/ppermute | solution.py:34
  38.5 18.0 %collective-permute-start.12 = (f32[16,80,256]{2,1,0:T(8,128)}, f32[16,80,256]{2,1,0:T(8,128)}, u32[]{:S(2)}, u32[]{:S(2)}) collective-permute-start(f32[16,80,256]{2,1,0:T(8,128)} %get-tuple-element.102), channel_id=1, source_target_pairs={{0,1},{1,9},{2,3},{3,11},{4,5},{5,13},{6,7},{7,15},{8,0},{9,8},{10... | collective-permute-start | bytes 3932168 | tf_op jit(solution)/shard_map/ppermute | solution.py:34
  38.6 4.5 %collective-permute-start.3 = (f32[1,3]{1,0:T(1,128)S(1)}, f32[1,3]{1,0:T(1,128)S(1)}, u32[]{:S(2)}, u32[]{:S(2)}) collective-permute-start(f32[1,3]{1,0:T(1,128)S(1)} %convert_element_type.15), channel_id=1, source_target_pairs={{0,8},{1,9},{2,10},{3,11},{4,12},{5,13},{6,14},{7,15},{8,0},{9,1},... | collective-permute-start | bytes 44 | tf_op jit(solution)/shard_map/ppermute | solution.py:34
  39.7 16.7 %collective-permute-start.7 = (f32[2,16,128]{2,1,0:T(8,128)}, f32[2,16,128]{2,1,0:T(8,128)S(1)}, u32[]{:S(2)}, u32[]{:S(2)}) collective-permute-start(f32[2,16,128]{2,1,0:T(8,128)} %maximum_select_fusion), channel_id=1, source_target_pairs={{0,1},{1,0},{2,3},{3,2},{4,5},{5,4},{6,7},{7,6},{8,9},{9,8},{10,11... | collective-permute-start | bytes 49160 | tf_op jit(solution)/shard_map/ppermute | solution.py:34
  41.1 23.1 %collective-permute-start.8 = (f32[15,96,256]{2,1,0:T(8,128)}, f32[15,96,256]{2,1,0:T(8,128)S(1)}, u32[]{:S(2)}, u32[]{:S(2)}) collective-permute-start(f32[15,96,256]{2,1,0:T(8,128)} %get-tuple-element.90), channel_id=1, source_target_pairs={{0,8},{1,9},{2,10},{3,11},{4,12},{5,13},{6,14},{7,15},{8,0},{9,1},... | collective-permute-start | bytes 4423688 | tf_op jit(solution)/shard_map/ppermute | solution.py:34
  43.0 27.1 %collective-permute-start.5 = (f32[16,80,256]{2,1,0:T(8,128)S(1)}, f32[16,80,256]{2,1,0:T(8,128)S(1)}, u32[]{:S(2)}, u32[]{:S(2)}) collective-permute-start(f32[16,80,256]{2,1,0:T(8,128)S(1)} %broadcast_select_fusion.own_ref), channel_id=1, source_target_pairs={{2,8},{3,9},{4,10},{5,11},{6,12},{7,13},{8,2},{9,3},{10,4},{11,5},... | collective-permute-start | bytes 3932168 | tf_op jit(solution)/shard_map/ppermute | solution.py:34
  56.5 13.6 %collective-permute-start.6 = (f32[16,80,256]{2,1,0:T(8,128)S(1)}, f32[16,80,256]{2,1,0:T(8,128)S(1)}, u32[]{:S(2)}, u32[]{:S(2)}) collective-permute-start(f32[16,80,256]{2,1,0:T(8,128)S(1)} %broadcast_select_fusion.own_ref), channel_id=1, source_target_pairs={{0,8},{1,9},{2,10},{3,11},{4,12},{5,13},{6,14},{7,15},{8,0},{9,1},... | collective-permute-start | bytes 3932168 | tf_op jit(solution)/shard_map/ppermute | solution.py:34
  56.5 27.7 %collective-permute-start.13 = (f32[16,80,256]{2,1,0:T(8,128)}, f32[16,80,256]{2,1,0:T(8,128)S(1)}, u32[]{:S(2)}, u32[]{:S(2)}) collective-permute-start(f32[16,80,256]{2,1,0:T(8,128)} %collective-permute-done.12.own_ref), channel_id=1, source_target_pairs={{2,8},{3,9},{4,10},{5,11},{6,12},{7,13},{8,2},{9,3},{10,4},{11,5},... | collective-permute-start | bytes 3932168 | tf_op jit(solution)/shard_map/ppermute | solution.py:34
  58.4 25.7 %collective-permute-start.14 = (f32[16,80,256]{2,1,0:T(8,128)}, f32[16,80,256]{2,1,0:T(8,128)S(1)}, u32[]{:S(2)}, u32[]{:S(2)}) collective-permute-start(f32[16,80,256]{2,1,0:T(8,128)} %collective-permute-done.12.own_ref), channel_id=1, source_target_pairs={{0,8},{1,9},{2,10},{3,11},{4,12},{5,13},{6,14},{7,15},{8,0},{9,1},... | collective-permute-start | bytes 3932168 | tf_op jit(solution)/shard_map/ppermute | solution.py:34
  73.2 21.5 %collective-permute-start.10 = (f32[15,64,256]{2,1,0:T(8,128)S(1)}, f32[15,64,256]{2,1,0:T(8,128)S(1)}, u32[]{:S(2)}, u32[]{:S(2)}) collective-permute-start(f32[15,64,256]{2,1,0:T(8,128)S(1)} %get-tuple-element.98), channel_id=1, source_target_pairs={{2,8},{3,9},{4,10},{5,11},{6,12},{7,13},{8,2},{9,3},{10,4},{11,5},... | collective-permute-start | bytes 2949128 | tf_op jit(solution)/shard_map/ppermute | solution.py:34
  76.5 18.1 %collective-permute-start.11 = (f32[15,64,256]{2,1,0:T(8,128)S(1)}, f32[15,64,256]{2,1,0:T(8,128)S(1)}, u32[]{:S(2)}, u32[]{:S(2)}) collective-permute-start(f32[15,64,256]{2,1,0:T(8,128)S(1)} %get-tuple-element.99), channel_id=1, source_target_pairs={{0,8},{1,9},{2,10},{3,11},{4,12},{5,13},{6,14},{7,15},{8,0},{9,1},... | collective-permute-start | bytes 2949128 | tf_op jit(solution)/shard_map/ppermute | solution.py:34
  88.4 11.4 %collective-permute-start.18 = (f32[15,32,256]{2,1,0:T(8,128)S(1)}, f32[15,32,256]{2,1,0:T(8,128)S(1)}, u32[]{:S(2)}, u32[]{:S(2)}) collective-permute-start(f32[15,32,256]{2,1,0:T(8,128)S(1)} %get-tuple-element.111), channel_id=1, source_target_pairs={{2,8},{3,9},{4,10},{5,11},{6,12},{7,13},{8,2},{9,3},{10,4},{11,5},... | collective-permute-start | bytes 1474568 | tf_op jit(solution)/shard_map/ppermute | solution.py:34
  91.7 8.1 %collective-permute-start.19 = (f32[15,32,256]{2,1,0:T(8,128)S(1)}, f32[15,32,256]{2,1,0:T(8,128)S(1)}, u32[]{:S(2)}, u32[]{:S(2)}) collective-permute-start(f32[15,32,256]{2,1,0:T(8,128)S(1)} %get-tuple-element.112), channel_id=1, source_target_pairs={{0,8},{1,9},{2,10},{3,11},{4,12},{5,13},{6,14},{7,15},{8,0},{9,1},... | collective-permute-start | bytes 1474568 | tf_op jit(solution)/shard_map/ppermute | solution.py:34
  100.9 13.2 %collective-permute-start.20 = (f32[16,32,256]{2,1,0:T(8,128)S(1)}, f32[16,32,256]{2,1,0:T(8,128)S(1)}, u32[]{:S(2)}, u32[]{:S(2)}) collective-permute-start(f32[16,32,256]{2,1,0:T(8,128)S(1)} %log_factor.7.refs_0_), channel_id=1, source_target_pairs={{0,16},{1,17},{2,18},{3,19},{4,20},{5,21},{6,22},{7,23},{8,24},{9,... | collective-permute-start | bytes 1572872 | tf_op jit(solution)/shard_map/ppermute | solution.py:34
  102.1 10.6 %collective-permute-start.15 = (f32[15,32,256]{2,1,0:T(8,128)S(1)}, f32[15,32,256]{2,1,0:T(8,128)S(1)}, u32[]{:S(2)}, u32[]{:S(2)}) collective-permute-start(f32[15,32,256]{2,1,0:T(8,128)S(1)} %get-tuple-element.104), channel_id=1, source_target_pairs={{2,8},{3,9},{4,10},{5,11},{6,12},{7,13},{8,2},{9,3},{10,4},{11,5},... | collective-permute-start | bytes 1474568 | tf_op jit(solution)/shard_map/ppermute | solution.py:34
  105.9 6.8 %collective-permute-start.16 = (f32[15,32,256]{2,1,0:T(8,128)S(1)}, f32[15,32,256]{2,1,0:T(8,128)S(1)}, u32[]{:S(2)}, u32[]{:S(2)}) collective-permute-start(f32[15,32,256]{2,1,0:T(8,128)S(1)} %get-tuple-element.105), channel_id=1, source_target_pairs={{0,8},{1,9},{2,10},{3,11},{4,12},{5,13},{6,14},{7,15},{8,0},{9,1},... | collective-permute-start | bytes 1474568 | tf_op jit(solution)/shard_map/ppermute | solution.py:34
  113.8 13.4 %collective-permute-start.17 = (f32[16,32,256]{2,1,0:T(8,128)S(1)}, f32[16,32,256]{2,1,0:T(8,128)}, u32[]{:S(2)}, u32[]{:S(2)}) collective-permute-start(f32[16,32,256]{2,1,0:T(8,128)S(1)} %log_factor.6.refs_0_), channel_id=1, source_target_pairs={{0,16},{1,17},{2,18},{3,19},{4,20},{5,21},{6,22},{7,23},{8,24},{9,... | collective-permute-start | bytes 1572872 | tf_op jit(solution)/shard_map/ppermute | solution.py:34
  115.8 16.5 %collective-permute-start.24 = (f32[16,32,256]{2,1,0:T(8,128)S(1)}, f32[16,32,256]{2,1,0:T(8,128)S(1)}, u32[]{:S(2)}, u32[]{:S(2)}) collective-permute-start(f32[16,32,256]{2,1,0:T(8,128)S(1)} %get-tuple-element.119.refs_0_.before_ref), channel_id=1, source_target_pairs={{0,1},{1,0},{2,3},{3,2},{4,5},{5,4},{6,7},{7,6},{8,9},{9,8},{10,11... | collective-permute-start | bytes 1572872 | tf_op jit(solution)/shard_map/ppermute | solution.py:34
  117.9 11.7 %collective-permute-start.21 = (f32[15,32,256]{2,1,0:T(8,128)}, f32[15,32,256]{2,1,0:T(8,128)}, u32[]{:S(2)}, u32[]{:S(2)}) collective-permute-start(f32[15,32,256]{2,1,0:T(8,128)} %get-tuple-element.113), channel_id=1, source_target_pairs={{2,8},{3,9},{4,10},{5,11},{6,12},{7,13},{8,2},{9,3},{10,4},{11,5},... | collective-permute-start | bytes 1474568 | tf_op jit(solution)/shard_map/ppermute | solution.py:34
  128.4 8.5 %collective-permute-start.23 = (f32[15,32,256]{2,1,0:T(8,128)S(1)}, f32[15,32,256]{2,1,0:T(8,128)S(1)}, u32[]{:S(2)}, u32[]{:S(2)}) collective-permute-start(f32[15,32,256]{2,1,0:T(8,128)S(1)} %get-tuple-element.115), channel_id=1, source_target_pairs={{0,8},{1,9},{2,10},{3,11},{4,12},{5,13},{6,14},{7,15},{8,0},{9,1},... | collective-permute-start | bytes 1474568 | tf_op jit(solution)/shard_map/ppermute | solution.py:34
  129.6 6.2 %collective-permute-start.27 = (f32[15,32,256]{2,1,0:T(8,128)}, f32[15,32,256]{2,1,0:T(8,128)S(1)}, u32[]{:S(2)}, u32[]{:S(2)}) collective-permute-start(f32[15,32,256]{2,1,0:T(8,128)} %copy-done.12), channel_id=1, source_target_pairs={{0,8},{1,9},{2,10},{3,11},{4,12},{5,13},{6,14},{7,15},{8,0},{9,1},... | collective-permute-start | bytes 1474568 | tf_op jit(solution)/shard_map/ppermute | solution.py:34
  129.6 10.4 %collective-permute-start.22 = (f32[15,32,256]{2,1,0:T(8,128)S(1)}, f32[15,32,256]{2,1,0:T(8,128)S(1)}, u32[]{:S(2)}, u32[]{:S(2)}) collective-permute-start(f32[15,32,256]{2,1,0:T(8,128)S(1)} %get-tuple-element.114), channel_id=1, source_target_pairs={{2,8},{3,9},{4,10},{5,11},{6,12},{7,13},{8,2},{9,3},{10,4},{11,5},... | collective-permute-start | bytes 1474568 | tf_op jit(solution)/shard_map/ppermute | solution.py:34
  132.4 12.7 %collective-permute-start.25 = (f32[15,32,256]{2,1,0:T(8,128)S(1)}, f32[15,32,256]{2,1,0:T(8,128)S(1)}, u32[]{:S(2)}, u32[]{:S(2)}) collective-permute-start(f32[15,32,256]{2,1,0:T(8,128)S(1)} %get-tuple-element.148), channel_id=1, source_target_pairs={{2,8},{3,9},{4,10},{5,11},{6,12},{7,13},{8,2},{9,3},{10,4},{11,5},... | collective-permute-start | bytes 1474568 | tf_op jit(solution)/shard_map/ppermute | solution.py:34
  135.3 9.8 %collective-permute-start.26 = (f32[15,32,256]{2,1,0:T(8,128)S(1)}, f32[15,32,256]{2,1,0:T(8,128)S(1)}, u32[]{:S(2)}, u32[]{:S(2)}) collective-permute-start(f32[15,32,256]{2,1,0:T(8,128)S(1)} %get-tuple-element.147), channel_id=1, source_target_pairs={{0,8},{1,9},{2,10},{3,11},{4,12},{5,13},{6,14},{7,15},{8,0},{9,1},... | collective-permute-start | bytes 1474568 | tf_op jit(solution)/shard_map/ppermute | solution.py:34
  140.1 6.1 %copy-start.1 = (f32[16,80,256]{2,1,0:T(8,128)S(1)}, f32[16,80,256]{2,1,0:T(8,128)}, u32[]{:S(2)}) copy-start(f32[16,80,256]{2,1,0:T(8,128)} %get-tuple-element.109.refs_1_) | copy-start | bytes 3932164
  141.1 5.1 %copy-start = (f32[16,80,256]{2,1,0:T(8,128)S(1)}, f32[16,80,256]{2,1,0:T(8,128)}, u32[]{:S(2)}) copy-start(f32[16,80,256]{2,1,0:T(8,128)} %get-tuple-element.108.refs_0_) | copy-start | bytes 3932164
  141.1 5.1 %copy-start.7 = (bf16[2,48,256]{2,1,0:T(8,128)(2,1)S(1)}, bf16[2,48,256]{2,1,0:T(8,128)(2,1)}, u32[]{:S(2)}) copy-start(bf16[2,48,256]{2,1,0:T(8,128)(2,1)} %get-tuple-element.131.refs_6_) | copy-start | bytes 147460
  141.2 5.1 %copy-start.10 = (bf16[2,32,256]{2,1,0:T(8,128)(2,1)S(1)}, bf16[2,32,256]{2,1,0:T(8,128)(2,1)}, u32[]{:S(2)}) copy-start(bf16[2,32,256]{2,1,0:T(8,128)(2,1)} %get-tuple-element.132.refs_7_) | copy-start | bytes 98308
  151.4 15.8 %collective-permute-start.28 = (f32[2,15,32,256]{3,2,1,0:T(8,128)S(1)}, f32[2,15,32,256]{3,2,1,0:T(8,128)S(1)}, u32[]{:S(2)}, u32[]{:S(2)}) collective-permute-start(f32[2,15,32,256]{3,2,1,0:T(8,128)S(1)} %get-tuple-element.133), channel_id=1, source_target_pairs={{2,8},{3,9},{4,10},{5,11},{6,12},{7,13},{8,2},{9,3},{10,4},{11,5},... | collective-permute-start | bytes 2949128 | tf_op jit(solution)/shard_map/ppermute | solution.py:34
  154.0 13.2 %collective-permute-start.29 = (f32[2,15,32,256]{3,2,1,0:T(8,128)S(1)}, f32[2,15,32,256]{3,2,1,0:T(8,128)S(1)}, u32[]{:S(2)}, u32[]{:S(2)}) collective-permute-start(f32[2,15,32,256]{3,2,1,0:T(8,128)S(1)} %get-tuple-element.134), channel_id=1, source_target_pairs={{0,8},{1,9},{2,10},{3,11},{4,12},{5,13},{6,14},{7,15},{8,0},{9,1},... | collective-permute-start | bytes 2949128 | tf_op jit(solution)/shard_map/ppermute | solution.py:34
  159.4 18.4 %collective-permute-start.34 = (f32[2,15,32,256]{3,2,1,0:T(8,128)S(1)}, f32[2,15,32,256]{3,2,1,0:T(8,128)S(1)}, u32[]{:S(2)}, u32[]{:S(2)}) collective-permute-start(f32[2,15,32,256]{3,2,1,0:T(8,128)S(1)} %get-tuple-element.143), channel_id=1, source_target_pairs={{2,8},{3,9},{4,10},{5,11},{6,12},{7,13},{8,2},{9,3},{10,4},{11,5},... | collective-permute-start | bytes 2949128 | tf_op jit(solution)/shard_map/ppermute | solution.py:34
  162.5 15.3 %collective-permute-start.35 = (f32[2,15,32,256]{3,2,1,0:T(8,128)S(1)}, f32[2,15,32,256]{3,2,1,0:T(8,128)S(1)}, u32[]{:S(2)}, u32[]{:S(2)}) collective-permute-start(f32[2,15,32,256]{3,2,1,0:T(8,128)S(1)} %get-tuple-element.144), channel_id=1, source_target_pairs={{0,8},{1,9},{2,10},{3,11},{4,12},{5,13},{6,14},{7,15},{8,0},{9,1},... | collective-permute-start | bytes 2949128 | tf_op jit(solution)/shard_map/ppermute | solution.py:34
  169.0 15.1 %collective-permute-start.30 = (f32[16,32,256]{2,1,0:T(8,128)S(1)}, f32[16,32,256]{2,1,0:T(8,128)S(1)}, u32[]{:S(2)}, u32[]{:S(2)}) collective-permute-start(f32[16,32,256]{2,1,0:T(8,128)S(1)} %log_factor.8.refs_0_), channel_id=1, source_target_pairs={{0,16},{2,18},{4,20},{6,22},{9,25},{11,27},{13,29},{15,31},{16,0},... | collective-permute-start | bytes 1572872 | tf_op jit(solution)/shard_map/ppermute | solution.py:34
  169.7 16.9 %collective-permute-start.31 = (f32[16,32,256]{2,1,0:T(8,128)S(1)}, f32[16,32,256]{2,1,0:T(8,128)S(1)}, u32[]{:S(2)}, u32[]{:S(2)}) collective-permute-start(f32[16,32,256]{2,1,0:T(8,128)S(1)} %log_factor.8.refs_0_), channel_id=1, source_target_pairs={{1,24},{3,26},{5,28},{7,30},{8,17},{10,19},{12,21},{14,23},{17,8},... | collective-permute-start | bytes 1572872 | tf_op jit(solution)/shard_map/ppermute | solution.py:34
  173.5 16.4 %collective-permute-start.32 = (f32[16,32,256]{2,1,0:T(8,128)S(1)}, f32[16,32,256]{2,1,0:T(8,128)S(1)}, u32[]{:S(2)}, u32[]{:S(2)}) collective-permute-start(f32[16,32,256]{2,1,0:T(8,128)S(1)} %log_factor.8.refs_0_), channel_id=1, source_target_pairs={{1,8},{3,10},{5,12},{7,14},{8,1},{10,3},{12,5},{14,7},{17,24},{19,... | collective-permute-start | bytes 1572872 | tf_op jit(solution)/shard_map/ppermute | solution.py:34
  179.5 10.6 %collective-permute-start.36 = (f32[16,32,256]{2,1,0:T(8,128)S(1)}, f32[16,32,256]{2,1,0:T(8,128)S(1)}, u32[]{:S(2)}, u32[]{:S(2)}) collective-permute-start(f32[16,32,256]{2,1,0:T(8,128)S(1)} %log_factor.9.refs_0_), channel_id=1, source_target_pairs={{0,16},{2,18},{4,20},{6,22},{9,25},{11,27},{13,29},{15,31},{16,0},... | collective-permute-start | bytes 1572872 | tf_op jit(solution)/shard_map/ppermute | solution.py:34
  180.2 17.4 %collective-permute-start.37 = (f32[16,32,256]{2,1,0:T(8,128)S(1)}, f32[16,32,256]{2,1,0:T(8,128)S(1)}, u32[]{:S(2)}, u32[]{:S(2)}) collective-permute-start(f32[16,32,256]{2,1,0:T(8,128)S(1)} %log_factor.9.refs_0_), channel_id=1, source_target_pairs={{1,24},{3,26},{5,28},{7,30},{8,17},{10,19},{12,21},{14,23},{17,8},... | collective-permute-start | bytes 1572872 | tf_op jit(solution)/shard_map/ppermute | solution.py:34
  184.1 15.3 %collective-permute-start.38 = (f32[16,32,256]{2,1,0:T(8,128)S(1)}, f32[16,32,256]{2,1,0:T(8,128)S(1)}, u32[]{:S(2)}, u32[]{:S(2)}) collective-permute-start(f32[16,32,256]{2,1,0:T(8,128)S(1)} %log_factor.9.refs_0_), channel_id=1, source_target_pairs={{1,8},{3,10},{5,12},{7,14},{8,1},{10,3},{12,5},{14,7},{17,24},{19,... | collective-permute-start | bytes 1572872 | tf_op jit(solution)/shard_map/ppermute | solution.py:34
  190.0 9.5 %collective-permute-start.33 = (f32[16,32,256]{2,1,0:T(8,128)S(1)}, f32[16,32,256]{2,1,0:T(8,128)S(1)}, u32[]{:S(2)}, u32[]{:S(2)}) collective-permute-start(f32[16,32,256]{2,1,0:T(8,128)S(1)} %last_update.2.refs_0_), channel_id=1, source_target_pairs={{0,8},{1,9},{2,10},{3,11},{4,12},{5,13},{6,14},{7,15},{8,0},{9,1},... | collective-permute-start | bytes 1572872 | tf_op jit(solution)/shard_map/ppermute | solution.py:34
  199.5 2.0 collective-permute-start.39
  (9 other events, 19.8 us)

commit v16 on v15

--- a/solution.py
+++ b/solution.py
@@ -200,7 +200,7 @@
         shape((2, 2 * 8 * planes, depth), BF16),
         shape((2, 2 * 8 * planes, depth), BF16),
     )
-    tables = call(kernel, out_shape, [VMEM, VMEM], "band_matrices", hbm=range(1, 6))(mine, other)
+    tables = call(kernel, out_shape, [VMEM, VMEM], "band_matrices")(mine, other)
     whole, inner_rows, edge_rows = tables[0:2], tables[2:4], tables[4:6]
     return Tables(whole, inner_rows, edge_rows, tables[6:8], tables[8:10])
 
@@ -218,7 +218,7 @@
 def make_windows(estimate, wide):
     planes, _, cells_z = estimate.shape
     shape = jax.ShapeDtypeStruct((planes, wide, cells_z), F32)
-    return call(window_kernel, (shape, shape), [VMEM], "estimate_windows", hbm=(0, 1))(estimate)
+    return call(window_kernel, (shape, shape), [VMEM], "estimate_windows")(estimate)
 
 
 def put_edges(out_ref, edge_refs):
@@ -232,11 +232,13 @@
         end -= far_ref.shape[1]
 
 
-def choose_kernel(window_ref, crossed_ref, out_ref, *edge_refs):
+def choose_kernel(window_ref, crossed_ref, out_ref, far_ref):
     straight = core() == half()
     for p in range(out_ref.shape[0]):
         out_ref[p] = jnp.where(straight, window_ref[p], crossed_ref[p])
-    put_edges(out_ref, edge_refs)
+    beyond = core() * (out_ref.shape[0] - far_ref.shape[0])
+    for p in range(far_ref.shape[0]):
+        far_ref[p] = out_ref[p + beyond]
 
 
 def edge_shapes(shape, radius, chunks):
@@ -246,10 +248,8 @@
 
 
 def choose(window, crossed, radius):
-    out_shape = edge_shapes(window.shape, radius, window.shape[1:2])
-    return call(choose_kernel, out_shape, [VMEM] * 2, "estimate", hbm=(2,))(
-        pltpu.with_memory_space_constraint(window, pltpu.HBM), crossed
-    )
+    out_shape = edge_shapes(window.shape, radius, window.shape[1:2])[:2]
+    return call(choose_kernel, out_shape, [VMEM] * 2, "estimate")(window, crossed)
 
 
 def shift_kernel(offsets_ref, acq_ref, first_ref, second_ref, turned_ref):
@@ -527,10 +527,10 @@
     put_edges(out_ref, edge_refs)
 
 
-def update(parts, radius):
+def update(parts, radius, hbm):
     kernel = functools.partial(update_kernel, count=len(parts))
     out_shape = edge_shapes(parts[0].shape, radius, parts[0].shape[1:2])
-    return call(kernel, out_shape, [VMEM] * len(parts), "update")(*parts)
+    return call(kernel, out_shape, [VMEM] * len(parts), "update", hbm=hbm)(*parts)
 
 
 def finish_kernel(*refs):
@@ -622,8 +622,9 @@
     first, second = shift_and_cut(offsets, acquired[0], near)
 
     arrived = send(after(first, tables.whole[0]), lambda g, c, q, r: (g, r, q, c) if c != r else None)
-    current, distant, close = choose(after(window, first), crossed, radius)
+    current, distant = choose(after(window, first), crossed, radius)
     second = send(after(second, current), lambda g, c, q, r: (g, r, q, 1 - c))
+    close = lax.dynamic_slice_in_dim(current, (1 - core()) * (planes - radius), radius, 0)
     distant, close = neighbours(distant, close)
     first = jnp.where(straight, first, arrived)
 
@@ -652,7 +653,7 @@
         chunks, before = [], []
         for total in totals:
             parts = [total] + [send(total, across(turn)) for turn in range(1, groups)]
-            rows, distant, close = update(parts, radius)
+            rows, distant, close = update(parts, radius, () if chunks else (2,))
             if total is totals[0]:
                 beyond = send(rows, to_row_partner)
             distant = after(distant, chunks[0][0]) if chunks else distant

time: 204 us -> 201 us (0.985)
  Pallas kernels: 58.7 us -> 55.8 us
  local copies, waits for them, and re-layouts: 6.67 us -> 9.56 us
    pallas_call x5, Pallas kernels: 9.95 us -> 7.07 us  [the longest x2 2.32 us: update(): call(kernel, out_shape, [VMEM] * len(parts), 'update', hbm=hbm)(*parts)]
    unnamed x34 -> x46, local copies, waits for them, and re-layouts: 6.59 us -> 9.39 us
  transfers between devices with their start and end apart: 40 -> 40, of which waited for: 17 -> 18; matrix products, arithmetic and copies ran while one was open for 2% -> 2% of each run, Pallas kernels for 24% -> 23%
where the time goes in v16:
time: 201 us; the launch traced here: 200 us
  starting transfers between devices  67.2 us (33%)
  waiting for transfers between devices  63 us (31%)
  Pallas kernels  55.8 us (28%)
  local copies, waits for them, and re-layouts  9.56 us (5%)
  other arithmetic  3.67 us (2%)
    ppermute x40, starting transfers between devices, send(): return lax.ppermute(array, AXES, moves(move))  67.2 us
    ppermute x40, waiting for transfers between devices, send(): return lax.ppermute(array, AXES, moves(move))  63 us
    pallas_call x8, Pallas kernels, blur_x(): call(kernel, (shape, shape), [VMEM] * len(operands), 'blur_x_far' if far...  15.1 us
    unnamed x46, local copies, waits for them, and re-layouts  9.39 us
    pallas_call x2, Pallas kernels, next_ratio(): return call(kernel, out_shape, [VMEM] * len(operands), 'ratio')(*operands)  9.34 us
    pallas_call x5, Pallas kernels, log_factor(): call(kernel, shape, [VMEM] * (3 + len(parts)), 'log_factor')  7.68 us
    pallas_call x2, Pallas kernels, first_ratio(): call(kernel, out_shape, in_specs, 'image_and_ratio', scratch, hbm=(len(ou...  7.38 us
    pallas_call x1, Pallas kernels, shift_and_cut(): call(shift_kernel, (shape, shape), [SMEM, VMEM], 'shift_recorded', scratch)  4.48 us
  transfers between devices with their start and end apart: 40, of which 18 were waited for; matrix products, arithmetic and copies ran while one was open for 2% of the time, Pallas kernels for 23%

profile of v16, /device:TPU:17, one launch (start us, length us, event | category | flops | bytes accessed | tf_op | source)
XLA Modules:
  0.0 200.0 jit_solution(5468800966255169611)
XLA Ops:
  0.0 1.6 copy-done.3
  5.4 3.0 %collective-permute-start.1 = (f32[1,16,128]{2,1,0:T(8,128)S(1)}, f32[1,16,128]{2,1,0:T(8,128)}, u32[]{:S(2)}, u32[]{:S(2)}) collective-permute-start(f32[1,16,128]{2,1,0:T(8,128)S(1)} %convert_element_type.14), channel_id=1, source_target_pairs={{0,8},{1,9},{2,10},{3,11},{4,12},{5,13},{6,14},{7,15},{8,0},{9,1},... | collective-permute-start | bytes 24584 | tf_op jit(solution)/shard_map/ppermute | solution.py:34
  9.6 2.0 %band_matrices.1 = (bf16[2,80,384]{2,1,0:T(8,128)(2,1)S(1)}, bf16[2,64,256]{2,1,0:T(8,128)(2,1)S(1)}, bf16[2,48,256]{2,1,0:T(8,128)(2,1)S(1)}, bf16[2,32,256]{2,...) custom-call(f32[1,384]{1,0:T(1,128)S(1)} %fusion.1.mine_ref, ...), custom_call_target="tpu_custom_call" | custom-call | tf_op jit(solution)/shard_map/band_matrices/pallas_call | solution.py:203
  15.5 1.6 copy-done.2
  17.1 4.5 %shift_recorded.1 = (f32[16,80,256]{2,1,0:T(8,128)}, f32[16,80,256]{2,1,0:T(8,128)}) custom-call(s32[1,3]{1,0:T(1,128)S(1)} %copy-done.18, f32[16,128,256]{2,1,0:T(8,128)S(1)} %bitcast.1), custom_call_target="tpu_custom_call" | custom-call | tf_op jit(solution)/shard_map/shift_recorded/pallas_call | solution.py:281
  21.6 1.9 collective-permute-start.4
  23.5 2.0 collective-permute-done.2.crossed_ref
  29.4 5.7 %collective-permute-start.9 = (f32[15,96,256]{2,1,0:T(8,128)}, f32[15,96,256]{2,1,0:T(8,128)}, u32[]{:S(2)}, u32[]{:S(2)}) collective-permute-start(f32[15,96,256]{2,1,0:T(8,128)} %get-tuple-element.89), channel_id=1, source_target_pairs={{2,8},{3,9},{4,10},{5,11},{6,12},{7,13},{8,2},{9,3},{10,4},{11,5},... | collective-permute-start | bytes 4423688 | tf_op jit(solution)/shard_map/ppermute | solution.py:34
  37.9 5.4 %collective-permute-done.4 = f32[16,80,256]{2,1,0:T(8,128)} collective-permute-done((f32[16,80,256]{2,1,0:T(8,128)}, f32[16,80,256]{2,1,0:T(8,128)}, u32[]{:S(2)}, u32[]{:S(2)}) %collective-permute-start.4) | collective-permute-done | bytes 1310752 | tf_op jit(solution)/shard_map/ppermute | solution.py:34
  44.8 8.2 %collective-permute-start.5 = (f32[16,80,256]{2,1,0:T(8,128)S(1)}, f32[16,80,256]{2,1,0:T(8,128)S(1)}, u32[]{:S(2)}, u32[]{:S(2)}) collective-permute-start(f32[16,80,256]{2,1,0:T(8,128)S(1)} %broadcast_select_fusion.own_ref), channel_id=1, source_target_pairs={{2,8},{3,9},{4,10},{5,11},{6,12},{7,13},{8,2},{9,3},{10,4},{11,5},... | collective-permute-start | bytes 3932168 | tf_op jit(solution)/shard_map/ppermute | solution.py:34
  53.0 2.4 %collective-permute-done.7 = f32[2,16,128]{2,1,0:T(8,128)S(1)} collective-permute-done((f32[2,16,128]{2,1,0:T(8,128)}, f32[2,16,128]{2,1,0:T(8,128)S(1)}, u32[]{:S(2)}, u32[]{:S(2)}) %collective-permute-start.7) | collective-permute-done | bytes 16416 | tf_op jit(solution)/shard_map/ppermute | solution.py:34
  55.4 3.6 %collective-permute-start.13 = (f32[16,80,256]{2,1,0:T(8,128)}, f32[16,80,256]{2,1,0:T(8,128)S(1)}, u32[]{:S(2)}, u32[]{:S(2)}) collective-permute-start(f32[16,80,256]{2,1,0:T(8,128)} %collective-permute-done.12.own_ref), channel_id=1, source_target_pairs={{2,8},{3,9},{4,10},{5,11},{6,12},{7,13},{8,2},{9,3},{10,4},{11,5},... | collective-permute-start | bytes 3932168 | tf_op jit(solution)/shard_map/ppermute | solution.py:34
  59.9 4.4 %blur_x_far.4 = (f32[16,96,256]{2,1,0:T(8,128)S(1)}, f32[16,96,256]{2,1,0:T(8,128)S(1)}) custom-call(bf16[2,256,384]{2,1,0:T(8,128)(2,1)S(1)} %get-tuple-element.77.hi_ref, bf16[2,256,384]{2,1,0:T(8,128)(2,1)S(1)} %get-tuple-element.78.lo_ref, f32[15,96,256]{2,1,0:T(8,128)} %collective-permute-done.9.refs_0_), custom_call_target="tpu_custom_call" | custom-call | tf_op jit(solution)/shard_map/blur_x_far/pallas_call | solution.py:329
  64.3 3.3 %blur_x_near.4 = (f32[16,96,256]{2,1,0:T(8,128)S(1)}, f32[16,96,256]{2,1,0:T(8,128)S(1)}) custom-call(bf16[2,256,384]{2,1,0:T(8,128)(2,1)S(1)} %get-tuple-element.77.hi_ref, bf16[2,256,384]{2,1,0:T(8,128)(2,1)S(1)} %get-tuple-element.78.lo_ref, f32[16,96,256]{2,1,0:T(8,128)S(1)} %get-tuple-element.85.refs_0_.before_ref, ...), custom_call_target="tpu_custom_call" | custom-call | tf_op jit(solution)/shard_map/blur_x_near/pallas_call | solution.py:329
  67.7 1.6 blur_yz.2.blurred_ref
  69.3 3.1 %image_and_ratio.2 = (f32[16,64,256]{2,1,0:T(8,128)S(1)}, f32[15,64,256]{2,1,0:T(8,128)S(1)}, f32[15,64,256]{2,1,0:T(8,128)S(1)}, f32[16,80,256]{2,1,0:T(8,128)}) custom-call(s32[2,3]{1,0:T(2,128)S(1)} %fusion.2.shift_ref, f32[16,80,256]{2,1,0:T(8,128)S(1)} %collective-permute-done.5.far_ref, f32[16,80,256]{2,1,0:T(8,128)S(1)} %collective-permute-done.6.near_ref, ...), custom_call_target="tpu_custom_call" | custom-call | tf_op jit(solution)/shard_map/image_and_ratio/pallas_call | solution.py:484
  72.4 2.7 %collective-permute-start.10 = (f32[15,64,256]{2,1,0:T(8,128)S(1)}, f32[15,64,256]{2,1,0:T(8,128)S(1)}, u32[]{:S(2)}, u32[]{:S(2)}) collective-permute-start(f32[15,64,256]{2,1,0:T(8,128)S(1)} %get-tuple-element.96), channel_id=1, source_target_pairs={{2,8},{3,9},{4,10},{5,11},{6,12},{7,13},{8,2},{9,3},{10,4},{11,5},... | collective-permute-start | bytes 2949128 | tf_op jit(solution)/shard_map/ppermute | solution.py:34
  75.2 1.6 blur_yz.3.blurred_ref
  76.7 5.9 %collective-permute-done.13.far_ref = f32[16,80,256]{2,1,0:T(8,128)S(1)} collective-permute-done((f32[16,80,256]{2,1,0:T(8,128)}, f32[16,80,256]{2,1,0:T(8,128)S(1)}, u32[]{:S(2)}, u32[]{:S(2)}) %collective-permute-start.13) | collective-permute-done | bytes 1310752 | tf_op jit(solution)/shard_map/ppermute | solution.py:34
  82.7 4.3 %image_and_ratio.3 = (f32[16,64,256]{2,1,0:T(8,128)S(1)}, f32[15,32,256]{2,1,0:T(8,128)S(1)}, f32[15,32,256]{2,1,0:T(8,128)S(1)}, f32[15,32,256]{2,1,0:T(8,128)S...) custom-call(s32[2,3]{1,0:T(2,128)S(1)} %fusion.2.shift_ref, f32[16,80,256]{2,1,0:T(8,128)S(1)} %collective-permute-done.13.far_ref, ...), custom_call_target="tpu_custom_call" | custom-call | tf_op jit(solution)/shard_map/image_and_ratio/pallas_call | solution.py:484
  86.9 3.3 %collective-permute-start.18 = (f32[15,32,256]{2,1,0:T(8,128)S(1)}, f32[15,32,256]{2,1,0:T(8,128)S(1)}, u32[]{:S(2)}, u32[]{:S(2)}) collective-permute-start(f32[15,32,256]{2,1,0:T(8,128)S(1)} %get-tuple-element.109), channel_id=1, source_target_pairs={{2,8},{3,9},{4,10},{5,11},{6,12},{7,13},{8,2},{9,3},{10,4},{11,5},... | collective-permute-start | bytes 1474568 | tf_op jit(solution)/shard_map/ppermute | solution.py:34
  90.4 2.8 %collective-permute-done.10.refs_0_ = f32[15,64,256]{2,1,0:T(8,128)S(1)} collective-permute-done((f32[15,64,256]{2,1,0:T(8,128)S(1)}, f32[15,64,256]{2,1,0:T(8,128)S(1)}, u32[]{:S(2)}, u32[]{:S(2)}) %collective-permute-start.10) | collective-permute-done | bytes 983072 | tf_op jit(solution)/shard_map/ppermute | solution.py:34
  93.2 2.2 %log_factor.5.before_ref = f32[16,64,256]{2,1,0:T(8,128)S(1)} custom-call(bf16[2,256,384]{2,1,0:T(8,128)(2,1)S(1)} %get-tuple-element.77.hi_ref, bf16[2,256,384]{2,1,0:T(8,128)(2,1)S(1)} %get-tuple-element.78.lo_ref, f32[16,96,256]{2,1,0:T(8,128)S(1)} %get-tuple-element.85.refs_0_.before_ref, f32[15,64,256]{2,1,0:T(8,128)S(1)} %collective-permute-done.10.refs_0_, ...), custom_call_target="tpu_custom_call" | custom-call | tf_op jit(solution)/shard_map/log_factor/pallas_call | solution.py:517
  95.4 2.8 %collective-permute-done.18.refs_0_ = f32[15,32,256]{2,1,0:T(8,128)S(1)} collective-permute-done((f32[15,32,256]{2,1,0:T(8,128)S(1)}, f32[15,32,256]{2,1,0:T(8,128)S(1)}, u32[]{:S(2)}, u32[]{:S(2)}) %collective-permute-start.18) | collective-permute-done | bytes 491552 | tf_op jit(solution)/shard_map/ppermute | solution.py:34
  100.5 3.9 %collective-permute-start.15 = (f32[15,32,256]{2,1,0:T(8,128)S(1)}, f32[15,32,256]{2,1,0:T(8,128)S(1)}, u32[]{:S(2)}, u32[]{:S(2)}) collective-permute-start(f32[15,32,256]{2,1,0:T(8,128)S(1)} %get-tuple-element.102), channel_id=1, source_target_pairs={{2,8},{3,9},{4,10},{5,11},{6,12},{7,13},{8,2},{9,3},{10,4},{11,5},... | collective-permute-start | bytes 1474568 | tf_op jit(solution)/shard_map/ppermute | solution.py:34
  104.5 6.7 %collective-permute-done.15.refs_0_ = f32[15,32,256]{2,1,0:T(8,128)S(1)} collective-permute-done((f32[15,32,256]{2,1,0:T(8,128)S(1)}, f32[15,32,256]{2,1,0:T(8,128)S(1)}, u32[]{:S(2)}, u32[]{:S(2)}) %collective-permute-start.15) | collective-permute-done | bytes 491552 | tf_op jit(solution)/shard_map/ppermute | solution.py:34
  114.0 4.1 %collective-permute-start.21 = (f32[15,32,256]{2,1,0:T(8,128)}, f32[15,32,256]{2,1,0:T(8,128)}, u32[]{:S(2)}, u32[]{:S(2)}) collective-permute-start(f32[15,32,256]{2,1,0:T(8,128)} %get-tuple-element.111), channel_id=1, source_target_pairs={{2,8},{3,9},{4,10},{5,11},{6,12},{7,13},{8,2},{9,3},{10,4},{11,5},... | collective-permute-start | bytes 1474568 | tf_op jit(solution)/shard_map/ppermute | solution.py:34
  118.1 7.2 %collective-permute-done.17.refs_1_ = f32[16,32,256]{2,1,0:T(8,128)} collective-permute-done((f32[16,32,256]{2,1,0:T(8,128)S(1)}, f32[16,32,256]{2,1,0:T(8,128)}, u32[]{:S(2)}, u32[]{:S(2)}) %collective-permute-start.17) | collective-permute-done | bytes 524320 | tf_op jit(solution)/shard_map/ppermute | solution.py:34
  127.1 1.9 collective-permute-start.22
  129.1 3.6 %collective-permute-start.25 = (f32[15,32,256]{2,1,0:T(8,128)S(1)}, f32[15,32,256]{2,1,0:T(8,128)S(1)}, u32[]{:S(2)}, u32[]{:S(2)}) collective-permute-start(f32[15,32,256]{2,1,0:T(8,128)S(1)} %get-tuple-element.146), channel_id=1, source_target_pairs={{2,8},{3,9},{4,10},{5,11},{6,12},{7,13},{8,2},{9,3},{10,4},{11,5},... | collective-permute-start | bytes 1474568 | tf_op jit(solution)/shard_map/ppermute | solution.py:34
  135.1 2.1 %blur_x_far.6 = (f32[16,32,256]{2,1,0:T(8,128)S(1)}, f32[16,32,256]{2,1,0:T(8,128)S(1)}) custom-call(bf16[2,256,384]{2,1,0:T(8,128)(2,1)S(1)} %get-tuple-element.77.hi_ref, bf16[2,256,384]{2,1,0:T(8,128)(2,1)S(1)} %get-tuple-element.78.lo_ref, f32[15,32,256]{2,1,0:T(8,128)} %collective-permute-done.21.refs_0_, ...), custom_call_target="tpu_custom_call" | custom-call | tf_op jit(solution)/shard_map/blur_x_far/pallas_call | solution.py:329
  138.6 3.9 %collective-permute-done.25.refs_0_ = f32[15,32,256]{2,1,0:T(8,128)S(1)} collective-permute-done((f32[15,32,256]{2,1,0:T(8,128)S(1)}, f32[15,32,256]{2,1,0:T(8,128)S(1)}, u32[]{:S(2)}, u32[]{:S(2)}) %collective-permute-start.25) | collective-permute-done | bytes 491552 | tf_op jit(solution)/shard_map/ppermute | solution.py:34
  143.6 5.2 %ratio.2 = (f32[16,32,256]{2,1,0:T(8,128)S(1)}, f32[16,32,256]{2,1,0:T(8,128)S(1)}, f32[2,15,32,256]{3,2,1,0:T(8,128)S(1)}, f32[2,15,32,256]{3,2,1,0:T(8,128)S(1)}, f32[2,16,32,256]{3,2,1,0:T(8,128)S(1)}) custom-call(f32[16,80,256]{2,1,0:T(8,128)S(1)} %copy-done, f32[16,80,256]{2,1,0:T(8,128)S(1)} %copy-done.1, ...), custom_call_target="tpu_custom_call" | custom-call | tf_op jit(solution)/shard_map/ratio/pallas_call | solution.py:472
  148.8 2.1 %collective-permute-start.28 = (f32[2,15,32,256]{3,2,1,0:T(8,128)S(1)}, f32[2,15,32,256]{3,2,1,0:T(8,128)S(1)}, u32[]{:S(2)}, u32[]{:S(2)}) collective-permute-start(f32[2,15,32,256]{3,2,1,0:T(8,128)S(1)} %get-tuple-element.131), channel_id=1, source_target_pairs={{2,8},{3,9},{4,10},{5,11},{6,12},{7,13},{8,2},{9,3},{10,4},{11,5},... | collective-permute-start | bytes 2949128 | tf_op jit(solution)/shard_map/ppermute | solution.py:34
  152.0 4.2 %ratio.3 = (f32[16,32,256]{2,1,0:T(8,128)S(1)}, f32[16,32,256]{2,1,0:T(8,128)S(1)}, f32[2,15,32,256]{3,2,1,0:T(8,128)S(1)}, f32[2,15,32,256]{3,2,1,0:T(8,128)S(1)}) custom-call(f32[16,80,256]{2,1,0:T(8,128)S(1)} %copy-done, f32[16,80,256]{2,1,0:T(8,128)S(1)} %copy-done.1, f32[16,32,256]{2,1,0:T(8,128)S(1)} %get-tuple-element.124.refs_3_.refs_2_, ...), custom_call_target="tpu_custom_call" | custom-call | tf_op jit(solution)/shard_map/ratio/pallas_call | solution.py:472
  156.2 3.6 %collective-permute-start.34 = (f32[2,15,32,256]{3,2,1,0:T(8,128)S(1)}, f32[2,15,32,256]{3,2,1,0:T(8,128)S(1)}, u32[]{:S(2)}, u32[]{:S(2)}) collective-permute-start(f32[2,15,32,256]{3,2,1,0:T(8,128)S(1)} %get-tuple-element.141), channel_id=1, source_target_pairs={{2,8},{3,9},{4,10},{5,11},{6,12},{7,13},{8,2},{9,3},{10,4},{11,5},... | collective-permute-start | bytes 2949128 | tf_op jit(solution)/shard_map/ppermute | solution.py:34
  159.9 4.7 %collective-permute-done.28.refs_0_.refs_3_ = f32[2,15,32,256]{3,2,1,0:T(8,128)S(1)} collective-permute-done((f32[2,15,32,256]{3,2,1,0:T(8,128)S(1)}, f32[2,15,32,256]{3,2,1,0:T(8,128)S(1)}, u32[]{:S(2)}, u32[]{:S(2)}) %collective-permute-start.28) | collective-permute-done | bytes 983072 | tf_op jit(solution)/shard_map/ppermute | solution.py:34
  164.6 1.7 log_factor.8.refs_0_
  167.0 3.1 %collective-permute-start.31 = (f32[16,32,256]{2,1,0:T(8,128)S(1)}, f32[16,32,256]{2,1,0:T(8,128)S(1)}, u32[]{:S(2)}, u32[]{:S(2)}) collective-permute-start(f32[16,32,256]{2,1,0:T(8,128)S(1)} %log_factor.8.refs_0_), channel_id=1, source_target_pairs={{1,24},{3,26},{5,28},{7,30},{8,17},{10,19},{12,21},{14,23},{17,8},... | collective-permute-start | bytes 1572872 | tf_op jit(solution)/shard_map/ppermute | solution.py:34
  170.2 2.4 %collective-permute-start.32 = (f32[16,32,256]{2,1,0:T(8,128)S(1)}, f32[16,32,256]{2,1,0:T(8,128)S(1)}, u32[]{:S(2)}, u32[]{:S(2)}) collective-permute-start(f32[16,32,256]{2,1,0:T(8,128)S(1)} %log_factor.8.refs_0_), channel_id=1, source_target_pairs={{1,8},{3,10},{5,12},{7,14},{8,1},{10,3},{12,5},{14,7},{17,24},{19,... | collective-permute-start | bytes 1572872 | tf_op jit(solution)/shard_map/ppermute | solution.py:34
  172.6 2.6 %collective-permute-done.34.refs_0_.refs_3_ = f32[2,15,32,256]{3,2,1,0:T(8,128)S(1)} collective-permute-done((f32[2,15,32,256]{3,2,1,0:T(8,128)S(1)}, f32[2,15,32,256]{3,2,1,0:T(8,128)S(1)}, u32[]{:S(2)}, u32[]{:S(2)}) %collective-permute-start.34) | collective-permute-done | bytes 983072 | tf_op jit(solution)/shard_map/ppermute | solution.py:34
  175.2 1.7 log_factor.9.refs_0_
  177.6 3.1 %collective-permute-start.37 = (f32[16,32,256]{2,1,0:T(8,128)S(1)}, f32[16,32,256]{2,1,0:T(8,128)S(1)}, u32[]{:S(2)}, u32[]{:S(2)}) collective-permute-start(f32[16,32,256]{2,1,0:T(8,128)S(1)} %log_factor.9.refs_0_), channel_id=1, source_target_pairs={{1,24},{3,26},{5,28},{7,30},{8,17},{10,19},{12,21},{14,23},{17,8},... | collective-permute-start | bytes 1572872 | tf_op jit(solution)/shard_map/ppermute | solution.py:34
  180.7 2.4 %collective-permute-start.38 = (f32[16,32,256]{2,1,0:T(8,128)S(1)}, f32[16,32,256]{2,1,0:T(8,128)S(1)}, u32[]{:S(2)}, u32[]{:S(2)}) collective-permute-start(f32[16,32,256]{2,1,0:T(8,128)S(1)} %log_factor.9.refs_0_), channel_id=1, source_target_pairs={{1,8},{3,10},{5,12},{7,14},{8,1},{10,3},{12,5},{14,7},{17,24},{19,... | collective-permute-start | bytes 1572872 | tf_op jit(solution)/shard_map/ppermute | solution.py:34
  183.6 3.4 %collective-permute-done.32.refs_3_ = f32[16,32,256]{2,1,0:T(8,128)S(1)} collective-permute-done((f32[16,32,256]{2,1,0:T(8,128)S(1)}, f32[16,32,256]{2,1,0:T(8,128)S(1)}, u32[]{:S(2)}, u32[]{:S(2)}) %collective-permute-start.32) | collective-permute-done | bytes 524320 | tf_op jit(solution)/shard_map/ppermute | solution.py:34
  187.2 7.0 %collective-permute-done.37.refs_2_ = f32[16,32,256]{2,1,0:T(8,128)S(1)} collective-permute-done((f32[16,32,256]{2,1,0:T(8,128)S(1)}, f32[16,32,256]{2,1,0:T(8,128)S(1)}, u32[]{:S(2)}, u32[]{:S(2)}) %collective-permute-start.37) | collective-permute-done | bytes 524320 | tf_op jit(solution)/shard_map/ppermute | solution.py:34
  194.3 2.1 %collective-permute-done.38.refs_3_ = f32[16,32,256]{2,1,0:T(8,128)S(1)} collective-permute-done((f32[16,32,256]{2,1,0:T(8,128)S(1)}, f32[16,32,256]{2,1,0:T(8,128)S(1)}, u32[]{:S(2)}, u32[]{:S(2)}) %collective-permute-start.38) | collective-permute-done | bytes 524320 | tf_op jit(solution)/shard_map/ppermute | solution.py:34
  196.6 1.9 collective-permute-done.39.refs_3_
  (115 shorter events, 34.7 us)
Async XLA Ops:
  1.6 6.8 %copy-start.20 = (f32[1,61]{1,0:T(1,128)S(1)}, f32[1,61]{1,0:T(1,128)}, u32[]{:S(2)}) copy-start(f32[1,61]{1,0:T(1,128)} %param.13) | copy-start | bytes 736
  1.6 6.8 %copy-start.21 = (f32[1,31]{1,0:T(1,128)S(1)}, f32[1,31]{1,0:T(1,128)}, u32[]{:S(2)}) copy-start(f32[1,31]{1,0:T(1,128)} %param.12) | copy-start | bytes 376
  1.6 6.8 %copy-start.22 = (f32[1,31]{1,0:T(1,128)S(1)}, f32[1,31]{1,0:T(1,128)}, u32[]{:S(2)}) copy-start(f32[1,31]{1,0:T(1,128)} %param.11) | copy-start | bytes 376
  1.6 13.9 %copy-start.18 = (s32[1,3]{1,0:T(1,128)S(1)}, s32[1,3]{1,0:T(1,128)}, u32[]{:S(2)}) copy-start(s32[1,3]{1,0:T(1,128)} %offsets_ref.1) | copy-start | bytes 40
  4.1 21.4 %collective-permute-start.2 = (f32[16,96,256]{2,1,0:T(8,128)}, f32[16,96,256]{2,1,0:T(8,128)S(1)}, u32[]{:S(2)}, u32[]{:S(2)}) collective-permute-start(f32[16,96,256]{2,1,0:T(8,128)} %get-tuple-element.84), channel_id=1, source_target_pairs={{0,1},{2,3},{4,5},{6,7},{9,8},{11,10},{13,12},{15,14},{16,17},{18,... | collective-permute-start | bytes 4718600 | tf_op jit(solution)/shard_map/ppermute | solution.py:34
  5.4 8.7 %collective-permute-start.1 = (f32[1,16,128]{2,1,0:T(8,128)S(1)}, f32[1,16,128]{2,1,0:T(8,128)}, u32[]{:S(2)}, u32[]{:S(2)}) collective-permute-start(f32[1,16,128]{2,1,0:T(8,128)S(1)} %convert_element_type.14), channel_id=1, source_target_pairs={{0,8},{1,9},{2,10},{3,11},{4,12},{5,13},{6,14},{7,15},{8,0},{9,1},... | collective-permute-start | bytes 24584 | tf_op jit(solution)/shard_map/ppermute | solution.py:34
  8.4 1.2 collective-permute-start
  17.1 9.5 %copy-start.5 = (f32[16,96,256]{2,1,0:T(8,128)S(1)}, f32[16,96,256]{2,1,0:T(8,128)}, u32[]{:S(2)}) copy-start(f32[16,96,256]{2,1,0:T(8,128)} %copy-done.4) | copy-start | bytes 4718596
  21.6 21.7 %collective-permute-start.4 = (f32[16,80,256]{2,1,0:T(8,128)}, f32[16,80,256]{2,1,0:T(8,128)}, u32[]{:S(2)}, u32[]{:S(2)}) collective-permute-start(f32[16,80,256]{2,1,0:T(8,128)} %get-tuple-element.87), channel_id=1, source_target_pairs={{1,8},{3,10},{5,12},{7,14},{8,1},{10,3},{12,5},{14,7},{17,24},{19,... | collective-permute-start | bytes 3932168 | tf_op jit(solution)/shard_map/ppermute | solution.py:34
  29.4 29.6 %collective-permute-start.9 = (f32[15,96,256]{2,1,0:T(8,128)}, f32[15,96,256]{2,1,0:T(8,128)}, u32[]{:S(2)}, u32[]{:S(2)}) collective-permute-start(f32[15,96,256]{2,1,0:T(8,128)} %get-tuple-element.89), channel_id=1, source_target_pairs={{2,8},{3,9},{4,10},{5,11},{6,12},{7,13},{8,2},{9,3},{10,4},{11,5},... | collective-permute-start | bytes 4423688 | tf_op jit(solution)/shard_map/ppermute | solution.py:34
  35.1 20.3 %collective-permute-start.12 = (f32[16,80,256]{2,1,0:T(8,128)}, f32[16,80,256]{2,1,0:T(8,128)}, u32[]{:S(2)}, u32[]{:S(2)}) collective-permute-start(f32[16,80,256]{2,1,0:T(8,128)} %get-tuple-element.100), channel_id=1, source_target_pairs={{0,1},{1,9},{2,3},{3,11},{4,5},{5,13},{6,7},{7,15},{8,0},{9,8},{10... | collective-permute-start | bytes 3932168 | tf_op jit(solution)/shard_map/ppermute | solution.py:34
  35.2 9.6 %collective-permute-start.3 = (f32[1,3]{1,0:T(1,128)S(1)}, f32[1,3]{1,0:T(1,128)S(1)}, u32[]{:S(2)}, u32[]{:S(2)}) collective-permute-start(f32[1,3]{1,0:T(1,128)S(1)} %convert_element_type.15), channel_id=1, source_target_pairs={{0,8},{1,9},{2,10},{3,11},{4,12},{5,13},{6,14},{7,15},{8,0},{9,1},... | collective-permute-start | bytes 44 | tf_op jit(solution)/shard_map/ppermute | solution.py:34
  36.4 19.0 %collective-permute-start.7 = (f32[2,16,128]{2,1,0:T(8,128)}, f32[2,16,128]{2,1,0:T(8,128)S(1)}, u32[]{:S(2)}, u32[]{:S(2)}) collective-permute-start(f32[2,16,128]{2,1,0:T(8,128)} %maximum_select_fusion), channel_id=1, source_target_pairs={{0,1},{1,0},{2,3},{3,2},{4,5},{5,4},{6,7},{7,6},{8,9},{9,8},{10,11... | collective-permute-start | bytes 49160 | tf_op jit(solution)/shard_map/ppermute | solution.py:34
  43.3 21.0 %collective-permute-start.8 = (f32[15,96,256]{2,1,0:T(8,128)S(1)}, f32[15,96,256]{2,1,0:T(8,128)S(1)}, u32[]{:S(2)}, u32[]{:S(2)}) collective-permute-start(f32[15,96,256]{2,1,0:T(8,128)S(1)} %constant_dynamic-slice_fusion.2), channel_id=1, source_target_pairs={{0,8},{1,9},{2,10},{3,11},{4,12},{5,13},{6,14},{7,15},{8,0},{9,1},... | collective-permute-start | bytes 4423688 | tf_op jit(solution)/shard_map/ppermute | solution.py:34
  44.8 24.4 %collective-permute-start.5 = (f32[16,80,256]{2,1,0:T(8,128)S(1)}, f32[16,80,256]{2,1,0:T(8,128)S(1)}, u32[]{:S(2)}, u32[]{:S(2)}) collective-permute-start(f32[16,80,256]{2,1,0:T(8,128)S(1)} %broadcast_select_fusion.own_ref), channel_id=1, source_target_pairs={{2,8},{3,9},{4,10},{5,11},{6,12},{7,13},{8,2},{9,3},{10,4},{11,5},... | collective-permute-start | bytes 3932168 | tf_op jit(solution)/shard_map/ppermute | solution.py:34
  55.4 13.9 %collective-permute-start.6 = (f32[16,80,256]{2,1,0:T(8,128)S(1)}, f32[16,80,256]{2,1,0:T(8,128)S(1)}, u32[]{:S(2)}, u32[]{:S(2)}) collective-permute-start(f32[16,80,256]{2,1,0:T(8,128)S(1)} %broadcast_select_fusion.own_ref), channel_id=1, source_target_pairs={{0,8},{1,9},{2,10},{3,11},{4,12},{5,13},{6,14},{7,15},{8,0},{9,1},... | collective-permute-start | bytes 3932168 | tf_op jit(solution)/shard_map/ppermute | solution.py:34
  55.4 27.2 %collective-permute-start.13 = (f32[16,80,256]{2,1,0:T(8,128)}, f32[16,80,256]{2,1,0:T(8,128)S(1)}, u32[]{:S(2)}, u32[]{:S(2)}) collective-permute-start(f32[16,80,256]{2,1,0:T(8,128)} %collective-permute-done.12.own_ref), channel_id=1, source_target_pairs={{2,8},{3,9},{4,10},{5,11},{6,12},{7,13},{8,2},{9,3},{10,4},{11,5},... | collective-permute-start | bytes 3932168 | tf_op jit(solution)/shard_map/ppermute | solution.py:34
  59.0 23.6 %collective-permute-start.14 = (f32[16,80,256]{2,1,0:T(8,128)}, f32[16,80,256]{2,1,0:T(8,128)S(1)}, u32[]{:S(2)}, u32[]{:S(2)}) collective-permute-start(f32[16,80,256]{2,1,0:T(8,128)} %collective-permute-done.12.own_ref), channel_id=1, source_target_pairs={{0,8},{1,9},{2,10},{3,11},{4,12},{5,13},{6,14},{7,15},{8,0},{9,1},... | collective-permute-start | bytes 3932168 | tf_op jit(solution)/shard_map/ppermute | solution.py:34
  72.4 20.8 %collective-permute-start.10 = (f32[15,64,256]{2,1,0:T(8,128)S(1)}, f32[15,64,256]{2,1,0:T(8,128)S(1)}, u32[]{:S(2)}, u32[]{:S(2)}) collective-permute-start(f32[15,64,256]{2,1,0:T(8,128)S(1)} %get-tuple-element.96), channel_id=1, source_target_pairs={{2,8},{3,9},{4,10},{5,11},{6,12},{7,13},{8,2},{9,3},{10,4},{11,5},... | collective-permute-start | bytes 2949128 | tf_op jit(solution)/shard_map/ppermute | solution.py:34
  75.1 18.1 %collective-permute-start.11 = (f32[15,64,256]{2,1,0:T(8,128)S(1)}, f32[15,64,256]{2,1,0:T(8,128)S(1)}, u32[]{:S(2)}, u32[]{:S(2)}) collective-permute-start(f32[15,64,256]{2,1,0:T(8,128)S(1)} %get-tuple-element.97), channel_id=1, source_target_pairs={{0,8},{1,9},{2,10},{3,11},{4,12},{5,13},{6,14},{7,15},{8,0},{9,1},... | collective-permute-start | bytes 2949128 | tf_op jit(solution)/shard_map/ppermute | solution.py:34
  86.9 11.2 %collective-permute-start.18 = (f32[15,32,256]{2,1,0:T(8,128)S(1)}, f32[15,32,256]{2,1,0:T(8,128)S(1)}, u32[]{:S(2)}, u32[]{:S(2)}) collective-permute-start(f32[15,32,256]{2,1,0:T(8,128)S(1)} %get-tuple-element.109), channel_id=1, source_target_pairs={{2,8},{3,9},{4,10},{5,11},{6,12},{7,13},{8,2},{9,3},{10,4},{11,5},... | collective-permute-start | bytes 1474568 | tf_op jit(solution)/shard_map/ppermute | solution.py:34
  90.3 7.9 %collective-permute-start.19 = (f32[15,32,256]{2,1,0:T(8,128)S(1)}, f32[15,32,256]{2,1,0:T(8,128)S(1)}, u32[]{:S(2)}, u32[]{:S(2)}) collective-permute-start(f32[15,32,256]{2,1,0:T(8,128)S(1)} %get-tuple-element.110), channel_id=1, source_target_pairs={{0,8},{1,9},{2,10},{3,11},{4,12},{5,13},{6,14},{7,15},{8,0},{9,1},... | collective-permute-start | bytes 1474568 | tf_op jit(solution)/shard_map/ppermute | solution.py:34
  99.2 13.4 %collective-permute-start.20 = (f32[16,32,256]{2,1,0:T(8,128)S(1)}, f32[16,32,256]{2,1,0:T(8,128)S(1)}, u32[]{:S(2)}, u32[]{:S(2)}) collective-permute-start(f32[16,32,256]{2,1,0:T(8,128)S(1)} %log_factor.7.refs_0_), channel_id=1, source_target_pairs={{0,16},{1,17},{2,18},{3,19},{4,20},{5,21},{6,22},{7,23},{8,24},{9,... | collective-permute-start | bytes 1572872 | tf_op jit(solution)/shard_map/ppermute | solution.py:34
  100.5 10.7 %collective-permute-start.15 = (f32[15,32,256]{2,1,0:T(8,128)S(1)}, f32[15,32,256]{2,1,0:T(8,128)S(1)}, u32[]{:S(2)}, u32[]{:S(2)}) collective-permute-start(f32[15,32,256]{2,1,0:T(8,128)S(1)} %get-tuple-element.102), channel_id=1, source_target_pairs={{2,8},{3,9},{4,10},{5,11},{6,12},{7,13},{8,2},{9,3},{10,4},{11,5},... | collective-permute-start | bytes 1474568 | tf_op jit(solution)/shard_map/ppermute | solution.py:34
  104.4 6.8 %collective-permute-start.16 = (f32[15,32,256]{2,1,0:T(8,128)S(1)}, f32[15,32,256]{2,1,0:T(8,128)S(1)}, u32[]{:S(2)}, u32[]{:S(2)}) collective-permute-start(f32[15,32,256]{2,1,0:T(8,128)S(1)} %get-tuple-element.103), channel_id=1, source_target_pairs={{0,8},{1,9},{2,10},{3,11},{4,12},{5,13},{6,14},{7,15},{8,0},{9,1},... | collective-permute-start | bytes 1474568 | tf_op jit(solution)/shard_map/ppermute | solution.py:34
  112.3 12.9 %collective-permute-start.17 = (f32[16,32,256]{2,1,0:T(8,128)S(1)}, f32[16,32,256]{2,1,0:T(8,128)}, u32[]{:S(2)}, u32[]{:S(2)}) collective-permute-start(f32[16,32,256]{2,1,0:T(8,128)S(1)} %log_factor.6.refs_0_), channel_id=1, source_target_pairs={{0,16},{1,17},{2,18},{3,19},{4,20},{5,21},{6,22},{7,23},{8,24},{9,... | collective-permute-start | bytes 1572872 | tf_op jit(solution)/shard_map/ppermute | solution.py:34
  113.8 15.2 %collective-permute-start.24 = (f32[16,32,256]{2,1,0:T(8,128)S(1)}, f32[16,32,256]{2,1,0:T(8,128)S(1)}, u32[]{:S(2)}, u32[]{:S(2)}) collective-permute-start(f32[16,32,256]{2,1,0:T(8,128)S(1)} %get-tuple-element.117.refs_0_.before_ref), channel_id=1, source_target_pairs={{0,1},{1,0},{2,3},{3,2},{4,5},{5,4},{6,7},{7,6},{8,9},{9,8},{10,11... | collective-permute-start | bytes 1572872 | tf_op jit(solution)/shard_map/ppermute | solution.py:34
  114.0 13.1 %collective-permute-start.21 = (f32[15,32,256]{2,1,0:T(8,128)}, f32[15,32,256]{2,1,0:T(8,128)}, u32[]{:S(2)}, u32[]{:S(2)}) collective-permute-start(f32[15,32,256]{2,1,0:T(8,128)} %get-tuple-element.111), channel_id=1, source_target_pairs={{2,8},{3,9},{4,10},{5,11},{6,12},{7,13},{8,2},{9,3},{10,4},{11,5},... | collective-permute-start | bytes 1474568 | tf_op jit(solution)/shard_map/ppermute | solution.py:34
  126.5 7.5 %collective-permute-start.23 = (f32[15,32,256]{2,1,0:T(8,128)S(1)}, f32[15,32,256]{2,1,0:T(8,128)S(1)}, u32[]{:S(2)}, u32[]{:S(2)}) collective-permute-start(f32[15,32,256]{2,1,0:T(8,128)S(1)} %get-tuple-element.113), channel_id=1, source_target_pairs={{0,8},{1,9},{2,10},{3,11},{4,12},{5,13},{6,14},{7,15},{8,0},{9,1},... | collective-permute-start | bytes 1474568 | tf_op jit(solution)/shard_map/ppermute | solution.py:34
  126.6 6.3 %collective-permute-start.27 = (f32[15,32,256]{2,1,0:T(8,128)}, f32[15,32,256]{2,1,0:T(8,128)S(1)}, u32[]{:S(2)}, u32[]{:S(2)}) collective-permute-start(f32[15,32,256]{2,1,0:T(8,128)} %get-tuple-element.121), channel_id=1, source_target_pairs={{0,8},{1,9},{2,10},{3,11},{4,12},{5,13},{6,14},{7,15},{8,0},{9,1},... | collective-permute-start | bytes 1474568 | tf_op jit(solution)/shard_map/ppermute | solution.py:34
  127.1 10.4 %collective-permute-start.22 = (f32[15,32,256]{2,1,0:T(8,128)S(1)}, f32[15,32,256]{2,1,0:T(8,128)S(1)}, u32[]{:S(2)}, u32[]{:S(2)}) collective-permute-start(f32[15,32,256]{2,1,0:T(8,128)S(1)} %get-tuple-element.112), channel_id=1, source_target_pairs={{2,8},{3,9},{4,10},{5,11},{6,12},{7,13},{8,2},{9,3},{10,4},{11,5},... | collective-permute-start | bytes 1474568 | tf_op jit(solution)/shard_map/ppermute | solution.py:34
  129.1 13.4 %collective-permute-start.25 = (f32[15,32,256]{2,1,0:T(8,128)S(1)}, f32[15,32,256]{2,1,0:T(8,128)S(1)}, u32[]{:S(2)}, u32[]{:S(2)}) collective-permute-start(f32[15,32,256]{2,1,0:T(8,128)S(1)} %get-tuple-element.146), channel_id=1, source_target_pairs={{2,8},{3,9},{4,10},{5,11},{6,12},{7,13},{8,2},{9,3},{10,4},{11,5},... | collective-permute-start | bytes 1474568 | tf_op jit(solution)/shard_map/ppermute | solution.py:34
  132.7 9.7 %collective-permute-start.26 = (f32[15,32,256]{2,1,0:T(8,128)S(1)}, f32[15,32,256]{2,1,0:T(8,128)S(1)}, u32[]{:S(2)}, u32[]{:S(2)}) collective-permute-start(f32[15,32,256]{2,1,0:T(8,128)S(1)} %get-tuple-element.145), channel_id=1, source_target_pairs={{0,8},{1,9},{2,10},{3,11},{4,12},{5,13},{6,14},{7,15},{8,0},{9,1},... | collective-permute-start | bytes 1474568 | tf_op jit(solution)/shard_map/ppermute | solution.py:34
  137.5 6.1 %copy-start.1 = (f32[16,80,256]{2,1,0:T(8,128)S(1)}, f32[16,80,256]{2,1,0:T(8,128)}, u32[]{:S(2)}) copy-start(f32[16,80,256]{2,1,0:T(8,128)} %get-tuple-element.107.refs_1_) | copy-start | bytes 3932164
  138.5 5.0 %copy-start = (f32[16,80,256]{2,1,0:T(8,128)S(1)}, f32[16,80,256]{2,1,0:T(8,128)}, u32[]{:S(2)}) copy-start(f32[16,80,256]{2,1,0:T(8,128)} %get-tuple-element.106.refs_0_) | copy-start | bytes 3932164
  138.5 5.0 %copy-start.11 = (bf16[2,48,256]{2,1,0:T(8,128)(2,1)S(1)}, bf16[2,48,256]{2,1,0:T(8,128)(2,1)}, u32[]{:S(2)}) copy-start(bf16[2,48,256]{2,1,0:T(8,128)(2,1)} %copy-done.10) | copy-start | bytes 147460
  148.8 15.8 %collective-permute-start.28 = (f32[2,15,32,256]{3,2,1,0:T(8,128)S(1)}, f32[2,15,32,256]{3,2,1,0:T(8,128)S(1)}, u32[]{:S(2)}, u32[]{:S(2)}) collective-permute-start(f32[2,15,32,256]{3,2,1,0:T(8,128)S(1)} %get-tuple-element.131), channel_id=1, source_target_pairs={{2,8},{3,9},{4,10},{5,11},{6,12},{7,13},{8,2},{9,3},{10,4},{11,5},... | collective-permute-start | bytes 2949128 | tf_op jit(solution)/shard_map/ppermute | solution.py:34
  150.8 13.8 %collective-permute-start.29 = (f32[2,15,32,256]{3,2,1,0:T(8,128)S(1)}, f32[2,15,32,256]{3,2,1,0:T(8,128)S(1)}, u32[]{:S(2)}, u32[]{:S(2)}) collective-permute-start(f32[2,15,32,256]{3,2,1,0:T(8,128)S(1)} %get-tuple-element.132), channel_id=1, source_target_pairs={{0,8},{1,9},{2,10},{3,11},{4,12},{5,13},{6,14},{7,15},{8,0},{9,1},... | collective-permute-start | bytes 2949128 | tf_op jit(solution)/shard_map/ppermute | solution.py:34
  156.2 18.9 %collective-permute-start.34 = (f32[2,15,32,256]{3,2,1,0:T(8,128)S(1)}, f32[2,15,32,256]{3,2,1,0:T(8,128)S(1)}, u32[]{:S(2)}, u32[]{:S(2)}) collective-permute-start(f32[2,15,32,256]{3,2,1,0:T(8,128)S(1)} %get-tuple-element.141), channel_id=1, source_target_pairs={{2,8},{3,9},{4,10},{5,11},{6,12},{7,13},{8,2},{9,3},{10,4},{11,5},... | collective-permute-start | bytes 2949128 | tf_op jit(solution)/shard_map/ppermute | solution.py:34
  159.8 15.3 %collective-permute-start.35 = (f32[2,15,32,256]{3,2,1,0:T(8,128)S(1)}, f32[2,15,32,256]{3,2,1,0:T(8,128)S(1)}, u32[]{:S(2)}, u32[]{:S(2)}) collective-permute-start(f32[2,15,32,256]{3,2,1,0:T(8,128)S(1)} %get-tuple-element.142), channel_id=1, source_target_pairs={{0,8},{1,9},{2,10},{3,11},{4,12},{5,13},{6,14},{7,15},{8,0},{9,1},... | collective-permute-start | bytes 2949128 | tf_op jit(solution)/shard_map/ppermute | solution.py:34
  166.3 14.4 %collective-permute-start.30 = (f32[16,32,256]{2,1,0:T(8,128)S(1)}, f32[16,32,256]{2,1,0:T(8,128)S(1)}, u32[]{:S(2)}, u32[]{:S(2)}) collective-permute-start(f32[16,32,256]{2,1,0:T(8,128)S(1)} %log_factor.8.refs_0_), channel_id=1, source_target_pairs={{0,16},{2,18},{4,20},{6,22},{9,25},{11,27},{13,29},{15,31},{16,0},... | collective-permute-start | bytes 1572872 | tf_op jit(solution)/shard_map/ppermute | solution.py:34
  167.0 16.6 %collective-permute-start.31 = (f32[16,32,256]{2,1,0:T(8,128)S(1)}, f32[16,32,256]{2,1,0:T(8,128)S(1)}, u32[]{:S(2)}, u32[]{:S(2)}) collective-permute-start(f32[16,32,256]{2,1,0:T(8,128)S(1)} %log_factor.8.refs_0_), channel_id=1, source_target_pairs={{1,24},{3,26},{5,28},{7,30},{8,17},{10,19},{12,21},{14,23},{17,8},... | collective-permute-start | bytes 1572872 | tf_op jit(solution)/shard_map/ppermute | solution.py:34
  170.2 16.8 %collective-permute-start.32 = (f32[16,32,256]{2,1,0:T(8,128)S(1)}, f32[16,32,256]{2,1,0:T(8,128)S(1)}, u32[]{:S(2)}, u32[]{:S(2)}) collective-permute-start(f32[16,32,256]{2,1,0:T(8,128)S(1)} %log_factor.8.refs_0_), channel_id=1, source_target_pairs={{1,8},{3,10},{5,12},{7,14},{8,1},{10,3},{12,5},{14,7},{17,24},{19,... | collective-permute-start | bytes 1572872 | tf_op jit(solution)/shard_map/ppermute | solution.py:34
  176.9 10.4 %collective-permute-start.36 = (f32[16,32,256]{2,1,0:T(8,128)S(1)}, f32[16,32,256]{2,1,0:T(8,128)S(1)}, u32[]{:S(2)}, u32[]{:S(2)}) collective-permute-start(f32[16,32,256]{2,1,0:T(8,128)S(1)} %log_factor.9.refs_0_), channel_id=1, source_target_pairs={{0,16},{2,18},{4,20},{6,22},{9,25},{11,27},{13,29},{15,31},{16,0},... | collective-permute-start | bytes 1572872 | tf_op jit(solution)/shard_map/ppermute | solution.py:34
  177.6 16.7 %collective-permute-start.37 = (f32[16,32,256]{2,1,0:T(8,128)S(1)}, f32[16,32,256]{2,1,0:T(8,128)S(1)}, u32[]{:S(2)}, u32[]{:S(2)}) collective-permute-start(f32[16,32,256]{2,1,0:T(8,128)S(1)} %log_factor.9.refs_0_), channel_id=1, source_target_pairs={{1,24},{3,26},{5,28},{7,30},{8,17},{10,19},{12,21},{14,23},{17,8},... | collective-permute-start | bytes 1572872 | tf_op jit(solution)/shard_map/ppermute | solution.py:34
  180.7 15.7 %collective-permute-start.38 = (f32[16,32,256]{2,1,0:T(8,128)S(1)}, f32[16,32,256]{2,1,0:T(8,128)S(1)}, u32[]{:S(2)}, u32[]{:S(2)}) collective-permute-start(f32[16,32,256]{2,1,0:T(8,128)S(1)} %log_factor.9.refs_0_), channel_id=1, source_target_pairs={{1,8},{3,10},{5,12},{7,14},{8,1},{10,3},{12,5},{14,7},{17,24},{19,... | collective-permute-start | bytes 1572872 | tf_op jit(solution)/shard_map/ppermute | solution.py:34
  187.1 9.5 %collective-permute-start.33 = (f32[16,32,256]{2,1,0:T(8,128)S(1)}, f32[16,32,256]{2,1,0:T(8,128)S(1)}, u32[]{:S(2)}, u32[]{:S(2)}) collective-permute-start(f32[16,32,256]{2,1,0:T(8,128)S(1)} %last_update.2.refs_0_), channel_id=1, source_target_pairs={{0,8},{1,9},{2,10},{3,11},{4,12},{5,13},{6,14},{7,15},{8,0},{9,1},... | collective-permute-start | bytes 1572872 | tf_op jit(solution)/shard_map/ppermute | solution.py:34
  196.5 2.0 collective-permute-start.39
  (15 other events, 27.7 us)

commit v17 on v16

--- a/solution.py
+++ b/solution.py
@@ -205,20 +205,22 @@
     return Tables(whole, inner_rows, edge_rows, tables[6:8], tables[8:10])
 
 
-def window_kernel(estimate_ref, own_ref, other_ref):
-    cells_y = estimate_ref.shape[1]
-    groups = own_ref.shape[1] // GROUP
-    for side, out_ref in ((half(), own_ref), (1 - half(), other_ref)):
-        for group in range(groups):
-            local = wide_group(group, cells_y // 2 // GROUP, groups)
-            start = pl.multiple_of(group_row(side, local, cells_y), GROUP)
-            out_ref[:, group * GROUP:(group + 1) * GROUP, :] = estimate_ref[:, pl.ds(start, GROUP), :]
-
-
-def make_windows(estimate, wide):
+def window_rows(side, groups, cells_y):
+    for group in range(groups):
+        local = wide_group(group, cells_y // 2 // GROUP, groups)
+        start = pl.multiple_of(group_row(side, local, cells_y), GROUP)
+        yield slice(group * GROUP, (group + 1) * GROUP), pl.ds(start, GROUP)
+
+
+def window_kernel(estimate_ref, out_ref):
+    for rows, source in window_rows(1 - half(), out_ref.shape[1] // GROUP, estimate_ref.shape[1]):
+        out_ref[:, rows, :] = estimate_ref[:, source, :]
+
+
+def other_window(estimate, wide):
     planes, _, cells_z = estimate.shape
     shape = jax.ShapeDtypeStruct((planes, wide, cells_z), F32)
-    return call(window_kernel, (shape, shape), [VMEM], "estimate_windows")(estimate)
+    return call(window_kernel, shape, [VMEM], "other_window")(estimate)
 
 
 def put_edges(out_ref, edge_refs):
@@ -232,10 +234,10 @@
         end -= far_ref.shape[1]
 
 
-def choose_kernel(window_ref, crossed_ref, out_ref, far_ref):
+def choose_kernel(estimate_ref, crossed_ref, out_ref, far_ref):
     straight = core() == half()
-    for p in range(out_ref.shape[0]):
-        out_ref[p] = jnp.where(straight, window_ref[p], crossed_ref[p])
+    for rows, source in window_rows(half(), out_ref.shape[1] // GROUP, estimate_ref.shape[1]):
+        out_ref[:, rows, :] = jnp.where(straight, estimate_ref[:, source, :], crossed_ref[:, rows, :])
     beyond = core() * (out_ref.shape[0] - far_ref.shape[0])
     for p in range(far_ref.shape[0]):
         far_ref[p] = out_ref[p + beyond]
@@ -247,9 +249,9 @@
     return (jax.ShapeDtypeStruct(shape, F32), *edges)
 
 
-def choose(window, crossed, radius):
-    out_shape = edge_shapes(window.shape, radius, window.shape[1:2])[:2]
-    return call(choose_kernel, out_shape, [VMEM] * 2, "estimate")(window, crossed)
+def choose(estimate, crossed, radius):
+    out_shape = edge_shapes(crossed.shape, radius, crossed.shape[1:2])[:2]
+    return call(choose_kernel, out_shape, [VMEM] * 2, "estimate")(estimate, crossed)
 
 
 def shift_kernel(offsets_ref, acq_ref, first_ref, second_ref, turned_ref):
@@ -602,11 +604,11 @@
     def neighbours(far, near):
         return send(far, to_far), send(near, to_core_partner)
 
-    window, crossed = make_windows(estimate, wide)
-    crossed = send(crossed, across(0, lambda r: 1 - r, when=lambda c, r: c == r))
+    crossing = other_window(estimate, wide)
+    crossed = send(crossing, across(0, lambda r: 1 - r, when=lambda c, r: c == r))
 
     mine = [jnp.pad(row, ((0, 0), (0, 128 - row.shape[1]))) for row in (kern_x, kern_y, kern_z)]
-    mine = after(jnp.concatenate(mine, axis=1), window)
+    mine = after(jnp.concatenate(mine, axis=1), crossing)
     other = send(mine, to_core_partner)
     taps = kern_x.shape[1], taps_y, kern_z.shape[1]
     tables = make_tables(mine, other, taps, planes, cells_y, cells_z, (own_rows, near, wide))
@@ -622,7 +624,7 @@
     first, second = shift_and_cut(offsets, acquired[0], near)
 
     arrived = send(after(first, tables.whole[0]), lambda g, c, q, r: (g, r, q, c) if c != r else None)
-    current, distant = choose(after(window, first), crossed, radius)
+    current, distant = choose(after(estimate, first), crossed, radius)
     second = send(after(second, current), lambda g, c, q, r: (g, r, q, 1 - c))
     close = lax.dynamic_slice_in_dim(current, (1 - core()) * (planes - radius), radius, 0)
     distant, close = neighbours(distant, close)
@@ -668,7 +670,7 @@
         edge_parts, inner_parts = [blur_far(tables, *chunk) for chunk in chunks]
         halo_parts = blur_near(tables, beyond, close)
         *inner_spreads, distant_inner, close_inner, passed = next_ratio(
-            images, list(zip([after(after(part, distant), halo_parts[0]) for part in inner_parts], edge_parts)), None, tables.inner, tables.z, radius, 2 * (near - own_rows), 0
+            images, list(zip([after(after(part, distant), close) for part in inner_parts], edge_parts)), None, tables.inner, tables.z, radius, 2 * (near - own_rows), 0
         )
         halo_parts = blur_far(tables, distant, halo_parts)
         inner_side = neighbours(distant_inner, close_inner)

time: 201 us -> 200 us (level)
  waiting for transfers between devices: 63 us -> 58 us
  starting transfers between devices: 67.2 us -> 70.5 us
    ppermute x40, waiting for transfers between devices: 63 us -> 58 us  [send(): return lax.ppermute(array, AXES, moves(move))]
    ppermute x40, starting transfers between devices: 67.2 us -> 70.5 us  [send(): return lax.ppermute(array, AXES, moves(move))]
    unnamed x46 -> x44, local copies, waits for them, and re-layouts: 9.39 us -> 9.82 us
  transfers between devices with their start and end apart: 40 -> 40, of which waited for: 18 -> 17; matrix products, arithmetic and copies ran while one was open for 2% -> 2% of each run, Pallas kernels for 23% -> 24%
where the time goes in v17:
time: 200 us; the launch traced here: 199 us
  starting transfers between devices  70.5 us (35%)
  waiting for transfers between devices  58 us (29%)
  Pallas kernels  55.7 us (28%)
  local copies, waits for them, and re-layouts  9.99 us (5%)
  other arithmetic  3.67 us (2%)
    ppermute x40, starting transfers between devices, send(): return lax.ppermute(array, AXES, moves(move))  70.5 us
    ppermute x40, waiting for transfers between devices, send(): return lax.ppermute(array, AXES, moves(move))  58 us
    pallas_call x8, Pallas kernels, blur_x(): call(kernel, (shape, shape), [VMEM] * len(operands), 'blur_x_far' if far...  15.2 us
    unnamed x44, local copies, waits for them, and re-layouts  9.82 us
    pallas_call x2, Pallas kernels, next_ratio(): return call(kernel, out_shape, [VMEM] * len(operands), 'ratio')(*operands)  9.34 us
    pallas_call x5, Pallas kernels, log_factor(): call(kernel, shape, [VMEM] * (3 + len(parts)), 'log_factor')  7.68 us
    pallas_call x2, Pallas kernels, first_ratio(): call(kernel, out_shape, in_specs, 'image_and_ratio', scratch, hbm=(len(ou...  7.37 us
    pallas_call x1, Pallas kernels, shift_and_cut(): call(shift_kernel, (shape, shape), [SMEM, VMEM], 'shift_recorded', scratch)  4.47 us
  transfers between devices with their start and end apart: 40, of which 17 were waited for; matrix products, arithmetic and copies ran while one was open for 2% of the time, Pallas kernels for 24%

profile of v17, /device:TPU:17, one launch (start us, length us, event | category | flops | bytes accessed | tf_op | source)
XLA Modules:
  0.0 198.7 jit_solution(12095234530575238873)
XLA Ops:
  0.0 1.6 copy-done
  4.2 3.0 %collective-permute-start.1 = (f32[1,16,128]{2,1,0:T(8,128)S(1)}, f32[1,16,128]{2,1,0:T(8,128)}, u32[]{:S(2)}, u32[]{:S(2)}) collective-permute-start(f32[1,16,128]{2,1,0:T(8,128)S(1)} %convert_element_type.14), channel_id=1, source_target_pairs={{0,8},{1,9},{2,10},{3,11},{4,12},{5,13},{6,14},{7,15},{8,0},{9,1},... | collective-permute-start | bytes 24584 | tf_op jit(solution)/shard_map/ppermute | solution.py:34
  8.4 2.0 %band_matrices.1 = (bf16[2,80,384]{2,1,0:T(8,128)(2,1)S(1)}, bf16[2,64,256]{2,1,0:T(8,128)(2,1)S(1)}, bf16[2,48,256]{2,1,0:T(8,128)(2,1)S(1)}, bf16[2,32,256]{2,...) custom-call(f32[1,384]{1,0:T(1,128)S(1)} %fusion.1.mine_ref, ...), custom_call_target="tpu_custom_call" | custom-call | tf_op jit(solution)/shard_map/band_matrices/pallas_call | solution.py:203
  14.3 1.6 copy-done.4
  15.9 4.5 %shift_recorded.1 = (f32[16,80,256]{2,1,0:T(8,128)}, f32[16,80,256]{2,1,0:T(8,128)}) custom-call(s32[1,3]{1,0:T(1,128)S(1)} %copy-done.17, f32[16,128,256]{2,1,0:T(8,128)S(1)} %bitcast.1), custom_call_target="tpu_custom_call" | custom-call | tf_op jit(solution)/shard_map/shift_recorded/pallas_call | solution.py:283
  20.3 1.9 collective-permute-start.4
  22.2 2.0 %collective-permute-done.2.crossed_ref = f32[16,96,256]{2,1,0:T(8,128)S(1)} collective-permute-done((f32[16,96,256]{2,1,0:T(8,128)}, f32[16,96,256]{2,1,0:T(8,128)S(1)}, u32[]{:S(2)}, u32[]{:S(2)}) %collective-permute-start.2) | collective-permute-done | bytes 1572896 | tf_op jit(solution)/shard_map/ppermute | solution.py:34
  25.4 1.6 copy-done.1
  29.7 5.7 %collective-permute-start.9 = (f32[15,96,256]{2,1,0:T(8,128)}, f32[15,96,256]{2,1,0:T(8,128)}, u32[]{:S(2)}, u32[]{:S(2)}) collective-permute-start(f32[15,96,256]{2,1,0:T(8,128)} %get-tuple-element.85), channel_id=1, source_target_pairs={{2,8},{3,9},{4,10},{5,11},{6,12},{7,13},{8,2},{9,3},{10,4},{11,5},... | collective-permute-start | bytes 4423688 | tf_op jit(solution)/shard_map/ppermute | solution.py:34
  38.2 2.2 %collective-permute-done.4 = f32[16,80,256]{2,1,0:T(8,128)} collective-permute-done((f32[16,80,256]{2,1,0:T(8,128)}, f32[16,80,256]{2,1,0:T(8,128)}, u32[]{:S(2)}, u32[]{:S(2)}) %collective-permute-start.4) | collective-permute-done | bytes 1310752 | tf_op jit(solution)/shard_map/ppermute | solution.py:34
  42.0 8.2 %collective-permute-start.5 = (f32[16,80,256]{2,1,0:T(8,128)S(1)}, f32[16,80,256]{2,1,0:T(8,128)S(1)}, u32[]{:S(2)}, u32[]{:S(2)}) collective-permute-start(f32[16,80,256]{2,1,0:T(8,128)S(1)} %broadcast_select_fusion.own_ref), channel_id=1, source_target_pairs={{2,8},{3,9},{4,10},{5,11},{6,12},{7,13},{8,2},{9,3},{10,4},{11,5},... | collective-permute-start | bytes 3932168 | tf_op jit(solution)/shard_map/ppermute | solution.py:34
  50.2 4.0 %collective-permute-done.7 = f32[2,16,128]{2,1,0:T(8,128)S(1)} collective-permute-done((f32[2,16,128]{2,1,0:T(8,128)}, f32[2,16,128]{2,1,0:T(8,128)S(1)}, u32[]{:S(2)}, u32[]{:S(2)}) %collective-permute-start.7) | collective-permute-done | bytes 16416 | tf_op jit(solution)/shard_map/ppermute | solution.py:34
  54.1 3.6 %collective-permute-start.13 = (f32[16,80,256]{2,1,0:T(8,128)}, f32[16,80,256]{2,1,0:T(8,128)S(1)}, u32[]{:S(2)}, u32[]{:S(2)}) collective-permute-start(f32[16,80,256]{2,1,0:T(8,128)} %collective-permute-done.12.own_ref), channel_id=1, source_target_pairs={{2,8},{3,9},{4,10},{5,11},{6,12},{7,13},{8,2},{9,3},{10,4},{11,5},... | collective-permute-start | bytes 3932168 | tf_op jit(solution)/shard_map/ppermute | solution.py:34
  58.6 4.4 %blur_x_far.4 = (f32[16,96,256]{2,1,0:T(8,128)S(1)}, f32[16,96,256]{2,1,0:T(8,128)S(1)}) custom-call(bf16[2,256,384]{2,1,0:T(8,128)(2,1)S(1)} %get-tuple-element.74.hi_ref, bf16[2,256,384]{2,1,0:T(8,128)(2,1)S(1)} %get-tuple-element.75.lo_ref, f32[15,96,256]{2,1,0:T(8,128)} %collective-permute-done.9.refs_0_), custom_call_target="tpu_custom_call" | custom-call | tf_op jit(solution)/shard_map/blur_x_far/pallas_call | solution.py:331
  63.1 3.3 %blur_x_near.4 = (f32[16,96,256]{2,1,0:T(8,128)S(1)}, f32[16,96,256]{2,1,0:T(8,128)S(1)}) custom-call(bf16[2,256,384]{2,1,0:T(8,128)(2,1)S(1)} %get-tuple-element.74.hi_ref, bf16[2,256,384]{2,1,0:T(8,128)(2,1)S(1)} %get-tuple-element.75.lo_ref, f32[16,96,256]{2,1,0:T(8,128)S(1)} %get-tuple-element.81.refs_0_.before_ref, ...), custom_call_target="tpu_custom_call" | custom-call | tf_op jit(solution)/shard_map/blur_x_near/pallas_call | solution.py:331
  68.0 3.1 %image_and_ratio.2 = (f32[16,64,256]{2,1,0:T(8,128)S(1)}, f32[15,64,256]{2,1,0:T(8,128)S(1)}, f32[15,64,256]{2,1,0:T(8,128)S(1)}, f32[16,80,256]{2,1,0:T(8,128)}) custom-call(s32[2,3]{1,0:T(2,128)S(1)} %fusion.2.shift_ref, f32[16,80,256]{2,1,0:T(8,128)S(1)} %collective-permute-done.5.far_ref, f32[16,80,256]{2,1,0:T(8,128)S(1)} %collective-permute-done.6.near_ref, ...), custom_call_target="tpu_custom_call" | custom-call | tf_op jit(solution)/shard_map/image_and_ratio/pallas_call | solution.py:486
  71.1 2.4 %collective-permute-start.10 = (f32[15,64,256]{2,1,0:T(8,128)S(1)}, f32[15,64,256]{2,1,0:T(8,128)S(1)}, u32[]{:S(2)}, u32[]{:S(2)}) collective-permute-start(f32[15,64,256]{2,1,0:T(8,128)S(1)} %get-tuple-element.92), channel_id=1, source_target_pairs={{2,8},{3,9},{4,10},{5,11},{6,12},{7,13},{8,2},{9,3},{10,4},{11,5},... | collective-permute-start | bytes 2949128 | tf_op jit(solution)/shard_map/ppermute | solution.py:34
  75.3 5.9 %collective-permute-done.13.far_ref = f32[16,80,256]{2,1,0:T(8,128)S(1)} collective-permute-done((f32[16,80,256]{2,1,0:T(8,128)}, f32[16,80,256]{2,1,0:T(8,128)S(1)}, u32[]{:S(2)}, u32[]{:S(2)}) %collective-permute-start.13) | collective-permute-done | bytes 1310752 | tf_op jit(solution)/shard_map/ppermute | solution.py:34
  81.1 4.3 %image_and_ratio.3 = (f32[16,64,256]{2,1,0:T(8,128)S(1)}, f32[15,32,256]{2,1,0:T(8,128)S(1)}, f32[15,32,256]{2,1,0:T(8,128)S(1)}, f32[15,32,256]{2,1,0:T(8,128)S...) custom-call(s32[2,3]{1,0:T(2,128)S(1)} %fusion.2.shift_ref, f32[16,80,256]{2,1,0:T(8,128)S(1)} %collective-permute-done.13.far_ref, ...), custom_call_target="tpu_custom_call" | custom-call | tf_op jit(solution)/shard_map/image_and_ratio/pallas_call | solution.py:486
  85.4 3.3 %collective-permute-start.18 = (f32[15,32,256]{2,1,0:T(8,128)S(1)}, f32[15,32,256]{2,1,0:T(8,128)S(1)}, u32[]{:S(2)}, u32[]{:S(2)}) collective-permute-start(f32[15,32,256]{2,1,0:T(8,128)S(1)} %get-tuple-element.105), channel_id=1, source_target_pairs={{2,8},{3,9},{4,10},{5,11},{6,12},{7,13},{8,2},{9,3},{10,4},{11,5},... | collective-permute-start | bytes 1474568 | tf_op jit(solution)/shard_map/ppermute | solution.py:34
  88.8 2.8 %collective-permute-done.10.refs_0_ = f32[15,64,256]{2,1,0:T(8,128)S(1)} collective-permute-done((f32[15,64,256]{2,1,0:T(8,128)S(1)}, f32[15,64,256]{2,1,0:T(8,128)S(1)}, u32[]{:S(2)}, u32[]{:S(2)}) %collective-permute-start.10) | collective-permute-done | bytes 983072 | tf_op jit(solution)/shard_map/ppermute | solution.py:34
  91.6 2.2 %log_factor.5.before_ref = f32[16,64,256]{2,1,0:T(8,128)S(1)} custom-call(bf16[2,256,384]{2,1,0:T(8,128)(2,1)S(1)} %get-tuple-element.74.hi_ref, bf16[2,256,384]{2,1,0:T(8,128)(2,1)S(1)} %get-tuple-element.75.lo_ref, f32[16,96,256]{2,1,0:T(8,128)S(1)} %get-tuple-element.81.refs_0_.before_ref, f32[15,64,256]{2,1,0:T(8,128)S(1)} %collective-permute-done.10.refs_0_, ...), custom_call_target="tpu_custom_call" | custom-call | tf_op jit(solution)/shard_map/log_factor/pallas_call | solution.py:519
  93.8 3.0 %collective-permute-done.18.refs_0_ = f32[15,32,256]{2,1,0:T(8,128)S(1)} collective-permute-done((f32[15,32,256]{2,1,0:T(8,128)S(1)}, f32[15,32,256]{2,1,0:T(8,128)S(1)}, u32[]{:S(2)}, u32[]{:S(2)}) %collective-permute-start.18) | collective-permute-done | bytes 491552 | tf_op jit(solution)/shard_map/ppermute | solution.py:34
  99.1 3.8 %collective-permute-start.15 = (f32[15,32,256]{2,1,0:T(8,128)S(1)}, f32[15,32,256]{2,1,0:T(8,128)S(1)}, u32[]{:S(2)}, u32[]{:S(2)}) collective-permute-start(f32[15,32,256]{2,1,0:T(8,128)S(1)} %get-tuple-element.98), channel_id=1, source_target_pairs={{2,8},{3,9},{4,10},{5,11},{6,12},{7,13},{8,2},{9,3},{10,4},{11,5},... | collective-permute-start | bytes 1474568 | tf_op jit(solution)/shard_map/ppermute | solution.py:34
  103.0 6.7 %collective-permute-done.15.refs_0_ = f32[15,32,256]{2,1,0:T(8,128)S(1)} collective-permute-done((f32[15,32,256]{2,1,0:T(8,128)S(1)}, f32[15,32,256]{2,1,0:T(8,128)S(1)}, u32[]{:S(2)}, u32[]{:S(2)}) %collective-permute-start.15) | collective-permute-done | bytes 491552 | tf_op jit(solution)/shard_map/ppermute | solution.py:34
  112.2 2.1 %collective-permute-start.24 = (f32[16,32,256]{2,1,0:T(8,128)S(1)}, f32[16,32,256]{2,1,0:T(8,128)S(1)}, u32[]{:S(2)}, u32[]{:S(2)}) collective-permute-start(f32[16,32,256]{2,1,0:T(8,128)S(1)} %get-tuple-element.113.refs_0_.before_ref), channel_id=1, source_target_pairs={{0,1},{1,0},{2,3},{3,2},{4,5},{5,4},{6,7},{7,6},{8,9},{9,8},{10,11... | collective-permute-start | bytes 1572872 | tf_op jit(solution)/shard_map/ppermute | solution.py:34
  114.3 4.1 %collective-permute-start.21 = (f32[15,32,256]{2,1,0:T(8,128)}, f32[15,32,256]{2,1,0:T(8,128)}, u32[]{:S(2)}, u32[]{:S(2)}) collective-permute-start(f32[15,32,256]{2,1,0:T(8,128)} %get-tuple-element.107), channel_id=1, source_target_pairs={{2,8},{3,9},{4,10},{5,11},{6,12},{7,13},{8,2},{9,3},{10,4},{11,5},... | collective-permute-start | bytes 1474568 | tf_op jit(solution)/shard_map/ppermute | solution.py:34
  118.4 5.8 %collective-permute-done.17.refs_1_ = f32[16,32,256]{2,1,0:T(8,128)} collective-permute-done((f32[16,32,256]{2,1,0:T(8,128)S(1)}, f32[16,32,256]{2,1,0:T(8,128)}, u32[]{:S(2)}, u32[]{:S(2)}) %collective-permute-start.17) | collective-permute-done | bytes 524320 | tf_op jit(solution)/shard_map/ppermute | solution.py:34
  126.6 2.0 %collective-permute-start.22 = (f32[15,32,256]{2,1,0:T(8,128)S(1)}, f32[15,32,256]{2,1,0:T(8,128)S(1)}, u32[]{:S(2)}, u32[]{:S(2)}) collective-permute-start(f32[15,32,256]{2,1,0:T(8,128)S(1)} %get-tuple-element.108), channel_id=1, source_target_pairs={{2,8},{3,9},{4,10},{5,11},{6,12},{7,13},{8,2},{9,3},{10,4},{11,5},... | collective-permute-start | bytes 1474568 | tf_op jit(solution)/shard_map/ppermute | solution.py:34
  128.8 3.5 %collective-permute-start.25 = (f32[15,32,256]{2,1,0:T(8,128)S(1)}, f32[15,32,256]{2,1,0:T(8,128)S(1)}, u32[]{:S(2)}, u32[]{:S(2)}) collective-permute-start(f32[15,32,256]{2,1,0:T(8,128)S(1)} %get-tuple-element.142), channel_id=1, source_target_pairs={{2,8},{3,9},{4,10},{5,11},{6,12},{7,13},{8,2},{9,3},{10,4},{11,5},... | collective-permute-start | bytes 1474568 | tf_op jit(solution)/shard_map/ppermute | solution.py:34
  135.0 2.2 %blur_x_far.6 = (f32[16,32,256]{2,1,0:T(8,128)S(1)}, f32[16,32,256]{2,1,0:T(8,128)S(1)}) custom-call(bf16[2,256,384]{2,1,0:T(8,128)(2,1)S(1)} %get-tuple-element.74.hi_ref, bf16[2,256,384]{2,1,0:T(8,128)(2,1)S(1)} %get-tuple-element.75.lo_ref, f32[15,32,256]{2,1,0:T(8,128)} %collective-permute-done.21.refs_0_, ...), custom_call_target="tpu_custom_call" | custom-call | tf_op jit(solution)/shard_map/blur_x_far/pallas_call | solution.py:331
  138.2 3.8 %collective-permute-done.25.refs_0_ = f32[15,32,256]{2,1,0:T(8,128)S(1)} collective-permute-done((f32[15,32,256]{2,1,0:T(8,128)S(1)}, f32[15,32,256]{2,1,0:T(8,128)S(1)}, u32[]{:S(2)}, u32[]{:S(2)}) %collective-permute-start.25) | collective-permute-done | bytes 491552 | tf_op jit(solution)/shard_map/ppermute | solution.py:34
  142.1 5.2 %ratio.2 = (f32[16,32,256]{2,1,0:T(8,128)S(1)}, f32[16,32,256]{2,1,0:T(8,128)S(1)}, f32[2,15,32,256]{3,2,1,0:T(8,128)S(1)}, f32[2,15,32,256]{3,2,1,0:T(8,128)S(1)}, f32[2,16,32,256]{3,2,1,0:T(8,128)S(1)}) custom-call(f32[16,80,256]{2,1,0:T(8,128)S(1)} %copy-done.2, f32[16,80,256]{2,1,0:T(8,128)S(1)} %copy-done.3, ...), custom_call_target="tpu_custom_call" | custom-call | tf_op jit(solution)/shard_map/ratio/pallas_call | solution.py:474
  147.3 1.9 collective-permute-start.28
  152.0 4.2 %ratio.3 = (f32[16,32,256]{2,1,0:T(8,128)S(1)}, f32[16,32,256]{2,1,0:T(8,128)S(1)}, f32[2,15,32,256]{3,2,1,0:T(8,128)S(1)}, f32[2,15,32,256]{3,2,1,0:T(8,128)S(1)}) custom-call(f32[16,80,256]{2,1,0:T(8,128)S(1)} %copy-done.2, f32[16,80,256]{2,1,0:T(8,128)S(1)} %copy-done.3, f32[16,32,256]{2,1,0:T(8,128)S(1)} %get-tuple-element.119.refs_3_.refs_2_, ...), custom_call_target="tpu_custom_call" | custom-call | tf_op jit(solution)/shard_map/ratio/pallas_call | solution.py:474
  156.2 3.1 %collective-permute-start.34 = (f32[2,15,32,256]{3,2,1,0:T(8,128)S(1)}, f32[2,15,32,256]{3,2,1,0:T(8,128)S(1)}, u32[]{:S(2)}, u32[]{:S(2)}) collective-permute-start(f32[2,15,32,256]{3,2,1,0:T(8,128)S(1)} %get-tuple-element.137), channel_id=1, source_target_pairs={{2,8},{3,9},{4,10},{5,11},{6,12},{7,13},{8,2},{9,3},{10,4},{11,5},... | collective-permute-start | bytes 2949128 | tf_op jit(solution)/shard_map/ppermute | solution.py:34
  159.7 3.3 %collective-permute-done.28.refs_0_.refs_3_ = f32[2,15,32,256]{3,2,1,0:T(8,128)S(1)} collective-permute-done((f32[2,15,32,256]{3,2,1,0:T(8,128)S(1)}, f32[2,15,32,256]{3,2,1,0:T(8,128)S(1)}, u32[]{:S(2)}, u32[]{:S(2)}) %collective-permute-start.28) | collective-permute-done | bytes 983072 | tf_op jit(solution)/shard_map/ppermute | solution.py:34
  163.0 1.7 log_factor.8.refs_0_
  165.4 3.9 %collective-permute-start.31 = (f32[16,32,256]{2,1,0:T(8,128)S(1)}, f32[16,32,256]{2,1,0:T(8,128)S(1)}, u32[]{:S(2)}, u32[]{:S(2)}) collective-permute-start(f32[16,32,256]{2,1,0:T(8,128)S(1)} %log_factor.8.refs_0_), channel_id=1, source_target_pairs={{1,24},{3,26},{5,28},{7,30},{8,17},{10,19},{12,21},{14,23},{17,8},... | collective-permute-start | bytes 1572872 | tf_op jit(solution)/shard_map/ppermute | solution.py:34
  169.3 1.9 collective-permute-start.32
  171.2 2.3 %collective-permute-done.34.refs_0_.refs_3_ = f32[2,15,32,256]{3,2,1,0:T(8,128)S(1)} collective-permute-done((f32[2,15,32,256]{3,2,1,0:T(8,128)S(1)}, f32[2,15,32,256]{3,2,1,0:T(8,128)S(1)}, u32[]{:S(2)}, u32[]{:S(2)}) %collective-permute-start.34) | collective-permute-done | bytes 983072 | tf_op jit(solution)/shard_map/ppermute | solution.py:34
  173.5 1.7 log_factor.9.refs_0_
  175.9 3.9 %collective-permute-start.37 = (f32[16,32,256]{2,1,0:T(8,128)S(1)}, f32[16,32,256]{2,1,0:T(8,128)S(1)}, u32[]{:S(2)}, u32[]{:S(2)}) collective-permute-start(f32[16,32,256]{2,1,0:T(8,128)S(1)} %log_factor.9.refs_0_), channel_id=1, source_target_pairs={{1,24},{3,26},{5,28},{7,30},{8,17},{10,19},{12,21},{14,23},{17,8},... | collective-permute-start | bytes 1572872 | tf_op jit(solution)/shard_map/ppermute | solution.py:34
  179.8 1.9 collective-permute-start.38
  182.3 3.4 %collective-permute-done.32.refs_3_ = f32[16,32,256]{2,1,0:T(8,128)S(1)} collective-permute-done((f32[16,32,256]{2,1,0:T(8,128)S(1)}, f32[16,32,256]{2,1,0:T(8,128)S(1)}, u32[]{:S(2)}, u32[]{:S(2)}) %collective-permute-start.32) | collective-permute-done | bytes 524320 | tf_op jit(solution)/shard_map/ppermute | solution.py:34
  185.9 7.5 %collective-permute-done.37.refs_2_ = f32[16,32,256]{2,1,0:T(8,128)S(1)} collective-permute-done((f32[16,32,256]{2,1,0:T(8,128)S(1)}, f32[16,32,256]{2,1,0:T(8,128)S(1)}, u32[]{:S(2)}, u32[]{:S(2)}) %collective-permute-start.37) | collective-permute-done | bytes 524320 | tf_op jit(solution)/shard_map/ppermute | solution.py:34
  193.4 1.7 collective-permute-done.38.refs_3_
  195.3 1.9 collective-permute-done.39.refs_3_
  (113 shorter events, 37.9 us)
Async XLA Ops:
  1.6 5.6 %copy-start.19 = (f32[1,61]{1,0:T(1,128)S(1)}, f32[1,61]{1,0:T(1,128)}, u32[]{:S(2)}) copy-start(f32[1,61]{1,0:T(1,128)} %param.13) | copy-start | bytes 736
  1.6 5.6 %copy-start.20 = (f32[1,31]{1,0:T(1,128)S(1)}, f32[1,31]{1,0:T(1,128)}, u32[]{:S(2)}) copy-start(f32[1,31]{1,0:T(1,128)} %param.12) | copy-start | bytes 376
  1.6 5.6 %copy-start.21 = (f32[1,31]{1,0:T(1,128)S(1)}, f32[1,31]{1,0:T(1,128)}, u32[]{:S(2)}) copy-start(f32[1,31]{1,0:T(1,128)} %param.11) | copy-start | bytes 376
  1.6 12.7 %copy-start.17 = (s32[1,3]{1,0:T(1,128)S(1)}, s32[1,3]{1,0:T(1,128)}, u32[]{:S(2)}) copy-start(s32[1,3]{1,0:T(1,128)} %offsets_ref.1) | copy-start | bytes 40
  2.9 21.4 %collective-permute-start.2 = (f32[16,96,256]{2,1,0:T(8,128)}, f32[16,96,256]{2,1,0:T(8,128)S(1)}, u32[]{:S(2)}, u32[]{:S(2)}) collective-permute-start(f32[16,96,256]{2,1,0:T(8,128)} %other_window.1), channel_id=1, source_target_pairs={{0,1},{2,3},{4,5},{6,7},{9,8},{11,10},{13,12},{15,14},{16,17},{18,... | collective-permute-start | bytes 4718600 | tf_op jit(solution)/shard_map/ppermute | solution.py:34
  4.2 8.7 %collective-permute-start.1 = (f32[1,16,128]{2,1,0:T(8,128)S(1)}, f32[1,16,128]{2,1,0:T(8,128)}, u32[]{:S(2)}, u32[]{:S(2)}) collective-permute-start(f32[1,16,128]{2,1,0:T(8,128)S(1)} %convert_element_type.14), channel_id=1, source_target_pairs={{0,8},{1,9},{2,10},{3,11},{4,12},{5,13},{6,14},{7,15},{8,0},{9,1},... | collective-permute-start | bytes 24584 | tf_op jit(solution)/shard_map/ppermute | solution.py:34
  7.2 1.2 collective-permute-start
  20.3 20.1 %collective-permute-start.4 = (f32[16,80,256]{2,1,0:T(8,128)}, f32[16,80,256]{2,1,0:T(8,128)}, u32[]{:S(2)}, u32[]{:S(2)}) collective-permute-start(f32[16,80,256]{2,1,0:T(8,128)} %get-tuple-element.83), channel_id=1, source_target_pairs={{1,8},{3,10},{5,12},{7,14},{8,1},{10,3},{12,5},{14,7},{17,24},{19,... | collective-permute-start | bytes 3932168 | tf_op jit(solution)/shard_map/ppermute | solution.py:34
  29.7 28.0 %collective-permute-start.9 = (f32[15,96,256]{2,1,0:T(8,128)}, f32[15,96,256]{2,1,0:T(8,128)}, u32[]{:S(2)}, u32[]{:S(2)}) collective-permute-start(f32[15,96,256]{2,1,0:T(8,128)} %get-tuple-element.85), channel_id=1, source_target_pairs={{2,8},{3,9},{4,10},{5,11},{6,12},{7,13},{8,2},{9,3},{10,4},{11,5},... | collective-permute-start | bytes 4423688 | tf_op jit(solution)/shard_map/ppermute | solution.py:34
  35.5 18.7 %collective-permute-start.12 = (f32[16,80,256]{2,1,0:T(8,128)}, f32[16,80,256]{2,1,0:T(8,128)}, u32[]{:S(2)}, u32[]{:S(2)}) collective-permute-start(f32[16,80,256]{2,1,0:T(8,128)} %get-tuple-element.96), channel_id=1, source_target_pairs={{0,1},{1,9},{2,3},{3,11},{4,5},{5,13},{6,7},{7,15},{8,0},{9,8},{10... | collective-permute-start | bytes 3932168 | tf_op jit(solution)/shard_map/ppermute | solution.py:34
  35.5 6.4 %collective-permute-start.3 = (f32[1,3]{1,0:T(1,128)S(1)}, f32[1,3]{1,0:T(1,128)S(1)}, u32[]{:S(2)}, u32[]{:S(2)}) collective-permute-start(f32[1,3]{1,0:T(1,128)S(1)} %convert_element_type.15), channel_id=1, source_target_pairs={{0,8},{1,9},{2,10},{3,11},{4,12},{5,13},{6,14},{7,15},{8,0},{9,1},... | collective-permute-start | bytes 44 | tf_op jit(solution)/shard_map/ppermute | solution.py:34
  36.7 17.4 %collective-permute-start.7 = (f32[2,16,128]{2,1,0:T(8,128)}, f32[2,16,128]{2,1,0:T(8,128)S(1)}, u32[]{:S(2)}, u32[]{:S(2)}) collective-permute-start(f32[2,16,128]{2,1,0:T(8,128)} %maximum_select_fusion), channel_id=1, source_target_pairs={{0,1},{1,0},{2,3},{3,2},{4,5},{5,4},{6,7},{7,6},{8,9},{9,8},{10,11... | collective-permute-start | bytes 49160 | tf_op jit(solution)/shard_map/ppermute | solution.py:34
  40.5 22.6 %collective-permute-start.8 = (f32[15,96,256]{2,1,0:T(8,128)S(1)}, f32[15,96,256]{2,1,0:T(8,128)S(1)}, u32[]{:S(2)}, u32[]{:S(2)}) collective-permute-start(f32[15,96,256]{2,1,0:T(8,128)S(1)} %constant_dynamic-slice_fusion.2), channel_id=1, source_target_pairs={{0,8},{1,9},{2,10},{3,11},{4,12},{5,13},{6,14},{7,15},{8,0},{9,1},... | collective-permute-start | bytes 4423688 | tf_op jit(solution)/shard_map/ppermute | solution.py:34
  42.0 26.0 %collective-permute-start.5 = (f32[16,80,256]{2,1,0:T(8,128)S(1)}, f32[16,80,256]{2,1,0:T(8,128)S(1)}, u32[]{:S(2)}, u32[]{:S(2)}) collective-permute-start(f32[16,80,256]{2,1,0:T(8,128)S(1)} %broadcast_select_fusion.own_ref), channel_id=1, source_target_pairs={{2,8},{3,9},{4,10},{5,11},{6,12},{7,13},{8,2},{9,3},{10,4},{11,5},... | collective-permute-start | bytes 3932168 | tf_op jit(solution)/shard_map/ppermute | solution.py:34
  54.1 13.9 %collective-permute-start.6 = (f32[16,80,256]{2,1,0:T(8,128)S(1)}, f32[16,80,256]{2,1,0:T(8,128)S(1)}, u32[]{:S(2)}, u32[]{:S(2)}) collective-permute-start(f32[16,80,256]{2,1,0:T(8,128)S(1)} %broadcast_select_fusion.own_ref), channel_id=1, source_target_pairs={{0,8},{1,9},{2,10},{3,11},{4,12},{5,13},{6,14},{7,15},{8,0},{9,1},... | collective-permute-start | bytes 3932168 | tf_op jit(solution)/shard_map/ppermute | solution.py:34
  54.1 27.0 %collective-permute-start.13 = (f32[16,80,256]{2,1,0:T(8,128)}, f32[16,80,256]{2,1,0:T(8,128)S(1)}, u32[]{:S(2)}, u32[]{:S(2)}) collective-permute-start(f32[16,80,256]{2,1,0:T(8,128)} %collective-permute-done.12.own_ref), channel_id=1, source_target_pairs={{2,8},{3,9},{4,10},{5,11},{6,12},{7,13},{8,2},{9,3},{10,4},{11,5},... | collective-permute-start | bytes 3932168 | tf_op jit(solution)/shard_map/ppermute | solution.py:34
  57.7 23.4 %collective-permute-start.14 = (f32[16,80,256]{2,1,0:T(8,128)}, f32[16,80,256]{2,1,0:T(8,128)S(1)}, u32[]{:S(2)}, u32[]{:S(2)}) collective-permute-start(f32[16,80,256]{2,1,0:T(8,128)} %collective-permute-done.12.own_ref), channel_id=1, source_target_pairs={{0,8},{1,9},{2,10},{3,11},{4,12},{5,13},{6,14},{7,15},{8,0},{9,1},... | collective-permute-start | bytes 3932168 | tf_op jit(solution)/shard_map/ppermute | solution.py:34
  71.1 20.5 %collective-permute-start.10 = (f32[15,64,256]{2,1,0:T(8,128)S(1)}, f32[15,64,256]{2,1,0:T(8,128)S(1)}, u32[]{:S(2)}, u32[]{:S(2)}) collective-permute-start(f32[15,64,256]{2,1,0:T(8,128)S(1)} %get-tuple-element.92), channel_id=1, source_target_pairs={{2,8},{3,9},{4,10},{5,11},{6,12},{7,13},{8,2},{9,3},{10,4},{11,5},... | collective-permute-start | bytes 2949128 | tf_op jit(solution)/shard_map/ppermute | solution.py:34
  73.5 18.1 %collective-permute-start.11 = (f32[15,64,256]{2,1,0:T(8,128)S(1)}, f32[15,64,256]{2,1,0:T(8,128)S(1)}, u32[]{:S(2)}, u32[]{:S(2)}) collective-permute-start(f32[15,64,256]{2,1,0:T(8,128)S(1)} %get-tuple-element.93), channel_id=1, source_target_pairs={{0,8},{1,9},{2,10},{3,11},{4,12},{5,13},{6,14},{7,15},{8,0},{9,1},... | collective-permute-start | bytes 2949128 | tf_op jit(solution)/shard_map/ppermute | solution.py:34
  85.4 11.4 %collective-permute-start.18 = (f32[15,32,256]{2,1,0:T(8,128)S(1)}, f32[15,32,256]{2,1,0:T(8,128)S(1)}, u32[]{:S(2)}, u32[]{:S(2)}) collective-permute-start(f32[15,32,256]{2,1,0:T(8,128)S(1)} %get-tuple-element.105), channel_id=1, source_target_pairs={{2,8},{3,9},{4,10},{5,11},{6,12},{7,13},{8,2},{9,3},{10,4},{11,5},... | collective-permute-start | bytes 1474568 | tf_op jit(solution)/shard_map/ppermute | solution.py:34
  88.7 8.0 %collective-permute-start.19 = (f32[15,32,256]{2,1,0:T(8,128)S(1)}, f32[15,32,256]{2,1,0:T(8,128)S(1)}, u32[]{:S(2)}, u32[]{:S(2)}) collective-permute-start(f32[15,32,256]{2,1,0:T(8,128)S(1)} %get-tuple-element.106), channel_id=1, source_target_pairs={{0,8},{1,9},{2,10},{3,11},{4,12},{5,13},{6,14},{7,15},{8,0},{9,1},... | collective-permute-start | bytes 1474568 | tf_op jit(solution)/shard_map/ppermute | solution.py:34
  97.9 13.2 %collective-permute-start.20 = (f32[16,32,256]{2,1,0:T(8,128)S(1)}, f32[16,32,256]{2,1,0:T(8,128)S(1)}, u32[]{:S(2)}, u32[]{:S(2)}) collective-permute-start(f32[16,32,256]{2,1,0:T(8,128)S(1)} %log_factor.7.refs_0_), channel_id=1, source_target_pairs={{0,16},{1,17},{2,18},{3,19},{4,20},{5,21},{6,22},{7,23},{8,24},{9,... | collective-permute-start | bytes 1572872 | tf_op jit(solution)/shard_map/ppermute | solution.py:34
  99.1 10.6 %collective-permute-start.15 = (f32[15,32,256]{2,1,0:T(8,128)S(1)}, f32[15,32,256]{2,1,0:T(8,128)S(1)}, u32[]{:S(2)}, u32[]{:S(2)}) collective-permute-start(f32[15,32,256]{2,1,0:T(8,128)S(1)} %get-tuple-element.98), channel_id=1, source_target_pairs={{2,8},{3,9},{4,10},{5,11},{6,12},{7,13},{8,2},{9,3},{10,4},{11,5},... | collective-permute-start | bytes 1474568 | tf_op jit(solution)/shard_map/ppermute | solution.py:34
  102.9 6.8 %collective-permute-start.16 = (f32[15,32,256]{2,1,0:T(8,128)S(1)}, f32[15,32,256]{2,1,0:T(8,128)S(1)}, u32[]{:S(2)}, u32[]{:S(2)}) collective-permute-start(f32[15,32,256]{2,1,0:T(8,128)S(1)} %get-tuple-element.99), channel_id=1, source_target_pairs={{0,8},{1,9},{2,10},{3,11},{4,12},{5,13},{6,14},{7,15},{8,0},{9,1},... | collective-permute-start | bytes 1474568 | tf_op jit(solution)/shard_map/ppermute | solution.py:34
  110.8 13.4 %collective-permute-start.17 = (f32[16,32,256]{2,1,0:T(8,128)S(1)}, f32[16,32,256]{2,1,0:T(8,128)}, u32[]{:S(2)}, u32[]{:S(2)}) collective-permute-start(f32[16,32,256]{2,1,0:T(8,128)S(1)} %log_factor.6.refs_0_), channel_id=1, source_target_pairs={{0,16},{1,17},{2,18},{3,19},{4,20},{5,21},{6,22},{7,23},{8,24},{9,... | collective-permute-start | bytes 1572872 | tf_op jit(solution)/shard_map/ppermute | solution.py:34
  112.2 16.5 %collective-permute-start.24 = (f32[16,32,256]{2,1,0:T(8,128)S(1)}, f32[16,32,256]{2,1,0:T(8,128)S(1)}, u32[]{:S(2)}, u32[]{:S(2)}) collective-permute-start(f32[16,32,256]{2,1,0:T(8,128)S(1)} %get-tuple-element.113.refs_0_.before_ref), channel_id=1, source_target_pairs={{0,1},{1,0},{2,3},{3,2},{4,5},{5,4},{6,7},{7,6},{8,9},{9,8},{10,11... | collective-permute-start | bytes 1572872 | tf_op jit(solution)/shard_map/ppermute | solution.py:34
  114.3 12.3 %collective-permute-start.21 = (f32[15,32,256]{2,1,0:T(8,128)}, f32[15,32,256]{2,1,0:T(8,128)}, u32[]{:S(2)}, u32[]{:S(2)}) collective-permute-start(f32[15,32,256]{2,1,0:T(8,128)} %get-tuple-element.107), channel_id=1, source_target_pairs={{2,8},{3,9},{4,10},{5,11},{6,12},{7,13},{8,2},{9,3},{10,4},{11,5},... | collective-permute-start | bytes 1474568 | tf_op jit(solution)/shard_map/ppermute | solution.py:34
  125.4 8.5 %collective-permute-start.23 = (f32[15,32,256]{2,1,0:T(8,128)S(1)}, f32[15,32,256]{2,1,0:T(8,128)S(1)}, u32[]{:S(2)}, u32[]{:S(2)}) collective-permute-start(f32[15,32,256]{2,1,0:T(8,128)S(1)} %get-tuple-element.109), channel_id=1, source_target_pairs={{0,8},{1,9},{2,10},{3,11},{4,12},{5,13},{6,14},{7,15},{8,0},{9,1},... | collective-permute-start | bytes 1474568 | tf_op jit(solution)/shard_map/ppermute | solution.py:34
  126.5 6.2 %collective-permute-start.27 = (f32[15,32,256]{2,1,0:T(8,128)}, f32[15,32,256]{2,1,0:T(8,128)S(1)}, u32[]{:S(2)}, u32[]{:S(2)}) collective-permute-start(f32[15,32,256]{2,1,0:T(8,128)} %get-tuple-element.116), channel_id=1, source_target_pairs={{0,8},{1,9},{2,10},{3,11},{4,12},{5,13},{6,14},{7,15},{8,0},{9,1},... | collective-permute-start | bytes 1474568 | tf_op jit(solution)/shard_map/ppermute | solution.py:34
  126.6 10.6 %collective-permute-start.22 = (f32[15,32,256]{2,1,0:T(8,128)S(1)}, f32[15,32,256]{2,1,0:T(8,128)S(1)}, u32[]{:S(2)}, u32[]{:S(2)}) collective-permute-start(f32[15,32,256]{2,1,0:T(8,128)S(1)} %get-tuple-element.108), channel_id=1, source_target_pairs={{2,8},{3,9},{4,10},{5,11},{6,12},{7,13},{8,2},{9,3},{10,4},{11,5},... | collective-permute-start | bytes 1474568 | tf_op jit(solution)/shard_map/ppermute | solution.py:34
  128.8 13.3 %collective-permute-start.25 = (f32[15,32,256]{2,1,0:T(8,128)S(1)}, f32[15,32,256]{2,1,0:T(8,128)S(1)}, u32[]{:S(2)}, u32[]{:S(2)}) collective-permute-start(f32[15,32,256]{2,1,0:T(8,128)S(1)} %get-tuple-element.142), channel_id=1, source_target_pairs={{2,8},{3,9},{4,10},{5,11},{6,12},{7,13},{8,2},{9,3},{10,4},{11,5},... | collective-permute-start | bytes 1474568 | tf_op jit(solution)/shard_map/ppermute | solution.py:34
  132.3 9.8 %collective-permute-start.26 = (f32[15,32,256]{2,1,0:T(8,128)S(1)}, f32[15,32,256]{2,1,0:T(8,128)S(1)}, u32[]{:S(2)}, u32[]{:S(2)}) collective-permute-start(f32[15,32,256]{2,1,0:T(8,128)S(1)} %get-tuple-element.141), channel_id=1, source_target_pairs={{0,8},{1,9},{2,10},{3,11},{4,12},{5,13},{6,14},{7,15},{8,0},{9,1},... | collective-permute-start | bytes 1474568 | tf_op jit(solution)/shard_map/ppermute | solution.py:34
  135.0 7.1 %copy-start.3 = (f32[16,80,256]{2,1,0:T(8,128)S(1)}, f32[16,80,256]{2,1,0:T(8,128)}, u32[]{:S(2)}) copy-start(f32[16,80,256]{2,1,0:T(8,128)} %get-tuple-element.103.refs_1_) | copy-start | bytes 3932164
  137.2 4.9 %copy-start.2 = (f32[16,80,256]{2,1,0:T(8,128)S(1)}, f32[16,80,256]{2,1,0:T(8,128)}, u32[]{:S(2)}) copy-start(f32[16,80,256]{2,1,0:T(8,128)} %get-tuple-element.102.refs_0_) | copy-start | bytes 3932164
  137.2 4.9 %copy-start.10 = (bf16[2,48,256]{2,1,0:T(8,128)(2,1)S(1)}, bf16[2,48,256]{2,1,0:T(8,128)(2,1)}, u32[]{:S(2)}) copy-start(bf16[2,48,256]{2,1,0:T(8,128)(2,1)} %copy-done.9) | copy-start | bytes 147460
  137.2 4.9 %copy-start.16 = (bf16[2,32,256]{2,1,0:T(8,128)(2,1)S(1)}, bf16[2,32,256]{2,1,0:T(8,128)(2,1)}, u32[]{:S(2)}) copy-start(bf16[2,32,256]{2,1,0:T(8,128)(2,1)} %copy-done.15) | copy-start | bytes 98308
  147.3 15.7 %collective-permute-start.28 = (f32[2,15,32,256]{3,2,1,0:T(8,128)S(1)}, f32[2,15,32,256]{3,2,1,0:T(8,128)S(1)}, u32[]{:S(2)}, u32[]{:S(2)}) collective-permute-start(f32[2,15,32,256]{3,2,1,0:T(8,128)S(1)} %get-tuple-element.126), channel_id=1, source_target_pairs={{2,8},{3,9},{4,10},{5,11},{6,12},{7,13},{8,2},{9,3},{10,4},{11,5},... | collective-permute-start | bytes 2949128 | tf_op jit(solution)/shard_map/ppermute | solution.py:34
  149.2 13.8 %collective-permute-start.29 = (f32[2,15,32,256]{3,2,1,0:T(8,128)S(1)}, f32[2,15,32,256]{3,2,1,0:T(8,128)S(1)}, u32[]{:S(2)}, u32[]{:S(2)}) collective-permute-start(f32[2,15,32,256]{3,2,1,0:T(8,128)S(1)} %get-tuple-element.127), channel_id=1, source_target_pairs={{0,8},{1,9},{2,10},{3,11},{4,12},{5,13},{6,14},{7,15},{8,0},{9,1},... | collective-permute-start | bytes 2949128 | tf_op jit(solution)/shard_map/ppermute | solution.py:34
  156.2 17.3 %collective-permute-start.34 = (f32[2,15,32,256]{3,2,1,0:T(8,128)S(1)}, f32[2,15,32,256]{3,2,1,0:T(8,128)S(1)}, u32[]{:S(2)}, u32[]{:S(2)}) collective-permute-start(f32[2,15,32,256]{3,2,1,0:T(8,128)S(1)} %get-tuple-element.137), channel_id=1, source_target_pairs={{2,8},{3,9},{4,10},{5,11},{6,12},{7,13},{8,2},{9,3},{10,4},{11,5},... | collective-permute-start | bytes 2949128 | tf_op jit(solution)/shard_map/ppermute | solution.py:34
  159.3 14.2 %collective-permute-start.35 = (f32[2,15,32,256]{3,2,1,0:T(8,128)S(1)}, f32[2,15,32,256]{3,2,1,0:T(8,128)S(1)}, u32[]{:S(2)}, u32[]{:S(2)}) collective-permute-start(f32[2,15,32,256]{3,2,1,0:T(8,128)S(1)} %get-tuple-element.138), channel_id=1, source_target_pairs={{0,8},{1,9},{2,10},{3,11},{4,12},{5,13},{6,14},{7,15},{8,0},{9,1},... | collective-permute-start | bytes 2949128 | tf_op jit(solution)/shard_map/ppermute | solution.py:34
  164.7 15.1 %collective-permute-start.30 = (f32[16,32,256]{2,1,0:T(8,128)S(1)}, f32[16,32,256]{2,1,0:T(8,128)S(1)}, u32[]{:S(2)}, u32[]{:S(2)}) collective-permute-start(f32[16,32,256]{2,1,0:T(8,128)S(1)} %log_factor.8.refs_0_), channel_id=1, source_target_pairs={{0,16},{2,18},{4,20},{6,22},{9,25},{11,27},{13,29},{15,31},{16,0},... | collective-permute-start | bytes 1572872 | tf_op jit(solution)/shard_map/ppermute | solution.py:34
  165.4 16.9 %collective-permute-start.31 = (f32[16,32,256]{2,1,0:T(8,128)S(1)}, f32[16,32,256]{2,1,0:T(8,128)S(1)}, u32[]{:S(2)}, u32[]{:S(2)}) collective-permute-start(f32[16,32,256]{2,1,0:T(8,128)S(1)} %log_factor.8.refs_0_), channel_id=1, source_target_pairs={{1,24},{3,26},{5,28},{7,30},{8,17},{10,19},{12,21},{14,23},{17,8},... | collective-permute-start | bytes 1572872 | tf_op jit(solution)/shard_map/ppermute | solution.py:34
  169.3 16.4 %collective-permute-start.32 = (f32[16,32,256]{2,1,0:T(8,128)S(1)}, f32[16,32,256]{2,1,0:T(8,128)S(1)}, u32[]{:S(2)}, u32[]{:S(2)}) collective-permute-start(f32[16,32,256]{2,1,0:T(8,128)S(1)} %log_factor.8.refs_0_), channel_id=1, source_target_pairs={{1,8},{3,10},{5,12},{7,14},{8,1},{10,3},{12,5},{14,7},{17,24},{19,... | collective-permute-start | bytes 1572872 | tf_op jit(solution)/shard_map/ppermute | solution.py:34
  175.2 10.6 %collective-permute-start.36 = (f32[16,32,256]{2,1,0:T(8,128)S(1)}, f32[16,32,256]{2,1,0:T(8,128)S(1)}, u32[]{:S(2)}, u32[]{:S(2)}) collective-permute-start(f32[16,32,256]{2,1,0:T(8,128)S(1)} %log_factor.9.refs_0_), channel_id=1, source_target_pairs={{0,16},{2,18},{4,20},{6,22},{9,25},{11,27},{13,29},{15,31},{16,0},... | collective-permute-start | bytes 1572872 | tf_op jit(solution)/shard_map/ppermute | solution.py:34
  175.9 17.5 %collective-permute-start.37 = (f32[16,32,256]{2,1,0:T(8,128)S(1)}, f32[16,32,256]{2,1,0:T(8,128)S(1)}, u32[]{:S(2)}, u32[]{:S(2)}) collective-permute-start(f32[16,32,256]{2,1,0:T(8,128)S(1)} %log_factor.9.refs_0_), channel_id=1, source_target_pairs={{1,24},{3,26},{5,28},{7,30},{8,17},{10,19},{12,21},{14,23},{17,8},... | collective-permute-start | bytes 1572872 | tf_op jit(solution)/shard_map/ppermute | solution.py:34
  179.8 15.3 %collective-permute-start.38 = (f32[16,32,256]{2,1,0:T(8,128)S(1)}, f32[16,32,256]{2,1,0:T(8,128)S(1)}, u32[]{:S(2)}, u32[]{:S(2)}) collective-permute-start(f32[16,32,256]{2,1,0:T(8,128)S(1)} %log_factor.9.refs_0_), channel_id=1, source_target_pairs={{1,8},{3,10},{5,12},{7,14},{8,1},{10,3},{12,5},{14,7},{17,24},{19,... | collective-permute-start | bytes 1572872 | tf_op jit(solution)/shard_map/ppermute | solution.py:34
  185.8 9.5 %collective-permute-start.33 = (f32[16,32,256]{2,1,0:T(8,128)S(1)}, f32[16,32,256]{2,1,0:T(8,128)S(1)}, u32[]{:S(2)}, u32[]{:S(2)}) collective-permute-start(f32[16,32,256]{2,1,0:T(8,128)S(1)} %last_update.2.refs_0_), channel_id=1, source_target_pairs={{0,8},{1,9},{2,10},{3,11},{4,12},{5,13},{6,14},{7,15},{8,0},{9,1},... | collective-permute-start | bytes 1572872 | tf_op jit(solution)/shard_map/ppermute | solution.py:34
  195.2 2.0 collective-permute-start.39
  (14 other events, 17.5 us)

commit v18 on v17

--- a/solution.py
+++ b/solution.py
@@ -251,6 +251,7 @@
 
 def choose(estimate, crossed, radius):
     out_shape = edge_shapes(crossed.shape, radius, crossed.shape[1:2])[:2]
+    estimate, crossed = (pltpu.with_memory_space_constraint(array, pltpu.HBM) for array in (estimate, crossed))
     return call(choose_kernel, out_shape, [VMEM] * 2, "estimate")(estimate, crossed)
 
 

time: 200 us -> 198 us (0.990)
  waiting for transfers between devices: 58 us -> 63.5 us
  starting transfers between devices: 70.5 us -> 66.1 us
  local copies, waits for them, and re-layouts: 9.99 us -> 5.85 us
    ppermute x40, waiting for transfers between devices: 58 us -> 63.5 us  [send(): return lax.ppermute(array, AXES, moves(move))]
    ppermute x40, starting transfers between devices: 70.5 us -> 66.1 us  [send(): return lax.ppermute(array, AXES, moves(move))]
    unnamed x44 -> x38, local copies, waits for them, and re-layouts: 9.82 us -> 5.68 us
    pallas_call x1, Pallas kernels: 1.36 us -> 3.4 us  [choose(): call(choose_kernel, out_shape, [VMEM] * 2, 'estimate')(estimate, crossed)]
  transfers between devices with their start and end apart: 40 -> 40, of which waited for: 17 -> 18; matrix products, arithmetic and copies ran while one was open for 2% -> 2% of each run, Pallas kernels for 24% -> 25%
where the time goes in v18:
time: 198 us; the launch traced here: 197 us
  starting transfers between devices  66.1 us (33%)
  waiting for transfers between devices  63.5 us (32%)
  Pallas kernels  56.7 us (29%)
  local copies, waits for them, and re-layouts  5.85 us (3%)
  other arithmetic  3.67 us (2%)
    ppermute x40, starting transfers between devices, send(): return lax.ppermute(array, AXES, moves(move))  66.1 us
    ppermute x40, waiting for transfers between devices, send(): return lax.ppermute(array, AXES, moves(move))  63.5 us
    pallas_call x8, Pallas kernels, blur_x(): call(kernel, (shape, shape), [VMEM] * len(operands), 'blur_x_far' if far...  15.2 us
    pallas_call x2, Pallas kernels, next_ratio(): return call(kernel, out_shape, [VMEM] * len(operands), 'ratio')(*operands)  9.34 us
    pallas_call x5, Pallas kernels, log_factor(): call(kernel, shape, [VMEM] * (3 + len(parts)), 'log_factor')  7.68 us
    pallas_call x2, Pallas kernels, first_ratio(): call(kernel, out_shape, in_specs, 'image_and_ratio', scratch, hbm=(len(ou...  7.37 us
    unnamed x38, local copies, waits for them, and re-layouts  5.68 us
    pallas_call x1, Pallas kernels, shift_and_cut(): call(shift_kernel, (shape, shape), [SMEM, VMEM], 'shift_recorded', scratch)  4.5 us
  transfers between devices with their start and end apart: 40, of which 18 were waited for; matrix products, arithmetic and copies ran while one was open for 2% of the time, Pallas kernels for 25%

profile of v18, /device:TPU:17, one launch (start us, length us, event | category | flops | bytes accessed | tf_op | source)
XLA Modules:
  0.0 196.7 jit_solution(2545332432756356826)
XLA Ops:
  0.0 1.6 copy-done
  3.1 4.0 %collective-permute-start.1 = (f32[1,16,128]{2,1,0:T(8,128)S(1)}, f32[1,16,128]{2,1,0:T(8,128)}, u32[]{:S(2)}, u32[]{:S(2)}) collective-permute-start(f32[1,16,128]{2,1,0:T(8,128)S(1)} %convert_element_type.14), channel_id=1, source_target_pairs={{0,8},{1,9},{2,10},{3,11},{4,12},{5,13},{6,14},{7,15},{8,0},{9,1},... | collective-permute-start | bytes 24584 | tf_op jit(solution)/shard_map/ppermute | solution.py:34
  8.3 2.0 %band_matrices.1 = (bf16[2,80,384]{2,1,0:T(8,128)(2,1)S(1)}, bf16[2,64,256]{2,1,0:T(8,128)(2,1)S(1)}, bf16[2,48,256]{2,1,0:T(8,128)(2,1)S(1)}, bf16[2,32,256]{2,...) custom-call(f32[1,384]{1,0:T(1,128)S(1)} %fusion.1.mine_ref, ...), custom_call_target="tpu_custom_call" | custom-call | tf_op jit(solution)/shard_map/band_matrices/pallas_call | solution.py:203
  14.1 1.6 copy-done.3
  15.7 4.5 %shift_recorded.1 = (f32[16,80,256]{2,1,0:T(8,128)}, f32[16,80,256]{2,1,0:T(8,128)}) custom-call(s32[1,3]{1,0:T(1,128)S(1)} %copy-done.14, f32[16,128,256]{2,1,0:T(8,128)S(1)} %bitcast.1), custom_call_target="tpu_custom_call" | custom-call | tf_op jit(solution)/shard_map/shift_recorded/pallas_call | solution.py:284
  20.2 1.9 collective-permute-start.4
  23.0 3.4 %estimate.1 = (f32[16,96,256]{2,1,0:T(8,128)S(1)}, f32[15,96,256]{2,1,0:T(8,128)}) custom-call(f32[16,128,256]{2,1,0:T(8,128)} %estimate_ref.2, f32[16,96,256]{2,1,0:T(8,128)} %collective-permute-done.2.crossed_ref), custom_call_target="tpu_custom_call" | custom-call | tf_op jit(solution)/shard_map/estimate/pallas_call | solution.py:255
  26.4 4.3 %collective-permute-start.9 = (f32[15,96,256]{2,1,0:T(8,128)}, f32[15,96,256]{2,1,0:T(8,128)}, u32[]{:S(2)}, u32[]{:S(2)}) collective-permute-start(f32[15,96,256]{2,1,0:T(8,128)} %get-tuple-element.85), channel_id=1, source_target_pairs={{2,8},{3,9},{4,10},{5,11},{6,12},{7,13},{8,2},{9,3},{10,4},{11,5},... | collective-permute-start | bytes 4423688 | tf_op jit(solution)/shard_map/ppermute | solution.py:34
  33.7 11.2 %collective-permute-done.4 = f32[16,80,256]{2,1,0:T(8,128)} collective-permute-done((f32[16,80,256]{2,1,0:T(8,128)}, f32[16,80,256]{2,1,0:T(8,128)}, u32[]{:S(2)}, u32[]{:S(2)}) %collective-permute-start.4) | collective-permute-done | bytes 1310752 | tf_op jit(solution)/shard_map/ppermute | solution.py:34
  44.8 1.5 broadcast_select_fusion.own_ref
  46.4 6.9 %collective-permute-start.5 = (f32[16,80,256]{2,1,0:T(8,128)S(1)}, f32[16,80,256]{2,1,0:T(8,128)S(1)}, u32[]{:S(2)}, u32[]{:S(2)}) collective-permute-start(f32[16,80,256]{2,1,0:T(8,128)S(1)} %broadcast_select_fusion.own_ref), channel_id=1, source_target_pairs={{2,8},{3,9},{4,10},{5,11},{6,12},{7,13},{8,2},{9,3},{10,4},{11,5},... | collective-permute-start | bytes 3932168 | tf_op jit(solution)/shard_map/ppermute | solution.py:34
  54.1 3.3 %collective-permute-start.13 = (f32[16,80,256]{2,1,0:T(8,128)}, f32[16,80,256]{2,1,0:T(8,128)S(1)}, u32[]{:S(2)}, u32[]{:S(2)}) collective-permute-start(f32[16,80,256]{2,1,0:T(8,128)} %collective-permute-done.12.own_ref), channel_id=1, source_target_pairs={{2,8},{3,9},{4,10},{5,11},{6,12},{7,13},{8,2},{9,3},{10,4},{11,5},... | collective-permute-start | bytes 3932168 | tf_op jit(solution)/shard_map/ppermute | solution.py:34
  58.2 4.4 %blur_x_far.4 = (f32[16,96,256]{2,1,0:T(8,128)S(1)}, f32[16,96,256]{2,1,0:T(8,128)S(1)}) custom-call(bf16[2,256,384]{2,1,0:T(8,128)(2,1)S(1)} %get-tuple-element.74.hi_ref, bf16[2,256,384]{2,1,0:T(8,128)(2,1)S(1)} %get-tuple-element.75.lo_ref, f32[15,96,256]{2,1,0:T(8,128)} %collective-permute-done.9.refs_0_), custom_call_target="tpu_custom_call" | custom-call | tf_op jit(solution)/shard_map/blur_x_far/pallas_call | solution.py:332
  62.7 3.3 %blur_x_near.4 = (f32[16,96,256]{2,1,0:T(8,128)S(1)}, f32[16,96,256]{2,1,0:T(8,128)S(1)}) custom-call(bf16[2,256,384]{2,1,0:T(8,128)(2,1)S(1)} %get-tuple-element.74.hi_ref, bf16[2,256,384]{2,1,0:T(8,128)(2,1)S(1)} %get-tuple-element.75.lo_ref, f32[16,96,256]{2,1,0:T(8,128)S(1)} %get-tuple-element.81.refs_0_.before_ref, ...), custom_call_target="tpu_custom_call" | custom-call | tf_op jit(solution)/shard_map/blur_x_near/pallas_call | solution.py:332
  66.0 1.6 blur_yz.2.blurred_ref
  68.9 3.1 %image_and_ratio.2 = (f32[16,64,256]{2,1,0:T(8,128)S(1)}, f32[15,64,256]{2,1,0:T(8,128)S(1)}, f32[15,64,256]{2,1,0:T(8,128)S(1)}, f32[16,80,256]{2,1,0:T(8,128)}) custom-call(s32[2,3]{1,0:T(2,128)S(1)} %fusion.2.shift_ref, f32[16,80,256]{2,1,0:T(8,128)S(1)} %collective-permute-done.5.far_ref, f32[16,80,256]{2,1,0:T(8,128)S(1)} %collective-permute-done.6.near_ref, ...), custom_call_target="tpu_custom_call" | custom-call | tf_op jit(solution)/shard_map/image_and_ratio/pallas_call | solution.py:487
  72.0 3.3 %collective-permute-start.10 = (f32[15,64,256]{2,1,0:T(8,128)S(1)}, f32[15,64,256]{2,1,0:T(8,128)S(1)}, u32[]{:S(2)}, u32[]{:S(2)}) collective-permute-start(f32[15,64,256]{2,1,0:T(8,128)S(1)} %get-tuple-element.92), channel_id=1, source_target_pairs={{2,8},{3,9},{4,10},{5,11},{6,12},{7,13},{8,2},{9,3},{10,4},{11,5},... | collective-permute-start | bytes 2949128 | tf_op jit(solution)/shard_map/ppermute | solution.py:34
  75.4 1.6 blur_yz.3.blurred_ref
  77.0 5.9 %collective-permute-done.13.far_ref = f32[16,80,256]{2,1,0:T(8,128)S(1)} collective-permute-done((f32[16,80,256]{2,1,0:T(8,128)}, f32[16,80,256]{2,1,0:T(8,128)S(1)}, u32[]{:S(2)}, u32[]{:S(2)}) %collective-permute-start.13) | collective-permute-done | bytes 1310752 | tf_op jit(solution)/shard_map/ppermute | solution.py:34
  82.9 4.3 %image_and_ratio.3 = (f32[16,64,256]{2,1,0:T(8,128)S(1)}, f32[15,32,256]{2,1,0:T(8,128)S(1)}, f32[15,32,256]{2,1,0:T(8,128)S(1)}, f32[15,32,256]{2,1,0:T(8,128)S...) custom-call(s32[2,3]{1,0:T(2,128)S(1)} %fusion.2.shift_ref, f32[16,80,256]{2,1,0:T(8,128)S(1)} %collective-permute-done.13.far_ref, ...), custom_call_target="tpu_custom_call" | custom-call | tf_op jit(solution)/shard_map/image_and_ratio/pallas_call | solution.py:487
  87.2 3.3 %collective-permute-start.18 = (f32[15,32,256]{2,1,0:T(8,128)S(1)}, f32[15,32,256]{2,1,0:T(8,128)S(1)}, u32[]{:S(2)}, u32[]{:S(2)}) collective-permute-start(f32[15,32,256]{2,1,0:T(8,128)S(1)} %get-tuple-element.105), channel_id=1, source_target_pairs={{2,8},{3,9},{4,10},{5,11},{6,12},{7,13},{8,2},{9,3},{10,4},{11,5},... | collective-permute-start | bytes 1474568 | tf_op jit(solution)/shard_map/ppermute | solution.py:34
  90.6 2.8 %collective-permute-done.10.refs_0_ = f32[15,64,256]{2,1,0:T(8,128)S(1)} collective-permute-done((f32[15,64,256]{2,1,0:T(8,128)S(1)}, f32[15,64,256]{2,1,0:T(8,128)S(1)}, u32[]{:S(2)}, u32[]{:S(2)}) %collective-permute-start.10) | collective-permute-done | bytes 983072 | tf_op jit(solution)/shard_map/ppermute | solution.py:34
  93.5 2.2 %log_factor.5.before_ref = f32[16,64,256]{2,1,0:T(8,128)S(1)} custom-call(bf16[2,256,384]{2,1,0:T(8,128)(2,1)S(1)} %get-tuple-element.74.hi_ref, bf16[2,256,384]{2,1,0:T(8,128)(2,1)S(1)} %get-tuple-element.75.lo_ref, f32[16,96,256]{2,1,0:T(8,128)S(1)} %get-tuple-element.81.refs_0_.before_ref, f32[15,64,256]{2,1,0:T(8,128)S(1)} %collective-permute-done.10.refs_0_, ...), custom_call_target="tpu_custom_call" | custom-call | tf_op jit(solution)/shard_map/log_factor/pallas_call | solution.py:520
  95.6 2.8 %collective-permute-done.18.refs_0_ = f32[15,32,256]{2,1,0:T(8,128)S(1)} collective-permute-done((f32[15,32,256]{2,1,0:T(8,128)S(1)}, f32[15,32,256]{2,1,0:T(8,128)S(1)}, u32[]{:S(2)}, u32[]{:S(2)}) %collective-permute-start.18) | collective-permute-done | bytes 491552 | tf_op jit(solution)/shard_map/ppermute | solution.py:34
  100.8 3.9 %collective-permute-start.15 = (f32[15,32,256]{2,1,0:T(8,128)S(1)}, f32[15,32,256]{2,1,0:T(8,128)S(1)}, u32[]{:S(2)}, u32[]{:S(2)}) collective-permute-start(f32[15,32,256]{2,1,0:T(8,128)S(1)} %get-tuple-element.98), channel_id=1, source_target_pairs={{2,8},{3,9},{4,10},{5,11},{6,12},{7,13},{8,2},{9,3},{10,4},{11,5},... | collective-permute-start | bytes 1474568 | tf_op jit(solution)/shard_map/ppermute | solution.py:34
  104.8 6.4 %collective-permute-done.15.refs_0_ = f32[15,32,256]{2,1,0:T(8,128)S(1)} collective-permute-done((f32[15,32,256]{2,1,0:T(8,128)S(1)}, f32[15,32,256]{2,1,0:T(8,128)S(1)}, u32[]{:S(2)}, u32[]{:S(2)}) %collective-permute-start.15) | collective-permute-done | bytes 491552 | tf_op jit(solution)/shard_map/ppermute | solution.py:34
  113.7 4.1 %collective-permute-start.21 = (f32[15,32,256]{2,1,0:T(8,128)}, f32[15,32,256]{2,1,0:T(8,128)}, u32[]{:S(2)}, u32[]{:S(2)}) collective-permute-start(f32[15,32,256]{2,1,0:T(8,128)} %get-tuple-element.107), channel_id=1, source_target_pairs={{2,8},{3,9},{4,10},{5,11},{6,12},{7,13},{8,2},{9,3},{10,4},{11,5},... | collective-permute-start | bytes 1474568 | tf_op jit(solution)/shard_map/ppermute | solution.py:34
  117.9 5.9 %collective-permute-done.17.refs_1_ = f32[16,32,256]{2,1,0:T(8,128)} collective-permute-done((f32[16,32,256]{2,1,0:T(8,128)S(1)}, f32[16,32,256]{2,1,0:T(8,128)}, u32[]{:S(2)}, u32[]{:S(2)}) %collective-permute-start.17) | collective-permute-done | bytes 524320 | tf_op jit(solution)/shard_map/ppermute | solution.py:34
  125.5 2.6 %collective-permute-start.22 = (f32[15,32,256]{2,1,0:T(8,128)S(1)}, f32[15,32,256]{2,1,0:T(8,128)S(1)}, u32[]{:S(2)}, u32[]{:S(2)}) collective-permute-start(f32[15,32,256]{2,1,0:T(8,128)S(1)} %get-tuple-element.108), channel_id=1, source_target_pairs={{2,8},{3,9},{4,10},{5,11},{6,12},{7,13},{8,2},{9,3},{10,4},{11,5},... | collective-permute-start | bytes 1474568 | tf_op jit(solution)/shard_map/ppermute | solution.py:34
  128.2 3.0 %collective-permute-start.25 = (f32[15,32,256]{2,1,0:T(8,128)S(1)}, f32[15,32,256]{2,1,0:T(8,128)S(1)}, u32[]{:S(2)}, u32[]{:S(2)}) collective-permute-start(f32[15,32,256]{2,1,0:T(8,128)S(1)} %get-tuple-element.142), channel_id=1, source_target_pairs={{2,8},{3,9},{4,10},{5,11},{6,12},{7,13},{8,2},{9,3},{10,4},{11,5},... | collective-permute-start | bytes 1474568 | tf_op jit(solution)/shard_map/ppermute | solution.py:34
  133.6 2.2 %blur_x_far.6 = (f32[16,32,256]{2,1,0:T(8,128)S(1)}, f32[16,32,256]{2,1,0:T(8,128)S(1)}) custom-call(bf16[2,256,384]{2,1,0:T(8,128)(2,1)S(1)} %get-tuple-element.74.hi_ref, bf16[2,256,384]{2,1,0:T(8,128)(2,1)S(1)} %get-tuple-element.75.lo_ref, f32[15,32,256]{2,1,0:T(8,128)} %collective-permute-done.21.refs_0_, ...), custom_call_target="tpu_custom_call" | custom-call | tf_op jit(solution)/shard_map/blur_x_far/pallas_call | solution.py:332
  137.0 3.9 %collective-permute-done.25.refs_0_ = f32[15,32,256]{2,1,0:T(8,128)S(1)} collective-permute-done((f32[15,32,256]{2,1,0:T(8,128)S(1)}, f32[15,32,256]{2,1,0:T(8,128)S(1)}, u32[]{:S(2)}, u32[]{:S(2)}) %collective-permute-start.25) | collective-permute-done | bytes 491552 | tf_op jit(solution)/shard_map/ppermute | solution.py:34
  141.0 5.2 %ratio.2 = (f32[16,32,256]{2,1,0:T(8,128)S(1)}, f32[16,32,256]{2,1,0:T(8,128)S(1)}, f32[2,15,32,256]{3,2,1,0:T(8,128)S(1)}, f32[2,15,32,256]{3,2,1,0:T(8,128)S(1)}, f32[2,16,32,256]{3,2,1,0:T(8,128)S(1)}) custom-call(f32[16,80,256]{2,1,0:T(8,128)S(1)} %copy-done.1, f32[16,80,256]{2,1,0:T(8,128)S(1)} %copy-done.2, ...), custom_call_target="tpu_custom_call" | custom-call | tf_op jit(solution)/shard_map/ratio/pallas_call | solution.py:475
  146.1 2.5 %collective-permute-start.28 = (f32[2,15,32,256]{3,2,1,0:T(8,128)S(1)}, f32[2,15,32,256]{3,2,1,0:T(8,128)S(1)}, u32[]{:S(2)}, u32[]{:S(2)}) collective-permute-start(f32[2,15,32,256]{3,2,1,0:T(8,128)S(1)} %get-tuple-element.126), channel_id=1, source_target_pairs={{2,8},{3,9},{4,10},{5,11},{6,12},{7,13},{8,2},{9,3},{10,4},{11,5},... | collective-permute-start | bytes 2949128 | tf_op jit(solution)/shard_map/ppermute | solution.py:34
  150.9 4.2 %ratio.3 = (f32[16,32,256]{2,1,0:T(8,128)S(1)}, f32[16,32,256]{2,1,0:T(8,128)S(1)}, f32[2,15,32,256]{3,2,1,0:T(8,128)S(1)}, f32[2,15,32,256]{3,2,1,0:T(8,128)S(1)}) custom-call(f32[16,80,256]{2,1,0:T(8,128)S(1)} %copy-done.1, f32[16,80,256]{2,1,0:T(8,128)S(1)} %copy-done.2, f32[16,32,256]{2,1,0:T(8,128)S(1)} %get-tuple-element.119.refs_3_.refs_2_, ...), custom_call_target="tpu_custom_call" | custom-call | tf_op jit(solution)/shard_map/ratio/pallas_call | solution.py:475
  155.1 3.1 %collective-permute-start.34 = (f32[2,15,32,256]{3,2,1,0:T(8,128)S(1)}, f32[2,15,32,256]{3,2,1,0:T(8,128)S(1)}, u32[]{:S(2)}, u32[]{:S(2)}) collective-permute-start(f32[2,15,32,256]{3,2,1,0:T(8,128)S(1)} %get-tuple-element.137), channel_id=1, source_target_pairs={{2,8},{3,9},{4,10},{5,11},{6,12},{7,13},{8,2},{9,3},{10,4},{11,5},... | collective-permute-start | bytes 2949128 | tf_op jit(solution)/shard_map/ppermute | solution.py:34
  158.2 3.6 %collective-permute-done.28.refs_0_.refs_3_ = f32[2,15,32,256]{3,2,1,0:T(8,128)S(1)} collective-permute-done((f32[2,15,32,256]{3,2,1,0:T(8,128)S(1)}, f32[2,15,32,256]{3,2,1,0:T(8,128)S(1)}, u32[]{:S(2)}, u32[]{:S(2)}) %collective-permute-start.28) | collective-permute-done | bytes 983072 | tf_op jit(solution)/shard_map/ppermute | solution.py:34
  161.9 1.7 log_factor.8.refs_0_
  164.3 1.9 collective-permute-start.31
  166.2 3.8 %collective-permute-start.32 = (f32[16,32,256]{2,1,0:T(8,128)S(1)}, f32[16,32,256]{2,1,0:T(8,128)S(1)}, u32[]{:S(2)}, u32[]{:S(2)}) collective-permute-start(f32[16,32,256]{2,1,0:T(8,128)S(1)} %log_factor.8.refs_0_), channel_id=1, source_target_pairs={{1,8},{3,10},{5,12},{7,14},{8,1},{10,3},{12,5},{14,7},{17,24},{19,... | collective-permute-start | bytes 1572872 | tf_op jit(solution)/shard_map/ppermute | solution.py:34
  170.0 2.4 %collective-permute-done.34.refs_0_.refs_3_ = f32[2,15,32,256]{3,2,1,0:T(8,128)S(1)} collective-permute-done((f32[2,15,32,256]{3,2,1,0:T(8,128)S(1)}, f32[2,15,32,256]{3,2,1,0:T(8,128)S(1)}, u32[]{:S(2)}, u32[]{:S(2)}) %collective-permute-start.34) | collective-permute-done | bytes 983072 | tf_op jit(solution)/shard_map/ppermute | solution.py:34
  172.4 1.7 log_factor.9.refs_0_
  174.8 3.1 %collective-permute-start.37 = (f32[16,32,256]{2,1,0:T(8,128)S(1)}, f32[16,32,256]{2,1,0:T(8,128)S(1)}, u32[]{:S(2)}, u32[]{:S(2)}) collective-permute-start(f32[16,32,256]{2,1,0:T(8,128)S(1)} %log_factor.9.refs_0_), channel_id=1, source_target_pairs={{1,24},{3,26},{5,28},{7,30},{8,17},{10,19},{12,21},{14,23},{17,8},... | collective-permute-start | bytes 1572872 | tf_op jit(solution)/shard_map/ppermute | solution.py:34
  177.9 2.7 %collective-permute-start.38 = (f32[16,32,256]{2,1,0:T(8,128)S(1)}, f32[16,32,256]{2,1,0:T(8,128)S(1)}, u32[]{:S(2)}, u32[]{:S(2)}) collective-permute-start(f32[16,32,256]{2,1,0:T(8,128)S(1)} %log_factor.9.refs_0_), channel_id=1, source_target_pairs={{1,8},{3,10},{5,12},{7,14},{8,1},{10,3},{12,5},{14,7},{17,24},{19,... | collective-permute-start | bytes 1572872 | tf_op jit(solution)/shard_map/ppermute | solution.py:34
  180.6 2.9 %collective-permute-done.32.refs_3_ = f32[16,32,256]{2,1,0:T(8,128)S(1)} collective-permute-done((f32[16,32,256]{2,1,0:T(8,128)S(1)}, f32[16,32,256]{2,1,0:T(8,128)S(1)}, u32[]{:S(2)}, u32[]{:S(2)}) %collective-permute-start.32) | collective-permute-done | bytes 524320 | tf_op jit(solution)/shard_map/ppermute | solution.py:34
  183.7 7.2 %collective-permute-done.37.refs_2_ = f32[16,32,256]{2,1,0:T(8,128)S(1)} collective-permute-done((f32[16,32,256]{2,1,0:T(8,128)S(1)}, f32[16,32,256]{2,1,0:T(8,128)S(1)}, u32[]{:S(2)}, u32[]{:S(2)}) %collective-permute-start.37) | collective-permute-done | bytes 524320 | tf_op jit(solution)/shard_map/ppermute | solution.py:34
  190.8 2.3 %collective-permute-done.38.refs_3_ = f32[16,32,256]{2,1,0:T(8,128)S(1)} collective-permute-done((f32[16,32,256]{2,1,0:T(8,128)S(1)}, f32[16,32,256]{2,1,0:T(8,128)S(1)}, u32[]{:S(2)}, u32[]{:S(2)}) %collective-permute-start.38) | collective-permute-done | bytes 524320 | tf_op jit(solution)/shard_map/ppermute | solution.py:34
  193.3 1.9 collective-permute-done.39.refs_3_
  (107 shorter events, 29.1 us)
Async XLA Ops:
  1.6 5.4 %copy-start.16 = (f32[1,61]{1,0:T(1,128)S(1)}, f32[1,61]{1,0:T(1,128)}, u32[]{:S(2)}) copy-start(f32[1,61]{1,0:T(1,128)} %param.13) | copy-start | bytes 736
  1.6 5.4 %copy-start.17 = (f32[1,31]{1,0:T(1,128)S(1)}, f32[1,31]{1,0:T(1,128)}, u32[]{:S(2)}) copy-start(f32[1,31]{1,0:T(1,128)} %param.12) | copy-start | bytes 376
  1.6 5.4 %copy-start.18 = (f32[1,31]{1,0:T(1,128)S(1)}, f32[1,31]{1,0:T(1,128)}, u32[]{:S(2)}) copy-start(f32[1,31]{1,0:T(1,128)} %param.11) | copy-start | bytes 376
  1.6 12.5 %copy-start.14 = (s32[1,3]{1,0:T(1,128)S(1)}, s32[1,3]{1,0:T(1,128)}, u32[]{:S(2)}) copy-start(s32[1,3]{1,0:T(1,128)} %offsets_ref.1) | copy-start | bytes 40
  1.7 21.3 %collective-permute-start.2 = (f32[16,96,256]{2,1,0:T(8,128)S(1)}, f32[16,96,256]{2,1,0:T(8,128)}, u32[]{:S(2)}, u32[]{:S(2)}) collective-permute-start(f32[16,96,256]{2,1,0:T(8,128)S(1)} %other_window.1), channel_id=1, source_target_pairs={{0,1},{2,3},{4,5},{6,7},{9,8},{11,10},{13,12},{15,14},{16,17},{18,... | collective-permute-start | bytes 4718600 | tf_op jit(solution)/shard_map/ppermute | solution.py:34
  3.1 9.7 %collective-permute-start.1 = (f32[1,16,128]{2,1,0:T(8,128)S(1)}, f32[1,16,128]{2,1,0:T(8,128)}, u32[]{:S(2)}, u32[]{:S(2)}) collective-permute-start(f32[1,16,128]{2,1,0:T(8,128)S(1)} %convert_element_type.14), channel_id=1, source_target_pairs={{0,8},{1,9},{2,10},{3,11},{4,12},{5,13},{6,14},{7,15},{8,0},{9,1},... | collective-permute-start | bytes 24584 | tf_op jit(solution)/shard_map/ppermute | solution.py:34
  7.0 1.2 collective-permute-start
  20.2 24.6 %collective-permute-start.4 = (f32[16,80,256]{2,1,0:T(8,128)}, f32[16,80,256]{2,1,0:T(8,128)}, u32[]{:S(2)}, u32[]{:S(2)}) collective-permute-start(f32[16,80,256]{2,1,0:T(8,128)} %get-tuple-element.83), channel_id=1, source_target_pairs={{1,8},{3,10},{5,12},{7,14},{8,1},{10,3},{12,5},{14,7},{17,24},{19,... | collective-permute-start | bytes 3932168 | tf_op jit(solution)/shard_map/ppermute | solution.py:34
  26.4 30.9 %collective-permute-start.9 = (f32[15,96,256]{2,1,0:T(8,128)}, f32[15,96,256]{2,1,0:T(8,128)}, u32[]{:S(2)}, u32[]{:S(2)}) collective-permute-start(f32[15,96,256]{2,1,0:T(8,128)} %get-tuple-element.85), channel_id=1, source_target_pairs={{2,8},{3,9},{4,10},{5,11},{6,12},{7,13},{8,2},{9,3},{10,4},{11,5},... | collective-permute-start | bytes 4423688 | tf_op jit(solution)/shard_map/ppermute | solution.py:34
  30.7 23.3 %collective-permute-start.12 = (f32[16,80,256]{2,1,0:T(8,128)}, f32[16,80,256]{2,1,0:T(8,128)}, u32[]{:S(2)}, u32[]{:S(2)}) collective-permute-start(f32[16,80,256]{2,1,0:T(8,128)} %get-tuple-element.96), channel_id=1, source_target_pairs={{0,1},{1,9},{2,3},{3,11},{4,5},{5,13},{6,7},{7,15},{8,0},{9,8},{10... | collective-permute-start | bytes 3932168 | tf_op jit(solution)/shard_map/ppermute | solution.py:34
  30.8 15.6 %collective-permute-start.3 = (f32[1,3]{1,0:T(1,128)S(1)}, f32[1,3]{1,0:T(1,128)S(1)}, u32[]{:S(2)}, u32[]{:S(2)}) collective-permute-start(f32[1,3]{1,0:T(1,128)S(1)} %convert_element_type.15), channel_id=1, source_target_pairs={{0,8},{1,9},{2,10},{3,11},{4,12},{5,13},{6,14},{7,15},{8,0},{9,1},... | collective-permute-start | bytes 44 | tf_op jit(solution)/shard_map/ppermute | solution.py:34
  32.1 21.9 %collective-permute-start.7 = (f32[2,16,128]{2,1,0:T(8,128)}, f32[2,16,128]{2,1,0:T(8,128)S(1)}, u32[]{:S(2)}, u32[]{:S(2)}) collective-permute-start(f32[2,16,128]{2,1,0:T(8,128)} %maximum_select_fusion), channel_id=1, source_target_pairs={{0,1},{1,0},{2,3},{3,2},{4,5},{5,4},{6,7},{7,6},{8,9},{9,8},{10,11... | collective-permute-start | bytes 49160 | tf_op jit(solution)/shard_map/ppermute | solution.py:34
  44.8 17.8 %collective-permute-start.8 = (f32[15,96,256]{2,1,0:T(8,128)S(1)}, f32[15,96,256]{2,1,0:T(8,128)S(1)}, u32[]{:S(2)}, u32[]{:S(2)}) collective-permute-start(f32[15,96,256]{2,1,0:T(8,128)S(1)} %constant_dynamic-slice_fusion.2), channel_id=1, source_target_pairs={{0,8},{1,9},{2,10},{3,11},{4,12},{5,13},{6,14},{7,15},{8,0},{9,1},... | collective-permute-start | bytes 4423688 | tf_op jit(solution)/shard_map/ppermute | solution.py:34
  46.4 22.5 %collective-permute-start.5 = (f32[16,80,256]{2,1,0:T(8,128)S(1)}, f32[16,80,256]{2,1,0:T(8,128)S(1)}, u32[]{:S(2)}, u32[]{:S(2)}) collective-permute-start(f32[16,80,256]{2,1,0:T(8,128)S(1)} %broadcast_select_fusion.own_ref), channel_id=1, source_target_pairs={{2,8},{3,9},{4,10},{5,11},{6,12},{7,13},{8,2},{9,3},{10,4},{11,5},... | collective-permute-start | bytes 3932168 | tf_op jit(solution)/shard_map/ppermute | solution.py:34
  54.0 14.8 %collective-permute-start.6 = (f32[16,80,256]{2,1,0:T(8,128)S(1)}, f32[16,80,256]{2,1,0:T(8,128)S(1)}, u32[]{:S(2)}, u32[]{:S(2)}) collective-permute-start(f32[16,80,256]{2,1,0:T(8,128)S(1)} %broadcast_select_fusion.own_ref), channel_id=1, source_target_pairs={{0,8},{1,9},{2,10},{3,11},{4,12},{5,13},{6,14},{7,15},{8,0},{9,1},... | collective-permute-start | bytes 3932168 | tf_op jit(solution)/shard_map/ppermute | solution.py:34
  54.1 28.9 %collective-permute-start.13 = (f32[16,80,256]{2,1,0:T(8,128)}, f32[16,80,256]{2,1,0:T(8,128)S(1)}, u32[]{:S(2)}, u32[]{:S(2)}) collective-permute-start(f32[16,80,256]{2,1,0:T(8,128)} %collective-permute-done.12.own_ref), channel_id=1, source_target_pairs={{2,8},{3,9},{4,10},{5,11},{6,12},{7,13},{8,2},{9,3},{10,4},{11,5},... | collective-permute-start | bytes 3932168 | tf_op jit(solution)/shard_map/ppermute | solution.py:34
  57.4 25.6 %collective-permute-start.14 = (f32[16,80,256]{2,1,0:T(8,128)}, f32[16,80,256]{2,1,0:T(8,128)S(1)}, u32[]{:S(2)}, u32[]{:S(2)}) collective-permute-start(f32[16,80,256]{2,1,0:T(8,128)} %collective-permute-done.12.own_ref), channel_id=1, source_target_pairs={{0,8},{1,9},{2,10},{3,11},{4,12},{5,13},{6,14},{7,15},{8,0},{9,1},... | collective-permute-start | bytes 3932168 | tf_op jit(solution)/shard_map/ppermute | solution.py:34
  72.0 21.5 %collective-permute-start.10 = (f32[15,64,256]{2,1,0:T(8,128)S(1)}, f32[15,64,256]{2,1,0:T(8,128)S(1)}, u32[]{:S(2)}, u32[]{:S(2)}) collective-permute-start(f32[15,64,256]{2,1,0:T(8,128)S(1)} %get-tuple-element.92), channel_id=1, source_target_pairs={{2,8},{3,9},{4,10},{5,11},{6,12},{7,13},{8,2},{9,3},{10,4},{11,5},... | collective-permute-start | bytes 2949128 | tf_op jit(solution)/shard_map/ppermute | solution.py:34
  75.3 18.1 %collective-permute-start.11 = (f32[15,64,256]{2,1,0:T(8,128)S(1)}, f32[15,64,256]{2,1,0:T(8,128)S(1)}, u32[]{:S(2)}, u32[]{:S(2)}) collective-permute-start(f32[15,64,256]{2,1,0:T(8,128)S(1)} %get-tuple-element.93), channel_id=1, source_target_pairs={{0,8},{1,9},{2,10},{3,11},{4,12},{5,13},{6,14},{7,15},{8,0},{9,1},... | collective-permute-start | bytes 2949128 | tf_op jit(solution)/shard_map/ppermute | solution.py:34
  87.2 11.2 %collective-permute-start.18 = (f32[15,32,256]{2,1,0:T(8,128)S(1)}, f32[15,32,256]{2,1,0:T(8,128)S(1)}, u32[]{:S(2)}, u32[]{:S(2)}) collective-permute-start(f32[15,32,256]{2,1,0:T(8,128)S(1)} %get-tuple-element.105), channel_id=1, source_target_pairs={{2,8},{3,9},{4,10},{5,11},{6,12},{7,13},{8,2},{9,3},{10,4},{11,5},... | collective-permute-start | bytes 1474568 | tf_op jit(solution)/shard_map/ppermute | solution.py:34
  90.5 7.9 %collective-permute-start.19 = (f32[15,32,256]{2,1,0:T(8,128)S(1)}, f32[15,32,256]{2,1,0:T(8,128)S(1)}, u32[]{:S(2)}, u32[]{:S(2)}) collective-permute-start(f32[15,32,256]{2,1,0:T(8,128)S(1)} %get-tuple-element.106), channel_id=1, source_target_pairs={{0,8},{1,9},{2,10},{3,11},{4,12},{5,13},{6,14},{7,15},{8,0},{9,1},... | collective-permute-start | bytes 1474568 | tf_op jit(solution)/shard_map/ppermute | solution.py:34
  99.5 13.1 %collective-permute-start.20 = (f32[16,32,256]{2,1,0:T(8,128)S(1)}, f32[16,32,256]{2,1,0:T(8,128)S(1)}, u32[]{:S(2)}, u32[]{:S(2)}) collective-permute-start(f32[16,32,256]{2,1,0:T(8,128)S(1)} %log_factor.7.refs_0_), channel_id=1, source_target_pairs={{0,16},{1,17},{2,18},{3,19},{4,20},{5,21},{6,22},{7,23},{8,24},{9,... | collective-permute-start | bytes 1572872 | tf_op jit(solution)/shard_map/ppermute | solution.py:34
  100.8 10.4 %collective-permute-start.15 = (f32[15,32,256]{2,1,0:T(8,128)S(1)}, f32[15,32,256]{2,1,0:T(8,128)S(1)}, u32[]{:S(2)}, u32[]{:S(2)}) collective-permute-start(f32[15,32,256]{2,1,0:T(8,128)S(1)} %get-tuple-element.98), channel_id=1, source_target_pairs={{2,8},{3,9},{4,10},{5,11},{6,12},{7,13},{8,2},{9,3},{10,4},{11,5},... | collective-permute-start | bytes 1474568 | tf_op jit(solution)/shard_map/ppermute | solution.py:34
  104.7 6.5 %collective-permute-start.16 = (f32[15,32,256]{2,1,0:T(8,128)S(1)}, f32[15,32,256]{2,1,0:T(8,128)S(1)}, u32[]{:S(2)}, u32[]{:S(2)}) collective-permute-start(f32[15,32,256]{2,1,0:T(8,128)S(1)} %get-tuple-element.99), channel_id=1, source_target_pairs={{0,8},{1,9},{2,10},{3,11},{4,12},{5,13},{6,14},{7,15},{8,0},{9,1},... | collective-permute-start | bytes 1474568 | tf_op jit(solution)/shard_map/ppermute | solution.py:34
  112.3 11.5 %collective-permute-start.17 = (f32[16,32,256]{2,1,0:T(8,128)S(1)}, f32[16,32,256]{2,1,0:T(8,128)}, u32[]{:S(2)}, u32[]{:S(2)}) collective-permute-start(f32[16,32,256]{2,1,0:T(8,128)S(1)} %log_factor.6.refs_0_), channel_id=1, source_target_pairs={{0,16},{1,17},{2,18},{3,19},{4,20},{5,21},{6,22},{7,23},{8,24},{9,... | collective-permute-start | bytes 1572872 | tf_op jit(solution)/shard_map/ppermute | solution.py:34
  113.7 14.4 %collective-permute-start.24 = (f32[16,32,256]{2,1,0:T(8,128)S(1)}, f32[16,32,256]{2,1,0:T(8,128)S(1)}, u32[]{:S(2)}, u32[]{:S(2)}) collective-permute-start(f32[16,32,256]{2,1,0:T(8,128)S(1)} %get-tuple-element.113.refs_0_.before_ref), channel_id=1, source_target_pairs={{0,1},{1,0},{2,3},{3,2},{4,5},{5,4},{6,7},{7,6},{8,9},{9,8},{10,11... | collective-permute-start | bytes 1572872 | tf_op jit(solution)/shard_map/ppermute | solution.py:34
  113.7 11.8 %collective-permute-start.21 = (f32[15,32,256]{2,1,0:T(8,128)}, f32[15,32,256]{2,1,0:T(8,128)}, u32[]{:S(2)}, u32[]{:S(2)}) collective-permute-start(f32[15,32,256]{2,1,0:T(8,128)} %get-tuple-element.107), channel_id=1, source_target_pairs={{2,8},{3,9},{4,10},{5,11},{6,12},{7,13},{8,2},{9,3},{10,4},{11,5},... | collective-permute-start | bytes 1474568 | tf_op jit(solution)/shard_map/ppermute | solution.py:34
  125.0 7.5 %collective-permute-start.23 = (f32[15,32,256]{2,1,0:T(8,128)S(1)}, f32[15,32,256]{2,1,0:T(8,128)S(1)}, u32[]{:S(2)}, u32[]{:S(2)}) collective-permute-start(f32[15,32,256]{2,1,0:T(8,128)S(1)} %get-tuple-element.109), channel_id=1, source_target_pairs={{0,8},{1,9},{2,10},{3,11},{4,12},{5,13},{6,14},{7,15},{8,0},{9,1},... | collective-permute-start | bytes 1474568 | tf_op jit(solution)/shard_map/ppermute | solution.py:34
  125.0 6.3 %collective-permute-start.27 = (f32[15,32,256]{2,1,0:T(8,128)}, f32[15,32,256]{2,1,0:T(8,128)S(1)}, u32[]{:S(2)}, u32[]{:S(2)}) collective-permute-start(f32[15,32,256]{2,1,0:T(8,128)} %get-tuple-element.116), channel_id=1, source_target_pairs={{0,8},{1,9},{2,10},{3,11},{4,12},{5,13},{6,14},{7,15},{8,0},{9,1},... | collective-permute-start | bytes 1474568 | tf_op jit(solution)/shard_map/ppermute | solution.py:34
  125.5 10.4 %collective-permute-start.22 = (f32[15,32,256]{2,1,0:T(8,128)S(1)}, f32[15,32,256]{2,1,0:T(8,128)S(1)}, u32[]{:S(2)}, u32[]{:S(2)}) collective-permute-start(f32[15,32,256]{2,1,0:T(8,128)S(1)} %get-tuple-element.108), channel_id=1, source_target_pairs={{2,8},{3,9},{4,10},{5,11},{6,12},{7,13},{8,2},{9,3},{10,4},{11,5},... | collective-permute-start | bytes 1474568 | tf_op jit(solution)/shard_map/ppermute | solution.py:34
  128.2 12.7 %collective-permute-start.25 = (f32[15,32,256]{2,1,0:T(8,128)S(1)}, f32[15,32,256]{2,1,0:T(8,128)S(1)}, u32[]{:S(2)}, u32[]{:S(2)}) collective-permute-start(f32[15,32,256]{2,1,0:T(8,128)S(1)} %get-tuple-element.142), channel_id=1, source_target_pairs={{2,8},{3,9},{4,10},{5,11},{6,12},{7,13},{8,2},{9,3},{10,4},{11,5},... | collective-permute-start | bytes 1474568 | tf_op jit(solution)/shard_map/ppermute | solution.py:34
  131.2 9.7 %collective-permute-start.26 = (f32[15,32,256]{2,1,0:T(8,128)S(1)}, f32[15,32,256]{2,1,0:T(8,128)S(1)}, u32[]{:S(2)}, u32[]{:S(2)}) collective-permute-start(f32[15,32,256]{2,1,0:T(8,128)S(1)} %get-tuple-element.141), channel_id=1, source_target_pairs={{0,8},{1,9},{2,10},{3,11},{4,12},{5,13},{6,14},{7,15},{8,0},{9,1},... | collective-permute-start | bytes 1474568 | tf_op jit(solution)/shard_map/ppermute | solution.py:34
  133.6 7.4 %copy-start.2 = (f32[16,80,256]{2,1,0:T(8,128)S(1)}, f32[16,80,256]{2,1,0:T(8,128)}, u32[]{:S(2)}) copy-start(f32[16,80,256]{2,1,0:T(8,128)} %get-tuple-element.103.refs_1_) | copy-start | bytes 3932164
  135.7 5.2 %copy-start.1 = (f32[16,80,256]{2,1,0:T(8,128)S(1)}, f32[16,80,256]{2,1,0:T(8,128)}, u32[]{:S(2)}) copy-start(f32[16,80,256]{2,1,0:T(8,128)} %get-tuple-element.102.refs_0_) | copy-start | bytes 3932164
  135.7 5.2 %copy-start.7 = (bf16[2,48,256]{2,1,0:T(8,128)(2,1)S(1)}, bf16[2,48,256]{2,1,0:T(8,128)(2,1)}, u32[]{:S(2)}) copy-start(bf16[2,48,256]{2,1,0:T(8,128)(2,1)} %copy-done.6) | copy-start | bytes 147460
  135.8 5.2 %copy-start.13 = (bf16[2,32,256]{2,1,0:T(8,128)(2,1)S(1)}, bf16[2,32,256]{2,1,0:T(8,128)(2,1)}, u32[]{:S(2)}) copy-start(bf16[2,32,256]{2,1,0:T(8,128)(2,1)} %copy-done.12) | copy-start | bytes 98308
  146.1 15.7 %collective-permute-start.28 = (f32[2,15,32,256]{3,2,1,0:T(8,128)S(1)}, f32[2,15,32,256]{3,2,1,0:T(8,128)S(1)}, u32[]{:S(2)}, u32[]{:S(2)}) collective-permute-start(f32[2,15,32,256]{3,2,1,0:T(8,128)S(1)} %get-tuple-element.126), channel_id=1, source_target_pairs={{2,8},{3,9},{4,10},{5,11},{6,12},{7,13},{8,2},{9,3},{10,4},{11,5},... | collective-permute-start | bytes 2949128 | tf_op jit(solution)/shard_map/ppermute | solution.py:34
  148.6 13.2 %collective-permute-start.29 = (f32[2,15,32,256]{3,2,1,0:T(8,128)S(1)}, f32[2,15,32,256]{3,2,1,0:T(8,128)S(1)}, u32[]{:S(2)}, u32[]{:S(2)}) collective-permute-start(f32[2,15,32,256]{3,2,1,0:T(8,128)S(1)} %get-tuple-element.127), channel_id=1, source_target_pairs={{0,8},{1,9},{2,10},{3,11},{4,12},{5,13},{6,14},{7,15},{8,0},{9,1},... | collective-permute-start | bytes 2949128 | tf_op jit(solution)/shard_map/ppermute | solution.py:34
  155.1 17.3 %collective-permute-start.34 = (f32[2,15,32,256]{3,2,1,0:T(8,128)S(1)}, f32[2,15,32,256]{3,2,1,0:T(8,128)S(1)}, u32[]{:S(2)}, u32[]{:S(2)}) collective-permute-start(f32[2,15,32,256]{3,2,1,0:T(8,128)S(1)} %get-tuple-element.137), channel_id=1, source_target_pairs={{2,8},{3,9},{4,10},{5,11},{6,12},{7,13},{8,2},{9,3},{10,4},{11,5},... | collective-permute-start | bytes 2949128 | tf_op jit(solution)/shard_map/ppermute | solution.py:34
  158.2 14.2 %collective-permute-start.35 = (f32[2,15,32,256]{3,2,1,0:T(8,128)S(1)}, f32[2,15,32,256]{3,2,1,0:T(8,128)S(1)}, u32[]{:S(2)}, u32[]{:S(2)}) collective-permute-start(f32[2,15,32,256]{3,2,1,0:T(8,128)S(1)} %get-tuple-element.138), channel_id=1, source_target_pairs={{0,8},{1,9},{2,10},{3,11},{4,12},{5,13},{6,14},{7,15},{8,0},{9,1},... | collective-permute-start | bytes 2949128 | tf_op jit(solution)/shard_map/ppermute | solution.py:34
  163.6 14.3 %collective-permute-start.30 = (f32[16,32,256]{2,1,0:T(8,128)S(1)}, f32[16,32,256]{2,1,0:T(8,128)S(1)}, u32[]{:S(2)}, u32[]{:S(2)}) collective-permute-start(f32[16,32,256]{2,1,0:T(8,128)S(1)} %log_factor.8.refs_0_), channel_id=1, source_target_pairs={{0,16},{2,18},{4,20},{6,22},{9,25},{11,27},{13,29},{15,31},{16,0},... | collective-permute-start | bytes 1572872 | tf_op jit(solution)/shard_map/ppermute | solution.py:34
  164.3 16.3 %collective-permute-start.31 = (f32[16,32,256]{2,1,0:T(8,128)S(1)}, f32[16,32,256]{2,1,0:T(8,128)S(1)}, u32[]{:S(2)}, u32[]{:S(2)}) collective-permute-start(f32[16,32,256]{2,1,0:T(8,128)S(1)} %log_factor.8.refs_0_), channel_id=1, source_target_pairs={{1,24},{3,26},{5,28},{7,30},{8,17},{10,19},{12,21},{14,23},{17,8},... | collective-permute-start | bytes 1572872 | tf_op jit(solution)/shard_map/ppermute | solution.py:34
  166.2 17.3 %collective-permute-start.32 = (f32[16,32,256]{2,1,0:T(8,128)S(1)}, f32[16,32,256]{2,1,0:T(8,128)S(1)}, u32[]{:S(2)}, u32[]{:S(2)}) collective-permute-start(f32[16,32,256]{2,1,0:T(8,128)S(1)} %log_factor.8.refs_0_), channel_id=1, source_target_pairs={{1,8},{3,10},{5,12},{7,14},{8,1},{10,3},{12,5},{14,7},{17,24},{19,... | collective-permute-start | bytes 1572872 | tf_op jit(solution)/shard_map/ppermute | solution.py:34
  174.1 9.6 %collective-permute-start.36 = (f32[16,32,256]{2,1,0:T(8,128)S(1)}, f32[16,32,256]{2,1,0:T(8,128)S(1)}, u32[]{:S(2)}, u32[]{:S(2)}) collective-permute-start(f32[16,32,256]{2,1,0:T(8,128)S(1)} %log_factor.9.refs_0_), channel_id=1, source_target_pairs={{0,16},{2,18},{4,20},{6,22},{9,25},{11,27},{13,29},{15,31},{16,0},... | collective-permute-start | bytes 1572872 | tf_op jit(solution)/shard_map/ppermute | solution.py:34
  174.8 16.0 %collective-permute-start.37 = (f32[16,32,256]{2,1,0:T(8,128)S(1)}, f32[16,32,256]{2,1,0:T(8,128)S(1)}, u32[]{:S(2)}, u32[]{:S(2)}) collective-permute-start(f32[16,32,256]{2,1,0:T(8,128)S(1)} %log_factor.9.refs_0_), channel_id=1, source_target_pairs={{1,24},{3,26},{5,28},{7,30},{8,17},{10,19},{12,21},{14,23},{17,8},... | collective-permute-start | bytes 1572872 | tf_op jit(solution)/shard_map/ppermute | solution.py:34
  177.9 15.3 %collective-permute-start.38 = (f32[16,32,256]{2,1,0:T(8,128)S(1)}, f32[16,32,256]{2,1,0:T(8,128)S(1)}, u32[]{:S(2)}, u32[]{:S(2)}) collective-permute-start(f32[16,32,256]{2,1,0:T(8,128)S(1)} %log_factor.9.refs_0_), channel_id=1, source_target_pairs={{1,8},{3,10},{5,12},{7,14},{8,1},{10,3},{12,5},{14,7},{17,24},{19,... | collective-permute-start | bytes 1572872 | tf_op jit(solution)/shard_map/ppermute | solution.py:34
  183.6 9.8 %collective-permute-start.33 = (f32[16,32,256]{2,1,0:T(8,128)S(1)}, f32[16,32,256]{2,1,0:T(8,128)S(1)}, u32[]{:S(2)}, u32[]{:S(2)}) collective-permute-start(f32[16,32,256]{2,1,0:T(8,128)S(1)} %last_update.2.refs_0_), channel_id=1, source_target_pairs={{0,8},{1,9},{2,10},{3,11},{4,12},{5,13},{6,14},{7,15},{8,0},{9,1},... | collective-permute-start | bytes 1572872 | tf_op jit(solution)/shard_map/ppermute | solution.py:34
  193.2 2.0 %collective-permute-start.39 = (f32[16,32,256]{2,1,0:T(8,128)S(1)}, f32[16,32,256]{2,1,0:T(8,128)S(1)}, u32[]{:S(2)}, u32[]{:S(2)}) collective-permute-start(f32[16,32,256]{2,1,0:T(8,128)S(1)} %last_update.3.refs_2_), channel_id=1, source_target_pairs={{0,8},{1,9},{2,10},{3,11},{4,12},{5,13},{6,14},{7,15},{8,0},{9,1},... | collective-permute-start | bytes 1572872 | tf_op jit(solution)/shard_map/ppermute | solution.py:34
  (11 other events, 13.5 us)

commit v19 on v18

--- a/solution.py
+++ b/solution.py
@@ -631,7 +631,7 @@
     distant, close = neighbours(distant, close)
     first = jnp.where(straight, first, arrived)
 
-    masks = jnp.where(straight, masks, send(after(masks, current), to_row_partner))
+    masks = jnp.where(straight, masks, send(after(masks, second), to_row_partner))
 
     blocks = [(*neighbours(block, block), block) for block in (first, second)]
     wide_parts = blur_x(tables, (current, close), blur_x(tables, (distant,), (), planes), planes)

time: 198 us -> 198 us (level)
  waiting for transfers between devices: 63.5 us -> 67.4 us
  starting transfers between devices: 66.1 us -> 62.8 us
    ppermute x40, waiting for transfers between devices: 63.5 us -> 67.4 us  [send(): return lax.ppermute(array, AXES, moves(move))]
    ppermute x40, starting transfers between devices: 66.1 us -> 62.8 us  [send(): return lax.ppermute(array, AXES, moves(move))]
    unnamed x38 -> x40, local copies, waits for them, and re-layouts: 5.68 us -> 5.69 us
  transfers between devices with their start and end apart: 40 -> 40, of which waited for: 18 -> 19; matrix products, arithmetic and copies ran while one was open for 2% -> 2% of each run, Pallas kernels for 25% -> 25%
where the time goes in v19:
time: 198 us; the launch traced here: 197 us
  waiting for transfers between devices  67.4 us (34%)
  starting transfers between devices  62.8 us (32%)
  Pallas kernels  56.7 us (29%)
  local copies, waits for them, and re-layouts  5.87 us (3%)
  other arithmetic  3.67 us (2%)
    ppermute x40, waiting for transfers between devices, send(): return lax.ppermute(array, AXES, moves(move))  67.4 us
    ppermute x40, starting transfers between devices, send(): return lax.ppermute(array, AXES, moves(move))  62.8 us
    pallas_call x8, Pallas kernels, blur_x(): call(kernel, (shape, shape), [VMEM] * len(operands), 'blur_x_far' if far...  15.2 us
    pallas_call x2, Pallas kernels, next_ratio(): return call(kernel, out_shape, [VMEM] * len(operands), 'ratio')(*operands)  9.34 us
    pallas_call x5, Pallas kernels, log_factor(): call(kernel, shape, [VMEM] * (3 + len(parts)), 'log_factor')  7.69 us
    pallas_call x2, Pallas kernels, first_ratio(): call(kernel, out_shape, in_specs, 'image_and_ratio', scratch, hbm=(len(ou...  7.38 us
    unnamed x40, local copies, waits for them, and re-layouts  5.69 us
    pallas_call x1, Pallas kernels, shift_and_cut(): call(shift_kernel, (shape, shape), [SMEM, VMEM], 'shift_recorded', scratch)  4.48 us
  transfers between devices with their start and end apart: 40, of which 19 were waited for; matrix products, arithmetic and copies ran while one was open for 2% of the time, Pallas kernels for 25%

profile of v19, /device:TPU:17, one launch (start us, length us, event | category | flops | bytes accessed | tf_op | source)
XLA Modules:
  0.0 197.2 jit_solution(12720977254479493205)
XLA Ops:
  0.0 1.6 copy-done
  3.1 4.0 %collective-permute-start.1 = (f32[1,16,128]{2,1,0:T(8,128)S(1)}, f32[1,16,128]{2,1,0:T(8,128)}, u32[]{:S(2)}, u32[]{:S(2)}) collective-permute-start(f32[1,16,128]{2,1,0:T(8,128)S(1)} %convert_element_type.14), channel_id=1, source_target_pairs={{0,8},{1,9},{2,10},{3,11},{4,12},{5,13},{6,14},{7,15},{8,0},{9,1},... | collective-permute-start | bytes 24584 | tf_op jit(solution)/shard_map/ppermute | solution.py:34
  8.3 2.0 %band_matrices.1 = (bf16[2,80,384]{2,1,0:T(8,128)(2,1)S(1)}, bf16[2,64,256]{2,1,0:T(8,128)(2,1)S(1)}, bf16[2,48,256]{2,1,0:T(8,128)(2,1)S(1)}, bf16[2,32,256]{2,...) custom-call(f32[1,384]{1,0:T(1,128)S(1)} %fusion.1.mine_ref, ...), custom_call_target="tpu_custom_call" | custom-call | tf_op jit(solution)/shard_map/band_matrices/pallas_call | solution.py:203
  14.1 1.6 copy-done.3
  15.7 4.5 %shift_recorded.1 = (f32[16,80,256]{2,1,0:T(8,128)}, f32[16,80,256]{2,1,0:T(8,128)}) custom-call(s32[1,3]{1,0:T(1,128)S(1)} %copy-done.14, f32[16,128,256]{2,1,0:T(8,128)S(1)} %bitcast.1), custom_call_target="tpu_custom_call" | custom-call | tf_op jit(solution)/shard_map/shift_recorded/pallas_call | solution.py:284
  20.2 1.9 collective-permute-start.4
  23.0 3.4 %estimate.1 = (f32[16,96,256]{2,1,0:T(8,128)S(1)}, f32[15,96,256]{2,1,0:T(8,128)}) custom-call(f32[16,128,256]{2,1,0:T(8,128)} %estimate_ref.2, f32[16,96,256]{2,1,0:T(8,128)} %collective-permute-done.2.crossed_ref), custom_call_target="tpu_custom_call" | custom-call | tf_op jit(solution)/shard_map/estimate/pallas_call | solution.py:255
  26.4 4.3 %collective-permute-start.10 = (f32[15,96,256]{2,1,0:T(8,128)}, f32[15,96,256]{2,1,0:T(8,128)}, u32[]{:S(2)}, u32[]{:S(2)}) collective-permute-start(f32[15,96,256]{2,1,0:T(8,128)} %get-tuple-element.87), channel_id=1, source_target_pairs={{2,8},{3,9},{4,10},{5,11},{6,12},{7,13},{8,2},{9,3},{10,4},{11,5},... | collective-permute-start | bytes 4423688 | tf_op jit(solution)/shard_map/ppermute | solution.py:34
  32.3 12.4 %collective-permute-done.4 = f32[16,80,256]{2,1,0:T(8,128)} collective-permute-done((f32[16,80,256]{2,1,0:T(8,128)}, f32[16,80,256]{2,1,0:T(8,128)}, u32[]{:S(2)}, u32[]{:S(2)}) %collective-permute-start.4) | collective-permute-done | bytes 1310752 | tf_op jit(solution)/shard_map/ppermute | solution.py:34
  46.3 1.9 collective-permute-start.5
  48.8 4.8 %collective-permute-done.7.own_ref = f32[16,80,256]{2,1,0:T(8,128)} collective-permute-done((f32[16,80,256]{2,1,0:T(8,128)}, f32[16,80,256]{2,1,0:T(8,128)}, u32[]{:S(2)}, u32[]{:S(2)}) %collective-permute-start.7) | collective-permute-done | bytes 1310752 | tf_op jit(solution)/shard_map/ppermute | solution.py:34
  55.5 2.2 %collective-permute-done.8 = f32[2,16,128]{2,1,0:T(8,128)S(1)} collective-permute-done((f32[2,16,128]{2,1,0:T(8,128)S(1)}, f32[2,16,128]{2,1,0:T(8,128)S(1)}, u32[]{:S(2)}, u32[]{:S(2)}) %collective-permute-start.8) | collective-permute-done | bytes 16416 | tf_op jit(solution)/shard_map/ppermute | solution.py:34
  57.7 4.1 %collective-permute-start.13 = (f32[16,80,256]{2,1,0:T(8,128)}, f32[16,80,256]{2,1,0:T(8,128)S(1)}, u32[]{:S(2)}, u32[]{:S(2)}) collective-permute-start(f32[16,80,256]{2,1,0:T(8,128)} %collective-permute-done.7.own_ref), channel_id=1, source_target_pairs={{2,8},{3,9},{4,10},{5,11},{6,12},{7,13},{8,2},{9,3},{10,4},{11,5},... | collective-permute-start | bytes 3932168 | tf_op jit(solution)/shard_map/ppermute | solution.py:34
  62.7 4.4 %blur_x_far.4 = (f32[16,96,256]{2,1,0:T(8,128)S(1)}, f32[16,96,256]{2,1,0:T(8,128)S(1)}) custom-call(bf16[2,256,384]{2,1,0:T(8,128)(2,1)S(1)} %get-tuple-element.74.hi_ref, bf16[2,256,384]{2,1,0:T(8,128)(2,1)S(1)} %get-tuple-element.75.lo_ref, f32[15,96,256]{2,1,0:T(8,128)} %collective-permute-done.10.refs_0_), custom_call_target="tpu_custom_call" | custom-call | tf_op jit(solution)/shard_map/blur_x_far/pallas_call | solution.py:332
  67.2 3.3 %blur_x_near.4 = (f32[16,96,256]{2,1,0:T(8,128)S(1)}, f32[16,96,256]{2,1,0:T(8,128)S(1)}) custom-call(bf16[2,256,384]{2,1,0:T(8,128)(2,1)S(1)} %get-tuple-element.74.hi_ref, bf16[2,256,384]{2,1,0:T(8,128)(2,1)S(1)} %get-tuple-element.75.lo_ref, f32[16,96,256]{2,1,0:T(8,128)S(1)} %get-tuple-element.81.refs_0_.before_ref, ...), custom_call_target="tpu_custom_call" | custom-call | tf_op jit(solution)/shard_map/blur_x_near/pallas_call | solution.py:332
  72.1 3.1 %image_and_ratio.2 = (f32[16,64,256]{2,1,0:T(8,128)S(1)}, f32[15,64,256]{2,1,0:T(8,128)S(1)}, f32[15,64,256]{2,1,0:T(8,128)S(1)}, f32[16,80,256]{2,1,0:T(8,128)}) custom-call(s32[2,3]{1,0:T(2,128)S(1)} %fusion.2.shift_ref, f32[16,80,256]{2,1,0:T(8,128)S(1)} %collective-permute-done.5.far_ref, f32[16,80,256]{2,1,0:T(8,128)S(1)} %collective-permute-done.6.near_ref, ...), custom_call_target="tpu_custom_call" | custom-call | tf_op jit(solution)/shard_map/image_and_ratio/pallas_call | solution.py:487
  75.2 1.9 collective-permute-start.11
  77.8 1.6 blur_yz.3.blurred_ref
  79.4 4.3 %image_and_ratio.3 = (f32[16,64,256]{2,1,0:T(8,128)S(1)}, f32[15,32,256]{2,1,0:T(8,128)S(1)}, f32[15,32,256]{2,1,0:T(8,128)S(1)}, f32[15,32,256]{2,1,0:T(8,128)S...) custom-call(s32[2,3]{1,0:T(2,128)S(1)} %fusion.2.shift_ref, f32[16,80,256]{2,1,0:T(8,128)S(1)} %collective-permute-done.13.far_ref, ...), custom_call_target="tpu_custom_call" | custom-call | tf_op jit(solution)/shard_map/image_and_ratio/pallas_call | solution.py:487
  83.7 3.1 %collective-permute-start.18 = (f32[15,32,256]{2,1,0:T(8,128)S(1)}, f32[15,32,256]{2,1,0:T(8,128)S(1)}, u32[]{:S(2)}, u32[]{:S(2)}) collective-permute-start(f32[15,32,256]{2,1,0:T(8,128)S(1)} %get-tuple-element.105), channel_id=1, source_target_pairs={{2,8},{3,9},{4,10},{5,11},{6,12},{7,13},{8,2},{9,3},{10,4},{11,5},... | collective-permute-start | bytes 1474568 | tf_op jit(solution)/shard_map/ppermute | solution.py:34
  87.3 3.6 %collective-permute-done.11.refs_0_ = f32[15,64,256]{2,1,0:T(8,128)S(1)} collective-permute-done((f32[15,64,256]{2,1,0:T(8,128)S(1)}, f32[15,64,256]{2,1,0:T(8,128)S(1)}, u32[]{:S(2)}, u32[]{:S(2)}) %collective-permute-start.11) | collective-permute-done | bytes 983072 | tf_op jit(solution)/shard_map/ppermute | solution.py:34
  90.9 2.2 %log_factor.5.before_ref = f32[16,64,256]{2,1,0:T(8,128)S(1)} custom-call(bf16[2,256,384]{2,1,0:T(8,128)(2,1)S(1)} %get-tuple-element.74.hi_ref, bf16[2,256,384]{2,1,0:T(8,128)(2,1)S(1)} %get-tuple-element.75.lo_ref, f32[16,96,256]{2,1,0:T(8,128)S(1)} %get-tuple-element.81.refs_0_.before_ref, f32[15,64,256]{2,1,0:T(8,128)S(1)} %collective-permute-done.11.refs_0_, ...), custom_call_target="tpu_custom_call" | custom-call | tf_op jit(solution)/shard_map/log_factor/pallas_call | solution.py:520
  93.1 2.9 %collective-permute-done.18.refs_0_ = f32[15,32,256]{2,1,0:T(8,128)S(1)} collective-permute-done((f32[15,32,256]{2,1,0:T(8,128)S(1)}, f32[15,32,256]{2,1,0:T(8,128)S(1)}, u32[]{:S(2)}, u32[]{:S(2)}) %collective-permute-start.18) | collective-permute-done | bytes 491552 | tf_op jit(solution)/shard_map/ppermute | solution.py:34
  98.4 2.1 %collective-permute-start.15 = (f32[15,32,256]{2,1,0:T(8,128)S(1)}, f32[15,32,256]{2,1,0:T(8,128)S(1)}, u32[]{:S(2)}, u32[]{:S(2)}) collective-permute-start(f32[15,32,256]{2,1,0:T(8,128)S(1)} %get-tuple-element.98), channel_id=1, source_target_pairs={{2,8},{3,9},{4,10},{5,11},{6,12},{7,13},{8,2},{9,3},{10,4},{11,5},... | collective-permute-start | bytes 1474568 | tf_op jit(solution)/shard_map/ppermute | solution.py:34
  101.0 7.8 %collective-permute-done.15.refs_0_ = f32[15,32,256]{2,1,0:T(8,128)S(1)} collective-permute-done((f32[15,32,256]{2,1,0:T(8,128)S(1)}, f32[15,32,256]{2,1,0:T(8,128)S(1)}, u32[]{:S(2)}, u32[]{:S(2)}) %collective-permute-start.15) | collective-permute-done | bytes 491552 | tf_op jit(solution)/shard_map/ppermute | solution.py:34
  111.4 1.7 collective-permute-start.24
  113.1 4.1 %collective-permute-start.21 = (f32[15,32,256]{2,1,0:T(8,128)}, f32[15,32,256]{2,1,0:T(8,128)}, u32[]{:S(2)}, u32[]{:S(2)}) collective-permute-start(f32[15,32,256]{2,1,0:T(8,128)} %get-tuple-element.107), channel_id=1, source_target_pairs={{2,8},{3,9},{4,10},{5,11},{6,12},{7,13},{8,2},{9,3},{10,4},{11,5},... | collective-permute-start | bytes 1474568 | tf_op jit(solution)/shard_map/ppermute | solution.py:34
  117.2 6.0 %collective-permute-done.17.refs_1_ = f32[16,32,256]{2,1,0:T(8,128)} collective-permute-done((f32[16,32,256]{2,1,0:T(8,128)S(1)}, f32[16,32,256]{2,1,0:T(8,128)}, u32[]{:S(2)}, u32[]{:S(2)}) %collective-permute-start.17) | collective-permute-done | bytes 524320 | tf_op jit(solution)/shard_map/ppermute | solution.py:34
  125.8 1.9 collective-permute-start.22
  127.8 3.6 %collective-permute-start.25 = (f32[15,32,256]{2,1,0:T(8,128)S(1)}, f32[15,32,256]{2,1,0:T(8,128)S(1)}, u32[]{:S(2)}, u32[]{:S(2)}) collective-permute-start(f32[15,32,256]{2,1,0:T(8,128)S(1)} %get-tuple-element.142), channel_id=1, source_target_pairs={{2,8},{3,9},{4,10},{5,11},{6,12},{7,13},{8,2},{9,3},{10,4},{11,5},... | collective-permute-start | bytes 1474568 | tf_op jit(solution)/shard_map/ppermute | solution.py:34
  134.1 2.2 %blur_x_far.6 = (f32[16,32,256]{2,1,0:T(8,128)S(1)}, f32[16,32,256]{2,1,0:T(8,128)S(1)}) custom-call(bf16[2,256,384]{2,1,0:T(8,128)(2,1)S(1)} %get-tuple-element.74.hi_ref, bf16[2,256,384]{2,1,0:T(8,128)(2,1)S(1)} %get-tuple-element.75.lo_ref, f32[15,32,256]{2,1,0:T(8,128)} %collective-permute-done.21.refs_0_, ...), custom_call_target="tpu_custom_call" | custom-call | tf_op jit(solution)/shard_map/blur_x_far/pallas_call | solution.py:332
  137.4 3.8 %collective-permute-done.25.refs_0_ = f32[15,32,256]{2,1,0:T(8,128)S(1)} collective-permute-done((f32[15,32,256]{2,1,0:T(8,128)S(1)}, f32[15,32,256]{2,1,0:T(8,128)S(1)}, u32[]{:S(2)}, u32[]{:S(2)}) %collective-permute-start.25) | collective-permute-done | bytes 491552 | tf_op jit(solution)/shard_map/ppermute | solution.py:34
  141.2 5.2 %ratio.2 = (f32[16,32,256]{2,1,0:T(8,128)S(1)}, f32[16,32,256]{2,1,0:T(8,128)S(1)}, f32[2,15,32,256]{3,2,1,0:T(8,128)S(1)}, f32[2,15,32,256]{3,2,1,0:T(8,128)S(1)}, f32[2,16,32,256]{3,2,1,0:T(8,128)S(1)}) custom-call(f32[16,80,256]{2,1,0:T(8,128)S(1)} %copy-done.1, f32[16,80,256]{2,1,0:T(8,128)S(1)} %copy-done.2, ...), custom_call_target="tpu_custom_call" | custom-call | tf_op jit(solution)/shard_map/ratio/pallas_call | solution.py:475
  146.4 1.9 collective-permute-start.28
  151.2 4.2 %ratio.3 = (f32[16,32,256]{2,1,0:T(8,128)S(1)}, f32[16,32,256]{2,1,0:T(8,128)S(1)}, f32[2,15,32,256]{3,2,1,0:T(8,128)S(1)}, f32[2,15,32,256]{3,2,1,0:T(8,128)S(1)}) custom-call(f32[16,80,256]{2,1,0:T(8,128)S(1)} %copy-done.1, f32[16,80,256]{2,1,0:T(8,128)S(1)} %copy-done.2, f32[16,32,256]{2,1,0:T(8,128)S(1)} %get-tuple-element.119.refs_3_.refs_2_, ...), custom_call_target="tpu_custom_call" | custom-call | tf_op jit(solution)/shard_map/ratio/pallas_call | solution.py:475
  155.4 3.0 %collective-permute-start.34 = (f32[2,15,32,256]{3,2,1,0:T(8,128)S(1)}, f32[2,15,32,256]{3,2,1,0:T(8,128)S(1)}, u32[]{:S(2)}, u32[]{:S(2)}) collective-permute-start(f32[2,15,32,256]{3,2,1,0:T(8,128)S(1)} %get-tuple-element.137), channel_id=1, source_target_pairs={{2,8},{3,9},{4,10},{5,11},{6,12},{7,13},{8,2},{9,3},{10,4},{11,5},... | collective-permute-start | bytes 2949128 | tf_op jit(solution)/shard_map/ppermute | solution.py:34
  158.8 3.3 %collective-permute-done.28.refs_0_.refs_3_ = f32[2,15,32,256]{3,2,1,0:T(8,128)S(1)} collective-permute-done((f32[2,15,32,256]{3,2,1,0:T(8,128)S(1)}, f32[2,15,32,256]{3,2,1,0:T(8,128)S(1)}, u32[]{:S(2)}, u32[]{:S(2)}) %collective-permute-start.28) | collective-permute-done | bytes 983072 | tf_op jit(solution)/shard_map/ppermute | solution.py:34
  162.1 1.7 log_factor.8.refs_0_
  164.5 2.5 %collective-permute-start.31 = (f32[16,32,256]{2,1,0:T(8,128)S(1)}, f32[16,32,256]{2,1,0:T(8,128)S(1)}, u32[]{:S(2)}, u32[]{:S(2)}) collective-permute-start(f32[16,32,256]{2,1,0:T(8,128)S(1)} %log_factor.8.refs_0_), channel_id=1, source_target_pairs={{1,24},{3,26},{5,28},{7,30},{8,17},{10,19},{12,21},{14,23},{17,8},... | collective-permute-start | bytes 1572872 | tf_op jit(solution)/shard_map/ppermute | solution.py:34
  167.0 3.0 %collective-permute-start.32 = (f32[16,32,256]{2,1,0:T(8,128)S(1)}, f32[16,32,256]{2,1,0:T(8,128)S(1)}, u32[]{:S(2)}, u32[]{:S(2)}) collective-permute-start(f32[16,32,256]{2,1,0:T(8,128)S(1)} %log_factor.8.refs_0_), channel_id=1, source_target_pairs={{1,8},{3,10},{5,12},{7,14},{8,1},{10,3},{12,5},{14,7},{17,24},{19,... | collective-permute-start | bytes 1572872 | tf_op jit(solution)/shard_map/ppermute | solution.py:34
  170.0 2.6 %collective-permute-done.34.refs_0_.refs_3_ = f32[2,15,32,256]{3,2,1,0:T(8,128)S(1)} collective-permute-done((f32[2,15,32,256]{3,2,1,0:T(8,128)S(1)}, f32[2,15,32,256]{3,2,1,0:T(8,128)S(1)}, u32[]{:S(2)}, u32[]{:S(2)}) %collective-permute-start.34) | collective-permute-done | bytes 983072 | tf_op jit(solution)/shard_map/ppermute | solution.py:34
  172.6 1.7 log_factor.9.refs_0_
  175.0 2.5 %collective-permute-start.37 = (f32[16,32,256]{2,1,0:T(8,128)S(1)}, f32[16,32,256]{2,1,0:T(8,128)S(1)}, u32[]{:S(2)}, u32[]{:S(2)}) collective-permute-start(f32[16,32,256]{2,1,0:T(8,128)S(1)} %log_factor.9.refs_0_), channel_id=1, source_target_pairs={{1,24},{3,26},{5,28},{7,30},{8,17},{10,19},{12,21},{14,23},{17,8},... | collective-permute-start | bytes 1572872 | tf_op jit(solution)/shard_map/ppermute | solution.py:34
  177.6 3.0 %collective-permute-start.38 = (f32[16,32,256]{2,1,0:T(8,128)S(1)}, f32[16,32,256]{2,1,0:T(8,128)S(1)}, u32[]{:S(2)}, u32[]{:S(2)}) collective-permute-start(f32[16,32,256]{2,1,0:T(8,128)S(1)} %log_factor.9.refs_0_), channel_id=1, source_target_pairs={{1,8},{3,10},{5,12},{7,14},{8,1},{10,3},{12,5},{14,7},{17,24},{19,... | collective-permute-start | bytes 1572872 | tf_op jit(solution)/shard_map/ppermute | solution.py:34
  180.7 3.5 %collective-permute-done.32.refs_3_ = f32[16,32,256]{2,1,0:T(8,128)S(1)} collective-permute-done((f32[16,32,256]{2,1,0:T(8,128)S(1)}, f32[16,32,256]{2,1,0:T(8,128)S(1)}, u32[]{:S(2)}, u32[]{:S(2)}) %collective-permute-start.32) | collective-permute-done | bytes 524320 | tf_op jit(solution)/shard_map/ppermute | solution.py:34
  184.4 7.0 %collective-permute-done.37.refs_2_ = f32[16,32,256]{2,1,0:T(8,128)S(1)} collective-permute-done((f32[16,32,256]{2,1,0:T(8,128)S(1)}, f32[16,32,256]{2,1,0:T(8,128)S(1)}, u32[]{:S(2)}, u32[]{:S(2)}) %collective-permute-start.37) | collective-permute-done | bytes 524320 | tf_op jit(solution)/shard_map/ppermute | solution.py:34
  191.3 2.3 %collective-permute-done.38.refs_3_ = f32[16,32,256]{2,1,0:T(8,128)S(1)} collective-permute-done((f32[16,32,256]{2,1,0:T(8,128)S(1)}, f32[16,32,256]{2,1,0:T(8,128)S(1)}, u32[]{:S(2)}, u32[]{:S(2)}) %collective-permute-start.38) | collective-permute-done | bytes 524320 | tf_op jit(solution)/shard_map/ppermute | solution.py:34
  193.8 1.9 collective-permute-done.39.refs_3_
  (109 shorter events, 34.9 us)
Async XLA Ops:
  1.6 5.4 %copy-start.17 = (f32[1,61]{1,0:T(1,128)S(1)}, f32[1,61]{1,0:T(1,128)}, u32[]{:S(2)}) copy-start(f32[1,61]{1,0:T(1,128)} %param.13) | copy-start | bytes 736
  1.6 5.4 %copy-start.18 = (f32[1,31]{1,0:T(1,128)S(1)}, f32[1,31]{1,0:T(1,128)}, u32[]{:S(2)}) copy-start(f32[1,31]{1,0:T(1,128)} %param.12) | copy-start | bytes 376
  1.6 5.4 %copy-start.19 = (f32[1,31]{1,0:T(1,128)S(1)}, f32[1,31]{1,0:T(1,128)}, u32[]{:S(2)}) copy-start(f32[1,31]{1,0:T(1,128)} %param.11) | copy-start | bytes 376
  1.6 12.5 %copy-start.14 = (s32[1,3]{1,0:T(1,128)S(1)}, s32[1,3]{1,0:T(1,128)}, u32[]{:S(2)}) copy-start(s32[1,3]{1,0:T(1,128)} %offsets_ref.1) | copy-start | bytes 40
  1.7 21.3 %collective-permute-start.2 = (f32[16,96,256]{2,1,0:T(8,128)S(1)}, f32[16,96,256]{2,1,0:T(8,128)}, u32[]{:S(2)}, u32[]{:S(2)}) collective-permute-start(f32[16,96,256]{2,1,0:T(8,128)S(1)} %other_window.1), channel_id=1, source_target_pairs={{0,1},{2,3},{4,5},{6,7},{9,8},{11,10},{13,12},{15,14},{16,17},{18,... | collective-permute-start | bytes 4718600 | tf_op jit(solution)/shard_map/ppermute | solution.py:34
  3.1 9.7 %collective-permute-start.1 = (f32[1,16,128]{2,1,0:T(8,128)S(1)}, f32[1,16,128]{2,1,0:T(8,128)}, u32[]{:S(2)}, u32[]{:S(2)}) collective-permute-start(f32[1,16,128]{2,1,0:T(8,128)S(1)} %convert_element_type.14), channel_id=1, source_target_pairs={{0,8},{1,9},{2,10},{3,11},{4,12},{5,13},{6,14},{7,15},{8,0},{9,1},... | collective-permute-start | bytes 24584 | tf_op jit(solution)/shard_map/ppermute | solution.py:34
  7.0 1.2 collective-permute-start
  20.2 24.6 %collective-permute-start.4 = (f32[16,80,256]{2,1,0:T(8,128)}, f32[16,80,256]{2,1,0:T(8,128)}, u32[]{:S(2)}, u32[]{:S(2)}) collective-permute-start(f32[16,80,256]{2,1,0:T(8,128)} %get-tuple-element.83), channel_id=1, source_target_pairs={{1,8},{3,10},{5,12},{7,14},{8,1},{10,3},{12,5},{14,7},{17,24},{19,... | collective-permute-start | bytes 3932168 | tf_op jit(solution)/shard_map/ppermute | solution.py:34
  26.4 35.4 %collective-permute-start.10 = (f32[15,96,256]{2,1,0:T(8,128)}, f32[15,96,256]{2,1,0:T(8,128)}, u32[]{:S(2)}, u32[]{:S(2)}) collective-permute-start(f32[15,96,256]{2,1,0:T(8,128)} %get-tuple-element.87), channel_id=1, source_target_pairs={{2,8},{3,9},{4,10},{5,11},{6,12},{7,13},{8,2},{9,3},{10,4},{11,5},... | collective-permute-start | bytes 4423688 | tf_op jit(solution)/shard_map/ppermute | solution.py:34
  30.7 22.9 %collective-permute-start.7 = (f32[16,80,256]{2,1,0:T(8,128)}, f32[16,80,256]{2,1,0:T(8,128)}, u32[]{:S(2)}, u32[]{:S(2)}) collective-permute-start(f32[16,80,256]{2,1,0:T(8,128)} %get-tuple-element.85), channel_id=1, source_target_pairs={{0,1},{1,9},{2,3},{3,11},{4,5},{5,13},{6,7},{7,15},{8,0},{9,8},{10... | collective-permute-start | bytes 3932168 | tf_op jit(solution)/shard_map/ppermute | solution.py:34
  30.9 23.9 %copy-start.15 = (f32[2,16,128]{2,1,0:T(8,128)S(1)}, f32[2,16,128]{2,1,0:T(8,128)}, u32[]{:S(2)}) copy-start(f32[2,16,128]{2,1,0:T(8,128)} %maximum_select_fusion) | copy-start | bytes 49156
  30.9 36.3 %collective-permute-start.9 = (f32[15,96,256]{2,1,0:T(8,128)S(1)}, f32[15,96,256]{2,1,0:T(8,128)S(1)}, u32[]{:S(2)}, u32[]{:S(2)}) collective-permute-start(f32[15,96,256]{2,1,0:T(8,128)S(1)} %constant_dynamic-slice_fusion.2), channel_id=1, source_target_pairs={{0,8},{1,9},{2,10},{3,11},{4,12},{5,13},{6,14},{7,15},{8,0},{9,1},... | collective-permute-start | bytes 4423688 | tf_op jit(solution)/shard_map/ppermute | solution.py:34
  46.3 25.8 %collective-permute-start.5 = (f32[16,80,256]{2,1,0:T(8,128)S(1)}, f32[16,80,256]{2,1,0:T(8,128)S(1)}, u32[]{:S(2)}, u32[]{:S(2)}) collective-permute-start(f32[16,80,256]{2,1,0:T(8,128)S(1)} %broadcast_select_fusion.own_ref), channel_id=1, source_target_pairs={{2,8},{3,9},{4,10},{5,11},{6,12},{7,13},{8,2},{9,3},{10,4},{11,5},... | collective-permute-start | bytes 3932168 | tf_op jit(solution)/shard_map/ppermute | solution.py:34
  48.2 23.9 %collective-permute-start.6 = (f32[16,80,256]{2,1,0:T(8,128)S(1)}, f32[16,80,256]{2,1,0:T(8,128)S(1)}, u32[]{:S(2)}, u32[]{:S(2)}) collective-permute-start(f32[16,80,256]{2,1,0:T(8,128)S(1)} %broadcast_select_fusion.own_ref), channel_id=1, source_target_pairs={{0,8},{1,9},{2,10},{3,11},{4,12},{5,13},{6,14},{7,15},{8,0},{9,1},... | collective-permute-start | bytes 3932168 | tf_op jit(solution)/shard_map/ppermute | solution.py:34
  53.7 1.1 collective-permute-start.3
  54.8 2.9 %collective-permute-start.8 = (f32[2,16,128]{2,1,0:T(8,128)S(1)}, f32[2,16,128]{2,1,0:T(8,128)S(1)}, u32[]{:S(2)}, u32[]{:S(2)}) collective-permute-start(f32[2,16,128]{2,1,0:T(8,128)S(1)} %copy-done.15), channel_id=1, source_target_pairs={{0,1},{1,0},{2,3},{3,2},{4,5},{5,4},{6,7},{7,6},{8,9},{9,8},{10,11... | collective-permute-start | bytes 49160 | tf_op jit(solution)/shard_map/ppermute | solution.py:34
  57.7 21.7 %collective-permute-start.13 = (f32[16,80,256]{2,1,0:T(8,128)}, f32[16,80,256]{2,1,0:T(8,128)S(1)}, u32[]{:S(2)}, u32[]{:S(2)}) collective-permute-start(f32[16,80,256]{2,1,0:T(8,128)} %collective-permute-done.7.own_ref), channel_id=1, source_target_pairs={{2,8},{3,9},{4,10},{5,11},{6,12},{7,13},{8,2},{9,3},{10,4},{11,5},... | collective-permute-start | bytes 3932168 | tf_op jit(solution)/shard_map/ppermute | solution.py:34
  61.8 17.5 %collective-permute-start.14 = (f32[16,80,256]{2,1,0:T(8,128)}, f32[16,80,256]{2,1,0:T(8,128)S(1)}, u32[]{:S(2)}, u32[]{:S(2)}) collective-permute-start(f32[16,80,256]{2,1,0:T(8,128)} %collective-permute-done.7.own_ref), channel_id=1, source_target_pairs={{0,8},{1,9},{2,10},{3,11},{4,12},{5,13},{6,14},{7,15},{8,0},{9,1},... | collective-permute-start | bytes 3932168 | tf_op jit(solution)/shard_map/ppermute | solution.py:34
  75.2 15.7 %collective-permute-start.11 = (f32[15,64,256]{2,1,0:T(8,128)S(1)}, f32[15,64,256]{2,1,0:T(8,128)S(1)}, u32[]{:S(2)}, u32[]{:S(2)}) collective-permute-start(f32[15,64,256]{2,1,0:T(8,128)S(1)} %get-tuple-element.94), channel_id=1, source_target_pairs={{2,8},{3,9},{4,10},{5,11},{6,12},{7,13},{8,2},{9,3},{10,4},{11,5},... | collective-permute-start | bytes 2949128 | tf_op jit(solution)/shard_map/ppermute | solution.py:34
  77.2 13.8 %collective-permute-start.12 = (f32[15,64,256]{2,1,0:T(8,128)S(1)}, f32[15,64,256]{2,1,0:T(8,128)S(1)}, u32[]{:S(2)}, u32[]{:S(2)}) collective-permute-start(f32[15,64,256]{2,1,0:T(8,128)S(1)} %get-tuple-element.95), channel_id=1, source_target_pairs={{0,8},{1,9},{2,10},{3,11},{4,12},{5,13},{6,14},{7,15},{8,0},{9,1},... | collective-permute-start | bytes 2949128 | tf_op jit(solution)/shard_map/ppermute | solution.py:34
  83.7 12.4 %collective-permute-start.18 = (f32[15,32,256]{2,1,0:T(8,128)S(1)}, f32[15,32,256]{2,1,0:T(8,128)S(1)}, u32[]{:S(2)}, u32[]{:S(2)}) collective-permute-start(f32[15,32,256]{2,1,0:T(8,128)S(1)} %get-tuple-element.105), channel_id=1, source_target_pairs={{2,8},{3,9},{4,10},{5,11},{6,12},{7,13},{8,2},{9,3},{10,4},{11,5},... | collective-permute-start | bytes 1474568 | tf_op jit(solution)/shard_map/ppermute | solution.py:34
  86.7 9.3 %collective-permute-start.19 = (f32[15,32,256]{2,1,0:T(8,128)S(1)}, f32[15,32,256]{2,1,0:T(8,128)S(1)}, u32[]{:S(2)}, u32[]{:S(2)}) collective-permute-start(f32[15,32,256]{2,1,0:T(8,128)S(1)} %get-tuple-element.106), channel_id=1, source_target_pairs={{0,8},{1,9},{2,10},{3,11},{4,12},{5,13},{6,14},{7,15},{8,0},{9,1},... | collective-permute-start | bytes 1474568 | tf_op jit(solution)/shard_map/ppermute | solution.py:34
  97.1 13.2 %collective-permute-start.20 = (f32[16,32,256]{2,1,0:T(8,128)S(1)}, f32[16,32,256]{2,1,0:T(8,128)S(1)}, u32[]{:S(2)}, u32[]{:S(2)}) collective-permute-start(f32[16,32,256]{2,1,0:T(8,128)S(1)} %log_factor.7.refs_0_), channel_id=1, source_target_pairs={{0,16},{1,17},{2,18},{3,19},{4,20},{5,21},{6,22},{7,23},{8,24},{9,... | collective-permute-start | bytes 1572872 | tf_op jit(solution)/shard_map/ppermute | solution.py:34
  98.4 10.4 %collective-permute-start.15 = (f32[15,32,256]{2,1,0:T(8,128)S(1)}, f32[15,32,256]{2,1,0:T(8,128)S(1)}, u32[]{:S(2)}, u32[]{:S(2)}) collective-permute-start(f32[15,32,256]{2,1,0:T(8,128)S(1)} %get-tuple-element.98), channel_id=1, source_target_pairs={{2,8},{3,9},{4,10},{5,11},{6,12},{7,13},{8,2},{9,3},{10,4},{11,5},... | collective-permute-start | bytes 1474568 | tf_op jit(solution)/shard_map/ppermute | solution.py:34
  100.5 8.4 %collective-permute-start.16 = (f32[15,32,256]{2,1,0:T(8,128)S(1)}, f32[15,32,256]{2,1,0:T(8,128)S(1)}, u32[]{:S(2)}, u32[]{:S(2)}) collective-permute-start(f32[15,32,256]{2,1,0:T(8,128)S(1)} %get-tuple-element.99), channel_id=1, source_target_pairs={{0,8},{1,9},{2,10},{3,11},{4,12},{5,13},{6,14},{7,15},{8,0},{9,1},... | collective-permute-start | bytes 1474568 | tf_op jit(solution)/shard_map/ppermute | solution.py:34
  109.9 13.3 %collective-permute-start.17 = (f32[16,32,256]{2,1,0:T(8,128)S(1)}, f32[16,32,256]{2,1,0:T(8,128)}, u32[]{:S(2)}, u32[]{:S(2)}) collective-permute-start(f32[16,32,256]{2,1,0:T(8,128)S(1)} %log_factor.6.refs_0_), channel_id=1, source_target_pairs={{0,16},{1,17},{2,18},{3,19},{4,20},{5,21},{6,22},{7,23},{8,24},{9,... | collective-permute-start | bytes 1572872 | tf_op jit(solution)/shard_map/ppermute | solution.py:34
  111.4 16.3 %collective-permute-start.24 = (f32[16,32,256]{2,1,0:T(8,128)S(1)}, f32[16,32,256]{2,1,0:T(8,128)S(1)}, u32[]{:S(2)}, u32[]{:S(2)}) collective-permute-start(f32[16,32,256]{2,1,0:T(8,128)S(1)} %get-tuple-element.113.refs_0_.before_ref), channel_id=1, source_target_pairs={{0,1},{1,0},{2,3},{3,2},{4,5},{5,4},{6,7},{7,6},{8,9},{9,8},{10,11... | collective-permute-start | bytes 1572872 | tf_op jit(solution)/shard_map/ppermute | solution.py:34
  113.1 12.6 %collective-permute-start.21 = (f32[15,32,256]{2,1,0:T(8,128)}, f32[15,32,256]{2,1,0:T(8,128)}, u32[]{:S(2)}, u32[]{:S(2)}) collective-permute-start(f32[15,32,256]{2,1,0:T(8,128)} %get-tuple-element.107), channel_id=1, source_target_pairs={{2,8},{3,9},{4,10},{5,11},{6,12},{7,13},{8,2},{9,3},{10,4},{11,5},... | collective-permute-start | bytes 1474568 | tf_op jit(solution)/shard_map/ppermute | solution.py:34
  124.4 8.6 %collective-permute-start.23 = (f32[15,32,256]{2,1,0:T(8,128)S(1)}, f32[15,32,256]{2,1,0:T(8,128)S(1)}, u32[]{:S(2)}, u32[]{:S(2)}) collective-permute-start(f32[15,32,256]{2,1,0:T(8,128)S(1)} %get-tuple-element.109), channel_id=1, source_target_pairs={{0,8},{1,9},{2,10},{3,11},{4,12},{5,13},{6,14},{7,15},{8,0},{9,1},... | collective-permute-start | bytes 1474568 | tf_op jit(solution)/shard_map/ppermute | solution.py:34
  125.7 6.2 %collective-permute-start.27 = (f32[15,32,256]{2,1,0:T(8,128)}, f32[15,32,256]{2,1,0:T(8,128)S(1)}, u32[]{:S(2)}, u32[]{:S(2)}) collective-permute-start(f32[15,32,256]{2,1,0:T(8,128)} %get-tuple-element.116), channel_id=1, source_target_pairs={{0,8},{1,9},{2,10},{3,11},{4,12},{5,13},{6,14},{7,15},{8,0},{9,1},... | collective-permute-start | bytes 1474568 | tf_op jit(solution)/shard_map/ppermute | solution.py:34
  125.8 10.6 %collective-permute-start.22 = (f32[15,32,256]{2,1,0:T(8,128)S(1)}, f32[15,32,256]{2,1,0:T(8,128)S(1)}, u32[]{:S(2)}, u32[]{:S(2)}) collective-permute-start(f32[15,32,256]{2,1,0:T(8,128)S(1)} %get-tuple-element.108), channel_id=1, source_target_pairs={{2,8},{3,9},{4,10},{5,11},{6,12},{7,13},{8,2},{9,3},{10,4},{11,5},... | collective-permute-start | bytes 1474568 | tf_op jit(solution)/shard_map/ppermute | solution.py:34
  127.8 13.4 %collective-permute-start.25 = (f32[15,32,256]{2,1,0:T(8,128)S(1)}, f32[15,32,256]{2,1,0:T(8,128)S(1)}, u32[]{:S(2)}, u32[]{:S(2)}) collective-permute-start(f32[15,32,256]{2,1,0:T(8,128)S(1)} %get-tuple-element.142), channel_id=1, source_target_pairs={{2,8},{3,9},{4,10},{5,11},{6,12},{7,13},{8,2},{9,3},{10,4},{11,5},... | collective-permute-start | bytes 1474568 | tf_op jit(solution)/shard_map/ppermute | solution.py:34
  131.4 9.8 %collective-permute-start.26 = (f32[15,32,256]{2,1,0:T(8,128)S(1)}, f32[15,32,256]{2,1,0:T(8,128)S(1)}, u32[]{:S(2)}, u32[]{:S(2)}) collective-permute-start(f32[15,32,256]{2,1,0:T(8,128)S(1)} %get-tuple-element.141), channel_id=1, source_target_pairs={{0,8},{1,9},{2,10},{3,11},{4,12},{5,13},{6,14},{7,15},{8,0},{9,1},... | collective-permute-start | bytes 1474568 | tf_op jit(solution)/shard_map/ppermute | solution.py:34
  134.1 7.1 %copy-start.2 = (f32[16,80,256]{2,1,0:T(8,128)S(1)}, f32[16,80,256]{2,1,0:T(8,128)}, u32[]{:S(2)}) copy-start(f32[16,80,256]{2,1,0:T(8,128)} %get-tuple-element.103.refs_1_) | copy-start | bytes 3932164
  136.3 4.9 %copy-start.1 = (f32[16,80,256]{2,1,0:T(8,128)S(1)}, f32[16,80,256]{2,1,0:T(8,128)}, u32[]{:S(2)}) copy-start(f32[16,80,256]{2,1,0:T(8,128)} %get-tuple-element.102.refs_0_) | copy-start | bytes 3932164
  136.3 4.9 %copy-start.7 = (bf16[2,48,256]{2,1,0:T(8,128)(2,1)S(1)}, bf16[2,48,256]{2,1,0:T(8,128)(2,1)}, u32[]{:S(2)}) copy-start(bf16[2,48,256]{2,1,0:T(8,128)(2,1)} %copy-done.6) | copy-start | bytes 147460
  146.4 15.7 %collective-permute-start.28 = (f32[2,15,32,256]{3,2,1,0:T(8,128)S(1)}, f32[2,15,32,256]{3,2,1,0:T(8,128)S(1)}, u32[]{:S(2)}, u32[]{:S(2)}) collective-permute-start(f32[2,15,32,256]{3,2,1,0:T(8,128)S(1)} %get-tuple-element.126), channel_id=1, source_target_pairs={{2,8},{3,9},{4,10},{5,11},{6,12},{7,13},{8,2},{9,3},{10,4},{11,5},... | collective-permute-start | bytes 2949128 | tf_op jit(solution)/shard_map/ppermute | solution.py:34
  148.3 13.8 %collective-permute-start.29 = (f32[2,15,32,256]{3,2,1,0:T(8,128)S(1)}, f32[2,15,32,256]{3,2,1,0:T(8,128)S(1)}, u32[]{:S(2)}, u32[]{:S(2)}) collective-permute-start(f32[2,15,32,256]{3,2,1,0:T(8,128)S(1)} %get-tuple-element.127), channel_id=1, source_target_pairs={{0,8},{1,9},{2,10},{3,11},{4,12},{5,13},{6,14},{7,15},{8,0},{9,1},... | collective-permute-start | bytes 2949128 | tf_op jit(solution)/shard_map/ppermute | solution.py:34
  155.4 17.2 %collective-permute-start.34 = (f32[2,15,32,256]{3,2,1,0:T(8,128)S(1)}, f32[2,15,32,256]{3,2,1,0:T(8,128)S(1)}, u32[]{:S(2)}, u32[]{:S(2)}) collective-permute-start(f32[2,15,32,256]{3,2,1,0:T(8,128)S(1)} %get-tuple-element.137), channel_id=1, source_target_pairs={{2,8},{3,9},{4,10},{5,11},{6,12},{7,13},{8,2},{9,3},{10,4},{11,5},... | collective-permute-start | bytes 2949128 | tf_op jit(solution)/shard_map/ppermute | solution.py:34
  158.4 14.2 %collective-permute-start.35 = (f32[2,15,32,256]{3,2,1,0:T(8,128)S(1)}, f32[2,15,32,256]{3,2,1,0:T(8,128)S(1)}, u32[]{:S(2)}, u32[]{:S(2)}) collective-permute-start(f32[2,15,32,256]{3,2,1,0:T(8,128)S(1)} %get-tuple-element.138), channel_id=1, source_target_pairs={{0,8},{1,9},{2,10},{3,11},{4,12},{5,13},{6,14},{7,15},{8,0},{9,1},... | collective-permute-start | bytes 2949128 | tf_op jit(solution)/shard_map/ppermute | solution.py:34
  163.8 13.8 %collective-permute-start.30 = (f32[16,32,256]{2,1,0:T(8,128)S(1)}, f32[16,32,256]{2,1,0:T(8,128)S(1)}, u32[]{:S(2)}, u32[]{:S(2)}) collective-permute-start(f32[16,32,256]{2,1,0:T(8,128)S(1)} %log_factor.8.refs_0_), channel_id=1, source_target_pairs={{0,16},{2,18},{4,20},{6,22},{9,25},{11,27},{13,29},{15,31},{16,0},... | collective-permute-start | bytes 1572872 | tf_op jit(solution)/shard_map/ppermute | solution.py:34
  164.5 16.2 %collective-permute-start.31 = (f32[16,32,256]{2,1,0:T(8,128)S(1)}, f32[16,32,256]{2,1,0:T(8,128)S(1)}, u32[]{:S(2)}, u32[]{:S(2)}) collective-permute-start(f32[16,32,256]{2,1,0:T(8,128)S(1)} %log_factor.8.refs_0_), channel_id=1, source_target_pairs={{1,24},{3,26},{5,28},{7,30},{8,17},{10,19},{12,21},{14,23},{17,8},... | collective-permute-start | bytes 1572872 | tf_op jit(solution)/shard_map/ppermute | solution.py:34
  167.0 17.1 %collective-permute-start.32 = (f32[16,32,256]{2,1,0:T(8,128)S(1)}, f32[16,32,256]{2,1,0:T(8,128)S(1)}, u32[]{:S(2)}, u32[]{:S(2)}) collective-permute-start(f32[16,32,256]{2,1,0:T(8,128)S(1)} %log_factor.8.refs_0_), channel_id=1, source_target_pairs={{1,8},{3,10},{5,12},{7,14},{8,1},{10,3},{12,5},{14,7},{17,24},{19,... | collective-permute-start | bytes 1572872 | tf_op jit(solution)/shard_map/ppermute | solution.py:34
  174.3 10.0 %collective-permute-start.36 = (f32[16,32,256]{2,1,0:T(8,128)S(1)}, f32[16,32,256]{2,1,0:T(8,128)S(1)}, u32[]{:S(2)}, u32[]{:S(2)}) collective-permute-start(f32[16,32,256]{2,1,0:T(8,128)S(1)} %log_factor.9.refs_0_), channel_id=1, source_target_pairs={{0,16},{2,18},{4,20},{6,22},{9,25},{11,27},{13,29},{15,31},{16,0},... | collective-permute-start | bytes 1572872 | tf_op jit(solution)/shard_map/ppermute | solution.py:34
  175.0 16.3 %collective-permute-start.37 = (f32[16,32,256]{2,1,0:T(8,128)S(1)}, f32[16,32,256]{2,1,0:T(8,128)S(1)}, u32[]{:S(2)}, u32[]{:S(2)}) collective-permute-start(f32[16,32,256]{2,1,0:T(8,128)S(1)} %log_factor.9.refs_0_), channel_id=1, source_target_pairs={{1,24},{3,26},{5,28},{7,30},{8,17},{10,19},{12,21},{14,23},{17,8},... | collective-permute-start | bytes 1572872 | tf_op jit(solution)/shard_map/ppermute | solution.py:34
  177.6 16.0 %collective-permute-start.38 = (f32[16,32,256]{2,1,0:T(8,128)S(1)}, f32[16,32,256]{2,1,0:T(8,128)S(1)}, u32[]{:S(2)}, u32[]{:S(2)}) collective-permute-start(f32[16,32,256]{2,1,0:T(8,128)S(1)} %log_factor.9.refs_0_), channel_id=1, source_target_pairs={{1,8},{3,10},{5,12},{7,14},{8,1},{10,3},{12,5},{14,7},{17,24},{19,... | collective-permute-start | bytes 1572872 | tf_op jit(solution)/shard_map/ppermute | solution.py:34
  184.3 9.5 %collective-permute-start.33 = (f32[16,32,256]{2,1,0:T(8,128)S(1)}, f32[16,32,256]{2,1,0:T(8,128)S(1)}, u32[]{:S(2)}, u32[]{:S(2)}) collective-permute-start(f32[16,32,256]{2,1,0:T(8,128)S(1)} %last_update.2.refs_0_), channel_id=1, source_target_pairs={{0,8},{1,9},{2,10},{3,11},{4,12},{5,13},{6,14},{7,15},{8,0},{9,1},... | collective-permute-start | bytes 1572872 | tf_op jit(solution)/shard_map/ppermute | solution.py:34
  193.7 2.0 %collective-permute-start.39 = (f32[16,32,256]{2,1,0:T(8,128)S(1)}, f32[16,32,256]{2,1,0:T(8,128)S(1)}, u32[]{:S(2)}, u32[]{:S(2)}) collective-permute-start(f32[16,32,256]{2,1,0:T(8,128)S(1)} %last_update.3.refs_2_), channel_id=1, source_target_pairs={{0,8},{1,9},{2,10},{3,11},{4,12},{5,13},{6,14},{7,15},{8,0},{9,1},... | collective-permute-start | bytes 1572872 | tf_op jit(solution)/shard_map/ppermute | solution.py:34
  (12 other events, 17.1 us)
